TPU v7x, 32 devices: a whole 2x2x4 slice. The times are simulated.
32 devices in a mesh: groups: 2 (over y), dp: 16 (over z, x, core), tensor: 1.
Axes of the slice: x: 2, y: 2, z: 4, core: 2. Of those that a mesh axis runs over, the one named last changes fastest.
Arguments:
- hidden_acts: bfloat16 [16384, 14336], P(('groups', 'dp'), 'tensor'), parts along dimension 0, may hold values from -6 to 6
- output_grads: bfloat16 [16384, 8192], P(('groups', 'dp'), 'tensor'), parts along dimension 0, may hold values from -6 to 6
- query_left: bfloat16 [64, 16, 14336], P('dp', None, 'tensor'), may hold values from -0.005859375 to 0.005859375
- query_right: bfloat16 [64, 16, 8192], P('dp', None, 'tensor'), may hold values from -0.0078125 to 0.0078125
- bucket_ids: int32 [128], P(('groups', 'dp')), parts along dimension 0, may hold values from 0 to 3, as said below
- seq_lengths: int32 [128], P(('groups', 'dp')), parts along dimension 0, may hold values from 0 to 512, as said below
Outputs:
- scores: float32 [64, 128], P('tensor', ('groups', 'dp')), parts along dimension 1
There are 2 independent parts, one for each index of `groups`. A program takes and returns all parts, laid end to end along the dimension named above; an argument that names none is the same for every part. Nothing has to cross between parts.
Inputs may be any that keep to these rules, and one draw needn't show every extreme that they name: `bucket_ids`: each group of 4 slots lists its used buckets first and empty slots (id 3) last; their bucket lengths sum to at most 512. `seq_lengths`: A slot of bucket 0 has length 1 to 128; of bucket 1 or 2, more than half of its bucket length and at most all of it; an empty slot has length 0.
All inputs are finite; a program needn't handle non-finite values.
Results may differ from a plain program's by a relative error of at most 0.0003.
Values may be sent and summed in bfloat16 or wider, within the bound.
No kernel may reach another device: no remote copies, remote signals or barrier semaphores. Data moves between devices by JAX's collectives and lax.ppermute only.
A program may use at most 128 MiB of HBM per device.

v0:
```python
import jax
import jax.numpy as jnp
from jax import lax
from jax.sharding import PartitionSpec as P

BUCKET = 128


def bucket_lengths(slot_ids):
    return BUCKET * jnp.where(
        slot_ids == 0, 1, jnp.where(slot_ids == 1, 2, jnp.where(slot_ids == 2, 4, 0))
    ).astype(jnp.int32)


def slot_matrix(slot_ids, lengths, positions):
    widths = bucket_lengths(slot_ids)
    starts = jnp.cumsum(widths) - widths
    place = jnp.arange(positions, dtype=jnp.int32)[:, None]
    inside = (place >= starts[None, :]) & (place < starts[None, :] + lengths[None, :])
    return inside.astype(jnp.float32)


def project(acts, factors):
    rows = factors.reshape(-1, factors.shape[2])
    return lax.dot_general(acts, rows, (((1,), (1,)), ((), ())), preferred_element_type=jnp.float32)


def on_device(hidden_acts, output_grads, query_left, query_right, bucket_ids, seq_lengths):
    tokens_here = hidden_acts.shape[0]
    rank_count = query_left.shape[1]
    left_all, right_all = (
        lax.all_gather(query_left, "dp", axis=0, tiled=True),
        lax.all_gather(query_right, "dp", axis=0, tiled=True),
    )
    left_proj = project(hidden_acts, left_all)
    right_proj = project(output_grads, right_all)
    queries = left_proj.shape[1] // rank_count
    left_terms = left_proj.reshape(tokens_here, queries, rank_count)
    right_terms = right_proj.reshape(tokens_here, queries, rank_count)
    left_terms, right_terms = lax.psum((left_terms, right_terms), "tensor")
    share_size = queries // lax.axis_size("tensor")
    first_query = lax.axis_index("tensor") * share_size
    left_terms = lax.dynamic_slice_in_dim(left_terms, first_query, share_size, 1)
    right_terms = lax.dynamic_slice_in_dim(right_terms, first_query, share_size, 1)
    token_term = jnp.sum(left_terms * right_terms, axis=2)
    slot_mask = slot_matrix(bucket_ids, seq_lengths, tokens_here)
    return jnp.dot(
        token_term.T, slot_mask, precision=lax.Precision.HIGHEST, preferred_element_type=jnp.float32
    )


def solution(mesh):
    return jax.shard_map(
        on_device,
        mesh=mesh,
        in_specs=(
            P(("groups", "dp"), "tensor"),
            P(("groups", "dp"), "tensor"),
            P("dp", None, "tensor"),
            P("dp", None, "tensor"),
            P(("groups", "dp")),
            P(("groups", "dp")),
        ),
        out_specs=P("tensor", ("groups", "dp")),
        check_vma=False,
    )
```

profile of v0, /device:TPU:9, one launch (start us, length us, event | category | flops | bytes accessed | tf_op | source)
XLA Modules:
  0.0 325.3 jit_solution(4220775443992451273)
XLA Ops:
  6.5 0.0 all-gather.5.cloned.1.call-start
  6.5 0.7 all-gather.5.cloned.1.call-update
  7.3 0.0 all-gather.3.cloned.1.call-start
  7.3 0.7 all-gather.3.cloned.1.call-update
  8.0 0.7 fusion.18
  8.7 0.2 reduce-window.9
  8.8 0.7 fusion.16
  9.5 126.6 %all-gather.5.cloned.1.call-done = bf16[64,16,8192]{2,1,0:T(8,128)(2,1)} async-done(((bf16[4,16,8192]{2,1,0:T(8,128)(2,1)}), bf16[64,16,8192]{2,1,0:T(8,128)(2,1)}) %all-gather.5.cloned.1.call-update) | async-done | bytes 16777232 | tf_op jit(solution)/shard_map/all_gather | solution.py:33
  136.2 18.7 %fusion.2 = f32[512,64,16]{0,1,2:T(8,128)S(1)} fusion(bf16[64,16,8192]{2,1,0:T(8,128)(2,1)} %all-gather.5.cloned.1.call-done, bf16[512,8192]{1,0:T(8,128)(2,1)} %param.7), kind=kOutput, calls=%fused_computation.2 | convolution fusion | flops 8589934592 | bytes 27262976 | tf_op jit(solution)/shard_map/dot_general | solution.py:25
  154.9 131.3 %all-gather.3.cloned.1.call-done = bf16[64,16,14336]{2,1,0:T(8,128)(2,1)} async-done(((bf16[4,16,14336]{2,1,0:T(8,128)(2,1)}), bf16[64,16,14336]{2,1,0:T(8,128)(2,1)}) %all-gather.3.cloned.1.call-update) | async-done | bytes 29360144 | tf_op jit(solution)/shard_map/all_gather | solution.py:32
  286.2 31.4 %multiply_reduce_fusion = f32[512,64]{0,1:T(8,128)S(1)} fusion(f32[512,64,16]{0,1,2:T(8,128)S(1)} %fusion.2, bf16[64,16,14336]{2,1,0:T(8,128)(2,1)} %all-gather.3.cloned.1.call-done, bf16[512,14336]{1,0:T(8,128)(2,1)} %param.6), kind=kOutput, calls=%fused_computation.6 | convolution fusion | flops 15033401344 | bytes 46268416 | tf_op jit(solution)/shard_map/dot_general | solution.py:25
  317.5 0.9 fusion.11
Async XLA Ops:
  6.5 129.6 %all-gather.5.cloned.1.call-start = ((), (), s32[]{:S(2)}) async-start(), calls=%async_computation.1 | async-start | bytes 17825792 | tf_op jit(solution)/shard_map/all_gather | solution.py:33
  7.3 278.9 %all-gather.3.cloned.1.call-start = ((), (), s32[]{:S(2)}) async-start(), calls=%async_computation | async-start | bytes 31195136 | tf_op jit(solution)/shard_map/all_gather | solution.py:32
Sparse Core Ops, SparseCore 0:
  9.5 126.6 all-gather.4
  137.8 148.3 all-gather.2
where the time goes:
time: 327 us; the launch traced here: 325 us
  waiting for transfers between devices  259 us (79%)
  matrix products  51 us (16%)
  between operations  13.4 us (4%)
    all_gather x1, waiting for transfers between devices, on_device(): lax.all_gather(query_left, 'dp', axis=0, tiled=True)  131 us
    all_gather x1, waiting for transfers between devices, on_device(): lax.all_gather(query_right, 'dp', axis=0, tiled=True)  127 us
    dot_general x2, matrix products, project(): lax.dot_general(acts, rows, (((1,), (1,)), ((), ())), preferred_element_t...  50.1 us
  transfers between devices with their start and end apart: 2, of which 2 were waited for; matrix products, arithmetic and copies ran while one was open for 6% of the time, Pallas kernels for 0%

commit v1 on v0

--- a/solution.py
+++ b/solution.py
@@ -1,6 +1,10 @@
+import functools
+
 import jax
 import jax.numpy as jnp
 from jax import lax
+from jax.experimental import pallas as pl
+from jax.experimental.pallas import tpu as pltpu
 from jax.sharding import PartitionSpec as P
 
 BUCKET = 128
@@ -25,7 +29,7 @@
     return lax.dot_general(acts, rows, (((1,), (1,)), ((), ())), preferred_element_type=jnp.float32)
 
 
-def on_device(hidden_acts, output_grads, query_left, query_right, bucket_ids, seq_lengths):
+def gather_whole(hidden_acts, output_grads, query_left, query_right, bucket_ids, seq_lengths):
     tokens_here = hidden_acts.shape[0]
     rank_count = query_left.shape[1]
     left_all, right_all = (
@@ -49,9 +53,180 @@
     )
 
 
+CORE, COLUMN, NEAR, ACROSS = 1, 2, 4, 12
+OPPOSITE = 8
+VMEM_LIMIT = 40 * 1024 * 1024
+
+
+def flip(array, code, count):
+    return lax.ppermute(array, "dp", [(i, i ^ code) for i in range(count)])
+
+
+def swap_groups(array):
+    return lax.ppermute(array, "groups", [(0, 1), (1, 0)])
+
+
+def lines(array, pairs):
+    return lax.ppermute(
+        array, "dp", [(a * 4 + rest, b * 4 + rest) for a, b in pairs for rest in range(4)]
+    )
+
+
+def proj_kernel(count, first_ref, own_ref, other_ref, *refs):
+    del first_ref
+    pieces, out_ref = refs[:count], refs[count]
+    step = pl.program_id(0)
+    rows = own_ref.shape[0]
+    factors = jnp.concatenate([p[...] for p in pieces], axis=0)
+    dims = (((1,), (1,)), ((), ()))
+    top = lax.dot_general(own_ref[...], factors, dims, preferred_element_type=jnp.float32)
+    low = lax.dot_general(other_ref[...], factors, dims, preferred_element_type=jnp.float32)
+
+    @pl.when(step == 0)
+    def _():
+        out_ref[:rows] = top
+        out_ref[rows:] = low
+
+    @pl.when(step > 0)
+    def _():
+        out_ref[:rows] += top
+        out_ref[rows:] += low
+
+
+def proj(own, other, pieces, first, block):
+    rows, depth = own.shape[0], pieces[0].shape[1]
+    steps = depth // block
+    held = sum(p.shape[0] for p in pieces)
+    tokens = pl.BlockSpec((rows, block), lambda k, first: (0, first[0] * steps + k))
+    return pl.pallas_call(
+        functools.partial(proj_kernel, len(pieces)),
+        out_shape=jax.ShapeDtypeStruct((2 * rows, held), jnp.float32),
+        grid_spec=pltpu.PrefetchScalarGridSpec(
+            num_scalar_prefetch=1,
+            grid=(steps,),
+            in_specs=[tokens, tokens]
+            + [pl.BlockSpec((p.shape[0], block), lambda k, first: (0, k)) for p in pieces],
+            out_specs=pl.BlockSpec((2 * rows, held), lambda k, first: (0, 0)),
+        ),
+        compiler_params=pltpu.CompilerParams(vmem_limit_bytes=VMEM_LIMIT),
+        cost_estimate=pl.CostEstimate(
+            flops=4 * rows * held * depth,
+            bytes_accessed=4 * rows * depth + 2 * held * depth + 8 * rows * held,
+            transcendentals=0,
+        ),
+    )(first, own, other, *pieces)
+
+
+def score_kernel(slots, spans_ref, mine_ref, theirs_ref, right_ref, out_ref):
+    rows = mine_ref.shape[0] // 2
+    place = lax.broadcasted_iota(jnp.int32, (rows, 1), 0)
+    for part in range(2):
+        here = slice(part * rows, (part + 1) * rows)
+        terms = (mine_ref[here] + theirs_ref[here]) * right_ref[here]
+        for j in range(slots):
+            k = part * slots + j
+            inside = (place >= spans_ref[0, k]) & (place < spans_ref[1, k])
+            out_ref[k : k + 1, :] = jnp.sum(
+                jnp.where(inside, terms, 0.0), axis=0, keepdims=True
+            )
+
+
+def score(spans, mine, theirs, right):
+    slots = spans.shape[1] // 2
+    return pl.pallas_call(
+        functools.partial(score_kernel, slots),
+        out_shape=jax.ShapeDtypeStruct((2 * slots, mine.shape[1]), jnp.float32),
+        in_specs=[pl.BlockSpec(memory_space=pltpu.SMEM)]
+        + [pl.BlockSpec(memory_space=pltpu.VMEM)] * 3,
+        out_specs=pl.BlockSpec(memory_space=pltpu.VMEM),
+        compiler_params=pltpu.CompilerParams(vmem_limit_bytes=VMEM_LIMIT),
+        cost_estimate=pl.CostEstimate(
+            flops=10 * mine.size, bytes_accessed=12 * mine.size, transcendentals=0
+        ),
+    )(spans, mine, theirs, right)
+
+
+def spans_of(slot_ids, lengths):
+    widths = bucket_lengths(slot_ids)
+    starts = jnp.cumsum(widths) - widths
+    return jnp.stack([starts, starts + lengths]).astype(jnp.int32)
+
+
+def relay(hidden_acts, output_grads, query_left, query_right, bucket_ids, seq_lengths):
+    count = lax.axis_size("dp")
+    me, group = lax.axis_index("dp"), lax.axis_index("groups")
+    z = me // 4
+    local, ranks = query_left.shape[:2]
+    left = query_left.reshape(local * ranks, -1)
+    half = left.shape[1] // 2
+    send = functools.partial(flip, count=count)
+
+    grads_there = send(output_grads, CORE)
+    acts_there = send(hidden_acts, CORE)
+    spans_here = spans_of(bucket_ids, seq_lengths)
+    spans = jnp.concatenate([spans_here, send(spans_here, CORE)], axis=1)
+
+    a, b, c = {}, {}, {}
+    a[0] = lax.dynamic_slice_in_dim(left, group * half, half, 1)
+    c[0] = lax.dynamic_slice_in_dim(left, (1 - group) * half, half, 1)
+    b[0] = query_right.reshape(local * ranks, -1)
+
+    def along_z(held):
+        held[NEAR] = send(held[0], NEAR)
+        held[ACROSS] = send(held[0], ACROSS)
+        outer = lines(held[ACROSS], [(1, 0), (2, 3)])
+        inner = lines(held[NEAR], [(2, 1), (1, 2)])
+        held[OPPOSITE] = jnp.where((z == 0) | (z == 3), outer, inner)
+
+    def over_x(held, code):
+        held[code | COLUMN] = send(held[code], COLUMN)
+
+    over_x(a, 0)
+    along_z(a)
+    over_x(b, 0)
+    for code in (NEAR, ACROSS, OPPOSITE):
+        over_x(a, code)
+    along_z(b)
+    b[NEAR | COLUMN] = send(b[COLUMN], NEAR)
+    for code in (ACROSS, OPPOSITE):
+        over_x(b, code)
+    order = (COLUMN, NEAR, ACROSS, NEAR | COLUMN, OPPOSITE, ACROSS | COLUMN, OPPOSITE | COLUMN)
+    for code in order:
+        c[code] = swap_groups(a[code])
+
+    mine = jnp.reshape(group, (1,)).astype(jnp.int32)
+    zero = jnp.zeros((1,), jnp.int32)
+    groups = (
+        (0, COLUMN, NEAR, ACROSS),
+        (NEAR | COLUMN, OPPOSITE, ACROSS | COLUMN, OPPOSITE | COLUMN),
+    )
+    sums = []
+    for codes in groups:
+        left_mine = proj(hidden_acts, acts_there, [a[k] for k in codes], mine, 1024)
+        left_theirs = proj(hidden_acts, acts_there, [c[k] for k in codes], 1 - mine, 1024)
+        right = proj(output_grads, grads_there, [b[k] for k in codes], zero, 1024)
+        sums.append(score(spans, left_mine, left_theirs, right))
+
+    slots = bucket_ids.shape[0]
+    table = jnp.concatenate(sums, axis=1)
+    table = jnp.sum(table.reshape(2 * slots, -1, ranks), axis=2).T.reshape(-1, local, 2 * slots)
+    ours, others = table[..., :slots], table[..., slots:]
+    others = send(others, CORE)
+    place = {code: k for k, code in enumerate(groups[0] + groups[1])}
+    rows = jnp.stack(
+        [others[place[k & ~CORE]] if k & CORE else ours[place[k]] for k in range(count)]
+    )
+    for bit in (1, 2, 4, 8):
+        paired = rows.reshape(-1, 2, bit, local, slots)
+        rows = jnp.where((me & bit) != 0, paired[:, ::-1], paired).reshape(rows.shape)
+    return rows.reshape(count * local, slots)
+
+
 def solution(mesh):
+    sizes = mesh.shape
+    fits = sizes["dp"] == 16 and sizes["groups"] == 2 and sizes["tensor"] == 1
     return jax.shard_map(
-        on_device,
+        relay if fits else gather_whole,
         mesh=mesh,
         in_specs=(
             P(("groups", "dp"), "tensor"),

time: 327 us -> 307 us (0.939)
  waiting for transfers between devices: 259 us -> 187 us
  Pallas kernels: 0 us -> 62.6 us
  matrix products: 51 us -> 0 us
  starting transfers between devices: 0.04 us -> 42.7 us
  between operations: 13.4 us -> 0.27 us
  local copies, waits for them, and re-layouts: 0 us -> 7.23 us
    all_gather x2 -> x0, waiting for transfers between devices: 258 us -> none  [the longest x1 131 us: on_device(): lax.all_gather(query_left, 'dp', axis=0, tiled=True)]
    ppermute x0 -> x27, waiting for transfers between devices: none -> 187 us  [the longest x16 144 us: flip(): return lax.ppermute(array, 'dp', [(i, i ^ code) for i in range(count)])]
    pallas_call x0 -> x8, Pallas kernels: none -> 62.6 us  [the longest x6 59.2 us: proj(): pl.pallas_call(functools.partial(proj_kernel, len(pieces)), out_shape=jax...]
    dot_general x3 -> x0, matrix products: 51 us -> none  [the longest x2 50.1 us: project(): lax.dot_general(acts, rows, (((1,), (1,)), ((), ())), preferred_element_t...]
    ppermute x0 -> x27, starting transfers between devices: none -> 42.7 us  [the longest x16 26.6 us: flip(): return lax.ppermute(array, 'dp', [(i, i ^ code) for i in range(count)])]
    unnamed x0 -> x23, local copies, waits for them, and re-layouts: none -> 4.44 us
  transfers between devices with their start and end apart: 2 -> 27, of which waited for: 2 -> 15; matrix products, arithmetic and copies ran while one was open for 6% -> 2% of each run, Pallas kernels for 0% -> 17%
where the time goes in v1:
time: 307 us; the launch traced here: 303 us
  waiting for transfers between devices  187 us (61%)
  Pallas kernels  62.6 us (20%)
  starting transfers between devices  42.7 us (14%)
  local copies, waits for them, and re-layouts  7.23 us (2%)
  other arithmetic  3.21 us (1%)
    ppermute x16, waiting for transfers between devices, flip(): return lax.ppermute(array, 'dp', [(i, i ^ code) for i in range(count)])  144 us
    pallas_call x6, Pallas kernels, proj(): pl.pallas_call(functools.partial(proj_kernel, len(pieces)), out_shape=jax...  59.2 us
    ppermute x7, waiting for transfers between devices, swap_groups(): return lax.ppermute(array, 'groups', [(0, 1), (1, 0)])  28 us
    ppermute x16, starting transfers between devices, flip(): return lax.ppermute(array, 'dp', [(i, i ^ code) for i in range(count)])  26.6 us
    ppermute x4, waiting for transfers between devices, lines(): lax.ppermute(array, 'dp', [(a * 4 + rest, b * 4 + rest) for a, b in pairs...  14.6 us
    ppermute x4, starting transfers between devices, lines(): lax.ppermute(array, 'dp', [(a * 4 + rest, b * 4 + rest) for a, b in pairs...  9.29 us
    ppermute x7, starting transfers between devices, swap_groups(): return lax.ppermute(array, 'groups', [(0, 1), (1, 0)])  6.79 us
  transfers between devices with their start and end apart: 27, of which 15 were waited for; matrix products, arithmetic and copies ran while one was open for 2% of the time, Pallas kernels for 17%

profile of v1, /device:TPU:9, one launch (start us, length us, event | category | flops | bytes accessed | tf_op | source)
XLA Modules:
  0.0 302.6 jit_solution(10951716962092784449)
XLA Ops:
  0.7 1.6 constant_dynamic-slice_fusion
  2.3 1.4 collective-permute-start.4
  3.7 2.2 collective-permute-start.3
  8.5 14.0 %collective-permute-done = s32[2,4]{1,0:T(2,128)S(1)} collective-permute-done((s32[2,4]{1,0:T(2,128)S(1)}, s32[2,4]{1,0:T(2,128)S(1)}, u32[]{:S(2)}, u32[]{:S(2)}) %collective-permute-start) | collective-permute-done | bytes 64 | tf_op jit(solution)/shard_map/ppermute | solution.py:62
  23.7 20.0 %collective-permute-done.4.refs_3_ = bf16[64,7168]{1,0:T(8,128)(2,1)} collective-permute-done((bf16[64,7168]{1,0:T(8,128)(2,1)S(1)}, bf16[64,7168]{1,0:T(8,128)(2,1)}, u32[]{:S(2)}, u32[]{:S(2)}) %collective-permute-start.4) | collective-permute-done | bytes 917536 | tf_op jit(solution)/shard_map/ppermute | solution.py:62
  45.7 1.3 collective-permute-start.10
  48.0 1.5 collective-permute-start.9
  49.4 40.9 %collective-permute-done.11.refs_3_ = bf16[64,8192]{1,0:T(8,128)(2,1)} collective-permute-done((bf16[64,8192]{1,0:T(8,128)(2,1)}, bf16[64,8192]{1,0:T(8,128)(2,1)}, u32[]{:S(2)}, u32[]{:S(2)}) %collective-permute-start.11) | collective-permute-done | bytes 1048608 | tf_op jit(solution)/shard_map/ppermute | solution.py:62
  90.3 2.3 collective-permute-start.22
  92.6 3.4 %collective-permute-start.23 = (bf16[64,8192]{1,0:T(8,128)(2,1)}, bf16[64,8192]{1,0:T(8,128)(2,1)}, u32[]{:S(2)}, u32[]{:S(2)}) collective-permute-start(bf16[64,8192]{1,0:T(8,128)(2,1)} %collective-permute-done.10.refs_2_), channel_id=1, source_target_pairs={{8,4},{9,5},{10,6},{11,7},{4,8},{5,9},{6,10},{7,11},{24,20},{25,21... | collective-permute-start | bytes 3145736 | tf_op jit(solution)/shard_map/ppermute | solution.py:70
  97.3 19.7 %collective-permute-done.15.refs_2_ = bf16[64,7168]{1,0:T(8,128)(2,1)} collective-permute-done((bf16[64,7168]{1,0:T(8,128)(2,1)}, bf16[64,7168]{1,0:T(8,128)(2,1)}, u32[]{:S(2)}, u32[]{:S(2)}) %collective-permute-start.15) | collective-permute-done | bytes 917536 | tf_op jit(solution)/shard_map/ppermute | solution.py:62
  117.1 1.3 collective-permute-start.13
  119.7 2.2 collective-permute-start.14
  122.0 1.4 broadcast_select_fusion.refs_1_
  123.3 13.1 %collective-permute-done.13 = bf16[64,7168]{1,0:T(8,128)(2,1)S(1)} collective-permute-done((bf16[64,7168]{1,0:T(8,128)(2,1)}, bf16[64,7168]{1,0:T(8,128)(2,1)S(1)}, u32[]{:S(2)}, u32[]{:S(2)}) %collective-permute-start.13) | collective-permute-done | bytes 917536 | tf_op jit(solution)/shard_map/ppermute | solution.py:70
  138.4 1.3 collective-permute-start.21
  139.8 1.5 collective-permute-done.14
  142.6 16.0 %collective-permute-done.24.refs_2_ = bf16[64,8192]{1,0:T(8,128)(2,1)S(1)} collective-permute-done((bf16[64,8192]{1,0:T(8,128)(2,1)}, bf16[64,8192]{1,0:T(8,128)(2,1)S(1)}, u32[]{:S(2)}, u32[]{:S(2)}) %collective-permute-start.24) | collective-permute-done | bytes 1048608 | tf_op jit(solution)/shard_map/ppermute | solution.py:62
  161.5 19.5 %collective-permute-done.25.refs_3_ = bf16[64,8192]{1,0:T(8,128)(2,1)S(1)} collective-permute-done((bf16[64,8192]{1,0:T(8,128)(2,1)S(1)}, bf16[64,8192]{1,0:T(8,128)(2,1)S(1)}, u32[]{:S(2)}, u32[]{:S(2)}) %collective-permute-start.25) | collective-permute-done | bytes 1048608 | tf_op jit(solution)/shard_map/ppermute | solution.py:62
  183.6 3.4 %copy-done = bf16[512,8192]{1,0:T(8,128)(2,1)S(1)} copy-done((bf16[512,8192]{1,0:T(8,128)(2,1)S(1)}, bf16[512,8192]{1,0:T(8,128)(2,1)}, u32[]{:S(2)}) %copy-start) | copy-done | bytes 8388632
  186.9 10.1 %shard_map.66.right_ref = f32[1024,256]{1,0:T(8,128)S(1)} custom-call(s32[1]{0:T(128)} %constant.46.clone.1.first_ref, bf16[512,8192]{1,0:T(8,128)(2,1)S(1)} %copy-done, bf16[512,8192]{1,0:T(8,128)(2,1)} %collective-permute-done.8.other_ref, bf16[64,8192]{1,0:T(8,128)(2,1)S(1)} %bitcast.31, bf16[64,8192]{1,0:T(8,128)(2,1)} %collective-permute-done.9.refs_1_, ...), custom_call_target="tpu_custom_call" | custom-call | flops 4294967296 | bytes 22020096 | tf_op jit(solution)/shard_map/pallas_call | solution.py:101
  197.1 9.8 %shard_map.70.right_ref = f32[1024,256]{1,0:T(8,128)S(1)} custom-call(s32[1]{0:T(128)} %constant.46.clone.1.first_ref, bf16[512,8192]{1,0:T(8,128)(2,1)S(1)} %copy-done, bf16[512,8192]{1,0:T(8,128)(2,1)} %collective-permute-done.8.other_ref, bf16[64,8192]{1,0:T(8,128)(2,1)S(1)} %collective-permute-done.21.refs_0_, ...), custom_call_target="tpu_custom_call" | custom-call | flops 4294967296 | bytes 22020096 | tf_op jit(solution)/shard_map/pallas_call | solution.py:101
  208.4 11.9 %collective-permute-done.16.refs_3_ = bf16[64,7168]{1,0:T(8,128)(2,1)S(1)} collective-permute-done((bf16[64,7168]{1,0:T(8,128)(2,1)S(1)}, bf16[64,7168]{1,0:T(8,128)(2,1)S(1)}, u32[]{:S(2)}, u32[]{:S(2)}) %collective-permute-start.16) | collective-permute-done | bytes 917536 | tf_op jit(solution)/shard_map/ppermute | solution.py:62
  221.8 9.9 %shard_map.64.mine_ref = f32[1024,256]{1,0:T(8,128)S(1)} custom-call(s32[1]{0:T(128)} %bitcast.4.first_ref, bf16[512,14336]{1,0:T(8,128)(2,1)} %own_ref.10, bf16[512,14336]{1,0:T(8,128)(2,1)} %collective-permute-done.1.other_ref, bf16[64,7168]{1,0:T(8,128)(2,1)S(1)} %get-tuple-element.6.refs_0_, bf16[64,7168]{1,0:T(8,128)(2,1)S(1)} %copy-done.3, ...), custom_call_target="tpu_custom_call" | custom-call | flops 3758096384 | bytes 19398656 | tf_op jit(solution)/shard_map/pallas_call | solution.py:101
  231.7 9.8 %shard_map.65.theirs_ref = f32[1024,256]{1,0:T(8,128)S(1)} custom-call(s32[1]{0:T(128)S(6)} %sub.15.first_ref, bf16[512,14336]{1,0:T(8,128)(2,1)} %own_ref.10, bf16[512,14336]{1,0:T(8,128)(2,1)} %collective-permute-done.1.other_ref, bf16[64,7168]{1,0:T(8,128)(2,1)S(1)} %get-tuple-element.5.refs_0_, bf16[64,7168]{1,0:T(8,128)(2,1)} %collective-permute-done.5.refs_1_, ...), custom_call_target="tpu_custom_call" | custom-call | flops 3758096384 | bytes 19398656 | tf_op jit(solution)/shard_map/pallas_call | solution.py:101
  241.5 1.7 shard_map.67
  243.2 9.8 %shard_map.68.mine_ref = f32[1024,256]{1,0:T(8,128)S(1)} custom-call(s32[1]{0:T(128)} %bitcast.4.first_ref, bf16[512,14336]{1,0:T(8,128)(2,1)} %own_ref.10, bf16[512,14336]{1,0:T(8,128)(2,1)} %collective-permute-done.1.other_ref, bf16[64,7168]{1,0:T(8,128)(2,1)S(1)} %collective-permute-done.12.refs_0_, bf16[64,7168]{1,0:T(8,128)(2,1)S(1)} %broadcast_select_fusion.1.refs_1_, ...), custom_call_target="tpu_custom_call" | custom-call | flops 3758096384 | bytes 19398656 | tf_op jit(solution)/shard_map/pallas_call | solution.py:101
  253.1 7.5 %collective-permute-done.17.refs_0_ = bf16[64,7168]{1,0:T(8,128)(2,1)S(1)} collective-permute-done((bf16[64,7168]{1,0:T(8,128)(2,1)S(1)}, bf16[64,7168]{1,0:T(8,128)(2,1)S(1)}, u32[]{:S(2)}, u32[]{:S(2)}) %collective-permute-start.17) | collective-permute-done | bytes 917536 | tf_op jit(solution)/shard_map/ppermute | solution.py:66
  260.6 19.7 %collective-permute-done.20.refs_3_ = bf16[64,7168]{1,0:T(8,128)(2,1)S(1)} collective-permute-done((bf16[64,7168]{1,0:T(8,128)(2,1)S(1)}, bf16[64,7168]{1,0:T(8,128)(2,1)S(1)}, u32[]{:S(2)}, u32[]{:S(2)}) %collective-permute-start.20) | collective-permute-done | bytes 917536 | tf_op jit(solution)/shard_map/ppermute | solution.py:66
  280.3 9.8 %shard_map.69.theirs_ref = f32[1024,256]{1,0:T(8,128)S(1)} custom-call(s32[1]{0:T(128)S(6)} %sub.15.first_ref, bf16[512,14336]{1,0:T(8,128)(2,1)} %own_ref.10, bf16[512,14336]{1,0:T(8,128)(2,1)} %collective-permute-done.1.other_ref, bf16[64,7168]{1,0:T(8,128)(2,1)S(1)} %collective-permute-done.17.refs_0_, ...), custom_call_target="tpu_custom_call" | custom-call | flops 3758096384 | bytes 19398656 | tf_op jit(solution)/shard_map/pallas_call | solution.py:101
  290.1 1.7 shard_map.71
  292.1 8.5 %collective-permute-start.26 = (f32[8,4,4]{2,1,0:T(4,128)S(1)}, f32[8,4,4]{2,1,0:T(4,128)S(1)}, u32[]{:S(2)}, u32[]{:S(2)}) collective-permute-start(f32[8,4,4]{2,1,0:T(4,128)S(1)} %slice.78), channel_id=1, source_target_pairs={{0,1},{1,0},{2,3},{3,2},{4,5},{5,4},{6,7},{7,6},{8,9},{9,8},{10,11... | collective-permute-start | bytes 1544 | tf_op jit(solution)/shard_map/ppermute | solution.py:62
  (75 shorter events, 24.2 us)
Async XLA Ops:
  0.0 183.6 %copy-start.1 = (bf16[4,16,8192]{2,1,0:T(8,128)(2,1)S(1)}, bf16[4,16,8192]{2,1,0:T(8,128)(2,1)}, u32[]{:S(2)}) copy-start(bf16[4,16,8192]{2,1,0:T(8,128)(2,1)} %param.9) | copy-start | bytes 3145732
  0.0 221.6 %collective-permute-start.1 = (bf16[512,14336]{1,0:T(8,128)(2,1)}, bf16[512,14336]{1,0:T(8,128)(2,1)}, u32[]{:S(2)}, u32[]{:S(2)}) collective-permute-start(bf16[512,14336]{1,0:T(8,128)(2,1)} %own_ref.10), channel_id=1, source_target_pairs={{0,1},{1,0},{2,3},{3,2},{4,5},{5,4},{6,7},{7,6},{8,9},{9,8},{10,11... | collective-permute-start | bytes 44040200 | tf_op jit(solution)/shard_map/ppermute | solution.py:62
  0.7 181.6 %collective-permute-start.8 = (bf16[512,8192]{1,0:T(8,128)(2,1)}, bf16[512,8192]{1,0:T(8,128)(2,1)}, u32[]{:S(2)}, u32[]{:S(2)}) collective-permute-start(bf16[512,8192]{1,0:T(8,128)(2,1)} %own_ref.11), channel_id=1, source_target_pairs={{0,1},{1,0},{2,3},{3,2},{4,5},{5,4},{6,7},{7,6},{8,9},{9,8},{10,11... | collective-permute-start | bytes 25165832 | tf_op jit(solution)/shard_map/ppermute | solution.py:62
  2.3 41.3 %collective-permute-start.4 = (bf16[64,7168]{1,0:T(8,128)(2,1)S(1)}, bf16[64,7168]{1,0:T(8,128)(2,1)}, u32[]{:S(2)}, u32[]{:S(2)}) collective-permute-start(bf16[64,7168]{1,0:T(8,128)(2,1)S(1)} %get-tuple-element.6.refs_0_), channel_id=1, source_target_pairs={{0,12},{1,13},{2,14},{3,15},{4,8},{5,9},{6,10},{7,11},{8,4},{9,5},... | collective-permute-start | bytes 2752520 | tf_op jit(solution)/shard_map/ppermute | solution.py:62
  3.7 42.0 %collective-permute-start.3 = (bf16[64,7168]{1,0:T(8,128)(2,1)S(1)}, bf16[64,7168]{1,0:T(8,128)(2,1)}, u32[]{:S(2)}, u32[]{:S(2)}) collective-permute-start(bf16[64,7168]{1,0:T(8,128)(2,1)S(1)} %get-tuple-element.6.refs_0_), channel_id=1, source_target_pairs={{0,4},{1,5},{2,6},{3,7},{4,0},{5,1},{6,2},{7,3},{8,12},{9,13},{10,... | collective-permute-start | bytes 2752520 | tf_op jit(solution)/shard_map/ppermute | solution.py:62
  7.4 15.1 %collective-permute-start = (s32[2,4]{1,0:T(2,128)S(1)}, s32[2,4]{1,0:T(2,128)S(1)}, u32[]{:S(2)}, u32[]{:S(2)}) collective-permute-start(s32[2,4]{1,0:T(2,128)S(1)} %pad_add_fusion), channel_id=1, source_target_pairs={{0,1},{1,0},{2,3},{3,2},{4,5},{5,4},{6,7},{7,6},{8,9},{9,8},{10,11... | collective-permute-start | bytes 104 | tf_op jit(solution)/shard_map/ppermute | solution.py:62
  22.5 24.6 %collective-permute-start.2 = (bf16[64,7168]{1,0:T(8,128)(2,1)S(1)}, bf16[64,7168]{1,0:T(8,128)(2,1)S(1)}, u32[]{:S(2)}, u32[]{:S(2)}) collective-permute-start(bf16[64,7168]{1,0:T(8,128)(2,1)S(1)} %get-tuple-element.6.refs_0_), channel_id=1, source_target_pairs={{0,2},{1,3},{2,0},{3,1},{4,6},{5,7},{6,4},{7,5},{8,10},{9,11},{10,... | collective-permute-start | bytes 2752520 | tf_op jit(solution)/shard_map/ppermute | solution.py:62
  43.6 46.7 %collective-permute-start.11 = (bf16[64,8192]{1,0:T(8,128)(2,1)}, bf16[64,8192]{1,0:T(8,128)(2,1)}, u32[]{:S(2)}, u32[]{:S(2)}) collective-permute-start(bf16[64,8192]{1,0:T(8,128)(2,1)} %bitcast.28), channel_id=1, source_target_pairs={{0,12},{1,13},{2,14},{3,15},{4,8},{5,9},{6,10},{7,11},{8,4},{9,5},... | collective-permute-start | bytes 3145736 | tf_op jit(solution)/shard_map/ppermute | solution.py:62
  45.7 46.9 %collective-permute-start.10 = (bf16[64,8192]{1,0:T(8,128)(2,1)}, bf16[64,8192]{1,0:T(8,128)(2,1)}, u32[]{:S(2)}, u32[]{:S(2)}) collective-permute-start(bf16[64,8192]{1,0:T(8,128)(2,1)} %bitcast.29), channel_id=1, source_target_pairs={{0,4},{1,5},{2,6},{3,7},{4,0},{5,1},{6,2},{7,3},{8,12},{9,13},{10,... | collective-permute-start | bytes 3145736 | tf_op jit(solution)/shard_map/ppermute | solution.py:62
  47.0 0.9 copy-start.2
  48.0 48.1 %collective-permute-start.9 = (bf16[64,8192]{1,0:T(8,128)(2,1)}, bf16[64,8192]{1,0:T(8,128)(2,1)}, u32[]{:S(2)}, u32[]{:S(2)}) collective-permute-start(bf16[64,8192]{1,0:T(8,128)(2,1)} %bitcast.30), channel_id=1, source_target_pairs={{0,2},{1,3},{2,0},{3,1},{4,6},{5,7},{6,4},{7,5},{8,10},{9,11},{10,... | collective-permute-start | bytes 3145736 | tf_op jit(solution)/shard_map/ppermute | solution.py:62
  90.3 28.1 %collective-permute-start.22 = (bf16[64,8192]{1,0:T(8,128)(2,1)}, bf16[64,8192]{1,0:T(8,128)(2,1)}, u32[]{:S(2)}, u32[]{:S(2)}) collective-permute-start(bf16[64,8192]{1,0:T(8,128)(2,1)} %collective-permute-done.11.refs_3_), channel_id=1, source_target_pairs={{4,0},{5,1},{6,2},{7,3},{8,12},{9,13},{10,14},{11,15},{20,16},{21,... | collective-permute-start | bytes 3145736 | tf_op jit(solution)/shard_map/ppermute | solution.py:70
  92.6 27.1 %collective-permute-start.23 = (bf16[64,8192]{1,0:T(8,128)(2,1)}, bf16[64,8192]{1,0:T(8,128)(2,1)}, u32[]{:S(2)}, u32[]{:S(2)}) collective-permute-start(bf16[64,8192]{1,0:T(8,128)(2,1)} %collective-permute-done.10.refs_2_), channel_id=1, source_target_pairs={{8,4},{9,5},{10,6},{11,7},{4,8},{5,9},{6,10},{7,11},{24,20},{25,21... | collective-permute-start | bytes 3145736 | tf_op jit(solution)/shard_map/ppermute | solution.py:70
  96.0 21.0 %collective-permute-start.15 = (bf16[64,7168]{1,0:T(8,128)(2,1)}, bf16[64,7168]{1,0:T(8,128)(2,1)}, u32[]{:S(2)}, u32[]{:S(2)}) collective-permute-start(bf16[64,7168]{1,0:T(8,128)(2,1)} %collective-permute-done.4.refs_3_), channel_id=1, source_target_pairs={{0,2},{1,3},{2,0},{3,1},{4,6},{5,7},{6,4},{7,5},{8,10},{9,11},{10,... | collective-permute-start | bytes 2752520 | tf_op jit(solution)/shard_map/ppermute | solution.py:62
  117.1 19.4 %collective-permute-start.13 = (bf16[64,7168]{1,0:T(8,128)(2,1)}, bf16[64,7168]{1,0:T(8,128)(2,1)S(1)}, u32[]{:S(2)}, u32[]{:S(2)}) collective-permute-start(bf16[64,7168]{1,0:T(8,128)(2,1)} %collective-permute-done.4.refs_3_), channel_id=1, source_target_pairs={{4,0},{5,1},{6,2},{7,3},{8,12},{9,13},{10,14},{11,15},{20,16},{21,... | collective-permute-start | bytes 2752520 | tf_op jit(solution)/shard_map/ppermute | solution.py:70
  118.4 20.0 %collective-permute-start.7 = (bf16[64,7168]{1,0:T(8,128)(2,1)}, bf16[64,7168]{1,0:T(8,128)(2,1)S(1)}, u32[]{:S(2)}, u32[]{:S(2)}) collective-permute-start(bf16[64,7168]{1,0:T(8,128)(2,1)} %collective-permute-done.4.refs_3_), channel_id=1, source_target_pairs={{0,16},{16,0},{1,17},{17,1},{2,18},{18,2},{3,19},{19,3},{4,20},{20... | collective-permute-start | bytes 2752520 | tf_op jit(solution)/shard_map/ppermute | solution.py:66
  119.7 21.5 %collective-permute-start.14 = (bf16[64,7168]{1,0:T(8,128)(2,1)}, bf16[64,7168]{1,0:T(8,128)(2,1)S(1)}, u32[]{:S(2)}, u32[]{:S(2)}) collective-permute-start(bf16[64,7168]{1,0:T(8,128)(2,1)} %collective-permute-done.3.refs_2_), channel_id=1, source_target_pairs={{8,4},{9,5},{10,6},{11,7},{4,8},{5,9},{6,10},{7,11},{24,20},{25,21... | collective-permute-start | bytes 2752520 | tf_op jit(solution)/shard_map/ppermute | solution.py:70
  136.4 22.1 %collective-permute-start.24 = (bf16[64,8192]{1,0:T(8,128)(2,1)}, bf16[64,8192]{1,0:T(8,128)(2,1)S(1)}, u32[]{:S(2)}, u32[]{:S(2)}) collective-permute-start(bf16[64,8192]{1,0:T(8,128)(2,1)} %collective-permute-done.11.refs_3_), channel_id=1, source_target_pairs={{0,2},{1,3},{2,0},{3,1},{4,6},{5,7},{6,4},{7,5},{8,10},{9,11},{10,... | collective-permute-start | bytes 3145736 | tf_op jit(solution)/shard_map/ppermute | solution.py:62
  138.4 21.8 %collective-permute-start.21 = (bf16[64,8192]{1,0:T(8,128)(2,1)}, bf16[64,8192]{1,0:T(8,128)(2,1)S(1)}, u32[]{:S(2)}, u32[]{:S(2)}) collective-permute-start(bf16[64,8192]{1,0:T(8,128)(2,1)} %collective-permute-done.9.refs_1_), channel_id=1, source_target_pairs={{0,4},{1,5},{2,6},{3,7},{4,0},{5,1},{6,2},{7,3},{8,12},{9,13},{10,... | collective-permute-start | bytes 3145736 | tf_op jit(solution)/shard_map/ppermute | solution.py:62
  141.3 39.8 %collective-permute-start.25 = (bf16[64,8192]{1,0:T(8,128)(2,1)S(1)}, bf16[64,8192]{1,0:T(8,128)(2,1)S(1)}, u32[]{:S(2)}, u32[]{:S(2)}) collective-permute-start(bf16[64,8192]{1,0:T(8,128)(2,1)S(1)} %broadcast_select_fusion.refs_1_), channel_id=1, source_target_pairs={{0,2},{1,3},{2,0},{3,1},{4,6},{5,7},{6,4},{7,5},{8,10},{9,11},{10,... | collective-permute-start | bytes 3145736 | tf_op jit(solution)/shard_map/ppermute | solution.py:62
  158.5 48.4 %collective-permute-start.12 = (bf16[64,7168]{1,0:T(8,128)(2,1)}, bf16[64,7168]{1,0:T(8,128)(2,1)S(1)}, u32[]{:S(2)}, u32[]{:S(2)}) collective-permute-start(bf16[64,7168]{1,0:T(8,128)(2,1)} %collective-permute-done.3.refs_2_), channel_id=1, source_target_pairs={{0,2},{1,3},{2,0},{3,1},{4,6},{5,7},{6,4},{7,5},{8,10},{9,11},{10,... | collective-permute-start | bytes 2752520 | tf_op jit(solution)/shard_map/ppermute | solution.py:62
  160.2 47.0 %collective-permute-start.6 = (bf16[64,7168]{1,0:T(8,128)(2,1)}, bf16[64,7168]{1,0:T(8,128)(2,1)S(1)}, u32[]{:S(2)}, u32[]{:S(2)}) collective-permute-start(bf16[64,7168]{1,0:T(8,128)(2,1)} %collective-permute-done.3.refs_2_), channel_id=1, source_target_pairs={{0,16},{16,0},{1,17},{17,1},{2,18},{18,2},{3,19},{19,3},{4,20},{20... | collective-permute-start | bytes 2752520 | tf_op jit(solution)/shard_map/ppermute | solution.py:66
  181.0 39.3 %collective-permute-start.16 = (bf16[64,7168]{1,0:T(8,128)(2,1)S(1)}, bf16[64,7168]{1,0:T(8,128)(2,1)S(1)}, u32[]{:S(2)}, u32[]{:S(2)}) collective-permute-start(bf16[64,7168]{1,0:T(8,128)(2,1)S(1)} %broadcast_select_fusion.1.refs_1_), channel_id=1, source_target_pairs={{0,2},{1,3},{2,0},{3,1},{4,6},{5,7},{6,4},{7,5},{8,10},{9,11},{10,... | collective-permute-start | bytes 2752520 | tf_op jit(solution)/shard_map/ppermute | solution.py:62
  182.3 49.4 %collective-permute-start.5 = (bf16[64,7168]{1,0:T(8,128)(2,1)}, bf16[64,7168]{1,0:T(8,128)(2,1)}, u32[]{:S(2)}, u32[]{:S(2)}) collective-permute-start(bf16[64,7168]{1,0:T(8,128)(2,1)} %copy-done.2), channel_id=1, source_target_pairs={{0,16},{16,0},{1,17},{17,1},{2,18},{18,2},{3,19},{19,3},{4,20},{20... | collective-permute-start | bytes 2752520 | tf_op jit(solution)/shard_map/ppermute | solution.py:66
  183.6 3.4 %copy-start = (bf16[512,8192]{1,0:T(8,128)(2,1)S(1)}, bf16[512,8192]{1,0:T(8,128)(2,1)}, u32[]{:S(2)}) copy-start(bf16[512,8192]{1,0:T(8,128)(2,1)} %own_ref.11) | copy-start | bytes 25165828
  197.1 24.8 %copy-start.3 = (bf16[64,7168]{1,0:T(8,128)(2,1)S(1)}, bf16[64,7168]{1,0:T(8,128)(2,1)}, u32[]{:S(2)}) copy-start(bf16[64,7168]{1,0:T(8,128)(2,1)} %copy-done.2) | copy-start | bytes 2752516
  206.9 46.2 %collective-permute-start.18 = (bf16[64,7168]{1,0:T(8,128)(2,1)S(1)}, bf16[64,7168]{1,0:T(8,128)(2,1)S(1)}, u32[]{:S(2)}, u32[]{:S(2)}) collective-permute-start(bf16[64,7168]{1,0:T(8,128)(2,1)S(1)} %broadcast_select_fusion.1.refs_1_), channel_id=1, source_target_pairs={{0,16},{16,0},{1,17},{17,1},{2,18},{18,2},{3,19},{19,3},{4,20},{20... | collective-permute-start | bytes 2752520 | tf_op jit(solution)/shard_map/ppermute | solution.py:66
  207.2 45.9 %collective-permute-start.19 = (bf16[64,7168]{1,0:T(8,128)(2,1)}, bf16[64,7168]{1,0:T(8,128)(2,1)S(1)}, u32[]{:S(2)}, u32[]{:S(2)}) collective-permute-start(bf16[64,7168]{1,0:T(8,128)(2,1)} %collective-permute-done.15.refs_2_), channel_id=1, source_target_pairs={{0,16},{16,0},{1,17},{17,1},{2,18},{18,2},{3,19},{19,3},{4,20},{20... | collective-permute-start | bytes 2752520 | tf_op jit(solution)/shard_map/ppermute | solution.py:66
  220.3 40.3 %collective-permute-start.17 = (bf16[64,7168]{1,0:T(8,128)(2,1)S(1)}, bf16[64,7168]{1,0:T(8,128)(2,1)S(1)}, u32[]{:S(2)}, u32[]{:S(2)}) collective-permute-start(bf16[64,7168]{1,0:T(8,128)(2,1)S(1)} %collective-permute-done.12.refs_0_), channel_id=1, source_target_pairs={{0,16},{16,0},{1,17},{17,1},{2,18},{18,2},{3,19},{19,3},{4,20},{20... | collective-permute-start | bytes 2752520 | tf_op jit(solution)/shard_map/ppermute | solution.py:66
  221.6 58.7 %collective-permute-start.20 = (bf16[64,7168]{1,0:T(8,128)(2,1)S(1)}, bf16[64,7168]{1,0:T(8,128)(2,1)S(1)}, u32[]{:S(2)}, u32[]{:S(2)}) collective-permute-start(bf16[64,7168]{1,0:T(8,128)(2,1)S(1)} %collective-permute-done.16.refs_3_), channel_id=1, source_target_pairs={{0,16},{16,0},{1,17},{17,1},{2,18},{18,2},{3,19},{19,3},{4,20},{20... | collective-permute-start | bytes 2752520 | tf_op jit(solution)/shard_map/ppermute | solution.py:66
  292.1 9.3 %collective-permute-start.26 = (f32[8,4,4]{2,1,0:T(4,128)S(1)}, f32[8,4,4]{2,1,0:T(4,128)S(1)}, u32[]{:S(2)}, u32[]{:S(2)}) collective-permute-start(f32[8,4,4]{2,1,0:T(4,128)S(1)} %slice.78), channel_id=1, source_target_pairs={{0,1},{1,0},{2,3},{3,2},{4,5},{5,4},{6,7},{7,6},{8,9},{9,8},{10,11... | collective-permute-start | bytes 1544 | tf_op jit(solution)/shard_map/ppermute | solution.py:62

commit v2 on v1

--- a/solution.py
+++ b/solution.py
@@ -55,6 +55,7 @@
 
 CORE, COLUMN, NEAR, ACROSS = 1, 2, 4, 12
 OPPOSITE = 8
+LITTLE = pl.CostEstimate(flops=1, bytes_accessed=1, transcendentals=0)
 VMEM_LIMIT = 40 * 1024 * 1024
 
 
@@ -64,6 +65,25 @@
 
 def swap_groups(array):
     return lax.ppermute(array, "groups", [(0, 1), (1, 0)])
+
+
+def after_kernel(count, *refs):
+    refs[-1][0] = refs[count][0]
+
+
+def after(turn, arrays):
+    count = len(arrays)
+    anywhere = pl.BlockSpec(memory_space=pl.ANY)
+    scalar = pl.BlockSpec(memory_space=pltpu.SMEM)
+    *arrays, turn = pl.pallas_call(
+        functools.partial(after_kernel, count),
+        out_shape=[jax.ShapeDtypeStruct(x.shape, x.dtype) for x in (*arrays, turn)],
+        in_specs=[anywhere] * count + [scalar],
+        out_specs=[anywhere] * count + [scalar],
+        input_output_aliases={i: i for i in range(count)},
+        cost_estimate=LITTLE,
+    )(*arrays, turn)
+    return turn, arrays
 
 
 def lines(array, pairs):
@@ -72,9 +92,8 @@
     )
 
 
-def proj_kernel(count, first_ref, own_ref, other_ref, *refs):
-    del first_ref
-    pieces, out_ref = refs[:count], refs[count]
+def proj_kernel(count, turn_ref, own_ref, other_ref, *refs):
+    pieces, (out_ref, next_ref) = refs[:count], refs[count:]
     step = pl.program_id(0)
     rows = own_ref.shape[0]
     factors = jnp.concatenate([p[...] for p in pieces], axis=0)
@@ -84,6 +103,7 @@
 
     @pl.when(step == 0)
     def _():
+        next_ref[0] = turn_ref[0]
         out_ref[:rows] = top
         out_ref[rows:] = low
 
@@ -93,28 +113,31 @@
         out_ref[rows:] += low
 
 
-def proj(own, other, pieces, first, block):
+def proj(turn, own, other, pieces, first, block):
     rows, depth = own.shape[0], pieces[0].shape[1]
     steps = depth // block
     held = sum(p.shape[0] for p in pieces)
-    tokens = pl.BlockSpec((rows, block), lambda k, first: (0, first[0] * steps + k))
-    return pl.pallas_call(
+    tokens = pl.BlockSpec((rows, block), lambda k, turn: (0, turn[1] * steps + k))
+    out, turn_next = pl.pallas_call(
         functools.partial(proj_kernel, len(pieces)),
-        out_shape=jax.ShapeDtypeStruct((2 * rows, held), jnp.float32),
+        out_shape=(
+            jax.ShapeDtypeStruct((2 * rows, held), jnp.float32),
+            jax.ShapeDtypeStruct((1,), jnp.int32),
+        ),
         grid_spec=pltpu.PrefetchScalarGridSpec(
             num_scalar_prefetch=1,
             grid=(steps,),
             in_specs=[tokens, tokens]
-            + [pl.BlockSpec((p.shape[0], block), lambda k, first: (0, k)) for p in pieces],
-            out_specs=pl.BlockSpec((2 * rows, held), lambda k, first: (0, 0)),
+            + [pl.BlockSpec((p.shape[0], block), lambda k, turn: (0, k)) for p in pieces],
+            out_specs=(
+                pl.BlockSpec((2 * rows, held), lambda k, turn: (0, 0)),
+                pl.BlockSpec(memory_space=pltpu.SMEM),
+            ),
         ),
         compiler_params=pltpu.CompilerParams(vmem_limit_bytes=VMEM_LIMIT),
-        cost_estimate=pl.CostEstimate(
-            flops=4 * rows * held * depth,
-            bytes_accessed=4 * rows * depth + 2 * held * depth + 8 * rows * held,
-            transcendentals=0,
-        ),
-    )(first, own, other, *pieces)
+        cost_estimate=LITTLE,
+    )(jnp.concatenate([turn, first]), own, other, *pieces)
+    return turn_next, out
 
 
 def score_kernel(slots, spans_ref, mine_ref, theirs_ref, right_ref, out_ref):
@@ -140,9 +163,7 @@
         + [pl.BlockSpec(memory_space=pltpu.VMEM)] * 3,
         out_specs=pl.BlockSpec(memory_space=pltpu.VMEM),
         compiler_params=pltpu.CompilerParams(vmem_limit_bytes=VMEM_LIMIT),
-        cost_estimate=pl.CostEstimate(
-            flops=10 * mine.size, bytes_accessed=12 * mine.size, transcendentals=0
-        ),
+        cost_estimate=LITTLE,
     )(spans, mine, theirs, right)
 
 
@@ -161,8 +182,8 @@
     half = left.shape[1] // 2
     send = functools.partial(flip, count=count)
 
+    acts_there = send(hidden_acts, CORE)
     grads_there = send(output_grads, CORE)
-    acts_there = send(hidden_acts, CORE)
     spans_here = spans_of(bucket_ids, seq_lengths)
     spans = jnp.concatenate([spans_here, send(spans_here, CORE)], axis=1)
 
@@ -170,56 +191,113 @@
     a[0] = lax.dynamic_slice_in_dim(left, group * half, half, 1)
     c[0] = lax.dynamic_slice_in_dim(left, (1 - group) * half, half, 1)
     b[0] = query_right.reshape(local * ranks, -1)
-
-    def along_z(held):
-        held[NEAR] = send(held[0], NEAR)
-        held[ACROSS] = send(held[0], ACROSS)
-        outer = lines(held[ACROSS], [(1, 0), (2, 3)])
-        inner = lines(held[NEAR], [(2, 1), (1, 2)])
-        held[OPPOSITE] = jnp.where((z == 0) | (z == 3), outer, inner)
+    at_end = (z == 0) | (z == 3)
+
+    def outer(held):
+        return lines(held[ACROSS], [(1, 0), (2, 3)])
+
+    def inner(held):
+        return lines(held[NEAR], [(2, 1), (1, 2)])
+
+    def opposite(far, close):
+        return jnp.where(at_end, far, close)
 
     def over_x(held, code):
         held[code | COLUMN] = send(held[code], COLUMN)
-
-    over_x(a, 0)
-    along_z(a)
-    over_x(b, 0)
-    for code in (NEAR, ACROSS, OPPOSITE):
-        over_x(a, code)
-    along_z(b)
-    b[NEAR | COLUMN] = send(b[COLUMN], NEAR)
-    for code in (ACROSS, OPPOSITE):
-        over_x(b, code)
-    order = (COLUMN, NEAR, ACROSS, NEAR | COLUMN, OPPOSITE, ACROSS | COLUMN, OPPOSITE | COLUMN)
-    for code in order:
-        c[code] = swap_groups(a[code])
 
     mine = jnp.reshape(group, (1,)).astype(jnp.int32)
     zero = jnp.zeros((1,), jnp.int32)
     groups = (
-        (0, COLUMN, NEAR, ACROSS),
-        (NEAR | COLUMN, OPPOSITE, ACROSS | COLUMN, OPPOSITE | COLUMN),
-    )
-    sums = []
-    for codes in groups:
-        left_mine = proj(hidden_acts, acts_there, [a[k] for k in codes], mine, 1024)
-        left_theirs = proj(hidden_acts, acts_there, [c[k] for k in codes], 1 - mine, 1024)
-        right = proj(output_grads, grads_there, [b[k] for k in codes], zero, 1024)
-        sums.append(score(spans, left_mine, left_theirs, right))
+        (0, COLUMN, NEAR),
+        (ACROSS, OPPOSITE, ACROSS | COLUMN),
+        (NEAR | COLUMN, OPPOSITE | COLUMN),
+    )
+    block = 1024
+
+    def times_a(turn, k):
+        return proj(turn, hidden_acts, acts_there, [a[i] for i in groups[k]], mine, block)
+
+    def times_c(turn, k):
+        return proj(turn, hidden_acts, acts_there, [c[i] for i in groups[k]], 1 - mine, block)
+
+    def times_b(turn, k):
+        return proj(turn, output_grads, grads_there, [b[i] for i in groups[k]], zero, block)
+
+    over_x(a, 0)
+    a[NEAR] = send(a[0], NEAR)
+    a[ACROSS] = send(a[0], ACROSS)
+
+    turn, (a[COLUMN], a[NEAR], b_out) = after(zero, [a[COLUMN], a[NEAR], b[0]])
+    close = inner(a)
+    b[COLUMN] = send(b_out, COLUMN)
+    c[COLUMN] = swap_groups(a[COLUMN])
+    turn, a_first = times_a(turn, 0)
+
+    turn, (a[ACROSS], b[COLUMN], c[COLUMN], b_out) = after(turn, [a[ACROSS], b[COLUMN], c[COLUMN], b_out])
+    far = outer(a)
+    over_x(a, NEAR)
+    b[NEAR] = send(b_out, NEAR)
+    c[NEAR] = swap_groups(a[NEAR])
+
+    turn, (far, close, a[NEAR | COLUMN], c[NEAR], b_out) = after(
+        turn, [far, close, a[NEAR | COLUMN], c[NEAR], b_out]
+    )
+    over_x(a, ACROSS)
+    c[ACROSS] = swap_groups(a[ACROSS])
+    b[ACROSS] = send(b_out, ACROSS)
+    a[OPPOSITE] = opposite(far, close)
+    turn, c_first = times_c(turn, 0)
+
+    turn, (a[ACROSS | COLUMN], b[NEAR], c[ACROSS]) = after(
+        turn, [a[ACROSS | COLUMN], b[NEAR], c[ACROSS]]
+    )
+    over_x(a, OPPOSITE)
+    close = inner(b)
+    c[OPPOSITE] = swap_groups(a[OPPOSITE])
+    c[NEAR | COLUMN] = swap_groups(a[NEAR | COLUMN])
+    turn, b_first = times_b(turn, 0)
+
+    turn, (a[OPPOSITE | COLUMN], b[ACROSS], c[OPPOSITE], b_over) = after(
+        turn, [a[OPPOSITE | COLUMN], b[ACROSS], c[OPPOSITE], b[COLUMN]]
+    )
+    far = outer(b)
+    over_x(b, ACROSS)
+    b[NEAR | COLUMN] = send(b_over, NEAR)
+    turn, a_second = times_a(turn, 1)
+
+    turn, (b[ACROSS | COLUMN], far, close, c[NEAR | COLUMN]) = after(
+        turn, [b[ACROSS | COLUMN], far, close, c[NEAR | COLUMN]]
+    )
+    b[OPPOSITE] = opposite(far, close)
+    over_x(b, OPPOSITE)
+    for code in (ACROSS | COLUMN, OPPOSITE | COLUMN):
+        c[code] = swap_groups(a[code])
+    turn, a_third = times_a(turn, 2)
+    turn, b_second = times_b(turn, 1)
+    turn, c_second = times_c(turn, 1)
+    sums = [
+        score(spans, a_first, c_first, b_first),
+        score(spans, a_second, c_second, b_second),
+    ]
+    turn, b_third = times_b(turn, 2)
+    turn, c_third = times_c(turn, 2)
+    sums.append(score(spans, a_third, c_third, b_third))
 
     slots = bucket_ids.shape[0]
-    table = jnp.concatenate(sums, axis=1)
-    table = jnp.sum(table.reshape(2 * slots, -1, ranks), axis=2).T.reshape(-1, local, 2 * slots)
-    ours, others = table[..., :slots], table[..., slots:]
-    others = send(others, CORE)
-    place = {code: k for k, code in enumerate(groups[0] + groups[1])}
-    rows = jnp.stack(
-        [others[place[k & ~CORE]] if k & CORE else ours[place[k]] for k in range(count)]
-    )
-    for bit in (1, 2, 4, 8):
-        paired = rows.reshape(-1, 2, bit, local, slots)
-        rows = jnp.where((me & bit) != 0, paired[:, ::-1], paired).reshape(rows.shape)
-    return rows.reshape(count * local, slots)
+    ours = jnp.concatenate([x[:slots] for x in sums], axis=1)
+    others = send(jnp.concatenate([x[slots:] for x in sums], axis=1), CORE)
+    codes = jnp.array([k for codes in groups for k in codes], jnp.int32)
+    owner = jnp.concatenate([me ^ codes, me ^ CORE ^ codes])
+    query = owner[:, None] * local + jnp.arange(local, dtype=jnp.int32)[None, :]
+    query = jnp.repeat(query.reshape(-1), ranks)
+    placed = query[None, :] == jnp.arange(count * local, dtype=jnp.int32)[:, None]
+    return lax.dot_general(
+        placed.astype(jnp.float32),
+        jnp.concatenate([ours, others], axis=1),
+        (((1,), (1,)), ((), ())),
+        precision=lax.Precision.HIGHEST,
+        preferred_element_type=jnp.float32,
+    )
 
 
 def solution(mesh):

time: 307 us -> 267 us (0.87)
  waiting for transfers between devices: 187 us -> 79.2 us
  Pallas kernels: 62.6 us -> 109 us
  local copies, waits for them, and re-layouts: 7.23 us -> 27.4 us
  other arithmetic: 3.21 us -> 10.5 us
  starting transfers between devices: 42.7 us -> 36.6 us
    ppermute x16, waiting for transfers between devices: 144 us -> 61 us  [flip(): return lax.ppermute(array, 'dp', [(i, i ^ code) for i in range(count)])]
    pallas_call x6 -> x15, Pallas kernels: 59.2 us -> 104 us  [the longest x9 97.8 us: proj(): pl.pallas_call(functools.partial(proj_kernel, len(pieces)), out_shape=(ja...]
    ppermute x7, waiting for transfers between devices: 28 us -> 0.02 us  [swap_groups(): return lax.ppermute(array, 'groups', [(0, 1), (1, 0)])]
    unnamed x23 -> x71, local copies, waits for them, and re-layouts: 4.44 us -> 24.2 us
    concatenate x1 -> x10, other arithmetic: 0.01 us -> 6.47 us  [the longest x9 6.39 us: proj(): jnp.concatenate([turn, first])]
    ppermute x16, starting transfers between devices: 26.6 us -> 20.6 us  [flip(): return lax.ppermute(array, 'dp', [(i, i ^ code) for i in range(count)])]
    ppermute x4, waiting for transfers between devices: 14.6 us -> 18.2 us  [lines(): lax.ppermute(array, 'dp', [(a * 4 + rest, b * 4 + rest) for a, b in pairs...]
  transfers between devices with their start and end apart: 27 -> 27, of which waited for: 15 -> 7; matrix products, arithmetic and copies ran while one was open for 2% -> 6% of each run, Pallas kernels for 17% -> 37%
where the time goes in v2:
time: 267 us; the launch traced here: 264 us
  Pallas kernels  109 us (41%)
  waiting for transfers between devices  79.2 us (30%)
  starting transfers between devices  36.6 us (14%)
  local copies, waits for them, and re-layouts  27.4 us (10%)
  other arithmetic  10.5 us (4%)
    pallas_call x9, Pallas kernels, proj(): pl.pallas_call(functools.partial(proj_kernel, len(pieces)), out_shape=(ja...  97.8 us
    ppermute x16, waiting for transfers between devices, flip(): return lax.ppermute(array, 'dp', [(i, i ^ code) for i in range(count)])  61 us
    unnamed x71, local copies, waits for them, and re-layouts  24.2 us
    ppermute x16, starting transfers between devices, flip(): return lax.ppermute(array, 'dp', [(i, i ^ code) for i in range(count)])  20.6 us
    ppermute x4, waiting for transfers between devices, lines(): lax.ppermute(array, 'dp', [(a * 4 + rest, b * 4 + rest) for a, b in pairs...  18.2 us
    ppermute x4, starting transfers between devices, lines(): lax.ppermute(array, 'dp', [(a * 4 + rest, b * 4 + rest) for a, b in pairs...  9.98 us
    concatenate x9, other arithmetic, proj(): jnp.concatenate([turn, first])  6.39 us
    pallas_call x6, Pallas kernels, after(): pl.pallas_call(functools.partial(after_kernel, count), out_shape=[jax.Sha...  6.12 us
  transfers between devices with their start and end apart: 27, of which 7 were waited for; matrix products, arithmetic and copies ran while one was open for 6% of the time, Pallas kernels for 37%

profile of v2, /device:TPU:9, one launch (start us, length us, event | category | flops | bytes accessed | tf_op | source)
XLA Modules:
  0.0 263.9 jit_solution(14221384605357473536)
XLA Ops:
  0.7 2.9 %constant_dynamic-slice_fusion = (bf16[64,7168]{1,0:T(8,128)(2,1)}, bf16[64,7168]{1,0:T(8,128)(2,1)}) fusion(bf16[64,14336]{1,0:T(8,128)(2,1)} %bitcast.19, s32[]{:T(128)S(6)} %select_n.42, s32[]{:T(128)S(6)} %select_n.41), kind=kLoop, calls=%fused_computation.32 | loop fusion | bytes 3670024 | tf_op jit(solution)/shard_map/dynamic_slice | solution.py:192
  3.5 1.4 collective-permute-start.1
  4.9 2.3 copy.33.refs_2_
  7.2 18.1 %collective-permute-done.2.refs_1_ = bf16[64,7168]{1,0:T(8,128)(2,1)} collective-permute-done((bf16[64,7168]{1,0:T(8,128)(2,1)}, bf16[64,7168]{1,0:T(8,128)(2,1)}, u32[]{:S(2)}, u32[]{:S(2)}) %collective-permute-start.2) | collective-permute-done | bytes 917536 | tf_op jit(solution)/shard_map/ppermute | solution.py:63
  26.7 1.3 collective-permute-start.5
  28.0 2.3 collective-permute-start.4
  33.6 11.0 %shard_map.74 = (f32[1024,192]{1,0:T(8,128)S(1)}, s32[1]{0:T(128)}) custom-call(s32[2]{0:T(128)S(1)} %pad_add_fusion.5.turn_ref, bf16[512,14336]{1,0:T(8,128)(2,1)} %own_ref.17, bf16[512,14336]{1,0:T(8,128)(2,1)} %collective-permute-done.3.other_ref, bf16[64,7168]{1,0:T(8,128)(2,1)} %get-tuple-element.98.refs_0_, bf16[64,7168]{1,0:T(8,128)(2,1)S(1)} %copy-done.16, ...), custom_call_target="tpu_custom_call" | custom-call | flops 1 | bytes 1 | tf_op jit(solution)/shard_map/pallas_call | solution.py:121
  45.7 24.2 %collective-permute-done.4.refs_0_ = bf16[64,7168]{1,0:T(8,128)(2,1)S(1)} collective-permute-done((bf16[64,7168]{1,0:T(8,128)(2,1)}, bf16[64,7168]{1,0:T(8,128)(2,1)S(1)}, u32[]{:S(2)}, u32[]{:S(2)}) %collective-permute-start.4) | collective-permute-done | bytes 917536 | tf_op jit(solution)/shard_map/ppermute | solution.py:63
  73.4 3.3 %collective-permute-start.8 = (bf16[64,7168]{1,0:T(8,128)(2,1)}, bf16[64,7168]{1,0:T(8,128)(2,1)}, u32[]{:S(2)}, u32[]{:S(2)}) collective-permute-start(bf16[64,7168]{1,0:T(8,128)(2,1)} %get-tuple-element.53.refs_2_), channel_id=1, source_target_pairs={{8,4},{9,5},{10,6},{11,7},{4,8},{5,9},{6,10},{7,11},{24,20},{25,21... | collective-permute-start | bytes 2752520 | tf_op jit(solution)/shard_map/ppermute | solution.py:90
  76.7 2.5 collective-permute-start.7
  79.2 14.5 %collective-permute-done.9.refs_2_ = bf16[64,7168]{1,0:T(8,128)(2,1)} collective-permute-done((bf16[64,7168]{1,0:T(8,128)(2,1)}, bf16[64,7168]{1,0:T(8,128)(2,1)}, u32[]{:S(2)}, u32[]{:S(2)}) %collective-permute-start.9) | collective-permute-done | bytes 917536 | tf_op jit(solution)/shard_map/ppermute | solution.py:63
  96.8 17.4 %collective-permute-done.7.refs_0_ = bf16[64,7168]{1,0:T(8,128)(2,1)} collective-permute-done((bf16[64,7168]{1,0:T(8,128)(2,1)}, bf16[64,7168]{1,0:T(8,128)(2,1)}, u32[]{:S(2)}, u32[]{:S(2)}) %collective-permute-start.7) | collective-permute-done | bytes 917536 | tf_op jit(solution)/shard_map/ppermute | solution.py:90
  115.3 1.5 collective-permute-start.16
  116.8 2.2 broadcast_select_fusion.1.refs_1_
  124.8 10.9 %shard_map.77 = (f32[1024,192]{1,0:T(8,128)S(1)}, s32[1]{0:T(128)}) custom-call(s32[2]{0:T(128)S(1)} %pad_add_fusion.6.turn_ref, bf16[512,14336]{1,0:T(8,128)(2,1)} %own_ref.17, bf16[512,14336]{1,0:T(8,128)(2,1)} %collective-permute-done.3.other_ref, bf16[64,7168]{1,0:T(8,128)(2,1)S(1)} %copy-done.17, bf16[64,7168]{1,0:T(8,128)(2,1)S(1)} %copy-done.21, ...), custom_call_target="tpu_custom_call" | custom-call | flops 1 | bytes 1 | tf_op jit(solution)/shard_map/pallas_call | solution.py:121
  137.9 1.9 collective-permute-start.20
  140.5 3.4 %copy-done = bf16[512,8192]{1,0:T(8,128)(2,1)S(1)} copy-done((bf16[512,8192]{1,0:T(8,128)(2,1)S(1)}, bf16[512,8192]{1,0:T(8,128)(2,1)}, u32[]{:S(2)}) %copy-start) | copy-done | bytes 8388632
  145.1 10.9 %shard_map.79 = (f32[1024,192]{1,0:T(8,128)S(1)}, s32[1]{0:T(128)}) custom-call(s32[2]{0:T(128)S(1)} %pad_add_fusion.4.turn_ref, bf16[512,8192]{1,0:T(8,128)(2,1)S(1)} %copy-done, bf16[512,8192]{1,0:T(8,128)(2,1)} %collective-permute-done.14.other_ref, bf16[64,8192]{1,0:T(8,128)(2,1)S(1)} %bitcast.18, bf16[64,8192]{1,0:T(8,128)(2,1)S(1)} %copy-done.2, ...), custom_call_target="tpu_custom_call" | custom-call | flops 1 | bytes 1 | tf_op jit(solution)/shard_map/pallas_call | solution.py:121
  157.0 3.7 %collective-permute-done.16.refs_1_ = bf16[64,8192]{1,0:T(8,128)(2,1)} collective-permute-done((bf16[64,8192]{1,0:T(8,128)(2,1)}, bf16[64,8192]{1,0:T(8,128)(2,1)}, u32[]{:S(2)}, u32[]{:S(2)}) %collective-permute-start.16) | collective-permute-done | bytes 1048608 | tf_op jit(solution)/shard_map/ppermute | solution.py:63
  161.9 2.3 collective-permute-start.19
  165.9 6.4 %collective-permute-start = (s32[2,4]{1,0:T(2,128)S(1)}, s32[2,4]{1,0:T(2,128)S(1)}, u32[]{:S(2)}, u32[]{:S(2)}) collective-permute-start(s32[2,4]{1,0:T(2,128)S(1)} %pad_add_fusion), channel_id=1, source_target_pairs={{0,1},{1,0},{2,3},{3,2},{4,5},{5,4},{6,7},{7,6},{8,9},{9,8},{10,11... | collective-permute-start | bytes 104 | tf_op jit(solution)/shard_map/ppermute | solution.py:63
  174.1 11.0 %shard_map.82 = (f32[1024,192]{1,0:T(8,128)S(1)}, s32[1]{0:T(128)}) custom-call(s32[2]{0:T(128)S(1)} %pad_add_fusion.7.turn_ref, bf16[512,14336]{1,0:T(8,128)(2,1)} %own_ref.17, bf16[512,14336]{1,0:T(8,128)(2,1)} %collective-permute-done.3.other_ref, bf16[64,7168]{1,0:T(8,128)(2,1)S(1)} %copy-done.19, bf16[64,7168]{1,0:T(8,128)(2,1)} %broadcast_select_fusion.1.refs_1_, ...), custom_call_target="tpu_custom_call" | custom-call | flops 1 | bytes 1 | tf_op jit(solution)/shard_map/pallas_call | solution.py:121
  188.6 1.4 broadcast_select_fusion.refs_1_
  196.9 1.9 shard_map.80
  198.8 10.9 %shard_map.84 = (f32[1024,128]{1,0:T(8,128)S(1)}, s32[1]{0:T(128)}) custom-call(s32[2]{0:T(128)S(1)} %pad_add_fusion.8.turn_ref, bf16[512,14336]{1,0:T(8,128)(2,1)} %own_ref.17, bf16[512,14336]{1,0:T(8,128)(2,1)} %collective-permute-done.3.other_ref, bf16[64,7168]{1,0:T(8,128)(2,1)} %get-tuple-element.77.refs_0_, bf16[64,7168]{1,0:T(8,128)(2,1)} %get-tuple-element.80.refs_1_), custom_call_target="tpu_custom_call" | custom-call | flops 1 | bytes 1 | tf_op jit(solution)/shard_map/pallas_call | solution.py:121
  210.4 11.0 %shard_map.85 = (f32[1024,192]{1,0:T(8,128)S(1)}, s32[1]{0:T(128)}) custom-call(s32[2]{0:T(128)S(1)} %pad_add_fusion.3.turn_ref, bf16[512,8192]{1,0:T(8,128)(2,1)S(1)} %bitcast.16, bf16[512,8192]{1,0:T(8,128)(2,1)} %collective-permute-done.14.other_ref, bf16[64,8192]{1,0:T(8,128)(2,1)} %get-tuple-element.76.refs_0_, ...), custom_call_target="tpu_custom_call" | custom-call | flops 1 | bytes 1 | tf_op jit(solution)/shard_map/pallas_call | solution.py:121
  222.1 11.1 %shard_map.86 = (f32[1024,192]{1,0:T(8,128)S(1)}, s32[1]{0:T(128)}) custom-call(s32[2]{0:T(128)S(1)} %pad_add_fusion.9.turn_ref, bf16[512,14336]{1,0:T(8,128)(2,1)} %own_ref.17, bf16[512,14336]{1,0:T(8,128)(2,1)} %collective-permute-done.3.other_ref, bf16[64,7168]{1,0:T(8,128)(2,1)S(1)} %copy-done.12, bf16[64,7168]{1,0:T(8,128)(2,1)} %get-tuple-element.87.refs_1_, ...), custom_call_target="tpu_custom_call" | custom-call | flops 1 | bytes 1 | tf_op jit(solution)/shard_map/pallas_call | solution.py:121
  233.2 1.9 shard_map.87
  235.8 10.5 %shard_map.88 = (f32[1024,128]{1,0:T(8,128)S(1)}, s32[1]{0:T(128)}) custom-call(s32[2]{0:T(128)S(1)} %pad_add_fusion.2.turn_ref, bf16[512,8192]{1,0:T(8,128)(2,1)S(1)} %bitcast.16, bf16[512,8192]{1,0:T(8,128)(2,1)} %collective-permute-done.14.other_ref, bf16[64,8192]{1,0:T(8,128)(2,1)} %collective-permute-done.23.refs_0_, ...), custom_call_target="tpu_custom_call" | custom-call | flops 1 | bytes 1 | tf_op jit(solution)/shard_map/pallas_call | solution.py:121
  247.1 10.5 %shard_map.89 = (f32[1024,128]{1,0:T(8,128)S(1)}, s32[1]{0:T(128)}) custom-call(s32[2]{0:T(128)S(1)} %pad_add_fusion.10.turn_ref, bf16[512,14336]{1,0:T(8,128)(2,1)} %own_ref.17, bf16[512,14336]{1,0:T(8,128)(2,1)} %collective-permute-done.3.other_ref, bf16[64,7168]{1,0:T(8,128)(2,1)S(1)} %copy-done.14, bf16[64,7168]{1,0:T(8,128)(2,1)S(1)} %collective-permute-done.25.refs_1_), custom_call_target="tpu_custom_call" | custom-call | flops 1 | bytes 1 | tf_op jit(solution)/shard_map/pallas_call | solution.py:121
  257.6 1.5 shard_map.90
  259.1 3.1 %collective-permute-start.26 = (f32[4,512]{1,0:T(4,128)S(1)}, f32[4,512]{1,0:T(4,128)S(1)}, u32[]{:S(2)}, u32[]{:S(2)}) collective-permute-start(f32[4,512]{1,0:T(4,128)S(1)} %pad_maximum_fusion), channel_id=1, source_target_pairs={{0,1},{1,0},{2,3},{3,2},{4,5},{5,4},{6,7},{7,6},{8,9},{9,8},{10,11... | collective-permute-start | bytes 24584 | tf_op jit(solution)/shard_map/ppermute | solution.py:63
  (139 shorter events, 44.7 us)
Async XLA Ops:
  0.0 31.5 %collective-permute-start.3 = (bf16[512,14336]{1,0:T(8,128)(2,1)}, bf16[512,14336]{1,0:T(8,128)(2,1)}, u32[]{:S(2)}, u32[]{:S(2)}) collective-permute-start(bf16[512,14336]{1,0:T(8,128)(2,1)} %own_ref.17), channel_id=1, source_target_pairs={{0,1},{1,0},{2,3},{3,2},{4,5},{5,4},{6,7},{7,6},{8,9},{9,8},{10,11... | collective-permute-start | bytes 44040200 | tf_op jit(solution)/shard_map/ppermute | solution.py:63
  0.7 139.8 %collective-permute-start.14 = (bf16[512,8192]{1,0:T(8,128)(2,1)}, bf16[512,8192]{1,0:T(8,128)(2,1)}, u32[]{:S(2)}, u32[]{:S(2)}) collective-permute-start(bf16[512,8192]{1,0:T(8,128)(2,1)} %own_ref.16), channel_id=1, source_target_pairs={{0,1},{1,0},{2,3},{3,2},{4,5},{5,4},{6,7},{7,6},{8,9},{9,8},{10,11... | collective-permute-start | bytes 25165832 | tf_op jit(solution)/shard_map/ppermute | solution.py:63
  3.5 21.7 %collective-permute-start.2 = (bf16[64,7168]{1,0:T(8,128)(2,1)}, bf16[64,7168]{1,0:T(8,128)(2,1)}, u32[]{:S(2)}, u32[]{:S(2)}) collective-permute-start(bf16[64,7168]{1,0:T(8,128)(2,1)} %get-tuple-element.98.refs_0_), channel_id=1, source_target_pairs={{0,4},{1,5},{2,6},{3,7},{4,0},{5,1},{6,2},{7,3},{8,12},{9,13},{10,... | collective-permute-start | bytes 2752520 | tf_op jit(solution)/shard_map/ppermute | solution.py:63
  3.5 21.7 %collective-permute-start.1 = (bf16[64,7168]{1,0:T(8,128)(2,1)}, bf16[64,7168]{1,0:T(8,128)(2,1)S(1)}, u32[]{:S(2)}, u32[]{:S(2)}) collective-permute-start(bf16[64,7168]{1,0:T(8,128)(2,1)} %get-tuple-element.98.refs_0_), channel_id=1, source_target_pairs={{0,2},{1,3},{2,0},{3,1},{4,6},{5,7},{6,4},{7,5},{8,10},{9,11},{10,... | collective-permute-start | bytes 2752520 | tf_op jit(solution)/shard_map/ppermute | solution.py:63
  26.7 43.2 %collective-permute-start.5 = (bf16[64,8192]{1,0:T(8,128)(2,1)}, bf16[64,8192]{1,0:T(8,128)(2,1)S(1)}, u32[]{:S(2)}, u32[]{:S(2)}) collective-permute-start(bf16[64,8192]{1,0:T(8,128)(2,1)} %get-tuple-element.55.refs_3_), channel_id=1, source_target_pairs={{0,2},{1,3},{2,0},{3,1},{4,6},{5,7},{6,4},{7,5},{8,10},{9,11},{10,... | collective-permute-start | bytes 3145736 | tf_op jit(solution)/shard_map/ppermute | solution.py:63
  28.0 41.9 %collective-permute-start.4 = (bf16[64,7168]{1,0:T(8,128)(2,1)}, bf16[64,7168]{1,0:T(8,128)(2,1)S(1)}, u32[]{:S(2)}, u32[]{:S(2)}) collective-permute-start(bf16[64,7168]{1,0:T(8,128)(2,1)} %get-tuple-element.98.refs_0_), channel_id=1, source_target_pairs={{0,12},{1,13},{2,14},{3,15},{4,8},{5,9},{6,10},{7,11},{8,4},{9,5},... | collective-permute-start | bytes 2752520 | tf_op jit(solution)/shard_map/ppermute | solution.py:63
  30.3 39.7 %collective-permute-start.6 = (bf16[64,7168]{1,0:T(8,128)(2,1)}, bf16[64,7168]{1,0:T(8,128)(2,1)S(1)}, u32[]{:S(2)}, u32[]{:S(2)}) collective-permute-start(bf16[64,7168]{1,0:T(8,128)(2,1)} %get-tuple-element.52.refs_1_), channel_id=1, source_target_pairs={{0,16},{16,0},{1,17},{17,1},{2,18},{18,2},{3,19},{19,3},{4,20},{20... | collective-permute-start | bytes 2752520 | tf_op jit(solution)/shard_map/ppermute | solution.py:67
  31.5 45.2 %collective-permute-start.10 = (bf16[64,7168]{1,0:T(8,128)(2,1)}, bf16[64,7168]{1,0:T(8,128)(2,1)S(1)}, u32[]{:S(2)}, u32[]{:S(2)}) collective-permute-start(bf16[64,7168]{1,0:T(8,128)(2,1)} %get-tuple-element.53.refs_2_), channel_id=1, source_target_pairs={{0,16},{16,0},{1,17},{17,1},{2,18},{18,2},{3,19},{19,3},{4,20},{20... | collective-permute-start | bytes 2752520 | tf_op jit(solution)/shard_map/ppermute | solution.py:67
  72.9 41.3 %collective-permute-start.12 = (bf16[64,8192]{1,0:T(8,128)(2,1)}, bf16[64,8192]{1,0:T(8,128)(2,1)S(1)}, u32[]{:S(2)}, u32[]{:S(2)}) collective-permute-start(bf16[64,8192]{1,0:T(8,128)(2,1)} %get-tuple-element.58.refs_4_), channel_id=1, source_target_pairs={{0,4},{1,5},{2,6},{3,7},{4,0},{5,1},{6,2},{7,3},{8,12},{9,13},{10,... | collective-permute-start | bytes 3145736 | tf_op jit(solution)/shard_map/ppermute | solution.py:63
  73.0 20.7 %collective-permute-start.9 = (bf16[64,7168]{1,0:T(8,128)(2,1)}, bf16[64,7168]{1,0:T(8,128)(2,1)}, u32[]{:S(2)}, u32[]{:S(2)}) collective-permute-start(bf16[64,7168]{1,0:T(8,128)(2,1)} %get-tuple-element.53.refs_2_), channel_id=1, source_target_pairs={{0,2},{1,3},{2,0},{3,1},{4,6},{5,7},{6,4},{7,5},{8,10},{9,11},{10,... | collective-permute-start | bytes 2752520 | tf_op jit(solution)/shard_map/ppermute | solution.py:63
  73.4 22.3 %collective-permute-start.8 = (bf16[64,7168]{1,0:T(8,128)(2,1)}, bf16[64,7168]{1,0:T(8,128)(2,1)}, u32[]{:S(2)}, u32[]{:S(2)}) collective-permute-start(bf16[64,7168]{1,0:T(8,128)(2,1)} %get-tuple-element.53.refs_2_), channel_id=1, source_target_pairs={{8,4},{9,5},{10,6},{11,7},{4,8},{5,9},{6,10},{7,11},{24,20},{25,21... | collective-permute-start | bytes 2752520 | tf_op jit(solution)/shard_map/ppermute | solution.py:90
  76.7 37.5 %copy-start.9 = (bf16[64,7168]{1,0:T(8,128)(2,1)}, bf16[64,7168]{1,0:T(8,128)(2,1)S(1)}, u32[]{:S(2)}) copy-start(bf16[64,7168]{1,0:T(8,128)(2,1)S(1)} %collective-permute-done.10.refs_3_) | copy-start | bytes 2752516
  76.7 37.5 %collective-permute-start.7 = (bf16[64,7168]{1,0:T(8,128)(2,1)}, bf16[64,7168]{1,0:T(8,128)(2,1)}, u32[]{:S(2)}, u32[]{:S(2)}) collective-permute-start(bf16[64,7168]{1,0:T(8,128)(2,1)} %get-tuple-element.57.refs_0_), channel_id=1, source_target_pairs={{4,0},{5,1},{6,2},{7,3},{8,12},{9,13},{10,14},{11,15},{20,16},{21,... | collective-permute-start | bytes 2752520 | tf_op jit(solution)/shard_map/ppermute | solution.py:90
  93.7 26.6 %collective-permute-start.13 = (bf16[64,7168]{1,0:T(8,128)(2,1)}, bf16[64,7168]{1,0:T(8,128)(2,1)S(1)}, u32[]{:S(2)}, u32[]{:S(2)}) collective-permute-start(bf16[64,7168]{1,0:T(8,128)(2,1)} %get-tuple-element.57.refs_0_), channel_id=1, source_target_pairs={{0,16},{16,0},{1,17},{17,1},{2,18},{18,2},{3,19},{19,3},{4,20},{20... | collective-permute-start | bytes 2752520 | tf_op jit(solution)/shard_map/ppermute | solution.py:67
  95.7 41.0 %collective-permute-start.11 = (bf16[64,7168]{1,0:T(8,128)(2,1)}, bf16[64,7168]{1,0:T(8,128)(2,1)}, u32[]{:S(2)}, u32[]{:S(2)}) collective-permute-start(bf16[64,7168]{1,0:T(8,128)(2,1)} %get-tuple-element.57.refs_0_), channel_id=1, source_target_pairs={{0,2},{1,3},{2,0},{3,1},{4,6},{5,7},{6,4},{7,5},{8,10},{9,11},{10,... | collective-permute-start | bytes 2752520 | tf_op jit(solution)/shard_map/ppermute | solution.py:63
  114.2 21.6 %copy-start.4 = (bf16[64,8192]{1,0:T(8,128)(2,1)}, bf16[64,8192]{1,0:T(8,128)(2,1)S(1)}, u32[]{:S(2)}) copy-start(bf16[64,8192]{1,0:T(8,128)(2,1)S(1)} %collective-permute-done.12.refs_1_) | copy-start | bytes 3145732
  115.3 45.4 %collective-permute-start.16 = (bf16[64,8192]{1,0:T(8,128)(2,1)}, bf16[64,8192]{1,0:T(8,128)(2,1)}, u32[]{:S(2)}, u32[]{:S(2)}) collective-permute-start(bf16[64,8192]{1,0:T(8,128)(2,1)} %get-tuple-element.71), channel_id=1, source_target_pairs={{0,12},{1,13},{2,14},{3,15},{4,8},{5,9},{6,10},{7,11},{8,4},{9,5},... | collective-permute-start | bytes 3145736 | tf_op jit(solution)/shard_map/ppermute | solution.py:63
  119.1 37.9 %collective-permute-start.17 = (bf16[64,7168]{1,0:T(8,128)(2,1)}, bf16[64,7168]{1,0:T(8,128)(2,1)}, u32[]{:S(2)}, u32[]{:S(2)}) collective-permute-start(bf16[64,7168]{1,0:T(8,128)(2,1)} %broadcast_select_fusion.1.refs_1_), channel_id=1, source_target_pairs={{0,16},{16,0},{1,17},{17,1},{2,18},{18,2},{3,19},{19,3},{4,20},{20... | collective-permute-start | bytes 2752520 | tf_op jit(solution)/shard_map/ppermute | solution.py:67
  120.3 36.7 %collective-permute-start.15 = (bf16[64,7168]{1,0:T(8,128)(2,1)}, bf16[64,7168]{1,0:T(8,128)(2,1)}, u32[]{:S(2)}, u32[]{:S(2)}) collective-permute-start(bf16[64,7168]{1,0:T(8,128)(2,1)} %broadcast_select_fusion.1.refs_1_), channel_id=1, source_target_pairs={{0,2},{1,3},{2,0},{3,1},{4,6},{5,7},{6,4},{7,5},{8,10},{9,11},{10,... | collective-permute-start | bytes 2752520 | tf_op jit(solution)/shard_map/ppermute | solution.py:63
  137.9 48.6 %collective-permute-start.20 = (bf16[64,8192]{1,0:T(8,128)(2,1)}, bf16[64,8192]{1,0:T(8,128)(2,1)}, u32[]{:S(2)}, u32[]{:S(2)}) collective-permute-start(bf16[64,8192]{1,0:T(8,128)(2,1)} %get-tuple-element.67.refs_2_), channel_id=1, source_target_pairs={{8,4},{9,5},{10,6},{11,7},{4,8},{5,9},{6,10},{7,11},{24,20},{25,21... | collective-permute-start | bytes 3145736 | tf_op jit(solution)/shard_map/ppermute | solution.py:90
  145.1 20.5 %copy-start.30 = (s32[4]{0:T(128)S(1)}, s32[4]{0:T(128)}, u32[]{:S(2)}) copy-start(s32[4]{0:T(128)} %param.11) | copy-start | bytes 52
  145.1 20.7 %copy-start.31 = (s32[4]{0:T(128)S(1)}, s32[4]{0:T(128)}, u32[]{:S(2)}) copy-start(s32[4]{0:T(128)} %param.12) | copy-start | bytes 52
  161.9 24.6 %collective-permute-start.19 = (bf16[64,8192]{1,0:T(8,128)(2,1)}, bf16[64,8192]{1,0:T(8,128)(2,1)}, u32[]{:S(2)}, u32[]{:S(2)}) collective-permute-start(bf16[64,8192]{1,0:T(8,128)(2,1)} %get-tuple-element.76.refs_0_), channel_id=1, source_target_pairs={{4,0},{5,1},{6,2},{7,3},{8,12},{9,13},{10,14},{11,15},{20,16},{21,... | collective-permute-start | bytes 3145736 | tf_op jit(solution)/shard_map/ppermute | solution.py:90
  164.1 22.4 %collective-permute-start.18 = (bf16[64,8192]{1,0:T(8,128)(2,1)}, bf16[64,8192]{1,0:T(8,128)(2,1)S(1)}, u32[]{:S(2)}, u32[]{:S(2)}) collective-permute-start(bf16[64,8192]{1,0:T(8,128)(2,1)} %get-tuple-element.76.refs_0_), channel_id=1, source_target_pairs={{0,2},{1,3},{2,0},{3,1},{4,6},{5,7},{6,4},{7,5},{8,10},{9,11},{10,... | collective-permute-start | bytes 3145736 | tf_op jit(solution)/shard_map/ppermute | solution.py:63
  165.1 21.0 %collective-permute-start.21 = (bf16[64,7168]{1,0:T(8,128)(2,1)}, bf16[64,7168]{1,0:T(8,128)(2,1)S(1)}, u32[]{:S(2)}, u32[]{:S(2)}) collective-permute-start(bf16[64,7168]{1,0:T(8,128)(2,1)} %get-tuple-element.77.refs_0_), channel_id=1, source_target_pairs={{0,16},{16,0},{1,17},{17,1},{2,18},{18,2},{3,19},{19,3},{4,20},{20... | collective-permute-start | bytes 2752520 | tf_op jit(solution)/shard_map/ppermute | solution.py:67
  165.9 26.6 %collective-permute-start = (s32[2,4]{1,0:T(2,128)S(1)}, s32[2,4]{1,0:T(2,128)S(1)}, u32[]{:S(2)}, u32[]{:S(2)}) collective-permute-start(s32[2,4]{1,0:T(2,128)S(1)} %pad_add_fusion), channel_id=1, source_target_pairs={{0,1},{1,0},{2,3},{3,2},{4,5},{5,4},{6,7},{7,6},{8,9},{9,8},{10,11... | collective-permute-start | bytes 104 | tf_op jit(solution)/shard_map/ppermute | solution.py:63
  174.1 17.1 %copy-start.32 = (s32[8]{0:T(128)S(1)}, s32[8]{0:T(128)}, u32[]{:S(2)}) copy-start(s32[8]{0:T(128)} %constant.49.clone) | copy-start | bytes 100
  186.1 36.0 %collective-permute-start.22 = (bf16[64,7168]{1,0:T(8,128)(2,1)}, bf16[64,7168]{1,0:T(8,128)(2,1)}, u32[]{:S(2)}, u32[]{:S(2)}) collective-permute-start(bf16[64,7168]{1,0:T(8,128)(2,1)} %get-tuple-element.74.refs_2_), channel_id=1, source_target_pairs={{0,16},{16,0},{1,17},{17,1},{2,18},{18,2},{3,19},{19,3},{4,20},{20... | collective-permute-start | bytes 2752520 | tf_op jit(solution)/shard_map/ppermute | solution.py:67
  186.5 49.3 %collective-permute-start.23 = (bf16[64,8192]{1,0:T(8,128)(2,1)S(1)}, bf16[64,8192]{1,0:T(8,128)(2,1)}, u32[]{:S(2)}, u32[]{:S(2)}) collective-permute-start(bf16[64,8192]{1,0:T(8,128)(2,1)S(1)} %copy-done.3), channel_id=1, source_target_pairs={{0,4},{1,5},{2,6},{3,7},{4,0},{5,1},{6,2},{7,3},{8,12},{9,13},{10,... | collective-permute-start | bytes 3145736 | tf_op jit(solution)/shard_map/ppermute | solution.py:63
  190.0 45.8 %collective-permute-start.24 = (bf16[64,8192]{1,0:T(8,128)(2,1)S(1)}, bf16[64,8192]{1,0:T(8,128)(2,1)S(1)}, u32[]{:S(2)}, u32[]{:S(2)}) collective-permute-start(bf16[64,8192]{1,0:T(8,128)(2,1)S(1)} %broadcast_select_fusion.refs_1_), channel_id=1, source_target_pairs={{0,2},{1,3},{2,0},{3,1},{4,6},{5,7},{6,4},{7,5},{8,10},{9,11},{10,... | collective-permute-start | bytes 3145736 | tf_op jit(solution)/shard_map/ppermute | solution.py:63
  191.2 55.8 %collective-permute-start.25 = (bf16[64,7168]{1,0:T(8,128)(2,1)}, bf16[64,7168]{1,0:T(8,128)(2,1)S(1)}, u32[]{:S(2)}, u32[]{:S(2)}) collective-permute-start(bf16[64,7168]{1,0:T(8,128)(2,1)} %get-tuple-element.80.refs_1_), channel_id=1, source_target_pairs={{0,16},{16,0},{1,17},{17,1},{2,18},{18,2},{3,19},{19,3},{4,20},{20... | collective-permute-start | bytes 2752520 | tf_op jit(solution)/shard_map/ppermute | solution.py:67
  259.1 4.0 %collective-permute-start.26 = (f32[4,512]{1,0:T(4,128)S(1)}, f32[4,512]{1,0:T(4,128)S(1)}, u32[]{:S(2)}, u32[]{:S(2)}) collective-permute-start(f32[4,512]{1,0:T(4,128)S(1)} %pad_maximum_fusion), channel_id=1, source_target_pairs={{0,1},{1,0},{2,3},{3,2},{4,5},{5,4},{6,7},{7,6},{8,9},{9,8},{10,11... | collective-permute-start | bytes 24584 | tf_op jit(solution)/shard_map/ppermute | solution.py:63
  (30 other events, 139.7 us)

commit v3 on v2

--- a/solution.py
+++ b/solution.py
@@ -53,10 +53,9 @@
     )
 
 
-CORE, COLUMN, NEAR, ACROSS = 1, 2, 4, 12
-OPPOSITE = 8
+CORE, COLUMN, NEAR, ACROSS, OPPOSITE = 1, 2, 4, 12, 8
 LITTLE = pl.CostEstimate(flops=1, bytes_accessed=1, transcendentals=0)
-VMEM_LIMIT = 40 * 1024 * 1024
+VMEM_LIMIT = 16 * 1024 * 1024
 
 
 def flip(array, code, count):
@@ -92,7 +91,7 @@
     )
 
 
-def proj_kernel(count, turn_ref, own_ref, other_ref, *refs):
+def proj_kernel(count, at_ref, own_ref, other_ref, *refs):
     pieces, (out_ref, next_ref) = refs[:count], refs[count:]
     step = pl.program_id(0)
     rows = own_ref.shape[0]
@@ -103,7 +102,7 @@
 
     @pl.when(step == 0)
     def _():
-        next_ref[0] = turn_ref[0]
+        next_ref[0] = at_ref[0]
         out_ref[:rows] = top
         out_ref[rows:] = low
 
@@ -113,11 +112,11 @@
         out_ref[rows:] += low
 
 
-def proj(turn, own, other, pieces, first, block):
-    rows, depth = own.shape[0], pieces[0].shape[1]
+def proj(turn, tokens, rows, pieces, first, block):
+    depth = pieces[0].shape[1]
     steps = depth // block
     held = sum(p.shape[0] for p in pieces)
-    tokens = pl.BlockSpec((rows, block), lambda k, turn: (0, turn[1] * steps + k))
+    (own, own_row), (other, other_row) = tokens
     out, turn_next = pl.pallas_call(
         functools.partial(proj_kernel, len(pieces)),
         out_shape=(
@@ -127,16 +126,19 @@
         grid_spec=pltpu.PrefetchScalarGridSpec(
             num_scalar_prefetch=1,
             grid=(steps,),
-            in_specs=[tokens, tokens]
-            + [pl.BlockSpec((p.shape[0], block), lambda k, turn: (0, k)) for p in pieces],
+            in_specs=[
+                pl.BlockSpec((rows, block), lambda k, at: (at[2], at[1] * steps + k)),
+                pl.BlockSpec((rows, block), lambda k, at: (at[3], at[1] * steps + k)),
+            ]
+            + [pl.BlockSpec((p.shape[0], block), lambda k, at: (0, k)) for p in pieces],
             out_specs=(
-                pl.BlockSpec((2 * rows, held), lambda k, turn: (0, 0)),
+                pl.BlockSpec((2 * rows, held), lambda k, at: (0, 0)),
                 pl.BlockSpec(memory_space=pltpu.SMEM),
             ),
         ),
         compiler_params=pltpu.CompilerParams(vmem_limit_bytes=VMEM_LIMIT),
         cost_estimate=LITTLE,
-    )(jnp.concatenate([turn, first]), own, other, *pieces)
+    )(jnp.concatenate([turn, first, own_row, other_row]), own, other, *pieces)
     return turn_next, out
 
 
@@ -183,110 +185,110 @@
     send = functools.partial(flip, count=count)
 
     acts_there = send(hidden_acts, CORE)
-    grads_there = send(output_grads, CORE)
+    pairs = [[i, i ^ CORE] for i in range(0, count, 2)]
+    grads_both = lax.all_gather(output_grads, "dp", axis_index_groups=pairs, axis=0, tiled=True)
     spans_here = spans_of(bucket_ids, seq_lengths)
     spans = jnp.concatenate([spans_here, send(spans_here, CORE)], axis=1)
 
     a, b, c = {}, {}, {}
-    a[0] = lax.dynamic_slice_in_dim(left, group * half, half, 1)
-    c[0] = lax.dynamic_slice_in_dim(left, (1 - group) * half, half, 1)
-    b[0] = query_right.reshape(local * ranks, -1)
+    a["own"] = lax.dynamic_slice_in_dim(left, group * half, half, 1)
+    c["own"] = lax.dynamic_slice_in_dim(left, (1 - group) * half, half, 1)
+    b["own"] = query_right.reshape(local * ranks, -1)
     at_end = (z == 0) | (z == 3)
 
-    def outer(held):
-        return lines(held[ACROSS], [(1, 0), (2, 3)])
-
-    def inner(held):
-        return lines(held[NEAR], [(2, 1), (1, 2)])
-
-    def opposite(far, close):
-        return jnp.where(at_end, far, close)
-
-    def over_x(held, code):
-        held[code | COLUMN] = send(held[code], COLUMN)
-
+    def near(piece):
+        return send(piece, NEAR)
+
+    def middle(piece):
+        return lines(piece, [(1, 2), (2, 1)])
+
+    def outward(piece):
+        return lines(piece, [(1, 0), (2, 3)])
+
+    def over_x(piece):
+        return send(piece, COLUMN)
+
+    core = (me & CORE).reshape(1).astype(jnp.int32)
     mine = jnp.reshape(group, (1,)).astype(jnp.int32)
     zero = jnp.zeros((1,), jnp.int32)
-    groups = (
-        (0, COLUMN, NEAR),
-        (ACROSS, OPPOSITE, ACROSS | COLUMN),
-        (NEAR | COLUMN, OPPOSITE | COLUMN),
-    )
+    acts = ((hidden_acts, zero), (acts_there, zero))
+    grads = ((grads_both, core), (grads_both, 1 - core))
+    groups = (("own", "x", "n", "f"), ("xf", "g", "xn", "xg"))
+    tokens_here = hidden_acts.shape[0]
     block = 1024
 
     def times_a(turn, k):
-        return proj(turn, hidden_acts, acts_there, [a[i] for i in groups[k]], mine, block)
+        return proj(turn, acts, tokens_here, [a[i] for i in groups[k]], mine, block)
 
     def times_c(turn, k):
-        return proj(turn, hidden_acts, acts_there, [c[i] for i in groups[k]], 1 - mine, block)
+        return proj(turn, acts, tokens_here, [c[i] for i in groups[k]], 1 - mine, block)
 
     def times_b(turn, k):
-        return proj(turn, output_grads, grads_there, [b[i] for i in groups[k]], zero, block)
-
-    over_x(a, 0)
-    a[NEAR] = send(a[0], NEAR)
-    a[ACROSS] = send(a[0], ACROSS)
-
-    turn, (a[COLUMN], a[NEAR], b_out) = after(zero, [a[COLUMN], a[NEAR], b[0]])
-    close = inner(a)
-    b[COLUMN] = send(b_out, COLUMN)
-    c[COLUMN] = swap_groups(a[COLUMN])
+        return proj(turn, grads, tokens_here, [b[i] for i in groups[k]], zero, block)
+
+    a["x"] = over_x(a["own"])
+    a["n"] = near(a["own"])
+    a_mid = middle(a["own"])
+
+    turn, (a["x"], a["n"], a_mid) = after(zero, [a["x"], a["n"], a_mid])
+    a_in = middle(a["n"])
+    a_out = outward(a_mid)
+    a["xn"] = over_x(a["n"])
+    c["x"] = swap_groups(a["x"])
+
+    turn, (a_in, a_out, a["xn"], c["x"], b_own) = after(turn, [a_in, a_out, a["xn"], c["x"], b["own"]])
+    a["f"] = jnp.where(at_end, a_out, a_mid)
+    a_last = outward(a_in)
+    a["xf"] = over_x(a["f"])
+    c["n"] = swap_groups(a["n"])
+    b_mid = middle(b_own)
     turn, a_first = times_a(turn, 0)
 
-    turn, (a[ACROSS], b[COLUMN], c[COLUMN], b_out) = after(turn, [a[ACROSS], b[COLUMN], c[COLUMN], b_out])
-    far = outer(a)
-    over_x(a, NEAR)
-    b[NEAR] = send(b_out, NEAR)
-    c[NEAR] = swap_groups(a[NEAR])
-
-    turn, (far, close, a[NEAR | COLUMN], c[NEAR], b_out) = after(
-        turn, [far, close, a[NEAR | COLUMN], c[NEAR], b_out]
-    )
-    over_x(a, ACROSS)
-    c[ACROSS] = swap_groups(a[ACROSS])
-    b[ACROSS] = send(b_out, ACROSS)
-    a[OPPOSITE] = opposite(far, close)
+    turn, (a_last, a["xf"], c["n"], b_mid, b_own) = after(turn, [a_last, a["xf"], c["n"], b_mid, b_own])
+    a["g"] = jnp.where(at_end, a_last, a_in)
+    b["n"] = near(b_own)
+    b["x"] = over_x(b_own)
+    c["f"] = swap_groups(a["f"])
+
+    turn, (b["n"], b["x"], c["f"]) = after(turn, [b["n"], b["x"], c["f"]])
+    b_in = middle(b["n"])
+    b_out = outward(b_mid)
+    a["xg"] = over_x(a["g"])
+    c["g"] = swap_groups(a["g"])
     turn, c_first = times_c(turn, 0)
 
-    turn, (a[ACROSS | COLUMN], b[NEAR], c[ACROSS]) = after(
-        turn, [a[ACROSS | COLUMN], b[NEAR], c[ACROSS]]
-    )
-    over_x(a, OPPOSITE)
-    close = inner(b)
-    c[OPPOSITE] = swap_groups(a[OPPOSITE])
-    c[NEAR | COLUMN] = swap_groups(a[NEAR | COLUMN])
+    turn, (b_in, b_out, a["xg"], c["g"]) = after(turn, [b_in, b_out, a["xg"], c["g"]])
+    b["f"] = jnp.where(at_end, b_out, b_mid)
+    b_last = outward(b_in)
+    b["xf"] = over_x(b["f"])
+    c["xf"] = swap_groups(a["xf"])
     turn, b_first = times_b(turn, 0)
 
-    turn, (a[OPPOSITE | COLUMN], b[ACROSS], c[OPPOSITE], b_over) = after(
-        turn, [a[OPPOSITE | COLUMN], b[ACROSS], c[OPPOSITE], b[COLUMN]]
-    )
-    far = outer(b)
-    over_x(b, ACROSS)
-    b[NEAR | COLUMN] = send(b_over, NEAR)
+    turn, (b_last, b["xf"], c["xf"]) = after(turn, [b_last, b["xf"], c["xf"]])
+    b["g"] = jnp.where(at_end, b_last, b_in)
+    b["xg"] = over_x(b["g"])
+    b["xn"] = near(b["x"])
+    c["xn"] = swap_groups(a["xn"])
     turn, a_second = times_a(turn, 1)
 
-    turn, (b[ACROSS | COLUMN], far, close, c[NEAR | COLUMN]) = after(
-        turn, [b[ACROSS | COLUMN], far, close, c[NEAR | COLUMN]]
-    )
-    b[OPPOSITE] = opposite(far, close)
-    over_x(b, OPPOSITE)
-    for code in (ACROSS | COLUMN, OPPOSITE | COLUMN):
-        c[code] = swap_groups(a[code])
-    turn, a_third = times_a(turn, 2)
+    turn, (b["xg"], b["xn"], c["xn"], c["g"]) = after(turn, [b["xg"], b["xn"], c["xn"], c["g"]])
+    split = c["g"].shape[0] // 2
+    c_top = over_x(c["g"][:split])
+    c_low = swap_groups(a["xg"][split:])
+    sums = [score(spans, a_first, c_first, b_first)]
     turn, b_second = times_b(turn, 1)
+    groups = (groups[0], ("xf", "g", "xn", "top", "low"))
+    c["top"], c["low"] = c_top, c_low
     turn, c_second = times_c(turn, 1)
-    sums = [
-        score(spans, a_first, c_first, b_first),
-        score(spans, a_second, c_second, b_second),
-    ]
-    turn, b_third = times_b(turn, 2)
-    turn, c_third = times_c(turn, 2)
-    sums.append(score(spans, a_third, c_third, b_third))
+    sums.append(score(spans, a_second, c_second, b_second))
 
     slots = bucket_ids.shape[0]
     ours = jnp.concatenate([x[:slots] for x in sums], axis=1)
     others = send(jnp.concatenate([x[slots:] for x in sums], axis=1), CORE)
-    codes = jnp.array([k for codes in groups for k in codes], jnp.int32)
+    f_code = jnp.where(at_end, OPPOSITE, ACROSS)
+    g_code = jnp.where(at_end, ACROSS, OPPOSITE)
+    codes = [0, COLUMN, NEAR, f_code, f_code | COLUMN, g_code, NEAR | COLUMN, g_code | COLUMN]
+    codes = jnp.stack([jnp.asarray(code, jnp.int32) for code in codes])
     owner = jnp.concatenate([me ^ codes, me ^ CORE ^ codes])
     query = owner[:, None] * local + jnp.arange(local, dtype=jnp.int32)[None, :]
     query = jnp.repeat(query.reshape(-1), ranks)

time: 267 us -> 266 us (level)
  Pallas kernels: 109 us -> 72.5 us
  local copies, waits for them, and re-layouts: 27.4 us -> 61.9 us
  waiting for transfers between devices: 79.2 us -> 47.6 us
  starting transfers between devices: 36.6 us -> 53.2 us
  between operations: 0.37 us -> 13.9 us
    ppermute x16 -> x14, waiting for transfers between devices: 61 us -> 18.7 us  [flip(): return lax.ppermute(array, 'dp', [(i, i ^ code) for i in range(count)])]
    pallas_call x9 -> x6, Pallas kernels: 97.8 us -> 61.4 us  [proj(): pl.pallas_call(functools.partial(proj_kernel, len(pieces)), out_shape=(ja...]
    unnamed x71 -> x103, local copies, waits for them, and re-layouts: 24.2 us -> 57.2 us
    ppermute x4 -> x8, starting transfers between devices: 9.98 us -> 23.6 us  [lines(): lax.ppermute(array, 'dp', [(a * 4 + rest, b * 4 + rest) for a, b in pairs...]
    ppermute x7, waiting for transfers between devices: 0.02 us -> 11.5 us  [swap_groups(): return lax.ppermute(array, 'groups', [(0, 1), (1, 0)])]
    select_n x2 -> x4, other arithmetic: 3.59 us -> 7.24 us  [the longest x1 2.33 us: relay(): b['f'] = jnp.where(at_end, b_out, b_mid)]
    ppermute x16 -> x14, starting transfers between devices: 20.6 us -> 22.9 us  [flip(): return lax.ppermute(array, 'dp', [(i, i ^ code) for i in range(count)])]
    concatenate x9 -> x6, other arithmetic: 6.39 us -> 4.27 us  [proj(): jnp.concatenate([turn, first, own_row, other_row])]
  transfers between devices with their start and end apart: 27 -> 30, of which waited for: 7 -> 9; matrix products, arithmetic and copies ran while one was open for 6% -> 7% of each run, Pallas kernels for 37% -> 23%
where the time goes in v3:
time: 266 us; the launch traced here: 262 us
  Pallas kernels  72.5 us (27%)
  local copies, waits for them, and re-layouts  61.9 us (23%)
  starting transfers between devices  53.2 us (20%)
  waiting for transfers between devices  47.6 us (18%)
  between operations  13.9 us (5%)
  other arithmetic  11.9 us (4%)
    pallas_call x6, Pallas kernels, proj(): pl.pallas_call(functools.partial(proj_kernel, len(pieces)), out_shape=(ja...  61.4 us
    unnamed x103, local copies, waits for them, and re-layouts  57.2 us
    ppermute x8, starting transfers between devices, lines(): lax.ppermute(array, 'dp', [(a * 4 + rest, b * 4 + rest) for a, b in pairs...  23.6 us
    ppermute x14, starting transfers between devices, flip(): return lax.ppermute(array, 'dp', [(i, i ^ code) for i in range(count)])  22.9 us
    ppermute x14, waiting for transfers between devices, flip(): return lax.ppermute(array, 'dp', [(i, i ^ code) for i in range(count)])  18.7 us
    ppermute x8, waiting for transfers between devices, lines(): lax.ppermute(array, 'dp', [(a * 4 + rest, b * 4 + rest) for a, b in pairs...  17.4 us
    ppermute x7, waiting for transfers between devices, swap_groups(): return lax.ppermute(array, 'groups', [(0, 1), (1, 0)])  11.5 us
    pallas_call x7, Pallas kernels, after(): pl.pallas_call(functools.partial(after_kernel, count), out_shape=[jax.Sha...  7.55 us
  transfers between devices with their start and end apart: 30, of which 9 were waited for; matrix products, arithmetic and copies ran while one was open for 7% of the time, Pallas kernels for 23%

profile of v3, /device:TPU:9, one launch (start us, length us, event | category | flops | bytes accessed | tf_op | source)
XLA Modules:
  0.0 261.8 jit_solution(12311591607211244226)
XLA Ops:
  7.3 2.5 constant_dynamic-slice_fusion
  11.2 4.3 %collective-permute-start.3 = (bf16[64,7168]{1,0:T(8,128)(2,1)S(1)}, bf16[64,7168]{1,0:T(8,128)(2,1)}, u32[]{:S(2)}, u32[]{:S(2)}) collective-permute-start(bf16[64,7168]{1,0:T(8,128)(2,1)S(1)} %get-tuple-element.96.refs_0_), channel_id=1, source_target_pairs={{4,8},{5,9},{6,10},{7,11},{8,4},{9,5},{10,6},{11,7},{20,24},{21,25... | collective-permute-start | bytes 2752520 | tf_op jit(solution)/shard_map/ppermute | solution.py:89
  16.5 14.6 %collective-permute-done.1.refs_0_ = bf16[64,7168]{1,0:T(8,128)(2,1)S(1)} collective-permute-done((bf16[64,7168]{1,0:T(8,128)(2,1)S(1)}, bf16[64,7168]{1,0:T(8,128)(2,1)S(1)}, u32[]{:S(2)}, u32[]{:S(2)}) %collective-permute-start.1) | collective-permute-done | bytes 917536 | tf_op jit(solution)/shard_map/ppermute | solution.py:62
  32.0 3.0 %collective-permute-done.3.refs_2_ = bf16[64,7168]{1,0:T(8,128)(2,1)} collective-permute-done((bf16[64,7168]{1,0:T(8,128)(2,1)S(1)}, bf16[64,7168]{1,0:T(8,128)(2,1)}, u32[]{:S(2)}, u32[]{:S(2)}) %collective-permute-start.3) | collective-permute-done | bytes 917536 | tf_op jit(solution)/shard_map/ppermute | solution.py:89
  35.6 3.1 %collective-permute-start.4 = (bf16[64,7168]{1,0:T(8,128)(2,1)}, bf16[64,7168]{1,0:T(8,128)(2,1)}, u32[]{:S(2)}, u32[]{:S(2)}) collective-permute-start(bf16[64,7168]{1,0:T(8,128)(2,1)} %get-tuple-element.50.refs_2_), channel_id=1, source_target_pairs={{4,8},{5,9},{6,10},{7,11},{8,4},{9,5},{10,6},{11,7},{20,24},{21,25... | collective-permute-start | bytes 2752520 | tf_op jit(solution)/shard_map/ppermute | solution.py:89
  39.0 2.2 collective-permute-start.5
  43.4 14.4 %collective-permute-done.4.refs_0_ = bf16[64,7168]{1,0:T(8,128)(2,1)} collective-permute-done((bf16[64,7168]{1,0:T(8,128)(2,1)}, bf16[64,7168]{1,0:T(8,128)(2,1)}, u32[]{:S(2)}, u32[]{:S(2)}) %collective-permute-start.4) | collective-permute-done | bytes 917536 | tf_op jit(solution)/shard_map/ppermute | solution.py:89
  59.0 1.5 collective-permute-done.7.refs_3_
  62.6 1.7 collective-permute-start.9
  64.3 2.5 collective-permute-start.12
  70.1 5.2 %copy-done.2 = bf16[512,14336]{1,0:T(8,128)(2,1)S(1)} copy-done((bf16[512,14336]{1,0:T(8,128)(2,1)S(1)}, bf16[512,14336]{1,0:T(8,128)(2,1)}, u32[]{:S(2)}) %copy-start.2) | copy-done | bytes 14680088
  78.9 9.8 %shard_map.66 = (f32[1024,256]{1,0:T(8,128)S(1)}, s32[1]{0:T(128)}) custom-call(s32[4]{0:T(128)S(1)} %pad_add_fusion.5.at_ref, bf16[512,14336]{1,0:T(8,128)(2,1)S(1)} %copy-done.2, bf16[512,14336]{1,0:T(8,128)(2,1)} %collective-permute-done.8.other_ref, bf16[64,7168]{1,0:T(8,128)(2,1)S(1)} %copy-done.35, bf16[64,7168]{1,0:T(8,128)(2,1)S(1)} %copy-done.30, ...), custom_call_target="tpu_custom_call" | custom-call | flops 1 | bytes 1 | tf_op jit(solution)/shard_map/pallas_call | solution.py:120
  94.4 4.3 %collective-permute-start.17 = (bf16[64,8192]{1,0:T(8,128)(2,1)}, bf16[64,8192]{1,0:T(8,128)(2,1)}, u32[]{:S(2)}, u32[]{:S(2)}) collective-permute-start(bf16[64,8192]{1,0:T(8,128)(2,1)} %get-tuple-element.68), channel_id=1, source_target_pairs={{4,0},{5,1},{6,2},{7,3},{8,12},{9,13},{10,14},{11,15},{20,16},{21,... | collective-permute-start | bytes 3145736 | tf_op jit(solution)/shard_map/ppermute | solution.py:89
  98.6 10.0 %collective-permute-done.15.refs_2_ = bf16[64,7168]{1,0:T(8,128)(2,1)S(1)} collective-permute-done((bf16[64,7168]{1,0:T(8,128)(2,1)S(1)}, bf16[64,7168]{1,0:T(8,128)(2,1)S(1)}, u32[]{:S(2)}, u32[]{:S(2)}) %collective-permute-start.15) | collective-permute-done | bytes 917536 | tf_op jit(solution)/shard_map/ppermute | solution.py:66
  108.7 2.5 collective-permute-done.13.refs_0_
  113.7 2.2 collective-permute-start.16
  119.7 5.2 %copy-done.3 = bf16[512,14336]{1,0:T(8,128)(2,1)S(1)} copy-done((bf16[512,14336]{1,0:T(8,128)(2,1)S(1)}, bf16[512,14336]{1,0:T(8,128)(2,1)}, u32[]{:S(2)}) %copy-start.3) | copy-done | bytes 14680088
  129.5 9.8 %shard_map.69 = (f32[1024,256]{1,0:T(8,128)S(1)}, s32[1]{0:T(128)}) custom-call(s32[4]{0:T(128)S(1)} %pad_add_fusion.4.at_ref, bf16[512,14336]{1,0:T(8,128)(2,1)S(1)} %copy-done.3, bf16[512,14336]{1,0:T(8,128)(2,1)} %collective-permute-done.8.other_ref, bf16[64,7168]{1,0:T(8,128)(2,1)S(1)} %copy-done.33, bf16[64,7168]{1,0:T(8,128)(2,1)S(1)} %copy-done.20, ...), custom_call_target="tpu_custom_call" | custom-call | flops 1 | bytes 1 | tf_op jit(solution)/shard_map/pallas_call | solution.py:120
  142.8 2.3 broadcast_select_fusion.1.refs_3_
  145.1 3.4 %collective-permute-start.20 = (bf16[64,8192]{1,0:T(8,128)(2,1)}, bf16[64,8192]{1,0:T(8,128)(2,1)}, u32[]{:S(2)}, u32[]{:S(2)}) collective-permute-start(bf16[64,8192]{1,0:T(8,128)(2,1)} %get-tuple-element.75), channel_id=1, source_target_pairs={{4,0},{5,1},{6,2},{7,3},{8,12},{9,13},{10,14},{11,15},{20,16},{21,... | collective-permute-start | bytes 3145736 | tf_op jit(solution)/shard_map/ppermute | solution.py:89
  150.3 5.8 %copy-done = bf16[1024,8192]{1,0:T(8,128)(2,1)S(1)} copy-done((bf16[1024,8192]{1,0:T(8,128)(2,1)S(1)}, bf16[1024,8192]{1,0:T(8,128)(2,1)}, u32[]{:S(2)}) %copy-start) | copy-done | bytes 16777240
  158.5 10.2 %shard_map.71 = (f32[1024,256]{1,0:T(8,128)S(1)}, s32[1]{0:T(128)}) custom-call(s32[4]{0:T(128)S(1)} %fusion.8.at_ref, bf16[1024,8192]{1,0:T(8,128)(2,1)S(1)} %copy-done, bf16[1024,8192]{1,0:T(8,128)(2,1)S(1)} %copy-done, bf16[64,8192]{1,0:T(8,128)(2,1)S(1)} %bitcast.23, bf16[64,8192]{1,0:T(8,128)(2,1)S(1)} %copy-done.14, bf16[64,8192]{1,0:T(8,128)(2,1)S(1)} %copy-done.12, ...), custom_call_target="tpu_custom_call" | custom-call | flops 1 | bytes 1 | tf_op jit(solution)/shard_map/pallas_call | solution.py:120
  171.9 2.3 broadcast_select_fusion.refs_1_
  176.3 14.4 %collective-permute-start = (s32[2,4]{1,0:T(2,128)S(1)}, s32[2,4]{1,0:T(2,128)S(1)}, u32[]{:S(2)}, u32[]{:S(2)}) collective-permute-start(s32[2,4]{1,0:T(2,128)S(1)} %pad_add_fusion), channel_id=1, source_target_pairs={{0,1},{1,0},{2,3},{3,2},{4,5},{5,4},{6,7},{7,6},{8,9},{9,8},{10,11... | collective-permute-start | bytes 104 | tf_op jit(solution)/shard_map/ppermute | solution.py:62
  192.7 5.2 %copy-done.4 = bf16[512,14336]{1,0:T(8,128)(2,1)S(1)} copy-done((bf16[512,14336]{1,0:T(8,128)(2,1)S(1)}, bf16[512,14336]{1,0:T(8,128)(2,1)}, u32[]{:S(2)}) %copy-start.4) | copy-done | bytes 14680088
  201.4 9.8 %shard_map.74 = (f32[1024,256]{1,0:T(8,128)S(1)}, s32[1]{0:T(128)}) custom-call(s32[4]{0:T(128)S(1)} %pad_add_fusion.3.at_ref, bf16[512,14336]{1,0:T(8,128)(2,1)S(1)} %copy-done.4, bf16[512,14336]{1,0:T(8,128)(2,1)} %collective-permute-done.8.other_ref, bf16[64,7168]{1,0:T(8,128)(2,1)S(1)} %copy-done.24, bf16[64,7168]{1,0:T(8,128)(2,1)S(1)} %copy-done.26, ...), custom_call_target="tpu_custom_call" | custom-call | flops 1 | bytes 1 | tf_op jit(solution)/shard_map/pallas_call | solution.py:120
  214.6 1.7 collective-permute-start.26
  220.1 1.7 shard_map.72
  222.5 5.8 %copy-done.1 = bf16[1024,8192]{1,0:T(8,128)(2,1)S(1)} copy-done((bf16[1024,8192]{1,0:T(8,128)(2,1)S(1)}, bf16[1024,8192]{1,0:T(8,128)(2,1)}, u32[]{:S(2)}) %copy-start.1) | copy-done | bytes 16777240
  228.3 11.7 %shard_map.76 = (f32[1024,256]{1,0:T(8,128)S(1)}, s32[1]{0:T(128)}) custom-call(s32[4]{0:T(128)S(1)} %fusion.10.at_ref, bf16[1024,8192]{1,0:T(8,128)(2,1)S(1)} %copy-done.1, bf16[1024,8192]{1,0:T(8,128)(2,1)S(1)} %copy-done.1, bf16[64,8192]{1,0:T(8,128)(2,1)S(1)} %copy-done.10, bf16[64,8192]{1,0:T(8,128)(2,1)} %broadcast_select_fusion.refs_1_, ...), custom_call_target="tpu_custom_call" | custom-call | flops 1 | bytes 1 | tf_op jit(solution)/shard_map/pallas_call | solution.py:120
  240.8 10.0 %shard_map.77 = (f32[1024,256]{1,0:T(8,128)S(1)}, s32[1]{0:T(128)}) custom-call(s32[4]{0:T(128)S(1)} %pad_add_fusion.2.at_ref, bf16[512,14336]{1,0:T(8,128)(2,1)S(1)} %bitcast.21, bf16[512,14336]{1,0:T(8,128)(2,1)} %collective-permute-done.8.other_ref, bf16[64,7168]{1,0:T(8,128)(2,1)} %get-tuple-element.90.refs_0_, bf16[64,7168]{1,0:T(8,128)(2,1)S(1)} %copy-done.6, ...), custom_call_target="tpu_custom_call" | custom-call | flops 1 | bytes 1 | tf_op jit(solution)/shard_map/pallas_call | solution.py:120
  250.9 1.8 shard_map.78
  (177 shorter events, 63.0 us)
Async XLA Ops:
  6.5 35.9 %copy-start.15 = (bf16[4,16,8192]{2,1,0:T(8,128)(2,1)S(1)}, bf16[4,16,8192]{2,1,0:T(8,128)(2,1)}, u32[]{:S(2)}) copy-start(bf16[4,16,8192]{2,1,0:T(8,128)(2,1)} %param.9) | copy-start | bytes 3145732
  6.5 143.7 %all-gather.2.cloned.1.call-start = ((), (), s32[]{:S(2)}) async-start(), calls=%async_computation | async-start | bytes 25165824 | tf_op jit(solution)/shard_map/all_gather | solution.py:189
  6.5 63.6 %collective-permute-start.8 = (bf16[512,14336]{1,0:T(8,128)(2,1)}, bf16[512,14336]{1,0:T(8,128)(2,1)}, u32[]{:S(2)}, u32[]{:S(2)}) collective-permute-start(bf16[512,14336]{1,0:T(8,128)(2,1)} %own_ref.7), channel_id=1, source_target_pairs={{0,1},{1,0},{2,3},{3,2},{4,5},{5,4},{6,7},{7,6},{8,9},{9,8},{10,11... | collective-permute-start | bytes 44040200 | tf_op jit(solution)/shard_map/ppermute | solution.py:62
  9.8 21.3 %collective-permute-start.1 = (bf16[64,7168]{1,0:T(8,128)(2,1)S(1)}, bf16[64,7168]{1,0:T(8,128)(2,1)S(1)}, u32[]{:S(2)}, u32[]{:S(2)}) collective-permute-start(bf16[64,7168]{1,0:T(8,128)(2,1)S(1)} %get-tuple-element.96.refs_0_), channel_id=1, source_target_pairs={{0,2},{1,3},{2,0},{3,1},{4,6},{5,7},{6,4},{7,5},{8,10},{9,11},{10,... | collective-permute-start | bytes 2752520 | tf_op jit(solution)/shard_map/ppermute | solution.py:62
  11.0 21.0 %collective-permute-start.2 = (bf16[64,7168]{1,0:T(8,128)(2,1)S(1)}, bf16[64,7168]{1,0:T(8,128)(2,1)S(1)}, u32[]{:S(2)}, u32[]{:S(2)}) collective-permute-start(bf16[64,7168]{1,0:T(8,128)(2,1)S(1)} %get-tuple-element.96.refs_0_), channel_id=1, source_target_pairs={{0,4},{1,5},{2,6},{3,7},{4,0},{5,1},{6,2},{7,3},{8,12},{9,13},{10,... | collective-permute-start | bytes 2752520 | tf_op jit(solution)/shard_map/ppermute | solution.py:62
  11.2 23.9 %collective-permute-start.3 = (bf16[64,7168]{1,0:T(8,128)(2,1)S(1)}, bf16[64,7168]{1,0:T(8,128)(2,1)}, u32[]{:S(2)}, u32[]{:S(2)}) collective-permute-start(bf16[64,7168]{1,0:T(8,128)(2,1)S(1)} %get-tuple-element.96.refs_0_), channel_id=1, source_target_pairs={{4,8},{5,9},{6,10},{7,11},{8,4},{9,5},{10,6},{11,7},{20,24},{21,25... | collective-permute-start | bytes 2752520 | tf_op jit(solution)/shard_map/ppermute | solution.py:89
  35.6 22.2 %collective-permute-start.4 = (bf16[64,7168]{1,0:T(8,128)(2,1)}, bf16[64,7168]{1,0:T(8,128)(2,1)}, u32[]{:S(2)}, u32[]{:S(2)}) collective-permute-start(bf16[64,7168]{1,0:T(8,128)(2,1)} %get-tuple-element.50.refs_2_), channel_id=1, source_target_pairs={{4,8},{5,9},{6,10},{7,11},{8,4},{9,5},{10,6},{11,7},{20,24},{21,25... | collective-permute-start | bytes 2752520 | tf_op jit(solution)/shard_map/ppermute | solution.py:89
  38.6 20.4 %collective-permute-start.6 = (bf16[64,7168]{1,0:T(8,128)(2,1)}, bf16[64,7168]{1,0:T(8,128)(2,1)S(1)}, u32[]{:S(2)}, u32[]{:S(2)}) collective-permute-start(bf16[64,7168]{1,0:T(8,128)(2,1)} %get-tuple-element.50.refs_2_), channel_id=1, source_target_pairs={{0,2},{1,3},{2,0},{3,1},{4,6},{5,7},{6,4},{7,5},{8,10},{9,11},{10,... | collective-permute-start | bytes 2752520 | tf_op jit(solution)/shard_map/ppermute | solution.py:62
  39.0 20.0 %collective-permute-start.5 = (bf16[64,7168]{1,0:T(8,128)(2,1)}, bf16[64,7168]{1,0:T(8,128)(2,1)}, u32[]{:S(2)}, u32[]{:S(2)}) collective-permute-start(bf16[64,7168]{1,0:T(8,128)(2,1)} %get-tuple-element.51), channel_id=1, source_target_pairs={{4,0},{5,1},{6,2},{7,3},{8,12},{9,13},{10,14},{11,15},{20,16},{21,... | collective-permute-start | bytes 2752520 | tf_op jit(solution)/shard_map/ppermute | solution.py:89
  41.2 19.3 %collective-permute-start.7 = (bf16[64,7168]{1,0:T(8,128)(2,1)}, bf16[64,7168]{1,0:T(8,128)(2,1)S(1)}, u32[]{:S(2)}, u32[]{:S(2)}) collective-permute-start(bf16[64,7168]{1,0:T(8,128)(2,1)} %get-tuple-element.52.refs_1_), channel_id=1, source_target_pairs={{0,16},{16,0},{1,17},{17,1},{2,18},{18,2},{3,19},{19,3},{4,20},{20... | collective-permute-start | bytes 2752520 | tf_op jit(solution)/shard_map/ppermute | solution.py:66
  57.7 32.0 %collective-permute-start.11 = (bf16[64,7168]{1,0:T(8,128)(2,1)}, bf16[64,7168]{1,0:T(8,128)(2,1)S(1)}, u32[]{:S(2)}, u32[]{:S(2)}) collective-permute-start(bf16[64,7168]{1,0:T(8,128)(2,1)} %get-tuple-element.50.refs_2_), channel_id=1, source_target_pairs={{0,16},{16,0},{1,17},{17,1},{2,18},{18,2},{3,19},{19,3},{4,20},{20... | collective-permute-start | bytes 2752520 | tf_op jit(solution)/shard_map/ppermute | solution.py:66
  62.6 27.1 %collective-permute-start.9 = (bf16[64,7168]{1,0:T(8,128)(2,1)}, bf16[64,7168]{1,0:T(8,128)(2,1)S(1)}, u32[]{:S(2)}, u32[]{:S(2)}) collective-permute-start(bf16[64,7168]{1,0:T(8,128)(2,1)} %get-tuple-element.57), channel_id=1, source_target_pairs={{4,0},{5,1},{6,2},{7,3},{8,12},{9,13},{10,14},{11,15},{20,16},{21,... | collective-permute-start | bytes 2752520 | tf_op jit(solution)/shard_map/ppermute | solution.py:89
  64.3 26.3 %collective-permute-start.12 = (bf16[64,8192]{1,0:T(8,128)(2,1)}, bf16[64,8192]{1,0:T(8,128)(2,1)}, u32[]{:S(2)}, u32[]{:S(2)}) collective-permute-start(bf16[64,8192]{1,0:T(8,128)(2,1)} %get-tuple-element.58.refs_4_), channel_id=1, source_target_pairs={{4,8},{5,9},{6,10},{7,11},{8,4},{9,5},{10,6},{11,7},{20,24},{21,25... | collective-permute-start | bytes 3145736 | tf_op jit(solution)/shard_map/ppermute | solution.py:89
  68.2 21.6 %collective-permute-start.10 = (bf16[64,7168]{1,0:T(8,128)(2,1)S(1)}, bf16[64,7168]{1,0:T(8,128)(2,1)S(1)}, u32[]{:S(2)}, u32[]{:S(2)}) collective-permute-start(bf16[64,7168]{1,0:T(8,128)(2,1)S(1)} %broadcast_select_fusion.3.refs_3_), channel_id=1, source_target_pairs={{0,2},{1,3},{2,0},{3,1},{4,6},{5,7},{6,4},{7,5},{8,10},{9,11},{10,... | collective-permute-start | bytes 2752520 | tf_op jit(solution)/shard_map/ppermute | solution.py:62
  92.8 18.4 %collective-permute-start.13 = (bf16[64,8192]{1,0:T(8,128)(2,1)}, bf16[64,8192]{1,0:T(8,128)(2,1)S(1)}, u32[]{:S(2)}, u32[]{:S(2)}) collective-permute-start(bf16[64,8192]{1,0:T(8,128)(2,1)} %get-tuple-element.60), channel_id=1, source_target_pairs={{0,4},{1,5},{2,6},{3,7},{4,0},{5,1},{6,2},{7,3},{8,12},{9,13},{10,... | collective-permute-start | bytes 3145736 | tf_op jit(solution)/shard_map/ppermute | solution.py:62
  92.8 18.4 %collective-permute-start.14 = (bf16[64,8192]{1,0:T(8,128)(2,1)}, bf16[64,8192]{1,0:T(8,128)(2,1)S(1)}, u32[]{:S(2)}, u32[]{:S(2)}) collective-permute-start(bf16[64,8192]{1,0:T(8,128)(2,1)} %get-tuple-element.60), channel_id=1, source_target_pairs={{0,2},{1,3},{2,0},{3,1},{4,6},{5,7},{6,4},{7,5},{8,10},{9,11},{10,... | collective-permute-start | bytes 3145736 | tf_op jit(solution)/shard_map/ppermute | solution.py:62
  93.2 15.5 %collective-permute-start.15 = (bf16[64,7168]{1,0:T(8,128)(2,1)S(1)}, bf16[64,7168]{1,0:T(8,128)(2,1)S(1)}, u32[]{:S(2)}, u32[]{:S(2)}) collective-permute-start(bf16[64,7168]{1,0:T(8,128)(2,1)S(1)} %broadcast_select_fusion.3.refs_3_), channel_id=1, source_target_pairs={{0,16},{16,0},{1,17},{17,1},{2,18},{18,2},{3,19},{19,3},{4,20},{20... | collective-permute-start | bytes 2752520 | tf_op jit(solution)/shard_map/ppermute | solution.py:66
  94.4 46.0 %collective-permute-start.17 = (bf16[64,8192]{1,0:T(8,128)(2,1)}, bf16[64,8192]{1,0:T(8,128)(2,1)}, u32[]{:S(2)}, u32[]{:S(2)}) collective-permute-start(bf16[64,8192]{1,0:T(8,128)(2,1)} %get-tuple-element.68), channel_id=1, source_target_pairs={{4,0},{5,1},{6,2},{7,3},{8,12},{9,13},{10,14},{11,15},{20,16},{21,... | collective-permute-start | bytes 3145736 | tf_op jit(solution)/shard_map/ppermute | solution.py:89
  113.7 26.7 %collective-permute-start.16 = (bf16[64,8192]{1,0:T(8,128)(2,1)}, bf16[64,8192]{1,0:T(8,128)(2,1)}, u32[]{:S(2)}, u32[]{:S(2)}) collective-permute-start(bf16[64,8192]{1,0:T(8,128)(2,1)} %get-tuple-element.67.refs_2_), channel_id=1, source_target_pairs={{4,8},{5,9},{6,10},{7,11},{8,4},{9,5},{10,6},{11,7},{20,24},{21,25... | collective-permute-start | bytes 3145736 | tf_op jit(solution)/shard_map/ppermute | solution.py:89
  117.1 23.2 %collective-permute-start.18 = (bf16[64,7168]{1,0:T(8,128)(2,1)S(1)}, bf16[64,7168]{1,0:T(8,128)(2,1)S(1)}, u32[]{:S(2)}, u32[]{:S(2)}) collective-permute-start(bf16[64,7168]{1,0:T(8,128)(2,1)S(1)} %broadcast_select_fusion.2.refs_1_), channel_id=1, source_target_pairs={{0,2},{1,3},{2,0},{3,1},{4,6},{5,7},{6,4},{7,5},{8,10},{9,11},{10,... | collective-permute-start | bytes 2752520 | tf_op jit(solution)/shard_map/ppermute | solution.py:62
  117.7 22.7 %collective-permute-start.19 = (bf16[64,7168]{1,0:T(8,128)(2,1)S(1)}, bf16[64,7168]{1,0:T(8,128)(2,1)S(1)}, u32[]{:S(2)}, u32[]{:S(2)}) collective-permute-start(bf16[64,7168]{1,0:T(8,128)(2,1)S(1)} %broadcast_select_fusion.2.refs_1_), channel_id=1, source_target_pairs={{0,16},{16,0},{1,17},{17,1},{2,18},{18,2},{3,19},{19,3},{4,20},{20... | collective-permute-start | bytes 2752520 | tf_op jit(solution)/shard_map/ppermute | solution.py:66
  145.1 24.6 %collective-permute-start.20 = (bf16[64,8192]{1,0:T(8,128)(2,1)}, bf16[64,8192]{1,0:T(8,128)(2,1)}, u32[]{:S(2)}, u32[]{:S(2)}) collective-permute-start(bf16[64,8192]{1,0:T(8,128)(2,1)} %get-tuple-element.75), channel_id=1, source_target_pairs={{4,0},{5,1},{6,2},{7,3},{8,12},{9,13},{10,14},{11,15},{20,16},{21,... | collective-permute-start | bytes 3145736 | tf_op jit(solution)/shard_map/ppermute | solution.py:89
  148.5 21.2 %collective-permute-start.21 = (bf16[64,8192]{1,0:T(8,128)(2,1)}, bf16[64,8192]{1,0:T(8,128)(2,1)S(1)}, u32[]{:S(2)}, u32[]{:S(2)}) collective-permute-start(bf16[64,8192]{1,0:T(8,128)(2,1)} %broadcast_select_fusion.1.refs_3_), channel_id=1, source_target_pairs={{0,2},{1,3},{2,0},{3,1},{4,6},{5,7},{6,4},{7,5},{8,10},{9,11},{10,... | collective-permute-start | bytes 3145736 | tf_op jit(solution)/shard_map/ppermute | solution.py:62
  149.3 20.5 %collective-permute-start.22 = (bf16[64,7168]{1,0:T(8,128)(2,1)}, bf16[64,7168]{1,0:T(8,128)(2,1)}, u32[]{:S(2)}, u32[]{:S(2)}) collective-permute-start(bf16[64,7168]{1,0:T(8,128)(2,1)} %get-tuple-element.76.refs_0_), channel_id=1, source_target_pairs={{0,16},{16,0},{1,17},{17,1},{2,18},{18,2},{3,19},{19,3},{4,20},{20... | collective-permute-start | bytes 2752520 | tf_op jit(solution)/shard_map/ppermute | solution.py:66
  149.5 62.7 %collective-permute-start.24 = (bf16[64,8192]{1,0:T(8,128)(2,1)}, bf16[64,8192]{1,0:T(8,128)(2,1)}, u32[]{:S(2)}, u32[]{:S(2)}) collective-permute-start(bf16[64,8192]{1,0:T(8,128)(2,1)} %get-tuple-element.72.refs_1_), channel_id=1, source_target_pairs={{0,4},{1,5},{2,6},{3,7},{4,0},{5,1},{6,2},{7,3},{8,12},{9,13},{10,... | collective-permute-start | bytes 3145736 | tf_op jit(solution)/shard_map/ppermute | solution.py:62
  158.5 32.4 %copy-start.8 = (bf16[64,7168]{1,0:T(8,128)(2,1)S(1)}, bf16[64,7168]{1,0:T(8,128)(2,1)}, u32[]{:S(2)}) copy-start(bf16[64,7168]{1,0:T(8,128)(2,1)} %get-tuple-element.80.refs_3_) | copy-start | bytes 2752516
  174.2 38.0 %collective-permute-start.23 = (bf16[64,8192]{1,0:T(8,128)(2,1)}, bf16[64,8192]{1,0:T(8,128)(2,1)}, u32[]{:S(2)}, u32[]{:S(2)}) collective-permute-start(bf16[64,8192]{1,0:T(8,128)(2,1)} %broadcast_select_fusion.refs_1_), channel_id=1, source_target_pairs={{0,2},{1,3},{2,0},{3,1},{4,6},{5,7},{6,4},{7,5},{8,10},{9,11},{10,... | collective-permute-start | bytes 3145736 | tf_op jit(solution)/shard_map/ppermute | solution.py:62
  174.9 37.2 %collective-permute-start.25 = (bf16[64,7168]{1,0:T(8,128)(2,1)}, bf16[64,7168]{1,0:T(8,128)(2,1)}, u32[]{:S(2)}, u32[]{:S(2)}) collective-permute-start(bf16[64,7168]{1,0:T(8,128)(2,1)} %get-tuple-element.79.refs_2_), channel_id=1, source_target_pairs={{0,16},{16,0},{1,17},{17,1},{2,18},{18,2},{3,19},{19,3},{4,20},{20... | collective-permute-start | bytes 2752520 | tf_op jit(solution)/shard_map/ppermute | solution.py:66
  176.3 40.0 %collective-permute-start = (s32[2,4]{1,0:T(2,128)S(1)}, s32[2,4]{1,0:T(2,128)S(1)}, u32[]{:S(2)}, u32[]{:S(2)}) collective-permute-start(s32[2,4]{1,0:T(2,128)S(1)} %pad_add_fusion), channel_id=1, source_target_pairs={{0,1},{1,0},{2,3},{3,2},{4,5},{5,4},{6,7},{7,6},{8,9},{9,8},{10,11... | collective-permute-start | bytes 104 | tf_op jit(solution)/shard_map/ppermute | solution.py:62
  192.4 48.4 %collective-permute-start.27 = (bf16[32,7168]{1,0:T(8,128)(2,1)}, bf16[32,7168]{1,0:T(8,128)(2,1)}, u32[]{:S(2)}, u32[]{:S(2)}) collective-permute-start(bf16[32,7168]{1,0:T(8,128)(2,1)} %slice.20), channel_id=1, source_target_pairs={{0,16},{16,0},{1,17},{17,1},{2,18},{18,2},{3,19},{19,3},{4,20},{20... | collective-permute-start | bytes 1376264 | tf_op jit(solution)/shard_map/ppermute | solution.py:66
  214.6 26.2 %collective-permute-start.26 = (bf16[32,7168]{1,0:T(8,128)(2,1)S(1)}, bf16[32,7168]{1,0:T(8,128)(2,1)S(1)}, u32[]{:S(2)}, u32[]{:S(2)}) collective-permute-start(bf16[32,7168]{1,0:T(8,128)(2,1)S(1)} %slice.19), channel_id=1, source_target_pairs={{0,2},{1,3},{2,0},{3,1},{4,6},{5,7},{6,4},{7,5},{8,10},{9,11},{10,... | collective-permute-start | bytes 1376264 | tf_op jit(solution)/shard_map/ppermute | solution.py:62
  252.7 1.5 collective-permute-start.28
  (49 other events, 258.6 us)
Sparse Core Ops, SparseCore 0:
  8.9 32.2 all-gather.1

commit v4 on v3

--- a/solution.py
+++ b/solution.py
@@ -55,7 +55,7 @@
 
 CORE, COLUMN, NEAR, ACROSS, OPPOSITE = 1, 2, 4, 12, 8
 LITTLE = pl.CostEstimate(flops=1, bytes_accessed=1, transcendentals=0)
-VMEM_LIMIT = 16 * 1024 * 1024
+VMEM_LIMIT = 63 * 1024 * 1024
 
 
 def flip(array, code, count):
@@ -72,7 +72,7 @@
 
 def after(turn, arrays):
     count = len(arrays)
-    anywhere = pl.BlockSpec(memory_space=pl.ANY)
+    anywhere = pl.BlockSpec(memory_space=pltpu.HBM)
     scalar = pl.BlockSpec(memory_space=pltpu.SMEM)
     *arrays, turn = pl.pallas_call(
         functools.partial(after_kernel, count),
@@ -80,6 +80,7 @@
         in_specs=[anywhere] * count + [scalar],
         out_specs=[anywhere] * count + [scalar],
         input_output_aliases={i: i for i in range(count)},
+        compiler_params=pltpu.CompilerParams(vmem_limit_bytes=VMEM_LIMIT),
         cost_estimate=LITTLE,
     )(*arrays, turn)
     return turn, arrays

time: 266 us -> 256 us (0.962)
  local copies, waits for them, and re-layouts: 61.9 us -> 15.2 us
  Pallas kernels: 72.5 us -> 89.3 us
  starting transfers between devices: 53.2 us -> 69.5 us
  other arithmetic: 11.9 us -> 16.5 us
    unnamed x103 -> x27, local copies, waits for them, and re-layouts: 57.2 us -> 8.76 us
    ppermute x14, starting transfers between devices: 22.9 us -> 39.9 us  [flip(): return lax.ppermute(array, 'dp', [(i, i ^ code) for i in range(count)])]
    pallas_call x6, Pallas kernels: 61.4 us -> 74.6 us  [proj(): pl.pallas_call(functools.partial(proj_kernel, len(pieces)), out_shape=(ja...]
    ppermute x14, waiting for transfers between devices: 18.7 us -> 23.7 us  [flip(): return lax.ppermute(array, 'dp', [(i, i ^ code) for i in range(count)])]
    pallas_call x2, Pallas kernels: 3.47 us -> 7.22 us  [score(): pl.pallas_call(functools.partial(score_kernel, slots), out_shape=jax.Shap...]
    concatenate x6, other arithmetic: 4.27 us -> 7.48 us  [proj(): jnp.concatenate([turn, first, own_row, other_row])]
  transfers between devices with their start and end apart: 30 -> 30, of which waited for: 9 -> 10; matrix products, arithmetic and copies ran while one was open for 7% -> 10% of each run, Pallas kernels for 23% -> 29%
where the time goes in v4:
time: 256 us; the launch traced here: 254 us
  Pallas kernels  89.3 us (35%)
  starting transfers between devices  69.5 us (27%)
  waiting for transfers between devices  48.6 us (19%)
  other arithmetic  16.5 us (6%)
  local copies, waits for them, and re-layouts  15.2 us (6%)
  between operations  13.7 us (5%)
    pallas_call x6, Pallas kernels, proj(): pl.pallas_call(functools.partial(proj_kernel, len(pieces)), out_shape=(ja...  74.6 us
    ppermute x14, starting transfers between devices, flip(): return lax.ppermute(array, 'dp', [(i, i ^ code) for i in range(count)])  39.9 us
    ppermute x14, waiting for transfers between devices, flip(): return lax.ppermute(array, 'dp', [(i, i ^ code) for i in range(count)])  23.7 us
    ppermute x8, starting transfers between devices, lines(): lax.ppermute(array, 'dp', [(a * 4 + rest, b * 4 + rest) for a, b in pairs...  23 us
    ppermute x8, waiting for transfers between devices, lines(): lax.ppermute(array, 'dp', [(a * 4 + rest, b * 4 + rest) for a, b in pairs...  15 us
    ppermute x7, waiting for transfers between devices, swap_groups(): return lax.ppermute(array, 'groups', [(0, 1), (1, 0)])  9.8 us
    unnamed x27, local copies, waits for them, and re-layouts  8.76 us
    concatenate x6, other arithmetic, proj(): jnp.concatenate([turn, first, own_row, other_row])  7.48 us
  transfers between devices with their start and end apart: 30, of which 10 were waited for; matrix products, arithmetic and copies ran while one was open for 10% of the time, Pallas kernels for 29%

profile of v4, /device:TPU:9, one launch (start us, length us, event | category | flops | bytes accessed | tf_op | source)
XLA Modules:
  0.0 253.5 jit_solution(17418682273808351928)
XLA Ops:
  7.3 2.5 constant_dynamic-slice_fusion
  11.2 4.3 %collective-permute-start.3 = (bf16[64,7168]{1,0:T(8,128)(2,1)S(1)}, bf16[64,7168]{1,0:T(8,128)(2,1)S(1)}, u32[]{:S(2)}, u32[]{:S(2)}) collective-permute-start(bf16[64,7168]{1,0:T(8,128)(2,1)S(1)} %get-tuple-element.96.refs_0_), channel_id=1, source_target_pairs={{4,8},{5,9},{6,10},{7,11},{8,4},{9,5},{10,6},{11,7},{20,24},{21,25... | collective-permute-start | bytes 2752520 | tf_op jit(solution)/shard_map/ppermute | solution.py:90
  15.5 15.5 %collective-permute-done.1.refs_0_ = bf16[64,7168]{1,0:T(8,128)(2,1)S(1)} collective-permute-done((bf16[64,7168]{1,0:T(8,128)(2,1)S(1)}, bf16[64,7168]{1,0:T(8,128)(2,1)S(1)}, u32[]{:S(2)}, u32[]{:S(2)}) %collective-permute-start.1) | collective-permute-done | bytes 917536 | tf_op jit(solution)/shard_map/ppermute | solution.py:62
  32.9 2.0 collective-permute-done.3.refs_2_
  36.4 3.1 %collective-permute-start.4 = (bf16[64,7168]{1,0:T(8,128)(2,1)}, bf16[64,7168]{1,0:T(8,128)(2,1)S(1)}, u32[]{:S(2)}, u32[]{:S(2)}) collective-permute-start(bf16[64,7168]{1,0:T(8,128)(2,1)} %get-tuple-element.50.refs_2_), channel_id=1, source_target_pairs={{4,8},{5,9},{6,10},{7,11},{8,4},{9,5},{10,6},{11,7},{20,24},{21,25... | collective-permute-start | bytes 2752520 | tf_op jit(solution)/shard_map/ppermute | solution.py:90
  39.8 2.2 collective-permute-start.5
  43.3 2.3 copy.41.refs_4_
  45.6 13.0 %collective-permute-done.4.refs_0_ = bf16[64,7168]{1,0:T(8,128)(2,1)S(1)} collective-permute-done((bf16[64,7168]{1,0:T(8,128)(2,1)}, bf16[64,7168]{1,0:T(8,128)(2,1)S(1)}, u32[]{:S(2)}, u32[]{:S(2)}) %collective-permute-start.4) | collective-permute-done | bytes 917536 | tf_op jit(solution)/shard_map/ppermute | solution.py:90
  59.8 1.6 collective-permute-done.7.refs_3_
  62.6 2.2 collective-permute-start.9
  64.9 2.5 collective-permute-start.12
  67.4 2.2 broadcast_select_fusion.3.refs_3_
  72.0 12.1 %shard_map.66 = (f32[1024,256]{1,0:T(8,128)}, s32[1]{0:T(128)}) custom-call(s32[4]{0:T(128)} %pad_add_fusion.5.at_ref, bf16[512,14336]{1,0:T(8,128)(2,1)} %own_ref.7, bf16[512,14336]{1,0:T(8,128)(2,1)} %collective-permute-done.8.other_ref, bf16[64,7168]{1,0:T(8,128)(2,1)} %copy-done.7, bf16[64,7168]{1,0:T(8,128)(2,1)} %get-tuple-element.52.refs_1_, ...), custom_call_target="tpu_custom_call" | custom-call | flops 1 | bytes 1 | tf_op jit(solution)/shard_map/pallas_call | solution.py:121
  84.1 1.5 collective-permute-done.10.refs_1_
  89.6 3.7 %collective-permute-start.17 = (bf16[64,8192]{1,0:T(8,128)(2,1)}, bf16[64,8192]{1,0:T(8,128)(2,1)}, u32[]{:S(2)}, u32[]{:S(2)}) collective-permute-start(bf16[64,8192]{1,0:T(8,128)(2,1)} %get-tuple-element.68), channel_id=1, source_target_pairs={{4,0},{5,1},{6,2},{7,3},{8,12},{9,13},{10,14},{11,15},{20,16},{21,... | collective-permute-start | bytes 3145736 | tf_op jit(solution)/shard_map/ppermute | solution.py:90
  93.3 8.0 %collective-permute-done.15.refs_2_ = bf16[64,7168]{1,0:T(8,128)(2,1)} collective-permute-done((bf16[64,7168]{1,0:T(8,128)(2,1)}, bf16[64,7168]{1,0:T(8,128)(2,1)}, u32[]{:S(2)}, u32[]{:S(2)}) %collective-permute-start.15) | collective-permute-done | bytes 917536 | tf_op jit(solution)/shard_map/ppermute | solution.py:66
  101.3 1.5 collective-permute-done.13.refs_0_
  102.8 4.7 %collective-permute-done.14.refs_1_ = bf16[64,8192]{1,0:T(8,128)(2,1)} collective-permute-done((bf16[64,8192]{1,0:T(8,128)(2,1)}, bf16[64,8192]{1,0:T(8,128)(2,1)}, u32[]{:S(2)}, u32[]{:S(2)}) %collective-permute-start.14) | collective-permute-done | bytes 1048608 | tf_op jit(solution)/shard_map/ppermute | solution.py:62
  108.6 2.6 %collective-permute-start.16 = (bf16[64,8192]{1,0:T(8,128)(2,1)}, bf16[64,8192]{1,0:T(8,128)(2,1)}, u32[]{:S(2)}, u32[]{:S(2)}) collective-permute-start(bf16[64,8192]{1,0:T(8,128)(2,1)} %get-tuple-element.67.refs_2_), channel_id=1, source_target_pairs={{4,8},{5,9},{6,10},{7,11},{8,4},{9,5},{10,6},{11,7},{20,24},{21,25... | collective-permute-start | bytes 3145736 | tf_op jit(solution)/shard_map/ppermute | solution.py:90
  115.6 12.0 %shard_map.69 = (f32[1024,256]{1,0:T(8,128)}, s32[1]{0:T(128)}) custom-call(s32[4]{0:T(128)} %pad_add_fusion.4.at_ref, bf16[512,14336]{1,0:T(8,128)(2,1)} %own_ref.7, bf16[512,14336]{1,0:T(8,128)(2,1)} %collective-permute-done.8.other_ref, bf16[64,7168]{1,0:T(8,128)(2,1)} %get-tuple-element.95.refs_0_, bf16[64,7168]{1,0:T(8,128)(2,1)} %get-tuple-element.63.refs_1_, ...), custom_call_target="tpu_custom_call" | custom-call | flops 1 | bytes 1 | tf_op jit(solution)/shard_map/pallas_call | solution.py:121
  129.8 2.3 broadcast_select_fusion.1.refs_3_
  132.1 2.3 collective-permute-start.20
  136.6 13.4 %shard_map.71 = (f32[1024,256]{1,0:T(8,128)}, s32[1]{0:T(128)}) custom-call(s32[4]{0:T(128)} %fusion.8.at_ref, bf16[1024,8192]{1,0:T(8,128)(2,1)} %all-gather.2.cloned.1.call-done.own_ref.other_ref, bf16[1024,8192]{1,0:T(8,128)(2,1)} %all-gather.2.cloned.1.call-done.own_ref.other_ref, bf16[64,8192]{1,0:T(8,128)(2,1)} %bitcast.21, ...), custom_call_target="tpu_custom_call" | custom-call | flops 1 | bytes 1 | tf_op jit(solution)/shard_map/pallas_call | solution.py:121
  152.2 2.3 broadcast_select_fusion.refs_1_
  156.7 30.0 %collective-permute-start = (s32[2,4]{1,0:T(2,128)S(1)}, s32[2,4]{1,0:T(2,128)S(1)}, u32[]{:S(2)}, u32[]{:S(2)}) collective-permute-start(s32[2,4]{1,0:T(2,128)S(1)} %pad_add_fusion), channel_id=1, source_target_pairs={{0,1},{1,0},{2,3},{3,2},{4,5},{5,4},{6,7},{7,6},{8,9},{9,8},{10,11... | collective-permute-start | bytes 104 | tf_op jit(solution)/shard_map/ppermute | solution.py:62
  186.8 1.8 slice.20
  190.0 11.9 %shard_map.74 = (f32[1024,256]{1,0:T(8,128)}, s32[1]{0:T(128)}) custom-call(s32[4]{0:T(128)} %pad_add_fusion.3.at_ref, bf16[512,14336]{1,0:T(8,128)(2,1)} %own_ref.7, bf16[512,14336]{1,0:T(8,128)(2,1)} %collective-permute-done.8.other_ref, bf16[64,7168]{1,0:T(8,128)(2,1)} %get-tuple-element.76.refs_0_, bf16[64,7168]{1,0:T(8,128)(2,1)} %broadcast_select_fusion.2.refs_1_, ...), custom_call_target="tpu_custom_call" | custom-call | flops 1 | bytes 1 | tf_op jit(solution)/shard_map/pallas_call | solution.py:121
  206.7 3.6 %shard_map.72 = f32[8,256]{1,0:T(8,128)} custom-call(s32[2,8]{1,0:T(2,128)} %pad_add_fusion.1.spans_ref, f32[1024,256]{1,0:T(8,128)} %get-tuple-element.56.mine_ref, f32[1024,256]{1,0:T(8,128)} %get-tuple-element.66.theirs_ref, f32[1024,256]{1,0:T(8,128)} %get-tuple-element.74.right_ref), custom_call_target="tpu_custom_call" | custom-call | flops 1 | bytes 1 | tf_op jit(solution)/shard_map/pallas_call | solution.py:162
  211.5 13.2 %shard_map.76 = (f32[1024,256]{1,0:T(8,128)}, s32[1]{0:T(128)}) custom-call(s32[4]{0:T(128)} %fusion.10.at_ref, bf16[1024,8192]{1,0:T(8,128)(2,1)} %all-gather.2.cloned.1.call-done.own_ref.other_ref, bf16[1024,8192]{1,0:T(8,128)(2,1)} %all-gather.2.cloned.1.call-done.own_ref.other_ref, bf16[64,8192]{1,0:T(8,128)(2,1)} %get-tuple-element.86.refs_0_, ...), custom_call_target="tpu_custom_call" | custom-call | flops 1 | bytes 1 | tf_op jit(solution)/shard_map/pallas_call | solution.py:121
  226.8 12.0 %shard_map.77 = (f32[1024,256]{1,0:T(8,128)}, s32[1]{0:T(128)}) custom-call(s32[4]{0:T(128)} %pad_add_fusion.2.at_ref, bf16[512,14336]{1,0:T(8,128)(2,1)} %own_ref.7, bf16[512,14336]{1,0:T(8,128)(2,1)} %collective-permute-done.8.other_ref, bf16[64,7168]{1,0:T(8,128)(2,1)} %get-tuple-element.90.refs_0_, bf16[64,7168]{1,0:T(8,128)(2,1)} %get-tuple-element.91.refs_1_, ...), custom_call_target="tpu_custom_call" | custom-call | flops 1 | bytes 1 | tf_op jit(solution)/shard_map/pallas_call | solution.py:121
  238.9 3.6 %shard_map.78 = f32[8,256]{1,0:T(8,128)} custom-call(s32[2,8]{1,0:T(2,128)} %pad_add_fusion.1.spans_ref, f32[1024,256]{1,0:T(8,128)} %get-tuple-element.81.mine_ref, f32[1024,256]{1,0:T(8,128)} %get-tuple-element.93.theirs_ref, f32[1024,256]{1,0:T(8,128)} %get-tuple-element.94.right_ref), custom_call_target="tpu_custom_call" | custom-call | flops 1 | bytes 1 | tf_op jit(solution)/shard_map/pallas_call | solution.py:162
  243.2 1.8 collective-permute-start.28
  (100 shorter events, 41.9 us)
Async XLA Ops:
  6.5 130.0 %all-gather.2.cloned.1.call-start = ((), (), s32[]{:S(2)}) async-start(), calls=%async_computation | async-start | bytes 25165824 | tf_op jit(solution)/shard_map/all_gather | solution.py:190
  6.5 65.5 %collective-permute-start.8 = (bf16[512,14336]{1,0:T(8,128)(2,1)}, bf16[512,14336]{1,0:T(8,128)(2,1)}, u32[]{:S(2)}, u32[]{:S(2)}) collective-permute-start(bf16[512,14336]{1,0:T(8,128)(2,1)} %own_ref.7), channel_id=1, source_target_pairs={{0,1},{1,0},{2,3},{3,2},{4,5},{5,4},{6,7},{7,6},{8,9},{9,8},{10,11... | collective-permute-start | bytes 44040200 | tf_op jit(solution)/shard_map/ppermute | solution.py:62
  9.8 22.2 %copy-start.7 = (bf16[64,7168]{1,0:T(8,128)(2,1)}, bf16[64,7168]{1,0:T(8,128)(2,1)S(1)}, u32[]{:S(2)}) copy-start(bf16[64,7168]{1,0:T(8,128)(2,1)S(1)} %get-tuple-element.96.refs_0_) | copy-start | bytes 2752516
  9.8 21.2 %collective-permute-start.1 = (bf16[64,7168]{1,0:T(8,128)(2,1)S(1)}, bf16[64,7168]{1,0:T(8,128)(2,1)S(1)}, u32[]{:S(2)}, u32[]{:S(2)}) collective-permute-start(bf16[64,7168]{1,0:T(8,128)(2,1)S(1)} %get-tuple-element.96.refs_0_), channel_id=1, source_target_pairs={{0,2},{1,3},{2,0},{3,1},{4,6},{5,7},{6,4},{7,5},{8,10},{9,11},{10,... | collective-permute-start | bytes 2752520 | tf_op jit(solution)/shard_map/ppermute | solution.py:62
  11.0 20.9 %collective-permute-start.2 = (bf16[64,7168]{1,0:T(8,128)(2,1)S(1)}, bf16[64,7168]{1,0:T(8,128)(2,1)S(1)}, u32[]{:S(2)}, u32[]{:S(2)}) collective-permute-start(bf16[64,7168]{1,0:T(8,128)(2,1)S(1)} %get-tuple-element.96.refs_0_), channel_id=1, source_target_pairs={{0,4},{1,5},{2,6},{3,7},{4,0},{5,1},{6,2},{7,3},{8,12},{9,13},{10,... | collective-permute-start | bytes 2752520 | tf_op jit(solution)/shard_map/ppermute | solution.py:62
  11.2 23.8 %collective-permute-start.3 = (bf16[64,7168]{1,0:T(8,128)(2,1)S(1)}, bf16[64,7168]{1,0:T(8,128)(2,1)S(1)}, u32[]{:S(2)}, u32[]{:S(2)}) collective-permute-start(bf16[64,7168]{1,0:T(8,128)(2,1)S(1)} %get-tuple-element.96.refs_0_), channel_id=1, source_target_pairs={{4,8},{5,9},{6,10},{7,11},{8,4},{9,5},{10,6},{11,7},{20,24},{21,25... | collective-permute-start | bytes 2752520 | tf_op jit(solution)/shard_map/ppermute | solution.py:90
  36.4 22.2 %collective-permute-start.4 = (bf16[64,7168]{1,0:T(8,128)(2,1)}, bf16[64,7168]{1,0:T(8,128)(2,1)S(1)}, u32[]{:S(2)}, u32[]{:S(2)}) collective-permute-start(bf16[64,7168]{1,0:T(8,128)(2,1)} %get-tuple-element.50.refs_2_), channel_id=1, source_target_pairs={{4,8},{5,9},{6,10},{7,11},{8,4},{9,5},{10,6},{11,7},{20,24},{21,25... | collective-permute-start | bytes 2752520 | tf_op jit(solution)/shard_map/ppermute | solution.py:90
  39.5 20.4 %collective-permute-start.6 = (bf16[64,7168]{1,0:T(8,128)(2,1)}, bf16[64,7168]{1,0:T(8,128)(2,1)}, u32[]{:S(2)}, u32[]{:S(2)}) collective-permute-start(bf16[64,7168]{1,0:T(8,128)(2,1)} %get-tuple-element.50.refs_2_), channel_id=1, source_target_pairs={{0,2},{1,3},{2,0},{3,1},{4,6},{5,7},{6,4},{7,5},{8,10},{9,11},{10,... | collective-permute-start | bytes 2752520 | tf_op jit(solution)/shard_map/ppermute | solution.py:62
  39.8 20.0 %collective-permute-start.5 = (bf16[64,7168]{1,0:T(8,128)(2,1)}, bf16[64,7168]{1,0:T(8,128)(2,1)}, u32[]{:S(2)}, u32[]{:S(2)}) collective-permute-start(bf16[64,7168]{1,0:T(8,128)(2,1)} %get-tuple-element.51), channel_id=1, source_target_pairs={{4,0},{5,1},{6,2},{7,3},{8,12},{9,13},{10,14},{11,15},{20,16},{21,... | collective-permute-start | bytes 2752520 | tf_op jit(solution)/shard_map/ppermute | solution.py:90
  42.0 19.4 %collective-permute-start.7 = (bf16[64,7168]{1,0:T(8,128)(2,1)}, bf16[64,7168]{1,0:T(8,128)(2,1)}, u32[]{:S(2)}, u32[]{:S(2)}) collective-permute-start(bf16[64,7168]{1,0:T(8,128)(2,1)} %get-tuple-element.52.refs_1_), channel_id=1, source_target_pairs={{0,16},{16,0},{1,17},{17,1},{2,18},{18,2},{3,19},{19,3},{4,20},{20... | collective-permute-start | bytes 2752520 | tf_op jit(solution)/shard_map/ppermute | solution.py:66
  58.6 25.5 %collective-permute-start.11 = (bf16[64,7168]{1,0:T(8,128)(2,1)}, bf16[64,7168]{1,0:T(8,128)(2,1)}, u32[]{:S(2)}, u32[]{:S(2)}) collective-permute-start(bf16[64,7168]{1,0:T(8,128)(2,1)} %get-tuple-element.50.refs_2_), channel_id=1, source_target_pairs={{0,16},{16,0},{1,17},{17,1},{2,18},{18,2},{3,19},{19,3},{4,20},{20... | collective-permute-start | bytes 2752520 | tf_op jit(solution)/shard_map/ppermute | solution.py:66
  62.6 21.5 %collective-permute-start.9 = (bf16[64,7168]{1,0:T(8,128)(2,1)}, bf16[64,7168]{1,0:T(8,128)(2,1)}, u32[]{:S(2)}, u32[]{:S(2)}) collective-permute-start(bf16[64,7168]{1,0:T(8,128)(2,1)} %get-tuple-element.57), channel_id=1, source_target_pairs={{4,0},{5,1},{6,2},{7,3},{8,12},{9,13},{10,14},{11,15},{20,16},{21,... | collective-permute-start | bytes 2752520 | tf_op jit(solution)/shard_map/ppermute | solution.py:90
  64.9 20.8 %collective-permute-start.12 = (bf16[64,8192]{1,0:T(8,128)(2,1)}, bf16[64,8192]{1,0:T(8,128)(2,1)}, u32[]{:S(2)}, u32[]{:S(2)}) collective-permute-start(bf16[64,8192]{1,0:T(8,128)(2,1)} %get-tuple-element.58.refs_4_), channel_id=1, source_target_pairs={{4,8},{5,9},{6,10},{7,11},{8,4},{9,5},{10,6},{11,7},{20,24},{21,25... | collective-permute-start | bytes 3145736 | tf_op jit(solution)/shard_map/ppermute | solution.py:90
  69.6 16.1 %collective-permute-start.10 = (bf16[64,7168]{1,0:T(8,128)(2,1)}, bf16[64,7168]{1,0:T(8,128)(2,1)}, u32[]{:S(2)}, u32[]{:S(2)}) collective-permute-start(bf16[64,7168]{1,0:T(8,128)(2,1)} %broadcast_select_fusion.3.refs_3_), channel_id=1, source_target_pairs={{0,2},{1,3},{2,0},{3,1},{4,6},{5,7},{6,4},{7,5},{8,10},{9,11},{10,... | collective-permute-start | bytes 2752520 | tf_op jit(solution)/shard_map/ppermute | solution.py:62
  72.0 39.2 %copy-start.2 = (bf16[64,7168]{1,0:T(8,128)(2,1)S(1)}, bf16[64,7168]{1,0:T(8,128)(2,1)}, u32[]{:S(2)}) copy-start(bf16[64,7168]{1,0:T(8,128)(2,1)} %get-tuple-element.57) | copy-start | bytes 2752516
  86.8 15.9 %collective-permute-start.13 = (bf16[64,8192]{1,0:T(8,128)(2,1)}, bf16[64,8192]{1,0:T(8,128)(2,1)}, u32[]{:S(2)}, u32[]{:S(2)}) collective-permute-start(bf16[64,8192]{1,0:T(8,128)(2,1)} %get-tuple-element.60), channel_id=1, source_target_pairs={{0,4},{1,5},{2,6},{3,7},{4,0},{5,1},{6,2},{7,3},{8,12},{9,13},{10,... | collective-permute-start | bytes 3145736 | tf_op jit(solution)/shard_map/ppermute | solution.py:62
  87.1 20.3 %collective-permute-start.14 = (bf16[64,8192]{1,0:T(8,128)(2,1)}, bf16[64,8192]{1,0:T(8,128)(2,1)}, u32[]{:S(2)}, u32[]{:S(2)}) collective-permute-start(bf16[64,8192]{1,0:T(8,128)(2,1)} %get-tuple-element.60), channel_id=1, source_target_pairs={{0,2},{1,3},{2,0},{3,1},{4,6},{5,7},{6,4},{7,5},{8,10},{9,11},{10,... | collective-permute-start | bytes 3145736 | tf_op jit(solution)/shard_map/ppermute | solution.py:62
  88.3 13.0 %collective-permute-start.15 = (bf16[64,7168]{1,0:T(8,128)(2,1)}, bf16[64,7168]{1,0:T(8,128)(2,1)}, u32[]{:S(2)}, u32[]{:S(2)}) collective-permute-start(bf16[64,7168]{1,0:T(8,128)(2,1)} %broadcast_select_fusion.3.refs_3_), channel_id=1, source_target_pairs={{0,16},{16,0},{1,17},{17,1},{2,18},{18,2},{3,19},{19,3},{4,20},{20... | collective-permute-start | bytes 2752520 | tf_op jit(solution)/shard_map/ppermute | solution.py:66
  89.6 38.1 %collective-permute-start.17 = (bf16[64,8192]{1,0:T(8,128)(2,1)}, bf16[64,8192]{1,0:T(8,128)(2,1)}, u32[]{:S(2)}, u32[]{:S(2)}) collective-permute-start(bf16[64,8192]{1,0:T(8,128)(2,1)} %get-tuple-element.68), channel_id=1, source_target_pairs={{4,0},{5,1},{6,2},{7,3},{8,12},{9,13},{10,14},{11,15},{20,16},{21,... | collective-permute-start | bytes 3145736 | tf_op jit(solution)/shard_map/ppermute | solution.py:90
  108.6 19.1 %collective-permute-start.16 = (bf16[64,8192]{1,0:T(8,128)(2,1)}, bf16[64,8192]{1,0:T(8,128)(2,1)}, u32[]{:S(2)}, u32[]{:S(2)}) collective-permute-start(bf16[64,8192]{1,0:T(8,128)(2,1)} %get-tuple-element.67.refs_2_), channel_id=1, source_target_pairs={{4,8},{5,9},{6,10},{7,11},{8,4},{9,5},{10,6},{11,7},{20,24},{21,25... | collective-permute-start | bytes 3145736 | tf_op jit(solution)/shard_map/ppermute | solution.py:90
  112.3 15.3 %collective-permute-start.18 = (bf16[64,7168]{1,0:T(8,128)(2,1)}, bf16[64,7168]{1,0:T(8,128)(2,1)}, u32[]{:S(2)}, u32[]{:S(2)}) collective-permute-start(bf16[64,7168]{1,0:T(8,128)(2,1)} %broadcast_select_fusion.2.refs_1_), channel_id=1, source_target_pairs={{0,2},{1,3},{2,0},{3,1},{4,6},{5,7},{6,4},{7,5},{8,10},{9,11},{10,... | collective-permute-start | bytes 2752520 | tf_op jit(solution)/shard_map/ppermute | solution.py:62
  113.1 14.5 %collective-permute-start.19 = (bf16[64,7168]{1,0:T(8,128)(2,1)}, bf16[64,7168]{1,0:T(8,128)(2,1)S(1)}, u32[]{:S(2)}, u32[]{:S(2)}) collective-permute-start(bf16[64,7168]{1,0:T(8,128)(2,1)} %broadcast_select_fusion.2.refs_1_), channel_id=1, source_target_pairs={{0,16},{16,0},{1,17},{17,1},{2,18},{18,2},{3,19},{19,3},{4,20},{20... | collective-permute-start | bytes 2752520 | tf_op jit(solution)/shard_map/ppermute | solution.py:66
  132.1 18.0 %collective-permute-start.20 = (bf16[64,8192]{1,0:T(8,128)(2,1)}, bf16[64,8192]{1,0:T(8,128)(2,1)}, u32[]{:S(2)}, u32[]{:S(2)}) collective-permute-start(bf16[64,8192]{1,0:T(8,128)(2,1)} %get-tuple-element.75), channel_id=1, source_target_pairs={{4,0},{5,1},{6,2},{7,3},{8,12},{9,13},{10,14},{11,15},{20,16},{21,... | collective-permute-start | bytes 3145736 | tf_op jit(solution)/shard_map/ppermute | solution.py:90
  134.4 15.7 %collective-permute-start.21 = (bf16[64,8192]{1,0:T(8,128)(2,1)}, bf16[64,8192]{1,0:T(8,128)(2,1)}, u32[]{:S(2)}, u32[]{:S(2)}) collective-permute-start(bf16[64,8192]{1,0:T(8,128)(2,1)} %broadcast_select_fusion.1.refs_3_), channel_id=1, source_target_pairs={{0,2},{1,3},{2,0},{3,1},{4,6},{5,7},{6,4},{7,5},{8,10},{9,11},{10,... | collective-permute-start | bytes 3145736 | tf_op jit(solution)/shard_map/ppermute | solution.py:62
  135.1 15.0 %collective-permute-start.22 = (bf16[64,7168]{1,0:T(8,128)(2,1)}, bf16[64,7168]{1,0:T(8,128)(2,1)S(1)}, u32[]{:S(2)}, u32[]{:S(2)}) collective-permute-start(bf16[64,7168]{1,0:T(8,128)(2,1)} %get-tuple-element.76.refs_0_), channel_id=1, source_target_pairs={{0,16},{16,0},{1,17},{17,1},{2,18},{18,2},{3,19},{19,3},{4,20},{20... | collective-permute-start | bytes 2752520 | tf_op jit(solution)/shard_map/ppermute | solution.py:66
  135.3 66.7 %collective-permute-start.24 = (bf16[64,8192]{1,0:T(8,128)(2,1)}, bf16[64,8192]{1,0:T(8,128)(2,1)}, u32[]{:S(2)}, u32[]{:S(2)}) collective-permute-start(bf16[64,8192]{1,0:T(8,128)(2,1)} %get-tuple-element.72.refs_1_), channel_id=1, source_target_pairs={{0,4},{1,5},{2,6},{3,7},{4,0},{5,1},{6,2},{7,3},{8,12},{9,13},{10,... | collective-permute-start | bytes 3145736 | tf_op jit(solution)/shard_map/ppermute | solution.py:62
  154.6 47.4 %collective-permute-start.23 = (bf16[64,8192]{1,0:T(8,128)(2,1)}, bf16[64,8192]{1,0:T(8,128)(2,1)}, u32[]{:S(2)}, u32[]{:S(2)}) collective-permute-start(bf16[64,8192]{1,0:T(8,128)(2,1)} %broadcast_select_fusion.refs_1_), channel_id=1, source_target_pairs={{0,2},{1,3},{2,0},{3,1},{4,6},{5,7},{6,4},{7,5},{8,10},{9,11},{10,... | collective-permute-start | bytes 3145736 | tf_op jit(solution)/shard_map/ppermute | solution.py:62
  155.2 46.7 %collective-permute-start.25 = (bf16[64,7168]{1,0:T(8,128)(2,1)}, bf16[64,7168]{1,0:T(8,128)(2,1)S(1)}, u32[]{:S(2)}, u32[]{:S(2)}) collective-permute-start(bf16[64,7168]{1,0:T(8,128)(2,1)} %get-tuple-element.79.refs_2_), channel_id=1, source_target_pairs={{0,16},{16,0},{1,17},{17,1},{2,18},{18,2},{3,19},{19,3},{4,20},{20... | collective-permute-start | bytes 2752520 | tf_op jit(solution)/shard_map/ppermute | solution.py:66
  156.7 49.3 %collective-permute-start = (s32[2,4]{1,0:T(2,128)S(1)}, s32[2,4]{1,0:T(2,128)S(1)}, u32[]{:S(2)}, u32[]{:S(2)}) collective-permute-start(s32[2,4]{1,0:T(2,128)S(1)} %pad_add_fusion), channel_id=1, source_target_pairs={{0,1},{1,0},{2,3},{3,2},{4,5},{5,4},{6,7},{7,6},{8,9},{9,8},{10,11... | collective-permute-start | bytes 104 | tf_op jit(solution)/shard_map/ppermute | solution.py:62
  189.9 36.2 %collective-permute-start.27 = (bf16[32,7168]{1,0:T(8,128)(2,1)}, bf16[32,7168]{1,0:T(8,128)(2,1)}, u32[]{:S(2)}, u32[]{:S(2)}) collective-permute-start(bf16[32,7168]{1,0:T(8,128)(2,1)} %slice.20), channel_id=1, source_target_pairs={{0,16},{16,0},{1,17},{17,1},{2,18},{18,2},{3,19},{19,3},{4,20},{20... | collective-permute-start | bytes 1376264 | tf_op jit(solution)/shard_map/ppermute | solution.py:66
  205.1 21.0 %collective-permute-start.26 = (bf16[32,7168]{1,0:T(8,128)(2,1)S(1)}, bf16[32,7168]{1,0:T(8,128)(2,1)S(1)}, u32[]{:S(2)}, u32[]{:S(2)}) collective-permute-start(bf16[32,7168]{1,0:T(8,128)(2,1)S(1)} %slice.19), channel_id=1, source_target_pairs={{0,2},{1,3},{2,0},{3,1},{4,6},{5,7},{6,4},{7,5},{8,10},{9,11},{10,... | collective-permute-start | bytes 1376264 | tf_op jit(solution)/shard_map/ppermute | solution.py:62
  243.2 2.6 %collective-permute-start.28 = (f32[4,512]{1,0:T(4,128)S(1)}, f32[4,512]{1,0:T(4,128)S(1)}, u32[]{:S(2)}, u32[]{:S(2)}) collective-permute-start(f32[4,512]{1,0:T(4,128)S(1)} %pad_maximum_fusion), channel_id=1, source_target_pairs={{0,1},{1,0},{2,3},{3,2},{4,5},{5,4},{6,7},{7,6},{8,9},{9,8},{10,11... | collective-permute-start | bytes 24584 | tf_op jit(solution)/shard_map/ppermute | solution.py:62
  (11 other events, 65.1 us)
Sparse Core Ops, SparseCore 0:
  8.9 32.2 all-gather.1

commit v5 on v4

v5 whole, which is shorter than its diff:
```python
import functools

import jax
import jax.numpy as jnp
from jax import lax
from jax.experimental import pallas as pl
from jax.experimental.pallas import tpu as pltpu
from jax.sharding import PartitionSpec as P

BUCKET = 128


def bucket_lengths(slot_ids):
    return BUCKET * jnp.where(
        slot_ids == 0, 1, jnp.where(slot_ids == 1, 2, jnp.where(slot_ids == 2, 4, 0))
    ).astype(jnp.int32)


def slot_matrix(slot_ids, lengths, positions):
    widths = bucket_lengths(slot_ids)
    starts = jnp.cumsum(widths) - widths
    place = jnp.arange(positions, dtype=jnp.int32)[:, None]
    inside = (place >= starts[None, :]) & (place < starts[None, :] + lengths[None, :])
    return inside.astype(jnp.float32)


def project(acts, factors):
    rows = factors.reshape(-1, factors.shape[2])
    return lax.dot_general(acts, rows, (((1,), (1,)), ((), ())), preferred_element_type=jnp.float32)


def gather_whole(hidden_acts, output_grads, query_left, query_right, bucket_ids, seq_lengths):
    tokens_here = hidden_acts.shape[0]
    rank_count = query_left.shape[1]
    left_all, right_all = (
        lax.all_gather(query_left, "dp", axis=0, tiled=True),
        lax.all_gather(query_right, "dp", axis=0, tiled=True),
    )
    left_proj = project(hidden_acts, left_all)
    right_proj = project(output_grads, right_all)
    queries = left_proj.shape[1] // rank_count
    left_terms = left_proj.reshape(tokens_here, queries, rank_count)
    right_terms = right_proj.reshape(tokens_here, queries, rank_count)
    left_terms, right_terms = lax.psum((left_terms, right_terms), "tensor")
    share_size = queries // lax.axis_size("tensor")
    first_query = lax.axis_index("tensor") * share_size
    left_terms = lax.dynamic_slice_in_dim(left_terms, first_query, share_size, 1)
    right_terms = lax.dynamic_slice_in_dim(right_terms, first_query, share_size, 1)
    token_term = jnp.sum(left_terms * right_terms, axis=2)
    slot_mask = slot_matrix(bucket_ids, seq_lengths, tokens_here)
    return jnp.dot(
        token_term.T, slot_mask, precision=lax.Precision.HIGHEST, preferred_element_type=jnp.float32
    )


CORE, COLUMN, NEAR, ACROSS, OPPOSITE = 1, 2, 4, 12, 8
LITTLE = pl.CostEstimate(flops=1, bytes_accessed=1, transcendentals=0)
VMEM_LIMIT = 63 * 1024 * 1024


def flip(array, code, count):
    return lax.ppermute(array, "dp", [(i, i ^ code) for i in range(count)])


def swap_groups(array):
    return lax.ppermute(array, "groups", [(0, 1), (1, 0)])


def after_kernel(count, merge, inside_ref, turn_ref, *refs):
    arrays, next_ref = refs[-1 - count : -1], refs[-1]
    next_ref[0] = turn_ref[0]
    if merge is not None:
        kept, over = (arrays[i] for i in merge)

        @pl.when(inside_ref[0] == 1)
        def _():
            def copy(sem):
                moved = pltpu.make_async_copy(over, kept, sem)
                moved.start()
                moved.wait()

            pl.run_scoped(copy, pltpu.SemaphoreType.DMA(()))


def after(turn, arrays, inside, merge=None, there=()):
    count = len(arrays)
    hbm = pl.BlockSpec(memory_space=pltpu.HBM)
    scalar = pl.BlockSpec(memory_space=pltpu.SMEM)
    *arrays, turn = pl.pallas_call(
        functools.partial(after_kernel, count, merge),
        out_shape=[jax.ShapeDtypeStruct(x.shape, x.dtype) for x in (*arrays, turn)],
        in_specs=[scalar] * 2 + [hbm] * (len(there) + count),
        out_specs=[hbm] * count + [scalar],
        input_output_aliases={2 + len(there) + i: i for i in range(count)},
        compiler_params=pltpu.CompilerParams(vmem_limit_bytes=VMEM_LIMIT),
        cost_estimate=LITTLE,
    )(inside, turn, *there, *arrays)
    return turn, arrays


def lines(array, pairs):
    return lax.ppermute(
        array, "dp", [(a * 4 + rest, b * 4 + rest) for a, b in pairs for rest in range(4)]
    )


def score_into(out_ref, spans_ref, terms_of, rows):
    slots = out_ref.shape[0] // 2
    place = lax.broadcasted_iota(jnp.int32, (rows, 1), 0)
    for part in range(2):
        terms = terms_of(slice(part * rows, (part + 1) * rows))
        for j in range(slots):
            k = part * slots + j
            inside = (place >= spans_ref[0, k]) & (place < spans_ref[1, k])
            out_ref[k : k + 1, :] = jnp.sum(jnp.where(inside, terms, 0.0), axis=0, keepdims=True)


def proj_kernel(count, last, turn_ref, at_ref, own_ref, other_ref, *refs):
    del at_ref
    pieces, refs = refs[:count], refs[count:]
    if last is None:
        acc_ref, next_ref = refs
    else:
        spans_ref, left_ref, second_ref, out_ref, next_ref, acc_ref = refs
    step = pl.program_id(0)
    rows = own_ref.shape[0]

    @pl.when(step == 0)
    def _():
        next_ref[0] = turn_ref[0]
        acc_ref[...] = jnp.zeros_like(acc_ref)

    factors = jnp.concatenate([p[...] for p in pieces], axis=0)
    for part, tokens in enumerate((own_ref, other_ref)):
        acc_ref[part * rows : (part + 1) * rows] += lax.dot_general(
            tokens[...], factors, (((1,), (1,)), ((), ())), preferred_element_type=jnp.float32
        )

    if last is not None:

        @pl.when(step == pl.num_programs(0) - 1)
        def _():
            def terms(here):
                if last:
                    return (left_ref[here] + second_ref[here]) * acc_ref[here]
                return (left_ref[here] + acc_ref[here]) * second_ref[here]

            score_into(out_ref, spans_ref, terms, rows)


def proj(turn, tokens, rows, pieces, first, steps, last=None, spans=None, others=()):
    depth = pieces[0].shape[1]
    block = depth // steps
    held = sum(p.shape[0] for p in pieces)
    (own, own_row), (other, other_row) = tokens
    whole = pl.BlockSpec((2 * rows, held), lambda k, turn, at: (0, 0))
    scalar = pl.BlockSpec(memory_space=pltpu.SMEM)
    if last is None:
        more_specs, more, scratch = [], (), []
        out_shape, out_spec = (2 * rows, held), whole
    else:
        more_specs, more = [scalar, whole, whole], (spans, *others)
        scratch = [pltpu.VMEM((2 * rows, held), jnp.float32)]
        out_shape = (spans.shape[1], held)
        out_spec = pl.BlockSpec(out_shape, lambda k, turn, at: (0, 0))
    out, turn_next = pl.pallas_call(
        functools.partial(proj_kernel, len(pieces), last),
        out_shape=(
            jax.ShapeDtypeStruct(out_shape, jnp.float32),
            jax.ShapeDtypeStruct((1,), jnp.int32),
        ),
        grid_spec=pltpu.PrefetchScalarGridSpec(
            num_scalar_prefetch=2,
            grid=(steps,),
            in_specs=[
                pl.BlockSpec((rows, block), lambda k, turn, at: (at[1], at[0] * steps + k)),
                pl.BlockSpec((rows, block), lambda k, turn, at: (at[2], at[0] * steps + k)),
            ]
            + [pl.BlockSpec((p.shape[0], block), lambda k, turn, at: (0, k)) for p in pieces]
            + more_specs,
            out_specs=(out_spec, scalar),
            scratch_shapes=scratch,
        ),
        compiler_params=pltpu.CompilerParams(vmem_limit_bytes=VMEM_LIMIT),
        cost_estimate=LITTLE,
    )(turn, jnp.concatenate([first, own_row, other_row]), own, other, *pieces, *more)
    return turn_next, out


def spans_of(slot_ids, lengths):
    widths = bucket_lengths(slot_ids)
    starts = jnp.cumsum(widths) - widths
    return jnp.stack([starts, starts + lengths]).astype(jnp.int32)


def relay(hidden_acts, output_grads, query_left, query_right, bucket_ids, seq_lengths):
    count = lax.axis_size("dp")
    me, group = lax.axis_index("dp"), lax.axis_index("groups")
    z = me // 4
    local, ranks = query_left.shape[:2]
    left = query_left.reshape(local * ranks, -1)
    half = left.shape[1] // 2
    send = functools.partial(flip, count=count)

    acts_there = send(hidden_acts, CORE)
    grads_there = send(output_grads, CORE)
    spans_here = spans_of(bucket_ids, seq_lengths)
    spans = jnp.concatenate([spans_here, send(spans_here, CORE)], axis=1)

    a, b, c = {}, {}, {}
    a["own"] = lax.dynamic_slice_in_dim(left, group * half, half, 1)
    c["own"] = lax.dynamic_slice_in_dim(left, (1 - group) * half, half, 1)
    b["own"] = query_right.reshape(local * ranks, -1)
    at_end = (z == 0) | (z == 3)

    def near(piece):
        return send(piece, NEAR)

    def middle(piece):
        return lines(piece, [(1, 2), (2, 1)])

    def outward(piece):
        return lines(piece, [(1, 0), (2, 3)])

    def over_x(piece):
        return send(piece, COLUMN)

    inside = (~at_end).reshape(1).astype(jnp.int32)
    mine = jnp.reshape(group, (1,)).astype(jnp.int32)
    zero = jnp.zeros((1,), jnp.int32)
    acts = ((hidden_acts, zero), (acts_there, zero))
    grads = ((output_grads, zero), (grads_there, zero))
    groups = (("own", "x", "n", "f"), ("xf", "g", "xn", "xg"))
    tokens_here = hidden_acts.shape[0]
    steps = 4

    def times_a(turn, k):
        return proj(turn, acts, tokens_here, [a[i] for i in groups[k]], mine, steps)

    def times_c(turn, k, *score):
        return proj(turn, acts, tokens_here, [c[i] for i in groups[k]], 1 - mine, steps, *score)

    def times_b(turn, k, *score):
        return proj(turn, grads, tokens_here, [b[i] for i in groups[k]], zero, steps, *score)

    a["x"] = over_x(a["own"])
    a["n"] = near(a["own"])
    a_mid = middle(a["own"])

    turn, (a["x"], a["n"], a_mid) = after(zero, [a["x"], a["n"], a_mid], inside, None, [acts_there])
    a_in = middle(a["n"])
    a_out = outward(a_mid)
    a["xn"] = over_x(a["n"])
    c["x"] = swap_groups(a["x"])

    turn, (a["f"], a_in, a["xn"], c["x"], b_own, a_mid) = after(
        turn, [a_out, a_in, a["xn"], c["x"], b["own"], a_mid], inside, (0, 5), [grads_there]
    )
    a_last = outward(a_in)
    a["xf"] = over_x(a["f"])
    c["n"] = swap_groups(a["n"])
    b_mid = middle(b_own)
    turn, a_first = times_a(turn, 0)

    turn, (a["g"], a["xf"], c["n"], b_mid, b_own, a_in) = after(
        turn, [a_last, a["xf"], c["n"], b_mid, b_own, a_in], inside, (0, 5)
    )
    b["n"] = near(b_own)
    b["x"] = over_x(b_own)
    c["f"] = swap_groups(a["f"])

    turn, (b["n"], b["x"], c["f"]) = after(turn, [b["n"], b["x"], c["f"]], inside)
    b_in = middle(b["n"])
    b_out = outward(b_mid)
    a["xg"] = over_x(a["g"])
    c["g"] = swap_groups(a["g"])
    turn, c_first = times_c(turn, 0)

    turn, (b["f"], b_in, a["xg"], c["g"], b_mid) = after(
        turn, [b_out, b_in, a["xg"], c["g"], b_mid], inside, (0, 4)
    )
    b_last = outward(b_in)
    b["xf"] = over_x(b["f"])
    c["xf"] = swap_groups(a["xf"])
    turn, score_first = times_b(turn, 0, True, spans, (a_first, c_first))

    turn, (b["g"], b["xf"], c["xf"], b_in) = after(turn, [b_last, b["xf"], c["xf"], b_in], inside, (0, 3))
    b["xg"] = over_x(b["g"])
    b["xn"] = near(b["x"])
    c["xn"] = swap_groups(a["xn"])
    turn, a_second = times_a(turn, 1)

    turn, (b["xg"], b["xn"], c["xn"], c["g"]) = after(turn, [b["xg"], b["xn"], c["xn"], c["g"]], inside)
    split = c["g"].shape[0] // 2
    c["top"] = over_x(c["g"][:split])
    c["low"] = swap_groups(a["xg"][split:])
    turn, b_second = times_b(turn, 1)
    groups = (groups[0], ("xf", "g", "xn", "top", "low"))
    turn, score_second = times_c(turn, 1, False, spans, (a_second, b_second))
    sums = [score_first, score_second]

    slots = bucket_ids.shape[0]
    ours = jnp.concatenate([x[:slots] for x in sums], axis=1)
    others = send(jnp.concatenate([x[slots:] for x in sums], axis=1), CORE)
    f_code = jnp.where(at_end, OPPOSITE, ACROSS)
    g_code = jnp.where(at_end, ACROSS, OPPOSITE)
    codes = [0, COLUMN, NEAR, f_code, f_code | COLUMN, g_code, NEAR | COLUMN, g_code | COLUMN]
    codes = jnp.stack([jnp.asarray(code, jnp.int32) for code in codes])
    owner = jnp.concatenate([me ^ codes, me ^ CORE ^ codes])
    query = owner[:, None] * local + jnp.arange(local, dtype=jnp.int32)[None, :]
    query = jnp.repeat(query.reshape(-1), ranks)
    placed = query[None, :] == jnp.arange(count * local, dtype=jnp.int32)[:, None]
    return lax.dot_general(
        placed.astype(jnp.float32),
        jnp.concatenate([ours, others], axis=1),
        (((1,), (1,)), ((), ())),
        precision=lax.Precision.HIGHEST,
        preferred_element_type=jnp.float32,
    )


def solution(mesh):
    sizes = mesh.shape
    fits = sizes["dp"] == 16 and sizes["groups"] == 2 and sizes["tensor"] == 1
    return jax.shard_map(
        relay if fits else gather_whole,
        mesh=mesh,
        in_specs=(
            P(("groups", "dp"), "tensor"),
            P(("groups", "dp"), "tensor"),
            P("dp", None, "tensor"),
            P("dp", None, "tensor"),
            P(("groups", "dp")),
            P(("groups", "dp")),
        ),
        out_specs=P("tensor", ("groups", "dp")),
        check_vma=False,
    )
```

time: 256 us -> 339 us (1.32)
  Pallas kernels: 89.3 us -> 202 us
  waiting for transfers between devices: 48.6 us -> 67.2 us
  starting transfers between devices: 69.5 us -> 52.7 us
  other arithmetic: 16.5 us -> 1 us
  between operations: 13.7 us -> 0.31 us
    pallas_call x15 -> x13, Pallas kernels: 89.3 us -> 202 us  [the longest x7 131 us: after(): pl.pallas_call(functools.partial(after_kernel, count, merge), out_shape=[...]
    ppermute x14 -> x15, starting transfers between devices: 39.9 us -> 21.7 us  [flip(): return lax.ppermute(array, 'dp', [(i, i ^ code) for i in range(count)])]
    ppermute x7, waiting for transfers between devices: 9.8 us -> 19 us  [swap_groups(): return lax.ppermute(array, 'groups', [(0, 1), (1, 0)])]
    select_n x4 -> x0, other arithmetic: 7.98 us -> none  [the longest x1 2.34 us: relay(): b['f'] = jnp.where(at_end, b_out, b_mid)]
    concatenate x6 -> x0, other arithmetic: 7.48 us -> none  [proj(): jnp.concatenate([turn, first, own_row, other_row])]
    ppermute x8, waiting for transfers between devices: 15 us -> 20.5 us  [lines(): lax.ppermute(array, 'dp', [(a * 4 + rest, b * 4 + rest) for a, b in pairs...]
    ppermute x14 -> x15, waiting for transfers between devices: 23.7 us -> 27.7 us  [flip(): return lax.ppermute(array, 'dp', [(i, i ^ code) for i in range(count)])]
    unnamed x27 -> x31, local copies, waits for them, and re-layouts: 8.76 us -> 6.83 us
  transfers between devices with their start and end apart: 30 -> 30, of which waited for: 10 -> 19; matrix products, arithmetic and copies ran while one was open for 10% -> 3% of each run, Pallas kernels for 29% -> 28%
where the time goes in v5:
time: 339 us
  Pallas kernels  202 us (60%)
  waiting for transfers between devices  67.2 us (20%)
  starting transfers between devices  52.7 us (16%)
  local copies, waits for them, and re-layouts  15.1 us (4%)
    pallas_call x7, Pallas kernels, after(): pl.pallas_call(functools.partial(after_kernel, count, merge), out_shape=[...  131 us
    pallas_call x6, Pallas kernels, proj(): pl.pallas_call(functools.partial(proj_kernel, len(pieces), last), out_sha...  70.8 us
    ppermute x15, waiting for transfers between devices, flip(): return lax.ppermute(array, 'dp', [(i, i ^ code) for i in range(count)])  27.7 us
    ppermute x8, starting transfers between devices, lines(): lax.ppermute(array, 'dp', [(a * 4 + rest, b * 4 + rest) for a, b in pairs...  23.2 us
    ppermute x15, starting transfers between devices, flip(): return lax.ppermute(array, 'dp', [(i, i ^ code) for i in range(count)])  21.7 us
    ppermute x8, waiting for transfers between devices, lines(): lax.ppermute(array, 'dp', [(a * 4 + rest, b * 4 + rest) for a, b in pairs...  20.5 us
    ppermute x7, waiting for transfers between devices, swap_groups(): return lax.ppermute(array, 'groups', [(0, 1), (1, 0)])  19 us
    ppermute x7, starting transfers between devices, swap_groups(): return lax.ppermute(array, 'groups', [(0, 1), (1, 0)])  7.86 us
  transfers between devices with their start and end apart: 30, of which 19 were waited for; matrix products, arithmetic and copies ran while one was open for 3% of the time, Pallas kernels for 28%

profile of v5, /device:TPU:9, one launch (start us, length us, event | category | flops | bytes accessed | tf_op | source)
XLA Modules:
  0.0 338.8 jit_solution(4963666823161948348)
XLA Ops:
  0.7 2.6 constant_dynamic-slice_fusion
  4.6 4.3 %collective-permute-start.3 = (bf16[64,7168]{1,0:T(8,128)(2,1)S(1)}, bf16[64,7168]{1,0:T(8,128)(2,1)S(1)}, u32[]{:S(2)}, u32[]{:S(2)}) collective-permute-start(bf16[64,7168]{1,0:T(8,128)(2,1)S(1)} %get-tuple-element.96.refs_0_), channel_id=1, source_target_pairs={{4,8},{5,9},{6,10},{7,11},{8,4},{9,5},{10,6},{11,7},{20,24},{21,25... | collective-permute-start | bytes 2752520 | tf_op jit(solution)/shard_map/ppermute | solution.py:102
  9.0 15.8 %collective-permute-done.1.refs_1_ = bf16[64,7168]{1,0:T(8,128)(2,1)S(1)} collective-permute-done((bf16[64,7168]{1,0:T(8,128)(2,1)S(1)}, bf16[64,7168]{1,0:T(8,128)(2,1)S(1)}, u32[]{:S(2)}, u32[]{:S(2)}) %collective-permute-start.1) | collective-permute-done | bytes 917536 | tf_op jit(solution)/shard_map/ppermute | solution.py:62
  25.6 2.9 collective-permute-done.3.refs_3_
  31.4 3.0 collective-permute-start.6
  36.0 2.2 copy.45.refs_5_
  38.2 11.6 %collective-permute-done.5.refs_1_ = bf16[64,7168]{1,0:T(8,128)(2,1)S(1)} collective-permute-done((bf16[64,7168]{1,0:T(8,128)(2,1)}, bf16[64,7168]{1,0:T(8,128)(2,1)S(1)}, u32[]{:S(2)}, u32[]{:S(2)}) %collective-permute-start.5) | collective-permute-done | bytes 917536 | tf_op jit(solution)/shard_map/ppermute | solution.py:102
  49.9 3.8 %collective-permute-done.6.refs_2_ = bf16[64,7168]{1,0:T(8,128)(2,1)S(1)} collective-permute-done((bf16[64,7168]{1,0:T(8,128)(2,1)}, bf16[64,7168]{1,0:T(8,128)(2,1)S(1)}, u32[]{:S(2)}, u32[]{:S(2)}) %collective-permute-start.6) | collective-permute-done | bytes 917536 | tf_op jit(solution)/shard_map/ppermute | solution.py:102
  56.2 30.0 %shard_map.65 = (bf16[64,7168]{1,0:T(8,128)(2,1)}, bf16[64,7168]{1,0:T(8,128)(2,1)}, bf16[64,7168]{1,0:T(8,128)(2,1)}, bf16[64,7168]{1,0:T(8,128)(2,1)}, bf16[64...) custom-call(s32[1]{0:T(128)} %bitcast.4.inside_ref, ...), custom_call_target="tpu_custom_call", output_to_operand_aliasing={{0}: (3, {}), {1}: (4, {}), {2}: (5, {}), {3}: (6, {}), {4}... | custom-call | flops 1 | bytes 1 | tf_op jit(solution)/shard_map/pallas_call | solution.py:89
  86.2 2.5 collective-permute-start.12
  90.3 2.2 collective-permute-start.9
  93.1 10.9 %shard_map.66 = (f32[1024,256]{1,0:T(8,128)}, s32[1]{0:T(128)}) custom-call(s32[1]{0:T(128)} %get-tuple-element.54.turn_ref, s32[3]{0:T(128)} %concatenate.29.at_ref, bf16[512,14336]{1,0:T(8,128)(2,1)} %own_ref.11, bf16[512,14336]{1,0:T(8,128)(2,1)} %collective-permute-done.refs_0_.other_ref, bf16[64,7168]{1,0:T(8,128)(2,1)} %copy-done.9, ...), custom_call_target="tpu_custom_call" | custom-call | flops 1 | bytes 1 | tf_op jit(solution)/shard_map/pallas_call | solution.py:166
  104.0 3.8 %collective-permute-done.11.refs_2_ = bf16[64,7168]{1,0:T(8,128)(2,1)} collective-permute-done((bf16[64,7168]{1,0:T(8,128)(2,1)}, bf16[64,7168]{1,0:T(8,128)(2,1)}, u32[]{:S(2)}, u32[]{:S(2)}) %collective-permute-start.11) | collective-permute-done | bytes 917536 | tf_op jit(solution)/shard_map/ppermute | solution.py:66
  109.9 30.0 %shard_map.67 = (bf16[64,7168]{1,0:T(8,128)(2,1)}, bf16[64,7168]{1,0:T(8,128)(2,1)}, bf16[64,7168]{1,0:T(8,128)(2,1)}, bf16[64,8192]{1,0:T(8,128)(2,1)}, bf16[64...) custom-call(s32[1]{0:T(128)} %bitcast.4.inside_ref, ...), custom_call_target="tpu_custom_call", output_to_operand_aliasing={{0}: (2, {}), {1}: (3, {}), {2}: (4, {}), {3}: (5, {}), {4}... | custom-call | flops 1 | bytes 1 | tf_op jit(solution)/shard_map/pallas_call | solution.py:89
  141.4 4.2 %collective-permute-start.16 = (bf16[64,8192]{1,0:T(8,128)(2,1)}, bf16[64,8192]{1,0:T(8,128)(2,1)}, u32[]{:S(2)}, u32[]{:S(2)}) collective-permute-start(bf16[64,8192]{1,0:T(8,128)(2,1)} %get-tuple-element.66.refs_4_), channel_id=1, source_target_pairs={{4,0},{5,1},{6,2},{7,3},{8,12},{9,13},{10,14},{11,15},{20,16},{21,... | collective-permute-start | bytes 3145736 | tf_op jit(solution)/shard_map/ppermute | solution.py:102
  145.6 12.0 %collective-permute-done.15.refs_2_ = bf16[64,7168]{1,0:T(8,128)(2,1)S(1)} collective-permute-done((bf16[64,7168]{1,0:T(8,128)(2,1)S(1)}, bf16[64,7168]{1,0:T(8,128)(2,1)S(1)}, u32[]{:S(2)}, u32[]{:S(2)}) %collective-permute-start.15) | collective-permute-done | bytes 917536 | tf_op jit(solution)/shard_map/ppermute | solution.py:66
  158.5 2.3 collective-permute-done.13.refs_0_
  162.1 3.2 collective-permute-start.17
  167.3 10.7 %shard_map.69 = (f32[1024,256]{1,0:T(8,128)}, s32[1]{0:T(128)}) custom-call(s32[1]{0:T(128)} %get-tuple-element.61.turn_ref, s32[3]{0:T(128)} %concatenate.30.at_ref, bf16[512,14336]{1,0:T(8,128)(2,1)} %own_ref.11, bf16[512,14336]{1,0:T(8,128)(2,1)} %collective-permute-done.refs_0_.other_ref, bf16[64,7168]{1,0:T(8,128)(2,1)} %get-tuple-element.95.refs_0_, ...), custom_call_target="tpu_custom_call" | custom-call | flops 1 | bytes 1 | tf_op jit(solution)/shard_map/pallas_call | solution.py:166
  178.0 2.7 collective-permute-done.18.refs_2_
  181.9 34.0 %shard_map.70 = (bf16[64,8192]{1,0:T(8,128)(2,1)}, bf16[64,8192]{1,0:T(8,128)(2,1)}, bf16[64,7168]{1,0:T(8,128)(2,1)}, bf16[64,7168]{1,0:T(8,128)(2,1)}, bf16[64,8192]{1,0:T(8,128)(2,1)}, /*index=5*/s32[1]{0:T(128)}) custom-call(s32[1]{0:T(128)} %bitcast.4.inside_ref, ...), custom_call_target="tpu_custom_call", output_to_operand_aliasing={{0}: (2, {}), {1}: (3, {}), {2}: (4, {}), {3}: (5, {}), {4}... | custom-call | flops 1 | bytes 1 | tf_op jit(solution)/shard_map/pallas_call | solution.py:89
  215.9 2.3 collective-permute-start.21
  220.7 8.5 %collective-permute-start.20 = (s32[2,4]{1,0:T(2,128)S(1)}, s32[2,4]{1,0:T(2,128)S(1)}, u32[]{:S(2)}, u32[]{:S(2)}) collective-permute-start(s32[2,4]{1,0:T(2,128)S(1)} %pad_add_fusion), channel_id=1, source_target_pairs={{0,1},{1,0},{2,3},{3,2},{4,5},{5,4},{6,7},{7,6},{8,9},{9,8},{10,11... | collective-permute-start | bytes 104 | tf_op jit(solution)/shard_map/ppermute | solution.py:62
  231.3 13.9 %shard_map.71 = (f32[8,256]{1,0:T(8,128)}, s32[1]{0:T(128)}) custom-call(s32[1]{0:T(128)} %get-tuple-element.69.turn_ref, s32[3]{0:T(128)} %broadcast_8_at_ref.2.at_ref, bf16[512,8192]{1,0:T(8,128)(2,1)} %own_ref.10, bf16[512,8192]{1,0:T(8,128)(2,1)} %collective-permute-done.4.refs_0_.other_ref, bf16[64,8192]{1,0:T(8,128)(2,1)} %bitcast.21, ...), custom_call_target="tpu_custom_call" | custom-call | flops 1 | bytes 1 | tf_op jit(solution)/shard_map/pallas_call | solution.py:166
  245.2 33.9 %shard_map.72 = (bf16[64,8192]{1,0:T(8,128)(2,1)}, bf16[64,8192]{1,0:T(8,128)(2,1)}, bf16[64,7168]{1,0:T(8,128)(2,1)}, bf16[64,8192]{1,0:T(8,128)(2,1)}, s32[1]{0:T(128)}) custom-call(s32[1]{0:T(128)} %bitcast.4.inside_ref, s32[1]{0:T(128)} %get-tuple-element.75.turn_ref, ...), custom_call_target="tpu_custom_call", output_to_operand_aliasing={{0}: (2, {}), {1}: (3, {}), {2}: (4, {}), {3}: (5, {})} | custom-call | flops 1 | bytes 1 | tf_op jit(solution)/shard_map/pallas_call | solution.py:89
  280.1 1.8 slice.20
  283.2 10.8 %shard_map.73 = (f32[1024,256]{1,0:T(8,128)}, s32[1]{0:T(128)}) custom-call(s32[1]{0:T(128)} %get-tuple-element.78.turn_ref, s32[3]{0:T(128)} %concatenate.29.at_ref, bf16[512,14336]{1,0:T(8,128)(2,1)} %own_ref.11, bf16[512,14336]{1,0:T(8,128)(2,1)} %collective-permute-done.refs_0_.other_ref, bf16[64,7168]{1,0:T(8,128)(2,1)} %get-tuple-element.77.refs_0_, ...), custom_call_target="tpu_custom_call" | custom-call | flops 1 | bytes 1 | tf_op jit(solution)/shard_map/pallas_call | solution.py:166
  294.0 3.2 collective-permute-done.26.refs_2_
  297.3 2.9 collective-permute-done.24.refs_0_
  302.9 11.6 %shard_map.75 = (f32[1024,256]{1,0:T(8,128)}, s32[1]{0:T(128)}) custom-call(s32[1]{0:T(128)} %get-tuple-element.84.turn_ref, s32[3]{0:T(128)} %broadcast_8_at_ref.2.at_ref, bf16[512,8192]{1,0:T(8,128)(2,1)} %own_ref.10, bf16[512,8192]{1,0:T(8,128)(2,1)} %collective-permute-done.4.refs_0_.other_ref, bf16[64,8192]{1,0:T(8,128)(2,1)} %get-tuple-element.85.refs_0_, ...), custom_call_target="tpu_custom_call" | custom-call | flops 1 | bytes 1 | tf_op jit(solution)/shard_map/pallas_call | solution.py:166
  315.3 12.9 %shard_map.76 = (f32[8,256]{1,0:T(8,128)}, s32[1]{0:T(128)}) custom-call(s32[1]{0:T(128)} %get-tuple-element.88.turn_ref, s32[3]{0:T(128)} %concatenate.30.at_ref, bf16[512,14336]{1,0:T(8,128)(2,1)} %own_ref.11, bf16[512,14336]{1,0:T(8,128)(2,1)} %collective-permute-done.refs_0_.other_ref, bf16[64,7168]{1,0:T(8,128)(2,1)} %get-tuple-element.89.refs_0_, ...), custom_call_target="tpu_custom_call" | custom-call | flops 1 | bytes 1 | tf_op jit(solution)/shard_map/pallas_call | solution.py:166
  329.0 8.1 %collective-permute-start.29 = (f32[4,512]{1,0:T(4,128)S(1)}, f32[4,512]{1,0:T(4,128)S(1)}, u32[]{:S(2)}, u32[]{:S(2)}) collective-permute-start(f32[4,512]{1,0:T(4,128)S(1)} %pad_maximum_fusion), channel_id=1, source_target_pairs={{0,1},{1,0},{2,3},{3,2},{4,5},{5,4},{6,7},{7,6},{8,9},{9,8},{10,11... | collective-permute-start | bytes 24584 | tf_op jit(solution)/shard_map/ppermute | solution.py:62
  (94 shorter events, 33.4 us)
Async XLA Ops:
  0.0 28.6 %collective-permute-start = (bf16[512,14336]{1,0:T(8,128)(2,1)}, bf16[512,14336]{1,0:T(8,128)(2,1)}, u32[]{:S(2)}, u32[]{:S(2)}) collective-permute-start(bf16[512,14336]{1,0:T(8,128)(2,1)} %own_ref.11), channel_id=1, source_target_pairs={{0,1},{1,0},{2,3},{3,2},{4,5},{5,4},{6,7},{7,6},{8,9},{9,8},{10,11... | collective-permute-start | bytes 44040200 | tf_op jit(solution)/shard_map/ppermute | solution.py:62
  0.7 37.6 %collective-permute-start.4 = (bf16[512,8192]{1,0:T(8,128)(2,1)}, bf16[512,8192]{1,0:T(8,128)(2,1)}, u32[]{:S(2)}, u32[]{:S(2)}) collective-permute-start(bf16[512,8192]{1,0:T(8,128)(2,1)} %own_ref.10), channel_id=1, source_target_pairs={{0,1},{1,0},{2,3},{3,2},{4,5},{5,4},{6,7},{7,6},{8,9},{9,8},{10,11... | collective-permute-start | bytes 25165832 | tf_op jit(solution)/shard_map/ppermute | solution.py:62
  3.2 21.5 %collective-permute-start.1 = (bf16[64,7168]{1,0:T(8,128)(2,1)S(1)}, bf16[64,7168]{1,0:T(8,128)(2,1)S(1)}, u32[]{:S(2)}, u32[]{:S(2)}) collective-permute-start(bf16[64,7168]{1,0:T(8,128)(2,1)S(1)} %get-tuple-element.96.refs_0_), channel_id=1, source_target_pairs={{0,2},{1,3},{2,0},{3,1},{4,6},{5,7},{6,4},{7,5},{8,10},{9,11},{10,... | collective-permute-start | bytes 2752520 | tf_op jit(solution)/shard_map/ppermute | solution.py:62
  4.4 21.2 %collective-permute-start.2 = (bf16[64,7168]{1,0:T(8,128)(2,1)S(1)}, bf16[64,7168]{1,0:T(8,128)(2,1)}, u32[]{:S(2)}, u32[]{:S(2)}) collective-permute-start(bf16[64,7168]{1,0:T(8,128)(2,1)S(1)} %get-tuple-element.96.refs_0_), channel_id=1, source_target_pairs={{0,4},{1,5},{2,6},{3,7},{4,0},{5,1},{6,2},{7,3},{8,12},{9,13},{10,... | collective-permute-start | bytes 2752520 | tf_op jit(solution)/shard_map/ppermute | solution.py:62
  4.6 23.9 %collective-permute-start.3 = (bf16[64,7168]{1,0:T(8,128)(2,1)S(1)}, bf16[64,7168]{1,0:T(8,128)(2,1)S(1)}, u32[]{:S(2)}, u32[]{:S(2)}) collective-permute-start(bf16[64,7168]{1,0:T(8,128)(2,1)S(1)} %get-tuple-element.96.refs_0_), channel_id=1, source_target_pairs={{4,8},{5,9},{6,10},{7,11},{8,4},{9,5},{10,6},{11,7},{20,24},{21,25... | collective-permute-start | bytes 2752520 | tf_op jit(solution)/shard_map/ppermute | solution.py:102
  30.0 19.8 %collective-permute-start.5 = (bf16[64,7168]{1,0:T(8,128)(2,1)}, bf16[64,7168]{1,0:T(8,128)(2,1)S(1)}, u32[]{:S(2)}, u32[]{:S(2)}) collective-permute-start(bf16[64,7168]{1,0:T(8,128)(2,1)} %get-tuple-element.51.refs_6_), channel_id=1, source_target_pairs={{4,0},{5,1},{6,2},{7,3},{8,12},{9,13},{10,14},{11,15},{20,16},{21,... | collective-permute-start | bytes 2752520 | tf_op jit(solution)/shard_map/ppermute | solution.py:102
  31.4 22.3 %collective-permute-start.6 = (bf16[64,7168]{1,0:T(8,128)(2,1)}, bf16[64,7168]{1,0:T(8,128)(2,1)S(1)}, u32[]{:S(2)}, u32[]{:S(2)}) collective-permute-start(bf16[64,7168]{1,0:T(8,128)(2,1)} %get-tuple-element.52.refs_2_), channel_id=1, source_target_pairs={{4,8},{5,9},{6,10},{7,11},{8,4},{9,5},{10,6},{11,7},{20,24},{21,25... | collective-permute-start | bytes 2752520 | tf_op jit(solution)/shard_map/ppermute | solution.py:102
  34.4 19.8 %collective-permute-start.7 = (bf16[64,7168]{1,0:T(8,128)(2,1)}, bf16[64,7168]{1,0:T(8,128)(2,1)S(1)}, u32[]{:S(2)}, u32[]{:S(2)}) collective-permute-start(bf16[64,7168]{1,0:T(8,128)(2,1)} %get-tuple-element.52.refs_2_), channel_id=1, source_target_pairs={{0,2},{1,3},{2,0},{3,1},{4,6},{5,7},{6,4},{7,5},{8,10},{9,11},{10,... | collective-permute-start | bytes 2752520 | tf_op jit(solution)/shard_map/ppermute | solution.py:62
  34.7 20.5 %collective-permute-start.8 = (bf16[64,7168]{1,0:T(8,128)(2,1)}, bf16[64,7168]{1,0:T(8,128)(2,1)S(1)}, u32[]{:S(2)}, u32[]{:S(2)}) collective-permute-start(bf16[64,7168]{1,0:T(8,128)(2,1)} %get-tuple-element.53.refs_1_), channel_id=1, source_target_pairs={{0,16},{16,0},{1,17},{17,1},{2,18},{18,2},{3,19},{19,3},{4,20},{20... | collective-permute-start | bytes 2752520 | tf_op jit(solution)/shard_map/ppermute | solution.py:66
  86.2 23.7 %collective-permute-start.12 = (bf16[64,8192]{1,0:T(8,128)(2,1)}, bf16[64,8192]{1,0:T(8,128)(2,1)}, u32[]{:S(2)}, u32[]{:S(2)}) collective-permute-start(bf16[64,8192]{1,0:T(8,128)(2,1)} %get-tuple-element.58.refs_4_), channel_id=1, source_target_pairs={{4,8},{5,9},{6,10},{7,11},{8,4},{9,5},{10,6},{11,7},{20,24},{21,25... | collective-permute-start | bytes 3145736 | tf_op jit(solution)/shard_map/ppermute | solution.py:102
  88.8 19.1 %collective-permute-start.11 = (bf16[64,7168]{1,0:T(8,128)(2,1)}, bf16[64,7168]{1,0:T(8,128)(2,1)}, u32[]{:S(2)}, u32[]{:S(2)}) collective-permute-start(bf16[64,7168]{1,0:T(8,128)(2,1)} %get-tuple-element.52.refs_2_), channel_id=1, source_target_pairs={{0,16},{16,0},{1,17},{17,1},{2,18},{18,2},{3,19},{19,3},{4,20},{20... | collective-permute-start | bytes 2752520 | tf_op jit(solution)/shard_map/ppermute | solution.py:66
  90.1 18.7 %collective-permute-start.10 = (bf16[64,7168]{1,0:T(8,128)(2,1)}, bf16[64,7168]{1,0:T(8,128)(2,1)}, u32[]{:S(2)}, u32[]{:S(2)}) collective-permute-start(bf16[64,7168]{1,0:T(8,128)(2,1)} %get-tuple-element.55.refs_3_), channel_id=1, source_target_pairs={{0,2},{1,3},{2,0},{3,1},{4,6},{5,7},{6,4},{7,5},{8,10},{9,11},{10,... | collective-permute-start | bytes 2752520 | tf_op jit(solution)/shard_map/ppermute | solution.py:62
  90.3 18.5 %collective-permute-start.9 = (bf16[64,7168]{1,0:T(8,128)(2,1)}, bf16[64,7168]{1,0:T(8,128)(2,1)}, u32[]{:S(2)}, u32[]{:S(2)}) collective-permute-start(bf16[64,7168]{1,0:T(8,128)(2,1)} %get-tuple-element.57.refs_5_), channel_id=1, source_target_pairs={{4,0},{5,1},{6,2},{7,3},{8,12},{9,13},{10,14},{11,15},{20,16},{21,... | collective-permute-start | bytes 2752520 | tf_op jit(solution)/shard_map/ppermute | solution.py:102
  139.9 20.9 %collective-permute-start.13 = (bf16[64,8192]{1,0:T(8,128)(2,1)}, bf16[64,8192]{1,0:T(8,128)(2,1)}, u32[]{:S(2)}, u32[]{:S(2)}) collective-permute-start(bf16[64,8192]{1,0:T(8,128)(2,1)} %get-tuple-element.60), channel_id=1, source_target_pairs={{0,4},{1,5},{2,6},{3,7},{4,0},{5,1},{6,2},{7,3},{8,12},{9,13},{10,... | collective-permute-start | bytes 3145736 | tf_op jit(solution)/shard_map/ppermute | solution.py:62
  140.0 20.9 %collective-permute-start.14 = (bf16[64,8192]{1,0:T(8,128)(2,1)}, bf16[64,8192]{1,0:T(8,128)(2,1)}, u32[]{:S(2)}, u32[]{:S(2)}) collective-permute-start(bf16[64,8192]{1,0:T(8,128)(2,1)} %get-tuple-element.60), channel_id=1, source_target_pairs={{0,2},{1,3},{2,0},{3,1},{4,6},{5,7},{6,4},{7,5},{8,10},{9,11},{10,... | collective-permute-start | bytes 3145736 | tf_op jit(solution)/shard_map/ppermute | solution.py:62
  140.1 17.4 %collective-permute-start.15 = (bf16[64,7168]{1,0:T(8,128)(2,1)S(1)}, bf16[64,7168]{1,0:T(8,128)(2,1)S(1)}, u32[]{:S(2)}, u32[]{:S(2)}) collective-permute-start(bf16[64,7168]{1,0:T(8,128)(2,1)S(1)} %copy-done.4), channel_id=1, source_target_pairs={{0,16},{16,0},{1,17},{17,1},{2,18},{18,2},{3,19},{19,3},{4,20},{20... | collective-permute-start | bytes 2752520 | tf_op jit(solution)/shard_map/ppermute | solution.py:66
  141.4 40.0 %collective-permute-start.16 = (bf16[64,8192]{1,0:T(8,128)(2,1)}, bf16[64,8192]{1,0:T(8,128)(2,1)}, u32[]{:S(2)}, u32[]{:S(2)}) collective-permute-start(bf16[64,8192]{1,0:T(8,128)(2,1)} %get-tuple-element.66.refs_4_), channel_id=1, source_target_pairs={{4,0},{5,1},{6,2},{7,3},{8,12},{9,13},{10,14},{11,15},{20,16},{21,... | collective-permute-start | bytes 3145736 | tf_op jit(solution)/shard_map/ppermute | solution.py:102
  162.1 19.7 %collective-permute-start.17 = (bf16[64,8192]{1,0:T(8,128)(2,1)}, bf16[64,8192]{1,0:T(8,128)(2,1)}, u32[]{:S(2)}, u32[]{:S(2)}) collective-permute-start(bf16[64,8192]{1,0:T(8,128)(2,1)} %get-tuple-element.67.refs_2_), channel_id=1, source_target_pairs={{4,8},{5,9},{6,10},{7,11},{8,4},{9,5},{10,6},{11,7},{20,24},{21,25... | collective-permute-start | bytes 3145736 | tf_op jit(solution)/shard_map/ppermute | solution.py:102
  165.3 15.4 %collective-permute-start.18 = (bf16[64,7168]{1,0:T(8,128)(2,1)}, bf16[64,7168]{1,0:T(8,128)(2,1)}, u32[]{:S(2)}, u32[]{:S(2)}) collective-permute-start(bf16[64,7168]{1,0:T(8,128)(2,1)} %get-tuple-element.68.refs_1_), channel_id=1, source_target_pairs={{0,2},{1,3},{2,0},{3,1},{4,6},{5,7},{6,4},{7,5},{8,10},{9,11},{10,... | collective-permute-start | bytes 2752520 | tf_op jit(solution)/shard_map/ppermute | solution.py:62
  165.4 15.4 %collective-permute-start.19 = (bf16[64,7168]{1,0:T(8,128)(2,1)}, bf16[64,7168]{1,0:T(8,128)(2,1)S(1)}, u32[]{:S(2)}, u32[]{:S(2)}) collective-permute-start(bf16[64,7168]{1,0:T(8,128)(2,1)} %get-tuple-element.68.refs_1_), channel_id=1, source_target_pairs={{0,16},{16,0},{1,17},{17,1},{2,18},{18,2},{3,19},{19,3},{4,20},{20... | collective-permute-start | bytes 2752520 | tf_op jit(solution)/shard_map/ppermute | solution.py:66
  167.3 53.3 %copy-start.13 = (s32[4]{0:T(128)S(1)}, s32[4]{0:T(128)}, u32[]{:S(2)}) copy-start(s32[4]{0:T(128)} %param.10) | copy-start | bytes 52
  167.3 53.4 %copy-start.14 = (s32[4]{0:T(128)S(1)}, s32[4]{0:T(128)}, u32[]{:S(2)}) copy-start(s32[4]{0:T(128)} %param.11) | copy-start | bytes 52
  215.9 29.2 %collective-permute-start.21 = (bf16[64,8192]{1,0:T(8,128)(2,1)}, bf16[64,8192]{1,0:T(8,128)(2,1)}, u32[]{:S(2)}, u32[]{:S(2)}) collective-permute-start(bf16[64,8192]{1,0:T(8,128)(2,1)} %get-tuple-element.76.refs_3_), channel_id=1, source_target_pairs={{4,0},{5,1},{6,2},{7,3},{8,12},{9,13},{10,14},{11,15},{20,16},{21,... | collective-permute-start | bytes 3145736 | tf_op jit(solution)/shard_map/ppermute | solution.py:102
  218.3 26.9 %collective-permute-start.22 = (bf16[64,8192]{1,0:T(8,128)(2,1)}, bf16[64,8192]{1,0:T(8,128)(2,1)}, u32[]{:S(2)}, u32[]{:S(2)}) collective-permute-start(bf16[64,8192]{1,0:T(8,128)(2,1)} %get-tuple-element.71.refs_3_), channel_id=1, source_target_pairs={{0,2},{1,3},{2,0},{3,1},{4,6},{5,7},{6,4},{7,5},{8,10},{9,11},{10,... | collective-permute-start | bytes 3145736 | tf_op jit(solution)/shard_map/ppermute | solution.py:62
  219.3 25.9 %collective-permute-start.23 = (bf16[64,7168]{1,0:T(8,128)(2,1)}, bf16[64,7168]{1,0:T(8,128)(2,1)}, u32[]{:S(2)}, u32[]{:S(2)}) collective-permute-start(bf16[64,7168]{1,0:T(8,128)(2,1)} %get-tuple-element.77.refs_0_), channel_id=1, source_target_pairs={{0,16},{16,0},{1,17},{17,1},{2,18},{18,2},{3,19},{19,3},{4,20},{20... | collective-permute-start | bytes 2752520 | tf_op jit(solution)/shard_map/ppermute | solution.py:66
  220.7 9.3 %collective-permute-start.20 = (s32[2,4]{1,0:T(2,128)S(1)}, s32[2,4]{1,0:T(2,128)S(1)}, u32[]{:S(2)}, u32[]{:S(2)}) collective-permute-start(s32[2,4]{1,0:T(2,128)S(1)} %pad_add_fusion), channel_id=1, source_target_pairs={{0,1},{1,0},{2,3},{3,2},{4,5},{5,4},{6,7},{7,6},{8,9},{9,8},{10,11... | collective-permute-start | bytes 104 | tf_op jit(solution)/shard_map/ppermute | solution.py:62
  230.7 66.6 %collective-permute-start.25 = (bf16[64,8192]{1,0:T(8,128)(2,1)}, bf16[64,8192]{1,0:T(8,128)(2,1)}, u32[]{:S(2)}, u32[]{:S(2)}) collective-permute-start(bf16[64,8192]{1,0:T(8,128)(2,1)} %get-tuple-element.70.refs_1_), channel_id=1, source_target_pairs={{0,4},{1,5},{2,6},{3,7},{4,0},{5,1},{6,2},{7,3},{8,12},{9,13},{10,... | collective-permute-start | bytes 3145736 | tf_op jit(solution)/shard_map/ppermute | solution.py:62
  279.1 21.0 %collective-permute-start.24 = (bf16[64,8192]{1,0:T(8,128)(2,1)}, bf16[64,8192]{1,0:T(8,128)(2,1)}, u32[]{:S(2)}, u32[]{:S(2)}) collective-permute-start(bf16[64,8192]{1,0:T(8,128)(2,1)} %get-tuple-element.82.refs_1_), channel_id=1, source_target_pairs={{0,2},{1,3},{2,0},{3,1},{4,6},{5,7},{6,4},{7,5},{8,10},{9,11},{10,... | collective-permute-start | bytes 3145736 | tf_op jit(solution)/shard_map/ppermute | solution.py:62
  279.8 17.4 %collective-permute-start.26 = (bf16[64,7168]{1,0:T(8,128)(2,1)S(1)}, bf16[64,7168]{1,0:T(8,128)(2,1)}, u32[]{:S(2)}, u32[]{:S(2)}) collective-permute-start(bf16[64,7168]{1,0:T(8,128)(2,1)S(1)} %copy-done.6), channel_id=1, source_target_pairs={{0,16},{16,0},{1,17},{17,1},{2,18},{18,2},{3,19},{19,3},{4,20},{20... | collective-permute-start | bytes 2752520 | tf_op jit(solution)/shard_map/ppermute | solution.py:66
  281.9 32.6 %collective-permute-start.28 = (bf16[32,7168]{1,0:T(8,128)(2,1)}, bf16[32,7168]{1,0:T(8,128)(2,1)}, u32[]{:S(2)}, u32[]{:S(2)}) collective-permute-start(bf16[32,7168]{1,0:T(8,128)(2,1)} %slice.20), channel_id=1, source_target_pairs={{0,16},{16,0},{1,17},{17,1},{2,18},{18,2},{3,19},{19,3},{4,20},{20... | collective-permute-start | bytes 1376264 | tf_op jit(solution)/shard_map/ppermute | solution.py:66
  302.4 12.2 %collective-permute-start.27 = (bf16[32,7168]{1,0:T(8,128)(2,1)S(1)}, bf16[32,7168]{1,0:T(8,128)(2,1)S(1)}, u32[]{:S(2)}, u32[]{:S(2)}) collective-permute-start(bf16[32,7168]{1,0:T(8,128)(2,1)S(1)} %slice.19), channel_id=1, source_target_pairs={{0,2},{1,3},{2,0},{3,1},{4,6},{5,7},{6,4},{7,5},{8,10},{9,11},{10,... | collective-permute-start | bytes 1376264 | tf_op jit(solution)/shard_map/ppermute | solution.py:62
  329.0 9.0 %collective-permute-start.29 = (f32[4,512]{1,0:T(4,128)S(1)}, f32[4,512]{1,0:T(4,128)S(1)}, u32[]{:S(2)}, u32[]{:S(2)}) collective-permute-start(f32[4,512]{1,0:T(4,128)S(1)} %pad_maximum_fusion), channel_id=1, source_target_pairs={{0,1},{1,0},{2,3},{3,2},{4,5},{5,4},{6,7},{7,6},{8,9},{9,8},{10,11... | collective-permute-start | bytes 24584 | tf_op jit(solution)/shard_map/ppermute | solution.py:62
  (13 other events, 156.4 us)

commit v6 on v5

--- a/solution.py
+++ b/solution.py
@@ -66,24 +66,40 @@
     return lax.ppermute(array, "groups", [(0, 1), (1, 0)])
 
 
+PARTS = 4
+
+
 def after_kernel(count, merge, inside_ref, turn_ref, *refs):
-    arrays, next_ref = refs[-1 - count : -1], refs[-1]
-    next_ref[0] = turn_ref[0]
-    if merge is not None:
+    if merge is None:
+        next_ref = refs[-1]
+    else:
+        refs, (held, arrived, gone) = refs[:-3], refs[-3:]
+        arrays, next_ref = refs[-1 - count : -1], refs[-1]
         kept, over = (arrays[i] for i in merge)
+        rows = held.shape[0] // PARTS
 
         @pl.when(inside_ref[0] == 1)
         def _():
-            def copy(sem):
-                moved = pltpu.make_async_copy(over, kept, sem)
-                moved.start()
-                moved.wait()
-
-            pl.run_scoped(copy, pltpu.SemaphoreType.DMA(()))
+            parts = [pl.ds(i * rows, rows) for i in range(PARTS)]
+            come = [pltpu.make_async_copy(over.at[p], held.at[p], arrived.at[i]) for i, p in enumerate(parts)]
+            go = [pltpu.make_async_copy(held.at[p], kept.at[p], gone.at[i]) for i, p in enumerate(parts)]
+            for copy in come:
+                copy.start()
+            for first, second in zip(come, go):
+                first.wait()
+                second.start()
+            for copy in go:
+                copy.wait()
+
+    next_ref[0] = turn_ref[0]
 
 
 def after(turn, arrays, inside, merge=None, there=()):
     count = len(arrays)
+    scratch = []
+    if merge is not None:
+        kept = arrays[merge[0]]
+        scratch = [pltpu.VMEM(kept.shape, kept.dtype)] + [pltpu.SemaphoreType.DMA((PARTS,))] * 2
     hbm = pl.BlockSpec(memory_space=pltpu.HBM)
     scalar = pl.BlockSpec(memory_space=pltpu.SMEM)
     *arrays, turn = pl.pallas_call(
@@ -92,6 +108,7 @@
         in_specs=[scalar] * 2 + [hbm] * (len(there) + count),
         out_specs=[hbm] * count + [scalar],
         input_output_aliases={2 + len(there) + i: i for i in range(count)},
+        scratch_shapes=scratch,
         compiler_params=pltpu.CompilerParams(vmem_limit_bytes=VMEM_LIMIT),
         cost_estimate=LITTLE,
     )(inside, turn, *there, *arrays)
@@ -187,6 +204,77 @@
     return turn_next, out
 
 
+def own_kernel(lefts, turn_ref, at_ref, acts_ref, grads_ref, left_ref, right_ref, spans_ref, before_ref, *refs):
+    out_ref, next_ref, left_acc, right_acc = refs[-4:]
+    step = pl.program_id(0)
+
+    def add(acc_ref, tokens_ref, factors_ref):
+        acc_ref[...] += lax.dot_general(
+            tokens_ref[...], factors_ref[...], (((1,), (1,)), ((), ())), preferred_element_type=jnp.float32
+        )
+
+    @pl.when(step == 0)
+    def _():
+        next_ref[0] = turn_ref[0]
+        out_ref[...] = before_ref[...]
+        left_acc[...] = jnp.zeros_like(left_acc)
+        right_acc[...] = jnp.zeros_like(right_acc)
+
+    @pl.when((at_ref[0] == 1) & (step < lefts))
+    def _():
+        add(left_acc, acts_ref, left_ref)
+
+    @pl.when((at_ref[0] == 1) & (step >= lefts))
+    def _():
+        add(right_acc, grads_ref, right_ref)
+
+    @pl.when((at_ref[0] == 1) & (step == pl.num_programs(0) - 1))
+    def _():
+        terms = left_acc[...] * right_acc[...]
+        place = lax.broadcasted_iota(jnp.int32, (terms.shape[0], 1), 0)
+        for j in range(out_ref.shape[0]):
+            inside = (place >= spans_ref[0, j]) & (place < spans_ref[1, j])
+            out_ref[j : j + 1, :] = jnp.sum(jnp.where(inside, terms, 0.0), axis=0, keepdims=True)
+
+
+def own_scores(turn, works, acts, grads, left, right, spans, before, passed, block=2048):
+    lefts, rights = left.shape[1] // block, right.shape[1] // block
+    rows, held = acts.shape[0], left.shape[0]
+    scalar = pl.BlockSpec(memory_space=pltpu.SMEM)
+    hbm = pl.BlockSpec(memory_space=pltpu.HBM)
+    small = pl.BlockSpec(before.shape, lambda k, turn, at: (0, 0))
+
+    def at_left(k, turn, at):
+        return (0, at[0] * jnp.minimum(k, lefts - 1))
+
+    def at_right(k, turn, at):
+        return (0, at[0] * jnp.maximum(k - lefts, 0))
+
+    *passed, out, turn = pl.pallas_call(
+        functools.partial(own_kernel, lefts),
+        out_shape=[jax.ShapeDtypeStruct(x.shape, x.dtype) for x in (*passed, before, turn)],
+        grid_spec=pltpu.PrefetchScalarGridSpec(
+            num_scalar_prefetch=2,
+            grid=(lefts + rights,),
+            in_specs=[
+                pl.BlockSpec((rows, block), at_left),
+                pl.BlockSpec((rows, block), at_right),
+                pl.BlockSpec((held, block), at_left),
+                pl.BlockSpec((held, block), at_right),
+                scalar,
+                small,
+            ]
+            + [hbm] * len(passed),
+            out_specs=[hbm] * len(passed) + [small, scalar],
+            scratch_shapes=[pltpu.VMEM((rows, held), jnp.float32)] * 2,
+        ),
+        input_output_aliases={8 + i: i for i in range(len(passed))},
+        compiler_params=pltpu.CompilerParams(vmem_limit_bytes=VMEM_LIMIT),
+        cost_estimate=LITTLE,
+    )(turn, works, acts, grads, left, right, spans, before, *passed)
+    return turn, out, passed
+
+
 def spans_of(slot_ids, lengths):
     widths = bucket_lengths(slot_ids)
     starts = jnp.cumsum(widths) - widths
@@ -209,7 +297,6 @@
 
     a, b, c = {}, {}, {}
     a["own"] = lax.dynamic_slice_in_dim(left, group * half, half, 1)
-    c["own"] = lax.dynamic_slice_in_dim(left, (1 - group) * half, half, 1)
     b["own"] = query_right.reshape(local * ranks, -1)
     at_end = (z == 0) | (z == 3)
 
@@ -230,7 +317,7 @@
     zero = jnp.zeros((1,), jnp.int32)
     acts = ((hidden_acts, zero), (acts_there, zero))
     grads = ((output_grads, zero), (grads_there, zero))
-    groups = (("own", "x", "n", "f"), ("xf", "g", "xn", "xg"))
+    groups = (("x", "n", "f"), ("xf", "g", "xn", "xg"))
     tokens_here = hidden_acts.shape[0]
     steps = 4
 
@@ -242,12 +329,18 @@
 
     def times_b(turn, k, *score):
         return proj(turn, grads, tokens_here, [b[i] for i in groups[k]], zero, steps, *score)
+
+    core = (me & CORE).reshape(1).astype(jnp.int32)
+    none = jnp.zeros((bucket_ids.shape[0], local * ranks), jnp.float32)
+    here = (hidden_acts, output_grads, left, b["own"], spans_here)
+    turn, own_first, (a["own"],) = own_scores(zero, core, *here, none, [a["own"]])
 
     a["x"] = over_x(a["own"])
     a["n"] = near(a["own"])
     a_mid = middle(a["own"])
 
-    turn, (a["x"], a["n"], a_mid) = after(zero, [a["x"], a["n"], a_mid], inside, None, [acts_there])
+    turn, own_first, _ = own_scores(turn, 1 - core, *here, own_first, [])
+    turn, (a["x"], a["n"], a_mid) = after(turn, [a["x"], a["n"], a_mid], inside, None, [acts_there])
     a_in = middle(a["n"])
     a_out = outward(a_mid)
     a["xn"] = over_x(a["n"])
@@ -268,6 +361,8 @@
     b["n"] = near(b_own)
     b["x"] = over_x(b_own)
     c["f"] = swap_groups(a["f"])
+    there = (acts_there, grads_there, left, b["own"], spans[:, bucket_ids.shape[0] :])
+    turn, own_second, _ = own_scores(turn, zero + 1, *there, none, [])
 
     turn, (b["n"], b["x"], c["f"]) = after(turn, [b["n"], b["x"], c["f"]], inside)
     b_in = middle(b["n"])
@@ -300,8 +395,8 @@
     sums = [score_first, score_second]
 
     slots = bucket_ids.shape[0]
-    ours = jnp.concatenate([x[:slots] for x in sums], axis=1)
-    others = send(jnp.concatenate([x[slots:] for x in sums], axis=1), CORE)
+    ours = jnp.concatenate([own_first] + [x[:slots] for x in sums], axis=1)
+    others = send(jnp.concatenate([own_second] + [x[slots:] for x in sums], axis=1), CORE)
     f_code = jnp.where(at_end, OPPOSITE, ACROSS)
     g_code = jnp.where(at_end, ACROSS, OPPOSITE)
     codes = [0, COLUMN, NEAR, f_code, f_code | COLUMN, g_code, NEAR | COLUMN, g_code | COLUMN]

time: 339 us -> 239 us (0.71)
  Pallas kernels: 202 us -> 124 us
  starting transfers between devices: 52.7 us -> 38.4 us
  waiting for transfers between devices: 67.2 us -> 56.8 us
    pallas_call x7, Pallas kernels: 131 us -> 16 us  [after(): pl.pallas_call(functools.partial(after_kernel, count, merge), out_shape=[...]
    pallas_call x0 -> x3, Pallas kernels: none -> 37.6 us  [own_scores(): pl.pallas_call(functools.partial(own_kernel, lefts), out_shape=[jax.Shape...]
    ppermute x15, starting transfers between devices: 21.7 us -> 9.22 us  [flip(): return lax.ppermute(array, 'dp', [(i, i ^ code) for i in range(count)])]
    ppermute x15, waiting for transfers between devices: 27.7 us -> 20 us  [flip(): return lax.ppermute(array, 'dp', [(i, i ^ code) for i in range(count)])]
  transfers between devices with their start and end apart: 30 -> 30, of which waited for: 19 -> 19; matrix products, arithmetic and copies ran while one was open for 3% -> 5% of each run, Pallas kernels for 28% -> 43%
where the time goes in v6:
time: 239 us; the launch traced here: 238 us
  Pallas kernels  124 us (52%)
  waiting for transfers between devices  56.8 us (24%)
  starting transfers between devices  38.4 us (16%)
  local copies, waits for them, and re-layouts  14.9 us (6%)
  other arithmetic  2.92 us (1%)
    pallas_call x6, Pallas kernels, proj(): pl.pallas_call(functools.partial(proj_kernel, len(pieces), last), out_sha...  70.2 us
    pallas_call x3, Pallas kernels, own_scores(): pl.pallas_call(functools.partial(own_kernel, lefts), out_shape=[jax.Shape...  37.6 us
    ppermute x8, starting transfers between devices, lines(): lax.ppermute(array, 'dp', [(a * 4 + rest, b * 4 + rest) for a, b in pairs...  23.5 us
    ppermute x15, waiting for transfers between devices, flip(): return lax.ppermute(array, 'dp', [(i, i ^ code) for i in range(count)])  20 us
    ppermute x8, waiting for transfers between devices, lines(): lax.ppermute(array, 'dp', [(a * 4 + rest, b * 4 + rest) for a, b in pairs...  19.1 us
    ppermute x7, waiting for transfers between devices, swap_groups(): return lax.ppermute(array, 'groups', [(0, 1), (1, 0)])  17.7 us
    pallas_call x7, Pallas kernels, after(): pl.pallas_call(functools.partial(after_kernel, count, merge), out_shape=[...  16 us
    ppermute x15, starting transfers between devices, flip(): return lax.ppermute(array, 'dp', [(i, i ^ code) for i in range(count)])  9.22 us
  transfers between devices with their start and end apart: 30, of which 19 were waited for; matrix products, arithmetic and copies ran while one was open for 5% of the time, Pallas kernels for 43%

profile of v6, /device:TPU:9, one launch (start us, length us, event | category | flops | bytes accessed | tf_op | source)
XLA Modules:
  0.0 238.0 jit_solution(9115400155876992236)
XLA Ops:
  2.7 2.2 constant_dynamic-slice_fusion.refs_0_
  5.5 16.2 %shard_map.64 = (bf16[64,7168]{1,0:T(8,128)(2,1)}, f32[4,64]{1,0:T(4,128)}, s32[1]{0:T(128)}) custom-call(s32[1]{0:T(128)} %constant.21.clone.1.turn_ref, s32[1]{0:T(128)} %bitcast.4.at_ref, bf16[512,14336]{1,0:T(8,128)(2,1)} %own_ref.11, bf16[512,8192]{1,0:T(8,128)(2,1)} %own_ref.10, bf16[64,14336]{1,0:T(8,128)(2,1)} %bitcast.22, ...), custom_call_target="tpu_custom_call", output_to_operand_aliasing={{0}: (8, {})} | custom-call | flops 1 | bytes 1 | tf_op jit(solution)/shard_map/pallas_call | solution.py:253
  23.1 4.3 %collective-permute-start.3 = (bf16[64,7168]{1,0:T(8,128)(2,1)}, bf16[64,7168]{1,0:T(8,128)(2,1)S(1)}, u32[]{:S(2)}, u32[]{:S(2)}) collective-permute-start(bf16[64,7168]{1,0:T(8,128)(2,1)} %get-tuple-element.61), channel_id=1, source_target_pairs={{4,8},{5,9},{6,10},{7,11},{8,4},{9,5},{10,6},{11,7},{20,24},{21,25... | collective-permute-start | bytes 2752520 | tf_op jit(solution)/shard_map/ppermute | solution.py:119
  27.4 4.7 %shard_map.65 = (f32[4,64]{1,0:T(4,128)}, s32[1]{0:T(128)}) custom-call(s32[1]{0:T(128)} %get-tuple-element.57.turn_ref, s32[1]{0:T(128)S(6)} %sub.16.at_ref, bf16[512,14336]{1,0:T(8,128)(2,1)} %own_ref.11, bf16[512,8192]{1,0:T(8,128)(2,1)} %own_ref.10, bf16[64,14336]{1,0:T(8,128)(2,1)} %bitcast.23, bf16[64,8192]{1,0:T(8,128)(2,1)} %bitcast.26, ...), custom_call_target="tpu_custom_call" | custom-call | flops 1 | bytes 1 | tf_op jit(solution)/shard_map/pallas_call | solution.py:253
  35.5 2.9 %collective-permute-done.3.refs_3_ = bf16[64,7168]{1,0:T(8,128)(2,1)S(1)} collective-permute-done((bf16[64,7168]{1,0:T(8,128)(2,1)}, bf16[64,7168]{1,0:T(8,128)(2,1)S(1)}, u32[]{:S(2)}, u32[]{:S(2)}) %collective-permute-start.3) | collective-permute-done | bytes 917536 | tf_op jit(solution)/shard_map/ppermute | solution.py:119
  41.9 3.4 %collective-permute-start.6 = (bf16[64,7168]{1,0:T(8,128)(2,1)}, bf16[64,7168]{1,0:T(8,128)(2,1)S(1)}, u32[]{:S(2)}, u32[]{:S(2)}) collective-permute-start(bf16[64,7168]{1,0:T(8,128)(2,1)} %get-tuple-element.64.refs_1_), channel_id=1, source_target_pairs={{4,8},{5,9},{6,10},{7,11},{8,4},{9,5},{10,6},{11,7},{20,24},{21,25... | collective-permute-start | bytes 2752520 | tf_op jit(solution)/shard_map/ppermute | solution.py:119
  46.8 2.3 copy.47.refs_5_
  49.1 8.5 %collective-permute-done.5.refs_1_ = bf16[64,7168]{1,0:T(8,128)(2,1)S(1)} collective-permute-done((bf16[64,7168]{1,0:T(8,128)(2,1)}, bf16[64,7168]{1,0:T(8,128)(2,1)S(1)}, u32[]{:S(2)}, u32[]{:S(2)}) %collective-permute-start.5) | collective-permute-done | bytes 917536 | tf_op jit(solution)/shard_map/ppermute | solution.py:119
  57.6 4.0 %collective-permute-done.6.refs_2_ = bf16[64,7168]{1,0:T(8,128)(2,1)S(1)} collective-permute-done((bf16[64,7168]{1,0:T(8,128)(2,1)}, bf16[64,7168]{1,0:T(8,128)(2,1)S(1)}, u32[]{:S(2)}, u32[]{:S(2)}) %collective-permute-start.6) | collective-permute-done | bytes 917536 | tf_op jit(solution)/shard_map/ppermute | solution.py:119
  63.7 3.1 %shard_map.67 = (bf16[64,7168]{1,0:T(8,128)(2,1)}, bf16[64,7168]{1,0:T(8,128)(2,1)}, bf16[64,7168]{1,0:T(8,128)(2,1)}, bf16[64,7168]{1,0:T(8,128)(2,1)}, bf16[64...) custom-call(s32[1]{0:T(128)} %bitcast.11.inside_ref, ...), custom_call_target="tpu_custom_call", output_to_operand_aliasing={{0}: (3, {}), {1}: (4, {}), {2}: (5, {}), {3}: (6, {}), {4}... | custom-call | flops 1 | bytes 1 | tf_op jit(solution)/shard_map/pallas_call | solution.py:105
  66.8 3.6 %collective-permute-start.12 = (bf16[64,8192]{1,0:T(8,128)(2,1)}, bf16[64,8192]{1,0:T(8,128)(2,1)}, u32[]{:S(2)}, u32[]{:S(2)}) collective-permute-start(bf16[64,8192]{1,0:T(8,128)(2,1)} %get-tuple-element.70.refs_4_), channel_id=1, source_target_pairs={{4,8},{5,9},{6,10},{7,11},{8,4},{9,5},{10,6},{11,7},{20,24},{21,25... | collective-permute-start | bytes 3145736 | tf_op jit(solution)/shard_map/ppermute | solution.py:119
  72.5 2.2 collective-permute-start.9
  75.2 10.7 %shard_map.68 = (f32[1024,192]{1,0:T(8,128)}, s32[1]{0:T(128)}) custom-call(s32[1]{0:T(128)} %get-tuple-element.66.turn_ref, s32[3]{0:T(128)} %concatenate.29.at_ref, bf16[512,14336]{1,0:T(8,128)(2,1)} %own_ref.11, bf16[512,14336]{1,0:T(8,128)(2,1)} %collective-permute-done.refs_0_.other_ref.acts_ref, bf16[64,7168]{1,0:T(8,128)(2,1)} %get-tuple-element.65.refs_0_, ...), custom_call_target="tpu_custom_call" | custom-call | flops 1 | bytes 1 | tf_op jit(solution)/shard_map/pallas_call | solution.py:183
  85.9 4.1 %collective-permute-done.11.refs_2_ = bf16[64,7168]{1,0:T(8,128)(2,1)} collective-permute-done((bf16[64,7168]{1,0:T(8,128)(2,1)}, bf16[64,7168]{1,0:T(8,128)(2,1)}, u32[]{:S(2)}, u32[]{:S(2)}) %collective-permute-start.11) | collective-permute-done | bytes 917536 | tf_op jit(solution)/shard_map/ppermute | solution.py:66
  92.0 3.1 %shard_map.69 = (bf16[64,7168]{1,0:T(8,128)(2,1)}, bf16[64,7168]{1,0:T(8,128)(2,1)}, bf16[64,7168]{1,0:T(8,128)(2,1)}, bf16[64,8192]{1,0:T(8,128)(2,1)}, bf16[64...) custom-call(s32[1]{0:T(128)} %bitcast.11.inside_ref, ...), custom_call_target="tpu_custom_call", output_to_operand_aliasing={{0}: (2, {}), {1}: (3, {}), {2}: (4, {}), {3}: (5, {}), {4}... | custom-call | flops 1 | bytes 1 | tf_op jit(solution)/shard_map/pallas_call | solution.py:105
  96.3 4.3 %collective-permute-start.17 = (bf16[64,8192]{1,0:T(8,128)(2,1)}, bf16[64,8192]{1,0:T(8,128)(2,1)}, u32[]{:S(2)}, u32[]{:S(2)}) collective-permute-start(bf16[64,8192]{1,0:T(8,128)(2,1)} %get-tuple-element.79.refs_4_), channel_id=1, source_target_pairs={{4,0},{5,1},{6,2},{7,3},{8,12},{9,13},{10,14},{11,15},{20,16},{21,... | collective-permute-start | bytes 3145736 | tf_op jit(solution)/shard_map/ppermute | solution.py:119
  101.1 16.8 %shard_map.70 = (f32[4,64]{1,0:T(4,128)}, s32[1]{0:T(128)}) custom-call(s32[1]{0:T(128)} %get-tuple-element.71.turn_ref, s32[1]{0:T(128)} %constant.60.clone.1.at_ref, bf16[512,14336]{1,0:T(8,128)(2,1)} %collective-permute-done.refs_0_.other_ref.acts_ref, bf16[512,8192]{1,0:T(8,128)(2,1)} %collective-permute-done.4.refs_0_.grads_ref.other_ref, ...), custom_call_target="tpu_custom_call" | custom-call | flops 1 | bytes 1 | tf_op jit(solution)/shard_map/pallas_call | solution.py:253
  125.2 10.6 %shard_map.72 = (f32[1024,192]{1,0:T(8,128)}, s32[1]{0:T(128)}) custom-call(s32[1]{0:T(128)} %get-tuple-element.74.turn_ref, s32[3]{0:T(128)} %concatenate.30.at_ref, bf16[512,14336]{1,0:T(8,128)(2,1)} %own_ref.11, bf16[512,14336]{1,0:T(8,128)(2,1)} %collective-permute-done.refs_0_.other_ref.acts_ref, bf16[64,7168]{1,0:T(8,128)(2,1)} %get-tuple-element.75.refs_0_, ...), custom_call_target="tpu_custom_call" | custom-call | flops 1 | bytes 1 | tf_op jit(solution)/shard_map/pallas_call | solution.py:183
  135.8 8.1 %collective-permute-done.19.refs_2_ = bf16[64,7168]{1,0:T(8,128)(2,1)} collective-permute-done((bf16[64,7168]{1,0:T(8,128)(2,1)}, bf16[64,7168]{1,0:T(8,128)(2,1)}, u32[]{:S(2)}, u32[]{:S(2)}) %collective-permute-start.19) | collective-permute-done | bytes 917536 | tf_op jit(solution)/shard_map/ppermute | solution.py:62
  144.6 3.3 %collective-permute-done.18.refs_1_ = bf16[64,8192]{1,0:T(8,128)(2,1)} collective-permute-done((bf16[64,8192]{1,0:T(8,128)(2,1)}, bf16[64,8192]{1,0:T(8,128)(2,1)}, u32[]{:S(2)}, u32[]{:S(2)}) %collective-permute-start.18) | collective-permute-done | bytes 1048608 | tf_op jit(solution)/shard_map/ppermute | solution.py:119
  147.8 3.1 %shard_map.73 = (bf16[64,8192]{1,0:T(8,128)(2,1)}, bf16[64,8192]{1,0:T(8,128)(2,1)}, bf16[64,7168]{1,0:T(8,128)(2,1)}, bf16[64,7168]{1,0:T(8,128)(2,1)}, bf16[64,8192]{1,0:T(8,128)(2,1)}, /*index=5*/s32[1]{0:T(128)}) custom-call(s32[1]{0:T(128)} %bitcast.11.inside_ref, ...), custom_call_target="tpu_custom_call", output_to_operand_aliasing={{0}: (2, {}), {1}: (3, {}), {2}: (4, {}), {3}: (5, {}), {4}... | custom-call | flops 1 | bytes 1 | tf_op jit(solution)/shard_map/pallas_call | solution.py:105
  151.0 2.3 collective-permute-start.21
  155.0 13.6 %shard_map.74 = (f32[8,192]{1,0:T(8,128)}, s32[1]{0:T(128)}) custom-call(s32[1]{0:T(128)} %get-tuple-element.82.turn_ref, s32[3]{0:T(128)} %broadcast_8_at_ref.2.at_ref, bf16[512,8192]{1,0:T(8,128)(2,1)} %own_ref.10, bf16[512,8192]{1,0:T(8,128)(2,1)} %collective-permute-done.4.refs_0_.grads_ref.other_ref, bf16[64,8192]{1,0:T(8,128)(2,1)} %get-tuple-element.83.refs_0_, ...), custom_call_target="tpu_custom_call" | custom-call | flops 1 | bytes 1 | tf_op jit(solution)/shard_map/pallas_call | solution.py:183
  168.7 6.7 %collective-permute-done.23.refs_2_ = bf16[64,7168]{1,0:T(8,128)(2,1)} collective-permute-done((bf16[64,7168]{1,0:T(8,128)(2,1)}, bf16[64,7168]{1,0:T(8,128)(2,1)}, u32[]{:S(2)}, u32[]{:S(2)}) %collective-permute-start.23) | collective-permute-done | bytes 917536 | tf_op jit(solution)/shard_map/ppermute | solution.py:66
  175.3 2.4 %collective-permute-done.22.refs_1_ = bf16[64,8192]{1,0:T(8,128)(2,1)} collective-permute-done((bf16[64,8192]{1,0:T(8,128)(2,1)}, bf16[64,8192]{1,0:T(8,128)(2,1)}, u32[]{:S(2)}, u32[]{:S(2)}) %collective-permute-start.22) | collective-permute-done | bytes 1048608 | tf_op jit(solution)/shard_map/ppermute | solution.py:62
  177.8 3.1 %shard_map.75 = (bf16[64,8192]{1,0:T(8,128)(2,1)}, bf16[64,8192]{1,0:T(8,128)(2,1)}, bf16[64,7168]{1,0:T(8,128)(2,1)}, bf16[64,8192]{1,0:T(8,128)(2,1)}, s32[1]{0:T(128)}) custom-call(s32[1]{0:T(128)} %bitcast.11.inside_ref, s32[1]{0:T(128)} %get-tuple-element.88.turn_ref, ...), custom_call_target="tpu_custom_call", output_to_operand_aliasing={{0}: (2, {}), {1}: (3, {}), {2}: (4, {}), {3}: (5, {})} | custom-call | flops 1 | bytes 1 | tf_op jit(solution)/shard_map/pallas_call | solution.py:105
  185.0 10.8 %shard_map.76 = (f32[1024,256]{1,0:T(8,128)}, s32[1]{0:T(128)}) custom-call(s32[1]{0:T(128)} %get-tuple-element.91.turn_ref, s32[3]{0:T(128)} %concatenate.29.at_ref, bf16[512,14336]{1,0:T(8,128)(2,1)} %own_ref.11, bf16[512,14336]{1,0:T(8,128)(2,1)} %collective-permute-done.refs_0_.other_ref.acts_ref, bf16[64,7168]{1,0:T(8,128)(2,1)} %get-tuple-element.90.refs_0_, ...), custom_call_target="tpu_custom_call" | custom-call | flops 1 | bytes 1 | tf_op jit(solution)/shard_map/pallas_call | solution.py:183
  195.9 6.2 %collective-permute-done.26.refs_2_ = bf16[64,7168]{1,0:T(8,128)(2,1)} collective-permute-done((bf16[64,7168]{1,0:T(8,128)(2,1)S(1)}, bf16[64,7168]{1,0:T(8,128)(2,1)}, u32[]{:S(2)}, u32[]{:S(2)}) %collective-permute-start.26) | collective-permute-done | bytes 917536 | tf_op jit(solution)/shard_map/ppermute | solution.py:66
  202.1 2.5 %collective-permute-done.24.refs_0_ = bf16[64,8192]{1,0:T(8,128)(2,1)} collective-permute-done((bf16[64,8192]{1,0:T(8,128)(2,1)}, bf16[64,8192]{1,0:T(8,128)(2,1)}, u32[]{:S(2)}, u32[]{:S(2)}) %collective-permute-start.24) | collective-permute-done | bytes 1048608 | tf_op jit(solution)/shard_map/ppermute | solution.py:62
  207.7 11.6 %shard_map.78 = (f32[1024,256]{1,0:T(8,128)}, s32[1]{0:T(128)}) custom-call(s32[1]{0:T(128)} %get-tuple-element.97.turn_ref, s32[3]{0:T(128)} %broadcast_8_at_ref.2.at_ref, bf16[512,8192]{1,0:T(8,128)(2,1)} %own_ref.10, bf16[512,8192]{1,0:T(8,128)(2,1)} %collective-permute-done.4.refs_0_.grads_ref.other_ref, bf16[64,8192]{1,0:T(8,128)(2,1)} %get-tuple-element.98.refs_0_, ...), custom_call_target="tpu_custom_call" | custom-call | flops 1 | bytes 1 | tf_op jit(solution)/shard_map/pallas_call | solution.py:183
  220.1 12.9 %shard_map.79 = (f32[8,256]{1,0:T(8,128)}, s32[1]{0:T(128)}) custom-call(s32[1]{0:T(128)} %get-tuple-element.101.turn_ref, s32[3]{0:T(128)} %concatenate.30.at_ref, bf16[512,14336]{1,0:T(8,128)(2,1)} %own_ref.11, bf16[512,14336]{1,0:T(8,128)(2,1)} %collective-permute-done.refs_0_.other_ref.acts_ref, bf16[64,7168]{1,0:T(8,128)(2,1)} %get-tuple-element.102.refs_0_, ...), custom_call_target="tpu_custom_call" | custom-call | flops 1 | bytes 1 | tf_op jit(solution)/shard_map/pallas_call | solution.py:183
  233.8 2.4 %collective-permute-start.29 = (f32[4,512]{1,0:T(4,128)S(1)}, f32[4,512]{1,0:T(4,128)S(1)}, u32[]{:S(2)}, u32[]{:S(2)}) collective-permute-start(f32[4,512]{1,0:T(4,128)S(1)} %pad_maximum_fusion), channel_id=1, source_target_pairs={{0,1},{1,0},{2,3},{3,2},{4,5},{5,4},{6,7},{7,6},{8,9},{9,8},{10,11... | collective-permute-start | bytes 24584 | tf_op jit(solution)/shard_map/ppermute | solution.py:62
  (98 shorter events, 41.8 us)
Async XLA Ops:
  0.0 38.4 %collective-permute-start = (bf16[512,14336]{1,0:T(8,128)(2,1)}, bf16[512,14336]{1,0:T(8,128)(2,1)}, u32[]{:S(2)}, u32[]{:S(2)}) collective-permute-start(bf16[512,14336]{1,0:T(8,128)(2,1)} %own_ref.11), channel_id=1, source_target_pairs={{0,1},{1,0},{2,3},{3,2},{4,5},{5,4},{6,7},{7,6},{8,9},{9,8},{10,11... | collective-permute-start | bytes 44040200 | tf_op jit(solution)/shard_map/ppermute | solution.py:62
  0.7 48.4 %collective-permute-start.4 = (bf16[512,8192]{1,0:T(8,128)(2,1)}, bf16[512,8192]{1,0:T(8,128)(2,1)}, u32[]{:S(2)}, u32[]{:S(2)}) collective-permute-start(bf16[512,8192]{1,0:T(8,128)(2,1)} %own_ref.10), channel_id=1, source_target_pairs={{0,1},{1,0},{2,3},{3,2},{4,5},{5,4},{6,7},{7,6},{8,9},{9,8},{10,11... | collective-permute-start | bytes 25165832 | tf_op jit(solution)/shard_map/ppermute | solution.py:62
  21.7 12.6 %collective-permute-start.1 = (bf16[64,7168]{1,0:T(8,128)(2,1)}, bf16[64,7168]{1,0:T(8,128)(2,1)}, u32[]{:S(2)}, u32[]{:S(2)}) collective-permute-start(bf16[64,7168]{1,0:T(8,128)(2,1)} %get-tuple-element.61), channel_id=1, source_target_pairs={{0,2},{1,3},{2,0},{3,1},{4,6},{5,7},{6,4},{7,5},{8,10},{9,11},{10,... | collective-permute-start | bytes 2752520 | tf_op jit(solution)/shard_map/ppermute | solution.py:62
  22.9 12.6 %collective-permute-start.2 = (bf16[64,7168]{1,0:T(8,128)(2,1)}, bf16[64,7168]{1,0:T(8,128)(2,1)}, u32[]{:S(2)}, u32[]{:S(2)}) collective-permute-start(bf16[64,7168]{1,0:T(8,128)(2,1)} %get-tuple-element.61), channel_id=1, source_target_pairs={{0,4},{1,5},{2,6},{3,7},{4,0},{5,1},{6,2},{7,3},{8,12},{9,13},{10,... | collective-permute-start | bytes 2752520 | tf_op jit(solution)/shard_map/ppermute | solution.py:62
  23.1 15.3 %collective-permute-start.3 = (bf16[64,7168]{1,0:T(8,128)(2,1)}, bf16[64,7168]{1,0:T(8,128)(2,1)S(1)}, u32[]{:S(2)}, u32[]{:S(2)}) collective-permute-start(bf16[64,7168]{1,0:T(8,128)(2,1)} %get-tuple-element.61), channel_id=1, source_target_pairs={{4,8},{5,9},{6,10},{7,11},{8,4},{9,5},{10,6},{11,7},{20,24},{21,25... | collective-permute-start | bytes 2752520 | tf_op jit(solution)/shard_map/ppermute | solution.py:119
  40.6 17.0 %collective-permute-start.5 = (bf16[64,7168]{1,0:T(8,128)(2,1)}, bf16[64,7168]{1,0:T(8,128)(2,1)S(1)}, u32[]{:S(2)}, u32[]{:S(2)}) collective-permute-start(bf16[64,7168]{1,0:T(8,128)(2,1)} %get-tuple-element.63.refs_6_), channel_id=1, source_target_pairs={{4,0},{5,1},{6,2},{7,3},{8,12},{9,13},{10,14},{11,15},{20,16},{21,... | collective-permute-start | bytes 2752520 | tf_op jit(solution)/shard_map/ppermute | solution.py:119
  41.9 19.7 %collective-permute-start.6 = (bf16[64,7168]{1,0:T(8,128)(2,1)}, bf16[64,7168]{1,0:T(8,128)(2,1)S(1)}, u32[]{:S(2)}, u32[]{:S(2)}) collective-permute-start(bf16[64,7168]{1,0:T(8,128)(2,1)} %get-tuple-element.64.refs_1_), channel_id=1, source_target_pairs={{4,8},{5,9},{6,10},{7,11},{8,4},{9,5},{10,6},{11,7},{20,24},{21,25... | collective-permute-start | bytes 2752520 | tf_op jit(solution)/shard_map/ppermute | solution.py:119
  45.3 16.4 %collective-permute-start.7 = (bf16[64,7168]{1,0:T(8,128)(2,1)}, bf16[64,7168]{1,0:T(8,128)(2,1)S(1)}, u32[]{:S(2)}, u32[]{:S(2)}) collective-permute-start(bf16[64,7168]{1,0:T(8,128)(2,1)} %get-tuple-element.64.refs_1_), channel_id=1, source_target_pairs={{0,2},{1,3},{2,0},{3,1},{4,6},{5,7},{6,4},{7,5},{8,10},{9,11},{10,... | collective-permute-start | bytes 2752520 | tf_op jit(solution)/shard_map/ppermute | solution.py:62
  45.6 17.2 %collective-permute-start.8 = (bf16[64,7168]{1,0:T(8,128)(2,1)}, bf16[64,7168]{1,0:T(8,128)(2,1)S(1)}, u32[]{:S(2)}, u32[]{:S(2)}) collective-permute-start(bf16[64,7168]{1,0:T(8,128)(2,1)} %get-tuple-element.65.refs_0_), channel_id=1, source_target_pairs={{0,16},{16,0},{1,17},{17,1},{2,18},{18,2},{3,19},{19,3},{4,20},{20... | collective-permute-start | bytes 2752520 | tf_op jit(solution)/shard_map/ppermute | solution.py:66
  66.8 25.1 %collective-permute-start.12 = (bf16[64,8192]{1,0:T(8,128)(2,1)}, bf16[64,8192]{1,0:T(8,128)(2,1)}, u32[]{:S(2)}, u32[]{:S(2)}) collective-permute-start(bf16[64,8192]{1,0:T(8,128)(2,1)} %get-tuple-element.70.refs_4_), channel_id=1, source_target_pairs={{4,8},{5,9},{6,10},{7,11},{8,4},{9,5},{10,6},{11,7},{20,24},{21,25... | collective-permute-start | bytes 3145736 | tf_op jit(solution)/shard_map/ppermute | solution.py:119
  70.4 19.6 %collective-permute-start.11 = (bf16[64,7168]{1,0:T(8,128)(2,1)}, bf16[64,7168]{1,0:T(8,128)(2,1)}, u32[]{:S(2)}, u32[]{:S(2)}) collective-permute-start(bf16[64,7168]{1,0:T(8,128)(2,1)} %get-tuple-element.64.refs_1_), channel_id=1, source_target_pairs={{0,16},{16,0},{1,17},{17,1},{2,18},{18,2},{3,19},{19,3},{4,20},{20... | collective-permute-start | bytes 2752520 | tf_op jit(solution)/shard_map/ppermute | solution.py:66
  71.7 19.9 %collective-permute-start.10 = (bf16[64,7168]{1,0:T(8,128)(2,1)}, bf16[64,7168]{1,0:T(8,128)(2,1)}, u32[]{:S(2)}, u32[]{:S(2)}) collective-permute-start(bf16[64,7168]{1,0:T(8,128)(2,1)} %get-tuple-element.67.refs_2_), channel_id=1, source_target_pairs={{0,2},{1,3},{2,0},{3,1},{4,6},{5,7},{6,4},{7,5},{8,10},{9,11},{10,... | collective-permute-start | bytes 2752520 | tf_op jit(solution)/shard_map/ppermute | solution.py:62
  72.5 19.5 %collective-permute-start.9 = (bf16[64,7168]{1,0:T(8,128)(2,1)}, bf16[64,7168]{1,0:T(8,128)(2,1)}, u32[]{:S(2)}, u32[]{:S(2)}) collective-permute-start(bf16[64,7168]{1,0:T(8,128)(2,1)} %get-tuple-element.69.refs_5_), channel_id=1, source_target_pairs={{4,0},{5,1},{6,2},{7,3},{8,12},{9,13},{10,14},{11,15},{20,16},{21,... | collective-permute-start | bytes 2752520 | tf_op jit(solution)/shard_map/ppermute | solution.py:119
  95.1 23.8 %collective-permute-start.14 = (bf16[64,8192]{1,0:T(8,128)(2,1)}, bf16[64,8192]{1,0:T(8,128)(2,1)}, u32[]{:S(2)}, u32[]{:S(2)}) collective-permute-start(bf16[64,8192]{1,0:T(8,128)(2,1)} %get-tuple-element.73), channel_id=1, source_target_pairs={{0,4},{1,5},{2,6},{3,7},{4,0},{5,1},{6,2},{7,3},{8,12},{9,13},{10,... | collective-permute-start | bytes 3145736 | tf_op jit(solution)/shard_map/ppermute | solution.py:62
  95.2 24.3 %collective-permute-start.15 = (bf16[64,8192]{1,0:T(8,128)(2,1)}, bf16[64,8192]{1,0:T(8,128)(2,1)}, u32[]{:S(2)}, u32[]{:S(2)}) collective-permute-start(bf16[64,8192]{1,0:T(8,128)(2,1)} %get-tuple-element.73), channel_id=1, source_target_pairs={{0,2},{1,3},{2,0},{3,1},{4,6},{5,7},{6,4},{7,5},{8,10},{9,11},{10,... | collective-permute-start | bytes 3145736 | tf_op jit(solution)/shard_map/ppermute | solution.py:62
  95.9 22.0 %collective-permute-start.16 = (bf16[64,7168]{1,0:T(8,128)(2,1)S(1)}, bf16[64,7168]{1,0:T(8,128)(2,1)}, u32[]{:S(2)}, u32[]{:S(2)}) collective-permute-start(bf16[64,7168]{1,0:T(8,128)(2,1)S(1)} %copy-done.4), channel_id=1, source_target_pairs={{0,16},{16,0},{1,17},{17,1},{2,18},{18,2},{3,19},{19,3},{4,20},{20... | collective-permute-start | bytes 2752520 | tf_op jit(solution)/shard_map/ppermute | solution.py:66
  96.3 4.3 %collective-permute-start.13 = (s32[2,4]{1,0:T(2,128)S(1)}, s32[2,4]{1,0:T(2,128)S(1)}, u32[]{:S(2)}, u32[]{:S(2)}) collective-permute-start(s32[2,4]{1,0:T(2,128)S(1)} %copy-done.9), channel_id=1, source_target_pairs={{0,1},{1,0},{2,3},{3,2},{4,5},{5,4},{6,7},{7,6},{8,9},{9,8},{10,11... | collective-permute-start | bytes 104 | tf_op jit(solution)/shard_map/ppermute | solution.py:62
  96.3 48.3 %collective-permute-start.17 = (bf16[64,8192]{1,0:T(8,128)(2,1)}, bf16[64,8192]{1,0:T(8,128)(2,1)}, u32[]{:S(2)}, u32[]{:S(2)}) collective-permute-start(bf16[64,8192]{1,0:T(8,128)(2,1)} %get-tuple-element.79.refs_4_), channel_id=1, source_target_pairs={{4,0},{5,1},{6,2},{7,3},{8,12},{9,13},{10,14},{11,15},{20,16},{21,... | collective-permute-start | bytes 3145736 | tf_op jit(solution)/shard_map/ppermute | solution.py:119
  120.6 27.3 %collective-permute-start.18 = (bf16[64,8192]{1,0:T(8,128)(2,1)}, bf16[64,8192]{1,0:T(8,128)(2,1)}, u32[]{:S(2)}, u32[]{:S(2)}) collective-permute-start(bf16[64,8192]{1,0:T(8,128)(2,1)} %get-tuple-element.80.refs_1_), channel_id=1, source_target_pairs={{4,8},{5,9},{6,10},{7,11},{8,4},{9,5},{10,6},{11,7},{20,24},{21,25... | collective-permute-start | bytes 3145736 | tf_op jit(solution)/shard_map/ppermute | solution.py:119
  122.7 21.2 %collective-permute-start.19 = (bf16[64,7168]{1,0:T(8,128)(2,1)}, bf16[64,7168]{1,0:T(8,128)(2,1)}, u32[]{:S(2)}, u32[]{:S(2)}) collective-permute-start(bf16[64,7168]{1,0:T(8,128)(2,1)} %get-tuple-element.81.refs_1_), channel_id=1, source_target_pairs={{0,2},{1,3},{2,0},{3,1},{4,6},{5,7},{6,4},{7,5},{8,10},{9,11},{10,... | collective-permute-start | bytes 2752520 | tf_op jit(solution)/shard_map/ppermute | solution.py:62
  123.4 21.2 %collective-permute-start.20 = (bf16[64,7168]{1,0:T(8,128)(2,1)}, bf16[64,7168]{1,0:T(8,128)(2,1)S(1)}, u32[]{:S(2)}, u32[]{:S(2)}) collective-permute-start(bf16[64,7168]{1,0:T(8,128)(2,1)} %get-tuple-element.81.refs_1_), channel_id=1, source_target_pairs={{0,16},{16,0},{1,17},{17,1},{2,18},{18,2},{3,19},{19,3},{4,20},{20... | collective-permute-start | bytes 2752520 | tf_op jit(solution)/shard_map/ppermute | solution.py:66
  125.2 28.6 %copy-start.12 = (s32[2,4]{1,0:T(2,128)S(1)}, s32[2,4]{1,0:T(2,128)}, u32[]{:S(2)}) copy-start(s32[2,4]{1,0:T(2,128)} %copy-done.11) | copy-start | bytes 100
  151.0 24.3 %collective-permute-start.21 = (bf16[64,8192]{1,0:T(8,128)(2,1)}, bf16[64,8192]{1,0:T(8,128)(2,1)}, u32[]{:S(2)}, u32[]{:S(2)}) collective-permute-start(bf16[64,8192]{1,0:T(8,128)(2,1)} %get-tuple-element.89.refs_3_), channel_id=1, source_target_pairs={{4,0},{5,1},{6,2},{7,3},{8,12},{9,13},{10,14},{11,15},{20,16},{21,... | collective-permute-start | bytes 3145736 | tf_op jit(solution)/shard_map/ppermute | solution.py:119
  153.3 24.5 %collective-permute-start.22 = (bf16[64,8192]{1,0:T(8,128)(2,1)}, bf16[64,8192]{1,0:T(8,128)(2,1)}, u32[]{:S(2)}, u32[]{:S(2)}) collective-permute-start(bf16[64,8192]{1,0:T(8,128)(2,1)} %get-tuple-element.84.refs_2_), channel_id=1, source_target_pairs={{0,2},{1,3},{2,0},{3,1},{4,6},{5,7},{6,4},{7,5},{8,10},{9,11},{10,... | collective-permute-start | bytes 3145736 | tf_op jit(solution)/shard_map/ppermute | solution.py:62
  153.8 21.5 %collective-permute-start.23 = (bf16[64,7168]{1,0:T(8,128)(2,1)}, bf16[64,7168]{1,0:T(8,128)(2,1)}, u32[]{:S(2)}, u32[]{:S(2)}) collective-permute-start(bf16[64,7168]{1,0:T(8,128)(2,1)} %get-tuple-element.90.refs_0_), channel_id=1, source_target_pairs={{0,16},{16,0},{1,17},{17,1},{2,18},{18,2},{3,19},{19,3},{4,20},{20... | collective-permute-start | bytes 2752520 | tf_op jit(solution)/shard_map/ppermute | solution.py:66
  154.4 47.7 %collective-permute-start.25 = (bf16[64,8192]{1,0:T(8,128)(2,1)}, bf16[64,8192]{1,0:T(8,128)(2,1)}, u32[]{:S(2)}, u32[]{:S(2)}) collective-permute-start(bf16[64,8192]{1,0:T(8,128)(2,1)} %get-tuple-element.83.refs_0_), channel_id=1, source_target_pairs={{0,4},{1,5},{2,6},{3,7},{4,0},{5,1},{6,2},{7,3},{8,12},{9,13},{10,... | collective-permute-start | bytes 3145736 | tf_op jit(solution)/shard_map/ppermute | solution.py:62
  155.0 26.6 %copy-start.6 = (bf16[64,7168]{1,0:T(8,128)(2,1)S(1)}, bf16[64,7168]{1,0:T(8,128)(2,1)}, u32[]{:S(2)}) copy-start(bf16[64,7168]{1,0:T(8,128)(2,1)} %get-tuple-element.92.refs_2_) | copy-start | bytes 2752516
  180.9 23.7 %collective-permute-start.24 = (bf16[64,8192]{1,0:T(8,128)(2,1)}, bf16[64,8192]{1,0:T(8,128)(2,1)}, u32[]{:S(2)}, u32[]{:S(2)}) collective-permute-start(bf16[64,8192]{1,0:T(8,128)(2,1)} %get-tuple-element.95.refs_1_), channel_id=1, source_target_pairs={{0,2},{1,3},{2,0},{3,1},{4,6},{5,7},{6,4},{7,5},{8,10},{9,11},{10,... | collective-permute-start | bytes 3145736 | tf_op jit(solution)/shard_map/ppermute | solution.py:62
  181.6 20.4 %collective-permute-start.26 = (bf16[64,7168]{1,0:T(8,128)(2,1)S(1)}, bf16[64,7168]{1,0:T(8,128)(2,1)}, u32[]{:S(2)}, u32[]{:S(2)}) collective-permute-start(bf16[64,7168]{1,0:T(8,128)(2,1)S(1)} %copy-done.6), channel_id=1, source_target_pairs={{0,16},{16,0},{1,17},{17,1},{2,18},{18,2},{3,19},{19,3},{4,20},{20... | collective-permute-start | bytes 2752520 | tf_op jit(solution)/shard_map/ppermute | solution.py:66
  183.6 35.7 %collective-permute-start.28 = (bf16[32,7168]{1,0:T(8,128)(2,1)}, bf16[32,7168]{1,0:T(8,128)(2,1)}, u32[]{:S(2)}, u32[]{:S(2)}) collective-permute-start(bf16[32,7168]{1,0:T(8,128)(2,1)} %slice.20), channel_id=1, source_target_pairs={{0,16},{16,0},{1,17},{17,1},{2,18},{18,2},{3,19},{19,3},{4,20},{20... | collective-permute-start | bytes 1376264 | tf_op jit(solution)/shard_map/ppermute | solution.py:66
  206.7 12.6 %collective-permute-start.27 = (bf16[32,7168]{1,0:T(8,128)(2,1)S(1)}, bf16[32,7168]{1,0:T(8,128)(2,1)S(1)}, u32[]{:S(2)}, u32[]{:S(2)}) collective-permute-start(bf16[32,7168]{1,0:T(8,128)(2,1)S(1)} %slice.19), channel_id=1, source_target_pairs={{0,2},{1,3},{2,0},{3,1},{4,6},{5,7},{6,4},{7,5},{8,10},{9,11},{10,... | collective-permute-start | bytes 1376264 | tf_op jit(solution)/shard_map/ppermute | solution.py:62
  233.8 3.3 %collective-permute-start.29 = (f32[4,512]{1,0:T(4,128)S(1)}, f32[4,512]{1,0:T(4,128)S(1)}, u32[]{:S(2)}, u32[]{:S(2)}) collective-permute-start(f32[4,512]{1,0:T(4,128)S(1)} %pad_maximum_fusion), channel_id=1, source_target_pairs={{0,1},{1,0},{2,3},{3,2},{4,5},{5,4},{6,7},{7,6},{8,9},{9,8},{10,11... | collective-permute-start | bytes 24584 | tf_op jit(solution)/shard_map/ppermute | solution.py:62
  (13 other events, 108.8 us)

commit v7 on v6

--- a/solution.py
+++ b/solution.py
@@ -291,7 +291,6 @@
     send = functools.partial(flip, count=count)
 
     acts_there = send(hidden_acts, CORE)
-    grads_there = send(output_grads, CORE)
     spans_here = spans_of(bucket_ids, seq_lengths)
     spans = jnp.concatenate([spans_here, send(spans_here, CORE)], axis=1)
 
@@ -309,6 +308,9 @@
     def outward(piece):
         return lines(piece, [(1, 0), (2, 3)])
 
+    def inward(piece):
+        return lines(piece, [(0, 1), (3, 2)])
+
     def over_x(piece):
         return send(piece, COLUMN)
 
@@ -316,7 +318,6 @@
     mine = jnp.reshape(group, (1,)).astype(jnp.int32)
     zero = jnp.zeros((1,), jnp.int32)
     acts = ((hidden_acts, zero), (acts_there, zero))
-    grads = ((output_grads, zero), (grads_there, zero))
     groups = (("x", "n", "f"), ("xf", "g", "xn", "xg"))
     tokens_here = hidden_acts.shape[0]
     steps = 4
@@ -330,65 +331,75 @@
     def times_b(turn, k, *score):
         return proj(turn, grads, tokens_here, [b[i] for i in groups[k]], zero, steps, *score)
 
-    core = (me & CORE).reshape(1).astype(jnp.int32)
     none = jnp.zeros((bucket_ids.shape[0], local * ranks), jnp.float32)
-    here = (hidden_acts, output_grads, left, b["own"], spans_here)
-    turn, own_first, (a["own"],) = own_scores(zero, core, *here, none, [a["own"]])
+    one = zero + 1
 
     a["x"] = over_x(a["own"])
     a["n"] = near(a["own"])
     a_mid = middle(a["own"])
-
-    turn, own_first, _ = own_scores(turn, 1 - core, *here, own_first, [])
-    turn, (a["x"], a["n"], a_mid) = after(turn, [a["x"], a["n"], a_mid], inside, None, [acts_there])
+    turn, own_first, _ = own_scores(
+        zero, one, hidden_acts, output_grads, left, b["own"], spans_here, none, []
+    )
+
+    turn, (a["x"], a["n"], a_mid, b_own) = after(
+        turn, [a["x"], a["n"], a_mid, b["own"]], inside, None, [acts_there]
+    )
+    b["x"] = over_x(b_own)
+    a_out = outward(a_mid)
     a_in = middle(a["n"])
-    a_out = outward(a_mid)
+    c["x"] = swap_groups(a["x"])
+    grads_there = send(output_grads, CORE)
+    grads = ((output_grads, zero), (grads_there, zero))
+
+    turn, (a["f"], a_in, c["x"], a_mid, b["x"], b_own) = after(
+        turn, [a_out, a_in, c["x"], a_mid, b["x"], b_own], inside, (0, 3), [grads_there]
+    )
+    a_last = outward(a_in)
     a["xn"] = over_x(a["n"])
-    c["x"] = swap_groups(a["x"])
-
-    turn, (a["f"], a_in, a["xn"], c["x"], b_own, a_mid) = after(
-        turn, [a_out, a_in, a["xn"], c["x"], b["own"], a_mid], inside, (0, 5), [grads_there]
-    )
-    a_last = outward(a_in)
     a["xf"] = over_x(a["f"])
+    b_mid = middle(b_own)
     c["n"] = swap_groups(a["n"])
-    b_mid = middle(b_own)
     turn, a_first = times_a(turn, 0)
 
-    turn, (a["g"], a["xf"], c["n"], b_mid, b_own, a_in) = after(
-        turn, [a_last, a["xf"], c["n"], b_mid, b_own, a_in], inside, (0, 5)
-    )
-    b["n"] = near(b_own)
-    b["x"] = over_x(b_own)
+    turn, (a["g"], a["xn"], b_mid, c["n"], a_in, b_own) = after(
+        turn, [a_last, a["xn"], b_mid, c["n"], a_in, b_own], inside, (0, 4)
+    )
+    b_out = outward(b_mid)
+    a["xg"] = over_x(a["g"])
+    b_near = inward(b_own)
     c["f"] = swap_groups(a["f"])
     there = (acts_there, grads_there, left, b["own"], spans[:, bucket_ids.shape[0] :])
-    turn, own_second, _ = own_scores(turn, zero + 1, *there, none, [])
-
-    turn, (b["n"], b["x"], c["f"]) = after(turn, [b["n"], b["x"], c["f"]], inside)
-    b_in = middle(b["n"])
-    b_out = outward(b_mid)
-    a["xg"] = over_x(a["g"])
+    turn, own_second, _ = own_scores(turn, one, *there, none, [])
+
+    turn, (b["f"], a["xf"], b_near, c["f"], b_mid, b_own) = after(
+        turn, [b_out, a["xf"], b_near, c["f"], b_mid, b_own], inside, (0, 4)
+    )
+    b_in = middle(b_near)
+    b_far = outward(b_own)
+    b["xf"] = over_x(b["f"])
     c["g"] = swap_groups(a["g"])
     turn, c_first = times_c(turn, 0)
 
-    turn, (b["f"], b_in, a["xg"], c["g"], b_mid) = after(
-        turn, [b_out, b_in, a["xg"], c["g"], b_mid], inside, (0, 4)
+    turn, (b["n"], b_in, a["xg"], c["g"], b_near) = after(
+        turn, [b_far, b_in, a["xg"], c["g"], b_near], inside, (0, 4)
     )
     b_last = outward(b_in)
-    b["xf"] = over_x(b["f"])
+    c["xn"] = swap_groups(a["xn"])
     c["xf"] = swap_groups(a["xf"])
-    turn, score_first = times_b(turn, 0, True, spans, (a_first, c_first))
-
-    turn, (b["g"], b["xf"], c["xf"], b_in) = after(turn, [b_last, b["xf"], c["xf"], b_in], inside, (0, 3))
+    turn, a_second = times_a(turn, 1)
+
+    split = c["g"].shape[0] // 2
+    turn, (b["g"], b["xf"], c["xn"], b_in, b_over) = after(
+        turn, [b_last, b["xf"], c["xn"], b_in, b["x"]], inside, (0, 3)
+    )
+    b["x"] = b_over
     b["xg"] = over_x(b["g"])
-    b["xn"] = near(b["x"])
-    c["xn"] = swap_groups(a["xn"])
-    turn, a_second = times_a(turn, 1)
-
-    turn, (b["xg"], b["xn"], c["xn"], c["g"]) = after(turn, [b["xg"], b["xn"], c["xn"], c["g"]], inside)
-    split = c["g"].shape[0] // 2
+    b["xn"] = near(b_over)
     c["top"] = over_x(c["g"][:split])
     c["low"] = swap_groups(a["xg"][split:])
+    turn, score_first = times_b(turn, 0, True, spans, (a_first, c_first))
+
+    turn, (b["xg"], b["xn"], c["xf"]) = after(turn, [b["xg"], b["xn"], c["xf"]], inside)
     turn, b_second = times_b(turn, 1)
     groups = (groups[0], ("xf", "g", "xn", "top", "low"))
     turn, score_second = times_c(turn, 1, False, spans, (a_second, b_second))

time: 239 us -> 239 us (level)
  starting transfers between devices: 38.4 us -> 50 us
  waiting for transfers between devices: 56.8 us -> 47 us
  Pallas kernels: 124 us -> 121 us
    ppermute x15 -> x14, starting transfers between devices: 9.22 us -> 17.7 us  [flip(): return lax.ppermute(array, 'dp', [(i, i ^ code) for i in range(count)])]
    ppermute x7, waiting for transfers between devices: 17.7 us -> 10.1 us  [swap_groups(): return lax.ppermute(array, 'groups', [(0, 1), (1, 0)])]
    ppermute x15 -> x14, waiting for transfers between devices: 20 us -> 14 us  [flip(): return lax.ppermute(array, 'dp', [(i, i ^ code) for i in range(count)])]
    pallas_call x3 -> x2, Pallas kernels: 37.6 us -> 32.9 us  [own_scores(): pl.pallas_call(functools.partial(own_kernel, lefts), out_shape=[jax.Shape...]
    ppermute x8 -> x10, waiting for transfers between devices: 19.1 us -> 22.9 us  [lines(): lax.ppermute(array, 'dp', [(a * 4 + rest, b * 4 + rest) for a, b in pairs...]
    ppermute x8 -> x10, starting transfers between devices: 23.5 us -> 25.7 us  [lines(): lax.ppermute(array, 'dp', [(a * 4 + rest, b * 4 + rest) for a, b in pairs...]
    unnamed x31 -> x29, local copies, waits for them, and re-layouts: 6.51 us -> 5.95 us
  transfers between devices with their start and end apart: 30 -> 31, of which waited for: 19 -> 13; matrix products, arithmetic and copies ran while one was open for 5% -> 6% of each run, Pallas kernels for 43% -> 40%
where the time goes in v7:
time: 239 us; the launch traced here: 237 us
  Pallas kernels  121 us (51%)
  starting transfers between devices  50 us (21%)
  waiting for transfers between devices  47 us (20%)
  local copies, waits for them, and re-layouts  14.9 us (6%)
  other arithmetic  2.97 us (1%)
    pallas_call x6, Pallas kernels, proj(): pl.pallas_call(functools.partial(proj_kernel, len(pieces), last), out_sha...  70.4 us
    pallas_call x2, Pallas kernels, own_scores(): pl.pallas_call(functools.partial(own_kernel, lefts), out_shape=[jax.Shape...  32.9 us
    ppermute x10, starting transfers between devices, lines(): lax.ppermute(array, 'dp', [(a * 4 + rest, b * 4 + rest) for a, b in pairs...  25.7 us
    ppermute x10, waiting for transfers between devices, lines(): lax.ppermute(array, 'dp', [(a * 4 + rest, b * 4 + rest) for a, b in pairs...  22.9 us
    pallas_call x7, Pallas kernels, after(): pl.pallas_call(functools.partial(after_kernel, count, merge), out_shape=[...  17.8 us
    ppermute x14, starting transfers between devices, flip(): return lax.ppermute(array, 'dp', [(i, i ^ code) for i in range(count)])  17.7 us
    ppermute x14, waiting for transfers between devices, flip(): return lax.ppermute(array, 'dp', [(i, i ^ code) for i in range(count)])  14 us
    ppermute x7, waiting for transfers between devices, swap_groups(): return lax.ppermute(array, 'groups', [(0, 1), (1, 0)])  10.1 us
  transfers between devices with their start and end apart: 31, of which 13 were waited for; matrix products, arithmetic and copies ran while one was open for 6% of the time, Pallas kernels for 40%

profile of v7, /device:TPU:9, one launch (start us, length us, event | category | flops | bytes accessed | tf_op | source)
XLA Modules:
  0.0 237.2 jit_solution(1650786801916869805)
XLA Ops:
  0.7 2.2 constant_dynamic-slice_fusion
  4.2 4.3 %collective-permute-start.3 = (bf16[64,7168]{1,0:T(8,128)(2,1)}, bf16[64,7168]{1,0:T(8,128)(2,1)S(1)}, u32[]{:S(2)}, u32[]{:S(2)}) collective-permute-start(bf16[64,7168]{1,0:T(8,128)(2,1)} %constant_dynamic-slice_fusion), channel_id=1, source_target_pairs={{4,8},{5,9},{6,10},{7,11},{8,4},{9,5},{10,6},{11,7},{20,24},{21,25... | collective-permute-start | bytes 2752520 | tf_op jit(solution)/shard_map/ppermute | solution.py:119
  11.2 16.2 %shard_map.64 = (f32[4,64]{1,0:T(4,128)}, s32[1]{0:T(128)}) custom-call(s32[1]{0:T(128)} %constant.21.clone.1.turn_ref, s32[1]{0:T(128)} %constant.18.clone.1.at_ref, bf16[512,14336]{1,0:T(8,128)(2,1)} %own_ref.11, bf16[512,8192]{1,0:T(8,128)(2,1)} %own_ref.10, bf16[64,14336]{1,0:T(8,128)(2,1)} %bitcast.21, bf16[64,8192]{1,0:T(8,128)(2,1)} %bitcast.23, ...), custom_call_target="tpu_custom_call" | custom-call | flops 1 | bytes 1 | tf_op jit(solution)/shard_map/pallas_call | solution.py:253
  27.4 2.3 copy.45.refs_4_
  33.5 1.9 collective-permute-start.6
  36.7 15.3 %collective-permute-done.5.refs_1_ = bf16[64,7168]{1,0:T(8,128)(2,1)S(1)} collective-permute-done((bf16[64,7168]{1,0:T(8,128)(2,1)}, bf16[64,7168]{1,0:T(8,128)(2,1)S(1)}, u32[]{:S(2)}, u32[]{:S(2)}) %collective-permute-start.5) | collective-permute-done | bytes 917536 | tf_op jit(solution)/shard_map/ppermute | solution.py:119
  52.1 3.9 %collective-permute-done.6.refs_2_ = bf16[64,7168]{1,0:T(8,128)(2,1)S(1)} collective-permute-done((bf16[64,7168]{1,0:T(8,128)(2,1)}, bf16[64,7168]{1,0:T(8,128)(2,1)S(1)}, u32[]{:S(2)}, u32[]{:S(2)}) %collective-permute-start.6) | collective-permute-done | bytes 917536 | tf_op jit(solution)/shard_map/ppermute | solution.py:119
  57.2 3.1 %shard_map.66 = (bf16[64,7168]{1,0:T(8,128)(2,1)}, bf16[64,7168]{1,0:T(8,128)(2,1)}, bf16[64,7168]{1,0:T(8,128)(2,1)}, bf16[64,7168]{1,0:T(8,128)(2,1)}, bf16[64...) custom-call(s32[1]{0:T(128)} %bitcast.10.inside_ref, ...), custom_call_target="tpu_custom_call", output_to_operand_aliasing={{0}: (3, {}), {1}: (4, {}), {2}: (5, {}), {3}: (6, {}), {4}... | custom-call | flops 1 | bytes 1 | tf_op jit(solution)/shard_map/pallas_call | solution.py:105
  60.3 2.9 %collective-permute-start.11 = (bf16[64,8192]{1,0:T(8,128)(2,1)}, bf16[64,8192]{1,0:T(8,128)(2,1)}, u32[]{:S(2)}, u32[]{:S(2)}) collective-permute-start(bf16[64,8192]{1,0:T(8,128)(2,1)} %get-tuple-element.68.refs_5_), channel_id=1, source_target_pairs={{4,8},{5,9},{6,10},{7,11},{8,4},{9,5},{10,6},{11,7},{20,24},{21,25... | collective-permute-start | bytes 3145736 | tf_op jit(solution)/shard_map/ppermute | solution.py:119
  65.6 2.2 collective-permute-start.9
  68.4 10.6 %shard_map.67 = (f32[1024,192]{1,0:T(8,128)}, s32[1]{0:T(128)}) custom-call(s32[1]{0:T(128)} %get-tuple-element.64.turn_ref, s32[3]{0:T(128)} %concatenate.29.at_ref, bf16[512,14336]{1,0:T(8,128)(2,1)} %own_ref.11, bf16[512,14336]{1,0:T(8,128)(2,1)} %collective-permute-done.refs_0_.other_ref.acts_ref, bf16[64,7168]{1,0:T(8,128)(2,1)} %get-tuple-element.62.refs_0_, ...), custom_call_target="tpu_custom_call" | custom-call | flops 1 | bytes 1 | tf_op jit(solution)/shard_map/pallas_call | solution.py:183
  79.0 3.5 %collective-permute-done.10.refs_1_ = bf16[64,7168]{1,0:T(8,128)(2,1)} collective-permute-done((bf16[64,7168]{1,0:T(8,128)(2,1)}, bf16[64,7168]{1,0:T(8,128)(2,1)}, u32[]{:S(2)}, u32[]{:S(2)}) %collective-permute-start.10) | collective-permute-done | bytes 917536 | tf_op jit(solution)/shard_map/ppermute | solution.py:62
  84.7 3.1 %shard_map.68 = (bf16[64,7168]{1,0:T(8,128)(2,1)}, bf16[64,7168]{1,0:T(8,128)(2,1)}, bf16[64,8192]{1,0:T(8,128)(2,1)}, bf16[64,7168]{1,0:T(8,128)(2,1)}, bf16[64...) custom-call(s32[1]{0:T(128)} %bitcast.10.inside_ref, ...), custom_call_target="tpu_custom_call", output_to_operand_aliasing={{0}: (2, {}), {1}: (3, {}), {2}: (4, {}), {3}: (5, {}), {4}... | custom-call | flops 1 | bytes 1 | tf_op jit(solution)/shard_map/pallas_call | solution.py:105
  87.8 2.3 collective-permute-start.14
  93.8 4.0 %collective-permute-start.13 = (s32[2,4]{1,0:T(2,128)S(1)}, s32[2,4]{1,0:T(2,128)S(1)}, u32[]{:S(2)}, u32[]{:S(2)}) collective-permute-start(s32[2,4]{1,0:T(2,128)S(1)} %copy-done.11), channel_id=1, source_target_pairs={{0,1},{1,0},{2,3},{3,2},{4,5},{5,4},{6,7},{7,6},{8,9},{9,8},{10,11... | collective-permute-start | bytes 104 | tf_op jit(solution)/shard_map/ppermute | solution.py:62
  99.2 16.8 %shard_map.69 = (f32[4,64]{1,0:T(4,128)}, s32[1]{0:T(128)}) custom-call(s32[1]{0:T(128)} %get-tuple-element.69.turn_ref, s32[1]{0:T(128)} %constant.18.clone.1.at_ref, bf16[512,14336]{1,0:T(8,128)(2,1)} %collective-permute-done.refs_0_.other_ref.acts_ref, bf16[512,8192]{1,0:T(8,128)(2,1)} %collective-permute-done.4.refs_0_.grads_ref.other_ref, ...), custom_call_target="tpu_custom_call" | custom-call | flops 1 | bytes 1 | tf_op jit(solution)/shard_map/pallas_call | solution.py:253
  116.0 3.1 %shard_map.70 = (bf16[64,8192]{1,0:T(8,128)(2,1)}, bf16[64,7168]{1,0:T(8,128)(2,1)}, bf16[64,8192]{1,0:T(8,128)(2,1)}, bf16[64,7168]{1,0:T(8,128)(2,1)}, bf16[64...) custom-call(s32[1]{0:T(128)} %bitcast.10.inside_ref, ...), custom_call_target="tpu_custom_call", output_to_operand_aliasing={{0}: (2, {}), {1}: (3, {}), {2}: (4, {}), {3}: (5, {}), {4}... | custom-call | flops 1 | bytes 1 | tf_op jit(solution)/shard_map/pallas_call | solution.py:105
  119.1 4.3 %collective-permute-start.18 = (bf16[64,8192]{1,0:T(8,128)(2,1)}, bf16[64,8192]{1,0:T(8,128)(2,1)}, u32[]{:S(2)}, u32[]{:S(2)}) collective-permute-start(bf16[64,8192]{1,0:T(8,128)(2,1)} %get-tuple-element.78), channel_id=1, source_target_pairs={{4,0},{5,1},{6,2},{7,3},{8,12},{9,13},{10,14},{11,15},{20,16},{21,... | collective-permute-start | bytes 3145736 | tf_op jit(solution)/shard_map/ppermute | solution.py:119
  123.4 2.8 %collective-permute-start.19 = (bf16[64,8192]{1,0:T(8,128)(2,1)}, bf16[64,8192]{1,0:T(8,128)(2,1)}, u32[]{:S(2)}, u32[]{:S(2)}) collective-permute-start(bf16[64,8192]{1,0:T(8,128)(2,1)} %get-tuple-element.79.refs_4_), channel_id=1, source_target_pairs={{4,8},{5,9},{6,10},{7,11},{8,4},{9,5},{10,6},{11,7},{20,24},{21,25... | collective-permute-start | bytes 3145736 | tf_op jit(solution)/shard_map/ppermute | solution.py:119
  128.5 10.5 %shard_map.71 = (f32[1024,192]{1,0:T(8,128)}, s32[1]{0:T(128)}) custom-call(s32[1]{0:T(128)} %get-tuple-element.73.turn_ref, s32[3]{0:T(128)} %concatenate.30.at_ref, bf16[512,14336]{1,0:T(8,128)(2,1)} %own_ref.11, bf16[512,14336]{1,0:T(8,128)(2,1)} %collective-permute-done.refs_0_.other_ref.acts_ref, bf16[64,7168]{1,0:T(8,128)(2,1)} %get-tuple-element.74.refs_0_, ...), custom_call_target="tpu_custom_call" | custom-call | flops 1 | bytes 1 | tf_op jit(solution)/shard_map/pallas_call | solution.py:183
  139.1 8.5 %collective-permute-done.20.refs_2_ = bf16[64,7168]{1,0:T(8,128)(2,1)S(1)} collective-permute-done((bf16[64,7168]{1,0:T(8,128)(2,1)}, bf16[64,7168]{1,0:T(8,128)(2,1)S(1)}, u32[]{:S(2)}, u32[]{:S(2)}) %collective-permute-start.20) | collective-permute-done | bytes 917536 | tf_op jit(solution)/shard_map/ppermute | solution.py:62
  147.7 2.1 collective-permute-done.19.refs_1_
  149.7 3.1 %shard_map.72 = (bf16[64,8192]{1,0:T(8,128)(2,1)}, bf16[64,8192]{1,0:T(8,128)(2,1)}, bf16[64,7168]{1,0:T(8,128)(2,1)}, bf16[64,7168]{1,0:T(8,128)(2,1)}, bf16[64,8192]{1,0:T(8,128)(2,1)}, /*index=5*/s32[1]{0:T(128)}) custom-call(s32[1]{0:T(128)} %bitcast.10.inside_ref, ...), custom_call_target="tpu_custom_call", output_to_operand_aliasing={{0}: (2, {}), {1}: (3, {}), {2}: (4, {}), {3}: (5, {}), {4}... | custom-call | flops 1 | bytes 1 | tf_op jit(solution)/shard_map/pallas_call | solution.py:105
  152.9 2.3 collective-permute-start.22
  155.2 11.0 %shard_map.73 = (f32[1024,256]{1,0:T(8,128)}, s32[1]{0:T(128)}) custom-call(s32[1]{0:T(128)} %get-tuple-element.81.turn_ref, s32[3]{0:T(128)} %concatenate.29.at_ref, bf16[512,14336]{1,0:T(8,128)(2,1)} %own_ref.11, bf16[512,14336]{1,0:T(8,128)(2,1)} %collective-permute-done.refs_0_.other_ref.acts_ref, bf16[64,7168]{1,0:T(8,128)(2,1)} %get-tuple-element.82.refs_0_, ...), custom_call_target="tpu_custom_call" | custom-call | flops 1 | bytes 1 | tf_op jit(solution)/shard_map/pallas_call | solution.py:183
  166.2 9.3 %collective-permute-done.24.refs_2_ = bf16[64,7168]{1,0:T(8,128)(2,1)} collective-permute-done((bf16[64,7168]{1,0:T(8,128)(2,1)}, bf16[64,7168]{1,0:T(8,128)(2,1)}, u32[]{:S(2)}, u32[]{:S(2)}) %collective-permute-start.24) | collective-permute-done | bytes 917536 | tf_op jit(solution)/shard_map/ppermute | solution.py:66
  175.5 3.1 %shard_map.74 = (bf16[64,8192]{1,0:T(8,128)(2,1)}, bf16[64,8192]{1,0:T(8,128)(2,1)}, bf16[64,7168]{1,0:T(8,128)(2,1)}, bf16[64,8192]{1,0:T(8,128)(2,1)}, bf16[64,8192]{1,0:T(8,128)(2,1)}, /*index=5*/s32[1]{0:T(128)}) custom-call(s32[1]{0:T(128)} %bitcast.10.inside_ref, ...), custom_call_target="tpu_custom_call", output_to_operand_aliasing={{0}: (2, {}), {1}: (3, {}), {2}: (4, {}), {3}: (5, {}), {4}... | custom-call | flops 1 | bytes 1 | tf_op jit(solution)/shard_map/pallas_call | solution.py:105
  180.5 1.9 slice.19
  185.8 13.6 %shard_map.75 = (f32[8,192]{1,0:T(8,128)}, s32[1]{0:T(128)}) custom-call(s32[1]{0:T(128)} %get-tuple-element.89.turn_ref, s32[3]{0:T(128)} %broadcast_8_at_ref.2.at_ref, bf16[512,8192]{1,0:T(8,128)(2,1)} %own_ref.10, bf16[512,8192]{1,0:T(8,128)(2,1)} %collective-permute-done.4.refs_0_.grads_ref.other_ref, bf16[64,8192]{1,0:T(8,128)(2,1)} %get-tuple-element.90.refs_0_, ...), custom_call_target="tpu_custom_call" | custom-call | flops 1 | bytes 1 | tf_op jit(solution)/shard_map/pallas_call | solution.py:183
  202.1 11.7 %shard_map.77 = (f32[1024,256]{1,0:T(8,128)}, s32[1]{0:T(128)}) custom-call(s32[1]{0:T(128)} %get-tuple-element.97.turn_ref, s32[3]{0:T(128)} %broadcast_8_at_ref.2.at_ref, bf16[512,8192]{1,0:T(8,128)(2,1)} %own_ref.10, bf16[512,8192]{1,0:T(8,128)(2,1)} %collective-permute-done.4.refs_0_.grads_ref.other_ref, bf16[64,8192]{1,0:T(8,128)(2,1)} %get-tuple-element.98.refs_0_, ...), custom_call_target="tpu_custom_call" | custom-call | flops 1 | bytes 1 | tf_op jit(solution)/shard_map/pallas_call | solution.py:183
  214.7 13.0 %shard_map.78 = (f32[8,256]{1,0:T(8,128)}, s32[1]{0:T(128)}) custom-call(s32[1]{0:T(128)} %get-tuple-element.101.turn_ref, s32[3]{0:T(128)} %concatenate.30.at_ref, bf16[512,14336]{1,0:T(8,128)(2,1)} %own_ref.11, bf16[512,14336]{1,0:T(8,128)(2,1)} %collective-permute-done.refs_0_.other_ref.acts_ref, bf16[64,7168]{1,0:T(8,128)(2,1)} %get-tuple-element.102.refs_0_, ...), custom_call_target="tpu_custom_call" | custom-call | flops 1 | bytes 1 | tf_op jit(solution)/shard_map/pallas_call | solution.py:183
  228.6 6.9 %collective-permute-start.30 = (f32[4,512]{1,0:T(4,128)S(1)}, f32[4,512]{1,0:T(4,128)S(1)}, u32[]{:S(2)}, u32[]{:S(2)}) collective-permute-start(f32[4,512]{1,0:T(4,128)S(1)} %pad_maximum_fusion), channel_id=1, source_target_pairs={{0,1},{1,0},{2,3},{3,2},{4,5},{5,4},{6,7},{7,6},{8,9},{9,8},{10,11... | collective-permute-start | bytes 24584 | tf_op jit(solution)/shard_map/ppermute | solution.py:62
  (97 shorter events, 35.1 us)
Async XLA Ops:
  0.0 29.8 %collective-permute-start = (bf16[512,14336]{1,0:T(8,128)(2,1)}, bf16[512,14336]{1,0:T(8,128)(2,1)}, u32[]{:S(2)}, u32[]{:S(2)}) collective-permute-start(bf16[512,14336]{1,0:T(8,128)(2,1)} %own_ref.11), channel_id=1, source_target_pairs={{0,1},{1,0},{2,3},{3,2},{4,5},{5,4},{6,7},{7,6},{8,9},{9,8},{10,11... | collective-permute-start | bytes 44040200 | tf_op jit(solution)/shard_map/ppermute | solution.py:62
  0.7 36.1 %collective-permute-start.4 = (bf16[512,8192]{1,0:T(8,128)(2,1)}, bf16[512,8192]{1,0:T(8,128)(2,1)}, u32[]{:S(2)}, u32[]{:S(2)}) collective-permute-start(bf16[512,8192]{1,0:T(8,128)(2,1)} %own_ref.10), channel_id=1, source_target_pairs={{0,1},{1,0},{2,3},{3,2},{4,5},{5,4},{6,7},{7,6},{8,9},{9,8},{10,11... | collective-permute-start | bytes 25165832 | tf_op jit(solution)/shard_map/ppermute | solution.py:62
  2.8 26.9 %collective-permute-start.1 = (bf16[64,7168]{1,0:T(8,128)(2,1)}, bf16[64,7168]{1,0:T(8,128)(2,1)}, u32[]{:S(2)}, u32[]{:S(2)}) collective-permute-start(bf16[64,7168]{1,0:T(8,128)(2,1)} %constant_dynamic-slice_fusion), channel_id=1, source_target_pairs={{0,2},{1,3},{2,0},{3,1},{4,6},{5,7},{6,4},{7,5},{8,10},{9,11},{10,... | collective-permute-start | bytes 2752520 | tf_op jit(solution)/shard_map/ppermute | solution.py:62
  4.1 25.7 %collective-permute-start.2 = (bf16[64,7168]{1,0:T(8,128)(2,1)}, bf16[64,7168]{1,0:T(8,128)(2,1)}, u32[]{:S(2)}, u32[]{:S(2)}) collective-permute-start(bf16[64,7168]{1,0:T(8,128)(2,1)} %constant_dynamic-slice_fusion), channel_id=1, source_target_pairs={{0,4},{1,5},{2,6},{3,7},{4,0},{5,1},{6,2},{7,3},{8,12},{9,13},{10,... | collective-permute-start | bytes 2752520 | tf_op jit(solution)/shard_map/ppermute | solution.py:62
  4.2 25.5 %collective-permute-start.3 = (bf16[64,7168]{1,0:T(8,128)(2,1)}, bf16[64,7168]{1,0:T(8,128)(2,1)S(1)}, u32[]{:S(2)}, u32[]{:S(2)}) collective-permute-start(bf16[64,7168]{1,0:T(8,128)(2,1)} %constant_dynamic-slice_fusion), channel_id=1, source_target_pairs={{4,8},{5,9},{6,10},{7,11},{8,4},{9,5},{10,6},{11,7},{20,24},{21,25... | collective-permute-start | bytes 2752520 | tf_op jit(solution)/shard_map/ppermute | solution.py:119
  31.8 25.1 %collective-permute-start.8 = (bf16[64,8192]{1,0:T(8,128)(2,1)}, bf16[64,8192]{1,0:T(8,128)(2,1)}, u32[]{:S(2)}, u32[]{:S(2)}) collective-permute-start(bf16[64,8192]{1,0:T(8,128)(2,1)} %get-tuple-element.63.refs_6_), channel_id=1, source_target_pairs={{0,2},{1,3},{2,0},{3,1},{4,6},{5,7},{6,4},{7,5},{8,10},{9,11},{10,... | collective-permute-start | bytes 3145736 | tf_op jit(solution)/shard_map/ppermute | solution.py:62
  32.2 19.9 %collective-permute-start.5 = (bf16[64,7168]{1,0:T(8,128)(2,1)}, bf16[64,7168]{1,0:T(8,128)(2,1)S(1)}, u32[]{:S(2)}, u32[]{:S(2)}) collective-permute-start(bf16[64,7168]{1,0:T(8,128)(2,1)} %get-tuple-element.60.refs_4_), channel_id=1, source_target_pairs={{4,0},{5,1},{6,2},{7,3},{8,12},{9,13},{10,14},{11,15},{20,16},{21,... | collective-permute-start | bytes 2752520 | tf_op jit(solution)/shard_map/ppermute | solution.py:119
  33.5 22.4 %collective-permute-start.6 = (bf16[64,7168]{1,0:T(8,128)(2,1)}, bf16[64,7168]{1,0:T(8,128)(2,1)S(1)}, u32[]{:S(2)}, u32[]{:S(2)}) collective-permute-start(bf16[64,7168]{1,0:T(8,128)(2,1)} %get-tuple-element.61.refs_1_), channel_id=1, source_target_pairs={{4,8},{5,9},{6,10},{7,11},{8,4},{9,5},{10,6},{11,7},{20,24},{21,25... | collective-permute-start | bytes 2752520 | tf_op jit(solution)/shard_map/ppermute | solution.py:119
  35.4 20.5 %collective-permute-start.7 = (bf16[64,7168]{1,0:T(8,128)(2,1)}, bf16[64,7168]{1,0:T(8,128)(2,1)S(1)}, u32[]{:S(2)}, u32[]{:S(2)}) collective-permute-start(bf16[64,7168]{1,0:T(8,128)(2,1)} %get-tuple-element.62.refs_0_), channel_id=1, source_target_pairs={{0,16},{16,0},{1,17},{17,1},{2,18},{18,2},{3,19},{19,3},{4,20},{20... | collective-permute-start | bytes 2752520 | tf_op jit(solution)/shard_map/ppermute | solution.py:66
  60.3 24.4 %collective-permute-start.11 = (bf16[64,8192]{1,0:T(8,128)(2,1)}, bf16[64,8192]{1,0:T(8,128)(2,1)}, u32[]{:S(2)}, u32[]{:S(2)}) collective-permute-start(bf16[64,8192]{1,0:T(8,128)(2,1)} %get-tuple-element.68.refs_5_), channel_id=1, source_target_pairs={{4,8},{5,9},{6,10},{7,11},{8,4},{9,5},{10,6},{11,7},{20,24},{21,25... | collective-permute-start | bytes 3145736 | tf_op jit(solution)/shard_map/ppermute | solution.py:119
  63.2 19.2 %collective-permute-start.10 = (bf16[64,7168]{1,0:T(8,128)(2,1)}, bf16[64,7168]{1,0:T(8,128)(2,1)}, u32[]{:S(2)}, u32[]{:S(2)}) collective-permute-start(bf16[64,7168]{1,0:T(8,128)(2,1)} %get-tuple-element.61.refs_1_), channel_id=1, source_target_pairs={{0,2},{1,3},{2,0},{3,1},{4,6},{5,7},{6,4},{7,5},{8,10},{9,11},{10,... | collective-permute-start | bytes 2752520 | tf_op jit(solution)/shard_map/ppermute | solution.py:62
  64.3 18.8 %collective-permute-start.12 = (bf16[64,7168]{1,0:T(8,128)(2,1)}, bf16[64,7168]{1,0:T(8,128)(2,1)}, u32[]{:S(2)}, u32[]{:S(2)}) collective-permute-start(bf16[64,7168]{1,0:T(8,128)(2,1)} %get-tuple-element.61.refs_1_), channel_id=1, source_target_pairs={{0,16},{16,0},{1,17},{17,1},{2,18},{18,2},{3,19},{19,3},{4,20},{20... | collective-permute-start | bytes 2752520 | tf_op jit(solution)/shard_map/ppermute | solution.py:66
  65.6 17.8 %collective-permute-start.9 = (bf16[64,7168]{1,0:T(8,128)(2,1)}, bf16[64,7168]{1,0:T(8,128)(2,1)}, u32[]{:S(2)}, u32[]{:S(2)}) collective-permute-start(bf16[64,7168]{1,0:T(8,128)(2,1)} %get-tuple-element.67.refs_4_), channel_id=1, source_target_pairs={{4,0},{5,1},{6,2},{7,3},{8,12},{9,13},{10,14},{11,15},{20,16},{21,... | collective-permute-start | bytes 2752520 | tf_op jit(solution)/shard_map/ppermute | solution.py:119
  87.8 28.1 %collective-permute-start.14 = (bf16[64,8192]{1,0:T(8,128)(2,1)}, bf16[64,8192]{1,0:T(8,128)(2,1)}, u32[]{:S(2)}, u32[]{:S(2)}) collective-permute-start(bf16[64,8192]{1,0:T(8,128)(2,1)} %get-tuple-element.71.refs_4_), channel_id=1, source_target_pairs={{4,0},{5,1},{6,2},{7,3},{8,12},{9,13},{10,14},{11,15},{20,16},{21,... | collective-permute-start | bytes 3145736 | tf_op jit(solution)/shard_map/ppermute | solution.py:119
  90.1 25.9 %collective-permute-start.16 = (bf16[64,8192]{1,0:T(8,128)(2,1)}, bf16[64,8192]{1,0:T(8,128)(2,1)}, u32[]{:S(2)}, u32[]{:S(2)}) collective-permute-start(bf16[64,8192]{1,0:T(8,128)(2,1)} %get-tuple-element.72.refs_5_), channel_id=1, source_target_pairs={{0,4},{1,5},{2,6},{3,7},{12,8},{13,9},{14,10},{15,11},{16,20},{17,... | collective-permute-start | bytes 3145736 | tf_op jit(solution)/shard_map/ppermute | solution.py:119
  91.4 24.6 %collective-permute-start.15 = (bf16[64,7168]{1,0:T(8,128)(2,1)S(1)}, bf16[64,7168]{1,0:T(8,128)(2,1)}, u32[]{:S(2)}, u32[]{:S(2)}) collective-permute-start(bf16[64,7168]{1,0:T(8,128)(2,1)S(1)} %copy-done.5), channel_id=1, source_target_pairs={{0,2},{1,3},{2,0},{3,1},{4,6},{5,7},{6,4},{7,5},{8,10},{9,11},{10,... | collective-permute-start | bytes 2752520 | tf_op jit(solution)/shard_map/ppermute | solution.py:62
  92.6 23.3 %collective-permute-start.17 = (bf16[64,7168]{1,0:T(8,128)(2,1)S(1)}, bf16[64,7168]{1,0:T(8,128)(2,1)}, u32[]{:S(2)}, u32[]{:S(2)}) collective-permute-start(bf16[64,7168]{1,0:T(8,128)(2,1)S(1)} %copy-done.5), channel_id=1, source_target_pairs={{0,16},{16,0},{1,17},{17,1},{2,18},{18,2},{3,19},{19,3},{4,20},{20... | collective-permute-start | bytes 2752520 | tf_op jit(solution)/shard_map/ppermute | solution.py:66
  93.8 4.8 %collective-permute-start.13 = (s32[2,4]{1,0:T(2,128)S(1)}, s32[2,4]{1,0:T(2,128)S(1)}, u32[]{:S(2)}, u32[]{:S(2)}) collective-permute-start(s32[2,4]{1,0:T(2,128)S(1)} %copy-done.11), channel_id=1, source_target_pairs={{0,1},{1,0},{2,3},{3,2},{4,5},{5,4},{6,7},{7,6},{8,9},{9,8},{10,11... | collective-permute-start | bytes 104 | tf_op jit(solution)/shard_map/ppermute | solution.py:62
  119.1 28.5 %collective-permute-start.18 = (bf16[64,8192]{1,0:T(8,128)(2,1)}, bf16[64,8192]{1,0:T(8,128)(2,1)}, u32[]{:S(2)}, u32[]{:S(2)}) collective-permute-start(bf16[64,8192]{1,0:T(8,128)(2,1)} %get-tuple-element.78), channel_id=1, source_target_pairs={{4,0},{5,1},{6,2},{7,3},{8,12},{9,13},{10,14},{11,15},{20,16},{21,... | collective-permute-start | bytes 3145736 | tf_op jit(solution)/shard_map/ppermute | solution.py:119
  123.4 26.3 %collective-permute-start.19 = (bf16[64,8192]{1,0:T(8,128)(2,1)}, bf16[64,8192]{1,0:T(8,128)(2,1)}, u32[]{:S(2)}, u32[]{:S(2)}) collective-permute-start(bf16[64,8192]{1,0:T(8,128)(2,1)} %get-tuple-element.79.refs_4_), channel_id=1, source_target_pairs={{4,8},{5,9},{6,10},{7,11},{8,4},{9,5},{10,6},{11,7},{20,24},{21,25... | collective-permute-start | bytes 3145736 | tf_op jit(solution)/shard_map/ppermute | solution.py:119
  126.2 21.3 %collective-permute-start.20 = (bf16[64,7168]{1,0:T(8,128)(2,1)}, bf16[64,7168]{1,0:T(8,128)(2,1)S(1)}, u32[]{:S(2)}, u32[]{:S(2)}) collective-permute-start(bf16[64,7168]{1,0:T(8,128)(2,1)} %get-tuple-element.80.refs_1_), channel_id=1, source_target_pairs={{0,2},{1,3},{2,0},{3,1},{4,6},{5,7},{6,4},{7,5},{8,10},{9,11},{10,... | collective-permute-start | bytes 2752520 | tf_op jit(solution)/shard_map/ppermute | solution.py:62
  126.7 21.0 %collective-permute-start.21 = (bf16[64,7168]{1,0:T(8,128)(2,1)}, bf16[64,7168]{1,0:T(8,128)(2,1)}, u32[]{:S(2)}, u32[]{:S(2)}) collective-permute-start(bf16[64,7168]{1,0:T(8,128)(2,1)} %get-tuple-element.80.refs_1_), channel_id=1, source_target_pairs={{0,16},{16,0},{1,17},{17,1},{2,18},{18,2},{3,19},{19,3},{4,20},{20... | collective-permute-start | bytes 2752520 | tf_op jit(solution)/shard_map/ppermute | solution.py:66
  127.8 47.7 %collective-permute-start.23 = (bf16[64,8192]{1,0:T(8,128)(2,1)}, bf16[64,8192]{1,0:T(8,128)(2,1)}, u32[]{:S(2)}, u32[]{:S(2)}) collective-permute-start(bf16[64,8192]{1,0:T(8,128)(2,1)} %get-tuple-element.87.refs_2_), channel_id=1, source_target_pairs={{0,2},{1,3},{2,0},{3,1},{4,6},{5,7},{6,4},{7,5},{8,10},{9,11},{10,... | collective-permute-start | bytes 3145736 | tf_op jit(solution)/shard_map/ppermute | solution.py:62
  152.9 22.7 %collective-permute-start.22 = (bf16[64,8192]{1,0:T(8,128)(2,1)}, bf16[64,8192]{1,0:T(8,128)(2,1)}, u32[]{:S(2)}, u32[]{:S(2)}) collective-permute-start(bf16[64,8192]{1,0:T(8,128)(2,1)} %get-tuple-element.86.refs_3_), channel_id=1, source_target_pairs={{4,0},{5,1},{6,2},{7,3},{8,12},{9,13},{10,14},{11,15},{20,16},{21,... | collective-permute-start | bytes 3145736 | tf_op jit(solution)/shard_map/ppermute | solution.py:119
  155.2 20.3 %collective-permute-start.24 = (bf16[64,7168]{1,0:T(8,128)(2,1)}, bf16[64,7168]{1,0:T(8,128)(2,1)}, u32[]{:S(2)}, u32[]{:S(2)}) collective-permute-start(bf16[64,7168]{1,0:T(8,128)(2,1)} %get-tuple-element.83.refs_2_), channel_id=1, source_target_pairs={{0,16},{16,0},{1,17},{17,1},{2,18},{18,2},{3,19},{19,3},{4,20},{20... | collective-permute-start | bytes 2752520 | tf_op jit(solution)/shard_map/ppermute | solution.py:66
  155.2 29.3 %copy-start.10 = (s32[2,4]{1,0:T(2,128)S(1)}, s32[2,4]{1,0:T(2,128)}, u32[]{:S(2)}) copy-start(s32[2,4]{1,0:T(2,128)} %copy-done.9) | copy-start | bytes 100
  178.7 22.3 %collective-permute-start.25 = (bf16[64,8192]{1,0:T(8,128)(2,1)}, bf16[64,8192]{1,0:T(8,128)(2,1)}, u32[]{:S(2)}, u32[]{:S(2)}) collective-permute-start(bf16[64,8192]{1,0:T(8,128)(2,1)} %get-tuple-element.96.refs_1_), channel_id=1, source_target_pairs={{0,2},{1,3},{2,0},{3,1},{4,6},{5,7},{6,4},{7,5},{8,10},{9,11},{10,... | collective-permute-start | bytes 3145736 | tf_op jit(solution)/shard_map/ppermute | solution.py:62
  178.7 22.2 %collective-permute-start.26 = (bf16[64,8192]{1,0:T(8,128)(2,1)}, bf16[64,8192]{1,0:T(8,128)(2,1)}, u32[]{:S(2)}, u32[]{:S(2)}) collective-permute-start(bf16[64,8192]{1,0:T(8,128)(2,1)} %get-tuple-element.90.refs_0_), channel_id=1, source_target_pairs={{0,4},{1,5},{2,6},{3,7},{4,0},{5,1},{6,2},{7,3},{8,12},{9,13},{10,... | collective-permute-start | bytes 3145736 | tf_op jit(solution)/shard_map/ppermute | solution.py:62
  178.9 21.3 %collective-permute-start.27 = (bf16[64,7168]{1,0:T(8,128)(2,1)}, bf16[64,7168]{1,0:T(8,128)(2,1)}, u32[]{:S(2)}, u32[]{:S(2)}) collective-permute-start(bf16[64,7168]{1,0:T(8,128)(2,1)} %get-tuple-element.82.refs_0_), channel_id=1, source_target_pairs={{0,16},{16,0},{1,17},{17,1},{2,18},{18,2},{3,19},{19,3},{4,20},{20... | collective-permute-start | bytes 2752520 | tf_op jit(solution)/shard_map/ppermute | solution.py:66
  182.4 31.4 %collective-permute-start.28 = (bf16[32,7168]{1,0:T(8,128)(2,1)}, bf16[32,7168]{1,0:T(8,128)(2,1)S(1)}, u32[]{:S(2)}, u32[]{:S(2)}) collective-permute-start(bf16[32,7168]{1,0:T(8,128)(2,1)} %slice.19), channel_id=1, source_target_pairs={{0,2},{1,3},{2,0},{3,1},{4,6},{5,7},{6,4},{7,5},{8,10},{9,11},{10,... | collective-permute-start | bytes 1376264 | tf_op jit(solution)/shard_map/ppermute | solution.py:62
  183.0 30.7 %collective-permute-start.29 = (bf16[32,7168]{1,0:T(8,128)(2,1)}, bf16[32,7168]{1,0:T(8,128)(2,1)S(1)}, u32[]{:S(2)}, u32[]{:S(2)}) collective-permute-start(bf16[32,7168]{1,0:T(8,128)(2,1)} %slice.20), channel_id=1, source_target_pairs={{0,16},{16,0},{1,17},{17,1},{2,18},{18,2},{3,19},{19,3},{4,20},{20... | collective-permute-start | bytes 1376264 | tf_op jit(solution)/shard_map/ppermute | solution.py:66
  228.6 7.8 %collective-permute-start.30 = (f32[4,512]{1,0:T(4,128)S(1)}, f32[4,512]{1,0:T(4,128)S(1)}, u32[]{:S(2)}, u32[]{:S(2)}) collective-permute-start(f32[4,512]{1,0:T(4,128)S(1)} %pad_maximum_fusion), channel_id=1, source_target_pairs={{0,1},{1,0},{2,3},{3,2},{4,5},{5,4},{6,7},{7,6},{8,9},{9,8},{10,11... | collective-permute-start | bytes 24584 | tf_op jit(solution)/shard_map/ppermute | solution.py:62
  (13 other events, 119.9 us)

commit v8 on v5

--- a/solution.py
+++ b/solution.py
@@ -66,24 +66,40 @@
     return lax.ppermute(array, "groups", [(0, 1), (1, 0)])
 
 
+PARTS = 4
+
+
 def after_kernel(count, merge, inside_ref, turn_ref, *refs):
-    arrays, next_ref = refs[-1 - count : -1], refs[-1]
-    next_ref[0] = turn_ref[0]
-    if merge is not None:
+    if merge is None:
+        next_ref = refs[-1]
+    else:
+        refs, (held, arrived, gone) = refs[:-3], refs[-3:]
+        arrays, next_ref = refs[-1 - count : -1], refs[-1]
         kept, over = (arrays[i] for i in merge)
+        rows = held.shape[0] // PARTS
 
         @pl.when(inside_ref[0] == 1)
         def _():
-            def copy(sem):
-                moved = pltpu.make_async_copy(over, kept, sem)
-                moved.start()
-                moved.wait()
-
-            pl.run_scoped(copy, pltpu.SemaphoreType.DMA(()))
+            parts = [pl.ds(i * rows, rows) for i in range(PARTS)]
+            come = [pltpu.make_async_copy(over.at[p], held.at[p], arrived.at[i]) for i, p in enumerate(parts)]
+            go = [pltpu.make_async_copy(held.at[p], kept.at[p], gone.at[i]) for i, p in enumerate(parts)]
+            for copy in come:
+                copy.start()
+            for first, second in zip(come, go):
+                first.wait()
+                second.start()
+            for copy in go:
+                copy.wait()
+
+    next_ref[0] = turn_ref[0]
 
 
 def after(turn, arrays, inside, merge=None, there=()):
     count = len(arrays)
+    scratch = []
+    if merge is not None:
+        kept = arrays[merge[0]]
+        scratch = [pltpu.VMEM(kept.shape, kept.dtype)] + [pltpu.SemaphoreType.DMA((PARTS,))] * 2
     hbm = pl.BlockSpec(memory_space=pltpu.HBM)
     scalar = pl.BlockSpec(memory_space=pltpu.SMEM)
     *arrays, turn = pl.pallas_call(
@@ -92,6 +108,7 @@
         in_specs=[scalar] * 2 + [hbm] * (len(there) + count),
         out_specs=[hbm] * count + [scalar],
         input_output_aliases={2 + len(there) + i: i for i in range(count)},
+        scratch_shapes=scratch,
         compiler_params=pltpu.CompilerParams(vmem_limit_bytes=VMEM_LIMIT),
         cost_estimate=LITTLE,
     )(inside, turn, *there, *arrays)
@@ -203,7 +220,6 @@
     send = functools.partial(flip, count=count)
 
     acts_there = send(hidden_acts, CORE)
-    grads_there = send(output_grads, CORE)
     spans_here = spans_of(bucket_ids, seq_lengths)
     spans = jnp.concatenate([spans_here, send(spans_here, CORE)], axis=1)
 
@@ -222,6 +238,9 @@
     def outward(piece):
         return lines(piece, [(1, 0), (2, 3)])
 
+    def across(piece):
+        return send(piece, ACROSS)
+
     def over_x(piece):
         return send(piece, COLUMN)
 
@@ -229,8 +248,7 @@
     mine = jnp.reshape(group, (1,)).astype(jnp.int32)
     zero = jnp.zeros((1,), jnp.int32)
     acts = ((hidden_acts, zero), (acts_there, zero))
-    grads = ((output_grads, zero), (grads_there, zero))
-    groups = (("own", "x", "n", "f"), ("xf", "g", "xn", "xg"))
+    groups = (("own", "x", "n", "f"), ("xo", "o", "xn", "xf"))
     tokens_here = hidden_acts.shape[0]
     steps = 4
 
@@ -243,69 +261,78 @@
     def times_b(turn, k, *score):
         return proj(turn, grads, tokens_here, [b[i] for i in groups[k]], zero, steps, *score)
 
+    def pause(turn):
+        return after(turn, [], inside)[0]
+
+    grads_there = send(output_grads, CORE)
+    grads = ((output_grads, zero), (grads_there, zero))
     a["x"] = over_x(a["own"])
     a["n"] = near(a["own"])
     a_mid = middle(a["own"])
-
-    turn, (a["x"], a["n"], a_mid) = after(zero, [a["x"], a["n"], a_mid], inside, None, [acts_there])
+    turn = pause(zero)
+
+    turn, (a["x"], a["n"], a_mid, b_own) = after(
+        turn, [a["x"], a["n"], a_mid, b["own"]], inside, None, [acts_there]
+    )
+    a_out = outward(a_mid)
     a_in = middle(a["n"])
-    a_out = outward(a_mid)
+    b["x"] = over_x(b_own)
+    c["x"] = swap_groups(a["x"])
+    turn = pause(turn)
+
+    turn, (a_out, a_in, b["x"], c["x"], b_own) = after(
+        turn, [a_out, a_in, b["x"], c["x"], b_own], inside, None, [grads_there]
+    )
+    a_last = outward(a_in)
     a["xn"] = over_x(a["n"])
-    c["x"] = swap_groups(a["x"])
-
-    turn, (a["f"], a_in, a["xn"], c["x"], b_own, a_mid) = after(
-        turn, [a_out, a_in, a["xn"], c["x"], b["own"], a_mid], inside, (0, 5), [grads_there]
-    )
-    a_last = outward(a_in)
+    c["n"] = swap_groups(a["n"])
+    b["f"] = across(b_own)
+    turn, (a["o"], a_in) = after(turn, [a_out, a_in], inside, (0, 1))
+    a["xo"] = over_x(a["o"])
+    turn = pause(turn)
+
+    turn, (a_last, a["xn"], c["n"], b_own) = after(turn, [a_last, a["xn"], c["n"], b["own"]], inside)
+    b["n"] = near(b_own)
+    turn, (a["f"], a_mid) = after(turn, [a_last, a_mid], inside, (0, 1))
     a["xf"] = over_x(a["f"])
-    c["n"] = swap_groups(a["n"])
-    b_mid = middle(b_own)
+    c["f"] = swap_groups(a["f"])
     turn, a_first = times_a(turn, 0)
 
-    turn, (a["g"], a["xf"], c["n"], b_mid, b_own, a_in) = after(
-        turn, [a_last, a["xf"], c["n"], b_mid, b_own, a_in], inside, (0, 5)
-    )
-    b["n"] = near(b_own)
-    b["x"] = over_x(b_own)
-    c["f"] = swap_groups(a["f"])
-
-    turn, (b["n"], b["x"], c["f"]) = after(turn, [b["n"], b["x"], c["f"]], inside)
+    turn, (a["xo"], c["f"], b["n"], a["o"], a["xn"]) = after(
+        turn, [a["xo"], c["f"], b["n"], a["o"], a["xn"]], inside
+    )
     b_in = middle(b["n"])
-    b_out = outward(b_mid)
-    a["xg"] = over_x(a["g"])
-    c["g"] = swap_groups(a["g"])
+    c["o"] = swap_groups(a["o"])
+    c["xn"] = swap_groups(a["xn"])
     turn, c_first = times_c(turn, 0)
 
-    turn, (b["f"], b_in, a["xg"], c["g"], b_mid) = after(
-        turn, [b_out, b_in, a["xg"], c["g"], b_mid], inside, (0, 4)
-    )
-    b_last = outward(b_in)
+    turn, (b["f"], a["xf"], c["o"], a["xo"]) = after(turn, [b["f"], a["xf"], c["o"], a["xo"]], inside)
+    b_out = outward(b["f"])
     b["xf"] = over_x(b["f"])
-    c["xf"] = swap_groups(a["xf"])
+    c["xo"] = swap_groups(a["xo"])
     turn, score_first = times_b(turn, 0, True, spans, (a_first, c_first))
 
-    turn, (b["g"], b["xf"], c["xf"], b_in) = after(turn, [b_last, b["xf"], c["xf"], b_in], inside, (0, 3))
-    b["xg"] = over_x(b["g"])
-    b["xn"] = near(b["x"])
-    c["xn"] = swap_groups(a["xn"])
+    split = c["f"].shape[0] // 2
+    turn, (b["o"], b["xf"], c["xn"], b_in, b_over, a["xf"], c["f"]) = after(
+        turn, [b_out, b["xf"], c["xn"], b_in, b["x"], a["xf"], c["f"]], inside, (0, 3)
+    )
+    b["xo"] = over_x(b["o"])
+    b["xn"] = near(b_over)
+    c["top"] = over_x(c["f"][:split])
+    c["low"] = swap_groups(a["xf"][split:])
     turn, a_second = times_a(turn, 1)
 
-    turn, (b["xg"], b["xn"], c["xn"], c["g"]) = after(turn, [b["xg"], b["xn"], c["xn"], c["g"]], inside)
-    split = c["g"].shape[0] // 2
-    c["top"] = over_x(c["g"][:split])
-    c["low"] = swap_groups(a["xg"][split:])
+    turn, (b["xo"], b["xn"], c["xo"]) = after(turn, [b["xo"], b["xn"], c["xo"]], inside)
     turn, b_second = times_b(turn, 1)
-    groups = (groups[0], ("xf", "g", "xn", "top", "low"))
+    groups = (groups[0], ("xo", "o", "xn", "top", "low"))
     turn, score_second = times_c(turn, 1, False, spans, (a_second, b_second))
     sums = [score_first, score_second]
 
     slots = bucket_ids.shape[0]
     ours = jnp.concatenate([x[:slots] for x in sums], axis=1)
     others = send(jnp.concatenate([x[slots:] for x in sums], axis=1), CORE)
-    f_code = jnp.where(at_end, OPPOSITE, ACROSS)
-    g_code = jnp.where(at_end, ACROSS, OPPOSITE)
-    codes = [0, COLUMN, NEAR, f_code, f_code | COLUMN, g_code, NEAR | COLUMN, g_code | COLUMN]
-    codes = jnp.stack([jnp.asarray(code, jnp.int32) for code in codes])
+    codes = (0, COLUMN, NEAR, ACROSS, OPPOSITE | COLUMN, OPPOSITE, NEAR | COLUMN, ACROSS | COLUMN)
+    codes = jnp.array(codes, jnp.int32)
     owner = jnp.concatenate([me ^ codes, me ^ CORE ^ codes])
     query = owner[:, None] * local + jnp.arange(local, dtype=jnp.int32)[None, :]
     query = jnp.repeat(query.reshape(-1), ranks)

time: 339 us -> 222 us (0.65)
  Pallas kernels: 202 us -> 90 us
  starting transfers between devices: 52.7 us -> 45.7 us
    pallas_call x7 -> x12, Pallas kernels: 131 us -> 19.3 us  [after(): pl.pallas_call(functools.partial(after_kernel, count, merge), out_shape=[...]
    ppermute x8 -> x6, waiting for transfers between devices: 20.5 us -> 30.5 us  [lines(): lax.ppermute(array, 'dp', [(a * 4 + rest, b * 4 + rest) for a, b in pairs...]
    ppermute x7, waiting for transfers between devices: 19 us -> 9.24 us  [swap_groups(): return lax.ppermute(array, 'groups', [(0, 1), (1, 0)])]
    ppermute x8 -> x6, starting transfers between devices: 23.2 us -> 16.5 us  [lines(): lax.ppermute(array, 'dp', [(a * 4 + rest, b * 4 + rest) for a, b in pairs...]
    ppermute x15 -> x16, waiting for transfers between devices: 27.7 us -> 26.6 us  [flip(): return lax.ppermute(array, 'dp', [(i, i ^ code) for i in range(count)])]
    ppermute x15 -> x16, starting transfers between devices: 21.7 us -> 21.1 us  [flip(): return lax.ppermute(array, 'dp', [(i, i ^ code) for i in range(count)])]
    unnamed x31 -> x22, local copies, waits for them, and re-layouts: 6.83 us -> 6.61 us
  transfers between devices with their start and end apart: 30 -> 29, of which waited for: 19 -> 15; matrix products, arithmetic and copies ran while one was open for 3% -> 6% of each run, Pallas kernels for 28% -> 33%
where the time goes in v8:
time: 222 us; the launch traced here: 220 us
  Pallas kernels  90 us (41%)
  waiting for transfers between devices  66.4 us (30%)
  starting transfers between devices  45.7 us (21%)
  local copies, waits for them, and re-layouts  15.6 us (7%)
    pallas_call x6, Pallas kernels, proj(): pl.pallas_call(functools.partial(proj_kernel, len(pieces), last), out_sha...  70.7 us
    ppermute x6, waiting for transfers between devices, lines(): lax.ppermute(array, 'dp', [(a * 4 + rest, b * 4 + rest) for a, b in pairs...  30.5 us
    ppermute x16, waiting for transfers between devices, flip(): return lax.ppermute(array, 'dp', [(i, i ^ code) for i in range(count)])  26.6 us
    ppermute x16, starting transfers between devices, flip(): return lax.ppermute(array, 'dp', [(i, i ^ code) for i in range(count)])  21.1 us
    pallas_call x12, Pallas kernels, after(): pl.pallas_call(functools.partial(after_kernel, count, merge), out_shape=[...  19.3 us
    ppermute x6, starting transfers between devices, lines(): lax.ppermute(array, 'dp', [(a * 4 + rest, b * 4 + rest) for a, b in pairs...  16.5 us
    ppermute x7, waiting for transfers between devices, swap_groups(): return lax.ppermute(array, 'groups', [(0, 1), (1, 0)])  9.24 us
    ppermute x7, starting transfers between devices, swap_groups(): return lax.ppermute(array, 'groups', [(0, 1), (1, 0)])  8.06 us
  transfers between devices with their start and end apart: 29, of which 15 were waited for; matrix products, arithmetic and copies ran while one was open for 6% of the time, Pallas kernels for 33%

profile of v8, /device:TPU:9, one launch (start us, length us, event | category | flops | bytes accessed | tf_op | source)
XLA Modules:
  0.0 219.8 jit_solution(14982101871425859920)
XLA Ops:
  0.7 2.8 %constant_dynamic-slice_fusion = (bf16[64,7168]{1,0:T(8,128)(2,1)}, bf16[64,7168]{1,0:T(8,128)(2,1)}) fusion(bf16[64,14336]{1,0:T(8,128)(2,1)} %bitcast.19, s32[]{:T(128)S(6)} %select_n.24, s32[]{:T(128)S(6)} %select_n.23), kind=kLoop, calls=%fused_computation.19 | loop fusion | bytes 3670024 | tf_op jit(solution)/shard_map/dynamic_slice | solution.py:228
  4.9 4.3 %collective-permute-start.3 = (bf16[64,7168]{1,0:T(8,128)(2,1)}, bf16[64,7168]{1,0:T(8,128)(2,1)S(1)}, u32[]{:S(2)}, u32[]{:S(2)}) collective-permute-start(bf16[64,7168]{1,0:T(8,128)(2,1)} %get-tuple-element.112.refs_0_), channel_id=1, source_target_pairs={{4,8},{5,9},{6,10},{7,11},{8,4},{9,5},{10,6},{11,7},{20,24},{21,25... | collective-permute-start | bytes 2752520 | tf_op jit(solution)/shard_map/ppermute | solution.py:119
  9.7 2.3 %copy.47.refs_4_ = bf16[64,8192]{1,0:T(8,128)(2,1)} copy(bf16[64,8192]{1,0:T(8,128)(2,1)} %bitcast.16) | data formatting | bytes 2097152
  12.1 13.1 %collective-permute-done.1.refs_1_ = bf16[64,7168]{1,0:T(8,128)(2,1)} collective-permute-done((bf16[64,7168]{1,0:T(8,128)(2,1)}, bf16[64,7168]{1,0:T(8,128)(2,1)}, u32[]{:S(2)}, u32[]{:S(2)}) %collective-permute-start.1) | collective-permute-done | bytes 917536 | tf_op jit(solution)/shard_map/ppermute | solution.py:62
  26.1 2.9 %collective-permute-done.3.refs_3_ = bf16[64,7168]{1,0:T(8,128)(2,1)S(1)} collective-permute-done((bf16[64,7168]{1,0:T(8,128)(2,1)}, bf16[64,7168]{1,0:T(8,128)(2,1)S(1)}, u32[]{:S(2)}, u32[]{:S(2)}) %collective-permute-start.3) | collective-permute-done | bytes 917536 | tf_op jit(solution)/shard_map/ppermute | solution.py:119
  32.8 3.1 %collective-permute-start.6 = (bf16[64,7168]{1,0:T(8,128)(2,1)}, bf16[64,7168]{1,0:T(8,128)(2,1)}, u32[]{:S(2)}, u32[]{:S(2)}) collective-permute-start(bf16[64,7168]{1,0:T(8,128)(2,1)} %get-tuple-element.60.refs_2_), channel_id=1, source_target_pairs={{4,8},{5,9},{6,10},{7,11},{8,4},{9,5},{10,6},{11,7},{20,24},{21,25... | collective-permute-start | bytes 2752520 | tf_op jit(solution)/shard_map/ppermute | solution.py:119
  38.3 12.7 %collective-permute-done.5.refs_1_ = bf16[64,7168]{1,0:T(8,128)(2,1)S(1)} collective-permute-done((bf16[64,7168]{1,0:T(8,128)(2,1)}, bf16[64,7168]{1,0:T(8,128)(2,1)S(1)}, u32[]{:S(2)}, u32[]{:S(2)}) %collective-permute-start.5) | collective-permute-done | bytes 917536 | tf_op jit(solution)/shard_map/ppermute | solution.py:119
  51.0 3.9 %collective-permute-done.6.refs_2_ = bf16[64,7168]{1,0:T(8,128)(2,1)} collective-permute-done((bf16[64,7168]{1,0:T(8,128)(2,1)}, bf16[64,7168]{1,0:T(8,128)(2,1)}, u32[]{:S(2)}, u32[]{:S(2)}) %collective-permute-start.6) | collective-permute-done | bytes 917536 | tf_op jit(solution)/shard_map/ppermute | solution.py:119
  56.7 2.3 %collective-permute-start.9 = (bf16[64,7168]{1,0:T(8,128)(2,1)}, bf16[64,7168]{1,0:T(8,128)(2,1)}, u32[]{:S(2)}, u32[]{:S(2)}) collective-permute-start(bf16[64,7168]{1,0:T(8,128)(2,1)} %get-tuple-element.65.refs_1_), channel_id=1, source_target_pairs={{4,0},{5,1},{6,2},{7,3},{8,12},{9,13},{10,14},{11,15},{20,16},{21,... | collective-permute-start | bytes 2752520 | tf_op jit(solution)/shard_map/ppermute | solution.py:119
  61.4 2.3 %copy.58.refs_3_ = bf16[64,8192]{1,0:T(8,128)(2,1)} copy(bf16[64,8192]{1,0:T(8,128)(2,1)} %bitcast.17) | data formatting | bytes 2097152
  63.7 11.0 %collective-permute-done.9.refs_0_ = bf16[64,7168]{1,0:T(8,128)(2,1)} collective-permute-done((bf16[64,7168]{1,0:T(8,128)(2,1)}, bf16[64,7168]{1,0:T(8,128)(2,1)}, u32[]{:S(2)}, u32[]{:S(2)}) %collective-permute-start.9) | collective-permute-done | bytes 917536 | tf_op jit(solution)/shard_map/ppermute | solution.py:119
  74.7 3.2 %shard_map.77 = (bf16[64,7168]{1,0:T(8,128)(2,1)}, bf16[64,7168]{1,0:T(8,128)(2,1)}, s32[1]{0:T(128)}) custom-call(s32[1]{0:T(128)} %bitcast.inside_ref, s32[1]{0:T(128)} %get-tuple-element.63.turn_ref, bf16[64,7168]{1,0:T(8,128)(2,1)} %get-tuple-element.64.refs_0_, ...), custom_call_target="tpu_custom_call", output_to_operand_aliasing={{0}: (2, {}), {1}: (3, {})} | custom-call | flops 1 | bytes 1 | tf_op jit(solution)/shard_map/pallas_call | solution.py:105
  81.5 3.2 %shard_map.80 = (bf16[64,7168]{1,0:T(8,128)(2,1)}, bf16[64,7168]{1,0:T(8,128)(2,1)}, s32[1]{0:T(128)}) custom-call(s32[1]{0:T(128)} %bitcast.inside_ref, s32[1]{0:T(128)} %get-tuple-element.67.turn_ref, bf16[64,7168]{1,0:T(8,128)(2,1)} %get-tuple-element.68.refs_0_, ...), custom_call_target="tpu_custom_call", output_to_operand_aliasing={{0}: (2, {}), {1}: (3, {})} | custom-call | flops 1 | bytes 1 | tf_op jit(solution)/shard_map/pallas_call | solution.py:105
  89.0 10.7 %shard_map.81 = (f32[1024,256]{1,0:T(8,128)}, s32[1]{0:T(128)}) custom-call(s32[1]{0:T(128)} %get-tuple-element.69.turn_ref, s32[3]{0:T(128)} %concatenate.25.at_ref, bf16[512,14336]{1,0:T(8,128)(2,1)} %own_ref.11, bf16[512,14336]{1,0:T(8,128)(2,1)} %collective-permute-done.refs_0_.other_ref, bf16[64,7168]{1,0:T(8,128)(2,1)} %get-tuple-element.112.refs_0_, ...), custom_call_target="tpu_custom_call" | custom-call | flops 1 | bytes 1 | tf_op jit(solution)/shard_map/pallas_call | solution.py:183
  99.7 2.8 %collective-permute-done.13.refs_1_ = bf16[64,7168]{1,0:T(8,128)(2,1)S(1)} collective-permute-done((bf16[64,7168]{1,0:T(8,128)(2,1)}, bf16[64,7168]{1,0:T(8,128)(2,1)S(1)}, u32[]{:S(2)}, u32[]{:S(2)}) %collective-permute-start.13) | collective-permute-done | bytes 917536 | tf_op jit(solution)/shard_map/ppermute | solution.py:66
  106.5 3.2 %collective-permute-start.22 = (bf16[64,8192]{1,0:T(8,128)(2,1)}, bf16[64,8192]{1,0:T(8,128)(2,1)}, u32[]{:S(2)}, u32[]{:S(2)}) collective-permute-start(bf16[64,8192]{1,0:T(8,128)(2,1)} %get-tuple-element.85.refs_2_), channel_id=1, source_target_pairs={{4,8},{5,9},{6,10},{7,11},{8,4},{9,5},{10,6},{11,7},{20,24},{21,25... | collective-permute-start | bytes 3145736 | tf_op jit(solution)/shard_map/ppermute | solution.py:119
  109.7 10.9 %shard_map.83 = (f32[1024,256]{1,0:T(8,128)}, s32[1]{0:T(128)}) custom-call(s32[1]{0:T(128)} %get-tuple-element.75.turn_ref, s32[3]{0:T(128)} %concatenate.26.at_ref, bf16[512,14336]{1,0:T(8,128)(2,1)} %own_ref.11, bf16[512,14336]{1,0:T(8,128)(2,1)} %collective-permute-done.refs_0_.other_ref, bf16[64,7168]{1,0:T(8,128)(2,1)} %get-tuple-element.111.refs_0_, ...), custom_call_target="tpu_custom_call" | custom-call | flops 1 | bytes 1 | tf_op jit(solution)/shard_map/pallas_call | solution.py:183
  120.6 8.1 %collective-permute-done.15.refs_0_ = bf16[64,8192]{1,0:T(8,128)(2,1)} collective-permute-done((bf16[64,8192]{1,0:T(8,128)(2,1)}, bf16[64,8192]{1,0:T(8,128)(2,1)}, u32[]{:S(2)}, u32[]{:S(2)}) %collective-permute-start.15) | collective-permute-done | bytes 1048608 | tf_op jit(solution)/shard_map/ppermute | solution.py:62
  129.8 2.3 %collective-permute-start.19 = (bf16[64,8192]{1,0:T(8,128)(2,1)}, bf16[64,8192]{1,0:T(8,128)(2,1)}, u32[]{:S(2)}, u32[]{:S(2)}) collective-permute-start(bf16[64,8192]{1,0:T(8,128)(2,1)} %get-tuple-element.86.refs_3_), channel_id=1, source_target_pairs={{4,0},{5,1},{6,2},{7,3},{8,12},{9,13},{10,14},{11,15},{20,16},{21,... | collective-permute-start | bytes 3145736 | tf_op jit(solution)/shard_map/ppermute | solution.py:119
  133.6 11.3 %collective-permute-start.18 = (s32[2,4]{1,0:T(2,128)S(1)}, s32[2,4]{1,0:T(2,128)S(1)}, u32[]{:S(2)}, u32[]{:S(2)}) collective-permute-start(s32[2,4]{1,0:T(2,128)S(1)} %pad_add_fusion), channel_id=1, source_target_pairs={{0,1},{1,0},{2,3},{3,2},{4,5},{5,4},{6,7},{7,6},{8,9},{9,8},{10,11... | collective-permute-start | bytes 104 | tf_op jit(solution)/shard_map/ppermute | solution.py:62
  146.9 13.8 %shard_map.85 = (f32[8,256]{1,0:T(8,128)}, s32[1]{0:T(128)}) custom-call(s32[1]{0:T(128)} %get-tuple-element.83.turn_ref, s32[3]{0:T(128)} %broadcast_8_at_ref.2.at_ref, bf16[512,8192]{1,0:T(8,128)(2,1)} %own_ref.10, bf16[512,8192]{1,0:T(8,128)(2,1)} %collective-permute-done.4.refs_0_.other_ref, bf16[64,8192]{1,0:T(8,128)(2,1)} %bitcast.18, ...), custom_call_target="tpu_custom_call" | custom-call | flops 1 | bytes 1 | tf_op jit(solution)/shard_map/pallas_call | solution.py:183
  160.7 3.2 %shard_map.86 = (bf16[64,8192]{1,0:T(8,128)(2,1)}, bf16[64,8192]{1,0:T(8,128)(2,1)}, bf16[64,7168]{1,0:T(8,128)(2,1)}, bf16[64,8192]{1,0:T(8,128)(2,1)}, bf16[64...) custom-call(s32[1]{0:T(128)} %bitcast.inside_ref, ...), custom_call_target="tpu_custom_call", output_to_operand_aliasing={{0}: (2, {}), {1}: (3, {}), {2}: (4, {}), {3}: (5, {}), {4}... | custom-call | flops 1 | bytes 1 | tf_op jit(solution)/shard_map/pallas_call | solution.py:105
  164.0 1.8 collective-permute-start.23
  165.8 1.7 collective-permute-start.25
  167.5 1.8 slice.19
  169.5 1.8 slice.20
  171.4 10.8 %shard_map.87 = (f32[1024,256]{1,0:T(8,128)}, s32[1]{0:T(128)}) custom-call(s32[1]{0:T(128)} %get-tuple-element.93.turn_ref, s32[3]{0:T(128)} %concatenate.25.at_ref, bf16[512,14336]{1,0:T(8,128)(2,1)} %own_ref.11, bf16[512,14336]{1,0:T(8,128)(2,1)} %collective-permute-done.refs_0_.other_ref, bf16[64,7168]{1,0:T(8,128)(2,1)} %get-tuple-element.94.refs_0_, ...), custom_call_target="tpu_custom_call" | custom-call | flops 1 | bytes 1 | tf_op jit(solution)/shard_map/pallas_call | solution.py:183
  182.2 5.8 %collective-permute-done.25.refs_2_ = bf16[64,7168]{1,0:T(8,128)(2,1)S(1)} collective-permute-done((bf16[64,7168]{1,0:T(8,128)(2,1)}, bf16[64,7168]{1,0:T(8,128)(2,1)S(1)}, u32[]{:S(2)}, u32[]{:S(2)}) %collective-permute-start.25) | collective-permute-done | bytes 917536 | tf_op jit(solution)/shard_map/ppermute | solution.py:66
  188.0 1.4 collective-permute-done.23.refs_0_
  191.3 11.6 %shard_map.89 = (f32[1024,256]{1,0:T(8,128)}, s32[1]{0:T(128)}) custom-call(s32[1]{0:T(128)} %get-tuple-element.99.turn_ref, s32[3]{0:T(128)} %broadcast_8_at_ref.2.at_ref, bf16[512,8192]{1,0:T(8,128)(2,1)} %own_ref.10, bf16[512,8192]{1,0:T(8,128)(2,1)} %collective-permute-done.4.refs_0_.other_ref, bf16[64,8192]{1,0:T(8,128)(2,1)} %get-tuple-element.100.refs_0_, ...), custom_call_target="tpu_custom_call" | custom-call | flops 1 | bytes 1 | tf_op jit(solution)/shard_map/pallas_call | solution.py:183
  203.0 12.9 %shard_map.90 = (f32[8,256]{1,0:T(8,128)}, s32[1]{0:T(128)}) custom-call(s32[1]{0:T(128)} %get-tuple-element.103.turn_ref, s32[3]{0:T(128)} %concatenate.26.at_ref, bf16[512,14336]{1,0:T(8,128)(2,1)} %own_ref.11, bf16[512,14336]{1,0:T(8,128)(2,1)} %collective-permute-done.refs_0_.other_ref, bf16[64,7168]{1,0:T(8,128)(2,1)} %get-tuple-element.104.refs_0_, ...), custom_call_target="tpu_custom_call" | custom-call | flops 1 | bytes 1 | tf_op jit(solution)/shard_map/pallas_call | solution.py:183
  216.7 1.5 collective-permute-start.28
  (87 shorter events, 34.9 us)
Async XLA Ops:
  0.0 29.0 %collective-permute-start = (bf16[512,14336]{1,0:T(8,128)(2,1)}, bf16[512,14336]{1,0:T(8,128)(2,1)}, u32[]{:S(2)}, u32[]{:S(2)}) collective-permute-start(bf16[512,14336]{1,0:T(8,128)(2,1)} %own_ref.11), channel_id=1, source_target_pairs={{0,1},{1,0},{2,3},{3,2},{4,5},{5,4},{6,7},{7,6},{8,9},{9,8},{10,11... | collective-permute-start | bytes 44040200 | tf_op jit(solution)/shard_map/ppermute | solution.py:62
  0.7 37.6 %collective-permute-start.4 = (bf16[512,8192]{1,0:T(8,128)(2,1)}, bf16[512,8192]{1,0:T(8,128)(2,1)}, u32[]{:S(2)}, u32[]{:S(2)}) collective-permute-start(bf16[512,8192]{1,0:T(8,128)(2,1)} %own_ref.10), channel_id=1, source_target_pairs={{0,1},{1,0},{2,3},{3,2},{4,5},{5,4},{6,7},{7,6},{8,9},{9,8},{10,11... | collective-permute-start | bytes 25165832 | tf_op jit(solution)/shard_map/ppermute | solution.py:62
  3.5 21.7 %collective-permute-start.1 = (bf16[64,7168]{1,0:T(8,128)(2,1)}, bf16[64,7168]{1,0:T(8,128)(2,1)}, u32[]{:S(2)}, u32[]{:S(2)}) collective-permute-start(bf16[64,7168]{1,0:T(8,128)(2,1)} %get-tuple-element.112.refs_0_), channel_id=1, source_target_pairs={{0,2},{1,3},{2,0},{3,1},{4,6},{5,7},{6,4},{7,5},{8,10},{9,11},{10,... | collective-permute-start | bytes 2752520 | tf_op jit(solution)/shard_map/ppermute | solution.py:62
  4.7 21.4 %collective-permute-start.2 = (bf16[64,7168]{1,0:T(8,128)(2,1)}, bf16[64,7168]{1,0:T(8,128)(2,1)}, u32[]{:S(2)}, u32[]{:S(2)}) collective-permute-start(bf16[64,7168]{1,0:T(8,128)(2,1)} %get-tuple-element.112.refs_0_), channel_id=1, source_target_pairs={{0,4},{1,5},{2,6},{3,7},{4,0},{5,1},{6,2},{7,3},{8,12},{9,13},{10,... | collective-permute-start | bytes 2752520 | tf_op jit(solution)/shard_map/ppermute | solution.py:62
  4.9 24.1 %collective-permute-start.3 = (bf16[64,7168]{1,0:T(8,128)(2,1)}, bf16[64,7168]{1,0:T(8,128)(2,1)S(1)}, u32[]{:S(2)}, u32[]{:S(2)}) collective-permute-start(bf16[64,7168]{1,0:T(8,128)(2,1)} %get-tuple-element.112.refs_0_), channel_id=1, source_target_pairs={{4,8},{5,9},{6,10},{7,11},{8,4},{9,5},{10,6},{11,7},{20,24},{21,25... | collective-permute-start | bytes 2752520 | tf_op jit(solution)/shard_map/ppermute | solution.py:119
  31.1 24.4 %collective-permute-start.7 = (bf16[64,8192]{1,0:T(8,128)(2,1)}, bf16[64,8192]{1,0:T(8,128)(2,1)}, u32[]{:S(2)}, u32[]{:S(2)}) collective-permute-start(bf16[64,8192]{1,0:T(8,128)(2,1)} %get-tuple-element.61.refs_5_), channel_id=1, source_target_pairs={{0,2},{1,3},{2,0},{3,1},{4,6},{5,7},{6,4},{7,5},{8,10},{9,11},{10,... | collective-permute-start | bytes 3145736 | tf_op jit(solution)/shard_map/ppermute | solution.py:62
  31.4 19.5 %collective-permute-start.5 = (bf16[64,7168]{1,0:T(8,128)(2,1)}, bf16[64,7168]{1,0:T(8,128)(2,1)S(1)}, u32[]{:S(2)}, u32[]{:S(2)}) collective-permute-start(bf16[64,7168]{1,0:T(8,128)(2,1)} %get-tuple-element.59.refs_1_), channel_id=1, source_target_pairs={{4,0},{5,1},{6,2},{7,3},{8,12},{9,13},{10,14},{11,15},{20,16},{21,... | collective-permute-start | bytes 2752520 | tf_op jit(solution)/shard_map/ppermute | solution.py:119
  32.8 22.1 %collective-permute-start.6 = (bf16[64,7168]{1,0:T(8,128)(2,1)}, bf16[64,7168]{1,0:T(8,128)(2,1)}, u32[]{:S(2)}, u32[]{:S(2)}) collective-permute-start(bf16[64,7168]{1,0:T(8,128)(2,1)} %get-tuple-element.60.refs_2_), channel_id=1, source_target_pairs={{4,8},{5,9},{6,10},{7,11},{8,4},{9,5},{10,6},{11,7},{20,24},{21,25... | collective-permute-start | bytes 2752520 | tf_op jit(solution)/shard_map/ppermute | solution.py:119
  35.8 19.7 %collective-permute-start.8 = (bf16[64,7168]{1,0:T(8,128)(2,1)}, bf16[64,7168]{1,0:T(8,128)(2,1)}, u32[]{:S(2)}, u32[]{:S(2)}) collective-permute-start(bf16[64,7168]{1,0:T(8,128)(2,1)} %get-tuple-element.62.refs_1_), channel_id=1, source_target_pairs={{0,16},{16,0},{1,17},{17,1},{2,18},{18,2},{3,19},{19,3},{4,20},{20... | collective-permute-start | bytes 2752520 | tf_op jit(solution)/shard_map/ppermute | solution.py:66
  56.7 18.0 %collective-permute-start.9 = (bf16[64,7168]{1,0:T(8,128)(2,1)}, bf16[64,7168]{1,0:T(8,128)(2,1)}, u32[]{:S(2)}, u32[]{:S(2)}) collective-permute-start(bf16[64,7168]{1,0:T(8,128)(2,1)} %get-tuple-element.65.refs_1_), channel_id=1, source_target_pairs={{4,0},{5,1},{6,2},{7,3},{8,12},{9,13},{10,14},{11,15},{20,16},{21,... | collective-permute-start | bytes 2752520 | tf_op jit(solution)/shard_map/ppermute | solution.py:119
  58.9 20.1 %collective-permute-start.10 = (bf16[64,7168]{1,0:T(8,128)(2,1)}, bf16[64,7168]{1,0:T(8,128)(2,1)S(1)}, u32[]{:S(2)}, u32[]{:S(2)}) collective-permute-start(bf16[64,7168]{1,0:T(8,128)(2,1)} %get-tuple-element.60.refs_2_), channel_id=1, source_target_pairs={{0,2},{1,3},{2,0},{3,1},{4,6},{5,7},{6,4},{7,5},{8,10},{9,11},{10,... | collective-permute-start | bytes 2752520 | tf_op jit(solution)/shard_map/ppermute | solution.py:62
  60.2 18.9 %collective-permute-start.11 = (bf16[64,7168]{1,0:T(8,128)(2,1)}, bf16[64,7168]{1,0:T(8,128)(2,1)}, u32[]{:S(2)}, u32[]{:S(2)}) collective-permute-start(bf16[64,7168]{1,0:T(8,128)(2,1)} %get-tuple-element.60.refs_2_), channel_id=1, source_target_pairs={{0,16},{16,0},{1,17},{17,1},{2,18},{18,2},{3,19},{19,3},{4,20},{20... | collective-permute-start | bytes 2752520 | tf_op jit(solution)/shard_map/ppermute | solution.py:66
  81.2 22.3 %collective-permute-start.14 = (bf16[64,8192]{1,0:T(8,128)(2,1)}, bf16[64,8192]{1,0:T(8,128)(2,1)}, u32[]{:S(2)}, u32[]{:S(2)}) collective-permute-start(bf16[64,8192]{1,0:T(8,128)(2,1)} %get-tuple-element.73), channel_id=1, source_target_pairs={{0,4},{1,5},{2,6},{3,7},{4,0},{5,1},{6,2},{7,3},{8,12},{9,13},{10,... | collective-permute-start | bytes 3145736 | tf_op jit(solution)/shard_map/ppermute | solution.py:62
  84.7 17.8 %collective-permute-start.13 = (bf16[64,7168]{1,0:T(8,128)(2,1)}, bf16[64,7168]{1,0:T(8,128)(2,1)S(1)}, u32[]{:S(2)}, u32[]{:S(2)}) collective-permute-start(bf16[64,7168]{1,0:T(8,128)(2,1)} %get-tuple-element.70.refs_3_), channel_id=1, source_target_pairs={{0,16},{16,0},{1,17},{17,1},{2,18},{18,2},{3,19},{19,3},{4,20},{20... | collective-permute-start | bytes 2752520 | tf_op jit(solution)/shard_map/ppermute | solution.py:66
  86.0 17.5 %collective-permute-start.12 = (bf16[64,7168]{1,0:T(8,128)(2,1)}, bf16[64,7168]{1,0:T(8,128)(2,1)}, u32[]{:S(2)}, u32[]{:S(2)}) collective-permute-start(bf16[64,7168]{1,0:T(8,128)(2,1)} %get-tuple-element.72.refs_3_), channel_id=1, source_target_pairs={{0,2},{1,3},{2,0},{3,1},{4,6},{5,7},{6,4},{7,5},{8,10},{9,11},{10,... | collective-permute-start | bytes 2752520 | tf_op jit(solution)/shard_map/ppermute | solution.py:62
  87.3 41.4 %collective-permute-start.15 = (bf16[64,8192]{1,0:T(8,128)(2,1)}, bf16[64,8192]{1,0:T(8,128)(2,1)}, u32[]{:S(2)}, u32[]{:S(2)}) collective-permute-start(bf16[64,8192]{1,0:T(8,128)(2,1)} %get-tuple-element.80), channel_id=1, source_target_pairs={{0,12},{1,13},{2,14},{3,15},{4,8},{5,9},{6,10},{7,11},{8,4},{9,5},... | collective-permute-start | bytes 3145736 | tf_op jit(solution)/shard_map/ppermute | solution.py:62
  88.7 39.9 %collective-permute-start.16 = (bf16[64,7168]{1,0:T(8,128)(2,1)}, bf16[64,7168]{1,0:T(8,128)(2,1)}, u32[]{:S(2)}, u32[]{:S(2)}) collective-permute-start(bf16[64,7168]{1,0:T(8,128)(2,1)} %get-tuple-element.70.refs_3_), channel_id=1, source_target_pairs={{0,2},{1,3},{2,0},{3,1},{4,6},{5,7},{6,4},{7,5},{8,10},{9,11},{10,... | collective-permute-start | bytes 2752520 | tf_op jit(solution)/shard_map/ppermute | solution.py:62
  104.7 24.0 %collective-permute-start.17 = (bf16[64,7168]{1,0:T(8,128)(2,1)}, bf16[64,7168]{1,0:T(8,128)(2,1)}, u32[]{:S(2)}, u32[]{:S(2)}) collective-permute-start(bf16[64,7168]{1,0:T(8,128)(2,1)} %get-tuple-element.81.refs_1_), channel_id=1, source_target_pairs={{0,16},{16,0},{1,17},{17,1},{2,18},{18,2},{3,19},{19,3},{4,20},{20... | collective-permute-start | bytes 2752520 | tf_op jit(solution)/shard_map/ppermute | solution.py:66
  106.5 54.2 %collective-permute-start.22 = (bf16[64,8192]{1,0:T(8,128)(2,1)}, bf16[64,8192]{1,0:T(8,128)(2,1)}, u32[]{:S(2)}, u32[]{:S(2)}) collective-permute-start(bf16[64,8192]{1,0:T(8,128)(2,1)} %get-tuple-element.85.refs_2_), channel_id=1, source_target_pairs={{4,8},{5,9},{6,10},{7,11},{8,4},{9,5},{10,6},{11,7},{20,24},{21,25... | collective-permute-start | bytes 3145736 | tf_op jit(solution)/shard_map/ppermute | solution.py:119
  109.6 22.5 %copy-start.3 = (bf16[64,7168]{1,0:T(8,128)(2,1)S(1)}, bf16[64,7168]{1,0:T(8,128)(2,1)}, u32[]{:S(2)}) copy-start(bf16[64,7168]{1,0:T(8,128)(2,1)} %get-tuple-element.91.refs_2_) | copy-start | bytes 2752516
  109.6 23.7 %copy-start.7 = (s32[4]{0:T(128)S(1)}, s32[4]{0:T(128)}, u32[]{:S(2)}) copy-start(s32[4]{0:T(128)} %param.11) | copy-start | bytes 52
  109.7 23.9 %copy-start.8 = (s32[4]{0:T(128)S(1)}, s32[4]{0:T(128)}, u32[]{:S(2)}) copy-start(s32[4]{0:T(128)} %param.12) | copy-start | bytes 52
  129.8 30.9 %collective-permute-start.19 = (bf16[64,8192]{1,0:T(8,128)(2,1)}, bf16[64,8192]{1,0:T(8,128)(2,1)}, u32[]{:S(2)}, u32[]{:S(2)}) collective-permute-start(bf16[64,8192]{1,0:T(8,128)(2,1)} %get-tuple-element.86.refs_3_), channel_id=1, source_target_pairs={{4,0},{5,1},{6,2},{7,3},{8,12},{9,13},{10,14},{11,15},{20,16},{21,... | collective-permute-start | bytes 3145736 | tf_op jit(solution)/shard_map/ppermute | solution.py:119
  132.2 28.6 %collective-permute-start.20 = (bf16[64,8192]{1,0:T(8,128)(2,1)}, bf16[64,8192]{1,0:T(8,128)(2,1)}, u32[]{:S(2)}, u32[]{:S(2)}) collective-permute-start(bf16[64,8192]{1,0:T(8,128)(2,1)} %get-tuple-element.86.refs_3_), channel_id=1, source_target_pairs={{0,2},{1,3},{2,0},{3,1},{4,6},{5,7},{6,4},{7,5},{8,10},{9,11},{10,... | collective-permute-start | bytes 3145736 | tf_op jit(solution)/shard_map/ppermute | solution.py:62
  132.2 28.5 %collective-permute-start.21 = (bf16[64,7168]{1,0:T(8,128)(2,1)S(1)}, bf16[64,7168]{1,0:T(8,128)(2,1)}, u32[]{:S(2)}, u32[]{:S(2)}) collective-permute-start(bf16[64,7168]{1,0:T(8,128)(2,1)S(1)} %copy-done.3), channel_id=1, source_target_pairs={{0,16},{16,0},{1,17},{17,1},{2,18},{18,2},{3,19},{19,3},{4,20},{20... | collective-permute-start | bytes 2752520 | tf_op jit(solution)/shard_map/ppermute | solution.py:66
  133.6 12.1 %collective-permute-start.18 = (s32[2,4]{1,0:T(2,128)S(1)}, s32[2,4]{1,0:T(2,128)S(1)}, u32[]{:S(2)}, u32[]{:S(2)}) collective-permute-start(s32[2,4]{1,0:T(2,128)S(1)} %pad_add_fusion), channel_id=1, source_target_pairs={{0,1},{1,0},{2,3},{3,2},{4,5},{5,4},{6,7},{7,6},{8,9},{9,8},{10,11... | collective-permute-start | bytes 104 | tf_op jit(solution)/shard_map/ppermute | solution.py:62
  164.0 25.4 %collective-permute-start.23 = (bf16[64,8192]{1,0:T(8,128)(2,1)}, bf16[64,8192]{1,0:T(8,128)(2,1)}, u32[]{:S(2)}, u32[]{:S(2)}) collective-permute-start(bf16[64,8192]{1,0:T(8,128)(2,1)} %get-tuple-element.97.refs_1_), channel_id=1, source_target_pairs={{0,2},{1,3},{2,0},{3,1},{4,6},{5,7},{6,4},{7,5},{8,10},{9,11},{10,... | collective-permute-start | bytes 3145736 | tf_op jit(solution)/shard_map/ppermute | solution.py:62
  165.8 24.4 %collective-permute-start.24 = (bf16[64,8192]{1,0:T(8,128)(2,1)}, bf16[64,8192]{1,0:T(8,128)(2,1)}, u32[]{:S(2)}, u32[]{:S(2)}) collective-permute-start(bf16[64,8192]{1,0:T(8,128)(2,1)} %get-tuple-element.98), channel_id=1, source_target_pairs={{0,4},{1,5},{2,6},{3,7},{4,0},{5,1},{6,2},{7,3},{8,12},{9,13},{10,... | collective-permute-start | bytes 3145736 | tf_op jit(solution)/shard_map/ppermute | solution.py:62
  165.8 22.2 %collective-permute-start.25 = (bf16[64,7168]{1,0:T(8,128)(2,1)}, bf16[64,7168]{1,0:T(8,128)(2,1)S(1)}, u32[]{:S(2)}, u32[]{:S(2)}) collective-permute-start(bf16[64,7168]{1,0:T(8,128)(2,1)} %get-tuple-element.94.refs_0_), channel_id=1, source_target_pairs={{0,16},{16,0},{1,17},{17,1},{2,18},{18,2},{3,19},{19,3},{4,20},{20... | collective-permute-start | bytes 2752520 | tf_op jit(solution)/shard_map/ppermute | solution.py:66
  169.3 33.6 %collective-permute-start.26 = (bf16[32,7168]{1,0:T(8,128)(2,1)}, bf16[32,7168]{1,0:T(8,128)(2,1)}, u32[]{:S(2)}, u32[]{:S(2)}) collective-permute-start(bf16[32,7168]{1,0:T(8,128)(2,1)} %slice.19), channel_id=1, source_target_pairs={{0,2},{1,3},{2,0},{3,1},{4,6},{5,7},{6,4},{7,5},{8,10},{9,11},{10,... | collective-permute-start | bytes 1376264 | tf_op jit(solution)/shard_map/ppermute | solution.py:62
  171.3 31.7 %collective-permute-start.27 = (bf16[32,7168]{1,0:T(8,128)(2,1)}, bf16[32,7168]{1,0:T(8,128)(2,1)}, u32[]{:S(2)}, u32[]{:S(2)}) collective-permute-start(bf16[32,7168]{1,0:T(8,128)(2,1)} %slice.20), channel_id=1, source_target_pairs={{0,16},{16,0},{1,17},{17,1},{2,18},{18,2},{3,19},{19,3},{4,20},{20... | collective-permute-start | bytes 1376264 | tf_op jit(solution)/shard_map/ppermute | solution.py:66
  216.7 2.4 %collective-permute-start.28 = (f32[4,512]{1,0:T(4,128)S(1)}, f32[4,512]{1,0:T(4,128)S(1)}, u32[]{:S(2)}, u32[]{:S(2)}) collective-permute-start(f32[4,512]{1,0:T(4,128)S(1)} %pad_maximum_fusion), channel_id=1, source_target_pairs={{0,1},{1,0},{2,3},{3,2},{4,5},{5,4},{6,7},{7,6},{8,9},{9,8},{10,11... | collective-permute-start | bytes 24584 | tf_op jit(solution)/shard_map/ppermute | solution.py:62
  (7 other events, 31.0 us)

commit v9 on v8

--- a/solution.py
+++ b/solution.py
@@ -69,41 +69,42 @@
 PARTS = 4
 
 
-def after_kernel(count, merge, inside_ref, turn_ref, *refs):
-    if merge is None:
-        next_ref = refs[-1]
-    else:
-        refs, (held, arrived, gone) = refs[:-3], refs[-3:]
-        arrays, next_ref = refs[-1 - count : -1], refs[-1]
-        kept, over = (arrays[i] for i in merge)
-        rows = held.shape[0] // PARTS
+def through(held, arrived, gone, source, target):
+    rows = source.shape[0] // PARTS
+    parts = [pl.ds(i * rows, rows) for i in range(PARTS)]
+    come = [pltpu.make_async_copy(source.at[p], held.at[p], arrived.at[i]) for i, p in enumerate(parts)]
+    go = [pltpu.make_async_copy(held.at[p], target.at[p], gone.at[i]) for i, p in enumerate(parts)]
+    for copy in come:
+        copy.start()
+    for first, second in zip(come, go):
+        first.wait()
+        second.start()
+    for copy in go:
+        copy.wait()
+
+
+def after_kernel(count, merges, inside_ref, turn_ref, *refs):
+    if merges:
+        refs, staging = refs[:-3], refs[-3:]
+        source, target = refs[0], refs[-1 - count]
 
         @pl.when(inside_ref[0] == 1)
         def _():
-            parts = [pl.ds(i * rows, rows) for i in range(PARTS)]
-            come = [pltpu.make_async_copy(over.at[p], held.at[p], arrived.at[i]) for i, p in enumerate(parts)]
-            go = [pltpu.make_async_copy(held.at[p], kept.at[p], gone.at[i]) for i, p in enumerate(parts)]
-            for copy in come:
-                copy.start()
-            for first, second in zip(come, go):
-                first.wait()
-                second.start()
-            for copy in go:
-                copy.wait()
-
-    next_ref[0] = turn_ref[0]
+            through(*staging, source, target)
+
+    refs[-1][0] = turn_ref[0]
 
 
 def after(turn, arrays, inside, merge=None, there=()):
     count = len(arrays)
     scratch = []
     if merge is not None:
-        kept = arrays[merge[0]]
-        scratch = [pltpu.VMEM(kept.shape, kept.dtype)] + [pltpu.SemaphoreType.DMA((PARTS,))] * 2
+        there = (merge, *there)
+        scratch = [pltpu.VMEM(merge.shape, merge.dtype)] + [pltpu.SemaphoreType.DMA((PARTS,))] * 2
     hbm = pl.BlockSpec(memory_space=pltpu.HBM)
     scalar = pl.BlockSpec(memory_space=pltpu.SMEM)
     *arrays, turn = pl.pallas_call(
-        functools.partial(after_kernel, count, merge),
+        functools.partial(after_kernel, count, merge is not None),
         out_shape=[jax.ShapeDtypeStruct(x.shape, x.dtype) for x in (*arrays, turn)],
         in_specs=[scalar] * 2 + [hbm] * (len(there) + count),
         out_specs=[hbm] * count + [scalar],
@@ -113,6 +114,44 @@
         cost_estimate=LITTLE,
     )(inside, turn, *there, *arrays)
     return turn, arrays
+
+
+def prepare_kernel(works_ref, turn_ref, first_ref, left_ref, right_ref, *refs):
+    half_ref, one_ref, two_ref, next_ref, half_held, right_held, arrived, gone = refs[-8:]
+    next_ref[0] = turn_ref[0]
+    width = half_ref.shape[1]
+
+    @pl.when(works_ref[0] == 1)
+    def _():
+        start = pl.multiple_of(first_ref[0] * width, width)
+        through(half_held, arrived, gone, left_ref.at[:, pl.ds(start, width)], half_ref)
+        for target in (one_ref, two_ref):
+            through(right_held, arrived, gone, right_ref, target)
+
+
+def prepare(turn, works, first, left, right, made, passed):
+    rows, width = left.shape[0], left.shape[1] // 2
+    shapes = [(rows, width), right.shape, right.shape]
+    out_shape = [jax.ShapeDtypeStruct(x, left.dtype) for x in shapes]
+    made = () if made is None else made
+    given = (*passed, *made)
+    hbm = pl.BlockSpec(memory_space=pltpu.HBM)
+    scalar = pl.BlockSpec(memory_space=pltpu.SMEM)
+    aliases = {5 + i: i for i in range(len(given))}
+    outs = pl.pallas_call(
+        prepare_kernel,
+        out_shape=[jax.ShapeDtypeStruct(x.shape, x.dtype) for x in passed]
+        + out_shape
+        + [jax.ShapeDtypeStruct(turn.shape, turn.dtype)],
+        in_specs=[scalar] * 3 + [hbm] * (2 + len(given)),
+        out_specs=[hbm] * (len(passed) + 3) + [scalar],
+        input_output_aliases=aliases,
+        scratch_shapes=[pltpu.VMEM((rows, width), left.dtype), pltpu.VMEM(right.shape, right.dtype)]
+        + [pltpu.SemaphoreType.DMA((PARTS,))] * 2,
+        compiler_params=pltpu.CompilerParams(vmem_limit_bytes=VMEM_LIMIT),
+        cost_estimate=LITTLE,
+    )(works, turn, first, left, right, *given)
+    return outs[-1], outs[len(passed) : -1], outs[: len(passed)]
 
 
 def lines(array, pairs):
@@ -225,7 +264,6 @@
 
     a, b, c = {}, {}, {}
     a["own"] = lax.dynamic_slice_in_dim(left, group * half, half, 1)
-    c["own"] = lax.dynamic_slice_in_dim(left, (1 - group) * half, half, 1)
     b["own"] = query_right.reshape(local * ranks, -1)
     at_end = (z == 0) | (z == 3)
 
@@ -266,40 +304,39 @@
 
     grads_there = send(output_grads, CORE)
     grads = ((output_grads, zero), (grads_there, zero))
+
+    core = (me & CORE).reshape(1).astype(jnp.int32)
+    copies = (1 - mine, left, b["own"])
+    turn, made, (a["own"],) = prepare(zero, core, *copies, None, [a["own"]])
+    a_mid = middle(a["own"])
+    a["n"] = near(a["own"])
     a["x"] = over_x(a["own"])
-    a["n"] = near(a["own"])
-    a_mid = middle(a["own"])
-    turn = pause(zero)
-
-    turn, (a["x"], a["n"], a_mid, b_own) = after(
-        turn, [a["x"], a["n"], a_mid, b["own"]], inside, None, [acts_there]
-    )
+    turn, (c["own"], b_one, b_two), _ = prepare(turn, 1 - core, *copies, made, [])
+
+    turn, (a_mid, a["n"], a["x"]) = after(turn, [a_mid, a["n"], a["x"]], inside, None, [acts_there])
     a_out = outward(a_mid)
     a_in = middle(a["n"])
-    b["x"] = over_x(b_own)
+    b["x"] = over_x(b_one)
     c["x"] = swap_groups(a["x"])
     turn = pause(turn)
 
-    turn, (a_out, a_in, b["x"], c["x"], b_own) = after(
-        turn, [a_out, a_in, b["x"], c["x"], b_own], inside, None, [grads_there]
-    )
+    turn, (a_out, b["x"], a_in, c["x"]) = after(turn, [a_out, b["x"], a_in, c["x"]], inside, None, [grads_there])
     a_last = outward(a_in)
     a["xn"] = over_x(a["n"])
     c["n"] = swap_groups(a["n"])
-    b["f"] = across(b_own)
-    turn, (a["o"], a_in) = after(turn, [a_out, a_in], inside, (0, 1))
+    b["f"] = across(b_one)
+    turn, (a["o"],) = after(turn, [a_out], inside, a_in)
     a["xo"] = over_x(a["o"])
     turn = pause(turn)
 
-    turn, (a_last, a["xn"], c["n"], b_own) = after(turn, [a_last, a["xn"], c["n"], b["own"]], inside)
-    b["n"] = near(b_own)
-    turn, (a["f"], a_mid) = after(turn, [a_last, a_mid], inside, (0, 1))
+    turn, (a["f"], a["xn"], c["n"], b_two) = after(turn, [a_last, a["xn"], c["n"], b_two], inside, a_mid)
+    b["n"] = near(b_two)
     a["xf"] = over_x(a["f"])
     c["f"] = swap_groups(a["f"])
     turn, a_first = times_a(turn, 0)
 
-    turn, (a["xo"], c["f"], b["n"], a["o"], a["xn"]) = after(
-        turn, [a["xo"], c["f"], b["n"], a["o"], a["xn"]], inside
+    turn, (b["n"], a["xo"], c["f"], a["o"], a["xn"]) = after(
+        turn, [b["n"], a["xo"], c["f"], a["o"], a["xn"]], inside
     )
     b_in = middle(b["n"])
     c["o"] = swap_groups(a["o"])
@@ -313,8 +350,8 @@
     turn, score_first = times_b(turn, 0, True, spans, (a_first, c_first))
 
     split = c["f"].shape[0] // 2
-    turn, (b["o"], b["xf"], c["xn"], b_in, b_over, a["xf"], c["f"]) = after(
-        turn, [b_out, b["xf"], c["xn"], b_in, b["x"], a["xf"], c["f"]], inside, (0, 3)
+    turn, (b["o"], b["xf"], c["xn"], b_over, a["xf"], c["f"]) = after(
+        turn, [b_out, b["xf"], c["xn"], b["x"], a["xf"], c["f"]], inside, b_in
     )
     b["xo"] = over_x(b["o"])
     b["xn"] = near(b_over)
@@ -322,7 +359,7 @@
     c["low"] = swap_groups(a["xf"][split:])
     turn, a_second = times_a(turn, 1)
 
-    turn, (b["xo"], b["xn"], c["xo"]) = after(turn, [b["xo"], b["xn"], c["xo"]], inside)
+    turn, (b["xo"], c["xo"], b["xn"]) = after(turn, [b["xo"], c["xo"], b["xn"]], inside)
     turn, b_second = times_b(turn, 1)
     groups = (groups[0], ("xo", "o", "xn", "top", "low"))
     turn, score_second = times_c(turn, 1, False, spans, (a_second, b_second))

time: 222 us -> 222 us (level)
  starting transfers between devices: 45.7 us -> 32.9 us
  waiting for transfers between devices: 66.4 us -> 77.1 us
  Pallas kernels: 90 us -> 96 us
  local copies, waits for them, and re-layouts: 15.6 us -> 10.5 us
    ppermute x16, waiting for transfers between devices: 26.6 us -> 44.7 us  [flip(): return lax.ppermute(array, 'dp', [(i, i ^ code) for i in range(count)])]
    ppermute x6, waiting for transfers between devices: 30.5 us -> 17.4 us  [lines(): lax.ppermute(array, 'dp', [(a * 4 + rest, b * 4 + rest) for a, b in pairs...]
    ppermute x16, starting transfers between devices: 21.1 us -> 9.86 us  [flip(): return lax.ppermute(array, 'dp', [(i, i ^ code) for i in range(count)])]
    pallas_call x12, Pallas kernels: 19.3 us -> 25.3 us  [the longest x10 17.6 us: after(): pl.pallas_call(functools.partial(after_kernel, count, merge is not None),...]
    ppermute x7, waiting for transfers between devices: 9.24 us -> 15 us  [swap_groups(): return lax.ppermute(array, 'groups', [(0, 1), (1, 0)])]
    unnamed x22, local copies, waits for them, and re-layouts: 6.61 us -> 1.97 us
  transfers between devices with their start and end apart: 29 -> 29, of which waited for: 15 -> 19; matrix products, arithmetic and copies ran while one was open for 6% -> 4% of each run, Pallas kernels for 33% -> 35%
where the time goes in v9:
time: 222 us; the launch traced here: 219 us
  Pallas kernels  96 us (43%)
  waiting for transfers between devices  77.1 us (35%)
  starting transfers between devices  32.9 us (15%)
  local copies, waits for them, and re-layouts  10.5 us (5%)
    pallas_call x6, Pallas kernels, proj(): pl.pallas_call(functools.partial(proj_kernel, len(pieces), last), out_sha...  70.7 us
    ppermute x16, waiting for transfers between devices, flip(): return lax.ppermute(array, 'dp', [(i, i ^ code) for i in range(count)])  44.7 us
    pallas_call x10, Pallas kernels, after(): pl.pallas_call(functools.partial(after_kernel, count, merge is not None),...  17.6 us
    ppermute x6, waiting for transfers between devices, lines(): lax.ppermute(array, 'dp', [(a * 4 + rest, b * 4 + rest) for a, b in pairs...  17.4 us
    ppermute x6, starting transfers between devices, lines(): lax.ppermute(array, 'dp', [(a * 4 + rest, b * 4 + rest) for a, b in pairs...  16.5 us
    ppermute x7, waiting for transfers between devices, swap_groups(): return lax.ppermute(array, 'groups', [(0, 1), (1, 0)])  15 us
    ppermute x16, starting transfers between devices, flip(): return lax.ppermute(array, 'dp', [(i, i ^ code) for i in range(count)])  9.86 us
    pallas_call x2, Pallas kernels, prepare(): pl.pallas_call(prepare_kernel, out_shape=[jax.ShapeDtypeStruct(x.shape, x...  7.73 us
  transfers between devices with their start and end apart: 29, of which 19 were waited for; matrix products, arithmetic and copies ran while one was open for 4% of the time, Pallas kernels for 35%

profile of v9, /device:TPU:9, one launch (start us, length us, event | category | flops | bytes accessed | tf_op | source)
XLA Modules:
  0.0 218.7 jit_solution(10653121978841095333)
XLA Ops:
  0.7 2.2 constant_dynamic-slice_fusion.refs_0_
  2.8 6.5 %shard_map.73 = (bf16[64,7168]{1,0:T(8,128)(2,1)}, bf16[64,7168]{1,0:T(8,128)(2,1)}, bf16[64,8192]{1,0:T(8,128)(2,1)}, bf16[64,8192]{1,0:T(8,128)(2,1)}, s32[1]{0:T(128)}) custom-call(s32[1]{0:T(128)} %bitcast.1.works_ref, s32[1]{0:T(128)} %constant.24.clone.1.turn_ref, s32[1]{0:T(128)S(6)} %sub.17.first_ref, ...), custom_call_target="tpu_custom_call", output_to_operand_aliasing={{0}: (5, {})} | custom-call | flops 1 | bytes 1 | tf_op jit(solution)/shard_map/pallas_call | solution.py:141
  9.3 3.2 %collective-permute-start.1 = (bf16[64,7168]{1,0:T(8,128)(2,1)}, bf16[64,7168]{1,0:T(8,128)(2,1)S(1)}, u32[]{:S(2)}, u32[]{:S(2)}) collective-permute-start(bf16[64,7168]{1,0:T(8,128)(2,1)} %get-tuple-element.68.refs_0_), channel_id=1, source_target_pairs={{4,8},{5,9},{6,10},{7,11},{8,4},{9,5},{10,6},{11,7},{20,24},{21,25... | collective-permute-start | bytes 2752520 | tf_op jit(solution)/shard_map/ppermute | solution.py:158
  15.1 13.8 %collective-permute-done.1.refs_1_ = bf16[64,7168]{1,0:T(8,128)(2,1)S(1)} collective-permute-done((bf16[64,7168]{1,0:T(8,128)(2,1)}, bf16[64,7168]{1,0:T(8,128)(2,1)S(1)}, u32[]{:S(2)}, u32[]{:S(2)}) %collective-permute-start.1) | collective-permute-done | bytes 917536 | tf_op jit(solution)/shard_map/ppermute | solution.py:158
  30.6 3.0 %collective-permute-done.3.refs_3_ = bf16[64,7168]{1,0:T(8,128)(2,1)} collective-permute-done((bf16[64,7168]{1,0:T(8,128)(2,1)}, bf16[64,7168]{1,0:T(8,128)(2,1)}, u32[]{:S(2)}, u32[]{:S(2)}) %collective-permute-start.3) | collective-permute-done | bytes 917536 | tf_op jit(solution)/shard_map/ppermute | solution.py:62
  34.8 5.2 %collective-permute-start.5 = (bf16[64,7168]{1,0:T(8,128)(2,1)}, bf16[64,7168]{1,0:T(8,128)(2,1)S(1)}, u32[]{:S(2)}, u32[]{:S(2)}) collective-permute-start(bf16[64,7168]{1,0:T(8,128)(2,1)} %get-tuple-element.70.refs_0_), channel_id=1, source_target_pairs={{4,0},{5,1},{6,2},{7,3},{8,12},{9,13},{10,14},{11,15},{20,16},{21,... | collective-permute-start | bytes 2752520 | tf_op jit(solution)/shard_map/ppermute | solution.py:158
  40.0 2.1 collective-permute-start.7
  44.5 8.4 %collective-permute-done.6.refs_2_ = bf16[64,8192]{1,0:T(8,128)(2,1)} collective-permute-done((bf16[64,8192]{1,0:T(8,128)(2,1)}, bf16[64,8192]{1,0:T(8,128)(2,1)}, u32[]{:S(2)}, u32[]{:S(2)}) %collective-permute-start.6) | collective-permute-done | bytes 1048608 | tf_op jit(solution)/shard_map/ppermute | solution.py:62
  56.8 2.2 collective-permute-done.8.refs_4_
  60.2 1.7 collective-permute-start.9
  61.9 3.2 %shard_map.78 = (bf16[64,7168]{1,0:T(8,128)(2,1)}, s32[1]{0:T(128)}) custom-call(s32[1]{0:T(128)} %bitcast.inside_ref, s32[1]{0:T(128)} %get-tuple-element.74.turn_ref, bf16[64,7168]{1,0:T(8,128)(2,1)} %get-tuple-element.75.refs_0_, bf16[64,7168]{1,0:T(8,128)(2,1)} %get-tuple-element.76.refs_1_), custom_call_target="tpu_custom_call", output_to_operand_aliasing={{0}: (3, {})} | custom-call | flops 1 | bytes 1 | tf_op jit(solution)/shard_map/pallas_call | solution.py:106
  66.3 7.6 %collective-permute-done.10.refs_2_ = bf16[64,7168]{1,0:T(8,128)(2,1)} collective-permute-done((bf16[64,7168]{1,0:T(8,128)(2,1)}, bf16[64,7168]{1,0:T(8,128)(2,1)}, u32[]{:S(2)}, u32[]{:S(2)}) %collective-permute-start.10) | collective-permute-done | bytes 917536 | tf_op jit(solution)/shard_map/ppermute | solution.py:62
  73.8 2.9 %collective-permute-done.11.refs_3_ = bf16[64,7168]{1,0:T(8,128)(2,1)} collective-permute-done((bf16[64,7168]{1,0:T(8,128)(2,1)}, bf16[64,7168]{1,0:T(8,128)(2,1)}, u32[]{:S(2)}, u32[]{:S(2)}) %collective-permute-start.11) | collective-permute-done | bytes 917536 | tf_op jit(solution)/shard_map/ppermute | solution.py:66
  76.7 2.1 collective-permute-done.9.refs_1_
  79.8 3.2 %shard_map.80 = (bf16[64,7168]{1,0:T(8,128)(2,1)}, bf16[64,7168]{1,0:T(8,128)(2,1)}, bf16[64,7168]{1,0:T(8,128)(2,1)}, bf16[64,8192]{1,0:T(8,128)(2,1)}, s32[1]{0:T(128)}) custom-call(s32[1]{0:T(128)} %bitcast.inside_ref, s32[1]{0:T(128)} %shard_map.79.turn_ref, ...), custom_call_target="tpu_custom_call", output_to_operand_aliasing={{0}: (3, {}), {1}: (4, {}), {2}: (5, {}), {3}: (6, {})} | custom-call | flops 1 | bytes 1 | tf_op jit(solution)/shard_map/pallas_call | solution.py:106
  85.6 10.8 %shard_map.81 = (f32[1024,256]{1,0:T(8,128)}, s32[1]{0:T(128)}) custom-call(s32[1]{0:T(128)} %get-tuple-element.79.turn_ref, s32[3]{0:T(128)} %concatenate.25.at_ref, bf16[512,14336]{1,0:T(8,128)(2,1)} %own_ref.11, bf16[512,14336]{1,0:T(8,128)(2,1)} %collective-permute-done.refs_0_.other_ref, bf16[64,7168]{1,0:T(8,128)(2,1)} %get-tuple-element.68.refs_0_, ...), custom_call_target="tpu_custom_call" | custom-call | flops 1 | bytes 1 | tf_op jit(solution)/shard_map/pallas_call | solution.py:222
  96.4 9.4 %collective-permute-done.13.refs_1_ = bf16[64,7168]{1,0:T(8,128)(2,1)} collective-permute-done((bf16[64,7168]{1,0:T(8,128)(2,1)}, bf16[64,7168]{1,0:T(8,128)(2,1)}, u32[]{:S(2)}, u32[]{:S(2)}) %collective-permute-start.13) | collective-permute-done | bytes 917536 | tf_op jit(solution)/shard_map/ppermute | solution.py:62
  105.8 2.7 %collective-permute-done.12.refs_0_ = bf16[64,8192]{1,0:T(8,128)(2,1)} collective-permute-done((bf16[64,8192]{1,0:T(8,128)(2,1)}, bf16[64,8192]{1,0:T(8,128)(2,1)}, u32[]{:S(2)}, u32[]{:S(2)}) %collective-permute-start.12) | collective-permute-done | bytes 1048608 | tf_op jit(solution)/shard_map/ppermute | solution.py:62
  110.4 2.1 collective-permute-start.19
  112.6 10.8 %shard_map.83 = (f32[1024,256]{1,0:T(8,128)}, s32[1]{0:T(128)}) custom-call(s32[1]{0:T(128)} %get-tuple-element.85.turn_ref, s32[3]{0:T(128)} %concatenate.26.at_ref, bf16[512,14336]{1,0:T(8,128)(2,1)} %own_ref.11, bf16[512,14336]{1,0:T(8,128)(2,1)} %collective-permute-done.refs_0_.other_ref, bf16[64,7168]{1,0:T(8,128)(2,1)} %get-tuple-element.86.refs_0_, ...), custom_call_target="tpu_custom_call" | custom-call | flops 1 | bytes 1 | tf_op jit(solution)/shard_map/pallas_call | solution.py:222
  123.4 8.1 %collective-permute-done.15.refs_0_ = bf16[64,8192]{1,0:T(8,128)(2,1)} collective-permute-done((bf16[64,8192]{1,0:T(8,128)(2,1)}, bf16[64,8192]{1,0:T(8,128)(2,1)}, u32[]{:S(2)}, u32[]{:S(2)}) %collective-permute-start.15) | collective-permute-done | bytes 1048608 | tf_op jit(solution)/shard_map/ppermute | solution.py:62
  133.6 2.3 %collective-permute-start.20 = (bf16[64,8192]{1,0:T(8,128)(2,1)}, bf16[64,8192]{1,0:T(8,128)(2,1)}, u32[]{:S(2)}, u32[]{:S(2)}) collective-permute-start(bf16[64,8192]{1,0:T(8,128)(2,1)} %get-tuple-element.96.refs_3_), channel_id=1, source_target_pairs={{4,0},{5,1},{6,2},{7,3},{8,12},{9,13},{10,14},{11,15},{20,16},{21,... | collective-permute-start | bytes 3145736 | tf_op jit(solution)/shard_map/ppermute | solution.py:158
  141.0 13.8 %shard_map.85 = (f32[8,256]{1,0:T(8,128)}, s32[1]{0:T(128)}) custom-call(s32[1]{0:T(128)} %get-tuple-element.93.turn_ref, s32[3]{0:T(128)} %broadcast_8_at_ref.2.at_ref, bf16[512,8192]{1,0:T(8,128)(2,1)} %own_ref.10, bf16[512,8192]{1,0:T(8,128)(2,1)} %collective-permute-done.4.refs_0_.other_ref, bf16[64,8192]{1,0:T(8,128)(2,1)} %bitcast.22, ...), custom_call_target="tpu_custom_call" | custom-call | flops 1 | bytes 1 | tf_op jit(solution)/shard_map/pallas_call | solution.py:222
  154.8 4.3 %collective-permute-done.22.refs_3_ = bf16[64,7168]{1,0:T(8,128)(2,1)S(1)} collective-permute-done((bf16[64,7168]{1,0:T(8,128)(2,1)}, bf16[64,7168]{1,0:T(8,128)(2,1)S(1)}, u32[]{:S(2)}, u32[]{:S(2)}) %collective-permute-start.22) | collective-permute-done | bytes 917536 | tf_op jit(solution)/shard_map/ppermute | solution.py:66
  160.0 3.2 %shard_map.86 = (bf16[64,8192]{1,0:T(8,128)(2,1)}, bf16[64,8192]{1,0:T(8,128)(2,1)}, bf16[64,7168]{1,0:T(8,128)(2,1)}, bf16[64,8192]{1,0:T(8,128)(2,1)}, bf16[64...) custom-call(s32[1]{0:T(128)} %bitcast.inside_ref, ...), custom_call_target="tpu_custom_call", output_to_operand_aliasing={{0}: (3, {}), {1}: (4, {}), {2}: (5, {}), {3}: (6, {}), {4}... | custom-call | flops 1 | bytes 1 | tf_op jit(solution)/shard_map/pallas_call | solution.py:106
  164.5 2.2 collective-permute-start.24
  166.7 1.8 slice.19
  168.7 1.8 slice.20
  170.7 10.8 %shard_map.87 = (f32[1024,256]{1,0:T(8,128)}, s32[1]{0:T(128)}) custom-call(s32[1]{0:T(128)} %get-tuple-element.103.turn_ref, s32[3]{0:T(128)} %concatenate.25.at_ref, bf16[512,14336]{1,0:T(8,128)(2,1)} %own_ref.11, bf16[512,14336]{1,0:T(8,128)(2,1)} %collective-permute-done.refs_0_.other_ref, bf16[64,7168]{1,0:T(8,128)(2,1)} %get-tuple-element.104.refs_0_, ...), custom_call_target="tpu_custom_call" | custom-call | flops 1 | bytes 1 | tf_op jit(solution)/shard_map/pallas_call | solution.py:222
  181.5 5.6 %collective-permute-done.24.refs_1_ = bf16[64,7168]{1,0:T(8,128)(2,1)S(1)} collective-permute-done((bf16[64,7168]{1,0:T(8,128)(2,1)}, bf16[64,7168]{1,0:T(8,128)(2,1)S(1)}, u32[]{:S(2)}, u32[]{:S(2)}) %collective-permute-start.24) | collective-permute-done | bytes 917536 | tf_op jit(solution)/shard_map/ppermute | solution.py:66
  190.9 11.6 %shard_map.89 = (f32[1024,256]{1,0:T(8,128)}, s32[1]{0:T(128)}) custom-call(s32[1]{0:T(128)} %get-tuple-element.109.turn_ref, s32[3]{0:T(128)} %broadcast_8_at_ref.2.at_ref, bf16[512,8192]{1,0:T(8,128)(2,1)} %own_ref.10, bf16[512,8192]{1,0:T(8,128)(2,1)} %collective-permute-done.4.refs_0_.other_ref, bf16[64,8192]{1,0:T(8,128)(2,1)} %get-tuple-element.110.refs_0_, ...), custom_call_target="tpu_custom_call" | custom-call | flops 1 | bytes 1 | tf_op jit(solution)/shard_map/pallas_call | solution.py:222
  202.5 12.9 %shard_map.90 = (f32[8,256]{1,0:T(8,128)}, s32[1]{0:T(128)}) custom-call(s32[1]{0:T(128)} %get-tuple-element.113.turn_ref, s32[3]{0:T(128)} %concatenate.26.at_ref, bf16[512,14336]{1,0:T(8,128)(2,1)} %own_ref.11, bf16[512,14336]{1,0:T(8,128)(2,1)} %collective-permute-done.refs_0_.other_ref, bf16[64,7168]{1,0:T(8,128)(2,1)} %get-tuple-element.114.refs_0_, ...), custom_call_target="tpu_custom_call" | custom-call | flops 1 | bytes 1 | tf_op jit(solution)/shard_map/pallas_call | solution.py:222
  (87 shorter events, 37.0 us)
Async XLA Ops:
  0.0 33.6 %collective-permute-start = (bf16[512,14336]{1,0:T(8,128)(2,1)}, bf16[512,14336]{1,0:T(8,128)(2,1)}, u32[]{:S(2)}, u32[]{:S(2)}) collective-permute-start(bf16[512,14336]{1,0:T(8,128)(2,1)} %own_ref.11), channel_id=1, source_target_pairs={{0,1},{1,0},{2,3},{3,2},{4,5},{5,4},{6,7},{7,6},{8,9},{9,8},{10,11... | collective-permute-start | bytes 44040200 | tf_op jit(solution)/shard_map/ppermute | solution.py:62
  0.7 53.4 %collective-permute-start.4 = (bf16[512,8192]{1,0:T(8,128)(2,1)}, bf16[512,8192]{1,0:T(8,128)(2,1)}, u32[]{:S(2)}, u32[]{:S(2)}) collective-permute-start(bf16[512,8192]{1,0:T(8,128)(2,1)} %own_ref.10), channel_id=1, source_target_pairs={{0,1},{1,0},{2,3},{3,2},{4,5},{5,4},{6,7},{7,6},{8,9},{9,8},{10,11... | collective-permute-start | bytes 25165832 | tf_op jit(solution)/shard_map/ppermute | solution.py:62
  9.3 19.7 %collective-permute-start.1 = (bf16[64,7168]{1,0:T(8,128)(2,1)}, bf16[64,7168]{1,0:T(8,128)(2,1)S(1)}, u32[]{:S(2)}, u32[]{:S(2)}) collective-permute-start(bf16[64,7168]{1,0:T(8,128)(2,1)} %get-tuple-element.68.refs_0_), channel_id=1, source_target_pairs={{4,8},{5,9},{6,10},{7,11},{8,4},{9,5},{10,6},{11,7},{20,24},{21,25... | collective-permute-start | bytes 2752520 | tf_op jit(solution)/shard_map/ppermute | solution.py:158
  12.5 18.1 %collective-permute-start.2 = (bf16[64,7168]{1,0:T(8,128)(2,1)}, bf16[64,7168]{1,0:T(8,128)(2,1)}, u32[]{:S(2)}, u32[]{:S(2)}) collective-permute-start(bf16[64,7168]{1,0:T(8,128)(2,1)} %get-tuple-element.68.refs_0_), channel_id=1, source_target_pairs={{0,4},{1,5},{2,6},{3,7},{4,0},{5,1},{6,2},{7,3},{8,12},{9,13},{10,... | collective-permute-start | bytes 2752520 | tf_op jit(solution)/shard_map/ppermute | solution.py:62
  12.6 21.0 %collective-permute-start.3 = (bf16[64,7168]{1,0:T(8,128)(2,1)}, bf16[64,7168]{1,0:T(8,128)(2,1)}, u32[]{:S(2)}, u32[]{:S(2)}) collective-permute-start(bf16[64,7168]{1,0:T(8,128)(2,1)} %get-tuple-element.68.refs_0_), channel_id=1, source_target_pairs={{0,2},{1,3},{2,0},{3,1},{4,6},{5,7},{6,4},{7,5},{8,10},{9,11},{10,... | collective-permute-start | bytes 2752520 | tf_op jit(solution)/shard_map/ppermute | solution.py:62
  29.0 23.9 %collective-permute-start.6 = (bf16[64,8192]{1,0:T(8,128)(2,1)}, bf16[64,8192]{1,0:T(8,128)(2,1)}, u32[]{:S(2)}, u32[]{:S(2)}) collective-permute-start(bf16[64,8192]{1,0:T(8,128)(2,1)} %get-tuple-element.71), channel_id=1, source_target_pairs={{0,2},{1,3},{2,0},{3,1},{4,6},{5,7},{6,4},{7,5},{8,10},{9,11},{10,... | collective-permute-start | bytes 3145736 | tf_op jit(solution)/shard_map/ppermute | solution.py:62
  34.8 20.6 %collective-permute-start.5 = (bf16[64,7168]{1,0:T(8,128)(2,1)}, bf16[64,7168]{1,0:T(8,128)(2,1)S(1)}, u32[]{:S(2)}, u32[]{:S(2)}) collective-permute-start(bf16[64,7168]{1,0:T(8,128)(2,1)} %get-tuple-element.70.refs_0_), channel_id=1, source_target_pairs={{4,0},{5,1},{6,2},{7,3},{8,12},{9,13},{10,14},{11,15},{20,16},{21,... | collective-permute-start | bytes 2752520 | tf_op jit(solution)/shard_map/ppermute | solution.py:158
  40.0 16.9 %collective-permute-start.7 = (bf16[64,7168]{1,0:T(8,128)(2,1)}, bf16[64,7168]{1,0:T(8,128)(2,1)}, u32[]{:S(2)}, u32[]{:S(2)}) collective-permute-start(bf16[64,7168]{1,0:T(8,128)(2,1)} %get-tuple-element.72.refs_2_), channel_id=1, source_target_pairs={{4,8},{5,9},{6,10},{7,11},{8,4},{9,5},{10,6},{11,7},{20,24},{21,25... | collective-permute-start | bytes 2752520 | tf_op jit(solution)/shard_map/ppermute | solution.py:158
  42.0 16.9 %collective-permute-start.8 = (bf16[64,7168]{1,0:T(8,128)(2,1)}, bf16[64,7168]{1,0:T(8,128)(2,1)}, u32[]{:S(2)}, u32[]{:S(2)}) collective-permute-start(bf16[64,7168]{1,0:T(8,128)(2,1)} %get-tuple-element.73.refs_1_), channel_id=1, source_target_pairs={{0,16},{16,0},{1,17},{17,1},{2,18},{18,2},{3,19},{19,3},{4,20},{20... | collective-permute-start | bytes 2752520 | tf_op jit(solution)/shard_map/ppermute | solution.py:66
  52.9 20.9 %collective-permute-start.10 = (bf16[64,7168]{1,0:T(8,128)(2,1)}, bf16[64,7168]{1,0:T(8,128)(2,1)}, u32[]{:S(2)}, u32[]{:S(2)}) collective-permute-start(bf16[64,7168]{1,0:T(8,128)(2,1)} %get-tuple-element.72.refs_2_), channel_id=1, source_target_pairs={{0,2},{1,3},{2,0},{3,1},{4,6},{5,7},{6,4},{7,5},{8,10},{9,11},{10,... | collective-permute-start | bytes 2752520 | tf_op jit(solution)/shard_map/ppermute | solution.py:62
  54.1 22.6 %collective-permute-start.11 = (bf16[64,7168]{1,0:T(8,128)(2,1)}, bf16[64,7168]{1,0:T(8,128)(2,1)}, u32[]{:S(2)}, u32[]{:S(2)}) collective-permute-start(bf16[64,7168]{1,0:T(8,128)(2,1)} %get-tuple-element.72.refs_2_), channel_id=1, source_target_pairs={{0,16},{16,0},{1,17},{17,1},{2,18},{18,2},{3,19},{19,3},{4,20},{20... | collective-permute-start | bytes 2752520 | tf_op jit(solution)/shard_map/ppermute | solution.py:66
  60.2 18.7 %collective-permute-start.9 = (bf16[64,7168]{1,0:T(8,128)(2,1)}, bf16[64,7168]{1,0:T(8,128)(2,1)S(1)}, u32[]{:S(2)}, u32[]{:S(2)}) collective-permute-start(bf16[64,7168]{1,0:T(8,128)(2,1)} %get-tuple-element.75.refs_0_), channel_id=1, source_target_pairs={{4,0},{5,1},{6,2},{7,3},{8,12},{9,13},{10,14},{11,15},{20,16},{21,... | collective-permute-start | bytes 2752520 | tf_op jit(solution)/shard_map/ppermute | solution.py:158
  82.9 25.6 %collective-permute-start.12 = (bf16[64,8192]{1,0:T(8,128)(2,1)}, bf16[64,8192]{1,0:T(8,128)(2,1)}, u32[]{:S(2)}, u32[]{:S(2)}) collective-permute-start(bf16[64,8192]{1,0:T(8,128)(2,1)} %get-tuple-element.82), channel_id=1, source_target_pairs={{0,4},{1,5},{2,6},{3,7},{4,0},{5,1},{6,2},{7,3},{8,12},{9,13},{10,... | collective-permute-start | bytes 3145736 | tf_op jit(solution)/shard_map/ppermute | solution.py:62
  83.0 22.8 %collective-permute-start.13 = (bf16[64,7168]{1,0:T(8,128)(2,1)}, bf16[64,7168]{1,0:T(8,128)(2,1)}, u32[]{:S(2)}, u32[]{:S(2)}) collective-permute-start(bf16[64,7168]{1,0:T(8,128)(2,1)} %get-tuple-element.83.refs_3_), channel_id=1, source_target_pairs={{0,2},{1,3},{2,0},{3,1},{4,6},{5,7},{6,4},{7,5},{8,10},{9,11},{10,... | collective-permute-start | bytes 2752520 | tf_op jit(solution)/shard_map/ppermute | solution.py:62
  83.3 22.5 %collective-permute-start.14 = (bf16[64,7168]{1,0:T(8,128)(2,1)}, bf16[64,7168]{1,0:T(8,128)(2,1)S(1)}, u32[]{:S(2)}, u32[]{:S(2)}) collective-permute-start(bf16[64,7168]{1,0:T(8,128)(2,1)} %get-tuple-element.80.refs_3_), channel_id=1, source_target_pairs={{0,16},{16,0},{1,17},{17,1},{2,18},{18,2},{3,19},{19,3},{4,20},{20... | collective-permute-start | bytes 2752520 | tf_op jit(solution)/shard_map/ppermute | solution.py:66
  83.6 48.0 %collective-permute-start.15 = (bf16[64,8192]{1,0:T(8,128)(2,1)}, bf16[64,8192]{1,0:T(8,128)(2,1)}, u32[]{:S(2)}, u32[]{:S(2)}) collective-permute-start(bf16[64,8192]{1,0:T(8,128)(2,1)} %get-tuple-element.71), channel_id=1, source_target_pairs={{0,12},{1,13},{2,14},{3,15},{4,8},{5,9},{6,10},{7,11},{8,4},{9,5},... | collective-permute-start | bytes 3145736 | tf_op jit(solution)/shard_map/ppermute | solution.py:62
  85.3 46.2 %collective-permute-start.16 = (bf16[64,7168]{1,0:T(8,128)(2,1)}, bf16[64,7168]{1,0:T(8,128)(2,1)}, u32[]{:S(2)}, u32[]{:S(2)}) collective-permute-start(bf16[64,7168]{1,0:T(8,128)(2,1)} %get-tuple-element.80.refs_3_), channel_id=1, source_target_pairs={{0,2},{1,3},{2,0},{3,1},{4,6},{5,7},{6,4},{7,5},{8,10},{9,11},{10,... | collective-permute-start | bytes 2752520 | tf_op jit(solution)/shard_map/ppermute | solution.py:62
  109.7 21.9 %collective-permute-start.17 = (bf16[64,7168]{1,0:T(8,128)(2,1)}, bf16[64,7168]{1,0:T(8,128)(2,1)S(1)}, u32[]{:S(2)}, u32[]{:S(2)}) collective-permute-start(bf16[64,7168]{1,0:T(8,128)(2,1)} %get-tuple-element.91.refs_1_), channel_id=1, source_target_pairs={{0,16},{16,0},{1,17},{17,1},{2,18},{18,2},{3,19},{19,3},{4,20},{20... | collective-permute-start | bytes 2752520 | tf_op jit(solution)/shard_map/ppermute | solution.py:66
  110.4 48.7 %collective-permute-start.19 = (bf16[64,8192]{1,0:T(8,128)(2,1)}, bf16[64,8192]{1,0:T(8,128)(2,1)}, u32[]{:S(2)}, u32[]{:S(2)}) collective-permute-start(bf16[64,8192]{1,0:T(8,128)(2,1)} %get-tuple-element.95.refs_2_), channel_id=1, source_target_pairs={{4,8},{5,9},{6,10},{7,11},{8,4},{9,5},{10,6},{11,7},{20,24},{21,25... | collective-permute-start | bytes 3145736 | tf_op jit(solution)/shard_map/ppermute | solution.py:158
  112.5 25.9 %copy-start.8 = (s32[4]{0:T(128)S(1)}, s32[4]{0:T(128)}, u32[]{:S(2)}) copy-start(s32[4]{0:T(128)} %param.11) | copy-start | bytes 52
  112.5 26.0 %copy-start.9 = (s32[4]{0:T(128)S(1)}, s32[4]{0:T(128)}, u32[]{:S(2)}) copy-start(s32[4]{0:T(128)} %param.12) | copy-start | bytes 52
  133.6 25.5 %collective-permute-start.20 = (bf16[64,8192]{1,0:T(8,128)(2,1)}, bf16[64,8192]{1,0:T(8,128)(2,1)}, u32[]{:S(2)}, u32[]{:S(2)}) collective-permute-start(bf16[64,8192]{1,0:T(8,128)(2,1)} %get-tuple-element.96.refs_3_), channel_id=1, source_target_pairs={{4,0},{5,1},{6,2},{7,3},{8,12},{9,13},{10,14},{11,15},{20,16},{21,... | collective-permute-start | bytes 3145736 | tf_op jit(solution)/shard_map/ppermute | solution.py:158
  135.9 24.1 %collective-permute-start.21 = (bf16[64,8192]{1,0:T(8,128)(2,1)}, bf16[64,8192]{1,0:T(8,128)(2,1)}, u32[]{:S(2)}, u32[]{:S(2)}) collective-permute-start(bf16[64,8192]{1,0:T(8,128)(2,1)} %get-tuple-element.96.refs_3_), channel_id=1, source_target_pairs={{0,2},{1,3},{2,0},{3,1},{4,6},{5,7},{6,4},{7,5},{8,10},{9,11},{10,... | collective-permute-start | bytes 3145736 | tf_op jit(solution)/shard_map/ppermute | solution.py:62
  137.1 22.0 %collective-permute-start.22 = (bf16[64,7168]{1,0:T(8,128)(2,1)}, bf16[64,7168]{1,0:T(8,128)(2,1)S(1)}, u32[]{:S(2)}, u32[]{:S(2)}) collective-permute-start(bf16[64,7168]{1,0:T(8,128)(2,1)} %get-tuple-element.101.refs_2_), channel_id=1, source_target_pairs={{0,16},{16,0},{1,17},{17,1},{2,18},{18,2},{3,19},{19,3},{4,20},{20... | collective-permute-start | bytes 2752520 | tf_op jit(solution)/shard_map/ppermute | solution.py:66
  138.6 1.2 collective-permute-start.18
  154.8 15.8 %copy-start.7 = (f32[8,256]{1,0:T(8,128)S(1)}, f32[8,256]{1,0:T(8,128)}, u32[]{:S(2)}) copy-start(f32[8,256]{1,0:T(8,128)} %get-tuple-element.99) | copy-start | bytes 24580
  163.2 24.8 %collective-permute-start.23 = (bf16[64,8192]{1,0:T(8,128)(2,1)}, bf16[64,8192]{1,0:T(8,128)(2,1)}, u32[]{:S(2)}, u32[]{:S(2)}) collective-permute-start(bf16[64,8192]{1,0:T(8,128)(2,1)} %get-tuple-element.107.refs_1_), channel_id=1, source_target_pairs={{0,2},{1,3},{2,0},{3,1},{4,6},{5,7},{6,4},{7,5},{8,10},{9,11},{10,... | collective-permute-start | bytes 3145736 | tf_op jit(solution)/shard_map/ppermute | solution.py:62
  164.5 25.1 %collective-permute-start.25 = (bf16[64,8192]{1,0:T(8,128)(2,1)}, bf16[64,8192]{1,0:T(8,128)(2,1)}, u32[]{:S(2)}, u32[]{:S(2)}) collective-permute-start(bf16[64,8192]{1,0:T(8,128)(2,1)} %get-tuple-element.108), channel_id=1, source_target_pairs={{0,4},{1,5},{2,6},{3,7},{4,0},{5,1},{6,2},{7,3},{8,12},{9,13},{10,... | collective-permute-start | bytes 3145736 | tf_op jit(solution)/shard_map/ppermute | solution.py:62
  164.5 22.6 %collective-permute-start.24 = (bf16[64,7168]{1,0:T(8,128)(2,1)}, bf16[64,7168]{1,0:T(8,128)(2,1)S(1)}, u32[]{:S(2)}, u32[]{:S(2)}) collective-permute-start(bf16[64,7168]{1,0:T(8,128)(2,1)} %get-tuple-element.104.refs_0_), channel_id=1, source_target_pairs={{0,16},{16,0},{1,17},{17,1},{2,18},{18,2},{3,19},{19,3},{4,20},{20... | collective-permute-start | bytes 2752520 | tf_op jit(solution)/shard_map/ppermute | solution.py:66
  168.6 33.9 %collective-permute-start.26 = (bf16[32,7168]{1,0:T(8,128)(2,1)}, bf16[32,7168]{1,0:T(8,128)(2,1)}, u32[]{:S(2)}, u32[]{:S(2)}) collective-permute-start(bf16[32,7168]{1,0:T(8,128)(2,1)} %slice.19), channel_id=1, source_target_pairs={{0,2},{1,3},{2,0},{3,1},{4,6},{5,7},{6,4},{7,5},{8,10},{9,11},{10,... | collective-permute-start | bytes 1376264 | tf_op jit(solution)/shard_map/ppermute | solution.py:62
  170.6 32.0 %collective-permute-start.27 = (bf16[32,7168]{1,0:T(8,128)(2,1)}, bf16[32,7168]{1,0:T(8,128)(2,1)}, u32[]{:S(2)}, u32[]{:S(2)}) collective-permute-start(bf16[32,7168]{1,0:T(8,128)(2,1)} %slice.20), channel_id=1, source_target_pairs={{0,16},{16,0},{1,17},{17,1},{2,18},{18,2},{3,19},{19,3},{4,20},{20... | collective-permute-start | bytes 1376264 | tf_op jit(solution)/shard_map/ppermute | solution.py:66
  216.2 1.7 collective-permute-start.28
  (8 other events, 32.1 us)

commit v10 on v9

--- a/solution.py
+++ b/solution.py
@@ -83,10 +83,10 @@
         copy.wait()
 
 
-def after_kernel(count, merges, inside_ref, turn_ref, *refs):
+def after_kernel(count, merges, turn_ref, *refs):
     if merges:
         refs, staging = refs[:-3], refs[-3:]
-        source, target = refs[0], refs[-1 - count]
+        inside_ref, source, target = refs[0], refs[1], refs[-1 - count]
 
         @pl.when(inside_ref[0] == 1)
         def _():
@@ -95,24 +95,25 @@
     refs[-1][0] = turn_ref[0]
 
 
-def after(turn, arrays, inside, merge=None, there=()):
+def after(turn, arrays, there=(), merge=None):
     count = len(arrays)
-    scratch = []
-    if merge is not None:
-        there = (merge, *there)
-        scratch = [pltpu.VMEM(merge.shape, merge.dtype)] + [pltpu.SemaphoreType.DMA((PARTS,))] * 2
     hbm = pl.BlockSpec(memory_space=pltpu.HBM)
     scalar = pl.BlockSpec(memory_space=pltpu.SMEM)
+    first, specs, scratch = (), [], []
+    if merge is not None:
+        first, specs = merge, [scalar, hbm]
+        scratch = [pltpu.VMEM(merge[1].shape, merge[1].dtype)] + [pltpu.SemaphoreType.DMA((PARTS,))] * 2
+    ahead = 1 + len(first) + len(there)
     *arrays, turn = pl.pallas_call(
         functools.partial(after_kernel, count, merge is not None),
         out_shape=[jax.ShapeDtypeStruct(x.shape, x.dtype) for x in (*arrays, turn)],
-        in_specs=[scalar] * 2 + [hbm] * (len(there) + count),
+        in_specs=[scalar] + specs + [hbm] * (len(there) + count),
         out_specs=[hbm] * count + [scalar],
-        input_output_aliases={2 + len(there) + i: i for i in range(count)},
+        input_output_aliases={ahead + i: i for i in range(count)},
         scratch_shapes=scratch,
         compiler_params=pltpu.CompilerParams(vmem_limit_bytes=VMEM_LIMIT),
         cost_estimate=LITTLE,
-    )(inside, turn, *there, *arrays)
+    )(turn, *first, *there, *arrays)
     return turn, arrays
 
 
@@ -152,12 +153,6 @@
         cost_estimate=LITTLE,
     )(works, turn, first, left, right, *given)
     return outs[-1], outs[len(passed) : -1], outs[: len(passed)]
-
-
-def lines(array, pairs):
-    return lax.ppermute(
-        array, "dp", [(a * 4 + rest, b * 4 + rest) for a, b in pairs for rest in range(4)]
-    )
 
 
 def score_into(out_ref, spans_ref, terms_of, rows):
@@ -252,7 +247,6 @@
 def relay(hidden_acts, output_grads, query_left, query_right, bucket_ids, seq_lengths):
     count = lax.axis_size("dp")
     me, group = lax.axis_index("dp"), lax.axis_index("groups")
-    z = me // 4
     local, ranks = query_left.shape[:2]
     left = query_left.reshape(local * ranks, -1)
     half = left.shape[1] // 2
@@ -265,16 +259,13 @@
     a, b, c = {}, {}, {}
     a["own"] = lax.dynamic_slice_in_dim(left, group * half, half, 1)
     b["own"] = query_right.reshape(local * ranks, -1)
-    at_end = (z == 0) | (z == 3)
 
     def near(piece):
         return send(piece, NEAR)
 
-    def middle(piece):
-        return lines(piece, [(1, 2), (2, 1)])
-
-    def outward(piece):
-        return lines(piece, [(1, 0), (2, 3)])
+    def lines(piece, pairs):
+        pairs = [(i * 4 + rest, j * 4 + rest) for i, j in pairs for rest in range(4)]
+        return lax.ppermute(piece, "dp", pairs)
 
     def across(piece):
         return send(piece, ACROSS)
@@ -282,11 +273,10 @@
     def over_x(piece):
         return send(piece, COLUMN)
 
-    inside = (~at_end).reshape(1).astype(jnp.int32)
     mine = jnp.reshape(group, (1,)).astype(jnp.int32)
     zero = jnp.zeros((1,), jnp.int32)
     acts = ((hidden_acts, zero), (acts_there, zero))
-    groups = (("own", "x", "n", "f"), ("xo", "o", "xn", "xf"))
+    groups = (("own", "x", "n", "f"), ("xn", "xf", "o", "xo"))
     tokens_here = hidden_acts.shape[0]
     steps = 4
 
@@ -299,8 +289,10 @@
     def times_b(turn, k, *score):
         return proj(turn, grads, tokens_here, [b[i] for i in groups[k]], zero, steps, *score)
 
+    inside = ((me // 4) % 3 != 0).reshape(1).astype(jnp.int32)
+
     def pause(turn):
-        return after(turn, [], inside)[0]
+        return after(turn, [])[0]
 
     grads_there = send(output_grads, CORE)
     grads = ((output_grads, zero), (grads_there, zero))
@@ -308,67 +300,69 @@
     core = (me & CORE).reshape(1).astype(jnp.int32)
     copies = (1 - mine, left, b["own"])
     turn, made, (a["own"],) = prepare(zero, core, *copies, None, [a["own"]])
-    a_mid = middle(a["own"])
+    a["x"] = over_x(a["own"])
     a["n"] = near(a["own"])
-    a["x"] = over_x(a["own"])
+    a_mid = lines(a["own"], [(1, 2), (2, 1)])
     turn, (c["own"], b_one, b_two), _ = prepare(turn, 1 - core, *copies, made, [])
 
-    turn, (a_mid, a["n"], a["x"]) = after(turn, [a_mid, a["n"], a["x"]], inside, None, [acts_there])
-    a_out = outward(a_mid)
-    a_in = middle(a["n"])
+    turn, (a["x"], a["n"], a_mid, b_one, ends) = after(
+        turn, [a["x"], a["n"], a_mid, b_one, a["own"]], [acts_there]
+    )
+    a_end = lines(ends, [(0, 3), (3, 0)])
+    a["own"] = ends
     b["x"] = over_x(b_one)
     c["x"] = swap_groups(a["x"])
     turn = pause(turn)
 
-    turn, (a_out, b["x"], a_in, c["x"]) = after(turn, [a_out, b["x"], a_in, c["x"]], inside, None, [grads_there])
-    a_last = outward(a_in)
+    turn, (a["f"], b["x"], c["x"], b_one, a["n"]) = after(
+        turn, [a_end, b["x"], c["x"], b_one, a["n"]], [grads_there], (inside, a_mid)
+    )
+    a["o"] = near(a["f"])
     a["xn"] = over_x(a["n"])
     c["n"] = swap_groups(a["n"])
     b["f"] = across(b_one)
-    turn, (a["o"],) = after(turn, [a_out], inside, a_in)
-    a["xo"] = over_x(a["o"])
-    turn = pause(turn)
-
-    turn, (a["f"], a["xn"], c["n"], b_two) = after(turn, [a_last, a["xn"], c["n"], b_two], inside, a_mid)
-    b["n"] = near(b_two)
+    turn, a_first = times_a(turn, 0)
+
+    turn, (a["o"], a["xn"], c["n"], b_two) = after(turn, [a["o"], a["xn"], c["n"], b_two])
     a["xf"] = over_x(a["f"])
     c["f"] = swap_groups(a["f"])
-    turn, a_first = times_a(turn, 0)
-
-    turn, (b["n"], a["xo"], c["f"], a["o"], a["xn"]) = after(
-        turn, [b["n"], a["xo"], c["f"], a["o"], a["xn"]], inside
-    )
-    b_in = middle(b["n"])
+    b["n"] = near(b_two)
+    turn = pause(turn)
+
+    turn, (a["xf"], c["f"], b["n"], b["f"], a["o"]) = after(turn, [a["xf"], c["f"], b["n"], b["f"], a["o"]])
+    a["xo"] = over_x(a["o"])
     c["o"] = swap_groups(a["o"])
+    b["o"] = near(b["f"])
+    turn, c_first = times_c(turn, 0)
+
+    turn, (a["xo"], c["o"], b["o"], a["xn"], b["x"]) = after(
+        turn, [a["xo"], c["o"], b["o"], a["xn"], b["x"]]
+    )
+    b["xf"] = over_x(b["f"])
     c["xn"] = swap_groups(a["xn"])
-    turn, c_first = times_c(turn, 0)
-
-    turn, (b["f"], a["xf"], c["o"], a["xo"]) = after(turn, [b["f"], a["xf"], c["o"], a["xo"]], inside)
-    b_out = outward(b["f"])
-    b["xf"] = over_x(b["f"])
-    c["xo"] = swap_groups(a["xo"])
+    b["xn"] = near(b["x"])
     turn, score_first = times_b(turn, 0, True, spans, (a_first, c_first))
 
-    split = c["f"].shape[0] // 2
-    turn, (b["o"], b["xf"], c["xn"], b_over, a["xf"], c["f"]) = after(
-        turn, [b_out, b["xf"], c["xn"], b["x"], a["xf"], c["f"]], inside, b_in
+    split = c["o"].shape[0] // 2
+    turn, (b["xf"], c["xn"], b["xn"], a["xf"], a["xo"], c["o"]) = after(
+        turn, [b["xf"], c["xn"], b["xn"], a["xf"], a["xo"], c["o"]]
     )
     b["xo"] = over_x(b["o"])
-    b["xn"] = near(b_over)
-    c["top"] = over_x(c["f"][:split])
-    c["low"] = swap_groups(a["xf"][split:])
+    c["xf"] = swap_groups(a["xf"])
+    c["top"] = over_x(c["o"][:split])
+    c["low"] = swap_groups(a["xo"][split:])
     turn, a_second = times_a(turn, 1)
 
-    turn, (b["xo"], c["xo"], b["xn"]) = after(turn, [b["xo"], c["xo"], b["xn"]], inside)
+    turn, (b["xo"], c["xf"]) = after(turn, [b["xo"], c["xf"]])
     turn, b_second = times_b(turn, 1)
-    groups = (groups[0], ("xo", "o", "xn", "top", "low"))
+    groups = (groups[0], ("xn", "xf", "o", "top", "low"))
     turn, score_second = times_c(turn, 1, False, spans, (a_second, b_second))
     sums = [score_first, score_second]
 
     slots = bucket_ids.shape[0]
     ours = jnp.concatenate([x[:slots] for x in sums], axis=1)
     others = send(jnp.concatenate([x[slots:] for x in sums], axis=1), CORE)
-    codes = (0, COLUMN, NEAR, ACROSS, OPPOSITE | COLUMN, OPPOSITE, NEAR | COLUMN, ACROSS | COLUMN)
+    codes = (0, COLUMN, NEAR, ACROSS, NEAR | COLUMN, ACROSS | COLUMN, OPPOSITE, OPPOSITE | COLUMN)
     codes = jnp.array(codes, jnp.int32)
     owner = jnp.concatenate([me ^ codes, me ^ CORE ^ codes])
     query = owner[:, None] * local + jnp.arange(local, dtype=jnp.int32)[None, :]

time: 222 us -> 236 us (1.063)
  waiting for transfers between devices: 77.1 us -> 99.9 us
  Pallas kernels: 96 us -> 90.8 us
  starting transfers between devices: 32.9 us -> 29 us
    ppermute x16 -> x18, waiting for transfers between devices: 44.7 us -> 69.4 us  [flip(): return lax.ppermute(array, 'dp', [(i, i ^ code) for i in range(count)])]
    ppermute x6 -> x2, waiting for transfers between devices: 17.4 us -> 3.13 us  [lines(): return lax.ppermute(piece, 'dp', pairs)]
    ppermute x7, waiting for transfers between devices: 15 us -> 27.3 us  [swap_groups(): return lax.ppermute(array, 'groups', [(0, 1), (1, 0)])]
    ppermute x6 -> x2, starting transfers between devices: 16.5 us -> 5.03 us  [lines(): return lax.ppermute(piece, 'dp', pairs)]
    ppermute x16 -> x18, starting transfers between devices: 9.86 us -> 19.1 us  [flip(): return lax.ppermute(array, 'dp', [(i, i ^ code) for i in range(count)])]
    pallas_call x10 -> x9, Pallas kernels: 17.6 us -> 12.4 us  [after(): pl.pallas_call(functools.partial(after_kernel, count, merge is not None),...]
  transfers between devices with their start and end apart: 29 -> 27, of which waited for: 19 -> 19; matrix products, arithmetic and copies ran while one was open for 4% -> 4% of each run, Pallas kernels for 35% -> 32%
where the time goes in v10:
time: 236 us; the launch traced here: 233 us
  waiting for transfers between devices  99.9 us (42%)
  Pallas kernels  90.8 us (38%)
  starting transfers between devices  29 us (12%)
  local copies, waits for them, and re-layouts  11.1 us (5%)
    pallas_call x6, Pallas kernels, proj(): pl.pallas_call(functools.partial(proj_kernel, len(pieces), last), out_sha...  70.7 us
    ppermute x18, waiting for transfers between devices, flip(): return lax.ppermute(array, 'dp', [(i, i ^ code) for i in range(count)])  69.4 us
    ppermute x7, waiting for transfers between devices, swap_groups(): return lax.ppermute(array, 'groups', [(0, 1), (1, 0)])  27.3 us
    ppermute x18, starting transfers between devices, flip(): return lax.ppermute(array, 'dp', [(i, i ^ code) for i in range(count)])  19.1 us
    pallas_call x9, Pallas kernels, after(): pl.pallas_call(functools.partial(after_kernel, count, merge is not None),...  12.4 us
    pallas_call x2, Pallas kernels, prepare(): pl.pallas_call(prepare_kernel, out_shape=[jax.ShapeDtypeStruct(x.shape, x...  7.64 us
    ppermute x2, starting transfers between devices, lines(): return lax.ppermute(piece, 'dp', pairs)  5.03 us
    ppermute x7, starting transfers between devices, swap_groups(): return lax.ppermute(array, 'groups', [(0, 1), (1, 0)])  4.82 us
  transfers between devices with their start and end apart: 27, of which 19 were waited for; matrix products, arithmetic and copies ran while one was open for 4% of the time, Pallas kernels for 32%

profile of v10, /device:TPU:9, one launch (start us, length us, event | category | flops | bytes accessed | tf_op | source)
XLA Modules:
  0.0 232.8 jit_solution(17635231305935520047)
XLA Ops:
  0.7 2.2 constant_dynamic-slice_fusion.refs_0_
  2.9 6.4 %shard_map.73 = (bf16[64,7168]{1,0:T(8,128)(2,1)}, bf16[64,7168]{1,0:T(8,128)(2,1)}, bf16[64,8192]{1,0:T(8,128)(2,1)}, bf16[64,8192]{1,0:T(8,128)(2,1)}, s32[1]{0:T(128)}) custom-call(s32[1]{0:T(128)} %bitcast.works_ref, s32[1]{0:T(128)} %constant.26.clone.1.turn_ref, s32[1]{0:T(128)S(6)} %sub.16.first_ref, ...), custom_call_target="tpu_custom_call", output_to_operand_aliasing={{0}: (5, {})} | custom-call | flops 1 | bytes 1 | tf_op jit(solution)/shard_map/pallas_call | solution.py:142
  10.8 4.3 %collective-permute-start.3 = (bf16[64,7168]{1,0:T(8,128)(2,1)}, bf16[64,7168]{1,0:T(8,128)(2,1)}, u32[]{:S(2)}, u32[]{:S(2)}) collective-permute-start(bf16[64,7168]{1,0:T(8,128)(2,1)} %get-tuple-element.69.refs_5_), channel_id=1, source_target_pairs={{4,8},{5,9},{6,10},{7,11},{8,4},{9,5},{10,6},{11,7},{20,24},{21,25... | collective-permute-start | bytes 2752520 | tf_op jit(solution)/shard_map/ppermute | solution.py:268
  16.3 10.7 %collective-permute-done.1.refs_1_ = bf16[64,7168]{1,0:T(8,128)(2,1)} collective-permute-done((bf16[64,7168]{1,0:T(8,128)(2,1)}, bf16[64,7168]{1,0:T(8,128)(2,1)}, u32[]{:S(2)}, u32[]{:S(2)}) %collective-permute-start.1) | collective-permute-done | bytes 917536 | tf_op jit(solution)/shard_map/ppermute | solution.py:62
  28.3 3.1 %collective-permute-done.3.refs_3_ = bf16[64,7168]{1,0:T(8,128)(2,1)} collective-permute-done((bf16[64,7168]{1,0:T(8,128)(2,1)}, bf16[64,7168]{1,0:T(8,128)(2,1)}, u32[]{:S(2)}, u32[]{:S(2)}) %collective-permute-start.3) | collective-permute-done | bytes 917536 | tf_op jit(solution)/shard_map/ppermute | solution.py:268
  33.6 1.3 collective-permute-start.7
  36.1 16.8 %collective-permute-done.7.refs_5_ = bf16[64,7168]{1,0:T(8,128)(2,1)} collective-permute-done((bf16[64,7168]{1,0:T(8,128)(2,1)}, bf16[64,7168]{1,0:T(8,128)(2,1)}, u32[]{:S(2)}, u32[]{:S(2)}) %collective-permute-start.7) | collective-permute-done | bytes 917536 | tf_op jit(solution)/shard_map/ppermute | solution.py:66
  52.9 1.5 collective-permute-done.6.refs_4_
  54.4 3.2 %shard_map.77 = (bf16[64,7168]{1,0:T(8,128)(2,1)}, bf16[64,8192]{1,0:T(8,128)(2,1)}, bf16[64,7168]{1,0:T(8,128)(2,1)}, bf16[64,8192]{1,0:T(8,128)(2,1)}, bf16[64,7168]{1,0:T(8,128)(2,1)}, /*index=5*/s32[1]{0:T(128)}) custom-call(s32[1]{0:T(128)} %shard_map.76.turn_ref, ...), custom_call_target="tpu_custom_call", output_to_operand_aliasing={{0}: (4, {}), {1}: (5, {}), {2}: (6, {}), {3}: (7, {}), {4}... | custom-call | flops 1 | bytes 1 | tf_op jit(solution)/shard_map/pallas_call | solution.py:107
  57.6 1.3 collective-permute-start.10
  60.0 1.7 collective-permute-start.14
  61.7 10.8 %shard_map.78 = (f32[1024,256]{1,0:T(8,128)}, s32[1]{0:T(128)}) custom-call(s32[1]{0:T(128)} %get-tuple-element.77.turn_ref, s32[3]{0:T(128)} %concatenate.25.at_ref, bf16[512,14336]{1,0:T(8,128)(2,1)} %own_ref.11, bf16[512,14336]{1,0:T(8,128)(2,1)} %collective-permute-done.refs_0_.other_ref, bf16[64,7168]{1,0:T(8,128)(2,1)} %get-tuple-element.73.refs_0_, ...), custom_call_target="tpu_custom_call" | custom-call | flops 1 | bytes 1 | tf_op jit(solution)/shard_map/pallas_call | solution.py:217
  72.5 5.4 %collective-permute-done.10.refs_2_ = bf16[64,7168]{1,0:T(8,128)(2,1)} collective-permute-done((bf16[64,7168]{1,0:T(8,128)(2,1)}, bf16[64,7168]{1,0:T(8,128)(2,1)}, u32[]{:S(2)}, u32[]{:S(2)}) %collective-permute-start.10) | collective-permute-done | bytes 917536 | tf_op jit(solution)/shard_map/ppermute | solution.py:66
  77.9 3.7 %collective-permute-done.8.refs_0_ = bf16[64,7168]{1,0:T(8,128)(2,1)S(1)} collective-permute-done((bf16[64,7168]{1,0:T(8,128)(2,1)}, bf16[64,7168]{1,0:T(8,128)(2,1)S(1)}, u32[]{:S(2)}, u32[]{:S(2)}) %collective-permute-start.8) | collective-permute-done | bytes 917536 | tf_op jit(solution)/shard_map/ppermute | solution.py:62
  85.5 18.7 %collective-permute-done.11.refs_0_ = bf16[64,7168]{1,0:T(8,128)(2,1)S(1)} collective-permute-done((bf16[64,7168]{1,0:T(8,128)(2,1)}, bf16[64,7168]{1,0:T(8,128)(2,1)S(1)}, u32[]{:S(2)}, u32[]{:S(2)}) %collective-permute-start.11) | collective-permute-done | bytes 917536 | tf_op jit(solution)/shard_map/ppermute | solution.py:62
  105.0 1.9 collective-permute-done.14.refs_3_
  106.9 18.3 %collective-permute-done.13.refs_2_ = bf16[64,8192]{1,0:T(8,128)(2,1)} collective-permute-done((bf16[64,8192]{1,0:T(8,128)(2,1)}, bf16[64,8192]{1,0:T(8,128)(2,1)}, u32[]{:S(2)}, u32[]{:S(2)}) %collective-permute-start.13) | collective-permute-done | bytes 1048608 | tf_op jit(solution)/shard_map/ppermute | solution.py:62
  126.4 2.0 collective-permute-start.17
  130.6 10.9 %shard_map.82 = (f32[1024,256]{1,0:T(8,128)}, s32[1]{0:T(128)}) custom-call(s32[1]{0:T(128)} %get-tuple-element.86.turn_ref, s32[3]{0:T(128)} %concatenate.26.at_ref, bf16[512,14336]{1,0:T(8,128)(2,1)} %own_ref.11, bf16[512,14336]{1,0:T(8,128)(2,1)} %collective-permute-done.refs_0_.other_ref, bf16[64,7168]{1,0:T(8,128)(2,1)} %get-tuple-element.87.refs_0_, ...), custom_call_target="tpu_custom_call" | custom-call | flops 1 | bytes 1 | tf_op jit(solution)/shard_map/pallas_call | solution.py:217
  141.5 8.4 %collective-permute-done.15.refs_0_ = bf16[64,7168]{1,0:T(8,128)(2,1)S(1)} collective-permute-done((bf16[64,7168]{1,0:T(8,128)(2,1)}, bf16[64,7168]{1,0:T(8,128)(2,1)S(1)}, u32[]{:S(2)}, u32[]{:S(2)}) %collective-permute-start.15) | collective-permute-done | bytes 917536 | tf_op jit(solution)/shard_map/ppermute | solution.py:62
  150.1 1.8 collective-permute-done.17.refs_2_
  155.2 2.1 collective-permute-start.18
  159.3 13.9 %shard_map.84 = (f32[8,256]{1,0:T(8,128)}, s32[1]{0:T(128)}) custom-call(s32[1]{0:T(128)} %get-tuple-element.96.turn_ref, s32[3]{0:T(128)} %broadcast_8_at_ref.2.at_ref, bf16[512,8192]{1,0:T(8,128)(2,1)} %own_ref.10, bf16[512,8192]{1,0:T(8,128)(2,1)} %collective-permute-done.4.refs_2_.other_ref, bf16[64,8192]{1,0:T(8,128)(2,1)} %bitcast.22, ...), custom_call_target="tpu_custom_call" | custom-call | flops 1 | bytes 1 | tf_op jit(solution)/shard_map/pallas_call | solution.py:217
  173.1 1.8 collective-permute-done.20.refs_1_
  174.9 1.6 collective-permute-done.21.refs_2_
  178.0 1.8 slice.19
  180.3 1.8 slice.20
  184.2 10.8 %shard_map.86 = (f32[1024,256]{1,0:T(8,128)}, s32[1]{0:T(128)}) custom-call(s32[1]{0:T(128)} %get-tuple-element.107.turn_ref, s32[3]{0:T(128)} %concatenate.25.at_ref, bf16[512,14336]{1,0:T(8,128)(2,1)} %own_ref.11, bf16[512,14336]{1,0:T(8,128)(2,1)} %collective-permute-done.refs_0_.other_ref, bf16[64,7168]{1,0:T(8,128)(2,1)} %get-tuple-element.103.refs_0_, ...), custom_call_target="tpu_custom_call" | custom-call | flops 1 | bytes 1 | tf_op jit(solution)/shard_map/pallas_call | solution.py:217
  195.0 2.5 %collective-permute-done.23.refs_1_ = bf16[64,7168]{1,0:T(8,128)(2,1)S(1)} collective-permute-done((bf16[64,7168]{1,0:T(8,128)(2,1)}, bf16[64,7168]{1,0:T(8,128)(2,1)S(1)}, u32[]{:S(2)}, u32[]{:S(2)}) %collective-permute-start.23) | collective-permute-done | bytes 917536 | tf_op jit(solution)/shard_map/ppermute | solution.py:66
  199.6 11.6 %shard_map.88 = (f32[1024,256]{1,0:T(8,128)}, s32[1]{0:T(128)}) custom-call(s32[1]{0:T(128)} %get-tuple-element.112.turn_ref, s32[3]{0:T(128)} %broadcast_8_at_ref.2.at_ref, bf16[512,8192]{1,0:T(8,128)(2,1)} %own_ref.10, bf16[512,8192]{1,0:T(8,128)(2,1)} %collective-permute-done.4.refs_2_.other_ref, bf16[64,8192]{1,0:T(8,128)(2,1)} %get-tuple-element.113.refs_0_, ...), custom_call_target="tpu_custom_call" | custom-call | flops 1 | bytes 1 | tf_op jit(solution)/shard_map/pallas_call | solution.py:217
  211.2 12.9 %shard_map.89 = (f32[8,256]{1,0:T(8,128)}, s32[1]{0:T(128)}) custom-call(s32[1]{0:T(128)} %get-tuple-element.116.turn_ref, s32[3]{0:T(128)} %concatenate.26.at_ref, bf16[512,14336]{1,0:T(8,128)(2,1)} %own_ref.11, bf16[512,14336]{1,0:T(8,128)(2,1)} %collective-permute-done.refs_0_.other_ref, bf16[64,7168]{1,0:T(8,128)(2,1)} %get-tuple-element.117.refs_0_, ...), custom_call_target="tpu_custom_call" | custom-call | flops 1 | bytes 1 | tf_op jit(solution)/shard_map/pallas_call | solution.py:217
  224.9 6.3 %collective-permute-start.26 = (f32[4,512]{1,0:T(4,128)S(1)}, f32[4,512]{1,0:T(4,128)S(1)}, u32[]{:S(2)}, u32[]{:S(2)}) collective-permute-start(f32[4,512]{1,0:T(4,128)S(1)} %pad_maximum_fusion), channel_id=1, source_target_pairs={{0,1},{1,0},{2,3},{3,2},{4,5},{5,4},{6,7},{7,6},{8,9},{9,8},{10,11... | collective-permute-start | bytes 24584 | tf_op jit(solution)/shard_map/ppermute | solution.py:62
  (80 shorter events, 30.9 us)
Async XLA Ops:
  0.0 31.4 %collective-permute-start = (bf16[512,14336]{1,0:T(8,128)(2,1)}, bf16[512,14336]{1,0:T(8,128)(2,1)}, u32[]{:S(2)}, u32[]{:S(2)}) collective-permute-start(bf16[512,14336]{1,0:T(8,128)(2,1)} %own_ref.11), channel_id=1, source_target_pairs={{0,1},{1,0},{2,3},{3,2},{4,5},{5,4},{6,7},{7,6},{8,9},{9,8},{10,11... | collective-permute-start | bytes 44040200 | tf_op jit(solution)/shard_map/ppermute | solution.py:62
  0.7 35.4 %collective-permute-start.4 = (bf16[512,8192]{1,0:T(8,128)(2,1)}, bf16[512,8192]{1,0:T(8,128)(2,1)}, u32[]{:S(2)}, u32[]{:S(2)}) collective-permute-start(bf16[512,8192]{1,0:T(8,128)(2,1)} %own_ref.10), channel_id=1, source_target_pairs={{0,1},{1,0},{2,3},{3,2},{4,5},{5,4},{6,7},{7,6},{8,9},{9,8},{10,11... | collective-permute-start | bytes 25165832 | tf_op jit(solution)/shard_map/ppermute | solution.py:62
  9.3 17.7 %collective-permute-start.1 = (bf16[64,7168]{1,0:T(8,128)(2,1)}, bf16[64,7168]{1,0:T(8,128)(2,1)}, u32[]{:S(2)}, u32[]{:S(2)}) collective-permute-start(bf16[64,7168]{1,0:T(8,128)(2,1)} %get-tuple-element.69.refs_5_), channel_id=1, source_target_pairs={{0,2},{1,3},{2,0},{3,1},{4,6},{5,7},{6,4},{7,5},{8,10},{9,11},{10,... | collective-permute-start | bytes 2752520 | tf_op jit(solution)/shard_map/ppermute | solution.py:62
  10.6 17.7 %collective-permute-start.2 = (bf16[64,7168]{1,0:T(8,128)(2,1)}, bf16[64,7168]{1,0:T(8,128)(2,1)S(1)}, u32[]{:S(2)}, u32[]{:S(2)}) collective-permute-start(bf16[64,7168]{1,0:T(8,128)(2,1)} %get-tuple-element.69.refs_5_), channel_id=1, source_target_pairs={{0,4},{1,5},{2,6},{3,7},{4,0},{5,1},{6,2},{7,3},{8,12},{9,13},{10,... | collective-permute-start | bytes 2752520 | tf_op jit(solution)/shard_map/ppermute | solution.py:62
  10.8 20.6 %collective-permute-start.3 = (bf16[64,7168]{1,0:T(8,128)(2,1)}, bf16[64,7168]{1,0:T(8,128)(2,1)}, u32[]{:S(2)}, u32[]{:S(2)}) collective-permute-start(bf16[64,7168]{1,0:T(8,128)(2,1)} %get-tuple-element.69.refs_5_), channel_id=1, source_target_pairs={{4,8},{5,9},{6,10},{7,11},{8,4},{9,5},{10,6},{11,7},{20,24},{21,25... | collective-permute-start | bytes 2752520 | tf_op jit(solution)/shard_map/ppermute | solution.py:268
  32.6 21.7 %collective-permute-start.6 = (bf16[64,8192]{1,0:T(8,128)(2,1)}, bf16[64,8192]{1,0:T(8,128)(2,1)}, u32[]{:S(2)}, u32[]{:S(2)}) collective-permute-start(bf16[64,8192]{1,0:T(8,128)(2,1)} %get-tuple-element.74.refs_6_), channel_id=1, source_target_pairs={{0,2},{1,3},{2,0},{3,1},{4,6},{5,7},{6,4},{7,5},{8,10},{9,11},{10,... | collective-permute-start | bytes 3145736 | tf_op jit(solution)/shard_map/ppermute | solution.py:62
  32.9 3.1 %collective-permute-start.5 = (bf16[64,7168]{1,0:T(8,128)(2,1)}, bf16[64,7168]{1,0:T(8,128)(2,1)S(1)}, u32[]{:S(2)}, u32[]{:S(2)}) collective-permute-start(bf16[64,7168]{1,0:T(8,128)(2,1)} %get-tuple-element.73.refs_0_), channel_id=1, source_target_pairs={{0,12},{1,13},{2,14},{3,15},{12,0},{13,1},{14,2},{15,3},{16,28},{1... | collective-permute-start | bytes 2752520 | tf_op jit(solution)/shard_map/ppermute | solution.py:268
  33.6 19.2 %collective-permute-start.7 = (bf16[64,7168]{1,0:T(8,128)(2,1)}, bf16[64,7168]{1,0:T(8,128)(2,1)}, u32[]{:S(2)}, u32[]{:S(2)}) collective-permute-start(bf16[64,7168]{1,0:T(8,128)(2,1)} %get-tuple-element.75.refs_1_), channel_id=1, source_target_pairs={{0,16},{16,0},{1,17},{17,1},{2,18},{18,2},{3,19},{19,3},{4,20},{20... | collective-permute-start | bytes 2752520 | tf_op jit(solution)/shard_map/ppermute | solution.py:66
  36.1 18.3 %copy-start.4 = (bf16[64,7168]{1,0:T(8,128)(2,1)}, bf16[64,7168]{1,0:T(8,128)(2,1)S(1)}, u32[]{:S(2)}) copy-start(bf16[64,7168]{1,0:T(8,128)(2,1)S(1)} %collective-permute-done.5.refs_3_) | copy-start | bytes 2752516
  57.6 20.3 %collective-permute-start.10 = (bf16[64,7168]{1,0:T(8,128)(2,1)}, bf16[64,7168]{1,0:T(8,128)(2,1)}, u32[]{:S(2)}, u32[]{:S(2)}) collective-permute-start(bf16[64,7168]{1,0:T(8,128)(2,1)} %get-tuple-element.78.refs_2_), channel_id=1, source_target_pairs={{0,16},{16,0},{1,17},{17,1},{2,18},{18,2},{3,19},{19,3},{4,20},{20... | collective-permute-start | bytes 2752520 | tf_op jit(solution)/shard_map/ppermute | solution.py:66
  58.9 22.8 %collective-permute-start.8 = (bf16[64,7168]{1,0:T(8,128)(2,1)}, bf16[64,7168]{1,0:T(8,128)(2,1)S(1)}, u32[]{:S(2)}, u32[]{:S(2)}) collective-permute-start(bf16[64,7168]{1,0:T(8,128)(2,1)} %get-tuple-element.79.refs_3_), channel_id=1, source_target_pairs={{0,4},{1,5},{2,6},{3,7},{4,0},{5,1},{6,2},{7,3},{8,12},{9,13},{10,... | collective-permute-start | bytes 2752520 | tf_op jit(solution)/shard_map/ppermute | solution.py:62
  58.9 22.8 %collective-permute-start.9 = (bf16[64,7168]{1,0:T(8,128)(2,1)}, bf16[64,7168]{1,0:T(8,128)(2,1)}, u32[]{:S(2)}, u32[]{:S(2)}) collective-permute-start(bf16[64,7168]{1,0:T(8,128)(2,1)} %get-tuple-element.78.refs_2_), channel_id=1, source_target_pairs={{0,2},{1,3},{2,0},{3,1},{4,6},{5,7},{6,4},{7,5},{8,10},{9,11},{10,... | collective-permute-start | bytes 2752520 | tf_op jit(solution)/shard_map/ppermute | solution.py:62
  60.0 46.9 %collective-permute-start.14 = (bf16[64,8192]{1,0:T(8,128)(2,1)}, bf16[64,8192]{1,0:T(8,128)(2,1)}, u32[]{:S(2)}, u32[]{:S(2)}) collective-permute-start(bf16[64,8192]{1,0:T(8,128)(2,1)} %get-tuple-element.84), channel_id=1, source_target_pairs={{0,12},{1,13},{2,14},{3,15},{4,8},{5,9},{6,10},{7,11},{8,4},{9,5},... | collective-permute-start | bytes 3145736 | tf_op jit(solution)/shard_map/ppermute | solution.py:62
  83.7 41.5 %collective-permute-start.13 = (bf16[64,8192]{1,0:T(8,128)(2,1)}, bf16[64,8192]{1,0:T(8,128)(2,1)}, u32[]{:S(2)}, u32[]{:S(2)}) collective-permute-start(bf16[64,8192]{1,0:T(8,128)(2,1)} %get-tuple-element.83), channel_id=1, source_target_pairs={{0,4},{1,5},{2,6},{3,7},{4,0},{5,1},{6,2},{7,3},{8,12},{9,13},{10,... | collective-permute-start | bytes 3145736 | tf_op jit(solution)/shard_map/ppermute | solution.py:62
  83.8 20.5 %collective-permute-start.11 = (bf16[64,7168]{1,0:T(8,128)(2,1)}, bf16[64,7168]{1,0:T(8,128)(2,1)S(1)}, u32[]{:S(2)}, u32[]{:S(2)}) collective-permute-start(bf16[64,7168]{1,0:T(8,128)(2,1)} %get-tuple-element.79.refs_3_), channel_id=1, source_target_pairs={{0,2},{1,3},{2,0},{3,1},{4,6},{5,7},{6,4},{7,5},{8,10},{9,11},{10,... | collective-permute-start | bytes 2752520 | tf_op jit(solution)/shard_map/ppermute | solution.py:62
  84.1 20.9 %collective-permute-start.12 = (bf16[64,7168]{1,0:T(8,128)(2,1)}, bf16[64,7168]{1,0:T(8,128)(2,1)}, u32[]{:S(2)}, u32[]{:S(2)}) collective-permute-start(bf16[64,7168]{1,0:T(8,128)(2,1)} %get-tuple-element.79.refs_3_), channel_id=1, source_target_pairs={{0,16},{16,0},{1,17},{17,1},{2,18},{18,2},{3,19},{19,3},{4,20},{20... | collective-permute-start | bytes 2752520 | tf_op jit(solution)/shard_map/ppermute | solution.py:66
  104.2 21.0 %copy-start.3 = (bf16[64,7168]{1,0:T(8,128)(2,1)}, bf16[64,7168]{1,0:T(8,128)(2,1)S(1)}, u32[]{:S(2)}) copy-start(bf16[64,7168]{1,0:T(8,128)(2,1)S(1)} %collective-permute-done.11.refs_0_) | copy-start | bytes 2752516
  126.4 25.5 %collective-permute-start.17 = (bf16[64,8192]{1,0:T(8,128)(2,1)}, bf16[64,8192]{1,0:T(8,128)(2,1)}, u32[]{:S(2)}, u32[]{:S(2)}) collective-permute-start(bf16[64,8192]{1,0:T(8,128)(2,1)} %get-tuple-element.93.refs_3_), channel_id=1, source_target_pairs={{0,4},{1,5},{2,6},{3,7},{4,0},{5,1},{6,2},{7,3},{8,12},{9,13},{10,... | collective-permute-start | bytes 3145736 | tf_op jit(solution)/shard_map/ppermute | solution.py:62
  128.4 21.5 %collective-permute-start.15 = (bf16[64,7168]{1,0:T(8,128)(2,1)}, bf16[64,7168]{1,0:T(8,128)(2,1)S(1)}, u32[]{:S(2)}, u32[]{:S(2)}) collective-permute-start(bf16[64,7168]{1,0:T(8,128)(2,1)} %get-tuple-element.92.refs_2_), channel_id=1, source_target_pairs={{0,2},{1,3},{2,0},{3,1},{4,6},{5,7},{6,4},{7,5},{8,10},{9,11},{10,... | collective-permute-start | bytes 2752520 | tf_op jit(solution)/shard_map/ppermute | solution.py:62
  128.8 21.2 %collective-permute-start.16 = (bf16[64,7168]{1,0:T(8,128)(2,1)}, bf16[64,7168]{1,0:T(8,128)(2,1)}, u32[]{:S(2)}, u32[]{:S(2)}) collective-permute-start(bf16[64,7168]{1,0:T(8,128)(2,1)} %get-tuple-element.92.refs_2_), channel_id=1, source_target_pairs={{0,16},{16,0},{1,17},{17,1},{2,18},{18,2},{3,19},{19,3},{4,20},{20... | collective-permute-start | bytes 2752520 | tf_op jit(solution)/shard_map/ppermute | solution.py:66
  129.6 43.5 %collective-permute-start.19 = (bf16[64,8192]{1,0:T(8,128)(2,1)}, bf16[64,8192]{1,0:T(8,128)(2,1)}, u32[]{:S(2)}, u32[]{:S(2)}) collective-permute-start(bf16[64,8192]{1,0:T(8,128)(2,1)} %get-tuple-element.93.refs_3_), channel_id=1, source_target_pairs={{0,2},{1,3},{2,0},{3,1},{4,6},{5,7},{6,4},{7,5},{8,10},{9,11},{10,... | collective-permute-start | bytes 3145736 | tf_op jit(solution)/shard_map/ppermute | solution.py:62
  130.6 23.9 %copy-start.7 = (s32[4]{0:T(128)S(1)}, s32[4]{0:T(128)}, u32[]{:S(2)}) copy-start(s32[4]{0:T(128)} %param.11) | copy-start | bytes 52
  130.6 24.1 %copy-start.8 = (s32[4]{0:T(128)S(1)}, s32[4]{0:T(128)}, u32[]{:S(2)}) copy-start(s32[4]{0:T(128)} %param.12) | copy-start | bytes 52
  153.1 23.5 %collective-permute-start.21 = (bf16[64,8192]{1,0:T(8,128)(2,1)}, bf16[64,8192]{1,0:T(8,128)(2,1)}, u32[]{:S(2)}, u32[]{:S(2)}) collective-permute-start(bf16[64,8192]{1,0:T(8,128)(2,1)} %get-tuple-element.97.refs_1_), channel_id=1, source_target_pairs={{0,4},{1,5},{2,6},{3,7},{4,0},{5,1},{6,2},{7,3},{8,12},{9,13},{10,... | collective-permute-start | bytes 3145736 | tf_op jit(solution)/shard_map/ppermute | solution.py:62
  154.3 20.7 %collective-permute-start.20 = (bf16[64,7168]{1,0:T(8,128)(2,1)}, bf16[64,7168]{1,0:T(8,128)(2,1)S(1)}, u32[]{:S(2)}, u32[]{:S(2)}) collective-permute-start(bf16[64,7168]{1,0:T(8,128)(2,1)} %get-tuple-element.103.refs_0_), channel_id=1, source_target_pairs={{0,16},{16,0},{1,17},{17,1},{2,18},{18,2},{3,19},{19,3},{4,20},{20... | collective-permute-start | bytes 2752520 | tf_op jit(solution)/shard_map/ppermute | solution.py:66
  154.7 40.3 %collective-permute-start.22 = (bf16[64,8192]{1,0:T(8,128)(2,1)}, bf16[64,8192]{1,0:T(8,128)(2,1)}, u32[]{:S(2)}, u32[]{:S(2)}) collective-permute-start(bf16[64,8192]{1,0:T(8,128)(2,1)} %get-tuple-element.111.refs_2_), channel_id=1, source_target_pairs={{0,2},{1,3},{2,0},{3,1},{4,6},{5,7},{6,4},{7,5},{8,10},{9,11},{10,... | collective-permute-start | bytes 3145736 | tf_op jit(solution)/shard_map/ppermute | solution.py:62
  155.2 2.9 %collective-permute-start.18 = (s32[2,4]{1,0:T(2,128)S(1)}, s32[2,4]{1,0:T(2,128)S(1)}, u32[]{:S(2)}, u32[]{:S(2)}) collective-permute-start(s32[2,4]{1,0:T(2,128)S(1)} %pad_add_fusion), channel_id=1, source_target_pairs={{0,1},{1,0},{2,3},{3,2},{4,5},{5,4},{6,7},{7,6},{8,9},{9,8},{10,11... | collective-permute-start | bytes 104 | tf_op jit(solution)/shard_map/ppermute | solution.py:62
  159.3 24.1 %copy-start.9 = (s32[8]{0:T(128)S(1)}, s32[8]{0:T(128)}, u32[]{:S(2)}) copy-start(s32[8]{0:T(128)} %constant.58.clone) | copy-start | bytes 100
  177.7 19.8 %collective-permute-start.23 = (bf16[64,7168]{1,0:T(8,128)(2,1)}, bf16[64,7168]{1,0:T(8,128)(2,1)S(1)}, u32[]{:S(2)}, u32[]{:S(2)}) collective-permute-start(bf16[64,7168]{1,0:T(8,128)(2,1)} %get-tuple-element.108.refs_1_), channel_id=1, source_target_pairs={{0,16},{16,0},{1,17},{17,1},{2,18},{18,2},{3,19},{19,3},{4,20},{20... | collective-permute-start | bytes 2752520 | tf_op jit(solution)/shard_map/ppermute | solution.py:66
  179.8 31.4 %collective-permute-start.24 = (bf16[32,7168]{1,0:T(8,128)(2,1)}, bf16[32,7168]{1,0:T(8,128)(2,1)}, u32[]{:S(2)}, u32[]{:S(2)}) collective-permute-start(bf16[32,7168]{1,0:T(8,128)(2,1)} %slice.19), channel_id=1, source_target_pairs={{0,2},{1,3},{2,0},{3,1},{4,6},{5,7},{6,4},{7,5},{8,10},{9,11},{10,... | collective-permute-start | bytes 1376264 | tf_op jit(solution)/shard_map/ppermute | solution.py:62
  182.1 29.1 %collective-permute-start.25 = (bf16[32,7168]{1,0:T(8,128)(2,1)}, bf16[32,7168]{1,0:T(8,128)(2,1)}, u32[]{:S(2)}, u32[]{:S(2)}) collective-permute-start(bf16[32,7168]{1,0:T(8,128)(2,1)} %slice.20), channel_id=1, source_target_pairs={{0,16},{16,0},{1,17},{17,1},{2,18},{18,2},{3,19},{19,3},{4,20},{20... | collective-permute-start | bytes 1376264 | tf_op jit(solution)/shard_map/ppermute | solution.py:66
  224.9 7.1 %collective-permute-start.26 = (f32[4,512]{1,0:T(4,128)S(1)}, f32[4,512]{1,0:T(4,128)S(1)}, u32[]{:S(2)}, u32[]{:S(2)}) collective-permute-start(f32[4,512]{1,0:T(4,128)S(1)} %pad_maximum_fusion), channel_id=1, source_target_pairs={{0,1},{1,0},{2,3},{3,2},{4,5},{5,4},{6,7},{7,6},{8,9},{9,8},{10,11... | collective-permute-start | bytes 24584 | tf_op jit(solution)/shard_map/ppermute | solution.py:62
  (5 other events, 8.6 us)

commit v11 on v10

--- a/solution.py
+++ b/solution.py
@@ -267,8 +267,11 @@
         pairs = [(i * 4 + rest, j * 4 + rest) for i, j in pairs for rest in range(4)]
         return lax.ppermute(piece, "dp", pairs)
 
-    def across(piece):
-        return send(piece, ACROSS)
+    def middle(piece):
+        return lines(piece, [(1, 2), (2, 1)])
+
+    def ends(piece):
+        return lines(piece, [(0, 3), (3, 0)])
 
     def over_x(piece):
         return send(piece, COLUMN)
@@ -302,14 +305,13 @@
     turn, made, (a["own"],) = prepare(zero, core, *copies, None, [a["own"]])
     a["x"] = over_x(a["own"])
     a["n"] = near(a["own"])
-    a_mid = lines(a["own"], [(1, 2), (2, 1)])
+    a_mid = middle(a["own"])
     turn, (c["own"], b_one, b_two), _ = prepare(turn, 1 - core, *copies, made, [])
 
-    turn, (a["x"], a["n"], a_mid, b_one, ends) = after(
+    turn, (a["x"], a["n"], a_mid, b_one, a["own"]) = after(
         turn, [a["x"], a["n"], a_mid, b_one, a["own"]], [acts_there]
     )
-    a_end = lines(ends, [(0, 3), (3, 0)])
-    a["own"] = ends
+    a_end = ends(a["own"])
     b["x"] = over_x(b_one)
     c["x"] = swap_groups(a["x"])
     turn = pause(turn)
@@ -320,40 +322,43 @@
     a["o"] = near(a["f"])
     a["xn"] = over_x(a["n"])
     c["n"] = swap_groups(a["n"])
-    b["f"] = across(b_one)
+    b_mid = middle(b_one)
     turn, a_first = times_a(turn, 0)
 
-    turn, (a["o"], a["xn"], c["n"], b_two) = after(turn, [a["o"], a["xn"], c["n"], b_two])
+    turn, (a["o"], a["xn"], c["n"], b_mid, b_two) = after(turn, [a["o"], a["xn"], c["n"], b_mid, b_two])
     a["xf"] = over_x(a["f"])
     c["f"] = swap_groups(a["f"])
-    b["n"] = near(b_two)
+    b_end = ends(b_two)
     turn = pause(turn)
 
-    turn, (a["xf"], c["f"], b["n"], b["f"], a["o"]) = after(turn, [a["xf"], c["f"], b["n"], b["f"], a["o"]])
+    turn, (b["f"], a["xf"], c["f"], a["o"], b_two) = after(
+        turn, [b_end, a["xf"], c["f"], a["o"], b_two], (), (inside, b_mid)
+    )
     a["xo"] = over_x(a["o"])
     c["o"] = swap_groups(a["o"])
     b["o"] = near(b["f"])
     turn, c_first = times_c(turn, 0)
 
-    turn, (a["xo"], c["o"], b["o"], a["xn"], b["x"]) = after(
-        turn, [a["xo"], c["o"], b["o"], a["xn"], b["x"]]
+    turn, (a["xo"], c["o"], b["o"], a["xn"], b_two) = after(
+        turn, [a["xo"], c["o"], b["o"], a["xn"], b_two]
     )
     b["xf"] = over_x(b["f"])
     c["xn"] = swap_groups(a["xn"])
-    b["xn"] = near(b["x"])
-    turn, score_first = times_b(turn, 0, True, spans, (a_first, c_first))
+    b["n"] = near(b_two)
+    turn, a_second = times_a(turn, 1)
 
     split = c["o"].shape[0] // 2
-    turn, (b["xf"], c["xn"], b["xn"], a["xf"], a["xo"], c["o"]) = after(
-        turn, [b["xf"], c["xn"], b["xn"], a["xf"], a["xo"], c["o"]]
+    turn, (b["xf"], c["xn"], b["n"], a["xf"], a["xo"], c["o"], b["x"]) = after(
+        turn, [b["xf"], c["xn"], b["n"], a["xf"], a["xo"], c["o"], b["x"]]
     )
     b["xo"] = over_x(b["o"])
     c["xf"] = swap_groups(a["xf"])
+    b["xn"] = near(b["x"])
     c["top"] = over_x(c["o"][:split])
     c["low"] = swap_groups(a["xo"][split:])
-    turn, a_second = times_a(turn, 1)
-
-    turn, (b["xo"], c["xf"]) = after(turn, [b["xo"], c["xf"]])
+    turn, score_first = times_b(turn, 0, True, spans, (a_first, c_first))
+
+    turn, (b["xo"], c["xf"], b["xn"]) = after(turn, [b["xo"], c["xf"], b["xn"]])
     turn, b_second = times_b(turn, 1)
     groups = (groups[0], ("xn", "xf", "o", "top", "low"))
     turn, score_second = times_c(turn, 1, False, spans, (a_second, b_second))

time: 236 us -> 225 us (0.953)
  waiting for transfers between devices: 99.9 us -> 85.4 us
  starting transfers between devices: 29 us -> 31.6 us
    ppermute x18 -> x17, waiting for transfers between devices: 69.4 us -> 54.7 us  [flip(): return lax.ppermute(array, 'dp', [(i, i ^ code) for i in range(count)])]
    ppermute x2 -> x4, starting transfers between devices: 5.03 us -> 10.6 us  [lines(): return lax.ppermute(piece, 'dp', pairs)]
    ppermute x18 -> x17, starting transfers between devices: 19.1 us -> 16.2 us  [flip(): return lax.ppermute(array, 'dp', [(i, i ^ code) for i in range(count)])]
  transfers between devices with their start and end apart: 27 -> 28, of which waited for: 19 -> 16; matrix products, arithmetic and copies ran while one was open for 4% -> 4% of each run, Pallas kernels for 32% -> 33%
where the time goes in v11:
time: 225 us; the launch traced here: 223 us
  Pallas kernels  92.9 us (41%)
  waiting for transfers between devices  85.4 us (38%)
  starting transfers between devices  31.6 us (14%)
  local copies, waits for them, and re-layouts  10.8 us (5%)
    pallas_call x6, Pallas kernels, proj(): pl.pallas_call(functools.partial(proj_kernel, len(pieces), last), out_sha...  70.7 us
    ppermute x17, waiting for transfers between devices, flip(): return lax.ppermute(array, 'dp', [(i, i ^ code) for i in range(count)])  54.7 us
    ppermute x7, waiting for transfers between devices, swap_groups(): return lax.ppermute(array, 'groups', [(0, 1), (1, 0)])  27.6 us
    ppermute x17, starting transfers between devices, flip(): return lax.ppermute(array, 'dp', [(i, i ^ code) for i in range(count)])  16.2 us
    pallas_call x9, Pallas kernels, after(): pl.pallas_call(functools.partial(after_kernel, count, merge is not None),...  14.5 us
    ppermute x4, starting transfers between devices, lines(): return lax.ppermute(piece, 'dp', pairs)  10.6 us
    pallas_call x2, Pallas kernels, prepare(): pl.pallas_call(prepare_kernel, out_shape=[jax.ShapeDtypeStruct(x.shape, x...  7.68 us
    ppermute x7, starting transfers between devices, swap_groups(): return lax.ppermute(array, 'groups', [(0, 1), (1, 0)])  4.75 us
  transfers between devices with their start and end apart: 28, of which 16 were waited for; matrix products, arithmetic and copies ran while one was open for 4% of the time, Pallas kernels for 33%

profile of v11, /device:TPU:9, one launch (start us, length us, event | category | flops | bytes accessed | tf_op | source)
XLA Modules:
  0.0 222.8 jit_solution(1586914448319028782)
XLA Ops:
  0.7 2.2 constant_dynamic-slice_fusion.refs_0_
  2.9 6.4 %shard_map.73 = (bf16[64,7168]{1,0:T(8,128)(2,1)}, bf16[64,7168]{1,0:T(8,128)(2,1)}, bf16[64,8192]{1,0:T(8,128)(2,1)}, bf16[64,8192]{1,0:T(8,128)(2,1)}, s32[1]{0:T(128)}) custom-call(s32[1]{0:T(128)} %bitcast.works_ref, s32[1]{0:T(128)} %constant.26.clone.1.turn_ref, s32[1]{0:T(128)S(6)} %sub.16.first_ref, ...), custom_call_target="tpu_custom_call", output_to_operand_aliasing={{0}: (5, {})} | custom-call | flops 1 | bytes 1 | tf_op jit(solution)/shard_map/pallas_call | solution.py:142
  10.7 4.3 %collective-permute-start.3 = (bf16[64,7168]{1,0:T(8,128)(2,1)}, bf16[64,7168]{1,0:T(8,128)(2,1)}, u32[]{:S(2)}, u32[]{:S(2)}) collective-permute-start(bf16[64,7168]{1,0:T(8,128)(2,1)} %get-tuple-element.72.refs_5_), channel_id=1, source_target_pairs={{4,8},{5,9},{6,10},{7,11},{8,4},{9,5},{10,6},{11,7},{20,24},{21,25... | collective-permute-start | bytes 2752520 | tf_op jit(solution)/shard_map/ppermute | solution.py:268
  16.3 10.7 %collective-permute-done.1.refs_1_ = bf16[64,7168]{1,0:T(8,128)(2,1)} collective-permute-done((bf16[64,7168]{1,0:T(8,128)(2,1)}, bf16[64,7168]{1,0:T(8,128)(2,1)}, u32[]{:S(2)}, u32[]{:S(2)}) %collective-permute-start.1) | collective-permute-done | bytes 917536 | tf_op jit(solution)/shard_map/ppermute | solution.py:62
  28.3 3.1 %collective-permute-done.3.refs_3_ = bf16[64,7168]{1,0:T(8,128)(2,1)} collective-permute-done((bf16[64,7168]{1,0:T(8,128)(2,1)}, bf16[64,7168]{1,0:T(8,128)(2,1)}, u32[]{:S(2)}, u32[]{:S(2)}) %collective-permute-start.3) | collective-permute-done | bytes 917536 | tf_op jit(solution)/shard_map/ppermute | solution.py:268
  33.6 1.3 collective-permute-start.7
  36.1 16.7 %collective-permute-done.7.refs_5_ = bf16[64,7168]{1,0:T(8,128)(2,1)} collective-permute-done((bf16[64,7168]{1,0:T(8,128)(2,1)}, bf16[64,7168]{1,0:T(8,128)(2,1)}, u32[]{:S(2)}, u32[]{:S(2)}) %collective-permute-start.7) | collective-permute-done | bytes 917536 | tf_op jit(solution)/shard_map/ppermute | solution.py:66
  52.9 1.5 collective-permute-done.6.refs_4_
  54.4 3.2 %shard_map.77 = (bf16[64,7168]{1,0:T(8,128)(2,1)}, bf16[64,8192]{1,0:T(8,128)(2,1)}, bf16[64,7168]{1,0:T(8,128)(2,1)}, bf16[64,8192]{1,0:T(8,128)(2,1)}, bf16[64,7168]{1,0:T(8,128)(2,1)}, /*index=5*/s32[1]{0:T(128)}) custom-call(s32[1]{0:T(128)} %shard_map.76.turn_ref, ...), custom_call_target="tpu_custom_call", output_to_operand_aliasing={{0}: (4, {}), {1}: (5, {}), {2}: (6, {}), {3}: (7, {}), {4}... | custom-call | flops 1 | bytes 1 | tf_op jit(solution)/shard_map/pallas_call | solution.py:107
  57.6 3.9 %collective-permute-start.11 = (bf16[64,8192]{1,0:T(8,128)(2,1)}, bf16[64,8192]{1,0:T(8,128)(2,1)}, u32[]{:S(2)}, u32[]{:S(2)}) collective-permute-start(bf16[64,8192]{1,0:T(8,128)(2,1)} %get-tuple-element.84), channel_id=1, source_target_pairs={{4,8},{5,9},{6,10},{7,11},{8,4},{9,5},{10,6},{11,7},{20,24},{21,25... | collective-permute-start | bytes 3145736 | tf_op jit(solution)/shard_map/ppermute | solution.py:268
  61.5 1.3 collective-permute-start.10
  63.6 10.8 %shard_map.78 = (f32[1024,256]{1,0:T(8,128)}, s32[1]{0:T(128)}) custom-call(s32[1]{0:T(128)} %get-tuple-element.80.turn_ref, s32[3]{0:T(128)} %concatenate.25.at_ref, bf16[512,14336]{1,0:T(8,128)(2,1)} %own_ref.11, bf16[512,14336]{1,0:T(8,128)(2,1)} %collective-permute-done.refs_0_.other_ref, bf16[64,7168]{1,0:T(8,128)(2,1)} %get-tuple-element.76.refs_0_, ...), custom_call_target="tpu_custom_call" | custom-call | flops 1 | bytes 1 | tf_op jit(solution)/shard_map/pallas_call | solution.py:217
  74.5 7.9 %collective-permute-done.10.refs_2_ = bf16[64,7168]{1,0:T(8,128)(2,1)} collective-permute-done((bf16[64,7168]{1,0:T(8,128)(2,1)}, bf16[64,7168]{1,0:T(8,128)(2,1)}, u32[]{:S(2)}, u32[]{:S(2)}) %collective-permute-start.10) | collective-permute-done | bytes 917536 | tf_op jit(solution)/shard_map/ppermute | solution.py:66
  85.6 1.6 collective-permute-start.12
  88.9 20.6 %collective-permute-done.13.refs_3_ = bf16[64,7168]{1,0:T(8,128)(2,1)S(1)} collective-permute-done((bf16[64,7168]{1,0:T(8,128)(2,1)}, bf16[64,7168]{1,0:T(8,128)(2,1)S(1)}, u32[]{:S(2)}, u32[]{:S(2)}) %collective-permute-start.13) | collective-permute-done | bytes 917536 | tf_op jit(solution)/shard_map/ppermute | solution.py:62
  110.4 3.2 %shard_map.81 = (bf16[64,8192]{1,0:T(8,128)(2,1)}, bf16[64,7168]{1,0:T(8,128)(2,1)}, bf16[64,7168]{1,0:T(8,128)(2,1)}, bf16[64,7168]{1,0:T(8,128)(2,1)}, bf16[64,8192]{1,0:T(8,128)(2,1)}, /*index=5*/s32[1]{0:T(128)}) custom-call(s32[1]{0:T(128)} %shard_map.80.turn_ref, ...), custom_call_target="tpu_custom_call", output_to_operand_aliasing={{0}: (3, {}), {1}: (4, {}), {2}: (5, {}), {3}: (6, {}), {4}... | custom-call | flops 1 | bytes 1 | tf_op jit(solution)/shard_map/pallas_call | solution.py:107
  113.6 3.2 %collective-permute-start.17 = (bf16[64,8192]{1,0:T(8,128)(2,1)}, bf16[64,8192]{1,0:T(8,128)(2,1)}, u32[]{:S(2)}, u32[]{:S(2)}) collective-permute-start(bf16[64,8192]{1,0:T(8,128)(2,1)} %get-tuple-element.97.refs_3_), channel_id=1, source_target_pairs={{0,4},{1,5},{2,6},{3,7},{4,0},{5,1},{6,2},{7,3},{8,12},{9,13},{10,... | collective-permute-start | bytes 3145736 | tf_op jit(solution)/shard_map/ppermute | solution.py:62
  119.0 10.7 %shard_map.82 = (f32[1024,256]{1,0:T(8,128)}, s32[1]{0:T(128)}) custom-call(s32[1]{0:T(128)} %get-tuple-element.90.turn_ref, s32[3]{0:T(128)} %concatenate.26.at_ref, bf16[512,14336]{1,0:T(8,128)(2,1)} %own_ref.11, bf16[512,14336]{1,0:T(8,128)(2,1)} %collective-permute-done.refs_0_.other_ref, bf16[64,7168]{1,0:T(8,128)(2,1)} %get-tuple-element.91.refs_0_, ...), custom_call_target="tpu_custom_call" | custom-call | flops 1 | bytes 1 | tf_op jit(solution)/shard_map/pallas_call | solution.py:217
  129.7 8.6 %collective-permute-done.15.refs_0_ = bf16[64,7168]{1,0:T(8,128)(2,1)S(1)} collective-permute-done((bf16[64,7168]{1,0:T(8,128)(2,1)}, bf16[64,7168]{1,0:T(8,128)(2,1)S(1)}, u32[]{:S(2)}, u32[]{:S(2)}) %collective-permute-start.15) | collective-permute-done | bytes 917536 | tf_op jit(solution)/shard_map/ppermute | solution.py:62
  138.3 2.0 collective-permute-done.17.refs_2_
  143.2 10.9 %shard_map.84 = (f32[1024,256]{1,0:T(8,128)}, s32[1]{0:T(128)}) custom-call(s32[1]{0:T(128)} %get-tuple-element.100.turn_ref, s32[3]{0:T(128)} %concatenate.25.at_ref, bf16[512,14336]{1,0:T(8,128)(2,1)} %own_ref.11, bf16[512,14336]{1,0:T(8,128)(2,1)} %collective-permute-done.refs_0_.other_ref, bf16[64,7168]{1,0:T(8,128)(2,1)} %get-tuple-element.101.refs_0_, ...), custom_call_target="tpu_custom_call" | custom-call | flops 1 | bytes 1 | tf_op jit(solution)/shard_map/pallas_call | solution.py:217
  154.1 6.7 %collective-permute-done.18.refs_0_ = bf16[64,8192]{1,0:T(8,128)(2,1)} collective-permute-done((bf16[64,8192]{1,0:T(8,128)(2,1)}, bf16[64,8192]{1,0:T(8,128)(2,1)}, u32[]{:S(2)}, u32[]{:S(2)}) %collective-permute-start.18) | collective-permute-done | bytes 1048608 | tf_op jit(solution)/shard_map/ppermute | solution.py:62
  160.8 2.5 %collective-permute-done.19.refs_1_ = bf16[64,7168]{1,0:T(8,128)(2,1)S(1)} collective-permute-done((bf16[64,7168]{1,0:T(8,128)(2,1)}, bf16[64,7168]{1,0:T(8,128)(2,1)S(1)}, u32[]{:S(2)}, u32[]{:S(2)}) %collective-permute-start.19) | collective-permute-done | bytes 917536 | tf_op jit(solution)/shard_map/ppermute | solution.py:66
  163.3 1.6 collective-permute-done.20.refs_2_
  166.1 1.5 collective-permute-start.24
  168.1 2.8 %collective-permute-start.21 = (s32[2,4]{1,0:T(2,128)S(1)}, s32[2,4]{1,0:T(2,128)S(1)}, u32[]{:S(2)}, u32[]{:S(2)}) collective-permute-start(s32[2,4]{1,0:T(2,128)S(1)} %pad_add_fusion), channel_id=1, source_target_pairs={{0,1},{1,0},{2,3},{3,2},{4,5},{5,4},{6,7},{7,6},{8,9},{9,8},{10,11... | collective-permute-start | bytes 104 | tf_op jit(solution)/shard_map/ppermute | solution.py:62
  170.9 1.9 slice.19
  173.0 1.8 slice.20
  177.3 13.7 %shard_map.86 = (f32[8,256]{1,0:T(8,128)}, s32[1]{0:T(128)}) custom-call(s32[1]{0:T(128)} %get-tuple-element.108.turn_ref, s32[3]{0:T(128)} %broadcast_8_at_ref.2.at_ref, bf16[512,8192]{1,0:T(8,128)(2,1)} %own_ref.10, bf16[512,8192]{1,0:T(8,128)(2,1)} %collective-permute-done.4.refs_2_.other_ref, bf16[64,8192]{1,0:T(8,128)(2,1)} %bitcast.22, ...), custom_call_target="tpu_custom_call" | custom-call | flops 1 | bytes 1 | tf_op jit(solution)/shard_map/pallas_call | solution.py:217
  193.2 11.6 %shard_map.88 = (f32[1024,256]{1,0:T(8,128)}, s32[1]{0:T(128)}) custom-call(s32[1]{0:T(128)} %get-tuple-element.117.turn_ref, s32[3]{0:T(128)} %broadcast_8_at_ref.2.at_ref, bf16[512,8192]{1,0:T(8,128)(2,1)} %own_ref.10, bf16[512,8192]{1,0:T(8,128)(2,1)} %collective-permute-done.4.refs_2_.other_ref, bf16[64,8192]{1,0:T(8,128)(2,1)} %get-tuple-element.118.refs_0_, ...), custom_call_target="tpu_custom_call" | custom-call | flops 1 | bytes 1 | tf_op jit(solution)/shard_map/pallas_call | solution.py:217
  204.8 12.9 %shard_map.89 = (f32[8,256]{1,0:T(8,128)}, s32[1]{0:T(128)}) custom-call(s32[1]{0:T(128)} %get-tuple-element.121.turn_ref, s32[3]{0:T(128)} %concatenate.26.at_ref, bf16[512,14336]{1,0:T(8,128)(2,1)} %own_ref.11, bf16[512,14336]{1,0:T(8,128)(2,1)} %collective-permute-done.refs_0_.other_ref, bf16[64,7168]{1,0:T(8,128)(2,1)} %get-tuple-element.122.refs_0_, ...), custom_call_target="tpu_custom_call" | custom-call | flops 1 | bytes 1 | tf_op jit(solution)/shard_map/pallas_call | solution.py:217
  218.5 2.6 %collective-permute-start.27 = (f32[4,512]{1,0:T(4,128)S(1)}, f32[4,512]{1,0:T(4,128)S(1)}, u32[]{:S(2)}, u32[]{:S(2)}) collective-permute-start(f32[4,512]{1,0:T(4,128)S(1)} %pad_maximum_fusion), channel_id=1, source_target_pairs={{0,1},{1,0},{2,3},{3,2},{4,5},{5,4},{6,7},{7,6},{8,9},{9,8},{10,11... | collective-permute-start | bytes 24584 | tf_op jit(solution)/shard_map/ppermute | solution.py:62
  (83 shorter events, 28.5 us)
Async XLA Ops:
  0.0 31.4 %collective-permute-start = (bf16[512,14336]{1,0:T(8,128)(2,1)}, bf16[512,14336]{1,0:T(8,128)(2,1)}, u32[]{:S(2)}, u32[]{:S(2)}) collective-permute-start(bf16[512,14336]{1,0:T(8,128)(2,1)} %own_ref.11), channel_id=1, source_target_pairs={{0,1},{1,0},{2,3},{3,2},{4,5},{5,4},{6,7},{7,6},{8,9},{9,8},{10,11... | collective-permute-start | bytes 44040200 | tf_op jit(solution)/shard_map/ppermute | solution.py:62
  0.7 35.4 %collective-permute-start.4 = (bf16[512,8192]{1,0:T(8,128)(2,1)}, bf16[512,8192]{1,0:T(8,128)(2,1)}, u32[]{:S(2)}, u32[]{:S(2)}) collective-permute-start(bf16[512,8192]{1,0:T(8,128)(2,1)} %own_ref.10), channel_id=1, source_target_pairs={{0,1},{1,0},{2,3},{3,2},{4,5},{5,4},{6,7},{7,6},{8,9},{9,8},{10,11... | collective-permute-start | bytes 25165832 | tf_op jit(solution)/shard_map/ppermute | solution.py:62
  9.2 17.8 %collective-permute-start.1 = (bf16[64,7168]{1,0:T(8,128)(2,1)}, bf16[64,7168]{1,0:T(8,128)(2,1)}, u32[]{:S(2)}, u32[]{:S(2)}) collective-permute-start(bf16[64,7168]{1,0:T(8,128)(2,1)} %get-tuple-element.72.refs_5_), channel_id=1, source_target_pairs={{0,2},{1,3},{2,0},{3,1},{4,6},{5,7},{6,4},{7,5},{8,10},{9,11},{10,... | collective-permute-start | bytes 2752520 | tf_op jit(solution)/shard_map/ppermute | solution.py:62
  10.5 17.7 %collective-permute-start.2 = (bf16[64,7168]{1,0:T(8,128)(2,1)}, bf16[64,7168]{1,0:T(8,128)(2,1)S(1)}, u32[]{:S(2)}, u32[]{:S(2)}) collective-permute-start(bf16[64,7168]{1,0:T(8,128)(2,1)} %get-tuple-element.72.refs_5_), channel_id=1, source_target_pairs={{0,4},{1,5},{2,6},{3,7},{4,0},{5,1},{6,2},{7,3},{8,12},{9,13},{10,... | collective-permute-start | bytes 2752520 | tf_op jit(solution)/shard_map/ppermute | solution.py:62
  10.7 20.7 %collective-permute-start.3 = (bf16[64,7168]{1,0:T(8,128)(2,1)}, bf16[64,7168]{1,0:T(8,128)(2,1)}, u32[]{:S(2)}, u32[]{:S(2)}) collective-permute-start(bf16[64,7168]{1,0:T(8,128)(2,1)} %get-tuple-element.72.refs_5_), channel_id=1, source_target_pairs={{4,8},{5,9},{6,10},{7,11},{8,4},{9,5},{10,6},{11,7},{20,24},{21,25... | collective-permute-start | bytes 2752520 | tf_op jit(solution)/shard_map/ppermute | solution.py:268
  32.6 21.8 %collective-permute-start.6 = (bf16[64,8192]{1,0:T(8,128)(2,1)}, bf16[64,8192]{1,0:T(8,128)(2,1)}, u32[]{:S(2)}, u32[]{:S(2)}) collective-permute-start(bf16[64,8192]{1,0:T(8,128)(2,1)} %get-tuple-element.77.refs_6_), channel_id=1, source_target_pairs={{0,2},{1,3},{2,0},{3,1},{4,6},{5,7},{6,4},{7,5},{8,10},{9,11},{10,... | collective-permute-start | bytes 3145736 | tf_op jit(solution)/shard_map/ppermute | solution.py:62
  32.9 3.2 %collective-permute-start.5 = (bf16[64,7168]{1,0:T(8,128)(2,1)}, bf16[64,7168]{1,0:T(8,128)(2,1)S(1)}, u32[]{:S(2)}, u32[]{:S(2)}) collective-permute-start(bf16[64,7168]{1,0:T(8,128)(2,1)} %get-tuple-element.76.refs_0_), channel_id=1, source_target_pairs={{0,12},{1,13},{2,14},{3,15},{12,0},{13,1},{14,2},{15,3},{16,28},{1... | collective-permute-start | bytes 2752520 | tf_op jit(solution)/shard_map/ppermute | solution.py:268
  33.6 19.3 %collective-permute-start.7 = (bf16[64,7168]{1,0:T(8,128)(2,1)}, bf16[64,7168]{1,0:T(8,128)(2,1)}, u32[]{:S(2)}, u32[]{:S(2)}) collective-permute-start(bf16[64,7168]{1,0:T(8,128)(2,1)} %get-tuple-element.78.refs_1_), channel_id=1, source_target_pairs={{0,16},{16,0},{1,17},{17,1},{2,18},{18,2},{3,19},{19,3},{4,20},{20... | collective-permute-start | bytes 2752520 | tf_op jit(solution)/shard_map/ppermute | solution.py:66
  36.1 18.3 %copy-start.4 = (bf16[64,7168]{1,0:T(8,128)(2,1)}, bf16[64,7168]{1,0:T(8,128)(2,1)S(1)}, u32[]{:S(2)}) copy-start(bf16[64,7168]{1,0:T(8,128)(2,1)S(1)} %collective-permute-done.5.refs_3_) | copy-start | bytes 2752516
  57.6 26.1 %collective-permute-start.11 = (bf16[64,8192]{1,0:T(8,128)(2,1)}, bf16[64,8192]{1,0:T(8,128)(2,1)}, u32[]{:S(2)}, u32[]{:S(2)}) collective-permute-start(bf16[64,8192]{1,0:T(8,128)(2,1)} %get-tuple-element.84), channel_id=1, source_target_pairs={{4,8},{5,9},{6,10},{7,11},{8,4},{9,5},{10,6},{11,7},{20,24},{21,25... | collective-permute-start | bytes 3145736 | tf_op jit(solution)/shard_map/ppermute | solution.py:268
  61.5 20.8 %collective-permute-start.10 = (bf16[64,7168]{1,0:T(8,128)(2,1)}, bf16[64,7168]{1,0:T(8,128)(2,1)}, u32[]{:S(2)}, u32[]{:S(2)}) collective-permute-start(bf16[64,7168]{1,0:T(8,128)(2,1)} %get-tuple-element.81.refs_2_), channel_id=1, source_target_pairs={{0,16},{16,0},{1,17},{17,1},{2,18},{18,2},{3,19},{19,3},{4,20},{20... | collective-permute-start | bytes 2752520 | tf_op jit(solution)/shard_map/ppermute | solution.py:66
  62.8 20.7 %collective-permute-start.8 = (bf16[64,7168]{1,0:T(8,128)(2,1)}, bf16[64,7168]{1,0:T(8,128)(2,1)S(1)}, u32[]{:S(2)}, u32[]{:S(2)}) collective-permute-start(bf16[64,7168]{1,0:T(8,128)(2,1)} %get-tuple-element.82.refs_3_), channel_id=1, source_target_pairs={{0,4},{1,5},{2,6},{3,7},{4,0},{5,1},{6,2},{7,3},{8,12},{9,13},{10,... | collective-permute-start | bytes 2752520 | tf_op jit(solution)/shard_map/ppermute | solution.py:62
  62.8 20.9 %collective-permute-start.9 = (bf16[64,7168]{1,0:T(8,128)(2,1)}, bf16[64,7168]{1,0:T(8,128)(2,1)}, u32[]{:S(2)}, u32[]{:S(2)}) collective-permute-start(bf16[64,7168]{1,0:T(8,128)(2,1)} %get-tuple-element.81.refs_2_), channel_id=1, source_target_pairs={{0,2},{1,3},{2,0},{3,1},{4,6},{5,7},{6,4},{7,5},{8,10},{9,11},{10,... | collective-permute-start | bytes 2752520 | tf_op jit(solution)/shard_map/ppermute | solution.py:62
  85.6 24.2 %collective-permute-start.12 = (bf16[64,8192]{1,0:T(8,128)(2,1)}, bf16[64,8192]{1,0:T(8,128)(2,1)}, u32[]{:S(2)}, u32[]{:S(2)}) collective-permute-start(bf16[64,8192]{1,0:T(8,128)(2,1)} %get-tuple-element.88.refs_6_), channel_id=1, source_target_pairs={{0,12},{1,13},{2,14},{3,15},{12,0},{13,1},{14,2},{15,3},{16,28},{1... | collective-permute-start | bytes 3145736 | tf_op jit(solution)/shard_map/ppermute | solution.py:268
  87.3 22.2 %collective-permute-start.13 = (bf16[64,7168]{1,0:T(8,128)(2,1)}, bf16[64,7168]{1,0:T(8,128)(2,1)S(1)}, u32[]{:S(2)}, u32[]{:S(2)}) collective-permute-start(bf16[64,7168]{1,0:T(8,128)(2,1)} %get-tuple-element.82.refs_3_), channel_id=1, source_target_pairs={{0,2},{1,3},{2,0},{3,1},{4,6},{5,7},{6,4},{7,5},{8,10},{9,11},{10,... | collective-permute-start | bytes 2752520 | tf_op jit(solution)/shard_map/ppermute | solution.py:62
  87.5 22.3 %collective-permute-start.14 = (bf16[64,7168]{1,0:T(8,128)(2,1)}, bf16[64,7168]{1,0:T(8,128)(2,1)}, u32[]{:S(2)}, u32[]{:S(2)}) collective-permute-start(bf16[64,7168]{1,0:T(8,128)(2,1)} %get-tuple-element.82.refs_3_), channel_id=1, source_target_pairs={{0,16},{16,0},{1,17},{17,1},{2,18},{18,2},{3,19},{19,3},{4,20},{20... | collective-permute-start | bytes 2752520 | tf_op jit(solution)/shard_map/ppermute | solution.py:66
  113.6 26.7 %collective-permute-start.17 = (bf16[64,8192]{1,0:T(8,128)(2,1)}, bf16[64,8192]{1,0:T(8,128)(2,1)}, u32[]{:S(2)}, u32[]{:S(2)}) collective-permute-start(bf16[64,8192]{1,0:T(8,128)(2,1)} %get-tuple-element.97.refs_3_), channel_id=1, source_target_pairs={{0,4},{1,5},{2,6},{3,7},{4,0},{5,1},{6,2},{7,3},{8,12},{9,13},{10,... | collective-permute-start | bytes 3145736 | tf_op jit(solution)/shard_map/ppermute | solution.py:62
  116.8 21.5 %collective-permute-start.15 = (bf16[64,7168]{1,0:T(8,128)(2,1)}, bf16[64,7168]{1,0:T(8,128)(2,1)S(1)}, u32[]{:S(2)}, u32[]{:S(2)}) collective-permute-start(bf16[64,7168]{1,0:T(8,128)(2,1)} %get-tuple-element.96.refs_2_), channel_id=1, source_target_pairs={{0,2},{1,3},{2,0},{3,1},{4,6},{5,7},{6,4},{7,5},{8,10},{9,11},{10,... | collective-permute-start | bytes 2752520 | tf_op jit(solution)/shard_map/ppermute | solution.py:62
  117.0 21.3 %collective-permute-start.16 = (bf16[64,7168]{1,0:T(8,128)(2,1)}, bf16[64,7168]{1,0:T(8,128)(2,1)}, u32[]{:S(2)}, u32[]{:S(2)}) collective-permute-start(bf16[64,7168]{1,0:T(8,128)(2,1)} %get-tuple-element.96.refs_2_), channel_id=1, source_target_pairs={{0,16},{16,0},{1,17},{17,1},{2,18},{18,2},{3,19},{19,3},{4,20},{20... | collective-permute-start | bytes 2752520 | tf_op jit(solution)/shard_map/ppermute | solution.py:66
  117.8 43.0 %collective-permute-start.18 = (bf16[64,8192]{1,0:T(8,128)(2,1)}, bf16[64,8192]{1,0:T(8,128)(2,1)}, u32[]{:S(2)}, u32[]{:S(2)}) collective-permute-start(bf16[64,8192]{1,0:T(8,128)(2,1)} %get-tuple-element.97.refs_3_), channel_id=1, source_target_pairs={{0,2},{1,3},{2,0},{3,1},{4,6},{5,7},{6,4},{7,5},{8,10},{9,11},{10,... | collective-permute-start | bytes 3145736 | tf_op jit(solution)/shard_map/ppermute | solution.py:62
  141.5 23.5 %collective-permute-start.20 = (bf16[64,8192]{1,0:T(8,128)(2,1)}, bf16[64,8192]{1,0:T(8,128)(2,1)}, u32[]{:S(2)}, u32[]{:S(2)}) collective-permute-start(bf16[64,8192]{1,0:T(8,128)(2,1)} %get-tuple-element.105), channel_id=1, source_target_pairs={{0,4},{1,5},{2,6},{3,7},{4,0},{5,1},{6,2},{7,3},{8,12},{9,13},{10,... | collective-permute-start | bytes 3145736 | tf_op jit(solution)/shard_map/ppermute | solution.py:62
  142.7 20.7 %collective-permute-start.19 = (bf16[64,7168]{1,0:T(8,128)(2,1)}, bf16[64,7168]{1,0:T(8,128)(2,1)S(1)}, u32[]{:S(2)}, u32[]{:S(2)}) collective-permute-start(bf16[64,7168]{1,0:T(8,128)(2,1)} %get-tuple-element.101.refs_0_), channel_id=1, source_target_pairs={{0,16},{16,0},{1,17},{17,1},{2,18},{18,2},{3,19},{19,3},{4,20},{20... | collective-permute-start | bytes 2752520 | tf_op jit(solution)/shard_map/ppermute | solution.py:66
  142.9 48.1 %collective-permute-start.22 = (bf16[64,8192]{1,0:T(8,128)(2,1)}, bf16[64,8192]{1,0:T(8,128)(2,1)}, u32[]{:S(2)}, u32[]{:S(2)}) collective-permute-start(bf16[64,8192]{1,0:T(8,128)(2,1)} %get-tuple-element.115.refs_2_), channel_id=1, source_target_pairs={{0,2},{1,3},{2,0},{3,1},{4,6},{5,7},{6,4},{7,5},{8,10},{9,11},{10,... | collective-permute-start | bytes 3145736 | tf_op jit(solution)/shard_map/ppermute | solution.py:62
  143.1 24.8 %copy-start.8 = (s32[4]{0:T(128)S(1)}, s32[4]{0:T(128)}, u32[]{:S(2)}) copy-start(s32[4]{0:T(128)} %param.11) | copy-start | bytes 52
  143.2 24.9 %copy-start.9 = (s32[4]{0:T(128)S(1)}, s32[4]{0:T(128)}, u32[]{:S(2)}) copy-start(s32[4]{0:T(128)} %param.12) | copy-start | bytes 52
  154.1 22.0 %copy-start.10 = (s32[8]{0:T(128)S(1)}, s32[8]{0:T(128)}, u32[]{:S(2)}) copy-start(s32[8]{0:T(128)} %constant.58.clone) | copy-start | bytes 100
  166.1 24.9 %collective-permute-start.24 = (bf16[64,8192]{1,0:T(8,128)(2,1)}, bf16[64,8192]{1,0:T(8,128)(2,1)}, u32[]{:S(2)}, u32[]{:S(2)}) collective-permute-start(bf16[64,8192]{1,0:T(8,128)(2,1)} %get-tuple-element.109.refs_1_), channel_id=1, source_target_pairs={{0,4},{1,5},{2,6},{3,7},{4,0},{5,1},{6,2},{7,3},{8,12},{9,13},{10,... | collective-permute-start | bytes 3145736 | tf_op jit(solution)/shard_map/ppermute | solution.py:62
  167.7 23.4 %collective-permute-start.23 = (bf16[64,7168]{1,0:T(8,128)(2,1)}, bf16[64,7168]{1,0:T(8,128)(2,1)S(1)}, u32[]{:S(2)}, u32[]{:S(2)}) collective-permute-start(bf16[64,7168]{1,0:T(8,128)(2,1)} %get-tuple-element.116), channel_id=1, source_target_pairs={{0,16},{16,0},{1,17},{17,1},{2,18},{18,2},{3,19},{19,3},{4,20},{20... | collective-permute-start | bytes 2752520 | tf_op jit(solution)/shard_map/ppermute | solution.py:66
  168.1 6.7 %collective-permute-start.21 = (s32[2,4]{1,0:T(2,128)S(1)}, s32[2,4]{1,0:T(2,128)S(1)}, u32[]{:S(2)}, u32[]{:S(2)}) collective-permute-start(s32[2,4]{1,0:T(2,128)S(1)} %pad_add_fusion), channel_id=1, source_target_pairs={{0,1},{1,0},{2,3},{3,2},{4,5},{5,4},{6,7},{7,6},{8,9},{9,8},{10,11... | collective-permute-start | bytes 104 | tf_op jit(solution)/shard_map/ppermute | solution.py:62
  172.7 32.1 %collective-permute-start.25 = (bf16[32,7168]{1,0:T(8,128)(2,1)}, bf16[32,7168]{1,0:T(8,128)(2,1)}, u32[]{:S(2)}, u32[]{:S(2)}) collective-permute-start(bf16[32,7168]{1,0:T(8,128)(2,1)} %slice.19), channel_id=1, source_target_pairs={{0,2},{1,3},{2,0},{3,1},{4,6},{5,7},{6,4},{7,5},{8,10},{9,11},{10,... | collective-permute-start | bytes 1376264 | tf_op jit(solution)/shard_map/ppermute | solution.py:62
  174.8 30.0 %collective-permute-start.26 = (bf16[32,7168]{1,0:T(8,128)(2,1)}, bf16[32,7168]{1,0:T(8,128)(2,1)}, u32[]{:S(2)}, u32[]{:S(2)}) collective-permute-start(bf16[32,7168]{1,0:T(8,128)(2,1)} %slice.20), channel_id=1, source_target_pairs={{0,16},{16,0},{1,17},{17,1},{2,18},{18,2},{3,19},{19,3},{4,20},{20... | collective-permute-start | bytes 1376264 | tf_op jit(solution)/shard_map/ppermute | solution.py:66
  218.5 3.4 %collective-permute-start.27 = (f32[4,512]{1,0:T(4,128)S(1)}, f32[4,512]{1,0:T(4,128)S(1)}, u32[]{:S(2)}, u32[]{:S(2)}) collective-permute-start(f32[4,512]{1,0:T(4,128)S(1)} %pad_maximum_fusion), channel_id=1, source_target_pairs={{0,1},{1,0},{2,3},{3,2},{4,5},{5,4},{6,7},{7,6},{8,9},{9,8},{10,11... | collective-permute-start | bytes 24584 | tf_op jit(solution)/shard_map/ppermute | solution.py:62
  (7 other events, 22.5 us)

commit v12 on v11

--- a/solution.py
+++ b/solution.py
@@ -55,7 +55,7 @@
 
 CORE, COLUMN, NEAR, ACROSS, OPPOSITE = 1, 2, 4, 12, 8
 LITTLE = pl.CostEstimate(flops=1, bytes_accessed=1, transcendentals=0)
-VMEM_LIMIT = 63 * 1024 * 1024
+VMEM_LIMIT = 127 * 512 * 1024
 
 
 def flip(array, code, count):
@@ -316,20 +316,20 @@
     c["x"] = swap_groups(a["x"])
     turn = pause(turn)
 
-    turn, (a["f"], b["x"], c["x"], b_one, a["n"]) = after(
-        turn, [a_end, b["x"], c["x"], b_one, a["n"]], [grads_there], (inside, a_mid)
+    turn, (a["f"], b["x"], c["x"], b_one) = after(
+        turn, [a_end, b["x"], c["x"], b_one], [grads_there], (inside, a_mid)
     )
     a["o"] = near(a["f"])
     a["xn"] = over_x(a["n"])
     c["n"] = swap_groups(a["n"])
     b_mid = middle(b_one)
-    turn, a_first = times_a(turn, 0)
-
-    turn, (a["o"], a["xn"], c["n"], b_mid, b_two) = after(turn, [a["o"], a["xn"], c["n"], b_mid, b_two])
+    turn = pause(turn)
+
+    turn, (c["n"], a["o"], a["xn"], b_mid, b_two) = after(turn, [c["n"], a["o"], a["xn"], b_mid, b_two])
     a["xf"] = over_x(a["f"])
     c["f"] = swap_groups(a["f"])
     b_end = ends(b_two)
-    turn = pause(turn)
+    turn, a_first = times_a(turn, 0)
 
     turn, (b["f"], a["xf"], c["f"], a["o"], b_two) = after(
         turn, [b_end, a["xf"], c["f"], a["o"], b_two], (), (inside, b_mid)

time: 225 us -> 223 us (level)
    ppermute x17, waiting for transfers between devices: 54.7 us -> 61.4 us  [flip(): return lax.ppermute(array, 'dp', [(i, i ^ code) for i in range(count)])]
    ppermute x7, waiting for transfers between devices: 27.6 us -> 21.3 us  [swap_groups(): return lax.ppermute(array, 'groups', [(0, 1), (1, 0)])]
  transfers between devices with their start and end apart: 28 -> 28, of which waited for: 16 -> 15; matrix products, arithmetic and copies ran while one was open for 4% -> 5% of each run, Pallas kernels for 33% -> 33%
where the time goes in v12:
time: 223 us; the launch traced here: 222 us
  Pallas kernels  92.5 us (41%)
  waiting for transfers between devices  85.7 us (38%)
  starting transfers between devices  30.3 us (14%)
  local copies, waits for them, and re-layouts  9.29 us (4%)
  other arithmetic  2.77 us (1%)
    pallas_call x6, Pallas kernels, proj(): pl.pallas_call(functools.partial(proj_kernel, len(pieces), last), out_sha...  70.6 us
    ppermute x17, waiting for transfers between devices, flip(): return lax.ppermute(array, 'dp', [(i, i ^ code) for i in range(count)])  61.4 us
    ppermute x7, waiting for transfers between devices, swap_groups(): return lax.ppermute(array, 'groups', [(0, 1), (1, 0)])  21.3 us
    pallas_call x9, Pallas kernels, after(): pl.pallas_call(functools.partial(after_kernel, count, merge is not None),...  14.3 us
    ppermute x17, starting transfers between devices, flip(): return lax.ppermute(array, 'dp', [(i, i ^ code) for i in range(count)])  14.2 us
    ppermute x4, starting transfers between devices, lines(): return lax.ppermute(piece, 'dp', pairs)  11.5 us
    pallas_call x2, Pallas kernels, prepare(): pl.pallas_call(prepare_kernel, out_shape=[jax.ShapeDtypeStruct(x.shape, x...  7.59 us
    ppermute x7, starting transfers between devices, swap_groups(): return lax.ppermute(array, 'groups', [(0, 1), (1, 0)])  4.62 us
  transfers between devices with their start and end apart: 28, of which 15 were waited for; matrix products, arithmetic and copies ran while one was open for 5% of the time, Pallas kernels for 33%

profile of v12, /device:TPU:9, one launch (start us, length us, event | category | flops | bytes accessed | tf_op | source)
XLA Modules:
  0.0 221.6 jit_solution(6093013978144083764)
XLA Ops:
  0.7 2.2 constant_dynamic-slice_fusion.refs_0_
  2.9 6.4 %shard_map.73 = (bf16[64,7168]{1,0:T(8,128)(2,1)}, bf16[64,7168]{1,0:T(8,128)(2,1)}, bf16[64,8192]{1,0:T(8,128)(2,1)}, bf16[64,8192]{1,0:T(8,128)(2,1)}, s32[1]{0:T(128)}) custom-call(s32[1]{0:T(128)} %bitcast.works_ref, s32[1]{0:T(128)} %constant.26.clone.1.turn_ref, s32[1]{0:T(128)S(6)} %sub.16.first_ref, ...), custom_call_target="tpu_custom_call", output_to_operand_aliasing={{0}: (5, {})} | custom-call | flops 1 | bytes 1 | tf_op jit(solution)/shard_map/pallas_call | solution.py:142
  9.3 1.3 collective-permute-start.1
  10.7 4.3 %collective-permute-start.3 = (bf16[64,7168]{1,0:T(8,128)(2,1)}, bf16[64,7168]{1,0:T(8,128)(2,1)}, u32[]{:S(2)}, u32[]{:S(2)}) collective-permute-start(bf16[64,7168]{1,0:T(8,128)(2,1)} %get-tuple-element.71.refs_5_), channel_id=1, source_target_pairs={{4,8},{5,9},{6,10},{7,11},{8,4},{9,5},{10,6},{11,7},{20,24},{21,25... | collective-permute-start | bytes 2752520 | tf_op jit(solution)/shard_map/ppermute | solution.py:268
  16.3 10.8 %collective-permute-done.1.refs_1_ = bf16[64,7168]{1,0:T(8,128)(2,1)} collective-permute-done((bf16[64,7168]{1,0:T(8,128)(2,1)}, bf16[64,7168]{1,0:T(8,128)(2,1)}, u32[]{:S(2)}, u32[]{:S(2)}) %collective-permute-start.1) | collective-permute-done | bytes 917536 | tf_op jit(solution)/shard_map/ppermute | solution.py:62
  27.1 1.3 collective-permute-done.2.refs_2_
  28.4 3.0 %collective-permute-done.3.refs_3_ = bf16[64,7168]{1,0:T(8,128)(2,1)} collective-permute-done((bf16[64,7168]{1,0:T(8,128)(2,1)}, bf16[64,7168]{1,0:T(8,128)(2,1)}, u32[]{:S(2)}, u32[]{:S(2)}) %collective-permute-start.3) | collective-permute-done | bytes 917536 | tf_op jit(solution)/shard_map/ppermute | solution.py:268
  32.9 1.6 collective-permute-start.5
  36.8 16.8 %collective-permute-done.7.refs_5_ = bf16[64,7168]{1,0:T(8,128)(2,1)} collective-permute-done((bf16[64,7168]{1,0:T(8,128)(2,1)}, bf16[64,7168]{1,0:T(8,128)(2,1)}, u32[]{:S(2)}, u32[]{:S(2)}) %collective-permute-start.7) | collective-permute-done | bytes 917536 | tf_op jit(solution)/shard_map/ppermute | solution.py:66
  54.4 3.2 %shard_map.77 = (bf16[64,7168]{1,0:T(8,128)(2,1)}, bf16[64,8192]{1,0:T(8,128)(2,1)}, bf16[64,7168]{1,0:T(8,128)(2,1)}, bf16[64,8192]{1,0:T(8,128)(2,1)}, s32[1]{0:T(128)}) custom-call(s32[1]{0:T(128)} %shard_map.76.turn_ref, s32[1]{0:T(128)} %bitcast.4.refs_0_, ...), custom_call_target="tpu_custom_call", output_to_operand_aliasing={{0}: (4, {}), {1}: (5, {}), {2}: (6, {}), {3}: (7, {})} | custom-call | flops 1 | bytes 1 | tf_op jit(solution)/shard_map/pallas_call | solution.py:107
  57.6 3.9 %collective-permute-start.11 = (bf16[64,8192]{1,0:T(8,128)(2,1)}, bf16[64,8192]{1,0:T(8,128)(2,1)}, u32[]{:S(2)}, u32[]{:S(2)}) collective-permute-start(bf16[64,8192]{1,0:T(8,128)(2,1)} %get-tuple-element.81), channel_id=1, source_target_pairs={{4,8},{5,9},{6,10},{7,11},{8,4},{9,5},{10,6},{11,7},{20,24},{21,25... | collective-permute-start | bytes 3145736 | tf_op jit(solution)/shard_map/ppermute | solution.py:268
  64.5 17.9 %collective-permute-done.10.refs_2_ = bf16[64,7168]{1,0:T(8,128)(2,1)} collective-permute-done((bf16[64,7168]{1,0:T(8,128)(2,1)}, bf16[64,7168]{1,0:T(8,128)(2,1)}, u32[]{:S(2)}, u32[]{:S(2)}) %collective-permute-start.10) | collective-permute-done | bytes 917536 | tf_op jit(solution)/shard_map/ppermute | solution.py:62
  85.9 1.6 collective-permute-start.12
  88.9 10.9 %shard_map.80 = (f32[1024,256]{1,0:T(8,128)}, s32[1]{0:T(128)}) custom-call(s32[1]{0:T(128)} %get-tuple-element.83.turn_ref, s32[3]{0:T(128)} %concatenate.25.at_ref, bf16[512,14336]{1,0:T(8,128)(2,1)} %own_ref.11, bf16[512,14336]{1,0:T(8,128)(2,1)} %collective-permute-done.refs_0_.other_ref, bf16[64,7168]{1,0:T(8,128)(2,1)} %get-tuple-element.75.refs_0_, ...), custom_call_target="tpu_custom_call" | custom-call | flops 1 | bytes 1 | tf_op jit(solution)/shard_map/pallas_call | solution.py:217
  99.8 10.3 %collective-permute-done.13.refs_3_ = bf16[64,7168]{1,0:T(8,128)(2,1)} collective-permute-done((bf16[64,7168]{1,0:T(8,128)(2,1)}, bf16[64,7168]{1,0:T(8,128)(2,1)}, u32[]{:S(2)}, u32[]{:S(2)}) %collective-permute-start.13) | collective-permute-done | bytes 917536 | tf_op jit(solution)/shard_map/ppermute | solution.py:62
  110.8 3.1 %shard_map.81 = (bf16[64,8192]{1,0:T(8,128)(2,1)}, bf16[64,7168]{1,0:T(8,128)(2,1)}, bf16[64,7168]{1,0:T(8,128)(2,1)}, bf16[64,7168]{1,0:T(8,128)(2,1)}, bf16[64,8192]{1,0:T(8,128)(2,1)}, /*index=5*/s32[1]{0:T(128)}) custom-call(s32[1]{0:T(128)} %get-tuple-element.84.turn_ref, ...), custom_call_target="tpu_custom_call", output_to_operand_aliasing={{0}: (3, {}), {1}: (4, {}), {2}: (5, {}), {3}: (6, {}), {4}... | custom-call | flops 1 | bytes 1 | tf_op jit(solution)/shard_map/pallas_call | solution.py:107
  113.8 1.9 collective-permute-start.17
  118.0 10.8 %shard_map.82 = (f32[1024,256]{1,0:T(8,128)}, s32[1]{0:T(128)}) custom-call(s32[1]{0:T(128)} %get-tuple-element.88.turn_ref, s32[3]{0:T(128)} %concatenate.26.at_ref, bf16[512,14336]{1,0:T(8,128)(2,1)} %own_ref.11, bf16[512,14336]{1,0:T(8,128)(2,1)} %collective-permute-done.refs_0_.other_ref, bf16[64,7168]{1,0:T(8,128)(2,1)} %get-tuple-element.89.refs_0_, ...), custom_call_target="tpu_custom_call" | custom-call | flops 1 | bytes 1 | tf_op jit(solution)/shard_map/pallas_call | solution.py:217
  128.8 8.5 %collective-permute-done.15.refs_0_ = bf16[64,7168]{1,0:T(8,128)(2,1)} collective-permute-done((bf16[64,7168]{1,0:T(8,128)(2,1)}, bf16[64,7168]{1,0:T(8,128)(2,1)}, u32[]{:S(2)}, u32[]{:S(2)}) %collective-permute-start.15) | collective-permute-done | bytes 917536 | tf_op jit(solution)/shard_map/ppermute | solution.py:62
  137.3 1.9 collective-permute-done.17.refs_2_
  140.4 1.2 collective-permute-start.20
  142.2 10.9 %shard_map.84 = (f32[1024,256]{1,0:T(8,128)}, s32[1]{0:T(128)}) custom-call(s32[1]{0:T(128)} %get-tuple-element.98.turn_ref, s32[3]{0:T(128)} %concatenate.25.at_ref, bf16[512,14336]{1,0:T(8,128)(2,1)} %own_ref.11, bf16[512,14336]{1,0:T(8,128)(2,1)} %collective-permute-done.refs_0_.other_ref, bf16[64,7168]{1,0:T(8,128)(2,1)} %get-tuple-element.99.refs_0_, ...), custom_call_target="tpu_custom_call" | custom-call | flops 1 | bytes 1 | tf_op jit(solution)/shard_map/pallas_call | solution.py:217
  153.1 6.6 %collective-permute-done.18.refs_0_ = bf16[64,8192]{1,0:T(8,128)(2,1)} collective-permute-done((bf16[64,8192]{1,0:T(8,128)(2,1)}, bf16[64,8192]{1,0:T(8,128)(2,1)}, u32[]{:S(2)}, u32[]{:S(2)}) %collective-permute-start.18) | collective-permute-done | bytes 1048608 | tf_op jit(solution)/shard_map/ppermute | solution.py:62
  159.7 2.6 %collective-permute-done.19.refs_1_ = bf16[64,7168]{1,0:T(8,128)(2,1)} collective-permute-done((bf16[64,7168]{1,0:T(8,128)(2,1)}, bf16[64,7168]{1,0:T(8,128)(2,1)}, u32[]{:S(2)}, u32[]{:S(2)}) %collective-permute-start.19) | collective-permute-done | bytes 917536 | tf_op jit(solution)/shard_map/ppermute | solution.py:66
  162.3 2.2 collective-permute-done.20.refs_2_
  167.1 2.8 %collective-permute-start.21 = (s32[2,4]{1,0:T(2,128)S(1)}, s32[2,4]{1,0:T(2,128)S(1)}, u32[]{:S(2)}, u32[]{:S(2)}) collective-permute-start(s32[2,4]{1,0:T(2,128)S(1)} %pad_add_fusion), channel_id=1, source_target_pairs={{0,1},{1,0},{2,3},{3,2},{4,5},{5,4},{6,7},{7,6},{8,9},{9,8},{10,11... | collective-permute-start | bytes 104 | tf_op jit(solution)/shard_map/ppermute | solution.py:62
  169.8 1.8 slice.19
  172.0 1.8 slice.20
  177.5 13.7 %shard_map.86 = (f32[8,256]{1,0:T(8,128)}, s32[1]{0:T(128)}) custom-call(s32[1]{0:T(128)} %get-tuple-element.106.turn_ref, s32[3]{0:T(128)} %broadcast_8_at_ref.2.at_ref, bf16[512,8192]{1,0:T(8,128)(2,1)} %own_ref.10, bf16[512,8192]{1,0:T(8,128)(2,1)} %collective-permute-done.4.refs_2_.other_ref, bf16[64,8192]{1,0:T(8,128)(2,1)} %bitcast.22, ...), custom_call_target="tpu_custom_call" | custom-call | flops 1 | bytes 1 | tf_op jit(solution)/shard_map/pallas_call | solution.py:217
  192.4 11.6 %shard_map.88 = (f32[1024,256]{1,0:T(8,128)}, s32[1]{0:T(128)}) custom-call(s32[1]{0:T(128)} %get-tuple-element.115.turn_ref, s32[3]{0:T(128)} %broadcast_8_at_ref.2.at_ref, bf16[512,8192]{1,0:T(8,128)(2,1)} %own_ref.10, bf16[512,8192]{1,0:T(8,128)(2,1)} %collective-permute-done.4.refs_2_.other_ref, bf16[64,8192]{1,0:T(8,128)(2,1)} %get-tuple-element.116.refs_0_, ...), custom_call_target="tpu_custom_call" | custom-call | flops 1 | bytes 1 | tf_op jit(solution)/shard_map/pallas_call | solution.py:217
  204.8 12.8 %shard_map.89 = (f32[8,256]{1,0:T(8,128)}, s32[1]{0:T(128)}) custom-call(s32[1]{0:T(128)} %get-tuple-element.119.turn_ref, s32[3]{0:T(128)} %concatenate.26.at_ref, bf16[512,14336]{1,0:T(8,128)(2,1)} %own_ref.11, bf16[512,14336]{1,0:T(8,128)(2,1)} %collective-permute-done.refs_0_.other_ref, bf16[64,7168]{1,0:T(8,128)(2,1)} %get-tuple-element.120.refs_0_, ...), custom_call_target="tpu_custom_call" | custom-call | flops 1 | bytes 1 | tf_op jit(solution)/shard_map/pallas_call | solution.py:217
  218.5 1.4 collective-permute-start.27
  (67 shorter events, 30.2 us)
Async XLA Ops:
  0.0 31.4 %collective-permute-start = (bf16[512,14336]{1,0:T(8,128)(2,1)}, bf16[512,14336]{1,0:T(8,128)(2,1)}, u32[]{:S(2)}, u32[]{:S(2)}) collective-permute-start(bf16[512,14336]{1,0:T(8,128)(2,1)} %own_ref.11), channel_id=1, source_target_pairs={{0,1},{1,0},{2,3},{3,2},{4,5},{5,4},{6,7},{7,6},{8,9},{9,8},{10,11... | collective-permute-start | bytes 44040200 | tf_op jit(solution)/shard_map/ppermute | solution.py:62
  0.7 36.1 %collective-permute-start.4 = (bf16[512,8192]{1,0:T(8,128)(2,1)}, bf16[512,8192]{1,0:T(8,128)(2,1)}, u32[]{:S(2)}, u32[]{:S(2)}) collective-permute-start(bf16[512,8192]{1,0:T(8,128)(2,1)} %own_ref.10), channel_id=1, source_target_pairs={{0,1},{1,0},{2,3},{3,2},{4,5},{5,4},{6,7},{7,6},{8,9},{9,8},{10,11... | collective-permute-start | bytes 25165832 | tf_op jit(solution)/shard_map/ppermute | solution.py:62
  9.3 17.8 %collective-permute-start.1 = (bf16[64,7168]{1,0:T(8,128)(2,1)}, bf16[64,7168]{1,0:T(8,128)(2,1)}, u32[]{:S(2)}, u32[]{:S(2)}) collective-permute-start(bf16[64,7168]{1,0:T(8,128)(2,1)} %get-tuple-element.71.refs_5_), channel_id=1, source_target_pairs={{0,2},{1,3},{2,0},{3,1},{4,6},{5,7},{6,4},{7,5},{8,10},{9,11},{10,... | collective-permute-start | bytes 2752520 | tf_op jit(solution)/shard_map/ppermute | solution.py:62
  10.6 17.8 %collective-permute-start.2 = (bf16[64,7168]{1,0:T(8,128)(2,1)}, bf16[64,7168]{1,0:T(8,128)(2,1)}, u32[]{:S(2)}, u32[]{:S(2)}) collective-permute-start(bf16[64,7168]{1,0:T(8,128)(2,1)} %get-tuple-element.71.refs_5_), channel_id=1, source_target_pairs={{0,4},{1,5},{2,6},{3,7},{4,0},{5,1},{6,2},{7,3},{8,12},{9,13},{10,... | collective-permute-start | bytes 2752520 | tf_op jit(solution)/shard_map/ppermute | solution.py:62
  10.7 20.7 %collective-permute-start.3 = (bf16[64,7168]{1,0:T(8,128)(2,1)}, bf16[64,7168]{1,0:T(8,128)(2,1)}, u32[]{:S(2)}, u32[]{:S(2)}) collective-permute-start(bf16[64,7168]{1,0:T(8,128)(2,1)} %get-tuple-element.71.refs_5_), channel_id=1, source_target_pairs={{4,8},{5,9},{6,10},{7,11},{8,4},{9,5},{10,6},{11,7},{20,24},{21,25... | collective-permute-start | bytes 2752520 | tf_op jit(solution)/shard_map/ppermute | solution.py:268
  32.6 21.8 %collective-permute-start.6 = (bf16[64,8192]{1,0:T(8,128)(2,1)}, bf16[64,8192]{1,0:T(8,128)(2,1)}, u32[]{:S(2)}, u32[]{:S(2)}) collective-permute-start(bf16[64,8192]{1,0:T(8,128)(2,1)} %get-tuple-element.76.refs_6_), channel_id=1, source_target_pairs={{0,2},{1,3},{2,0},{3,1},{4,6},{5,7},{6,4},{7,5},{8,10},{9,11},{10,... | collective-permute-start | bytes 3145736 | tf_op jit(solution)/shard_map/ppermute | solution.py:62
  32.9 3.9 %collective-permute-start.5 = (bf16[64,7168]{1,0:T(8,128)(2,1)}, bf16[64,7168]{1,0:T(8,128)(2,1)}, u32[]{:S(2)}, u32[]{:S(2)}) collective-permute-start(bf16[64,7168]{1,0:T(8,128)(2,1)} %get-tuple-element.75.refs_0_), channel_id=1, source_target_pairs={{0,12},{1,13},{2,14},{3,15},{12,0},{13,1},{14,2},{15,3},{16,28},{1... | collective-permute-start | bytes 2752520 | tf_op jit(solution)/shard_map/ppermute | solution.py:268
  34.5 19.2 %collective-permute-start.7 = (bf16[64,7168]{1,0:T(8,128)(2,1)}, bf16[64,7168]{1,0:T(8,128)(2,1)}, u32[]{:S(2)}, u32[]{:S(2)}) collective-permute-start(bf16[64,7168]{1,0:T(8,128)(2,1)} %get-tuple-element.77.refs_1_), channel_id=1, source_target_pairs={{0,16},{16,0},{1,17},{17,1},{2,18},{18,2},{3,19},{19,3},{4,20},{20... | collective-permute-start | bytes 2752520 | tf_op jit(solution)/shard_map/ppermute | solution.py:66
  57.6 27.2 %collective-permute-start.11 = (bf16[64,8192]{1,0:T(8,128)(2,1)}, bf16[64,8192]{1,0:T(8,128)(2,1)}, u32[]{:S(2)}, u32[]{:S(2)}) collective-permute-start(bf16[64,8192]{1,0:T(8,128)(2,1)} %get-tuple-element.81), channel_id=1, source_target_pairs={{4,8},{5,9},{6,10},{7,11},{8,4},{9,5},{10,6},{11,7},{20,24},{21,25... | collective-permute-start | bytes 3145736 | tf_op jit(solution)/shard_map/ppermute | solution.py:268
  61.5 20.9 %collective-permute-start.10 = (bf16[64,7168]{1,0:T(8,128)(2,1)}, bf16[64,7168]{1,0:T(8,128)(2,1)}, u32[]{:S(2)}, u32[]{:S(2)}) collective-permute-start(bf16[64,7168]{1,0:T(8,128)(2,1)} %get-tuple-element.79.refs_2_), channel_id=1, source_target_pairs={{0,2},{1,3},{2,0},{3,1},{4,6},{5,7},{6,4},{7,5},{8,10},{9,11},{10,... | collective-permute-start | bytes 2752520 | tf_op jit(solution)/shard_map/ppermute | solution.py:62
  62.1 21.4 %collective-permute-start.8 = (bf16[64,7168]{1,0:T(8,128)(2,1)}, bf16[64,7168]{1,0:T(8,128)(2,1)}, u32[]{:S(2)}, u32[]{:S(2)}) collective-permute-start(bf16[64,7168]{1,0:T(8,128)(2,1)} %get-tuple-element.79.refs_2_), channel_id=1, source_target_pairs={{0,16},{16,0},{1,17},{17,1},{2,18},{18,2},{3,19},{19,3},{4,20},{20... | collective-permute-start | bytes 2752520 | tf_op jit(solution)/shard_map/ppermute | solution.py:66
  63.3 21.4 %collective-permute-start.9 = (bf16[64,7168]{1,0:T(8,128)(2,1)}, bf16[64,7168]{1,0:T(8,128)(2,1)}, u32[]{:S(2)}, u32[]{:S(2)}) collective-permute-start(bf16[64,7168]{1,0:T(8,128)(2,1)} %get-tuple-element.80.refs_3_), channel_id=1, source_target_pairs={{0,4},{1,5},{2,6},{3,7},{4,0},{5,1},{6,2},{7,3},{8,12},{9,13},{10,... | collective-permute-start | bytes 2752520 | tf_op jit(solution)/shard_map/ppermute | solution.py:62
  85.9 24.9 %collective-permute-start.12 = (bf16[64,8192]{1,0:T(8,128)(2,1)}, bf16[64,8192]{1,0:T(8,128)(2,1)}, u32[]{:S(2)}, u32[]{:S(2)}) collective-permute-start(bf16[64,8192]{1,0:T(8,128)(2,1)} %get-tuple-element.86.refs_6_), channel_id=1, source_target_pairs={{0,12},{1,13},{2,14},{3,15},{12,0},{13,1},{14,2},{15,3},{16,28},{1... | collective-permute-start | bytes 3145736 | tf_op jit(solution)/shard_map/ppermute | solution.py:268
  87.5 22.5 %collective-permute-start.13 = (bf16[64,7168]{1,0:T(8,128)(2,1)}, bf16[64,7168]{1,0:T(8,128)(2,1)}, u32[]{:S(2)}, u32[]{:S(2)}) collective-permute-start(bf16[64,7168]{1,0:T(8,128)(2,1)} %get-tuple-element.80.refs_3_), channel_id=1, source_target_pairs={{0,2},{1,3},{2,0},{3,1},{4,6},{5,7},{6,4},{7,5},{8,10},{9,11},{10,... | collective-permute-start | bytes 2752520 | tf_op jit(solution)/shard_map/ppermute | solution.py:62
  88.2 22.6 %collective-permute-start.14 = (bf16[64,7168]{1,0:T(8,128)(2,1)}, bf16[64,7168]{1,0:T(8,128)(2,1)}, u32[]{:S(2)}, u32[]{:S(2)}) collective-permute-start(bf16[64,7168]{1,0:T(8,128)(2,1)} %get-tuple-element.80.refs_3_), channel_id=1, source_target_pairs={{0,16},{16,0},{1,17},{17,1},{2,18},{18,2},{3,19},{19,3},{4,20},{20... | collective-permute-start | bytes 2752520 | tf_op jit(solution)/shard_map/ppermute | solution.py:66
  113.8 25.4 %collective-permute-start.17 = (bf16[64,8192]{1,0:T(8,128)(2,1)}, bf16[64,8192]{1,0:T(8,128)(2,1)}, u32[]{:S(2)}, u32[]{:S(2)}) collective-permute-start(bf16[64,8192]{1,0:T(8,128)(2,1)} %get-tuple-element.95.refs_3_), channel_id=1, source_target_pairs={{0,4},{1,5},{2,6},{3,7},{4,0},{5,1},{6,2},{7,3},{8,12},{9,13},{10,... | collective-permute-start | bytes 3145736 | tf_op jit(solution)/shard_map/ppermute | solution.py:62
  115.7 21.5 %collective-permute-start.15 = (bf16[64,7168]{1,0:T(8,128)(2,1)}, bf16[64,7168]{1,0:T(8,128)(2,1)}, u32[]{:S(2)}, u32[]{:S(2)}) collective-permute-start(bf16[64,7168]{1,0:T(8,128)(2,1)} %get-tuple-element.94.refs_2_), channel_id=1, source_target_pairs={{0,2},{1,3},{2,0},{3,1},{4,6},{5,7},{6,4},{7,5},{8,10},{9,11},{10,... | collective-permute-start | bytes 2752520 | tf_op jit(solution)/shard_map/ppermute | solution.py:62
  115.9 21.3 %collective-permute-start.16 = (bf16[64,7168]{1,0:T(8,128)(2,1)}, bf16[64,7168]{1,0:T(8,128)(2,1)}, u32[]{:S(2)}, u32[]{:S(2)}) collective-permute-start(bf16[64,7168]{1,0:T(8,128)(2,1)} %get-tuple-element.94.refs_2_), channel_id=1, source_target_pairs={{0,16},{16,0},{1,17},{17,1},{2,18},{18,2},{3,19},{19,3},{4,20},{20... | collective-permute-start | bytes 2752520 | tf_op jit(solution)/shard_map/ppermute | solution.py:66
  116.8 43.0 %collective-permute-start.18 = (bf16[64,8192]{1,0:T(8,128)(2,1)}, bf16[64,8192]{1,0:T(8,128)(2,1)}, u32[]{:S(2)}, u32[]{:S(2)}) collective-permute-start(bf16[64,8192]{1,0:T(8,128)(2,1)} %get-tuple-element.95.refs_3_), channel_id=1, source_target_pairs={{0,2},{1,3},{2,0},{3,1},{4,6},{5,7},{6,4},{7,5},{8,10},{9,11},{10,... | collective-permute-start | bytes 3145736 | tf_op jit(solution)/shard_map/ppermute | solution.py:62
  140.4 24.1 %collective-permute-start.20 = (bf16[64,8192]{1,0:T(8,128)(2,1)}, bf16[64,8192]{1,0:T(8,128)(2,1)}, u32[]{:S(2)}, u32[]{:S(2)}) collective-permute-start(bf16[64,8192]{1,0:T(8,128)(2,1)} %get-tuple-element.103), channel_id=1, source_target_pairs={{0,4},{1,5},{2,6},{3,7},{4,0},{5,1},{6,2},{7,3},{8,12},{9,13},{10,... | collective-permute-start | bytes 3145736 | tf_op jit(solution)/shard_map/ppermute | solution.py:62
  141.7 20.7 %collective-permute-start.19 = (bf16[64,7168]{1,0:T(8,128)(2,1)}, bf16[64,7168]{1,0:T(8,128)(2,1)}, u32[]{:S(2)}, u32[]{:S(2)}) collective-permute-start(bf16[64,7168]{1,0:T(8,128)(2,1)} %get-tuple-element.99.refs_0_), channel_id=1, source_target_pairs={{0,16},{16,0},{1,17},{17,1},{2,18},{18,2},{3,19},{19,3},{4,20},{20... | collective-permute-start | bytes 2752520 | tf_op jit(solution)/shard_map/ppermute | solution.py:66
  141.9 49.4 %collective-permute-start.22 = (bf16[64,8192]{1,0:T(8,128)(2,1)}, bf16[64,8192]{1,0:T(8,128)(2,1)}, u32[]{:S(2)}, u32[]{:S(2)}) collective-permute-start(bf16[64,8192]{1,0:T(8,128)(2,1)} %get-tuple-element.113.refs_2_), channel_id=1, source_target_pairs={{0,2},{1,3},{2,0},{3,1},{4,6},{5,7},{6,4},{7,5},{8,10},{9,11},{10,... | collective-permute-start | bytes 3145736 | tf_op jit(solution)/shard_map/ppermute | solution.py:62
  142.2 24.6 %copy-start.1 = (s32[4]{0:T(128)S(1)}, s32[4]{0:T(128)}, u32[]{:S(2)}) copy-start(s32[4]{0:T(128)} %param.11) | copy-start | bytes 52
  142.2 24.8 %copy-start.2 = (s32[4]{0:T(128)S(1)}, s32[4]{0:T(128)}, u32[]{:S(2)}) copy-start(s32[4]{0:T(128)} %param.12) | copy-start | bytes 52
  165.6 25.6 %collective-permute-start.24 = (bf16[64,8192]{1,0:T(8,128)(2,1)}, bf16[64,8192]{1,0:T(8,128)(2,1)}, u32[]{:S(2)}, u32[]{:S(2)}) collective-permute-start(bf16[64,8192]{1,0:T(8,128)(2,1)} %get-tuple-element.107.refs_1_), channel_id=1, source_target_pairs={{0,4},{1,5},{2,6},{3,7},{4,0},{5,1},{6,2},{7,3},{8,12},{9,13},{10,... | collective-permute-start | bytes 3145736 | tf_op jit(solution)/shard_map/ppermute | solution.py:62
  166.6 24.6 %collective-permute-start.23 = (bf16[64,7168]{1,0:T(8,128)(2,1)}, bf16[64,7168]{1,0:T(8,128)(2,1)}, u32[]{:S(2)}, u32[]{:S(2)}) collective-permute-start(bf16[64,7168]{1,0:T(8,128)(2,1)} %get-tuple-element.114), channel_id=1, source_target_pairs={{0,16},{16,0},{1,17},{17,1},{2,18},{18,2},{3,19},{19,3},{4,20},{20... | collective-permute-start | bytes 2752520 | tf_op jit(solution)/shard_map/ppermute | solution.py:66
  167.1 6.8 %collective-permute-start.21 = (s32[2,4]{1,0:T(2,128)S(1)}, s32[2,4]{1,0:T(2,128)S(1)}, u32[]{:S(2)}, u32[]{:S(2)}) collective-permute-start(s32[2,4]{1,0:T(2,128)S(1)} %pad_add_fusion), channel_id=1, source_target_pairs={{0,1},{1,0},{2,3},{3,2},{4,5},{5,4},{6,7},{7,6},{8,9},{9,8},{10,11... | collective-permute-start | bytes 104 | tf_op jit(solution)/shard_map/ppermute | solution.py:62
  171.6 32.4 %collective-permute-start.25 = (bf16[32,7168]{1,0:T(8,128)(2,1)}, bf16[32,7168]{1,0:T(8,128)(2,1)S(1)}, u32[]{:S(2)}, u32[]{:S(2)}) collective-permute-start(bf16[32,7168]{1,0:T(8,128)(2,1)} %slice.19), channel_id=1, source_target_pairs={{0,2},{1,3},{2,0},{3,1},{4,6},{5,7},{6,4},{7,5},{8,10},{9,11},{10,... | collective-permute-start | bytes 1376264 | tf_op jit(solution)/shard_map/ppermute | solution.py:62
  173.8 30.2 %collective-permute-start.26 = (bf16[32,7168]{1,0:T(8,128)(2,1)}, bf16[32,7168]{1,0:T(8,128)(2,1)}, u32[]{:S(2)}, u32[]{:S(2)}) collective-permute-start(bf16[32,7168]{1,0:T(8,128)(2,1)} %slice.20), channel_id=1, source_target_pairs={{0,16},{16,0},{1,17},{17,1},{2,18},{18,2},{3,19},{19,3},{4,20},{20... | collective-permute-start | bytes 1376264 | tf_op jit(solution)/shard_map/ppermute | solution.py:66
  204.0 0.8 copy-start
  218.5 2.4 %collective-permute-start.27 = (f32[4,512]{1,0:T(4,128)S(1)}, f32[4,512]{1,0:T(4,128)S(1)}, u32[]{:S(2)}, u32[]{:S(2)}) collective-permute-start(f32[4,512]{1,0:T(4,128)S(1)} %pad_maximum_fusion), channel_id=1, source_target_pairs={{0,1},{1,0},{2,3},{3,2},{4,5},{5,4},{6,7},{7,6},{8,9},{9,8},{10,11... | collective-permute-start | bytes 24584 | tf_op jit(solution)/shard_map/ppermute | solution.py:62

commit v13 on v12

--- a/solution.py
+++ b/solution.py
@@ -199,7 +199,7 @@
             score_into(out_ref, spans_ref, terms, rows)
 
 
-def proj(turn, tokens, rows, pieces, first, steps, last=None, spans=None, others=()):
+def proj(turn, tokens, rows, pieces, first, steps, last=None, spans=None, others=(), column=0):
     depth = pieces[0].shape[1]
     block = depth // steps
     held = sum(p.shape[0] for p in pieces)
@@ -210,7 +210,8 @@
         more_specs, more, scratch = [], (), []
         out_shape, out_spec = (2 * rows, held), whole
     else:
-        more_specs, more = [scalar, whole, whole], (spans, *others)
+        part = pl.BlockSpec((2 * rows, held), lambda k, turn, at: (0, column))
+        more_specs, more = [scalar, part, whole], (spans, *others)
         scratch = [pltpu.VMEM((2 * rows, held), jnp.float32)]
         out_shape = (spans.shape[1], held)
         out_spec = pl.BlockSpec(out_shape, lambda k, turn, at: (0, 0))
@@ -283,9 +284,6 @@
     tokens_here = hidden_acts.shape[0]
     steps = 4
 
-    def times_a(turn, k):
-        return proj(turn, acts, tokens_here, [a[i] for i in groups[k]], mine, steps)
-
     def times_c(turn, k, *score):
         return proj(turn, acts, tokens_here, [c[i] for i in groups[k]], 1 - mine, steps, *score)
 
@@ -325,11 +323,11 @@
     b_mid = middle(b_one)
     turn = pause(turn)
 
-    turn, (c["n"], a["o"], a["xn"], b_mid, b_two) = after(turn, [c["n"], a["o"], a["xn"], b_mid, b_two])
+    turn, (a["xn"], c["n"], a["o"], b_mid, b_two) = after(turn, [a["xn"], c["n"], a["o"], b_mid, b_two])
     a["xf"] = over_x(a["f"])
     c["f"] = swap_groups(a["f"])
     b_end = ends(b_two)
-    turn, a_first = times_a(turn, 0)
+    turn = pause(turn)
 
     turn, (b["f"], a["xf"], c["f"], a["o"], b_two) = after(
         turn, [b_end, a["xf"], c["f"], a["o"], b_two], (), (inside, b_mid)
@@ -345,23 +343,23 @@
     b["xf"] = over_x(b["f"])
     c["xn"] = swap_groups(a["xn"])
     b["n"] = near(b_two)
-    turn, a_second = times_a(turn, 1)
+    turn, a_all = proj(turn, acts, tokens_here, [a[i] for i in groups[0] + groups[1]], mine, steps)
 
     split = c["o"].shape[0] // 2
-    turn, (b["xf"], c["xn"], b["n"], a["xf"], a["xo"], c["o"], b["x"]) = after(
-        turn, [b["xf"], c["xn"], b["n"], a["xf"], a["xo"], c["o"], b["x"]]
+    turn, (b["xf"], c["xn"], b["n"], a["xo"], c["o"], b["x"]) = after(
+        turn, [b["xf"], c["xn"], b["n"], a["xo"], c["o"], b["x"]]
     )
     b["xo"] = over_x(b["o"])
     c["xf"] = swap_groups(a["xf"])
     b["xn"] = near(b["x"])
     c["top"] = over_x(c["o"][:split])
     c["low"] = swap_groups(a["xo"][split:])
-    turn, score_first = times_b(turn, 0, True, spans, (a_first, c_first))
+    turn, score_first = times_b(turn, 0, True, spans, (a_all, c_first), 0)
 
     turn, (b["xo"], c["xf"], b["xn"]) = after(turn, [b["xo"], c["xf"], b["xn"]])
     turn, b_second = times_b(turn, 1)
     groups = (groups[0], ("xn", "xf", "o", "top", "low"))
-    turn, score_second = times_c(turn, 1, False, spans, (a_second, b_second))
+    turn, score_second = times_c(turn, 1, False, spans, (a_all, b_second), 1)
     sums = [score_first, score_second]
 
     slots = bucket_ids.shape[0]

time: 223 us -> 223 us (level)
  Pallas kernels: 92.5 us -> 86.8 us
  waiting for transfers between devices: 85.7 us -> 90.6 us
    pallas_call x6 -> x5, Pallas kernels: 70.6 us -> 63.4 us  [proj(): pl.pallas_call(functools.partial(proj_kernel, len(pieces), last), out_sha...]
    ppermute x17, waiting for transfers between devices: 61.4 us -> 66.3 us  [flip(): return lax.ppermute(array, 'dp', [(i, i ^ code) for i in range(count)])]
    pallas_call x9 -> x10, Pallas kernels: 14.3 us -> 15.6 us  [after(): pl.pallas_call(functools.partial(after_kernel, count, merge is not None),...]
  transfers between devices with their start and end apart: 28 -> 28, of which waited for: 15 -> 16; matrix products, arithmetic and copies ran while one was open for 5% -> 5% of each run, Pallas kernels for 33% -> 30%
where the time goes in v13:
time: 223 us; the launch traced here: 221 us
  waiting for transfers between devices  90.6 us (41%)
  Pallas kernels  86.8 us (39%)
  starting transfers between devices  30.9 us (14%)
  local copies, waits for them, and re-layouts  9.24 us (4%)
  other arithmetic  2.92 us (1%)
    ppermute x17, waiting for transfers between devices, flip(): return lax.ppermute(array, 'dp', [(i, i ^ code) for i in range(count)])  66.3 us
    pallas_call x5, Pallas kernels, proj(): pl.pallas_call(functools.partial(proj_kernel, len(pieces), last), out_sha...  63.4 us
    ppermute x7, waiting for transfers between devices, swap_groups(): return lax.ppermute(array, 'groups', [(0, 1), (1, 0)])  21.3 us
    pallas_call x10, Pallas kernels, after(): pl.pallas_call(functools.partial(after_kernel, count, merge is not None),...  15.6 us
    ppermute x17, starting transfers between devices, flip(): return lax.ppermute(array, 'dp', [(i, i ^ code) for i in range(count)])  14.8 us
    ppermute x4, starting transfers between devices, lines(): return lax.ppermute(piece, 'dp', pairs)  11.5 us
    pallas_call x2, Pallas kernels, prepare(): pl.pallas_call(prepare_kernel, out_shape=[jax.ShapeDtypeStruct(x.shape, x...  7.75 us
    ppermute x7, starting transfers between devices, swap_groups(): return lax.ppermute(array, 'groups', [(0, 1), (1, 0)])  4.62 us
  transfers between devices with their start and end apart: 28, of which 16 were waited for; matrix products, arithmetic and copies ran while one was open for 5% of the time, Pallas kernels for 30%

profile of v13, /device:TPU:9, one launch (start us, length us, event | category | flops | bytes accessed | tf_op | source)
XLA Modules:
  0.0 221.4 jit_solution(8410563298530233001)
XLA Ops:
  0.7 2.2 constant_dynamic-slice_fusion.refs_0_
  2.9 6.5 %shard_map.73 = (bf16[64,7168]{1,0:T(8,128)(2,1)}, bf16[64,7168]{1,0:T(8,128)(2,1)}, bf16[64,8192]{1,0:T(8,128)(2,1)}, bf16[64,8192]{1,0:T(8,128)(2,1)}, s32[1]{0:T(128)}) custom-call(s32[1]{0:T(128)} %bitcast.works_ref, s32[1]{0:T(128)} %constant.26.clone.1.turn_ref, s32[1]{0:T(128)S(6)} %sub.16.first_ref, ...), custom_call_target="tpu_custom_call", output_to_operand_aliasing={{0}: (5, {})} | custom-call | flops 1 | bytes 1 | tf_op jit(solution)/shard_map/pallas_call | solution.py:142
  9.3 1.3 collective-permute-start.1
  10.8 4.3 %collective-permute-start.3 = (bf16[64,7168]{1,0:T(8,128)(2,1)}, bf16[64,7168]{1,0:T(8,128)(2,1)}, u32[]{:S(2)}, u32[]{:S(2)}) collective-permute-start(bf16[64,7168]{1,0:T(8,128)(2,1)} %get-tuple-element.68.refs_5_), channel_id=1, source_target_pairs={{4,8},{5,9},{6,10},{7,11},{8,4},{9,5},{10,6},{11,7},{20,24},{21,25... | collective-permute-start | bytes 2752520 | tf_op jit(solution)/shard_map/ppermute | solution.py:269
  15.1 1.3 shard_map.74
  16.4 10.6 %collective-permute-done.1.refs_1_ = bf16[64,7168]{1,0:T(8,128)(2,1)} collective-permute-done((bf16[64,7168]{1,0:T(8,128)(2,1)}, bf16[64,7168]{1,0:T(8,128)(2,1)}, u32[]{:S(2)}, u32[]{:S(2)}) %collective-permute-start.1) | collective-permute-done | bytes 917536 | tf_op jit(solution)/shard_map/ppermute | solution.py:62
  27.0 1.4 collective-permute-done.2.refs_2_
  28.4 3.0 %collective-permute-done.3.refs_3_ = bf16[64,7168]{1,0:T(8,128)(2,1)} collective-permute-done((bf16[64,7168]{1,0:T(8,128)(2,1)}, bf16[64,7168]{1,0:T(8,128)(2,1)}, u32[]{:S(2)}, u32[]{:S(2)}) %collective-permute-start.3) | collective-permute-done | bytes 917536 | tf_op jit(solution)/shard_map/ppermute | solution.py:269
  32.9 1.6 collective-permute-start.5
  36.9 16.7 %collective-permute-done.7.refs_5_ = bf16[64,7168]{1,0:T(8,128)(2,1)} collective-permute-done((bf16[64,7168]{1,0:T(8,128)(2,1)}, bf16[64,7168]{1,0:T(8,128)(2,1)}, u32[]{:S(2)}, u32[]{:S(2)}) %collective-permute-start.7) | collective-permute-done | bytes 917536 | tf_op jit(solution)/shard_map/ppermute | solution.py:66
  54.3 3.2 %shard_map.77 = (bf16[64,7168]{1,0:T(8,128)(2,1)}, bf16[64,8192]{1,0:T(8,128)(2,1)}, bf16[64,7168]{1,0:T(8,128)(2,1)}, bf16[64,8192]{1,0:T(8,128)(2,1)}, s32[1]{0:T(128)}) custom-call(s32[1]{0:T(128)} %shard_map.76.turn_ref, s32[1]{0:T(128)} %bitcast.4.refs_0_, ...), custom_call_target="tpu_custom_call", output_to_operand_aliasing={{0}: (4, {}), {1}: (5, {}), {2}: (6, {}), {3}: (7, {})} | custom-call | flops 1 | bytes 1 | tf_op jit(solution)/shard_map/pallas_call | solution.py:107
  57.5 3.9 %collective-permute-start.11 = (bf16[64,8192]{1,0:T(8,128)(2,1)}, bf16[64,8192]{1,0:T(8,128)(2,1)}, u32[]{:S(2)}, u32[]{:S(2)}) collective-permute-start(bf16[64,8192]{1,0:T(8,128)(2,1)} %get-tuple-element.78), channel_id=1, source_target_pairs={{4,8},{5,9},{6,10},{7,11},{8,4},{9,5},{10,6},{11,7},{20,24},{21,25... | collective-permute-start | bytes 3145736 | tf_op jit(solution)/shard_map/ppermute | solution.py:269
  64.4 17.9 %collective-permute-done.8.refs_0_ = bf16[64,7168]{1,0:T(8,128)(2,1)} collective-permute-done((bf16[64,7168]{1,0:T(8,128)(2,1)}, bf16[64,7168]{1,0:T(8,128)(2,1)}, u32[]{:S(2)}, u32[]{:S(2)}) %collective-permute-start.8) | collective-permute-done | bytes 917536 | tf_op jit(solution)/shard_map/ppermute | solution.py:62
  85.7 1.7 collective-permute-start.12
  89.4 20.6 %collective-permute-done.13.refs_3_ = bf16[64,7168]{1,0:T(8,128)(2,1)} collective-permute-done((bf16[64,7168]{1,0:T(8,128)(2,1)}, bf16[64,7168]{1,0:T(8,128)(2,1)}, u32[]{:S(2)}, u32[]{:S(2)}) %collective-permute-start.13) | collective-permute-done | bytes 917536 | tf_op jit(solution)/shard_map/ppermute | solution.py:62
  110.7 3.2 %shard_map.81 = (bf16[64,8192]{1,0:T(8,128)(2,1)}, bf16[64,7168]{1,0:T(8,128)(2,1)}, bf16[64,7168]{1,0:T(8,128)(2,1)}, bf16[64,7168]{1,0:T(8,128)(2,1)}, bf16[64,8192]{1,0:T(8,128)(2,1)}, /*index=5*/s32[1]{0:T(128)}) custom-call(s32[1]{0:T(128)} %shard_map.80.turn_ref, ...), custom_call_target="tpu_custom_call", output_to_operand_aliasing={{0}: (3, {}), {1}: (4, {}), {2}: (5, {}), {3}: (6, {}), {4}... | custom-call | flops 1 | bytes 1 | tf_op jit(solution)/shard_map/pallas_call | solution.py:107
  113.9 1.5 collective-permute-start.17
  117.6 10.8 %shard_map.82 = (f32[1024,256]{1,0:T(8,128)}, s32[1]{0:T(128)}) custom-call(s32[1]{0:T(128)} %get-tuple-element.84.turn_ref, s32[3]{0:T(128)} %concatenate.24.at_ref, bf16[512,14336]{1,0:T(8,128)(2,1)} %own_ref.9, bf16[512,14336]{1,0:T(8,128)(2,1)} %collective-permute-done.refs_0_.other_ref, bf16[64,7168]{1,0:T(8,128)(2,1)} %get-tuple-element.85.refs_0_, ...), custom_call_target="tpu_custom_call" | custom-call | flops 1 | bytes 1 | tf_op jit(solution)/shard_map/pallas_call | solution.py:218
  128.5 8.5 %collective-permute-done.15.refs_0_ = bf16[64,7168]{1,0:T(8,128)(2,1)} collective-permute-done((bf16[64,7168]{1,0:T(8,128)(2,1)}, bf16[64,7168]{1,0:T(8,128)(2,1)}, u32[]{:S(2)}, u32[]{:S(2)}) %collective-permute-start.15) | collective-permute-done | bytes 917536 | tf_op jit(solution)/shard_map/ppermute | solution.py:62
  137.2 1.4 collective-permute-done.17.refs_2_
  139.8 1.5 collective-permute-start.20
  142.6 14.4 %shard_map.84 = (f32[1024,512]{1,0:T(8,128)}, s32[1]{0:T(128)}) custom-call(s32[1]{0:T(128)} %get-tuple-element.94.turn_ref, s32[3]{0:T(128)} %concatenate.25.at_ref, bf16[512,14336]{1,0:T(8,128)(2,1)} %own_ref.9, bf16[512,14336]{1,0:T(8,128)(2,1)} %collective-permute-done.refs_0_.other_ref, bf16[64,7168]{1,0:T(8,128)(2,1)} %get-tuple-element.72.refs_0_, ...), custom_call_target="tpu_custom_call" | custom-call | flops 1 | bytes 1 | tf_op jit(solution)/shard_map/pallas_call | solution.py:218
  157.1 2.4 %collective-permute-done.18.refs_0_ = bf16[64,8192]{1,0:T(8,128)(2,1)} collective-permute-done((bf16[64,8192]{1,0:T(8,128)(2,1)}, bf16[64,8192]{1,0:T(8,128)(2,1)}, u32[]{:S(2)}, u32[]{:S(2)}) %collective-permute-start.18) | collective-permute-done | bytes 1048608 | tf_op jit(solution)/shard_map/ppermute | solution.py:62
  159.4 2.5 %collective-permute-done.19.refs_1_ = bf16[64,7168]{1,0:T(8,128)(2,1)} collective-permute-done((bf16[64,7168]{1,0:T(8,128)(2,1)}, bf16[64,7168]{1,0:T(8,128)(2,1)}, u32[]{:S(2)}, u32[]{:S(2)}) %collective-permute-start.19) | collective-permute-done | bytes 917536 | tf_op jit(solution)/shard_map/ppermute | solution.py:66
  162.0 1.6 collective-permute-done.20.refs_2_
  164.7 1.5 collective-permute-start.24
  166.7 2.8 %collective-permute-start.21 = (s32[2,4]{1,0:T(2,128)S(1)}, s32[2,4]{1,0:T(2,128)S(1)}, u32[]{:S(2)}, u32[]{:S(2)}) collective-permute-start(s32[2,4]{1,0:T(2,128)S(1)} %pad_add_fusion), channel_id=1, source_target_pairs={{0,1},{1,0},{2,3},{3,2},{4,5},{5,4},{6,7},{7,6},{8,9},{9,8},{10,11... | collective-permute-start | bytes 104 | tf_op jit(solution)/shard_map/ppermute | solution.py:62
  169.5 1.8 slice.19
  171.9 1.8 slice.20
  177.5 13.7 %shard_map.86 = (f32[8,256]{1,0:T(8,128)}, s32[1]{0:T(128)}) custom-call(s32[1]{0:T(128)} %get-tuple-element.102.turn_ref, s32[3]{0:T(128)} %broadcast_8_at_ref.2.at_ref, bf16[512,8192]{1,0:T(8,128)(2,1)} %own_ref.8, bf16[512,8192]{1,0:T(8,128)(2,1)} %collective-permute-done.4.refs_2_.other_ref, bf16[64,8192]{1,0:T(8,128)(2,1)} %bitcast.22, ...), custom_call_target="tpu_custom_call" | custom-call | flops 1 | bytes 1 | tf_op jit(solution)/shard_map/pallas_call | solution.py:218
  192.5 11.6 %shard_map.88 = (f32[1024,256]{1,0:T(8,128)}, s32[1]{0:T(128)}) custom-call(s32[1]{0:T(128)} %get-tuple-element.110.turn_ref, s32[3]{0:T(128)} %broadcast_8_at_ref.2.at_ref, bf16[512,8192]{1,0:T(8,128)(2,1)} %own_ref.8, bf16[512,8192]{1,0:T(8,128)(2,1)} %collective-permute-done.4.refs_2_.other_ref, bf16[64,8192]{1,0:T(8,128)(2,1)} %get-tuple-element.111.refs_0_, ...), custom_call_target="tpu_custom_call" | custom-call | flops 1 | bytes 1 | tf_op jit(solution)/shard_map/pallas_call | solution.py:218
  204.9 12.9 %shard_map.89 = (f32[8,256]{1,0:T(8,128)}, s32[1]{0:T(128)}) custom-call(s32[1]{0:T(128)} %get-tuple-element.114.turn_ref, s32[3]{0:T(128)} %concatenate.24.at_ref, bf16[512,14336]{1,0:T(8,128)(2,1)} %own_ref.9, bf16[512,14336]{1,0:T(8,128)(2,1)} %collective-permute-done.refs_0_.other_ref, bf16[64,7168]{1,0:T(8,128)(2,1)} %get-tuple-element.115.refs_0_, ...), custom_call_target="tpu_custom_call" | custom-call | flops 1 | bytes 1 | tf_op jit(solution)/shard_map/pallas_call | solution.py:218
  (67 shorter events, 31.1 us)
Async XLA Ops:
  0.0 31.4 %collective-permute-start = (bf16[512,14336]{1,0:T(8,128)(2,1)}, bf16[512,14336]{1,0:T(8,128)(2,1)}, u32[]{:S(2)}, u32[]{:S(2)}) collective-permute-start(bf16[512,14336]{1,0:T(8,128)(2,1)} %own_ref.9), channel_id=1, source_target_pairs={{0,1},{1,0},{2,3},{3,2},{4,5},{5,4},{6,7},{7,6},{8,9},{9,8},{10,11... | collective-permute-start | bytes 44040200 | tf_op jit(solution)/shard_map/ppermute | solution.py:62
  0.7 36.2 %collective-permute-start.4 = (bf16[512,8192]{1,0:T(8,128)(2,1)}, bf16[512,8192]{1,0:T(8,128)(2,1)}, u32[]{:S(2)}, u32[]{:S(2)}) collective-permute-start(bf16[512,8192]{1,0:T(8,128)(2,1)} %own_ref.8), channel_id=1, source_target_pairs={{0,1},{1,0},{2,3},{3,2},{4,5},{5,4},{6,7},{7,6},{8,9},{9,8},{10,11... | collective-permute-start | bytes 25165832 | tf_op jit(solution)/shard_map/ppermute | solution.py:62
  9.3 17.6 %collective-permute-start.1 = (bf16[64,7168]{1,0:T(8,128)(2,1)}, bf16[64,7168]{1,0:T(8,128)(2,1)}, u32[]{:S(2)}, u32[]{:S(2)}) collective-permute-start(bf16[64,7168]{1,0:T(8,128)(2,1)} %get-tuple-element.68.refs_5_), channel_id=1, source_target_pairs={{0,2},{1,3},{2,0},{3,1},{4,6},{5,7},{6,4},{7,5},{8,10},{9,11},{10,... | collective-permute-start | bytes 2752520 | tf_op jit(solution)/shard_map/ppermute | solution.py:62
  10.6 17.7 %collective-permute-start.2 = (bf16[64,7168]{1,0:T(8,128)(2,1)}, bf16[64,7168]{1,0:T(8,128)(2,1)}, u32[]{:S(2)}, u32[]{:S(2)}) collective-permute-start(bf16[64,7168]{1,0:T(8,128)(2,1)} %get-tuple-element.68.refs_5_), channel_id=1, source_target_pairs={{0,4},{1,5},{2,6},{3,7},{4,0},{5,1},{6,2},{7,3},{8,12},{9,13},{10,... | collective-permute-start | bytes 2752520 | tf_op jit(solution)/shard_map/ppermute | solution.py:62
  10.8 20.6 %collective-permute-start.3 = (bf16[64,7168]{1,0:T(8,128)(2,1)}, bf16[64,7168]{1,0:T(8,128)(2,1)}, u32[]{:S(2)}, u32[]{:S(2)}) collective-permute-start(bf16[64,7168]{1,0:T(8,128)(2,1)} %get-tuple-element.68.refs_5_), channel_id=1, source_target_pairs={{4,8},{5,9},{6,10},{7,11},{8,4},{9,5},{10,6},{11,7},{20,24},{21,25... | collective-permute-start | bytes 2752520 | tf_op jit(solution)/shard_map/ppermute | solution.py:269
  32.6 21.7 %collective-permute-start.6 = (bf16[64,8192]{1,0:T(8,128)(2,1)}, bf16[64,8192]{1,0:T(8,128)(2,1)}, u32[]{:S(2)}, u32[]{:S(2)}) collective-permute-start(bf16[64,8192]{1,0:T(8,128)(2,1)} %get-tuple-element.73.refs_6_), channel_id=1, source_target_pairs={{0,2},{1,3},{2,0},{3,1},{4,6},{5,7},{6,4},{7,5},{8,10},{9,11},{10,... | collective-permute-start | bytes 3145736 | tf_op jit(solution)/shard_map/ppermute | solution.py:62
  32.9 4.0 %collective-permute-start.5 = (bf16[64,7168]{1,0:T(8,128)(2,1)}, bf16[64,7168]{1,0:T(8,128)(2,1)}, u32[]{:S(2)}, u32[]{:S(2)}) collective-permute-start(bf16[64,7168]{1,0:T(8,128)(2,1)} %get-tuple-element.72.refs_0_), channel_id=1, source_target_pairs={{0,12},{1,13},{2,14},{3,15},{12,0},{13,1},{14,2},{15,3},{16,28},{1... | collective-permute-start | bytes 2752520 | tf_op jit(solution)/shard_map/ppermute | solution.py:269
  34.5 19.1 %collective-permute-start.7 = (bf16[64,7168]{1,0:T(8,128)(2,1)}, bf16[64,7168]{1,0:T(8,128)(2,1)}, u32[]{:S(2)}, u32[]{:S(2)}) collective-permute-start(bf16[64,7168]{1,0:T(8,128)(2,1)} %get-tuple-element.74.refs_1_), channel_id=1, source_target_pairs={{0,16},{16,0},{1,17},{17,1},{2,18},{18,2},{3,19},{19,3},{4,20},{20... | collective-permute-start | bytes 2752520 | tf_op jit(solution)/shard_map/ppermute | solution.py:66
  57.5 27.1 %collective-permute-start.11 = (bf16[64,8192]{1,0:T(8,128)(2,1)}, bf16[64,8192]{1,0:T(8,128)(2,1)}, u32[]{:S(2)}, u32[]{:S(2)}) collective-permute-start(bf16[64,8192]{1,0:T(8,128)(2,1)} %get-tuple-element.78), channel_id=1, source_target_pairs={{4,8},{5,9},{6,10},{7,11},{8,4},{9,5},{10,6},{11,7},{20,24},{21,25... | collective-permute-start | bytes 3145736 | tf_op jit(solution)/shard_map/ppermute | solution.py:269
  61.4 20.8 %collective-permute-start.8 = (bf16[64,7168]{1,0:T(8,128)(2,1)}, bf16[64,7168]{1,0:T(8,128)(2,1)}, u32[]{:S(2)}, u32[]{:S(2)}) collective-permute-start(bf16[64,7168]{1,0:T(8,128)(2,1)} %get-tuple-element.76.refs_2_), channel_id=1, source_target_pairs={{0,2},{1,3},{2,0},{3,1},{4,6},{5,7},{6,4},{7,5},{8,10},{9,11},{10,... | collective-permute-start | bytes 2752520 | tf_op jit(solution)/shard_map/ppermute | solution.py:62
  62.0 21.3 %collective-permute-start.9 = (bf16[64,7168]{1,0:T(8,128)(2,1)}, bf16[64,7168]{1,0:T(8,128)(2,1)}, u32[]{:S(2)}, u32[]{:S(2)}) collective-permute-start(bf16[64,7168]{1,0:T(8,128)(2,1)} %get-tuple-element.76.refs_2_), channel_id=1, source_target_pairs={{0,16},{16,0},{1,17},{17,1},{2,18},{18,2},{3,19},{19,3},{4,20},{20... | collective-permute-start | bytes 2752520 | tf_op jit(solution)/shard_map/ppermute | solution.py:66
  63.2 21.3 %collective-permute-start.10 = (bf16[64,7168]{1,0:T(8,128)(2,1)}, bf16[64,7168]{1,0:T(8,128)(2,1)}, u32[]{:S(2)}, u32[]{:S(2)}) collective-permute-start(bf16[64,7168]{1,0:T(8,128)(2,1)} %get-tuple-element.77.refs_3_), channel_id=1, source_target_pairs={{0,4},{1,5},{2,6},{3,7},{4,0},{5,1},{6,2},{7,3},{8,12},{9,13},{10,... | collective-permute-start | bytes 2752520 | tf_op jit(solution)/shard_map/ppermute | solution.py:62
  85.7 25.0 %collective-permute-start.12 = (bf16[64,8192]{1,0:T(8,128)(2,1)}, bf16[64,8192]{1,0:T(8,128)(2,1)}, u32[]{:S(2)}, u32[]{:S(2)}) collective-permute-start(bf16[64,8192]{1,0:T(8,128)(2,1)} %get-tuple-element.82.refs_6_), channel_id=1, source_target_pairs={{0,12},{1,13},{2,14},{3,15},{12,0},{13,1},{14,2},{15,3},{16,28},{1... | collective-permute-start | bytes 3145736 | tf_op jit(solution)/shard_map/ppermute | solution.py:269
  87.4 22.6 %collective-permute-start.13 = (bf16[64,7168]{1,0:T(8,128)(2,1)}, bf16[64,7168]{1,0:T(8,128)(2,1)}, u32[]{:S(2)}, u32[]{:S(2)}) collective-permute-start(bf16[64,7168]{1,0:T(8,128)(2,1)} %get-tuple-element.77.refs_3_), channel_id=1, source_target_pairs={{0,2},{1,3},{2,0},{3,1},{4,6},{5,7},{6,4},{7,5},{8,10},{9,11},{10,... | collective-permute-start | bytes 2752520 | tf_op jit(solution)/shard_map/ppermute | solution.py:62
  88.0 22.7 %collective-permute-start.14 = (bf16[64,7168]{1,0:T(8,128)(2,1)}, bf16[64,7168]{1,0:T(8,128)(2,1)}, u32[]{:S(2)}, u32[]{:S(2)}) collective-permute-start(bf16[64,7168]{1,0:T(8,128)(2,1)} %get-tuple-element.77.refs_3_), channel_id=1, source_target_pairs={{0,16},{16,0},{1,17},{17,1},{2,18},{18,2},{3,19},{19,3},{4,20},{20... | collective-permute-start | bytes 2752520 | tf_op jit(solution)/shard_map/ppermute | solution.py:66
  113.9 24.7 %collective-permute-start.17 = (bf16[64,8192]{1,0:T(8,128)(2,1)}, bf16[64,8192]{1,0:T(8,128)(2,1)}, u32[]{:S(2)}, u32[]{:S(2)}) collective-permute-start(bf16[64,8192]{1,0:T(8,128)(2,1)} %get-tuple-element.91.refs_3_), channel_id=1, source_target_pairs={{0,4},{1,5},{2,6},{3,7},{4,0},{5,1},{6,2},{7,3},{8,12},{9,13},{10,... | collective-permute-start | bytes 3145736 | tf_op jit(solution)/shard_map/ppermute | solution.py:62
  115.4 21.5 %collective-permute-start.15 = (bf16[64,7168]{1,0:T(8,128)(2,1)}, bf16[64,7168]{1,0:T(8,128)(2,1)}, u32[]{:S(2)}, u32[]{:S(2)}) collective-permute-start(bf16[64,7168]{1,0:T(8,128)(2,1)} %get-tuple-element.90.refs_6_), channel_id=1, source_target_pairs={{0,2},{1,3},{2,0},{3,1},{4,6},{5,7},{6,4},{7,5},{8,10},{9,11},{10,... | collective-permute-start | bytes 2752520 | tf_op jit(solution)/shard_map/ppermute | solution.py:62
  115.8 21.4 %collective-permute-start.16 = (bf16[64,7168]{1,0:T(8,128)(2,1)}, bf16[64,7168]{1,0:T(8,128)(2,1)}, u32[]{:S(2)}, u32[]{:S(2)}) collective-permute-start(bf16[64,7168]{1,0:T(8,128)(2,1)} %get-tuple-element.90.refs_6_), channel_id=1, source_target_pairs={{0,16},{16,0},{1,17},{17,1},{2,18},{18,2},{3,19},{19,3},{4,20},{20... | collective-permute-start | bytes 2752520 | tf_op jit(solution)/shard_map/ppermute | solution.py:66
  116.5 42.9 %collective-permute-start.18 = (bf16[64,8192]{1,0:T(8,128)(2,1)}, bf16[64,8192]{1,0:T(8,128)(2,1)}, u32[]{:S(2)}, u32[]{:S(2)}) collective-permute-start(bf16[64,8192]{1,0:T(8,128)(2,1)} %get-tuple-element.91.refs_3_), channel_id=1, source_target_pairs={{0,2},{1,3},{2,0},{3,1},{4,6},{5,7},{6,4},{7,5},{8,10},{9,11},{10,... | collective-permute-start | bytes 3145736 | tf_op jit(solution)/shard_map/ppermute | solution.py:62
  139.8 23.8 %collective-permute-start.20 = (bf16[64,8192]{1,0:T(8,128)(2,1)}, bf16[64,8192]{1,0:T(8,128)(2,1)}, u32[]{:S(2)}, u32[]{:S(2)}) collective-permute-start(bf16[64,8192]{1,0:T(8,128)(2,1)} %get-tuple-element.99), channel_id=1, source_target_pairs={{0,4},{1,5},{2,6},{3,7},{4,0},{5,1},{6,2},{7,3},{8,12},{9,13},{10,... | collective-permute-start | bytes 3145736 | tf_op jit(solution)/shard_map/ppermute | solution.py:62
  141.3 20.7 %collective-permute-start.19 = (bf16[64,7168]{1,0:T(8,128)(2,1)}, bf16[64,7168]{1,0:T(8,128)(2,1)}, u32[]{:S(2)}, u32[]{:S(2)}) collective-permute-start(bf16[64,7168]{1,0:T(8,128)(2,1)} %get-tuple-element.95.refs_4_), channel_id=1, source_target_pairs={{0,16},{16,0},{1,17},{17,1},{2,18},{18,2},{3,19},{19,3},{4,20},{20... | collective-permute-start | bytes 2752520 | tf_op jit(solution)/shard_map/ppermute | solution.py:66
  142.1 49.2 %collective-permute-start.22 = (bf16[64,8192]{1,0:T(8,128)(2,1)}, bf16[64,8192]{1,0:T(8,128)(2,1)}, u32[]{:S(2)}, u32[]{:S(2)}) collective-permute-start(bf16[64,8192]{1,0:T(8,128)(2,1)} %get-tuple-element.109.refs_2_), channel_id=1, source_target_pairs={{0,2},{1,3},{2,0},{3,1},{4,6},{5,7},{6,4},{7,5},{8,10},{9,11},{10,... | collective-permute-start | bytes 3145736 | tf_op jit(solution)/shard_map/ppermute | solution.py:62
  142.6 23.9 %copy-start.1 = (s32[4]{0:T(128)S(1)}, s32[4]{0:T(128)}, u32[]{:S(2)}) copy-start(s32[4]{0:T(128)} %param.11) | copy-start | bytes 52
  142.6 24.1 %copy-start.2 = (s32[4]{0:T(128)S(1)}, s32[4]{0:T(128)}, u32[]{:S(2)}) copy-start(s32[4]{0:T(128)} %param.12) | copy-start | bytes 52
  164.7 26.6 %collective-permute-start.24 = (bf16[64,8192]{1,0:T(8,128)(2,1)}, bf16[64,8192]{1,0:T(8,128)(2,1)}, u32[]{:S(2)}, u32[]{:S(2)}) collective-permute-start(bf16[64,8192]{1,0:T(8,128)(2,1)} %get-tuple-element.103.refs_1_), channel_id=1, source_target_pairs={{0,4},{1,5},{2,6},{3,7},{4,0},{5,1},{6,2},{7,3},{8,12},{9,13},{10,... | collective-permute-start | bytes 3145736 | tf_op jit(solution)/shard_map/ppermute | solution.py:62
  166.3 25.0 %collective-permute-start.23 = (bf16[64,7168]{1,0:T(8,128)(2,1)}, bf16[64,7168]{1,0:T(8,128)(2,1)}, u32[]{:S(2)}, u32[]{:S(2)}) collective-permute-start(bf16[64,7168]{1,0:T(8,128)(2,1)} %get-tuple-element.96.refs_5_), channel_id=1, source_target_pairs={{0,16},{16,0},{1,17},{17,1},{2,18},{18,2},{3,19},{19,3},{4,20},{20... | collective-permute-start | bytes 2752520 | tf_op jit(solution)/shard_map/ppermute | solution.py:66
  166.7 7.0 %collective-permute-start.21 = (s32[2,4]{1,0:T(2,128)S(1)}, s32[2,4]{1,0:T(2,128)S(1)}, u32[]{:S(2)}, u32[]{:S(2)}) collective-permute-start(s32[2,4]{1,0:T(2,128)S(1)} %pad_add_fusion), channel_id=1, source_target_pairs={{0,1},{1,0},{2,3},{3,2},{4,5},{5,4},{6,7},{7,6},{8,9},{9,8},{10,11... | collective-permute-start | bytes 104 | tf_op jit(solution)/shard_map/ppermute | solution.py:62
  171.3 32.8 %collective-permute-start.25 = (bf16[32,7168]{1,0:T(8,128)(2,1)}, bf16[32,7168]{1,0:T(8,128)(2,1)S(1)}, u32[]{:S(2)}, u32[]{:S(2)}) collective-permute-start(bf16[32,7168]{1,0:T(8,128)(2,1)} %slice.19), channel_id=1, source_target_pairs={{0,2},{1,3},{2,0},{3,1},{4,6},{5,7},{6,4},{7,5},{8,10},{9,11},{10,... | collective-permute-start | bytes 1376264 | tf_op jit(solution)/shard_map/ppermute | solution.py:62
  173.7 30.4 %collective-permute-start.26 = (bf16[32,7168]{1,0:T(8,128)(2,1)}, bf16[32,7168]{1,0:T(8,128)(2,1)}, u32[]{:S(2)}, u32[]{:S(2)}) collective-permute-start(bf16[32,7168]{1,0:T(8,128)(2,1)} %slice.20), channel_id=1, source_target_pairs={{0,16},{16,0},{1,17},{17,1},{2,18},{18,2},{3,19},{19,3},{4,20},{20... | collective-permute-start | bytes 1376264 | tf_op jit(solution)/shard_map/ppermute | solution.py:66
  204.1 0.8 copy-start
  218.5 2.1 collective-permute-start.27

commit v14 on v9

--- a/solution.py
+++ b/solution.py
@@ -55,7 +55,7 @@
 
 CORE, COLUMN, NEAR, ACROSS, OPPOSITE = 1, 2, 4, 12, 8
 LITTLE = pl.CostEstimate(flops=1, bytes_accessed=1, transcendentals=0)
-VMEM_LIMIT = 63 * 1024 * 1024
+VMEM_LIMIT = 127 * 512 * 1024
 
 
 def flip(array, code, count):
@@ -338,20 +338,19 @@
     turn, (b["n"], a["xo"], c["f"], a["o"], a["xn"]) = after(
         turn, [b["n"], a["xo"], c["f"], a["o"], a["xn"]], inside
     )
-    b_in = middle(b["n"])
     c["o"] = swap_groups(a["o"])
     c["xn"] = swap_groups(a["xn"])
     turn, c_first = times_c(turn, 0)
 
     turn, (b["f"], a["xf"], c["o"], a["xo"]) = after(turn, [b["f"], a["xf"], c["o"], a["xo"]], inside)
-    b_out = outward(b["f"])
+    b["o"] = near(b["f"])
     b["xf"] = over_x(b["f"])
     c["xo"] = swap_groups(a["xo"])
     turn, score_first = times_b(turn, 0, True, spans, (a_first, c_first))
 
     split = c["f"].shape[0] // 2
     turn, (b["o"], b["xf"], c["xn"], b_over, a["xf"], c["f"]) = after(
-        turn, [b_out, b["xf"], c["xn"], b["x"], a["xf"], c["f"]], inside, b_in
+        turn, [b["o"], b["xf"], c["xn"], b["x"], a["xf"], c["f"]], inside
     )
     b["xo"] = over_x(b["o"])
     b["xn"] = near(b_over)

time: 222 us -> 218 us (0.982)
  waiting for transfers between devices: 77.1 us -> 70.5 us
  other arithmetic: 1 us -> 3.55 us
    ppermute x16 -> x17, starting transfers between devices: 9.86 us -> 13.8 us  [flip(): return lax.ppermute(array, 'dp', [(i, i ^ code) for i in range(count)])]
    ppermute x16 -> x17, waiting for transfers between devices: 44.7 us -> 41.1 us  [flip(): return lax.ppermute(array, 'dp', [(i, i ^ code) for i in range(count)])]
    ppermute x6 -> x4, starting transfers between devices: 16.5 us -> 13.7 us  [lines(): lax.ppermute(array, 'dp', [(a * 4 + rest, b * 4 + rest) for a, b in pairs...]
    ppermute x6 -> x4, waiting for transfers between devices: 17.4 us -> 16.5 us  [lines(): lax.ppermute(array, 'dp', [(a * 4 + rest, b * 4 + rest) for a, b in pairs...]
  transfers between devices with their start and end apart: 29 -> 28, of which waited for: 19 -> 19; matrix products, arithmetic and copies ran while one was open for 4% -> 6% of each run, Pallas kernels for 35% -> 35%
where the time goes in v14:
time: 218 us; the launch traced here: 215 us
  Pallas kernels  94.2 us (43%)
  waiting for transfers between devices  70.5 us (32%)
  starting transfers between devices  34.3 us (16%)
  local copies, waits for them, and re-layouts  10.7 us (5%)
  other arithmetic  3.55 us (2%)
    pallas_call x6, Pallas kernels, proj(): pl.pallas_call(functools.partial(proj_kernel, len(pieces), last), out_sha...  70.9 us
    ppermute x17, waiting for transfers between devices, flip(): return lax.ppermute(array, 'dp', [(i, i ^ code) for i in range(count)])  41.1 us
    ppermute x4, waiting for transfers between devices, lines(): lax.ppermute(array, 'dp', [(a * 4 + rest, b * 4 + rest) for a, b in pairs...  16.5 us
    pallas_call x10, Pallas kernels, after(): pl.pallas_call(functools.partial(after_kernel, count, merge is not None),...  15.5 us
    ppermute x17, starting transfers between devices, flip(): return lax.ppermute(array, 'dp', [(i, i ^ code) for i in range(count)])  13.8 us
    ppermute x4, starting transfers between devices, lines(): lax.ppermute(array, 'dp', [(a * 4 + rest, b * 4 + rest) for a, b in pairs...  13.7 us
    ppermute x7, waiting for transfers between devices, swap_groups(): return lax.ppermute(array, 'groups', [(0, 1), (1, 0)])  13 us
    pallas_call x2, Pallas kernels, prepare(): pl.pallas_call(prepare_kernel, out_shape=[jax.ShapeDtypeStruct(x.shape, x...  7.75 us
  transfers between devices with their start and end apart: 28, of which 19 were waited for; matrix products, arithmetic and copies ran while one was open for 6% of the time, Pallas kernels for 35%

profile of v14, /device:TPU:9, one launch (start us, length us, event | category | flops | bytes accessed | tf_op | source)
XLA Modules:
  0.0 215.0 jit_solution(12166544263699349658)
XLA Ops:
  0.7 2.2 %constant_dynamic-slice_fusion.refs_0_ = bf16[64,7168]{1,0:T(8,128)(2,1)} fusion(bf16[64,14336]{1,0:T(8,128)(2,1)} %bitcast.17, s32[]{:T(128)S(6)} %select_n.20), kind=kLoop, calls=%fused_computation.19 | loop fusion | bytes 1835012 | tf_op jit(solution)/shard_map/dynamic_slice | solution.py:266
  2.9 6.4 %shard_map.73 = (bf16[64,7168]{1,0:T(8,128)(2,1)}, bf16[64,7168]{1,0:T(8,128)(2,1)}, bf16[64,8192]{1,0:T(8,128)(2,1)}, bf16[64,8192]{1,0:T(8,128)(2,1)}, s32[1]{0:T(128)}) custom-call(s32[1]{0:T(128)} %bitcast.1.works_ref, s32[1]{0:T(128)} %constant.24.clone.1.turn_ref, s32[1]{0:T(128)S(6)} %sub.17.first_ref, ...), custom_call_target="tpu_custom_call", output_to_operand_aliasing={{0}: (5, {})} | custom-call | flops 1 | bytes 1 | tf_op jit(solution)/shard_map/pallas_call | solution.py:141
  9.3 3.2 %collective-permute-start.1 = (bf16[64,7168]{1,0:T(8,128)(2,1)}, bf16[64,7168]{1,0:T(8,128)(2,1)}, u32[]{:S(2)}, u32[]{:S(2)}) collective-permute-start(bf16[64,7168]{1,0:T(8,128)(2,1)} %get-tuple-element.68.refs_0_), channel_id=1, source_target_pairs={{4,8},{5,9},{6,10},{7,11},{8,4},{9,5},{10,6},{11,7},{20,24},{21,25... | collective-permute-start | bytes 2752520 | tf_op jit(solution)/shard_map/ppermute | solution.py:158
  15.2 13.8 %collective-permute-done.1.refs_1_ = bf16[64,7168]{1,0:T(8,128)(2,1)} collective-permute-done((bf16[64,7168]{1,0:T(8,128)(2,1)}, bf16[64,7168]{1,0:T(8,128)(2,1)}, u32[]{:S(2)}, u32[]{:S(2)}) %collective-permute-start.1) | collective-permute-done | bytes 917536 | tf_op jit(solution)/shard_map/ppermute | solution.py:158
  30.7 2.8 %collective-permute-done.3.refs_3_ = bf16[64,7168]{1,0:T(8,128)(2,1)} collective-permute-done((bf16[64,7168]{1,0:T(8,128)(2,1)}, bf16[64,7168]{1,0:T(8,128)(2,1)}, u32[]{:S(2)}, u32[]{:S(2)}) %collective-permute-start.3) | collective-permute-done | bytes 917536 | tf_op jit(solution)/shard_map/ppermute | solution.py:62
  34.7 6.2 %collective-permute-start.5 = (bf16[64,7168]{1,0:T(8,128)(2,1)}, bf16[64,7168]{1,0:T(8,128)(2,1)}, u32[]{:S(2)}, u32[]{:S(2)}) collective-permute-start(bf16[64,7168]{1,0:T(8,128)(2,1)} %get-tuple-element.70.refs_0_), channel_id=1, source_target_pairs={{4,0},{5,1},{6,2},{7,3},{8,12},{9,13},{10,14},{11,15},{20,16},{21,... | collective-permute-start | bytes 2752520 | tf_op jit(solution)/shard_map/ppermute | solution.py:158
  40.9 2.1 collective-permute-start.7
  45.4 7.5 %collective-permute-done.6.refs_2_ = bf16[64,8192]{1,0:T(8,128)(2,1)} collective-permute-done((bf16[64,8192]{1,0:T(8,128)(2,1)}, bf16[64,8192]{1,0:T(8,128)(2,1)}, u32[]{:S(2)}, u32[]{:S(2)}) %collective-permute-start.6) | collective-permute-done | bytes 1048608 | tf_op jit(solution)/shard_map/ppermute | solution.py:62
  55.4 2.5 %collective-permute-done.7.refs_3_ = bf16[64,7168]{1,0:T(8,128)(2,1)} collective-permute-done((bf16[64,7168]{1,0:T(8,128)(2,1)}, bf16[64,7168]{1,0:T(8,128)(2,1)}, u32[]{:S(2)}, u32[]{:S(2)}) %collective-permute-start.7) | collective-permute-done | bytes 917536 | tf_op jit(solution)/shard_map/ppermute | solution.py:158
  57.8 3.0 %collective-permute-done.8.refs_4_ = bf16[64,7168]{1,0:T(8,128)(2,1)} collective-permute-done((bf16[64,7168]{1,0:T(8,128)(2,1)}, bf16[64,7168]{1,0:T(8,128)(2,1)}, u32[]{:S(2)}, u32[]{:S(2)}) %collective-permute-start.8) | collective-permute-done | bytes 917536 | tf_op jit(solution)/shard_map/ppermute | solution.py:66
  62.0 2.2 %collective-permute-start.9 = (bf16[64,7168]{1,0:T(8,128)(2,1)}, bf16[64,7168]{1,0:T(8,128)(2,1)}, u32[]{:S(2)}, u32[]{:S(2)}) collective-permute-start(bf16[64,7168]{1,0:T(8,128)(2,1)} %get-tuple-element.75.refs_0_), channel_id=1, source_target_pairs={{4,0},{5,1},{6,2},{7,3},{8,12},{9,13},{10,14},{11,15},{20,16},{21,... | collective-permute-start | bytes 2752520 | tf_op jit(solution)/shard_map/ppermute | solution.py:158
  64.2 3.1 %shard_map.78 = (bf16[64,7168]{1,0:T(8,128)(2,1)}, s32[1]{0:T(128)}) custom-call(s32[1]{0:T(128)} %bitcast.inside_ref, s32[1]{0:T(128)} %get-tuple-element.74.turn_ref, bf16[64,7168]{1,0:T(8,128)(2,1)} %get-tuple-element.75.refs_0_, bf16[64,7168]{1,0:T(8,128)(2,1)} %get-tuple-element.76.refs_1_), custom_call_target="tpu_custom_call", output_to_operand_aliasing={{0}: (3, {})} | custom-call | flops 1 | bytes 1 | tf_op jit(solution)/shard_map/pallas_call | solution.py:106
  68.5 5.5 %collective-permute-done.10.refs_2_ = bf16[64,7168]{1,0:T(8,128)(2,1)} collective-permute-done((bf16[64,7168]{1,0:T(8,128)(2,1)}, bf16[64,7168]{1,0:T(8,128)(2,1)}, u32[]{:S(2)}, u32[]{:S(2)}) %collective-permute-start.10) | collective-permute-done | bytes 917536 | tf_op jit(solution)/shard_map/ppermute | solution.py:62
  74.0 3.7 %collective-permute-done.11.refs_3_ = bf16[64,7168]{1,0:T(8,128)(2,1)} collective-permute-done((bf16[64,7168]{1,0:T(8,128)(2,1)}, bf16[64,7168]{1,0:T(8,128)(2,1)}, u32[]{:S(2)}, u32[]{:S(2)}) %collective-permute-start.11) | collective-permute-done | bytes 917536 | tf_op jit(solution)/shard_map/ppermute | solution.py:66
  77.9 3.1 %shard_map.80 = (bf16[64,7168]{1,0:T(8,128)(2,1)}, bf16[64,7168]{1,0:T(8,128)(2,1)}, bf16[64,7168]{1,0:T(8,128)(2,1)}, bf16[64,8192]{1,0:T(8,128)(2,1)}, s32[1]{0:T(128)}) custom-call(s32[1]{0:T(128)} %bitcast.inside_ref, s32[1]{0:T(128)} %shard_map.79.turn_ref, ...), custom_call_target="tpu_custom_call", output_to_operand_aliasing={{0}: (3, {}), {1}: (4, {}), {2}: (5, {}), {3}: (6, {})} | custom-call | flops 1 | bytes 1 | tf_op jit(solution)/shard_map/pallas_call | solution.py:106
  85.5 10.8 %shard_map.81 = (f32[1024,256]{1,0:T(8,128)}, s32[1]{0:T(128)}) custom-call(s32[1]{0:T(128)} %get-tuple-element.79.turn_ref, s32[3]{0:T(128)} %concatenate.25.at_ref, bf16[512,14336]{1,0:T(8,128)(2,1)} %own_ref.11, bf16[512,14336]{1,0:T(8,128)(2,1)} %collective-permute-done.refs_0_.other_ref, bf16[64,7168]{1,0:T(8,128)(2,1)} %get-tuple-element.68.refs_0_, ...), custom_call_target="tpu_custom_call" | custom-call | flops 1 | bytes 1 | tf_op jit(solution)/shard_map/pallas_call | solution.py:222
  96.4 7.6 %collective-permute-done.13.refs_1_ = bf16[64,7168]{1,0:T(8,128)(2,1)} collective-permute-done((bf16[64,7168]{1,0:T(8,128)(2,1)}, bf16[64,7168]{1,0:T(8,128)(2,1)}, u32[]{:S(2)}, u32[]{:S(2)}) %collective-permute-start.13) | collective-permute-done | bytes 917536 | tf_op jit(solution)/shard_map/ppermute | solution.py:62
  104.0 2.7 %collective-permute-done.12.refs_0_ = bf16[64,8192]{1,0:T(8,128)(2,1)} collective-permute-done((bf16[64,8192]{1,0:T(8,128)(2,1)}, bf16[64,8192]{1,0:T(8,128)(2,1)}, u32[]{:S(2)}, u32[]{:S(2)}) %collective-permute-start.12) | collective-permute-done | bytes 1048608 | tf_op jit(solution)/shard_map/ppermute | solution.py:62
  109.6 10.9 %shard_map.83 = (f32[1024,256]{1,0:T(8,128)}, s32[1]{0:T(128)}) custom-call(s32[1]{0:T(128)} %get-tuple-element.85.turn_ref, s32[3]{0:T(128)} %concatenate.26.at_ref, bf16[512,14336]{1,0:T(8,128)(2,1)} %own_ref.11, bf16[512,14336]{1,0:T(8,128)(2,1)} %collective-permute-done.refs_0_.other_ref, bf16[64,7168]{1,0:T(8,128)(2,1)} %get-tuple-element.86.refs_0_, ...), custom_call_target="tpu_custom_call" | custom-call | flops 1 | bytes 1 | tf_op jit(solution)/shard_map/pallas_call | solution.py:222
  120.5 9.0 %collective-permute-done.15.refs_0_ = bf16[64,8192]{1,0:T(8,128)(2,1)} collective-permute-done((bf16[64,8192]{1,0:T(8,128)(2,1)}, bf16[64,8192]{1,0:T(8,128)(2,1)}, u32[]{:S(2)}, u32[]{:S(2)}) %collective-permute-start.15) | collective-permute-done | bytes 1048608 | tf_op jit(solution)/shard_map/ppermute | solution.py:62
  134.9 13.8 %shard_map.85 = (f32[8,256]{1,0:T(8,128)}, s32[1]{0:T(128)}) custom-call(s32[1]{0:T(128)} %get-tuple-element.93.turn_ref, s32[3]{0:T(128)} %broadcast_8_at_ref.2.at_ref, bf16[512,8192]{1,0:T(8,128)(2,1)} %own_ref.10, bf16[512,8192]{1,0:T(8,128)(2,1)} %collective-permute-done.4.refs_0_.other_ref, bf16[64,8192]{1,0:T(8,128)(2,1)} %bitcast.22, ...), custom_call_target="tpu_custom_call" | custom-call | flops 1 | bytes 1 | tf_op jit(solution)/shard_map/pallas_call | solution.py:222
  148.8 5.2 %collective-permute-done.21.refs_2_ = bf16[64,7168]{1,0:T(8,128)(2,1)} collective-permute-done((bf16[64,7168]{1,0:T(8,128)(2,1)}, bf16[64,7168]{1,0:T(8,128)(2,1)}, u32[]{:S(2)}, u32[]{:S(2)}) %collective-permute-start.21) | collective-permute-done | bytes 917536 | tf_op jit(solution)/shard_map/ppermute | solution.py:66
  154.4 1.8 collective-permute-done.20.refs_1_
  159.8 1.8 slice.19
  162.3 1.8 slice.20
  166.5 1.4 fusion.10
  167.8 10.9 %shard_map.87 = (f32[1024,256]{1,0:T(8,128)}, s32[1]{0:T(128)}) custom-call(s32[1]{0:T(128)} %get-tuple-element.103.turn_ref, s32[3]{0:T(128)} %concatenate.25.at_ref, bf16[512,14336]{1,0:T(8,128)(2,1)} %own_ref.11, bf16[512,14336]{1,0:T(8,128)(2,1)} %collective-permute-done.refs_0_.other_ref, bf16[64,7168]{1,0:T(8,128)(2,1)} %get-tuple-element.104.refs_0_, ...), custom_call_target="tpu_custom_call" | custom-call | flops 1 | bytes 1 | tf_op jit(solution)/shard_map/pallas_call | solution.py:222
  179.9 2.1 collective-permute-done.22.refs_0_
  183.4 11.7 %shard_map.89 = (f32[1024,256]{1,0:T(8,128)}, s32[1]{0:T(128)}) custom-call(s32[1]{0:T(128)} %get-tuple-element.109.turn_ref, s32[3]{0:T(128)} %broadcast_8_at_ref.2.at_ref, bf16[512,8192]{1,0:T(8,128)(2,1)} %own_ref.10, bf16[512,8192]{1,0:T(8,128)(2,1)} %collective-permute-done.4.refs_0_.other_ref, bf16[64,8192]{1,0:T(8,128)(2,1)} %get-tuple-element.110.refs_0_, ...), custom_call_target="tpu_custom_call" | custom-call | flops 1 | bytes 1 | tf_op jit(solution)/shard_map/pallas_call | solution.py:222
  195.8 12.9 %shard_map.90 = (f32[8,256]{1,0:T(8,128)}, s32[1]{0:T(128)}) custom-call(s32[1]{0:T(128)} %get-tuple-element.113.turn_ref, s32[3]{0:T(128)} %concatenate.26.at_ref, bf16[512,14336]{1,0:T(8,128)(2,1)} %own_ref.11, bf16[512,14336]{1,0:T(8,128)(2,1)} %collective-permute-done.refs_0_.other_ref, bf16[64,7168]{1,0:T(8,128)(2,1)} %get-tuple-element.114.refs_0_, ...), custom_call_target="tpu_custom_call" | custom-call | flops 1 | bytes 1 | tf_op jit(solution)/shard_map/pallas_call | solution.py:222
  210.2 2.4 %collective-permute-start.27 = (f32[4,512]{1,0:T(4,128)S(1)}, f32[4,512]{1,0:T(4,128)S(1)}, u32[]{:S(2)}, u32[]{:S(2)}) collective-permute-start(f32[4,512]{1,0:T(4,128)S(1)} %pad_maximum_fusion), channel_id=1, source_target_pairs={{0,1},{1,0},{2,3},{3,2},{4,5},{5,4},{6,7},{7,6},{8,9},{9,8},{10,11... | collective-permute-start | bytes 24584 | tf_op jit(solution)/shard_map/ppermute | solution.py:62
  213.5 1.5 fusion
  (69 shorter events, 39.2 us)
Async XLA Ops:
  0.0 33.5 %collective-permute-start = (bf16[512,14336]{1,0:T(8,128)(2,1)}, bf16[512,14336]{1,0:T(8,128)(2,1)}, u32[]{:S(2)}, u32[]{:S(2)}) collective-permute-start(bf16[512,14336]{1,0:T(8,128)(2,1)} %own_ref.11), channel_id=1, source_target_pairs={{0,1},{1,0},{2,3},{3,2},{4,5},{5,4},{6,7},{7,6},{8,9},{9,8},{10,11... | collective-permute-start | bytes 44040200 | tf_op jit(solution)/shard_map/ppermute | solution.py:62
  0.7 53.5 %collective-permute-start.4 = (bf16[512,8192]{1,0:T(8,128)(2,1)}, bf16[512,8192]{1,0:T(8,128)(2,1)}, u32[]{:S(2)}, u32[]{:S(2)}) collective-permute-start(bf16[512,8192]{1,0:T(8,128)(2,1)} %own_ref.10), channel_id=1, source_target_pairs={{0,1},{1,0},{2,3},{3,2},{4,5},{5,4},{6,7},{7,6},{8,9},{9,8},{10,11... | collective-permute-start | bytes 25165832 | tf_op jit(solution)/shard_map/ppermute | solution.py:62
  9.3 19.7 %collective-permute-start.1 = (bf16[64,7168]{1,0:T(8,128)(2,1)}, bf16[64,7168]{1,0:T(8,128)(2,1)}, u32[]{:S(2)}, u32[]{:S(2)}) collective-permute-start(bf16[64,7168]{1,0:T(8,128)(2,1)} %get-tuple-element.68.refs_0_), channel_id=1, source_target_pairs={{4,8},{5,9},{6,10},{7,11},{8,4},{9,5},{10,6},{11,7},{20,24},{21,25... | collective-permute-start | bytes 2752520 | tf_op jit(solution)/shard_map/ppermute | solution.py:158
  12.5 18.2 %collective-permute-start.2 = (bf16[64,7168]{1,0:T(8,128)(2,1)}, bf16[64,7168]{1,0:T(8,128)(2,1)}, u32[]{:S(2)}, u32[]{:S(2)}) collective-permute-start(bf16[64,7168]{1,0:T(8,128)(2,1)} %get-tuple-element.68.refs_0_), channel_id=1, source_target_pairs={{0,4},{1,5},{2,6},{3,7},{4,0},{5,1},{6,2},{7,3},{8,12},{9,13},{10,... | collective-permute-start | bytes 2752520 | tf_op jit(solution)/shard_map/ppermute | solution.py:62
  12.6 20.9 %collective-permute-start.3 = (bf16[64,7168]{1,0:T(8,128)(2,1)}, bf16[64,7168]{1,0:T(8,128)(2,1)}, u32[]{:S(2)}, u32[]{:S(2)}) collective-permute-start(bf16[64,7168]{1,0:T(8,128)(2,1)} %get-tuple-element.68.refs_0_), channel_id=1, source_target_pairs={{0,2},{1,3},{2,0},{3,1},{4,6},{5,7},{6,4},{7,5},{8,10},{9,11},{10,... | collective-permute-start | bytes 2752520 | tf_op jit(solution)/shard_map/ppermute | solution.py:62
  29.0 23.9 %collective-permute-start.6 = (bf16[64,8192]{1,0:T(8,128)(2,1)}, bf16[64,8192]{1,0:T(8,128)(2,1)}, u32[]{:S(2)}, u32[]{:S(2)}) collective-permute-start(bf16[64,8192]{1,0:T(8,128)(2,1)} %get-tuple-element.71), channel_id=1, source_target_pairs={{0,2},{1,3},{2,0},{3,1},{4,6},{5,7},{6,4},{7,5},{8,10},{9,11},{10,... | collective-permute-start | bytes 3145736 | tf_op jit(solution)/shard_map/ppermute | solution.py:62
  34.7 20.7 %collective-permute-start.5 = (bf16[64,7168]{1,0:T(8,128)(2,1)}, bf16[64,7168]{1,0:T(8,128)(2,1)}, u32[]{:S(2)}, u32[]{:S(2)}) collective-permute-start(bf16[64,7168]{1,0:T(8,128)(2,1)} %get-tuple-element.70.refs_0_), channel_id=1, source_target_pairs={{4,0},{5,1},{6,2},{7,3},{8,12},{9,13},{10,14},{11,15},{20,16},{21,... | collective-permute-start | bytes 2752520 | tf_op jit(solution)/shard_map/ppermute | solution.py:158
  40.9 16.9 %collective-permute-start.7 = (bf16[64,7168]{1,0:T(8,128)(2,1)}, bf16[64,7168]{1,0:T(8,128)(2,1)}, u32[]{:S(2)}, u32[]{:S(2)}) collective-permute-start(bf16[64,7168]{1,0:T(8,128)(2,1)} %get-tuple-element.72.refs_2_), channel_id=1, source_target_pairs={{4,8},{5,9},{6,10},{7,11},{8,4},{9,5},{10,6},{11,7},{20,24},{21,25... | collective-permute-start | bytes 2752520 | tf_op jit(solution)/shard_map/ppermute | solution.py:158
  43.0 17.9 %collective-permute-start.8 = (bf16[64,7168]{1,0:T(8,128)(2,1)}, bf16[64,7168]{1,0:T(8,128)(2,1)}, u32[]{:S(2)}, u32[]{:S(2)}) collective-permute-start(bf16[64,7168]{1,0:T(8,128)(2,1)} %get-tuple-element.73.refs_1_), channel_id=1, source_target_pairs={{0,16},{16,0},{1,17},{17,1},{2,18},{18,2},{3,19},{19,3},{4,20},{20... | collective-permute-start | bytes 2752520 | tf_op jit(solution)/shard_map/ppermute | solution.py:66
  52.9 21.1 %collective-permute-start.10 = (bf16[64,7168]{1,0:T(8,128)(2,1)}, bf16[64,7168]{1,0:T(8,128)(2,1)}, u32[]{:S(2)}, u32[]{:S(2)}) collective-permute-start(bf16[64,7168]{1,0:T(8,128)(2,1)} %get-tuple-element.72.refs_2_), channel_id=1, source_target_pairs={{0,2},{1,3},{2,0},{3,1},{4,6},{5,7},{6,4},{7,5},{8,10},{9,11},{10,... | collective-permute-start | bytes 2752520 | tf_op jit(solution)/shard_map/ppermute | solution.py:62
  54.1 23.6 %collective-permute-start.11 = (bf16[64,7168]{1,0:T(8,128)(2,1)}, bf16[64,7168]{1,0:T(8,128)(2,1)}, u32[]{:S(2)}, u32[]{:S(2)}) collective-permute-start(bf16[64,7168]{1,0:T(8,128)(2,1)} %get-tuple-element.72.refs_2_), channel_id=1, source_target_pairs={{0,16},{16,0},{1,17},{17,1},{2,18},{18,2},{3,19},{19,3},{4,20},{20... | collective-permute-start | bytes 2752520 | tf_op jit(solution)/shard_map/ppermute | solution.py:66
  62.0 15.9 %collective-permute-start.9 = (bf16[64,7168]{1,0:T(8,128)(2,1)}, bf16[64,7168]{1,0:T(8,128)(2,1)}, u32[]{:S(2)}, u32[]{:S(2)}) collective-permute-start(bf16[64,7168]{1,0:T(8,128)(2,1)} %get-tuple-element.75.refs_0_), channel_id=1, source_target_pairs={{4,0},{5,1},{6,2},{7,3},{8,12},{9,13},{10,14},{11,15},{20,16},{21,... | collective-permute-start | bytes 2752520 | tf_op jit(solution)/shard_map/ppermute | solution.py:158
  81.1 25.6 %collective-permute-start.12 = (bf16[64,8192]{1,0:T(8,128)(2,1)}, bf16[64,8192]{1,0:T(8,128)(2,1)}, u32[]{:S(2)}, u32[]{:S(2)}) collective-permute-start(bf16[64,8192]{1,0:T(8,128)(2,1)} %get-tuple-element.82), channel_id=1, source_target_pairs={{0,4},{1,5},{2,6},{3,7},{4,0},{5,1},{6,2},{7,3},{8,12},{9,13},{10,... | collective-permute-start | bytes 3145736 | tf_op jit(solution)/shard_map/ppermute | solution.py:62
  81.1 22.8 %collective-permute-start.13 = (bf16[64,7168]{1,0:T(8,128)(2,1)}, bf16[64,7168]{1,0:T(8,128)(2,1)}, u32[]{:S(2)}, u32[]{:S(2)}) collective-permute-start(bf16[64,7168]{1,0:T(8,128)(2,1)} %get-tuple-element.83.refs_3_), channel_id=1, source_target_pairs={{0,2},{1,3},{2,0},{3,1},{4,6},{5,7},{6,4},{7,5},{8,10},{9,11},{10,... | collective-permute-start | bytes 2752520 | tf_op jit(solution)/shard_map/ppermute | solution.py:62
  82.2 21.7 %collective-permute-start.14 = (bf16[64,7168]{1,0:T(8,128)(2,1)}, bf16[64,7168]{1,0:T(8,128)(2,1)}, u32[]{:S(2)}, u32[]{:S(2)}) collective-permute-start(bf16[64,7168]{1,0:T(8,128)(2,1)} %get-tuple-element.80.refs_3_), channel_id=1, source_target_pairs={{0,16},{16,0},{1,17},{17,1},{2,18},{18,2},{3,19},{19,3},{4,20},{20... | collective-permute-start | bytes 2752520 | tf_op jit(solution)/shard_map/ppermute | solution.py:66
  83.5 46.0 %collective-permute-start.15 = (bf16[64,8192]{1,0:T(8,128)(2,1)}, bf16[64,8192]{1,0:T(8,128)(2,1)}, u32[]{:S(2)}, u32[]{:S(2)}) collective-permute-start(bf16[64,8192]{1,0:T(8,128)(2,1)} %get-tuple-element.71), channel_id=1, source_target_pairs={{0,12},{1,13},{2,14},{3,15},{4,8},{5,9},{6,10},{7,11},{8,4},{9,5},... | collective-permute-start | bytes 3145736 | tf_op jit(solution)/shard_map/ppermute | solution.py:62
  85.3 44.2 %collective-permute-start.16 = (bf16[64,7168]{1,0:T(8,128)(2,1)}, bf16[64,7168]{1,0:T(8,128)(2,1)}, u32[]{:S(2)}, u32[]{:S(2)}) collective-permute-start(bf16[64,7168]{1,0:T(8,128)(2,1)} %get-tuple-element.80.refs_3_), channel_id=1, source_target_pairs={{0,2},{1,3},{2,0},{3,1},{4,6},{5,7},{6,4},{7,5},{8,10},{9,11},{10,... | collective-permute-start | bytes 2752520 | tf_op jit(solution)/shard_map/ppermute | solution.py:62
  107.9 21.5 %collective-permute-start.17 = (bf16[64,7168]{1,0:T(8,128)(2,1)}, bf16[64,7168]{1,0:T(8,128)(2,1)}, u32[]{:S(2)}, u32[]{:S(2)}) collective-permute-start(bf16[64,7168]{1,0:T(8,128)(2,1)} %get-tuple-element.91.refs_1_), channel_id=1, source_target_pairs={{0,16},{16,0},{1,17},{17,1},{2,18},{18,2},{3,19},{19,3},{4,20},{20... | collective-permute-start | bytes 2752520 | tf_op jit(solution)/shard_map/ppermute | solution.py:66
  109.6 22.7 %copy-start.1 = (s32[4]{0:T(128)S(1)}, s32[4]{0:T(128)}, u32[]{:S(2)}) copy-start(s32[4]{0:T(128)} %param.11) | copy-start | bytes 52
  109.6 22.9 %copy-start.2 = (s32[4]{0:T(128)S(1)}, s32[4]{0:T(128)}, u32[]{:S(2)}) copy-start(s32[4]{0:T(128)} %param.12) | copy-start | bytes 52
  130.5 23.9 %collective-permute-start.19 = (bf16[64,8192]{1,0:T(8,128)(2,1)}, bf16[64,8192]{1,0:T(8,128)(2,1)}, u32[]{:S(2)}, u32[]{:S(2)}) collective-permute-start(bf16[64,8192]{1,0:T(8,128)(2,1)} %get-tuple-element.96.refs_3_), channel_id=1, source_target_pairs={{0,4},{1,5},{2,6},{3,7},{4,0},{5,1},{6,2},{7,3},{8,12},{9,13},{10,... | collective-permute-start | bytes 3145736 | tf_op jit(solution)/shard_map/ppermute | solution.py:62
  130.8 25.4 %collective-permute-start.20 = (bf16[64,8192]{1,0:T(8,128)(2,1)}, bf16[64,8192]{1,0:T(8,128)(2,1)}, u32[]{:S(2)}, u32[]{:S(2)}) collective-permute-start(bf16[64,8192]{1,0:T(8,128)(2,1)} %get-tuple-element.96.refs_3_), channel_id=1, source_target_pairs={{0,2},{1,3},{2,0},{3,1},{4,6},{5,7},{6,4},{7,5},{8,10},{9,11},{10,... | collective-permute-start | bytes 3145736 | tf_op jit(solution)/shard_map/ppermute | solution.py:62
  131.9 22.0 %collective-permute-start.21 = (bf16[64,7168]{1,0:T(8,128)(2,1)}, bf16[64,7168]{1,0:T(8,128)(2,1)}, u32[]{:S(2)}, u32[]{:S(2)}) collective-permute-start(bf16[64,7168]{1,0:T(8,128)(2,1)} %get-tuple-element.101.refs_2_), channel_id=1, source_target_pairs={{0,16},{16,0},{1,17},{17,1},{2,18},{18,2},{3,19},{19,3},{4,20},{20... | collective-permute-start | bytes 2752520 | tf_op jit(solution)/shard_map/ppermute | solution.py:66
  132.5 1.2 collective-permute-start.18
  157.4 24.6 %collective-permute-start.22 = (bf16[64,8192]{1,0:T(8,128)(2,1)}, bf16[64,8192]{1,0:T(8,128)(2,1)}, u32[]{:S(2)}, u32[]{:S(2)}) collective-permute-start(bf16[64,8192]{1,0:T(8,128)(2,1)} %get-tuple-element.107.refs_1_), channel_id=1, source_target_pairs={{0,2},{1,3},{2,0},{3,1},{4,6},{5,7},{6,4},{7,5},{8,10},{9,11},{10,... | collective-permute-start | bytes 3145736 | tf_op jit(solution)/shard_map/ppermute | solution.py:62
  158.3 23.9 %collective-permute-start.24 = (bf16[64,8192]{1,0:T(8,128)(2,1)}, bf16[64,8192]{1,0:T(8,128)(2,1)}, u32[]{:S(2)}, u32[]{:S(2)}) collective-permute-start(bf16[64,8192]{1,0:T(8,128)(2,1)} %get-tuple-element.108), channel_id=1, source_target_pairs={{0,4},{1,5},{2,6},{3,7},{4,0},{5,1},{6,2},{7,3},{8,12},{9,13},{10,... | collective-permute-start | bytes 3145736 | tf_op jit(solution)/shard_map/ppermute | solution.py:62
  159.3 20.5 %collective-permute-start.23 = (bf16[64,7168]{1,0:T(8,128)(2,1)}, bf16[64,7168]{1,0:T(8,128)(2,1)}, u32[]{:S(2)}, u32[]{:S(2)}) collective-permute-start(bf16[64,7168]{1,0:T(8,128)(2,1)} %get-tuple-element.104.refs_0_), channel_id=1, source_target_pairs={{0,16},{16,0},{1,17},{17,1},{2,18},{18,2},{3,19},{19,3},{4,20},{20... | collective-permute-start | bytes 2752520 | tf_op jit(solution)/shard_map/ppermute | solution.py:66
  161.6 33.4 %collective-permute-start.25 = (bf16[32,7168]{1,0:T(8,128)(2,1)}, bf16[32,7168]{1,0:T(8,128)(2,1)S(1)}, u32[]{:S(2)}, u32[]{:S(2)}) collective-permute-start(bf16[32,7168]{1,0:T(8,128)(2,1)} %slice.19), channel_id=1, source_target_pairs={{0,2},{1,3},{2,0},{3,1},{4,6},{5,7},{6,4},{7,5},{8,10},{9,11},{10,... | collective-permute-start | bytes 1376264 | tf_op jit(solution)/shard_map/ppermute | solution.py:62
  164.1 30.9 %collective-permute-start.26 = (bf16[32,7168]{1,0:T(8,128)(2,1)}, bf16[32,7168]{1,0:T(8,128)(2,1)}, u32[]{:S(2)}, u32[]{:S(2)}) collective-permute-start(bf16[32,7168]{1,0:T(8,128)(2,1)} %slice.20), channel_id=1, source_target_pairs={{0,16},{16,0},{1,17},{17,1},{2,18},{18,2},{3,19},{19,3},{4,20},{20... | collective-permute-start | bytes 1376264 | tf_op jit(solution)/shard_map/ppermute | solution.py:66
  195.0 0.8 copy-start
  210.2 3.4 %collective-permute-start.27 = (f32[4,512]{1,0:T(4,128)S(1)}, f32[4,512]{1,0:T(4,128)S(1)}, u32[]{:S(2)}, u32[]{:S(2)}) collective-permute-start(f32[4,512]{1,0:T(4,128)S(1)} %pad_maximum_fusion), channel_id=1, source_target_pairs={{0,1},{1,0},{2,3},{3,2},{4,5},{5,4},{6,7},{7,6},{8,9},{9,8},{10,11... | collective-permute-start | bytes 24584 | tf_op jit(solution)/shard_map/ppermute | solution.py:62

commit v15 on v14

--- a/solution.py
+++ b/solution.py
@@ -55,7 +55,7 @@
 
 CORE, COLUMN, NEAR, ACROSS, OPPOSITE = 1, 2, 4, 12, 8
 LITTLE = pl.CostEstimate(flops=1, bytes_accessed=1, transcendentals=0)
-VMEM_LIMIT = 127 * 512 * 1024
+VMEM_LIMIT = 255 * 256 * 1024
 
 
 def flip(array, code, count):
@@ -273,8 +273,8 @@
     def middle(piece):
         return lines(piece, [(1, 2), (2, 1)])
 
-    def outward(piece):
-        return lines(piece, [(1, 0), (2, 3)])
+    def ends(piece):
+        return lines(piece, [(0, 3), (3, 0)])
 
     def across(piece):
         return send(piece, ACROSS)
@@ -286,7 +286,7 @@
     mine = jnp.reshape(group, (1,)).astype(jnp.int32)
     zero = jnp.zeros((1,), jnp.int32)
     acts = ((hidden_acts, zero), (acts_there, zero))
-    groups = (("own", "x", "n", "f"), ("xo", "o", "xn", "xf"))
+    groups = (("own", "x", "n", "f"), ("xn", "xf", "o", "xo"))
     tokens_here = hidden_acts.shape[0]
     steps = 4
 
@@ -302,80 +302,82 @@
     def pause(turn):
         return after(turn, [], inside)[0]
 
-    grads_there = send(output_grads, CORE)
-    grads = ((output_grads, zero), (grads_there, zero))
-
-    core = (me & CORE).reshape(1).astype(jnp.int32)
-    copies = (1 - mine, left, b["own"])
-    turn, made, (a["own"],) = prepare(zero, core, *copies, None, [a["own"]])
-    a_mid = middle(a["own"])
-    a["n"] = near(a["own"])
-    a["x"] = over_x(a["own"])
-    turn, (c["own"], b_one, b_two), _ = prepare(turn, 1 - core, *copies, made, [])
-
-    turn, (a_mid, a["n"], a["x"]) = after(turn, [a_mid, a["n"], a["x"]], inside, None, [acts_there])
-    a_out = outward(a_mid)
-    a_in = middle(a["n"])
-    b["x"] = over_x(b_one)
-    c["x"] = swap_groups(a["x"])
-    turn = pause(turn)
-
-    turn, (a_out, b["x"], a_in, c["x"]) = after(turn, [a_out, b["x"], a_in, c["x"]], inside, None, [grads_there])
-    a_last = outward(a_in)
-    a["xn"] = over_x(a["n"])
-    c["n"] = swap_groups(a["n"])
-    b["f"] = across(b_one)
-    turn, (a["o"],) = after(turn, [a_out], inside, a_in)
-    a["xo"] = over_x(a["o"])
-    turn = pause(turn)
-
-    turn, (a["f"], a["xn"], c["n"], b_two) = after(turn, [a_last, a["xn"], c["n"], b_two], inside, a_mid)
-    b["n"] = near(b_two)
-    a["xf"] = over_x(a["f"])
-    c["f"] = swap_groups(a["f"])
-    turn, a_first = times_a(turn, 0)
-
-    turn, (b["n"], a["xo"], c["f"], a["o"], a["xn"]) = after(
-        turn, [b["n"], a["xo"], c["f"], a["o"], a["xn"]], inside
-    )
-    c["o"] = swap_groups(a["o"])
-    c["xn"] = swap_groups(a["xn"])
-    turn, c_first = times_c(turn, 0)
-
-    turn, (b["f"], a["xf"], c["o"], a["xo"]) = after(turn, [b["f"], a["xf"], c["o"], a["xo"]], inside)
-    b["o"] = near(b["f"])
-    b["xf"] = over_x(b["f"])
-    c["xo"] = swap_groups(a["xo"])
-    turn, score_first = times_b(turn, 0, True, spans, (a_first, c_first))
-
-    split = c["f"].shape[0] // 2
-    turn, (b["o"], b["xf"], c["xn"], b_over, a["xf"], c["f"]) = after(
-        turn, [b["o"], b["xf"], c["xn"], b["x"], a["xf"], c["f"]], inside
-    )
-    b["xo"] = over_x(b["o"])
-    b["xn"] = near(b_over)
-    c["top"] = over_x(c["f"][:split])
-    c["low"] = swap_groups(a["xf"][split:])
-    turn, a_second = times_a(turn, 1)
-
-    turn, (b["xo"], c["xo"], b["xn"]) = after(turn, [b["xo"], c["xo"], b["xn"]], inside)
-    turn, b_second = times_b(turn, 1)
-    groups = (groups[0], ("xo", "o", "xn", "top", "low"))
-    turn, score_second = times_c(turn, 1, False, spans, (a_second, b_second))
-    sums = [score_first, score_second]
-
-    slots = bucket_ids.shape[0]
-    ours = jnp.concatenate([x[:slots] for x in sums], axis=1)
-    others = send(jnp.concatenate([x[slots:] for x in sums], axis=1), CORE)
-    codes = (0, COLUMN, NEAR, ACROSS, OPPOSITE | COLUMN, OPPOSITE, NEAR | COLUMN, ACROSS | COLUMN)
+    codes = (0, COLUMN, NEAR, ACROSS, NEAR | COLUMN, ACROSS | COLUMN, OPPOSITE, OPPOSITE | COLUMN)
     codes = jnp.array(codes, jnp.int32)
     owner = jnp.concatenate([me ^ codes, me ^ CORE ^ codes])
     query = owner[:, None] * local + jnp.arange(local, dtype=jnp.int32)[None, :]
     query = jnp.repeat(query.reshape(-1), ranks)
     placed = query[None, :] == jnp.arange(count * local, dtype=jnp.int32)[:, None]
+    placed = placed.astype(jnp.float32)
+
+    grads_there = send(output_grads, CORE)
+    grads = ((output_grads, zero), (grads_there, zero))
+
+    core = (me & CORE).reshape(1).astype(jnp.int32)
+    copies = (1 - mine, left, b["own"])
+    turn, made, (a["own"],) = prepare(zero, core, *copies, None, [a["own"]])
+    a["x"] = over_x(a["own"])
+    a["n"] = near(a["own"])
+    a_mid = middle(a["own"])
+    turn, (c["own"], b_one, b_two), _ = prepare(turn, 1 - core, *copies, made, [])
+
+    turn, (a["x"], a["n"], a_mid, a["own"]) = after(
+        turn, [a["x"], a["n"], a_mid, a["own"]], inside, None, [acts_there]
+    )
+    a_end = ends(a["own"])
+    b["x"] = over_x(b_one)
+    c["x"] = swap_groups(a["x"])
+    turn = pause(turn)
+
+    turn, (a["f"], b["x"], c["x"]) = after(turn, [a_end, b["x"], c["x"]], inside, a_mid, [grads_there])
+    a["o"] = near(a["f"])
+    a["xn"] = over_x(a["n"])
+    c["n"] = swap_groups(a["n"])
+    b["f"] = across(b_one)
+    turn = pause(turn)
+
+    turn, (a["o"], a["xn"], c["n"], b_two) = after(turn, [a["o"], a["xn"], c["n"], b_two], inside)
+    b["n"] = near(b_two)
+    a["xf"] = over_x(a["f"])
+    c["f"] = swap_groups(a["f"])
+    turn, a_first = times_a(turn, 0)
+
+    turn, (b["n"], a["xf"], c["f"], a["o"], a["xn"]) = after(
+        turn, [b["n"], a["xf"], c["f"], a["o"], a["xn"]], inside
+    )
+    a["xo"] = over_x(a["o"])
+    c["o"] = swap_groups(a["o"])
+    c["xn"] = swap_groups(a["xn"])
+    turn, c_first = times_c(turn, 0)
+
+    turn, (b["f"], a["xo"], c["o"], a["xf"]) = after(turn, [b["f"], a["xo"], c["o"], a["xf"]], inside)
+    b["o"] = near(b["f"])
+    b["xf"] = over_x(b["f"])
+    c["xf"] = swap_groups(a["xf"])
+    turn, score_first = times_b(turn, 0, True, spans, (a_first, c_first))
+
+    split = c["o"].shape[0] // 2
+    turn, (b["o"], b["xf"], c["xn"], b_over, a["xo"], c["o"], placed) = after(
+        turn, [b["o"], b["xf"], c["xn"], b["x"], a["xo"], c["o"], placed], inside
+    )
+    b["xo"] = over_x(b["o"])
+    b["xn"] = near(b_over)
+    c["top"] = over_x(c["o"][:split])
+    c["low"] = swap_groups(a["xo"][split:])
+    turn, a_second = times_a(turn, 1)
+
+    turn, (b["xo"], c["xf"], b["xn"]) = after(turn, [b["xo"], c["xf"], b["xn"]], inside)
+    turn, b_second = times_b(turn, 1)
+    groups = (groups[0], ("xn", "xf", "o", "top", "low"))
+    turn, score_second = times_c(turn, 1, False, spans, (a_second, b_second))
+    sums = [score_first, score_second]
+
+    slots = bucket_ids.shape[0]
+    others = [send(x, CORE) for x in sums]
+    held = [x[:slots] for x in sums] + [x[slots:] for x in others]
     return lax.dot_general(
-        placed.astype(jnp.float32),
-        jnp.concatenate([ours, others], axis=1),
+        placed,
+        jnp.concatenate(held, axis=1),
         (((1,), (1,)), ((), ())),
         precision=lax.Precision.HIGHEST,
         preferred_element_type=jnp.float32,

time: 218 us -> 226 us (1.037)
  starting transfers between devices: 34.3 us -> 62.6 us
  waiting for transfers between devices: 70.5 us -> 58.4 us
  Pallas kernels: 94.2 us -> 91 us
  local copies, waits for them, and re-layouts: 10.7 us -> 8.43 us
    ppermute x17 -> x19, starting transfers between devices: 13.8 us -> 53.1 us  [flip(): return lax.ppermute(array, 'dp', [(i, i ^ code) for i in range(count)])]
    ppermute x4 -> x2, waiting for transfers between devices: 16.5 us -> 2.34 us  [lines(): lax.ppermute(array, 'dp', [(a * 4 + rest, b * 4 + rest) for a, b in pairs...]
    ppermute x4 -> x2, starting transfers between devices: 13.7 us -> 5.93 us  [lines(): lax.ppermute(array, 'dp', [(a * 4 + rest, b * 4 + rest) for a, b in pairs...]
    ppermute x7, waiting for transfers between devices: 13 us -> 18.5 us  [swap_groups(): return lax.ppermute(array, 'groups', [(0, 1), (1, 0)])]
    ppermute x17 -> x19, waiting for transfers between devices: 41.1 us -> 37.5 us  [flip(): return lax.ppermute(array, 'dp', [(i, i ^ code) for i in range(count)])]
    ppermute x7, starting transfers between devices: 6.77 us -> 3.55 us  [swap_groups(): return lax.ppermute(array, 'groups', [(0, 1), (1, 0)])]
    pallas_call x10 -> x9, Pallas kernels: 15.5 us -> 12.5 us  [after(): pl.pallas_call(functools.partial(after_kernel, count, merge is not None),...]
    slice x4 -> x6, local copies, waits for them, and re-layouts: 5.8 us -> 4.38 us  [the longest x1 1.85 us: relay(): c['top'] = over_x(c['o'][:split])]
  transfers between devices with their start and end apart: 28 -> 28, of which waited for: 19 -> 11; matrix products, arithmetic and copies ran while one was open for 6% -> 5% of each run, Pallas kernels for 35% -> 39%
where the time goes in v15:
time: 226 us; the launch traced here: 224 us
  Pallas kernels  91 us (40%)
  starting transfers between devices  62.6 us (28%)
  waiting for transfers between devices  58.4 us (26%)
  local copies, waits for them, and re-layouts  8.43 us (4%)
    pallas_call x6, Pallas kernels, proj(): pl.pallas_call(functools.partial(proj_kernel, len(pieces), last), out_sha...  70.8 us
    ppermute x19, starting transfers between devices, flip(): return lax.ppermute(array, 'dp', [(i, i ^ code) for i in range(count)])  53.1 us
    ppermute x19, waiting for transfers between devices, flip(): return lax.ppermute(array, 'dp', [(i, i ^ code) for i in range(count)])  37.5 us
    ppermute x7, waiting for transfers between devices, swap_groups(): return lax.ppermute(array, 'groups', [(0, 1), (1, 0)])  18.5 us
    pallas_call x9, Pallas kernels, after(): pl.pallas_call(functools.partial(after_kernel, count, merge is not None),...  12.5 us
    pallas_call x2, Pallas kernels, prepare(): pl.pallas_call(prepare_kernel, out_shape=[jax.ShapeDtypeStruct(x.shape, x...  7.71 us
    ppermute x2, starting transfers between devices, lines(): lax.ppermute(array, 'dp', [(a * 4 + rest, b * 4 + rest) for a, b in pairs...  5.93 us
  transfers between devices with their start and end apart: 28, of which 11 were waited for; matrix products, arithmetic and copies ran while one was open for 5% of the time, Pallas kernels for 39%

profile of v15, /device:TPU:9, one launch (start us, length us, event | category | flops | bytes accessed | tf_op | source)
XLA Modules:
  0.0 224.3 jit_solution(16682899984786288888)
XLA Ops:
  0.7 2.2 constant_dynamic-slice_fusion.refs_0_
  2.9 6.4 %shard_map.73 = (bf16[64,7168]{1,0:T(8,128)(2,1)}, bf16[64,7168]{1,0:T(8,128)(2,1)}, bf16[64,8192]{1,0:T(8,128)(2,1)}, bf16[64,8192]{1,0:T(8,128)(2,1)}, s32[1]{0:T(128)}) custom-call(s32[1]{0:T(128)} %bitcast.1.works_ref, s32[1]{0:T(128)} %constant.14.clone.1.turn_ref, s32[1]{0:T(128)S(6)} %sub.17.first_ref, ...), custom_call_target="tpu_custom_call", output_to_operand_aliasing={{0}: (5, {})} | custom-call | flops 1 | bytes 1 | tf_op jit(solution)/shard_map/pallas_call | solution.py:141
  9.3 1.3 collective-permute-start.1
  10.7 4.3 %collective-permute-start.3 = (bf16[64,7168]{1,0:T(8,128)(2,1)}, bf16[64,7168]{1,0:T(8,128)(2,1)}, u32[]{:S(2)}, u32[]{:S(2)}) collective-permute-start(bf16[64,7168]{1,0:T(8,128)(2,1)} %get-tuple-element.67.refs_4_), channel_id=1, source_target_pairs={{4,8},{5,9},{6,10},{7,11},{8,4},{9,5},{10,6},{11,7},{20,24},{21,25... | collective-permute-start | bytes 2752520 | tf_op jit(solution)/shard_map/ppermute | solution.py:158
  15.1 1.3 shard_map.74
  16.4 11.8 %collective-permute-done.1.refs_1_ = bf16[64,7168]{1,0:T(8,128)(2,1)} collective-permute-done((bf16[64,7168]{1,0:T(8,128)(2,1)}, bf16[64,7168]{1,0:T(8,128)(2,1)}, u32[]{:S(2)}, u32[]{:S(2)}) %collective-permute-start.1) | collective-permute-done | bytes 917536 | tf_op jit(solution)/shard_map/ppermute | solution.py:62
  28.1 1.2 collective-permute-start.6
  29.4 2.3 %collective-permute-done.3.refs_3_ = bf16[64,7168]{1,0:T(8,128)(2,1)} collective-permute-done((bf16[64,7168]{1,0:T(8,128)(2,1)}, bf16[64,7168]{1,0:T(8,128)(2,1)}, u32[]{:S(2)}, u32[]{:S(2)}) %collective-permute-start.3) | collective-permute-done | bytes 917536 | tf_op jit(solution)/shard_map/ppermute | solution.py:158
  32.9 1.6 collective-permute-start.5
  34.5 1.2 collective-permute-start.7
  37.1 12.7 %collective-permute-done.6.refs_3_ = bf16[64,8192]{1,0:T(8,128)(2,1)} collective-permute-done((bf16[64,8192]{1,0:T(8,128)(2,1)}, bf16[64,8192]{1,0:T(8,128)(2,1)}, u32[]{:S(2)}, u32[]{:S(2)}) %collective-permute-start.6) | collective-permute-done | bytes 1048608 | tf_op jit(solution)/shard_map/ppermute | solution.py:62
  49.8 7.3 %collective-permute-start.9 = (bf16[64,7168]{1,0:T(8,128)(2,1)}, bf16[64,7168]{1,0:T(8,128)(2,1)}, u32[]{:S(2)}, u32[]{:S(2)}) collective-permute-start(bf16[64,7168]{1,0:T(8,128)(2,1)} %get-tuple-element.75.refs_2_), channel_id=1, source_target_pairs={{0,2},{1,3},{2,0},{3,1},{4,6},{5,7},{6,4},{7,5},{8,10},{9,11},{10,... | collective-permute-start | bytes 2752520 | tf_op jit(solution)/shard_map/ppermute | solution.py:62
  57.2 3.2 %shard_map.77 = (bf16[64,7168]{1,0:T(8,128)(2,1)}, bf16[64,8192]{1,0:T(8,128)(2,1)}, bf16[64,7168]{1,0:T(8,128)(2,1)}, s32[1]{0:T(128)}) custom-call(s32[1]{0:T(128)} %bitcast.inside_ref, s32[1]{0:T(128)} %shard_map.76.turn_ref, bf16[64,7168]{1,0:T(8,128)(2,1)} %get-tuple-element.69.refs_0_, ...), custom_call_target="tpu_custom_call", output_to_operand_aliasing={{0}: (4, {}), {1}: (5, {}), {2}: (6, {})} | custom-call | flops 1 | bytes 1 | tf_op jit(solution)/shard_map/pallas_call | solution.py:106
  61.7 11.1 %collective-permute-done.10.refs_2_ = bf16[64,7168]{1,0:T(8,128)(2,1)} collective-permute-done((bf16[64,7168]{1,0:T(8,128)(2,1)}, bf16[64,7168]{1,0:T(8,128)(2,1)}, u32[]{:S(2)}, u32[]{:S(2)}) %collective-permute-start.10) | collective-permute-done | bytes 917536 | tf_op jit(solution)/shard_map/ppermute | solution.py:66
  72.8 5.3 %collective-permute-done.8.refs_0_ = bf16[64,7168]{1,0:T(8,128)(2,1)} collective-permute-done((bf16[64,7168]{1,0:T(8,128)(2,1)}, bf16[64,7168]{1,0:T(8,128)(2,1)}, u32[]{:S(2)}, u32[]{:S(2)}) %collective-permute-start.8) | collective-permute-done | bytes 917536 | tf_op jit(solution)/shard_map/ppermute | solution.py:62
  79.3 14.6 %collective-permute-start.12 = (bf16[64,7168]{1,0:T(8,128)(2,1)}, bf16[64,7168]{1,0:T(8,128)(2,1)}, u32[]{:S(2)}, u32[]{:S(2)}) collective-permute-start(bf16[64,7168]{1,0:T(8,128)(2,1)} %get-tuple-element.74.refs_3_), channel_id=1, source_target_pairs={{0,2},{1,3},{2,0},{3,1},{4,6},{5,7},{6,4},{7,5},{8,10},{9,11},{10,... | collective-permute-start | bytes 2752520 | tf_op jit(solution)/shard_map/ppermute | solution.py:62
  94.4 10.8 %shard_map.80 = (f32[1024,256]{1,0:T(8,128)}, s32[1]{0:T(128)}) custom-call(s32[1]{0:T(128)} %get-tuple-element.77.turn_ref, s32[3]{0:T(128)} %concatenate.21.at_ref, bf16[512,14336]{1,0:T(8,128)(2,1)} %own_ref.11, bf16[512,14336]{1,0:T(8,128)(2,1)} %collective-permute-done.refs_0_.other_ref, bf16[64,7168]{1,0:T(8,128)(2,1)} %get-tuple-element.70.refs_0_, ...), custom_call_target="tpu_custom_call" | custom-call | flops 1 | bytes 1 | tf_op jit(solution)/shard_map/pallas_call | solution.py:222
  105.2 7.4 %collective-permute-done.12.refs_1_ = bf16[64,7168]{1,0:T(8,128)(2,1)} collective-permute-done((bf16[64,7168]{1,0:T(8,128)(2,1)}, bf16[64,7168]{1,0:T(8,128)(2,1)}, u32[]{:S(2)}, u32[]{:S(2)}) %collective-permute-start.12) | collective-permute-done | bytes 917536 | tf_op jit(solution)/shard_map/ppermute | solution.py:62
  115.0 19.1 %collective-permute-start.15 = (bf16[64,7168]{1,0:T(8,128)(2,1)}, bf16[64,7168]{1,0:T(8,128)(2,1)}, u32[]{:S(2)}, u32[]{:S(2)}) collective-permute-start(bf16[64,7168]{1,0:T(8,128)(2,1)} %get-tuple-element.88.refs_2_), channel_id=1, source_target_pairs={{0,2},{1,3},{2,0},{3,1},{4,6},{5,7},{6,4},{7,5},{8,10},{9,11},{10,... | collective-permute-start | bytes 2752520 | tf_op jit(solution)/shard_map/ppermute | solution.py:62
  134.8 10.8 %shard_map.82 = (f32[1024,256]{1,0:T(8,128)}, s32[1]{0:T(128)}) custom-call(s32[1]{0:T(128)} %get-tuple-element.82.turn_ref, s32[3]{0:T(128)} %concatenate.22.at_ref, bf16[512,14336]{1,0:T(8,128)(2,1)} %own_ref.11, bf16[512,14336]{1,0:T(8,128)(2,1)} %collective-permute-done.refs_0_.other_ref, bf16[64,7168]{1,0:T(8,128)(2,1)} %get-tuple-element.83.refs_0_, ...), custom_call_target="tpu_custom_call" | custom-call | flops 1 | bytes 1 | tf_op jit(solution)/shard_map/pallas_call | solution.py:222
  147.7 2.3 %collective-permute-start.18 = (bf16[64,8192]{1,0:T(8,128)(2,1)}, bf16[64,8192]{1,0:T(8,128)(2,1)}, u32[]{:S(2)}, u32[]{:S(2)}) collective-permute-start(bf16[64,8192]{1,0:T(8,128)(2,1)} %get-tuple-element.93.refs_3_), channel_id=1, source_target_pairs={{0,4},{1,5},{2,6},{3,7},{4,0},{5,1},{6,2},{7,3},{8,12},{9,13},{10,... | collective-permute-start | bytes 3145736 | tf_op jit(solution)/shard_map/ppermute | solution.py:62
  153.1 13.8 %shard_map.84 = (f32[8,256]{1,0:T(8,128)}, s32[1]{0:T(128)}) custom-call(s32[1]{0:T(128)} %get-tuple-element.90.turn_ref, s32[3]{0:T(128)} %broadcast_7_at_ref.2.at_ref, bf16[512,8192]{1,0:T(8,128)(2,1)} %own_ref.10, bf16[512,8192]{1,0:T(8,128)(2,1)} %collective-permute-done.4.refs_1_.other_ref, bf16[64,8192]{1,0:T(8,128)(2,1)} %bitcast.23, ...), custom_call_target="tpu_custom_call" | custom-call | flops 1 | bytes 1 | tf_op jit(solution)/shard_map/pallas_call | solution.py:222
  168.1 1.5 collective-permute-start.21
  170.6 1.9 slice.19
  172.6 1.8 slice.20
  174.9 10.8 %shard_map.86 = (f32[1024,256]{1,0:T(8,128)}, s32[1]{0:T(128)}) custom-call(s32[1]{0:T(128)} %get-tuple-element.102.turn_ref, s32[3]{0:T(128)} %concatenate.21.at_ref, bf16[512,14336]{1,0:T(8,128)(2,1)} %own_ref.11, bf16[512,14336]{1,0:T(8,128)(2,1)} %collective-permute-done.refs_0_.other_ref, bf16[64,7168]{1,0:T(8,128)(2,1)} %get-tuple-element.97.refs_0_, ...), custom_call_target="tpu_custom_call" | custom-call | flops 1 | bytes 1 | tf_op jit(solution)/shard_map/pallas_call | solution.py:222
  185.7 5.1 %collective-permute-done.22.refs_1_ = bf16[64,7168]{1,0:T(8,128)(2,1)} collective-permute-done((bf16[64,7168]{1,0:T(8,128)(2,1)}, bf16[64,7168]{1,0:T(8,128)(2,1)}, u32[]{:S(2)}, u32[]{:S(2)}) %collective-permute-start.22) | collective-permute-done | bytes 917536 | tf_op jit(solution)/shard_map/ppermute | solution.py:66
  190.8 3.5 %collective-permute-start.26 = (f32[8,256]{1,0:T(8,128)S(1)}, f32[8,256]{1,0:T(8,128)S(1)}, u32[]{:S(2)}, u32[]{:S(2)}) collective-permute-start(f32[8,256]{1,0:T(8,128)S(1)} %copy-done), channel_id=1, source_target_pairs={{0,1},{1,0},{2,3},{3,2},{4,5},{5,4},{6,7},{7,6},{8,9},{9,8},{10,11... | collective-permute-start | bytes 24584 | tf_op jit(solution)/shard_map/ppermute | solution.py:62
  195.5 11.7 %shard_map.88 = (f32[1024,256]{1,0:T(8,128)}, s32[1]{0:T(128)}) custom-call(s32[1]{0:T(128)} %get-tuple-element.108.turn_ref, s32[3]{0:T(128)} %broadcast_7_at_ref.2.at_ref, bf16[512,8192]{1,0:T(8,128)(2,1)} %own_ref.10, bf16[512,8192]{1,0:T(8,128)(2,1)} %collective-permute-done.4.refs_1_.other_ref, bf16[64,8192]{1,0:T(8,128)(2,1)} %get-tuple-element.109.refs_0_, ...), custom_call_target="tpu_custom_call" | custom-call | flops 1 | bytes 1 | tf_op jit(solution)/shard_map/pallas_call | solution.py:222
  207.2 12.9 %shard_map.89 = (f32[8,256]{1,0:T(8,128)}, s32[1]{0:T(128)}) custom-call(s32[1]{0:T(128)} %get-tuple-element.112.turn_ref, s32[3]{0:T(128)} %concatenate.22.at_ref, bf16[512,14336]{1,0:T(8,128)(2,1)} %own_ref.11, bf16[512,14336]{1,0:T(8,128)(2,1)} %collective-permute-done.refs_0_.other_ref, bf16[64,7168]{1,0:T(8,128)(2,1)} %get-tuple-element.113.refs_0_, ...), custom_call_target="tpu_custom_call" | custom-call | flops 1 | bytes 1 | tf_op jit(solution)/shard_map/pallas_call | solution.py:222
  220.1 1.2 collective-permute-start.27
  222.4 1.9 fusion.1
  (72 shorter events, 19.8 us)
Async XLA Ops:
  0.0 31.7 %collective-permute-start = (bf16[512,14336]{1,0:T(8,128)(2,1)}, bf16[512,14336]{1,0:T(8,128)(2,1)}, u32[]{:S(2)}, u32[]{:S(2)}) collective-permute-start(bf16[512,14336]{1,0:T(8,128)(2,1)} %own_ref.11), channel_id=1, source_target_pairs={{0,1},{1,0},{2,3},{3,2},{4,5},{5,4},{6,7},{7,6},{8,9},{9,8},{10,11... | collective-permute-start | bytes 44040200 | tf_op jit(solution)/shard_map/ppermute | solution.py:62
  0.7 56.3 %collective-permute-start.4 = (bf16[512,8192]{1,0:T(8,128)(2,1)}, bf16[512,8192]{1,0:T(8,128)(2,1)}, u32[]{:S(2)}, u32[]{:S(2)}) collective-permute-start(bf16[512,8192]{1,0:T(8,128)(2,1)} %own_ref.10), channel_id=1, source_target_pairs={{0,1},{1,0},{2,3},{3,2},{4,5},{5,4},{6,7},{7,6},{8,9},{9,8},{10,11... | collective-permute-start | bytes 25165832 | tf_op jit(solution)/shard_map/ppermute | solution.py:62
  9.3 18.9 %collective-permute-start.1 = (bf16[64,7168]{1,0:T(8,128)(2,1)}, bf16[64,7168]{1,0:T(8,128)(2,1)}, u32[]{:S(2)}, u32[]{:S(2)}) collective-permute-start(bf16[64,7168]{1,0:T(8,128)(2,1)} %get-tuple-element.67.refs_4_), channel_id=1, source_target_pairs={{0,2},{1,3},{2,0},{3,1},{4,6},{5,7},{6,4},{7,5},{8,10},{9,11},{10,... | collective-permute-start | bytes 2752520 | tf_op jit(solution)/shard_map/ppermute | solution.py:62
  10.5 18.8 %collective-permute-start.2 = (bf16[64,7168]{1,0:T(8,128)(2,1)}, bf16[64,7168]{1,0:T(8,128)(2,1)}, u32[]{:S(2)}, u32[]{:S(2)}) collective-permute-start(bf16[64,7168]{1,0:T(8,128)(2,1)} %get-tuple-element.67.refs_4_), channel_id=1, source_target_pairs={{0,4},{1,5},{2,6},{3,7},{4,0},{5,1},{6,2},{7,3},{8,12},{9,13},{10,... | collective-permute-start | bytes 2752520 | tf_op jit(solution)/shard_map/ppermute | solution.py:62
  10.7 21.0 %collective-permute-start.3 = (bf16[64,7168]{1,0:T(8,128)(2,1)}, bf16[64,7168]{1,0:T(8,128)(2,1)}, u32[]{:S(2)}, u32[]{:S(2)}) collective-permute-start(bf16[64,7168]{1,0:T(8,128)(2,1)} %get-tuple-element.67.refs_4_), channel_id=1, source_target_pairs={{4,8},{5,9},{6,10},{7,11},{8,4},{9,5},{10,6},{11,7},{20,24},{21,25... | collective-permute-start | bytes 2752520 | tf_op jit(solution)/shard_map/ppermute | solution.py:158
  28.1 21.6 %collective-permute-start.6 = (bf16[64,8192]{1,0:T(8,128)(2,1)}, bf16[64,8192]{1,0:T(8,128)(2,1)}, u32[]{:S(2)}, u32[]{:S(2)}) collective-permute-start(bf16[64,8192]{1,0:T(8,128)(2,1)} %get-tuple-element.71), channel_id=1, source_target_pairs={{0,2},{1,3},{2,0},{3,1},{4,6},{5,7},{6,4},{7,5},{8,10},{9,11},{10,... | collective-permute-start | bytes 3145736 | tf_op jit(solution)/shard_map/ppermute | solution.py:62
  32.9 24.2 %collective-permute-start.5 = (bf16[64,7168]{1,0:T(8,128)(2,1)}, bf16[64,7168]{1,0:T(8,128)(2,1)}, u32[]{:S(2)}, u32[]{:S(2)}) collective-permute-start(bf16[64,7168]{1,0:T(8,128)(2,1)} %get-tuple-element.70.refs_0_), channel_id=1, source_target_pairs={{0,12},{1,13},{2,14},{3,15},{12,0},{13,1},{14,2},{15,3},{16,28},{1... | collective-permute-start | bytes 2752520 | tf_op jit(solution)/shard_map/ppermute | solution.py:158
  34.5 22.8 %collective-permute-start.7 = (bf16[64,7168]{1,0:T(8,128)(2,1)}, bf16[64,7168]{1,0:T(8,128)(2,1)}, u32[]{:S(2)}, u32[]{:S(2)}) collective-permute-start(bf16[64,7168]{1,0:T(8,128)(2,1)} %get-tuple-element.72.refs_1_), channel_id=1, source_target_pairs={{0,16},{16,0},{1,17},{17,1},{2,18},{18,2},{3,19},{19,3},{4,20},{20... | collective-permute-start | bytes 2752520 | tf_op jit(solution)/shard_map/ppermute | solution.py:66
  36.8 36.0 %collective-permute-start.10 = (bf16[64,7168]{1,0:T(8,128)(2,1)}, bf16[64,7168]{1,0:T(8,128)(2,1)}, u32[]{:S(2)}, u32[]{:S(2)}) collective-permute-start(bf16[64,7168]{1,0:T(8,128)(2,1)} %get-tuple-element.75.refs_2_), channel_id=1, source_target_pairs={{0,16},{16,0},{1,17},{17,1},{2,18},{18,2},{3,19},{19,3},{4,20},{20... | collective-permute-start | bytes 2752520 | tf_op jit(solution)/shard_map/ppermute | solution.py:66
  49.8 23.0 %collective-permute-start.9 = (bf16[64,7168]{1,0:T(8,128)(2,1)}, bf16[64,7168]{1,0:T(8,128)(2,1)}, u32[]{:S(2)}, u32[]{:S(2)}) collective-permute-start(bf16[64,7168]{1,0:T(8,128)(2,1)} %get-tuple-element.75.refs_2_), channel_id=1, source_target_pairs={{0,2},{1,3},{2,0},{3,1},{4,6},{5,7},{6,4},{7,5},{8,10},{9,11},{10,... | collective-permute-start | bytes 2752520 | tf_op jit(solution)/shard_map/ppermute | solution.py:62
  60.4 17.6 %collective-permute-start.8 = (bf16[64,7168]{1,0:T(8,128)(2,1)}, bf16[64,7168]{1,0:T(8,128)(2,1)}, u32[]{:S(2)}, u32[]{:S(2)}) collective-permute-start(bf16[64,7168]{1,0:T(8,128)(2,1)} %get-tuple-element.74.refs_3_), channel_id=1, source_target_pairs={{0,4},{1,5},{2,6},{3,7},{4,0},{5,1},{6,2},{7,3},{8,12},{9,13},{10,... | collective-permute-start | bytes 2752520 | tf_op jit(solution)/shard_map/ppermute | solution.py:62
  79.3 34.5 %collective-permute-start.11 = (bf16[64,8192]{1,0:T(8,128)(2,1)}, bf16[64,8192]{1,0:T(8,128)(2,1)}, u32[]{:S(2)}, u32[]{:S(2)}) collective-permute-start(bf16[64,8192]{1,0:T(8,128)(2,1)} %get-tuple-element.79), channel_id=1, source_target_pairs={{0,4},{1,5},{2,6},{3,7},{4,0},{5,1},{6,2},{7,3},{8,12},{9,13},{10,... | collective-permute-start | bytes 3145736 | tf_op jit(solution)/shard_map/ppermute | solution.py:62
  79.3 33.3 %collective-permute-start.12 = (bf16[64,7168]{1,0:T(8,128)(2,1)}, bf16[64,7168]{1,0:T(8,128)(2,1)}, u32[]{:S(2)}, u32[]{:S(2)}) collective-permute-start(bf16[64,7168]{1,0:T(8,128)(2,1)} %get-tuple-element.74.refs_3_), channel_id=1, source_target_pairs={{0,2},{1,3},{2,0},{3,1},{4,6},{5,7},{6,4},{7,5},{8,10},{9,11},{10,... | collective-permute-start | bytes 2752520 | tf_op jit(solution)/shard_map/ppermute | solution.py:62
  93.9 19.9 %collective-permute-start.13 = (bf16[64,7168]{1,0:T(8,128)(2,1)}, bf16[64,7168]{1,0:T(8,128)(2,1)}, u32[]{:S(2)}, u32[]{:S(2)}) collective-permute-start(bf16[64,7168]{1,0:T(8,128)(2,1)} %get-tuple-element.74.refs_3_), channel_id=1, source_target_pairs={{0,16},{16,0},{1,17},{17,1},{2,18},{18,2},{3,19},{19,3},{4,20},{20... | collective-permute-start | bytes 2752520 | tf_op jit(solution)/shard_map/ppermute | solution.py:66
  93.9 51.6 %collective-permute-start.14 = (bf16[64,8192]{1,0:T(8,128)(2,1)}, bf16[64,8192]{1,0:T(8,128)(2,1)}, u32[]{:S(2)}, u32[]{:S(2)}) collective-permute-start(bf16[64,8192]{1,0:T(8,128)(2,1)} %get-tuple-element.71), channel_id=1, source_target_pairs={{0,12},{1,13},{2,14},{3,15},{4,8},{5,9},{6,10},{7,11},{8,4},{9,5},... | collective-permute-start | bytes 3145736 | tf_op jit(solution)/shard_map/ppermute | solution.py:62
  94.4 40.1 %copy-start.1 = (s32[4]{0:T(128)S(1)}, s32[4]{0:T(128)}, u32[]{:S(2)}) copy-start(s32[4]{0:T(128)} %param.11) | copy-start | bytes 52
  115.0 30.6 %collective-permute-start.15 = (bf16[64,7168]{1,0:T(8,128)(2,1)}, bf16[64,7168]{1,0:T(8,128)(2,1)}, u32[]{:S(2)}, u32[]{:S(2)}) collective-permute-start(bf16[64,7168]{1,0:T(8,128)(2,1)} %get-tuple-element.88.refs_2_), channel_id=1, source_target_pairs={{0,2},{1,3},{2,0},{3,1},{4,6},{5,7},{6,4},{7,5},{8,10},{9,11},{10,... | collective-permute-start | bytes 2752520 | tf_op jit(solution)/shard_map/ppermute | solution.py:62
  134.0 12.6 %collective-permute-start.16 = (bf16[64,7168]{1,0:T(8,128)(2,1)}, bf16[64,7168]{1,0:T(8,128)(2,1)}, u32[]{:S(2)}, u32[]{:S(2)}) collective-permute-start(bf16[64,7168]{1,0:T(8,128)(2,1)} %get-tuple-element.88.refs_2_), channel_id=1, source_target_pairs={{0,16},{16,0},{1,17},{17,1},{2,18},{18,2},{3,19},{19,3},{4,20},{20... | collective-permute-start | bytes 2752520 | tf_op jit(solution)/shard_map/ppermute | solution.py:66
  134.7 15.3 %copy-start.2 = (s32[4]{0:T(128)S(1)}, s32[4]{0:T(128)}, u32[]{:S(2)}) copy-start(s32[4]{0:T(128)} %param.12) | copy-start | bytes 52
  134.7 15.9 %copy-start.3 = (s32[8]{0:T(128)S(1)}, s32[8]{0:T(128)}, u32[]{:S(2)}) copy-start(s32[8]{0:T(128)} %constant.51.clone) | copy-start | bytes 100
  147.7 19.1 %collective-permute-start.18 = (bf16[64,8192]{1,0:T(8,128)(2,1)}, bf16[64,8192]{1,0:T(8,128)(2,1)}, u32[]{:S(2)}, u32[]{:S(2)}) collective-permute-start(bf16[64,8192]{1,0:T(8,128)(2,1)} %get-tuple-element.93.refs_3_), channel_id=1, source_target_pairs={{0,4},{1,5},{2,6},{3,7},{4,0},{5,1},{6,2},{7,3},{8,12},{9,13},{10,... | collective-permute-start | bytes 3145736 | tf_op jit(solution)/shard_map/ppermute | solution.py:62
  150.0 16.9 %collective-permute-start.19 = (bf16[64,8192]{1,0:T(8,128)(2,1)}, bf16[64,8192]{1,0:T(8,128)(2,1)}, u32[]{:S(2)}, u32[]{:S(2)}) collective-permute-start(bf16[64,8192]{1,0:T(8,128)(2,1)} %get-tuple-element.93.refs_3_), channel_id=1, source_target_pairs={{0,2},{1,3},{2,0},{3,1},{4,6},{5,7},{6,4},{7,5},{8,10},{9,11},{10,... | collective-permute-start | bytes 3145736 | tf_op jit(solution)/shard_map/ppermute | solution.py:62
  150.1 16.8 %collective-permute-start.20 = (bf16[64,7168]{1,0:T(8,128)(2,1)}, bf16[64,7168]{1,0:T(8,128)(2,1)}, u32[]{:S(2)}, u32[]{:S(2)}) collective-permute-start(bf16[64,7168]{1,0:T(8,128)(2,1)} %get-tuple-element.97.refs_0_), channel_id=1, source_target_pairs={{0,16},{16,0},{1,17},{17,1},{2,18},{18,2},{3,19},{19,3},{4,20},{20... | collective-permute-start | bytes 2752520 | tf_op jit(solution)/shard_map/ppermute | solution.py:66
  150.7 1.2 collective-permute-start.17
  168.1 26.2 %collective-permute-start.21 = (bf16[64,8192]{1,0:T(8,128)(2,1)}, bf16[64,8192]{1,0:T(8,128)(2,1)}, u32[]{:S(2)}, u32[]{:S(2)}) collective-permute-start(bf16[64,8192]{1,0:T(8,128)(2,1)} %get-tuple-element.106.refs_2_), channel_id=1, source_target_pairs={{0,2},{1,3},{2,0},{3,1},{4,6},{5,7},{6,4},{7,5},{8,10},{9,11},{10,... | collective-permute-start | bytes 3145736 | tf_op jit(solution)/shard_map/ppermute | solution.py:62
  169.6 24.7 %collective-permute-start.23 = (bf16[64,8192]{1,0:T(8,128)(2,1)}, bf16[64,8192]{1,0:T(8,128)(2,1)}, u32[]{:S(2)}, u32[]{:S(2)}) collective-permute-start(bf16[64,8192]{1,0:T(8,128)(2,1)} %get-tuple-element.107), channel_id=1, source_target_pairs={{0,4},{1,5},{2,6},{3,7},{4,0},{5,1},{6,2},{7,3},{8,12},{9,13},{10,... | collective-permute-start | bytes 3145736 | tf_op jit(solution)/shard_map/ppermute | solution.py:62
  169.6 21.1 %collective-permute-start.22 = (bf16[64,7168]{1,0:T(8,128)(2,1)}, bf16[64,7168]{1,0:T(8,128)(2,1)}, u32[]{:S(2)}, u32[]{:S(2)}) collective-permute-start(bf16[64,7168]{1,0:T(8,128)(2,1)} %get-tuple-element.103.refs_1_), channel_id=1, source_target_pairs={{0,16},{16,0},{1,17},{17,1},{2,18},{18,2},{3,19},{19,3},{4,20},{20... | collective-permute-start | bytes 2752520 | tf_op jit(solution)/shard_map/ppermute | solution.py:66
  172.5 34.7 %collective-permute-start.24 = (bf16[32,7168]{1,0:T(8,128)(2,1)}, bf16[32,7168]{1,0:T(8,128)(2,1)}, u32[]{:S(2)}, u32[]{:S(2)}) collective-permute-start(bf16[32,7168]{1,0:T(8,128)(2,1)} %slice.19), channel_id=1, source_target_pairs={{0,2},{1,3},{2,0},{3,1},{4,6},{5,7},{6,4},{7,5},{8,10},{9,11},{10,... | collective-permute-start | bytes 1376264 | tf_op jit(solution)/shard_map/ppermute | solution.py:62
  174.4 32.8 %collective-permute-start.25 = (bf16[32,7168]{1,0:T(8,128)(2,1)}, bf16[32,7168]{1,0:T(8,128)(2,1)}, u32[]{:S(2)}, u32[]{:S(2)}) collective-permute-start(bf16[32,7168]{1,0:T(8,128)(2,1)} %slice.20), channel_id=1, source_target_pairs={{0,16},{16,0},{1,17},{17,1},{2,18},{18,2},{3,19},{19,3},{4,20},{20... | collective-permute-start | bytes 1376264 | tf_op jit(solution)/shard_map/ppermute | solution.py:66
  174.9 15.9 %copy-start = (f32[8,256]{1,0:T(8,128)S(1)}, f32[8,256]{1,0:T(8,128)}, u32[]{:S(2)}) copy-start(f32[8,256]{1,0:T(8,128)} %get-tuple-element.101) | copy-start | bytes 24580
  190.8 30.6 %collective-permute-start.26 = (f32[8,256]{1,0:T(8,128)S(1)}, f32[8,256]{1,0:T(8,128)S(1)}, u32[]{:S(2)}, u32[]{:S(2)}) collective-permute-start(f32[8,256]{1,0:T(8,128)S(1)} %copy-done), channel_id=1, source_target_pairs={{0,1},{1,0},{2,3},{3,2},{4,5},{5,4},{6,7},{7,6},{8,9},{9,8},{10,11... | collective-permute-start | bytes 24584 | tf_op jit(solution)/shard_map/ppermute | solution.py:62
  220.1 2.3 %collective-permute-start.27 = (f32[8,256]{1,0:T(8,128)}, f32[8,256]{1,0:T(8,128)S(1)}, u32[]{:S(2)}, u32[]{:S(2)}) collective-permute-start(f32[8,256]{1,0:T(8,128)} %get-tuple-element.118), channel_id=1, source_target_pairs={{0,1},{1,0},{2,3},{3,2},{4,5},{5,4},{6,7},{7,6},{8,9},{9,8},{10,11... | collective-permute-start | bytes 24584 | tf_op jit(solution)/shard_map/ppermute | solution.py:62

commit v16 on v15

--- a/solution.py
+++ b/solution.py
@@ -259,8 +259,7 @@
     send = functools.partial(flip, count=count)
 
     acts_there = send(hidden_acts, CORE)
-    spans_here = spans_of(bucket_ids, seq_lengths)
-    spans = jnp.concatenate([spans_here, send(spans_here, CORE)], axis=1)
+    sizes_there = send(jnp.concatenate([bucket_ids, seq_lengths]), CORE)
 
     a, b, c = {}, {}, {}
     a["own"] = lax.dynamic_slice_in_dim(left, group * half, half, 1)
@@ -315,11 +314,13 @@
 
     core = (me & CORE).reshape(1).astype(jnp.int32)
     copies = (1 - mine, left, b["own"])
-    turn, made, (a["own"],) = prepare(zero, core, *copies, None, [a["own"]])
+    turn, made, (a["own"], sizes_there) = prepare(zero, core, *copies, None, [a["own"], sizes_there])
     a["x"] = over_x(a["own"])
     a["n"] = near(a["own"])
     a_mid = middle(a["own"])
     turn, (c["own"], b_one, b_two), _ = prepare(turn, 1 - core, *copies, made, [])
+    spans = [spans_of(bucket_ids, seq_lengths), spans_of(*jnp.split(sizes_there, 2))]
+    spans = jnp.concatenate(spans, axis=1)
 
     turn, (a["x"], a["n"], a_mid, a["own"]) = after(
         turn, [a["x"], a["n"], a_mid, a["own"]], inside, None, [acts_there]

time: 226 us -> 244 us (1.080)
  waiting for transfers between devices: 58.4 us -> 67.5 us
  starting transfers between devices: 62.6 us -> 69.1 us
    ppermute x19, waiting for transfers between devices: 37.5 us -> 56.2 us  [flip(): return lax.ppermute(array, 'dp', [(i, i ^ code) for i in range(count)])]
    ppermute x7, waiting for transfers between devices: 18.5 us -> 9.06 us  [swap_groups(): return lax.ppermute(array, 'groups', [(0, 1), (1, 0)])]
    ppermute x19, starting transfers between devices: 53.1 us -> 56.9 us  [flip(): return lax.ppermute(array, 'dp', [(i, i ^ code) for i in range(count)])]
    ppermute x7, starting transfers between devices: 3.55 us -> 6.21 us  [swap_groups(): return lax.ppermute(array, 'groups', [(0, 1), (1, 0)])]
  transfers between devices with their start and end apart: 28 -> 28, of which waited for: 11 -> 13; matrix products, arithmetic and copies ran while one was open for 5% -> 5% of each run, Pallas kernels for 39% -> 36%
where the time goes in v16:
time: 244 us; the launch traced here: 241 us
  Pallas kernels  91 us (37%)
  starting transfers between devices  69.1 us (28%)
  waiting for transfers between devices  67.5 us (28%)
  local copies, waits for them, and re-layouts  8.97 us (4%)
  other arithmetic  2.74 us (1%)
    pallas_call x6, Pallas kernels, proj(): pl.pallas_call(functools.partial(proj_kernel, len(pieces), last), out_sha...  70.8 us
    ppermute x19, starting transfers between devices, flip(): return lax.ppermute(array, 'dp', [(i, i ^ code) for i in range(count)])  56.9 us
    ppermute x19, waiting for transfers between devices, flip(): return lax.ppermute(array, 'dp', [(i, i ^ code) for i in range(count)])  56.2 us
    pallas_call x9, Pallas kernels, after(): pl.pallas_call(functools.partial(after_kernel, count, merge is not None),...  12.5 us
    ppermute x7, waiting for transfers between devices, swap_groups(): return lax.ppermute(array, 'groups', [(0, 1), (1, 0)])  9.06 us
    pallas_call x2, Pallas kernels, prepare(): pl.pallas_call(prepare_kernel, out_shape=[jax.ShapeDtypeStruct(x.shape, x...  7.71 us
    ppermute x7, starting transfers between devices, swap_groups(): return lax.ppermute(array, 'groups', [(0, 1), (1, 0)])  6.21 us
    ppermute x2, starting transfers between devices, lines(): lax.ppermute(array, 'dp', [(a * 4 + rest, b * 4 + rest) for a, b in pairs...  5.93 us
  transfers between devices with their start and end apart: 28, of which 13 were waited for; matrix products, arithmetic and copies ran while one was open for 5% of the time, Pallas kernels for 36%

profile of v16, /device:TPU:9, one launch (start us, length us, event | category | flops | bytes accessed | tf_op | source)
XLA Modules:
  0.0 241.4 jit_solution(743290592914873536)
XLA Ops:
  1.9 2.2 constant_dynamic-slice_fusion.refs_0_
  4.1 9.9 %collective-permute-done.refs_1_ = s32[8]{0:T(128)S(1)} collective-permute-done((s32[8]{0:T(128)S(1)}, s32[8]{0:T(128)S(1)}, u32[]{:S(2)}, u32[]{:S(2)}) %collective-permute-start) | collective-permute-done | bytes 64 | tf_op jit(solution)/shard_map/ppermute | solution.py:62
  14.6 6.4 %shard_map.73 = (bf16[64,7168]{1,0:T(8,128)(2,1)}, s32[8]{0:T(128)}, bf16[64,7168]{1,0:T(8,128)(2,1)}, bf16[64,8192]{1,0:T(8,128)(2,1)}, bf16[64,8192]{1,0:T(8,128)(2,1)}, /*index=5*/s32[1]{0:T(128)}) custom-call(s32[1]{0:T(128)} %bitcast.1.works_ref, s32[1]{0:T(128)} %constant.24.clone.1.turn_ref, ...), custom_call_target="tpu_custom_call", output_to_operand_aliasing={{0}: (5, {}), {1}: (6, {})} | custom-call | flops 1 | bytes 1 | tf_op jit(solution)/shard_map/pallas_call | solution.py:141
  22.4 4.3 %collective-permute-start.4 = (bf16[64,7168]{1,0:T(8,128)(2,1)}, bf16[64,7168]{1,0:T(8,128)(2,1)}, u32[]{:S(2)}, u32[]{:S(2)}) collective-permute-start(bf16[64,7168]{1,0:T(8,128)(2,1)} %get-tuple-element.68.refs_4_), channel_id=1, source_target_pairs={{4,8},{5,9},{6,10},{7,11},{8,4},{9,5},{10,6},{11,7},{20,24},{21,25... | collective-permute-start | bytes 2752520 | tf_op jit(solution)/shard_map/ppermute | solution.py:158
  26.8 1.3 shard_map.74
  28.1 11.8 %collective-permute-done.2.refs_1_ = bf16[64,7168]{1,0:T(8,128)(2,1)} collective-permute-done((bf16[64,7168]{1,0:T(8,128)(2,1)}, bf16[64,7168]{1,0:T(8,128)(2,1)}, u32[]{:S(2)}, u32[]{:S(2)}) %collective-permute-start.2) | collective-permute-done | bytes 917536 | tf_op jit(solution)/shard_map/ppermute | solution.py:62
  41.1 2.2 collective-permute-done.4.refs_3_
  44.4 1.6 collective-permute-start.6
  48.4 18.7 %collective-permute-start.10 = (bf16[64,7168]{1,0:T(8,128)(2,1)}, bf16[64,7168]{1,0:T(8,128)(2,1)}, u32[]{:S(2)}, u32[]{:S(2)}) collective-permute-start(bf16[64,7168]{1,0:T(8,128)(2,1)} %get-tuple-element.76.refs_2_), channel_id=1, source_target_pairs={{0,2},{1,3},{2,0},{3,1},{4,6},{5,7},{6,4},{7,5},{8,10},{9,11},{10,... | collective-permute-start | bytes 2752520 | tf_op jit(solution)/shard_map/ppermute | solution.py:62
  67.1 1.5 collective-permute-start.11
  68.6 3.2 %shard_map.77 = (bf16[64,7168]{1,0:T(8,128)(2,1)}, bf16[64,8192]{1,0:T(8,128)(2,1)}, bf16[64,7168]{1,0:T(8,128)(2,1)}, s32[1]{0:T(128)}) custom-call(s32[1]{0:T(128)} %bitcast.inside_ref, s32[1]{0:T(128)} %shard_map.76.turn_ref, bf16[64,7168]{1,0:T(8,128)(2,1)} %get-tuple-element.70.refs_0_, ...), custom_call_target="tpu_custom_call", output_to_operand_aliasing={{0}: (4, {}), {1}: (5, {}), {2}: (6, {})} | custom-call | flops 1 | bytes 1 | tf_op jit(solution)/shard_map/pallas_call | solution.py:106
  73.0 7.5 %collective-permute-done.10.refs_1_ = bf16[64,7168]{1,0:T(8,128)(2,1)} collective-permute-done((bf16[64,7168]{1,0:T(8,128)(2,1)}, bf16[64,7168]{1,0:T(8,128)(2,1)}, u32[]{:S(2)}, u32[]{:S(2)}) %collective-permute-start.10) | collective-permute-done | bytes 917536 | tf_op jit(solution)/shard_map/ppermute | solution.py:62
  80.6 3.6 %collective-permute-done.11.refs_2_ = bf16[64,7168]{1,0:T(8,128)(2,1)} collective-permute-done((bf16[64,7168]{1,0:T(8,128)(2,1)}, bf16[64,7168]{1,0:T(8,128)(2,1)}, u32[]{:S(2)}, u32[]{:S(2)}) %collective-permute-start.11) | collective-permute-done | bytes 917536 | tf_op jit(solution)/shard_map/ppermute | solution.py:66
  84.1 5.3 %collective-permute-done.9.refs_0_ = bf16[64,7168]{1,0:T(8,128)(2,1)} collective-permute-done((bf16[64,7168]{1,0:T(8,128)(2,1)}, bf16[64,7168]{1,0:T(8,128)(2,1)}, u32[]{:S(2)}, u32[]{:S(2)}) %collective-permute-start.9) | collective-permute-done | bytes 917536 | tf_op jit(solution)/shard_map/ppermute | solution.py:62
  90.7 27.3 %collective-permute-start.13 = (bf16[64,7168]{1,0:T(8,128)(2,1)}, bf16[64,7168]{1,0:T(8,128)(2,1)}, u32[]{:S(2)}, u32[]{:S(2)}) collective-permute-start(bf16[64,7168]{1,0:T(8,128)(2,1)} %get-tuple-element.75.refs_3_), channel_id=1, source_target_pairs={{0,2},{1,3},{2,0},{3,1},{4,6},{5,7},{6,4},{7,5},{8,10},{9,11},{10,... | collective-permute-start | bytes 2752520 | tf_op jit(solution)/shard_map/ppermute | solution.py:62
  118.6 10.8 %shard_map.80 = (f32[1024,256]{1,0:T(8,128)}, s32[1]{0:T(128)}) custom-call(s32[1]{0:T(128)} %get-tuple-element.78.turn_ref, s32[3]{0:T(128)} %concatenate.25.at_ref, bf16[512,14336]{1,0:T(8,128)(2,1)} %own_ref.11, bf16[512,14336]{1,0:T(8,128)(2,1)} %collective-permute-done.1.refs_0_.other_ref, bf16[64,7168]{1,0:T(8,128)(2,1)} %get-tuple-element.71.refs_0_, ...), custom_call_target="tpu_custom_call" | custom-call | flops 1 | bytes 1 | tf_op jit(solution)/shard_map/pallas_call | solution.py:222
  129.4 9.6 %collective-permute-done.13.refs_1_ = bf16[64,7168]{1,0:T(8,128)(2,1)} collective-permute-done((bf16[64,7168]{1,0:T(8,128)(2,1)}, bf16[64,7168]{1,0:T(8,128)(2,1)}, u32[]{:S(2)}, u32[]{:S(2)}) %collective-permute-start.13) | collective-permute-done | bytes 917536 | tf_op jit(solution)/shard_map/ppermute | solution.py:62
  139.1 1.3 collective-permute-done.14.refs_2_
  144.2 10.8 %shard_map.82 = (f32[1024,256]{1,0:T(8,128)}, s32[1]{0:T(128)}) custom-call(s32[1]{0:T(128)} %get-tuple-element.83.turn_ref, s32[3]{0:T(128)} %concatenate.26.at_ref, bf16[512,14336]{1,0:T(8,128)(2,1)} %own_ref.11, bf16[512,14336]{1,0:T(8,128)(2,1)} %collective-permute-done.1.refs_0_.other_ref, bf16[64,7168]{1,0:T(8,128)(2,1)} %get-tuple-element.84.refs_0_, ...), custom_call_target="tpu_custom_call" | custom-call | flops 1 | bytes 1 | tf_op jit(solution)/shard_map/pallas_call | solution.py:222
  155.0 7.8 %collective-permute-done.16.refs_1_ = bf16[64,7168]{1,0:T(8,128)(2,1)} collective-permute-done((bf16[64,7168]{1,0:T(8,128)(2,1)}, bf16[64,7168]{1,0:T(8,128)(2,1)}, u32[]{:S(2)}, u32[]{:S(2)}) %collective-permute-start.16) | collective-permute-done | bytes 917536 | tf_op jit(solution)/shard_map/ppermute | solution.py:62
  164.9 2.7 %collective-permute-start.18 = (bf16[64,8192]{1,0:T(8,128)(2,1)}, bf16[64,8192]{1,0:T(8,128)(2,1)}, u32[]{:S(2)}, u32[]{:S(2)}) collective-permute-start(bf16[64,8192]{1,0:T(8,128)(2,1)} %get-tuple-element.94.refs_3_), channel_id=1, source_target_pairs={{0,4},{1,5},{2,6},{3,7},{4,0},{5,1},{6,2},{7,3},{8,12},{9,13},{10,... | collective-permute-start | bytes 3145736 | tf_op jit(solution)/shard_map/ppermute | solution.py:62
  172.0 13.8 %shard_map.84 = (f32[8,256]{1,0:T(8,128)}, s32[1]{0:T(128)}) custom-call(s32[1]{0:T(128)} %get-tuple-element.91.turn_ref, s32[3]{0:T(128)} %broadcast_7_at_ref.2.at_ref, bf16[512,8192]{1,0:T(8,128)(2,1)} %own_ref.10, bf16[512,8192]{1,0:T(8,128)(2,1)} %collective-permute-done.5.refs_1_.other_ref, bf16[64,8192]{1,0:T(8,128)(2,1)} %bitcast.35, ...), custom_call_target="tpu_custom_call" | custom-call | flops 1 | bytes 1 | tf_op jit(solution)/shard_map/pallas_call | solution.py:222
  185.8 3.1 %collective-permute-done.20.refs_2_ = bf16[64,7168]{1,0:T(8,128)(2,1)} collective-permute-done((bf16[64,7168]{1,0:T(8,128)(2,1)}, bf16[64,7168]{1,0:T(8,128)(2,1)}, u32[]{:S(2)}, u32[]{:S(2)}) %collective-permute-start.20) | collective-permute-done | bytes 917536 | tf_op jit(solution)/shard_map/ppermute | solution.py:66
  188.9 3.9 %collective-permute-done.19.refs_1_ = bf16[64,8192]{1,0:T(8,128)(2,1)} collective-permute-done((bf16[64,8192]{1,0:T(8,128)(2,1)}, bf16[64,8192]{1,0:T(8,128)(2,1)}, u32[]{:S(2)}, u32[]{:S(2)}) %collective-permute-start.19) | collective-permute-done | bytes 1048608 | tf_op jit(solution)/shard_map/ppermute | solution.py:62
  194.7 1.5 collective-permute-start.22
  196.2 1.9 slice.19
  198.0 1.3 collective-permute-start.24
  199.3 1.8 slice.20
  201.2 10.8 %shard_map.86 = (f32[1024,256]{1,0:T(8,128)}, s32[1]{0:T(128)}) custom-call(s32[1]{0:T(128)} %get-tuple-element.104.turn_ref, s32[3]{0:T(128)} %concatenate.25.at_ref, bf16[512,14336]{1,0:T(8,128)(2,1)} %own_ref.11, bf16[512,14336]{1,0:T(8,128)(2,1)} %collective-permute-done.1.refs_0_.other_ref, bf16[64,7168]{1,0:T(8,128)(2,1)} %get-tuple-element.99.refs_0_, ...), custom_call_target="tpu_custom_call" | custom-call | flops 1 | bytes 1 | tf_op jit(solution)/shard_map/pallas_call | solution.py:222
  213.3 11.7 %shard_map.88 = (f32[1024,256]{1,0:T(8,128)}, s32[1]{0:T(128)}) custom-call(s32[1]{0:T(128)} %get-tuple-element.110.turn_ref, s32[3]{0:T(128)} %broadcast_7_at_ref.2.at_ref, bf16[512,8192]{1,0:T(8,128)(2,1)} %own_ref.10, bf16[512,8192]{1,0:T(8,128)(2,1)} %collective-permute-done.5.refs_1_.other_ref, bf16[64,8192]{1,0:T(8,128)(2,1)} %get-tuple-element.111.refs_0_, ...), custom_call_target="tpu_custom_call" | custom-call | flops 1 | bytes 1 | tf_op jit(solution)/shard_map/pallas_call | solution.py:222
  225.0 13.0 %shard_map.89 = (f32[8,256]{1,0:T(8,128)}, s32[1]{0:T(128)}) custom-call(s32[1]{0:T(128)} %get-tuple-element.114.turn_ref, s32[3]{0:T(128)} %concatenate.26.at_ref, bf16[512,14336]{1,0:T(8,128)(2,1)} %own_ref.11, bf16[512,14336]{1,0:T(8,128)(2,1)} %collective-permute-done.1.refs_0_.other_ref, bf16[64,7168]{1,0:T(8,128)(2,1)} %get-tuple-element.115.refs_0_, ...), custom_call_target="tpu_custom_call" | custom-call | flops 1 | bytes 1 | tf_op jit(solution)/shard_map/pallas_call | solution.py:222
  239.5 1.9 fusion.1
  (79 shorter events, 26.6 us)
Async XLA Ops:
  0.0 43.2 %collective-permute-start.1 = (bf16[512,14336]{1,0:T(8,128)(2,1)}, bf16[512,14336]{1,0:T(8,128)(2,1)}, u32[]{:S(2)}, u32[]{:S(2)}) collective-permute-start(bf16[512,14336]{1,0:T(8,128)(2,1)} %own_ref.11), channel_id=1, source_target_pairs={{0,1},{1,0},{2,3},{3,2},{4,5},{5,4},{6,7},{7,6},{8,9},{9,8},{10,11... | collective-permute-start | bytes 44040200 | tf_op jit(solution)/shard_map/ppermute | solution.py:62
  0.7 67.9 %collective-permute-start.5 = (bf16[512,8192]{1,0:T(8,128)(2,1)}, bf16[512,8192]{1,0:T(8,128)(2,1)}, u32[]{:S(2)}, u32[]{:S(2)}) collective-permute-start(bf16[512,8192]{1,0:T(8,128)(2,1)} %own_ref.10), channel_id=1, source_target_pairs={{0,1},{1,0},{2,3},{3,2},{4,5},{5,4},{6,7},{7,6},{8,9},{9,8},{10,11... | collective-permute-start | bytes 25165832 | tf_op jit(solution)/shard_map/ppermute | solution.py:62
  1.4 12.6 %collective-permute-start = (s32[8]{0:T(128)S(1)}, s32[8]{0:T(128)S(1)}, u32[]{:S(2)}, u32[]{:S(2)}) collective-permute-start(s32[8]{0:T(128)S(1)} %pad_add_fusion), channel_id=1, source_target_pairs={{0,1},{1,0},{2,3},{3,2},{4,5},{5,4},{6,7},{7,6},{8,9},{9,8},{10,11... | collective-permute-start | bytes 104 | tf_op jit(solution)/shard_map/ppermute | solution.py:62
  21.0 18.9 %collective-permute-start.2 = (bf16[64,7168]{1,0:T(8,128)(2,1)}, bf16[64,7168]{1,0:T(8,128)(2,1)}, u32[]{:S(2)}, u32[]{:S(2)}) collective-permute-start(bf16[64,7168]{1,0:T(8,128)(2,1)} %get-tuple-element.68.refs_4_), channel_id=1, source_target_pairs={{0,2},{1,3},{2,0},{3,1},{4,6},{5,7},{6,4},{7,5},{8,10},{9,11},{10,... | collective-permute-start | bytes 2752520 | tf_op jit(solution)/shard_map/ppermute | solution.py:62
  22.3 18.8 %collective-permute-start.3 = (bf16[64,7168]{1,0:T(8,128)(2,1)}, bf16[64,7168]{1,0:T(8,128)(2,1)}, u32[]{:S(2)}, u32[]{:S(2)}) collective-permute-start(bf16[64,7168]{1,0:T(8,128)(2,1)} %get-tuple-element.68.refs_4_), channel_id=1, source_target_pairs={{0,4},{1,5},{2,6},{3,7},{4,0},{5,1},{6,2},{7,3},{8,12},{9,13},{10,... | collective-permute-start | bytes 2752520 | tf_op jit(solution)/shard_map/ppermute | solution.py:62
  22.4 20.8 %collective-permute-start.4 = (bf16[64,7168]{1,0:T(8,128)(2,1)}, bf16[64,7168]{1,0:T(8,128)(2,1)}, u32[]{:S(2)}, u32[]{:S(2)}) collective-permute-start(bf16[64,7168]{1,0:T(8,128)(2,1)} %get-tuple-element.68.refs_4_), channel_id=1, source_target_pairs={{4,8},{5,9},{6,10},{7,11},{8,4},{9,5},{10,6},{11,7},{20,24},{21,25... | collective-permute-start | bytes 2752520 | tf_op jit(solution)/shard_map/ppermute | solution.py:158
  39.8 27.2 %collective-permute-start.7 = (bf16[64,8192]{1,0:T(8,128)(2,1)}, bf16[64,8192]{1,0:T(8,128)(2,1)}, u32[]{:S(2)}, u32[]{:S(2)}) collective-permute-start(bf16[64,8192]{1,0:T(8,128)(2,1)} %get-tuple-element.72), channel_id=1, source_target_pairs={{0,2},{1,3},{2,0},{3,1},{4,6},{5,7},{6,4},{7,5},{8,10},{9,11},{10,... | collective-permute-start | bytes 3145736 | tf_op jit(solution)/shard_map/ppermute | solution.py:62
  44.4 24.1 %collective-permute-start.6 = (bf16[64,7168]{1,0:T(8,128)(2,1)}, bf16[64,7168]{1,0:T(8,128)(2,1)}, u32[]{:S(2)}, u32[]{:S(2)}) collective-permute-start(bf16[64,7168]{1,0:T(8,128)(2,1)} %get-tuple-element.71.refs_0_), channel_id=1, source_target_pairs={{0,12},{1,13},{2,14},{3,15},{12,0},{13,1},{14,2},{15,3},{16,28},{1... | collective-permute-start | bytes 2752520 | tf_op jit(solution)/shard_map/ppermute | solution.py:158
  46.0 22.6 %collective-permute-start.8 = (bf16[64,7168]{1,0:T(8,128)(2,1)}, bf16[64,7168]{1,0:T(8,128)(2,1)}, u32[]{:S(2)}, u32[]{:S(2)}) collective-permute-start(bf16[64,7168]{1,0:T(8,128)(2,1)} %get-tuple-element.73.refs_1_), channel_id=1, source_target_pairs={{0,16},{16,0},{1,17},{17,1},{2,18},{18,2},{3,19},{19,3},{4,20},{20... | collective-permute-start | bytes 2752520 | tf_op jit(solution)/shard_map/ppermute | solution.py:66
  48.4 32.2 %collective-permute-start.10 = (bf16[64,7168]{1,0:T(8,128)(2,1)}, bf16[64,7168]{1,0:T(8,128)(2,1)}, u32[]{:S(2)}, u32[]{:S(2)}) collective-permute-start(bf16[64,7168]{1,0:T(8,128)(2,1)} %get-tuple-element.76.refs_2_), channel_id=1, source_target_pairs={{0,2},{1,3},{2,0},{3,1},{4,6},{5,7},{6,4},{7,5},{8,10},{9,11},{10,... | collective-permute-start | bytes 2752520 | tf_op jit(solution)/shard_map/ppermute | solution.py:62
  67.1 17.0 %collective-permute-start.11 = (bf16[64,7168]{1,0:T(8,128)(2,1)}, bf16[64,7168]{1,0:T(8,128)(2,1)}, u32[]{:S(2)}, u32[]{:S(2)}) collective-permute-start(bf16[64,7168]{1,0:T(8,128)(2,1)} %get-tuple-element.76.refs_2_), channel_id=1, source_target_pairs={{0,16},{16,0},{1,17},{17,1},{2,18},{18,2},{3,19},{19,3},{4,20},{20... | collective-permute-start | bytes 2752520 | tf_op jit(solution)/shard_map/ppermute | solution.py:66
  71.8 17.6 %collective-permute-start.9 = (bf16[64,7168]{1,0:T(8,128)(2,1)}, bf16[64,7168]{1,0:T(8,128)(2,1)}, u32[]{:S(2)}, u32[]{:S(2)}) collective-permute-start(bf16[64,7168]{1,0:T(8,128)(2,1)} %get-tuple-element.75.refs_3_), channel_id=1, source_target_pairs={{0,4},{1,5},{2,6},{3,7},{4,0},{5,1},{6,2},{7,3},{8,12},{9,13},{10,... | collective-permute-start | bytes 2752520 | tf_op jit(solution)/shard_map/ppermute | solution.py:62
  90.6 49.8 %collective-permute-start.12 = (bf16[64,8192]{1,0:T(8,128)(2,1)}, bf16[64,8192]{1,0:T(8,128)(2,1)}, u32[]{:S(2)}, u32[]{:S(2)}) collective-permute-start(bf16[64,8192]{1,0:T(8,128)(2,1)} %get-tuple-element.80), channel_id=1, source_target_pairs={{0,4},{1,5},{2,6},{3,7},{4,0},{5,1},{6,2},{7,3},{8,12},{9,13},{10,... | collective-permute-start | bytes 3145736 | tf_op jit(solution)/shard_map/ppermute | solution.py:62
  90.7 48.4 %collective-permute-start.13 = (bf16[64,7168]{1,0:T(8,128)(2,1)}, bf16[64,7168]{1,0:T(8,128)(2,1)}, u32[]{:S(2)}, u32[]{:S(2)}) collective-permute-start(bf16[64,7168]{1,0:T(8,128)(2,1)} %get-tuple-element.75.refs_3_), channel_id=1, source_target_pairs={{0,2},{1,3},{2,0},{3,1},{4,6},{5,7},{6,4},{7,5},{8,10},{9,11},{10,... | collective-permute-start | bytes 2752520 | tf_op jit(solution)/shard_map/ppermute | solution.py:62
  118.0 22.4 %collective-permute-start.14 = (bf16[64,7168]{1,0:T(8,128)(2,1)}, bf16[64,7168]{1,0:T(8,128)(2,1)}, u32[]{:S(2)}, u32[]{:S(2)}) collective-permute-start(bf16[64,7168]{1,0:T(8,128)(2,1)} %get-tuple-element.75.refs_3_), channel_id=1, source_target_pairs={{0,16},{16,0},{1,17},{17,1},{2,18},{18,2},{3,19},{19,3},{4,20},{20... | collective-permute-start | bytes 2752520 | tf_op jit(solution)/shard_map/ppermute | solution.py:66
  118.1 36.9 %collective-permute-start.15 = (bf16[64,8192]{1,0:T(8,128)(2,1)}, bf16[64,8192]{1,0:T(8,128)(2,1)}, u32[]{:S(2)}, u32[]{:S(2)}) collective-permute-start(bf16[64,8192]{1,0:T(8,128)(2,1)} %get-tuple-element.72), channel_id=1, source_target_pairs={{0,12},{1,13},{2,14},{3,15},{4,8},{5,9},{6,10},{7,11},{8,4},{9,5},... | collective-permute-start | bytes 3145736 | tf_op jit(solution)/shard_map/ppermute | solution.py:62
  118.6 25.4 %copy-start.5 = (s32[8]{0:T(128)S(1)}, s32[8]{0:T(128)}, u32[]{:S(2)}) copy-start(s32[8]{0:T(128)} %constant.52.clone) | copy-start | bytes 100
  141.6 21.2 %collective-permute-start.16 = (bf16[64,7168]{1,0:T(8,128)(2,1)}, bf16[64,7168]{1,0:T(8,128)(2,1)}, u32[]{:S(2)}, u32[]{:S(2)}) collective-permute-start(bf16[64,7168]{1,0:T(8,128)(2,1)} %get-tuple-element.89.refs_2_), channel_id=1, source_target_pairs={{0,2},{1,3},{2,0},{3,1},{4,6},{5,7},{6,4},{7,5},{8,10},{9,11},{10,... | collective-permute-start | bytes 2752520 | tf_op jit(solution)/shard_map/ppermute | solution.py:62
  142.6 21.2 %collective-permute-start.17 = (bf16[64,7168]{1,0:T(8,128)(2,1)}, bf16[64,7168]{1,0:T(8,128)(2,1)}, u32[]{:S(2)}, u32[]{:S(2)}) collective-permute-start(bf16[64,7168]{1,0:T(8,128)(2,1)} %get-tuple-element.89.refs_2_), channel_id=1, source_target_pairs={{0,16},{16,0},{1,17},{17,1},{2,18},{18,2},{3,19},{19,3},{4,20},{20... | collective-permute-start | bytes 2752520 | tf_op jit(solution)/shard_map/ppermute | solution.py:66
  144.1 24.1 %copy-start.4 = (s32[4]{0:T(128)S(1)}, s32[4]{0:T(128)}, u32[]{:S(2)}) copy-start(s32[4]{0:T(128)} %param.11) | copy-start | bytes 52
  144.2 25.6 %copy-start.3 = (s32[4]{0:T(128)S(1)}, s32[4]{0:T(128)}, u32[]{:S(2)}) copy-start(s32[4]{0:T(128)} %param.12) | copy-start | bytes 52
  144.2 26.3 %copy-start.1 = (s32[8]{0:T(128)S(1)}, s32[8]{0:T(128)}, u32[]{:S(2)}) copy-start(s32[8]{0:T(128)} %get-tuple-element.95) | copy-start | bytes 100
  164.9 23.9 %collective-permute-start.18 = (bf16[64,8192]{1,0:T(8,128)(2,1)}, bf16[64,8192]{1,0:T(8,128)(2,1)}, u32[]{:S(2)}, u32[]{:S(2)}) collective-permute-start(bf16[64,8192]{1,0:T(8,128)(2,1)} %get-tuple-element.94.refs_3_), channel_id=1, source_target_pairs={{0,4},{1,5},{2,6},{3,7},{4,0},{5,1},{6,2},{7,3},{8,12},{9,13},{10,... | collective-permute-start | bytes 3145736 | tf_op jit(solution)/shard_map/ppermute | solution.py:62
  167.6 25.2 %collective-permute-start.19 = (bf16[64,8192]{1,0:T(8,128)(2,1)}, bf16[64,8192]{1,0:T(8,128)(2,1)}, u32[]{:S(2)}, u32[]{:S(2)}) collective-permute-start(bf16[64,8192]{1,0:T(8,128)(2,1)} %get-tuple-element.94.refs_3_), channel_id=1, source_target_pairs={{0,2},{1,3},{2,0},{3,1},{4,6},{5,7},{6,4},{7,5},{8,10},{9,11},{10,... | collective-permute-start | bytes 3145736 | tf_op jit(solution)/shard_map/ppermute | solution.py:62
  168.7 20.1 %collective-permute-start.20 = (bf16[64,7168]{1,0:T(8,128)(2,1)}, bf16[64,7168]{1,0:T(8,128)(2,1)}, u32[]{:S(2)}, u32[]{:S(2)}) collective-permute-start(bf16[64,7168]{1,0:T(8,128)(2,1)} %get-tuple-element.99.refs_0_), channel_id=1, source_target_pairs={{0,16},{16,0},{1,17},{17,1},{2,18},{18,2},{3,19},{19,3},{4,20},{20... | collective-permute-start | bytes 2752520 | tf_op jit(solution)/shard_map/ppermute | solution.py:66
  194.0 18.1 %collective-permute-start.21 = (bf16[64,8192]{1,0:T(8,128)(2,1)}, bf16[64,8192]{1,0:T(8,128)(2,1)}, u32[]{:S(2)}, u32[]{:S(2)}) collective-permute-start(bf16[64,8192]{1,0:T(8,128)(2,1)} %get-tuple-element.108.refs_2_), channel_id=1, source_target_pairs={{0,2},{1,3},{2,0},{3,1},{4,6},{5,7},{6,4},{7,5},{8,10},{9,11},{10,... | collective-permute-start | bytes 3145736 | tf_op jit(solution)/shard_map/ppermute | solution.py:62
  194.7 17.4 %collective-permute-start.23 = (bf16[64,8192]{1,0:T(8,128)(2,1)}, bf16[64,8192]{1,0:T(8,128)(2,1)}, u32[]{:S(2)}, u32[]{:S(2)}) collective-permute-start(bf16[64,8192]{1,0:T(8,128)(2,1)} %get-tuple-element.109), channel_id=1, source_target_pairs={{0,4},{1,5},{2,6},{3,7},{4,0},{5,1},{6,2},{7,3},{8,12},{9,13},{10,... | collective-permute-start | bytes 3145736 | tf_op jit(solution)/shard_map/ppermute | solution.py:62
  194.7 17.3 %collective-permute-start.22 = (bf16[64,7168]{1,0:T(8,128)(2,1)}, bf16[64,7168]{1,0:T(8,128)(2,1)}, u32[]{:S(2)}, u32[]{:S(2)}) collective-permute-start(bf16[64,7168]{1,0:T(8,128)(2,1)} %get-tuple-element.105.refs_1_), channel_id=1, source_target_pairs={{0,16},{16,0},{1,17},{17,1},{2,18},{18,2},{3,19},{19,3},{4,20},{20... | collective-permute-start | bytes 2752520 | tf_op jit(solution)/shard_map/ppermute | solution.py:66
  198.0 27.0 %collective-permute-start.24 = (bf16[32,7168]{1,0:T(8,128)(2,1)}, bf16[32,7168]{1,0:T(8,128)(2,1)}, u32[]{:S(2)}, u32[]{:S(2)}) collective-permute-start(bf16[32,7168]{1,0:T(8,128)(2,1)} %slice.19), channel_id=1, source_target_pairs={{0,2},{1,3},{2,0},{3,1},{4,6},{5,7},{6,4},{7,5},{8,10},{9,11},{10,... | collective-permute-start | bytes 1376264 | tf_op jit(solution)/shard_map/ppermute | solution.py:62
  201.2 23.8 %collective-permute-start.25 = (bf16[32,7168]{1,0:T(8,128)(2,1)}, bf16[32,7168]{1,0:T(8,128)(2,1)}, u32[]{:S(2)}, u32[]{:S(2)}) collective-permute-start(bf16[32,7168]{1,0:T(8,128)(2,1)} %slice.20), channel_id=1, source_target_pairs={{0,16},{16,0},{1,17},{17,1},{2,18},{18,2},{3,19},{19,3},{4,20},{20... | collective-permute-start | bytes 1376264 | tf_op jit(solution)/shard_map/ppermute | solution.py:66
  212.0 26.5 %collective-permute-start.26 = (f32[8,256]{1,0:T(8,128)S(1)}, f32[8,256]{1,0:T(8,128)S(1)}, u32[]{:S(2)}, u32[]{:S(2)}) collective-permute-start(f32[8,256]{1,0:T(8,128)S(1)} %copy-done.2), channel_id=1, source_target_pairs={{0,1},{1,0},{2,3},{3,2},{4,5},{5,4},{6,7},{7,6},{8,9},{9,8},{10,11... | collective-permute-start | bytes 24584 | tf_op jit(solution)/shard_map/ppermute | solution.py:62
  238.0 1.6 collective-permute-start.27
  (2 other events, 11.4 us)

commit v17 on v14

--- a/solution.py
+++ b/solution.py
@@ -55,7 +55,7 @@
 
 CORE, COLUMN, NEAR, ACROSS, OPPOSITE = 1, 2, 4, 12, 8
 LITTLE = pl.CostEstimate(flops=1, bytes_accessed=1, transcendentals=0)
-VMEM_LIMIT = 127 * 512 * 1024
+VMEM_LIMIT = 255 * 256 * 1024
 
 
 def flip(array, code, count):
@@ -308,12 +308,12 @@
     core = (me & CORE).reshape(1).astype(jnp.int32)
     copies = (1 - mine, left, b["own"])
     turn, made, (a["own"],) = prepare(zero, core, *copies, None, [a["own"]])
+    a["x"] = over_x(a["own"])
+    a["n"] = near(a["own"])
     a_mid = middle(a["own"])
-    a["n"] = near(a["own"])
-    a["x"] = over_x(a["own"])
     turn, (c["own"], b_one, b_two), _ = prepare(turn, 1 - core, *copies, made, [])
 
-    turn, (a_mid, a["n"], a["x"]) = after(turn, [a_mid, a["n"], a["x"]], inside, None, [acts_there])
+    turn, (a["x"], a["n"], a_mid) = after(turn, [a["x"], a["n"], a_mid], inside, None, [acts_there])
     a_out = outward(a_mid)
     a_in = middle(a["n"])
     b["x"] = over_x(b_one)
@@ -329,7 +329,8 @@
     a["xo"] = over_x(a["o"])
     turn = pause(turn)
 
-    turn, (a["f"], a["xn"], c["n"], b_two) = after(turn, [a_last, a["xn"], c["n"], b_two], inside, a_mid)
+    turn, (a_last, a["xn"], c["n"], b_two) = after(turn, [a_last, a["xn"], c["n"], b_two], inside)
+    turn, (a["f"],) = after(turn, [a_last], inside, a_mid)
     b["n"] = near(b_two)
     a["xf"] = over_x(a["f"])
     c["f"] = swap_groups(a["f"])

time: 218 us -> 224 us (1.028)
  waiting for transfers between devices: 70.5 us -> 80.7 us
  other arithmetic: 3.55 us -> 1 us
    ppermute x7, waiting for transfers between devices: 13 us -> 24.1 us  [swap_groups(): return lax.ppermute(array, 'groups', [(0, 1), (1, 0)])]
    ppermute x4, waiting for transfers between devices: 16.5 us -> 8.12 us  [lines(): lax.ppermute(array, 'dp', [(a * 4 + rest, b * 4 + rest) for a, b in pairs...]
    ppermute x17, waiting for transfers between devices: 41.1 us -> 48.5 us  [flip(): return lax.ppermute(array, 'dp', [(i, i ^ code) for i in range(count)])]
    pallas_call x10 -> x11, Pallas kernels: 15.5 us -> 16.7 us  [after(): pl.pallas_call(functools.partial(after_kernel, count, merge is not None),...]
  transfers between devices with their start and end apart: 28 -> 28, of which waited for: 19 -> 15; matrix products, arithmetic and copies ran while one was open for 6% -> 4% of each run, Pallas kernels for 35% -> 35%
where the time goes in v17:
time: 224 us; the launch traced here: 222 us
  Pallas kernels  95 us (42%)
  waiting for transfers between devices  80.7 us (36%)
  starting transfers between devices  35 us (16%)
  local copies, waits for them, and re-layouts  9.29 us (4%)
    pallas_call x6, Pallas kernels, proj(): pl.pallas_call(functools.partial(proj_kernel, len(pieces), last), out_sha...  70.7 us
    ppermute x17, waiting for transfers between devices, flip(): return lax.ppermute(array, 'dp', [(i, i ^ code) for i in range(count)])  48.5 us
    ppermute x7, waiting for transfers between devices, swap_groups(): return lax.ppermute(array, 'groups', [(0, 1), (1, 0)])  24.1 us
    pallas_call x11, Pallas kernels, after(): pl.pallas_call(functools.partial(after_kernel, count, merge is not None),...  16.7 us
    ppermute x17, starting transfers between devices, flip(): return lax.ppermute(array, 'dp', [(i, i ^ code) for i in range(count)])  13.7 us
    ppermute x4, starting transfers between devices, lines(): lax.ppermute(array, 'dp', [(a * 4 + rest, b * 4 + rest) for a, b in pairs...  12.4 us
    ppermute x7, starting transfers between devices, swap_groups(): return lax.ppermute(array, 'groups', [(0, 1), (1, 0)])  8.82 us
    ppermute x4, waiting for transfers between devices, lines(): lax.ppermute(array, 'dp', [(a * 4 + rest, b * 4 + rest) for a, b in pairs...  8.12 us
  transfers between devices with their start and end apart: 28, of which 15 were waited for; matrix products, arithmetic and copies ran while one was open for 4% of the time, Pallas kernels for 35%

profile of v17, /device:TPU:9, one launch (start us, length us, event | category | flops | bytes accessed | tf_op | source)
XLA Modules:
  0.0 222.0 jit_solution(5510816240428033141)
XLA Ops:
  0.7 2.2 constant_dynamic-slice_fusion.refs_0_
  2.9 6.4 %shard_map.73 = (bf16[64,7168]{1,0:T(8,128)(2,1)}, bf16[64,7168]{1,0:T(8,128)(2,1)}, bf16[64,8192]{1,0:T(8,128)(2,1)}, bf16[64,8192]{1,0:T(8,128)(2,1)}, s32[1]{0:T(128)}) custom-call(s32[1]{0:T(128)} %bitcast.1.works_ref, s32[1]{0:T(128)} %constant.24.clone.1.turn_ref, s32[1]{0:T(128)S(6)} %sub.17.first_ref, ...), custom_call_target="tpu_custom_call", output_to_operand_aliasing={{0}: (5, {})} | custom-call | flops 1 | bytes 1 | tf_op jit(solution)/shard_map/pallas_call | solution.py:141
  10.7 4.3 %collective-permute-start.3 = (bf16[64,7168]{1,0:T(8,128)(2,1)}, bf16[64,7168]{1,0:T(8,128)(2,1)}, u32[]{:S(2)}, u32[]{:S(2)}) collective-permute-start(bf16[64,7168]{1,0:T(8,128)(2,1)} %get-tuple-element.70.refs_0_), channel_id=1, source_target_pairs={{4,8},{5,9},{6,10},{7,11},{8,4},{9,5},{10,6},{11,7},{20,24},{21,25... | collective-permute-start | bytes 2752520 | tf_op jit(solution)/shard_map/ppermute | solution.py:158
  16.3 11.8 %collective-permute-done.1.refs_1_ = bf16[64,7168]{1,0:T(8,128)(2,1)} collective-permute-done((bf16[64,7168]{1,0:T(8,128)(2,1)}, bf16[64,7168]{1,0:T(8,128)(2,1)}, u32[]{:S(2)}, u32[]{:S(2)}) %collective-permute-start.1) | collective-permute-done | bytes 917536 | tf_op jit(solution)/shard_map/ppermute | solution.py:62
  29.4 2.4 %collective-permute-done.3.refs_3_ = bf16[64,7168]{1,0:T(8,128)(2,1)} collective-permute-done((bf16[64,7168]{1,0:T(8,128)(2,1)}, bf16[64,7168]{1,0:T(8,128)(2,1)}, u32[]{:S(2)}, u32[]{:S(2)}) %collective-permute-start.3) | collective-permute-done | bytes 917536 | tf_op jit(solution)/shard_map/ppermute | solution.py:158
  32.9 2.2 %collective-permute-start.5 = (bf16[64,7168]{1,0:T(8,128)(2,1)}, bf16[64,7168]{1,0:T(8,128)(2,1)}, u32[]{:S(2)}, u32[]{:S(2)}) collective-permute-start(bf16[64,7168]{1,0:T(8,128)(2,1)} %get-tuple-element.72.refs_0_), channel_id=1, source_target_pairs={{4,0},{5,1},{6,2},{7,3},{8,12},{9,13},{10,14},{11,15},{20,16},{21,... | collective-permute-start | bytes 2752520 | tf_op jit(solution)/shard_map/ppermute | solution.py:158
  35.1 3.6 %collective-permute-start.7 = (bf16[64,7168]{1,0:T(8,128)(2,1)}, bf16[64,7168]{1,0:T(8,128)(2,1)}, u32[]{:S(2)}, u32[]{:S(2)}) collective-permute-start(bf16[64,7168]{1,0:T(8,128)(2,1)} %get-tuple-element.74.refs_2_), channel_id=1, source_target_pairs={{4,8},{5,9},{6,10},{7,11},{8,4},{9,5},{10,6},{11,7},{20,24},{21,25... | collective-permute-start | bytes 2752520 | tf_op jit(solution)/shard_map/ppermute | solution.py:158
  41.2 8.5 %collective-permute-done.6.refs_2_ = bf16[64,8192]{1,0:T(8,128)(2,1)} collective-permute-done((bf16[64,8192]{1,0:T(8,128)(2,1)}, bf16[64,8192]{1,0:T(8,128)(2,1)}, u32[]{:S(2)}, u32[]{:S(2)}) %collective-permute-start.6) | collective-permute-done | bytes 1048608 | tf_op jit(solution)/shard_map/ppermute | solution.py:62
  52.2 4.0 %collective-permute-done.7.refs_3_ = bf16[64,7168]{1,0:T(8,128)(2,1)} collective-permute-done((bf16[64,7168]{1,0:T(8,128)(2,1)}, bf16[64,7168]{1,0:T(8,128)(2,1)}, u32[]{:S(2)}, u32[]{:S(2)}) %collective-permute-start.7) | collective-permute-done | bytes 917536 | tf_op jit(solution)/shard_map/ppermute | solution.py:158
  56.2 5.4 %collective-permute-done.8.refs_4_ = bf16[64,7168]{1,0:T(8,128)(2,1)} collective-permute-done((bf16[64,7168]{1,0:T(8,128)(2,1)}, bf16[64,7168]{1,0:T(8,128)(2,1)}, u32[]{:S(2)}, u32[]{:S(2)}) %collective-permute-start.8) | collective-permute-done | bytes 917536 | tf_op jit(solution)/shard_map/ppermute | solution.py:66
  62.8 2.2 %collective-permute-start.9 = (bf16[64,7168]{1,0:T(8,128)(2,1)}, bf16[64,7168]{1,0:T(8,128)(2,1)}, u32[]{:S(2)}, u32[]{:S(2)}) collective-permute-start(bf16[64,7168]{1,0:T(8,128)(2,1)} %get-tuple-element.77.refs_0_), channel_id=1, source_target_pairs={{4,0},{5,1},{6,2},{7,3},{8,12},{9,13},{10,14},{11,15},{20,16},{21,... | collective-permute-start | bytes 2752520 | tf_op jit(solution)/shard_map/ppermute | solution.py:158
  65.0 3.2 %shard_map.78 = (bf16[64,7168]{1,0:T(8,128)(2,1)}, s32[1]{0:T(128)}) custom-call(s32[1]{0:T(128)} %bitcast.inside_ref, s32[1]{0:T(128)} %get-tuple-element.76.turn_ref, bf16[64,7168]{1,0:T(8,128)(2,1)} %get-tuple-element.77.refs_0_, bf16[64,7168]{1,0:T(8,128)(2,1)} %get-tuple-element.78.refs_1_), custom_call_target="tpu_custom_call", output_to_operand_aliasing={{0}: (3, {})} | custom-call | flops 1 | bytes 1 | tf_op jit(solution)/shard_map/pallas_call | solution.py:106
  69.4 8.3 %collective-permute-done.11.refs_2_ = bf16[64,7168]{1,0:T(8,128)(2,1)} collective-permute-done((bf16[64,7168]{1,0:T(8,128)(2,1)}, bf16[64,7168]{1,0:T(8,128)(2,1)}, u32[]{:S(2)}, u32[]{:S(2)}) %collective-permute-start.11) | collective-permute-done | bytes 917536 | tf_op jit(solution)/shard_map/ppermute | solution.py:66
  77.7 1.7 collective-permute-done.9.refs_0_
  80.6 2.3 %collective-permute-start.12 = (bf16[64,8192]{1,0:T(8,128)(2,1)}, bf16[64,8192]{1,0:T(8,128)(2,1)}, u32[]{:S(2)}, u32[]{:S(2)}) collective-permute-start(bf16[64,8192]{1,0:T(8,128)(2,1)} %get-tuple-element.86), channel_id=1, source_target_pairs={{0,4},{1,5},{2,6},{3,7},{4,0},{5,1},{6,2},{7,3},{8,12},{9,13},{10,... | collective-permute-start | bytes 3145736 | tf_op jit(solution)/shard_map/ppermute | solution.py:62
  83.1 3.2 %shard_map.81 = (bf16[64,7168]{1,0:T(8,128)(2,1)}, s32[1]{0:T(128)}) custom-call(s32[1]{0:T(128)} %bitcast.inside_ref, s32[1]{0:T(128)} %get-tuple-element.81.turn_ref, bf16[64,7168]{1,0:T(8,128)(2,1)} %get-tuple-element.72.refs_0_, bf16[64,7168]{1,0:T(8,128)(2,1)} %get-tuple-element.82.refs_1_), custom_call_target="tpu_custom_call", output_to_operand_aliasing={{0}: (3, {})} | custom-call | flops 1 | bytes 1 | tf_op jit(solution)/shard_map/pallas_call | solution.py:106
  89.4 10.8 %shard_map.82 = (f32[1024,256]{1,0:T(8,128)}, s32[1]{0:T(128)}) custom-call(s32[1]{0:T(128)} %get-tuple-element.83.turn_ref, s32[3]{0:T(128)} %concatenate.25.at_ref, bf16[512,14336]{1,0:T(8,128)(2,1)} %own_ref.11, bf16[512,14336]{1,0:T(8,128)(2,1)} %collective-permute-done.refs_0_.other_ref, bf16[64,7168]{1,0:T(8,128)(2,1)} %get-tuple-element.70.refs_0_, ...), custom_call_target="tpu_custom_call" | custom-call | flops 1 | bytes 1 | tf_op jit(solution)/shard_map/pallas_call | solution.py:222
  100.1 5.5 %collective-permute-done.13.refs_1_ = bf16[64,7168]{1,0:T(8,128)(2,1)} collective-permute-done((bf16[64,7168]{1,0:T(8,128)(2,1)}, bf16[64,7168]{1,0:T(8,128)(2,1)}, u32[]{:S(2)}, u32[]{:S(2)}) %collective-permute-start.13) | collective-permute-done | bytes 917536 | tf_op jit(solution)/shard_map/ppermute | solution.py:62
  105.6 17.9 %collective-permute-done.12.refs_0_ = bf16[64,8192]{1,0:T(8,128)(2,1)} collective-permute-done((bf16[64,8192]{1,0:T(8,128)(2,1)}, bf16[64,8192]{1,0:T(8,128)(2,1)}, u32[]{:S(2)}, u32[]{:S(2)}) %collective-permute-start.12) | collective-permute-done | bytes 1048608 | tf_op jit(solution)/shard_map/ppermute | solution.py:62
  126.6 10.8 %shard_map.84 = (f32[1024,256]{1,0:T(8,128)}, s32[1]{0:T(128)}) custom-call(s32[1]{0:T(128)} %get-tuple-element.89.turn_ref, s32[3]{0:T(128)} %concatenate.26.at_ref, bf16[512,14336]{1,0:T(8,128)(2,1)} %own_ref.11, bf16[512,14336]{1,0:T(8,128)(2,1)} %collective-permute-done.refs_0_.other_ref, bf16[64,7168]{1,0:T(8,128)(2,1)} %get-tuple-element.90.refs_0_, ...), custom_call_target="tpu_custom_call" | custom-call | flops 1 | bytes 1 | tf_op jit(solution)/shard_map/pallas_call | solution.py:222
  137.4 6.0 %collective-permute-done.17.refs_2_ = bf16[64,7168]{1,0:T(8,128)(2,1)} collective-permute-done((bf16[64,7168]{1,0:T(8,128)(2,1)}, bf16[64,7168]{1,0:T(8,128)(2,1)}, u32[]{:S(2)}, u32[]{:S(2)}) %collective-permute-start.17) | collective-permute-done | bytes 917536 | tf_op jit(solution)/shard_map/ppermute | solution.py:66
  144.6 2.1 collective-permute-start.19
  147.0 2.2 collective-permute-start.21
  151.8 13.8 %shard_map.86 = (f32[8,256]{1,0:T(8,128)}, s32[1]{0:T(128)}) custom-call(s32[1]{0:T(128)} %get-tuple-element.97.turn_ref, s32[3]{0:T(128)} %broadcast_8_at_ref.2.at_ref, bf16[512,8192]{1,0:T(8,128)(2,1)} %own_ref.10, bf16[512,8192]{1,0:T(8,128)(2,1)} %collective-permute-done.4.refs_0_.other_ref, bf16[64,8192]{1,0:T(8,128)(2,1)} %bitcast.22, ...), custom_call_target="tpu_custom_call" | custom-call | flops 1 | bytes 1 | tf_op jit(solution)/shard_map/pallas_call | solution.py:222
  168.1 1.8 slice.19
  170.2 1.8 slice.20
  172.0 1.5 collective-permute-start.26
  174.3 10.9 %shard_map.88 = (f32[1024,256]{1,0:T(8,128)}, s32[1]{0:T(128)}) custom-call(s32[1]{0:T(128)} %get-tuple-element.107.turn_ref, s32[3]{0:T(128)} %concatenate.25.at_ref, bf16[512,14336]{1,0:T(8,128)(2,1)} %own_ref.11, bf16[512,14336]{1,0:T(8,128)(2,1)} %collective-permute-done.refs_0_.other_ref, bf16[64,7168]{1,0:T(8,128)(2,1)} %get-tuple-element.108.refs_0_, ...), custom_call_target="tpu_custom_call" | custom-call | flops 1 | bytes 1 | tf_op jit(solution)/shard_map/pallas_call | solution.py:222
  185.2 4.4 %collective-permute-done.23.refs_1_ = bf16[64,7168]{1,0:T(8,128)(2,1)} collective-permute-done((bf16[64,7168]{1,0:T(8,128)(2,1)}, bf16[64,7168]{1,0:T(8,128)(2,1)}, u32[]{:S(2)}, u32[]{:S(2)}) %collective-permute-start.23) | collective-permute-done | bytes 917536 | tf_op jit(solution)/shard_map/ppermute | solution.py:66
  189.5 2.1 collective-permute-done.22.refs_0_
  193.7 11.6 %shard_map.90 = (f32[1024,256]{1,0:T(8,128)}, s32[1]{0:T(128)}) custom-call(s32[1]{0:T(128)} %get-tuple-element.113.turn_ref, s32[3]{0:T(128)} %broadcast_8_at_ref.2.at_ref, bf16[512,8192]{1,0:T(8,128)(2,1)} %own_ref.10, bf16[512,8192]{1,0:T(8,128)(2,1)} %collective-permute-done.4.refs_0_.other_ref, bf16[64,8192]{1,0:T(8,128)(2,1)} %get-tuple-element.114.refs_0_, ...), custom_call_target="tpu_custom_call" | custom-call | flops 1 | bytes 1 | tf_op jit(solution)/shard_map/pallas_call | solution.py:222
  205.3 12.9 %shard_map.91 = (f32[8,256]{1,0:T(8,128)}, s32[1]{0:T(128)}) custom-call(s32[1]{0:T(128)} %get-tuple-element.117.turn_ref, s32[3]{0:T(128)} %concatenate.26.at_ref, bf16[512,14336]{1,0:T(8,128)(2,1)} %own_ref.11, bf16[512,14336]{1,0:T(8,128)(2,1)} %collective-permute-done.refs_0_.other_ref, bf16[64,7168]{1,0:T(8,128)(2,1)} %get-tuple-element.118.refs_0_, ...), custom_call_target="tpu_custom_call" | custom-call | flops 1 | bytes 1 | tf_op jit(solution)/shard_map/pallas_call | solution.py:222
  (70 shorter events, 33.8 us)
Async XLA Ops:
  0.0 31.7 %collective-permute-start = (bf16[512,14336]{1,0:T(8,128)(2,1)}, bf16[512,14336]{1,0:T(8,128)(2,1)}, u32[]{:S(2)}, u32[]{:S(2)}) collective-permute-start(bf16[512,14336]{1,0:T(8,128)(2,1)} %own_ref.11), channel_id=1, source_target_pairs={{0,1},{1,0},{2,3},{3,2},{4,5},{5,4},{6,7},{7,6},{8,9},{9,8},{10,11... | collective-permute-start | bytes 44040200 | tf_op jit(solution)/shard_map/ppermute | solution.py:62
  0.7 50.3 %collective-permute-start.4 = (bf16[512,8192]{1,0:T(8,128)(2,1)}, bf16[512,8192]{1,0:T(8,128)(2,1)}, u32[]{:S(2)}, u32[]{:S(2)}) collective-permute-start(bf16[512,8192]{1,0:T(8,128)(2,1)} %own_ref.10), channel_id=1, source_target_pairs={{0,1},{1,0},{2,3},{3,2},{4,5},{5,4},{6,7},{7,6},{8,9},{9,8},{10,11... | collective-permute-start | bytes 25165832 | tf_op jit(solution)/shard_map/ppermute | solution.py:62
  9.3 18.9 %collective-permute-start.1 = (bf16[64,7168]{1,0:T(8,128)(2,1)}, bf16[64,7168]{1,0:T(8,128)(2,1)}, u32[]{:S(2)}, u32[]{:S(2)}) collective-permute-start(bf16[64,7168]{1,0:T(8,128)(2,1)} %get-tuple-element.70.refs_0_), channel_id=1, source_target_pairs={{0,2},{1,3},{2,0},{3,1},{4,6},{5,7},{6,4},{7,5},{8,10},{9,11},{10,... | collective-permute-start | bytes 2752520 | tf_op jit(solution)/shard_map/ppermute | solution.py:62
  10.6 18.8 %collective-permute-start.2 = (bf16[64,7168]{1,0:T(8,128)(2,1)}, bf16[64,7168]{1,0:T(8,128)(2,1)}, u32[]{:S(2)}, u32[]{:S(2)}) collective-permute-start(bf16[64,7168]{1,0:T(8,128)(2,1)} %get-tuple-element.70.refs_0_), channel_id=1, source_target_pairs={{0,4},{1,5},{2,6},{3,7},{4,0},{5,1},{6,2},{7,3},{8,12},{9,13},{10,... | collective-permute-start | bytes 2752520 | tf_op jit(solution)/shard_map/ppermute | solution.py:62
  10.7 21.0 %collective-permute-start.3 = (bf16[64,7168]{1,0:T(8,128)(2,1)}, bf16[64,7168]{1,0:T(8,128)(2,1)}, u32[]{:S(2)}, u32[]{:S(2)}) collective-permute-start(bf16[64,7168]{1,0:T(8,128)(2,1)} %get-tuple-element.70.refs_0_), channel_id=1, source_target_pairs={{4,8},{5,9},{6,10},{7,11},{8,4},{9,5},{10,6},{11,7},{20,24},{21,25... | collective-permute-start | bytes 2752520 | tf_op jit(solution)/shard_map/ppermute | solution.py:158
  28.1 21.6 %collective-permute-start.6 = (bf16[64,8192]{1,0:T(8,128)(2,1)}, bf16[64,8192]{1,0:T(8,128)(2,1)}, u32[]{:S(2)}, u32[]{:S(2)}) collective-permute-start(bf16[64,8192]{1,0:T(8,128)(2,1)} %get-tuple-element.73), channel_id=1, source_target_pairs={{0,2},{1,3},{2,0},{3,1},{4,6},{5,7},{6,4},{7,5},{8,10},{9,11},{10,... | collective-permute-start | bytes 3145736 | tf_op jit(solution)/shard_map/ppermute | solution.py:62
  32.9 19.3 %collective-permute-start.5 = (bf16[64,7168]{1,0:T(8,128)(2,1)}, bf16[64,7168]{1,0:T(8,128)(2,1)}, u32[]{:S(2)}, u32[]{:S(2)}) collective-permute-start(bf16[64,7168]{1,0:T(8,128)(2,1)} %get-tuple-element.72.refs_0_), channel_id=1, source_target_pairs={{4,0},{5,1},{6,2},{7,3},{8,12},{9,13},{10,14},{11,15},{20,16},{21,... | collective-permute-start | bytes 2752520 | tf_op jit(solution)/shard_map/ppermute | solution.py:158
  35.1 21.1 %collective-permute-start.7 = (bf16[64,7168]{1,0:T(8,128)(2,1)}, bf16[64,7168]{1,0:T(8,128)(2,1)}, u32[]{:S(2)}, u32[]{:S(2)}) collective-permute-start(bf16[64,7168]{1,0:T(8,128)(2,1)} %get-tuple-element.74.refs_2_), channel_id=1, source_target_pairs={{4,8},{5,9},{6,10},{7,11},{8,4},{9,5},{10,6},{11,7},{20,24},{21,25... | collective-permute-start | bytes 2752520 | tf_op jit(solution)/shard_map/ppermute | solution.py:158
  38.8 22.8 %collective-permute-start.8 = (bf16[64,7168]{1,0:T(8,128)(2,1)}, bf16[64,7168]{1,0:T(8,128)(2,1)}, u32[]{:S(2)}, u32[]{:S(2)}) collective-permute-start(bf16[64,7168]{1,0:T(8,128)(2,1)} %get-tuple-element.75.refs_1_), channel_id=1, source_target_pairs={{0,16},{16,0},{1,17},{17,1},{2,18},{18,2},{3,19},{19,3},{4,20},{20... | collective-permute-start | bytes 2752520 | tf_op jit(solution)/shard_map/ppermute | solution.py:66
  49.8 19.6 %collective-permute-start.10 = (bf16[64,7168]{1,0:T(8,128)(2,1)}, bf16[64,7168]{1,0:T(8,128)(2,1)}, u32[]{:S(2)}, u32[]{:S(2)}) collective-permute-start(bf16[64,7168]{1,0:T(8,128)(2,1)} %get-tuple-element.74.refs_2_), channel_id=1, source_target_pairs={{0,2},{1,3},{2,0},{3,1},{4,6},{5,7},{6,4},{7,5},{8,10},{9,11},{10,... | collective-permute-start | bytes 2752520 | tf_op jit(solution)/shard_map/ppermute | solution.py:62
  51.0 26.7 %collective-permute-start.11 = (bf16[64,7168]{1,0:T(8,128)(2,1)}, bf16[64,7168]{1,0:T(8,128)(2,1)}, u32[]{:S(2)}, u32[]{:S(2)}) collective-permute-start(bf16[64,7168]{1,0:T(8,128)(2,1)} %get-tuple-element.74.refs_2_), channel_id=1, source_target_pairs={{0,16},{16,0},{1,17},{17,1},{2,18},{18,2},{3,19},{19,3},{4,20},{20... | collective-permute-start | bytes 2752520 | tf_op jit(solution)/shard_map/ppermute | solution.py:66
  62.8 16.7 %collective-permute-start.9 = (bf16[64,7168]{1,0:T(8,128)(2,1)}, bf16[64,7168]{1,0:T(8,128)(2,1)}, u32[]{:S(2)}, u32[]{:S(2)}) collective-permute-start(bf16[64,7168]{1,0:T(8,128)(2,1)} %get-tuple-element.77.refs_0_), channel_id=1, source_target_pairs={{4,0},{5,1},{6,2},{7,3},{8,12},{9,13},{10,14},{11,15},{20,16},{21,... | collective-permute-start | bytes 2752520 | tf_op jit(solution)/shard_map/ppermute | solution.py:158
  80.6 43.0 %collective-permute-start.12 = (bf16[64,8192]{1,0:T(8,128)(2,1)}, bf16[64,8192]{1,0:T(8,128)(2,1)}, u32[]{:S(2)}, u32[]{:S(2)}) collective-permute-start(bf16[64,8192]{1,0:T(8,128)(2,1)} %get-tuple-element.86), channel_id=1, source_target_pairs={{0,4},{1,5},{2,6},{3,7},{4,0},{5,1},{6,2},{7,3},{8,12},{9,13},{10,... | collective-permute-start | bytes 3145736 | tf_op jit(solution)/shard_map/ppermute | solution.py:62
  82.8 22.8 %collective-permute-start.13 = (bf16[64,7168]{1,0:T(8,128)(2,1)}, bf16[64,7168]{1,0:T(8,128)(2,1)}, u32[]{:S(2)}, u32[]{:S(2)}) collective-permute-start(bf16[64,7168]{1,0:T(8,128)(2,1)} %get-tuple-element.87.refs_3_), channel_id=1, source_target_pairs={{0,2},{1,3},{2,0},{3,1},{4,6},{5,7},{6,4},{7,5},{8,10},{9,11},{10,... | collective-permute-start | bytes 2752520 | tf_op jit(solution)/shard_map/ppermute | solution.py:62
  86.3 19.3 %collective-permute-start.14 = (bf16[64,7168]{1,0:T(8,128)(2,1)}, bf16[64,7168]{1,0:T(8,128)(2,1)}, u32[]{:S(2)}, u32[]{:S(2)}) collective-permute-start(bf16[64,7168]{1,0:T(8,128)(2,1)} %get-tuple-element.84.refs_3_), channel_id=1, source_target_pairs={{0,16},{16,0},{1,17},{17,1},{2,18},{18,2},{3,19},{19,3},{4,20},{20... | collective-permute-start | bytes 2752520 | tf_op jit(solution)/shard_map/ppermute | solution.py:66
  87.6 49.8 %collective-permute-start.15 = (bf16[64,8192]{1,0:T(8,128)(2,1)}, bf16[64,8192]{1,0:T(8,128)(2,1)}, u32[]{:S(2)}, u32[]{:S(2)}) collective-permute-start(bf16[64,8192]{1,0:T(8,128)(2,1)} %get-tuple-element.73), channel_id=1, source_target_pairs={{0,12},{1,13},{2,14},{3,15},{4,8},{5,9},{6,10},{7,11},{8,4},{9,5},... | collective-permute-start | bytes 3145736 | tf_op jit(solution)/shard_map/ppermute | solution.py:62
  88.1 49.3 %collective-permute-start.16 = (bf16[64,7168]{1,0:T(8,128)(2,1)}, bf16[64,7168]{1,0:T(8,128)(2,1)}, u32[]{:S(2)}, u32[]{:S(2)}) collective-permute-start(bf16[64,7168]{1,0:T(8,128)(2,1)} %get-tuple-element.84.refs_3_), channel_id=1, source_target_pairs={{0,2},{1,3},{2,0},{3,1},{4,6},{5,7},{6,4},{7,5},{8,10},{9,11},{10,... | collective-permute-start | bytes 2752520 | tf_op jit(solution)/shard_map/ppermute | solution.py:62
  124.7 18.7 %collective-permute-start.17 = (bf16[64,7168]{1,0:T(8,128)(2,1)}, bf16[64,7168]{1,0:T(8,128)(2,1)}, u32[]{:S(2)}, u32[]{:S(2)}) collective-permute-start(bf16[64,7168]{1,0:T(8,128)(2,1)} %get-tuple-element.95.refs_1_), channel_id=1, source_target_pairs={{0,16},{16,0},{1,17},{17,1},{2,18},{18,2},{3,19},{19,3},{4,20},{20... | collective-permute-start | bytes 2752520 | tf_op jit(solution)/shard_map/ppermute | solution.py:66
  126.6 22.6 %copy-start = (s32[4]{0:T(128)S(1)}, s32[4]{0:T(128)}, u32[]{:S(2)}) copy-start(s32[4]{0:T(128)} %param.11) | copy-start | bytes 52
  126.6 22.8 %copy-start.1 = (s32[4]{0:T(128)S(1)}, s32[4]{0:T(128)}, u32[]{:S(2)}) copy-start(s32[4]{0:T(128)} %param.12) | copy-start | bytes 52
  144.6 21.0 %collective-permute-start.19 = (bf16[64,8192]{1,0:T(8,128)(2,1)}, bf16[64,8192]{1,0:T(8,128)(2,1)}, u32[]{:S(2)}, u32[]{:S(2)}) collective-permute-start(bf16[64,8192]{1,0:T(8,128)(2,1)} %get-tuple-element.100.refs_3_), channel_id=1, source_target_pairs={{0,4},{1,5},{2,6},{3,7},{4,0},{5,1},{6,2},{7,3},{8,12},{9,13},{10,... | collective-permute-start | bytes 3145736 | tf_op jit(solution)/shard_map/ppermute | solution.py:62
  146.8 18.8 %collective-permute-start.20 = (bf16[64,8192]{1,0:T(8,128)(2,1)}, bf16[64,8192]{1,0:T(8,128)(2,1)}, u32[]{:S(2)}, u32[]{:S(2)}) collective-permute-start(bf16[64,8192]{1,0:T(8,128)(2,1)} %get-tuple-element.100.refs_3_), channel_id=1, source_target_pairs={{0,2},{1,3},{2,0},{3,1},{4,6},{5,7},{6,4},{7,5},{8,10},{9,11},{10,... | collective-permute-start | bytes 3145736 | tf_op jit(solution)/shard_map/ppermute | solution.py:62
  147.0 18.6 %collective-permute-start.21 = (bf16[64,7168]{1,0:T(8,128)(2,1)}, bf16[64,7168]{1,0:T(8,128)(2,1)}, u32[]{:S(2)}, u32[]{:S(2)}) collective-permute-start(bf16[64,7168]{1,0:T(8,128)(2,1)} %get-tuple-element.105.refs_2_), channel_id=1, source_target_pairs={{0,16},{16,0},{1,17},{17,1},{2,18},{18,2},{3,19},{19,3},{4,20},{20... | collective-permute-start | bytes 2752520 | tf_op jit(solution)/shard_map/ppermute | solution.py:66
  149.4 1.2 collective-permute-start.18
  151.8 21.6 %copy-start.2 = (s32[8]{0:T(128)S(1)}, s32[8]{0:T(128)}, u32[]{:S(2)}) copy-start(s32[8]{0:T(128)} %constant.51.clone) | copy-start | bytes 100
  166.7 25.0 %collective-permute-start.22 = (bf16[64,8192]{1,0:T(8,128)(2,1)}, bf16[64,8192]{1,0:T(8,128)(2,1)}, u32[]{:S(2)}, u32[]{:S(2)}) collective-permute-start(bf16[64,8192]{1,0:T(8,128)(2,1)} %get-tuple-element.111.refs_1_), channel_id=1, source_target_pairs={{0,2},{1,3},{2,0},{3,1},{4,6},{5,7},{6,4},{7,5},{8,10},{9,11},{10,... | collective-permute-start | bytes 3145736 | tf_op jit(solution)/shard_map/ppermute | solution.py:62
  168.0 24.6 %collective-permute-start.24 = (bf16[64,8192]{1,0:T(8,128)(2,1)}, bf16[64,8192]{1,0:T(8,128)(2,1)}, u32[]{:S(2)}, u32[]{:S(2)}) collective-permute-start(bf16[64,8192]{1,0:T(8,128)(2,1)} %get-tuple-element.112), channel_id=1, source_target_pairs={{0,4},{1,5},{2,6},{3,7},{4,0},{5,1},{6,2},{7,3},{8,12},{9,13},{10,... | collective-permute-start | bytes 3145736 | tf_op jit(solution)/shard_map/ppermute | solution.py:62
  168.1 21.5 %collective-permute-start.23 = (bf16[64,7168]{1,0:T(8,128)(2,1)}, bf16[64,7168]{1,0:T(8,128)(2,1)}, u32[]{:S(2)}, u32[]{:S(2)}) collective-permute-start(bf16[64,7168]{1,0:T(8,128)(2,1)} %get-tuple-element.108.refs_0_), channel_id=1, source_target_pairs={{0,16},{16,0},{1,17},{17,1},{2,18},{18,2},{3,19},{19,3},{4,20},{20... | collective-permute-start | bytes 2752520 | tf_op jit(solution)/shard_map/ppermute | solution.py:66
  169.9 35.4 %collective-permute-start.25 = (bf16[32,7168]{1,0:T(8,128)(2,1)}, bf16[32,7168]{1,0:T(8,128)(2,1)}, u32[]{:S(2)}, u32[]{:S(2)}) collective-permute-start(bf16[32,7168]{1,0:T(8,128)(2,1)} %slice.19), channel_id=1, source_target_pairs={{0,2},{1,3},{2,0},{3,1},{4,6},{5,7},{6,4},{7,5},{8,10},{9,11},{10,... | collective-permute-start | bytes 1376264 | tf_op jit(solution)/shard_map/ppermute | solution.py:62
  172.0 33.3 %collective-permute-start.26 = (bf16[32,7168]{1,0:T(8,128)(2,1)}, bf16[32,7168]{1,0:T(8,128)(2,1)}, u32[]{:S(2)}, u32[]{:S(2)}) collective-permute-start(bf16[32,7168]{1,0:T(8,128)(2,1)} %slice.20), channel_id=1, source_target_pairs={{0,16},{16,0},{1,17},{17,1},{2,18},{18,2},{3,19},{19,3},{4,20},{20... | collective-permute-start | bytes 1376264 | tf_op jit(solution)/shard_map/ppermute | solution.py:66
  219.0 2.2 collective-permute-start.27

commit v18 on v17

--- a/solution.py
+++ b/solution.py
@@ -305,13 +305,11 @@
     grads_there = send(output_grads, CORE)
     grads = ((output_grads, zero), (grads_there, zero))
 
-    core = (me & CORE).reshape(1).astype(jnp.int32)
     copies = (1 - mine, left, b["own"])
-    turn, made, (a["own"],) = prepare(zero, core, *copies, None, [a["own"]])
     a["x"] = over_x(a["own"])
     a["n"] = near(a["own"])
     a_mid = middle(a["own"])
-    turn, (c["own"], b_one, b_two), _ = prepare(turn, 1 - core, *copies, made, [])
+    turn, (c["own"], b_one, b_two), _ = prepare(zero, zero + 1, *copies, None, [])
 
     turn, (a["x"], a["n"], a_mid) = after(turn, [a["x"], a["n"], a_mid], inside, None, [acts_there])
     a_out = outward(a_mid)

time: 224 us -> 208 us (0.929)
  waiting for transfers between devices: 80.7 us -> 50.1 us
  starting transfers between devices: 35 us -> 49.4 us
    ppermute x17, waiting for transfers between devices: 48.5 us -> 31.8 us  [flip(): return lax.ppermute(array, 'dp', [(i, i ^ code) for i in range(count)])]
    ppermute x17, starting transfers between devices: 13.7 us -> 29.5 us  [flip(): return lax.ppermute(array, 'dp', [(i, i ^ code) for i in range(count)])]
    ppermute x7, waiting for transfers between devices: 24.1 us -> 12 us  [swap_groups(): return lax.ppermute(array, 'groups', [(0, 1), (1, 0)])]
    pallas_call x2 -> x1, Pallas kernels: 7.63 us -> 6.43 us  [prepare(): pl.pallas_call(prepare_kernel, out_shape=[jax.ShapeDtypeStruct(x.shape, x...]
  transfers between devices with their start and end apart: 28 -> 28, of which waited for: 15 -> 16; matrix products, arithmetic and copies ran while one was open for 4% -> 5% of each run, Pallas kernels for 35% -> 38%
where the time goes in v18:
time: 208 us; the launch traced here: 204 us
  Pallas kernels  93.6 us (45%)
  waiting for transfers between devices  50.1 us (24%)
  starting transfers between devices  49.4 us (24%)
  local copies, waits for them, and re-layouts  9.27 us (4%)
    pallas_call x6, Pallas kernels, proj(): pl.pallas_call(functools.partial(proj_kernel, len(pieces), last), out_sha...  70.8 us
    ppermute x17, waiting for transfers between devices, flip(): return lax.ppermute(array, 'dp', [(i, i ^ code) for i in range(count)])  31.8 us
    ppermute x17, starting transfers between devices, flip(): return lax.ppermute(array, 'dp', [(i, i ^ code) for i in range(count)])  29.5 us
    pallas_call x11, Pallas kernels, after(): pl.pallas_call(functools.partial(after_kernel, count, merge is not None),...  16.3 us
    ppermute x7, waiting for transfers between devices, swap_groups(): return lax.ppermute(array, 'groups', [(0, 1), (1, 0)])  12 us
    ppermute x4, starting transfers between devices, lines(): lax.ppermute(array, 'dp', [(a * 4 + rest, b * 4 + rest) for a, b in pairs...  11.9 us
    ppermute x7, starting transfers between devices, swap_groups(): return lax.ppermute(array, 'groups', [(0, 1), (1, 0)])  7.88 us
    pallas_call x1, Pallas kernels, prepare(): pl.pallas_call(prepare_kernel, out_shape=[jax.ShapeDtypeStruct(x.shape, x...  6.43 us
  transfers between devices with their start and end apart: 28, of which 16 were waited for; matrix products, arithmetic and copies ran while one was open for 5% of the time, Pallas kernels for 38%

profile of v18, /device:TPU:9, one launch (start us, length us, event | category | flops | bytes accessed | tf_op | source)
XLA Modules:
  0.0 204.4 jit_solution(6989452485532489548)
XLA Ops:
  0.7 2.2 %constant_dynamic-slice_fusion.refs_0_ = bf16[64,7168]{1,0:T(8,128)(2,1)} fusion(bf16[64,14336]{1,0:T(8,128)(2,1)} %bitcast.18, s32[]{:T(128)S(6)} %select_n.20), kind=kLoop, calls=%fused_computation.19 | loop fusion | bytes 1835012 | tf_op jit(solution)/shard_map/dynamic_slice | solution.py:266
  4.2 4.3 %collective-permute-start.3 = (bf16[64,7168]{1,0:T(8,128)(2,1)}, bf16[64,7168]{1,0:T(8,128)(2,1)}, u32[]{:S(2)}, u32[]{:S(2)}) collective-permute-start(bf16[64,7168]{1,0:T(8,128)(2,1)} %constant_dynamic-slice_fusion.refs_0_), channel_id=1, source_target_pairs={{4,8},{5,9},{6,10},{7,11},{8,4},{9,5},{10,6},{11,7},{20,24},{21,25... | collective-permute-start | bytes 2752520 | tf_op jit(solution)/shard_map/ppermute | solution.py:158
  8.6 6.4 %shard_map.73 = (bf16[64,7168]{1,0:T(8,128)(2,1)}, bf16[64,8192]{1,0:T(8,128)(2,1)}, bf16[64,8192]{1,0:T(8,128)(2,1)}, s32[1]{0:T(128)}) custom-call(s32[1]{0:T(128)} %constant.14.clone.1.works_ref, s32[1]{0:T(128)} %constant.24.clone.1.turn_ref, s32[1]{0:T(128)S(6)} %sub.13.first_ref, bf16[64,14336]{1,0:T(8,128)(2,1)} %bitcast.19, bf16[64,8192]{1,0:T(8,128)(2,1)} %bitcast.16), custom_call_target="tpu_custom_call" | custom-call | flops 1 | bytes 1 | tf_op jit(solution)/shard_map/pallas_call | solution.py:141
  15.0 9.6 %collective-permute-done.1.refs_1_ = bf16[64,7168]{1,0:T(8,128)(2,1)} collective-permute-done((bf16[64,7168]{1,0:T(8,128)(2,1)}, bf16[64,7168]{1,0:T(8,128)(2,1)}, u32[]{:S(2)}, u32[]{:S(2)}) %collective-permute-start.1) | collective-permute-done | bytes 917536 | tf_op jit(solution)/shard_map/ppermute | solution.py:62
  25.8 2.7 %collective-permute-done.3.refs_3_ = bf16[64,7168]{1,0:T(8,128)(2,1)} collective-permute-done((bf16[64,7168]{1,0:T(8,128)(2,1)}, bf16[64,7168]{1,0:T(8,128)(2,1)}, u32[]{:S(2)}, u32[]{:S(2)}) %collective-permute-start.3) | collective-permute-done | bytes 917536 | tf_op jit(solution)/shard_map/ppermute | solution.py:158
  29.6 2.3 %collective-permute-start.5 = (bf16[64,7168]{1,0:T(8,128)(2,1)}, bf16[64,7168]{1,0:T(8,128)(2,1)}, u32[]{:S(2)}, u32[]{:S(2)}) collective-permute-start(bf16[64,7168]{1,0:T(8,128)(2,1)} %get-tuple-element.62.refs_0_), channel_id=1, source_target_pairs={{4,0},{5,1},{6,2},{7,3},{8,12},{9,13},{10,14},{11,15},{20,16},{21,... | collective-permute-start | bytes 2752520 | tf_op jit(solution)/shard_map/ppermute | solution.py:158
  31.9 3.0 %collective-permute-start.7 = (bf16[64,7168]{1,0:T(8,128)(2,1)}, bf16[64,7168]{1,0:T(8,128)(2,1)}, u32[]{:S(2)}, u32[]{:S(2)}) collective-permute-start(bf16[64,7168]{1,0:T(8,128)(2,1)} %get-tuple-element.64.refs_2_), channel_id=1, source_target_pairs={{4,8},{5,9},{6,10},{7,11},{8,4},{9,5},{10,6},{11,7},{20,24},{21,25... | collective-permute-start | bytes 2752520 | tf_op jit(solution)/shard_map/ppermute | solution.py:158
  35.0 1.3 collective-permute-start.8
  37.4 10.8 %collective-permute-done.6.refs_2_ = bf16[64,8192]{1,0:T(8,128)(2,1)} collective-permute-done((bf16[64,8192]{1,0:T(8,128)(2,1)}, bf16[64,8192]{1,0:T(8,128)(2,1)}, u32[]{:S(2)}, u32[]{:S(2)}) %collective-permute-start.6) | collective-permute-done | bytes 1048608 | tf_op jit(solution)/shard_map/ppermute | solution.py:62
  50.6 3.6 %collective-permute-done.7.refs_3_ = bf16[64,7168]{1,0:T(8,128)(2,1)} collective-permute-done((bf16[64,7168]{1,0:T(8,128)(2,1)}, bf16[64,7168]{1,0:T(8,128)(2,1)}, u32[]{:S(2)}, u32[]{:S(2)}) %collective-permute-start.7) | collective-permute-done | bytes 917536 | tf_op jit(solution)/shard_map/ppermute | solution.py:158
  56.0 2.3 %collective-permute-start.9 = (bf16[64,7168]{1,0:T(8,128)(2,1)}, bf16[64,7168]{1,0:T(8,128)(2,1)}, u32[]{:S(2)}, u32[]{:S(2)}) collective-permute-start(bf16[64,7168]{1,0:T(8,128)(2,1)} %get-tuple-element.67.refs_0_), channel_id=1, source_target_pairs={{4,0},{5,1},{6,2},{7,3},{8,12},{9,13},{10,14},{11,15},{20,16},{21,... | collective-permute-start | bytes 2752520 | tf_op jit(solution)/shard_map/ppermute | solution.py:158
  58.3 3.1 %shard_map.77 = (bf16[64,7168]{1,0:T(8,128)(2,1)}, s32[1]{0:T(128)}) custom-call(s32[1]{0:T(128)} %bitcast.inside_ref, s32[1]{0:T(128)} %get-tuple-element.66.turn_ref, bf16[64,7168]{1,0:T(8,128)(2,1)} %get-tuple-element.67.refs_0_, bf16[64,7168]{1,0:T(8,128)(2,1)} %get-tuple-element.68.refs_1_), custom_call_target="tpu_custom_call", output_to_operand_aliasing={{0}: (3, {})} | custom-call | flops 1 | bytes 1 | tf_op jit(solution)/shard_map/pallas_call | solution.py:106
  62.5 5.5 %collective-permute-done.10.refs_1_ = bf16[64,7168]{1,0:T(8,128)(2,1)} collective-permute-done((bf16[64,7168]{1,0:T(8,128)(2,1)}, bf16[64,7168]{1,0:T(8,128)(2,1)}, u32[]{:S(2)}, u32[]{:S(2)}) %collective-permute-start.10) | collective-permute-done | bytes 917536 | tf_op jit(solution)/shard_map/ppermute | solution.py:62
  68.1 6.5 %collective-permute-done.11.refs_2_ = bf16[64,7168]{1,0:T(8,128)(2,1)} collective-permute-done((bf16[64,7168]{1,0:T(8,128)(2,1)}, bf16[64,7168]{1,0:T(8,128)(2,1)}, u32[]{:S(2)}, u32[]{:S(2)}) %collective-permute-start.11) | collective-permute-done | bytes 917536 | tf_op jit(solution)/shard_map/ppermute | solution.py:66
  76.1 3.1 %shard_map.80 = (bf16[64,7168]{1,0:T(8,128)(2,1)}, s32[1]{0:T(128)}) custom-call(s32[1]{0:T(128)} %bitcast.inside_ref, s32[1]{0:T(128)} %get-tuple-element.71.turn_ref, bf16[64,7168]{1,0:T(8,128)(2,1)} %get-tuple-element.62.refs_0_, bf16[64,7168]{1,0:T(8,128)(2,1)} %get-tuple-element.72.refs_1_), custom_call_target="tpu_custom_call", output_to_operand_aliasing={{0}: (3, {})} | custom-call | flops 1 | bytes 1 | tf_op jit(solution)/shard_map/pallas_call | solution.py:106
  79.2 1.3 collective-permute-start.14
  82.9 10.8 %shard_map.81 = (f32[1024,256]{1,0:T(8,128)}, s32[1]{0:T(128)}) custom-call(s32[1]{0:T(128)} %get-tuple-element.73.turn_ref, s32[3]{0:T(128)} %concatenate.25.at_ref, bf16[512,14336]{1,0:T(8,128)(2,1)} %own_ref.11, bf16[512,14336]{1,0:T(8,128)(2,1)} %collective-permute-done.refs_0_.other_ref, bf16[64,7168]{1,0:T(8,128)(2,1)} %constant_dynamic-slice_fusion.refs_0_, ...), custom_call_target="tpu_custom_call" | custom-call | flops 1 | bytes 1 | tf_op jit(solution)/shard_map/pallas_call | solution.py:222
  94.0 1.5 collective-permute-done.12.refs_0_
  96.7 1.3 collective-permute-start.17
  98.5 10.8 %shard_map.83 = (f32[1024,256]{1,0:T(8,128)}, s32[1]{0:T(128)}) custom-call(s32[1]{0:T(128)} %get-tuple-element.79.turn_ref, s32[3]{0:T(128)} %concatenate.26.at_ref, bf16[512,14336]{1,0:T(8,128)(2,1)} %own_ref.11, bf16[512,14336]{1,0:T(8,128)(2,1)} %collective-permute-done.refs_0_.other_ref, bf16[64,7168]{1,0:T(8,128)(2,1)} %get-tuple-element.80.refs_0_, ...), custom_call_target="tpu_custom_call" | custom-call | flops 1 | bytes 1 | tf_op jit(solution)/shard_map/pallas_call | solution.py:222
  113.0 7.9 %collective-permute-start.19 = (bf16[64,8192]{1,0:T(8,128)(2,1)}, bf16[64,8192]{1,0:T(8,128)(2,1)}, u32[]{:S(2)}, u32[]{:S(2)}) collective-permute-start(bf16[64,8192]{1,0:T(8,128)(2,1)} %get-tuple-element.90.refs_3_), channel_id=1, source_target_pairs={{0,4},{1,5},{2,6},{3,7},{4,0},{5,1},{6,2},{7,3},{8,12},{9,13},{10,... | collective-permute-start | bytes 3145736 | tf_op jit(solution)/shard_map/ppermute | solution.py:62
  122.5 10.0 %collective-permute-start.18 = (s32[2,4]{1,0:T(2,128)S(1)}, s32[2,4]{1,0:T(2,128)S(1)}, u32[]{:S(2)}, u32[]{:S(2)}) collective-permute-start(s32[2,4]{1,0:T(2,128)S(1)} %pad_add_fusion), channel_id=1, source_target_pairs={{0,1},{1,0},{2,3},{3,2},{4,5},{5,4},{6,7},{7,6},{8,9},{9,8},{10,11... | collective-permute-start | bytes 104 | tf_op jit(solution)/shard_map/ppermute | solution.py:62
  134.5 13.8 %shard_map.85 = (f32[8,256]{1,0:T(8,128)}, s32[1]{0:T(128)}) custom-call(s32[1]{0:T(128)} %get-tuple-element.87.turn_ref, s32[3]{0:T(128)} %broadcast_8_at_ref.2.at_ref, bf16[512,8192]{1,0:T(8,128)(2,1)} %own_ref.10, bf16[512,8192]{1,0:T(8,128)(2,1)} %collective-permute-done.4.refs_0_.other_ref, bf16[64,8192]{1,0:T(8,128)(2,1)} %bitcast.17, ...), custom_call_target="tpu_custom_call" | custom-call | flops 1 | bytes 1 | tf_op jit(solution)/shard_map/pallas_call | solution.py:222
  149.8 1.7 collective-permute-start.24
  152.7 1.8 slice.19
  155.7 1.8 slice.20
  158.7 10.9 %shard_map.87 = (f32[1024,256]{1,0:T(8,128)}, s32[1]{0:T(128)}) custom-call(s32[1]{0:T(128)} %get-tuple-element.97.turn_ref, s32[3]{0:T(128)} %concatenate.25.at_ref, bf16[512,14336]{1,0:T(8,128)(2,1)} %own_ref.11, bf16[512,14336]{1,0:T(8,128)(2,1)} %collective-permute-done.refs_0_.other_ref, bf16[64,7168]{1,0:T(8,128)(2,1)} %get-tuple-element.98.refs_0_, ...), custom_call_target="tpu_custom_call" | custom-call | flops 1 | bytes 1 | tf_op jit(solution)/shard_map/pallas_call | solution.py:222
  169.5 3.2 %collective-permute-done.23.refs_1_ = bf16[64,7168]{1,0:T(8,128)(2,1)} collective-permute-done((bf16[64,7168]{1,0:T(8,128)(2,1)}, bf16[64,7168]{1,0:T(8,128)(2,1)}, u32[]{:S(2)}, u32[]{:S(2)}) %collective-permute-start.23) | collective-permute-done | bytes 917536 | tf_op jit(solution)/shard_map/ppermute | solution.py:66
  172.7 1.5 collective-permute-done.22.refs_0_
  175.8 11.7 %shard_map.89 = (f32[1024,256]{1,0:T(8,128)}, s32[1]{0:T(128)}) custom-call(s32[1]{0:T(128)} %get-tuple-element.103.turn_ref, s32[3]{0:T(128)} %broadcast_8_at_ref.2.at_ref, bf16[512,8192]{1,0:T(8,128)(2,1)} %own_ref.10, bf16[512,8192]{1,0:T(8,128)(2,1)} %collective-permute-done.4.refs_0_.other_ref, bf16[64,8192]{1,0:T(8,128)(2,1)} %get-tuple-element.104.refs_0_, ...), custom_call_target="tpu_custom_call" | custom-call | flops 1 | bytes 1 | tf_op jit(solution)/shard_map/pallas_call | solution.py:222
  187.5 12.9 %shard_map.90 = (f32[8,256]{1,0:T(8,128)}, s32[1]{0:T(128)}) custom-call(s32[1]{0:T(128)} %get-tuple-element.107.turn_ref, s32[3]{0:T(128)} %concatenate.26.at_ref, bf16[512,14336]{1,0:T(8,128)(2,1)} %own_ref.11, bf16[512,14336]{1,0:T(8,128)(2,1)} %collective-permute-done.refs_0_.other_ref, bf16[64,7168]{1,0:T(8,128)(2,1)} %get-tuple-element.108.refs_0_, ...), custom_call_target="tpu_custom_call" | custom-call | flops 1 | bytes 1 | tf_op jit(solution)/shard_map/pallas_call | solution.py:222
  201.2 1.6 collective-permute-start.27
  (69 shorter events, 32.9 us)
Async XLA Ops:
  0.0 28.5 %collective-permute-start = (bf16[512,14336]{1,0:T(8,128)(2,1)}, bf16[512,14336]{1,0:T(8,128)(2,1)}, u32[]{:S(2)}, u32[]{:S(2)}) collective-permute-start(bf16[512,14336]{1,0:T(8,128)(2,1)} %own_ref.11), channel_id=1, source_target_pairs={{0,1},{1,0},{2,3},{3,2},{4,5},{5,4},{6,7},{7,6},{8,9},{9,8},{10,11... | collective-permute-start | bytes 44040200 | tf_op jit(solution)/shard_map/ppermute | solution.py:62
  0.7 48.7 %collective-permute-start.4 = (bf16[512,8192]{1,0:T(8,128)(2,1)}, bf16[512,8192]{1,0:T(8,128)(2,1)}, u32[]{:S(2)}, u32[]{:S(2)}) collective-permute-start(bf16[512,8192]{1,0:T(8,128)(2,1)} %own_ref.10), channel_id=1, source_target_pairs={{0,1},{1,0},{2,3},{3,2},{4,5},{5,4},{6,7},{7,6},{8,9},{9,8},{10,11... | collective-permute-start | bytes 25165832 | tf_op jit(solution)/shard_map/ppermute | solution.py:62
  2.9 21.7 %collective-permute-start.1 = (bf16[64,7168]{1,0:T(8,128)(2,1)}, bf16[64,7168]{1,0:T(8,128)(2,1)}, u32[]{:S(2)}, u32[]{:S(2)}) collective-permute-start(bf16[64,7168]{1,0:T(8,128)(2,1)} %constant_dynamic-slice_fusion.refs_0_), channel_id=1, source_target_pairs={{0,2},{1,3},{2,0},{3,1},{4,6},{5,7},{6,4},{7,5},{8,10},{9,11},{10,... | collective-permute-start | bytes 2752520 | tf_op jit(solution)/shard_map/ppermute | solution.py:62
  4.1 21.7 %collective-permute-start.2 = (bf16[64,7168]{1,0:T(8,128)(2,1)}, bf16[64,7168]{1,0:T(8,128)(2,1)}, u32[]{:S(2)}, u32[]{:S(2)}) collective-permute-start(bf16[64,7168]{1,0:T(8,128)(2,1)} %constant_dynamic-slice_fusion.refs_0_), channel_id=1, source_target_pairs={{0,4},{1,5},{2,6},{3,7},{4,0},{5,1},{6,2},{7,3},{8,12},{9,13},{10,... | collective-permute-start | bytes 2752520 | tf_op jit(solution)/shard_map/ppermute | solution.py:62
  4.2 24.3 %collective-permute-start.3 = (bf16[64,7168]{1,0:T(8,128)(2,1)}, bf16[64,7168]{1,0:T(8,128)(2,1)}, u32[]{:S(2)}, u32[]{:S(2)}) collective-permute-start(bf16[64,7168]{1,0:T(8,128)(2,1)} %constant_dynamic-slice_fusion.refs_0_), channel_id=1, source_target_pairs={{4,8},{5,9},{6,10},{7,11},{8,4},{9,5},{10,6},{11,7},{20,24},{21,25... | collective-permute-start | bytes 2752520 | tf_op jit(solution)/shard_map/ppermute | solution.py:158
  24.6 23.6 %collective-permute-start.6 = (bf16[64,8192]{1,0:T(8,128)(2,1)}, bf16[64,8192]{1,0:T(8,128)(2,1)}, u32[]{:S(2)}, u32[]{:S(2)}) collective-permute-start(bf16[64,8192]{1,0:T(8,128)(2,1)} %get-tuple-element.63), channel_id=1, source_target_pairs={{0,2},{1,3},{2,0},{3,1},{4,6},{5,7},{6,4},{7,5},{8,10},{9,11},{10,... | collective-permute-start | bytes 3145736 | tf_op jit(solution)/shard_map/ppermute | solution.py:62
  29.6 21.1 %collective-permute-start.5 = (bf16[64,7168]{1,0:T(8,128)(2,1)}, bf16[64,7168]{1,0:T(8,128)(2,1)}, u32[]{:S(2)}, u32[]{:S(2)}) collective-permute-start(bf16[64,7168]{1,0:T(8,128)(2,1)} %get-tuple-element.62.refs_0_), channel_id=1, source_target_pairs={{4,0},{5,1},{6,2},{7,3},{8,12},{9,13},{10,14},{11,15},{20,16},{21,... | collective-permute-start | bytes 2752520 | tf_op jit(solution)/shard_map/ppermute | solution.py:158
  31.9 22.4 %collective-permute-start.7 = (bf16[64,7168]{1,0:T(8,128)(2,1)}, bf16[64,7168]{1,0:T(8,128)(2,1)}, u32[]{:S(2)}, u32[]{:S(2)}) collective-permute-start(bf16[64,7168]{1,0:T(8,128)(2,1)} %get-tuple-element.64.refs_2_), channel_id=1, source_target_pairs={{4,8},{5,9},{6,10},{7,11},{8,4},{9,5},{10,6},{11,7},{20,24},{21,25... | collective-permute-start | bytes 2752520 | tf_op jit(solution)/shard_map/ppermute | solution.py:158
  35.0 20.0 %collective-permute-start.8 = (bf16[64,7168]{1,0:T(8,128)(2,1)}, bf16[64,7168]{1,0:T(8,128)(2,1)}, u32[]{:S(2)}, u32[]{:S(2)}) collective-permute-start(bf16[64,7168]{1,0:T(8,128)(2,1)} %get-tuple-element.65.refs_1_), channel_id=1, source_target_pairs={{0,16},{16,0},{1,17},{17,1},{2,18},{18,2},{3,19},{19,3},{4,20},{20... | collective-permute-start | bytes 2752520 | tf_op jit(solution)/shard_map/ppermute | solution.py:66
  48.2 19.9 %collective-permute-start.10 = (bf16[64,7168]{1,0:T(8,128)(2,1)}, bf16[64,7168]{1,0:T(8,128)(2,1)}, u32[]{:S(2)}, u32[]{:S(2)}) collective-permute-start(bf16[64,7168]{1,0:T(8,128)(2,1)} %get-tuple-element.64.refs_2_), channel_id=1, source_target_pairs={{0,2},{1,3},{2,0},{3,1},{4,6},{5,7},{6,4},{7,5},{8,10},{9,11},{10,... | collective-permute-start | bytes 2752520 | tf_op jit(solution)/shard_map/ppermute | solution.py:62
  49.4 25.2 %collective-permute-start.11 = (bf16[64,7168]{1,0:T(8,128)(2,1)}, bf16[64,7168]{1,0:T(8,128)(2,1)}, u32[]{:S(2)}, u32[]{:S(2)}) collective-permute-start(bf16[64,7168]{1,0:T(8,128)(2,1)} %get-tuple-element.64.refs_2_), channel_id=1, source_target_pairs={{0,16},{16,0},{1,17},{17,1},{2,18},{18,2},{3,19},{19,3},{4,20},{20... | collective-permute-start | bytes 2752520 | tf_op jit(solution)/shard_map/ppermute | solution.py:66
  56.0 18.6 %collective-permute-start.9 = (bf16[64,7168]{1,0:T(8,128)(2,1)}, bf16[64,7168]{1,0:T(8,128)(2,1)}, u32[]{:S(2)}, u32[]{:S(2)}) collective-permute-start(bf16[64,7168]{1,0:T(8,128)(2,1)} %get-tuple-element.67.refs_0_), channel_id=1, source_target_pairs={{4,0},{5,1},{6,2},{7,3},{8,12},{9,13},{10,14},{11,15},{20,16},{21,... | collective-permute-start | bytes 2752520 | tf_op jit(solution)/shard_map/ppermute | solution.py:158
  75.7 19.8 %collective-permute-start.12 = (bf16[64,8192]{1,0:T(8,128)(2,1)}, bf16[64,8192]{1,0:T(8,128)(2,1)}, u32[]{:S(2)}, u32[]{:S(2)}) collective-permute-start(bf16[64,8192]{1,0:T(8,128)(2,1)} %get-tuple-element.76), channel_id=1, source_target_pairs={{0,4},{1,5},{2,6},{3,7},{4,0},{5,1},{6,2},{7,3},{8,12},{9,13},{10,... | collective-permute-start | bytes 3145736 | tf_op jit(solution)/shard_map/ppermute | solution.py:62
  75.8 17.9 %collective-permute-start.13 = (bf16[64,7168]{1,0:T(8,128)(2,1)}, bf16[64,7168]{1,0:T(8,128)(2,1)}, u32[]{:S(2)}, u32[]{:S(2)}) collective-permute-start(bf16[64,7168]{1,0:T(8,128)(2,1)} %get-tuple-element.77.refs_3_), channel_id=1, source_target_pairs={{0,2},{1,3},{2,0},{3,1},{4,6},{5,7},{6,4},{7,5},{8,10},{9,11},{10,... | collective-permute-start | bytes 2752520 | tf_op jit(solution)/shard_map/ppermute | solution.py:62
  79.2 14.8 %collective-permute-start.14 = (bf16[64,7168]{1,0:T(8,128)(2,1)}, bf16[64,7168]{1,0:T(8,128)(2,1)}, u32[]{:S(2)}, u32[]{:S(2)}) collective-permute-start(bf16[64,7168]{1,0:T(8,128)(2,1)} %get-tuple-element.74.refs_3_), channel_id=1, source_target_pairs={{0,16},{16,0},{1,17},{17,1},{2,18},{18,2},{3,19},{19,3},{4,20},{20... | collective-permute-start | bytes 2752520 | tf_op jit(solution)/shard_map/ppermute | solution.py:66
  80.5 28.8 %collective-permute-start.15 = (bf16[64,8192]{1,0:T(8,128)(2,1)}, bf16[64,8192]{1,0:T(8,128)(2,1)}, u32[]{:S(2)}, u32[]{:S(2)}) collective-permute-start(bf16[64,8192]{1,0:T(8,128)(2,1)} %get-tuple-element.63), channel_id=1, source_target_pairs={{0,12},{1,13},{2,14},{3,15},{4,8},{5,9},{6,10},{7,11},{8,4},{9,5},... | collective-permute-start | bytes 3145736 | tf_op jit(solution)/shard_map/ppermute | solution.py:62
  81.7 28.8 %collective-permute-start.16 = (bf16[64,7168]{1,0:T(8,128)(2,1)}, bf16[64,7168]{1,0:T(8,128)(2,1)}, u32[]{:S(2)}, u32[]{:S(2)}) collective-permute-start(bf16[64,7168]{1,0:T(8,128)(2,1)} %get-tuple-element.74.refs_3_), channel_id=1, source_target_pairs={{0,2},{1,3},{2,0},{3,1},{4,6},{5,7},{6,4},{7,5},{8,10},{9,11},{10,... | collective-permute-start | bytes 2752520 | tf_op jit(solution)/shard_map/ppermute | solution.py:62
  96.7 15.1 %collective-permute-start.17 = (bf16[64,7168]{1,0:T(8,128)(2,1)}, bf16[64,7168]{1,0:T(8,128)(2,1)}, u32[]{:S(2)}, u32[]{:S(2)}) collective-permute-start(bf16[64,7168]{1,0:T(8,128)(2,1)} %get-tuple-element.85.refs_1_), channel_id=1, source_target_pairs={{0,16},{16,0},{1,17},{17,1},{2,18},{18,2},{3,19},{19,3},{4,20},{20... | collective-permute-start | bytes 2752520 | tf_op jit(solution)/shard_map/ppermute | solution.py:66
  98.5 23.8 %copy-start = (s32[4]{0:T(128)S(1)}, s32[4]{0:T(128)}, u32[]{:S(2)}) copy-start(s32[4]{0:T(128)} %param.11) | copy-start | bytes 52
  98.5 24.0 %copy-start.1 = (s32[4]{0:T(128)S(1)}, s32[4]{0:T(128)}, u32[]{:S(2)}) copy-start(s32[4]{0:T(128)} %param.12) | copy-start | bytes 52
  113.0 35.4 %collective-permute-start.19 = (bf16[64,8192]{1,0:T(8,128)(2,1)}, bf16[64,8192]{1,0:T(8,128)(2,1)}, u32[]{:S(2)}, u32[]{:S(2)}) collective-permute-start(bf16[64,8192]{1,0:T(8,128)(2,1)} %get-tuple-element.90.refs_3_), channel_id=1, source_target_pairs={{0,4},{1,5},{2,6},{3,7},{4,0},{5,1},{6,2},{7,3},{8,12},{9,13},{10,... | collective-permute-start | bytes 3145736 | tf_op jit(solution)/shard_map/ppermute | solution.py:62
  120.8 27.5 %collective-permute-start.20 = (bf16[64,8192]{1,0:T(8,128)(2,1)}, bf16[64,8192]{1,0:T(8,128)(2,1)}, u32[]{:S(2)}, u32[]{:S(2)}) collective-permute-start(bf16[64,8192]{1,0:T(8,128)(2,1)} %get-tuple-element.90.refs_3_), channel_id=1, source_target_pairs={{0,2},{1,3},{2,0},{3,1},{4,6},{5,7},{6,4},{7,5},{8,10},{9,11},{10,... | collective-permute-start | bytes 3145736 | tf_op jit(solution)/shard_map/ppermute | solution.py:62
  121.1 27.3 %collective-permute-start.21 = (bf16[64,7168]{1,0:T(8,128)(2,1)}, bf16[64,7168]{1,0:T(8,128)(2,1)}, u32[]{:S(2)}, u32[]{:S(2)}) collective-permute-start(bf16[64,7168]{1,0:T(8,128)(2,1)} %get-tuple-element.95.refs_2_), channel_id=1, source_target_pairs={{0,16},{16,0},{1,17},{17,1},{2,18},{18,2},{3,19},{19,3},{4,20},{20... | collective-permute-start | bytes 2752520 | tf_op jit(solution)/shard_map/ppermute | solution.py:66
  122.5 10.8 %collective-permute-start.18 = (s32[2,4]{1,0:T(2,128)S(1)}, s32[2,4]{1,0:T(2,128)S(1)}, u32[]{:S(2)}, u32[]{:S(2)}) collective-permute-start(s32[2,4]{1,0:T(2,128)S(1)} %pad_add_fusion), channel_id=1, source_target_pairs={{0,1},{1,0},{2,3},{3,2},{4,5},{5,4},{6,7},{7,6},{8,9},{9,8},{10,11... | collective-permute-start | bytes 104 | tf_op jit(solution)/shard_map/ppermute | solution.py:62
  134.5 23.3 %copy-start.2 = (s32[8]{0:T(128)S(1)}, s32[8]{0:T(128)}, u32[]{:S(2)}) copy-start(s32[8]{0:T(128)} %constant.51.clone) | copy-start | bytes 100
  149.4 24.8 %collective-permute-start.22 = (bf16[64,8192]{1,0:T(8,128)(2,1)}, bf16[64,8192]{1,0:T(8,128)(2,1)}, u32[]{:S(2)}, u32[]{:S(2)}) collective-permute-start(bf16[64,8192]{1,0:T(8,128)(2,1)} %get-tuple-element.101.refs_1_), channel_id=1, source_target_pairs={{0,2},{1,3},{2,0},{3,1},{4,6},{5,7},{6,4},{7,5},{8,10},{9,11},{10,... | collective-permute-start | bytes 3145736 | tf_op jit(solution)/shard_map/ppermute | solution.py:62
  149.8 24.9 %collective-permute-start.24 = (bf16[64,8192]{1,0:T(8,128)(2,1)}, bf16[64,8192]{1,0:T(8,128)(2,1)}, u32[]{:S(2)}, u32[]{:S(2)}) collective-permute-start(bf16[64,8192]{1,0:T(8,128)(2,1)} %get-tuple-element.102), channel_id=1, source_target_pairs={{0,4},{1,5},{2,6},{3,7},{4,0},{5,1},{6,2},{7,3},{8,12},{9,13},{10,... | collective-permute-start | bytes 3145736 | tf_op jit(solution)/shard_map/ppermute | solution.py:62
  151.4 21.3 %collective-permute-start.23 = (bf16[64,7168]{1,0:T(8,128)(2,1)}, bf16[64,7168]{1,0:T(8,128)(2,1)}, u32[]{:S(2)}, u32[]{:S(2)}) collective-permute-start(bf16[64,7168]{1,0:T(8,128)(2,1)} %get-tuple-element.98.refs_0_), channel_id=1, source_target_pairs={{0,16},{16,0},{1,17},{17,1},{2,18},{18,2},{3,19},{19,3},{4,20},{20... | collective-permute-start | bytes 2752520 | tf_op jit(solution)/shard_map/ppermute | solution.py:66
  154.5 32.9 %collective-permute-start.25 = (bf16[32,7168]{1,0:T(8,128)(2,1)}, bf16[32,7168]{1,0:T(8,128)(2,1)}, u32[]{:S(2)}, u32[]{:S(2)}) collective-permute-start(bf16[32,7168]{1,0:T(8,128)(2,1)} %slice.19), channel_id=1, source_target_pairs={{0,2},{1,3},{2,0},{3,1},{4,6},{5,7},{6,4},{7,5},{8,10},{9,11},{10,... | collective-permute-start | bytes 1376264 | tf_op jit(solution)/shard_map/ppermute | solution.py:62
  157.5 29.9 %collective-permute-start.26 = (bf16[32,7168]{1,0:T(8,128)(2,1)}, bf16[32,7168]{1,0:T(8,128)(2,1)}, u32[]{:S(2)}, u32[]{:S(2)}) collective-permute-start(bf16[32,7168]{1,0:T(8,128)(2,1)} %slice.20), channel_id=1, source_target_pairs={{0,16},{16,0},{1,17},{17,1},{2,18},{18,2},{3,19},{19,3},{4,20},{20... | collective-permute-start | bytes 1376264 | tf_op jit(solution)/shard_map/ppermute | solution.py:66
  201.2 2.4 %collective-permute-start.27 = (f32[4,512]{1,0:T(4,128)S(1)}, f32[4,512]{1,0:T(4,128)S(1)}, u32[]{:S(2)}, u32[]{:S(2)}) collective-permute-start(f32[4,512]{1,0:T(4,128)S(1)} %pad_maximum_fusion), channel_id=1, source_target_pairs={{0,1},{1,0},{2,3},{3,2},{4,5},{5,4},{6,7},{7,6},{8,9},{9,8},{10,11... | collective-permute-start | bytes 24584 | tf_op jit(solution)/shard_map/ppermute | solution.py:62

commit v19 on v15

--- a/solution.py
+++ b/solution.py
@@ -313,13 +313,11 @@
     grads_there = send(output_grads, CORE)
     grads = ((output_grads, zero), (grads_there, zero))
 
-    core = (me & CORE).reshape(1).astype(jnp.int32)
     copies = (1 - mine, left, b["own"])
-    turn, made, (a["own"],) = prepare(zero, core, *copies, None, [a["own"]])
     a["x"] = over_x(a["own"])
     a["n"] = near(a["own"])
     a_mid = middle(a["own"])
-    turn, (c["own"], b_one, b_two), _ = prepare(turn, 1 - core, *copies, made, [])
+    turn, (c["own"], b_one, b_two), _ = prepare(zero, zero + 1, *copies, None, [])
 
     turn, (a["x"], a["n"], a_mid, a["own"]) = after(
         turn, [a["x"], a["n"], a_mid, a["own"]], inside, None, [acts_there]

time: 226 us -> 205 us (0.907)
  starting transfers between devices: 62.6 us -> 42.9 us
    ppermute x19, starting transfers between devices: 53.1 us -> 30.1 us  [flip(): return lax.ppermute(array, 'dp', [(i, i ^ code) for i in range(count)])]
    ppermute x19, waiting for transfers between devices: 37.5 us -> 32.7 us  [flip(): return lax.ppermute(array, 'dp', [(i, i ^ code) for i in range(count)])]
    ppermute x7, waiting for transfers between devices: 18.5 us -> 23 us  [swap_groups(): return lax.ppermute(array, 'groups', [(0, 1), (1, 0)])]
    ppermute x7, starting transfers between devices: 3.55 us -> 6.89 us  [swap_groups(): return lax.ppermute(array, 'groups', [(0, 1), (1, 0)])]
    pallas_call x2 -> x1, Pallas kernels: 7.71 us -> 6.41 us  [prepare(): pl.pallas_call(prepare_kernel, out_shape=[jax.ShapeDtypeStruct(x.shape, x...]
  transfers between devices with their start and end apart: 28 -> 28, of which waited for: 11 -> 11; matrix products, arithmetic and copies ran while one was open for 5% -> 5% of each run, Pallas kernels for 39% -> 42%
where the time goes in v19:
time: 205 us; the launch traced here: 203 us
  Pallas kernels  89.8 us (44%)
  waiting for transfers between devices  58.4 us (28%)
  starting transfers between devices  42.9 us (21%)
  local copies, waits for them, and re-layouts  8.51 us (4%)
    pallas_call x6, Pallas kernels, proj(): pl.pallas_call(functools.partial(proj_kernel, len(pieces), last), out_sha...  71 us
    ppermute x19, waiting for transfers between devices, flip(): return lax.ppermute(array, 'dp', [(i, i ^ code) for i in range(count)])  32.7 us
    ppermute x19, starting transfers between devices, flip(): return lax.ppermute(array, 'dp', [(i, i ^ code) for i in range(count)])  30.1 us
    ppermute x7, waiting for transfers between devices, swap_groups(): return lax.ppermute(array, 'groups', [(0, 1), (1, 0)])  23 us
    pallas_call x9, Pallas kernels, after(): pl.pallas_call(functools.partial(after_kernel, count, merge is not None),...  12.4 us
    ppermute x7, starting transfers between devices, swap_groups(): return lax.ppermute(array, 'groups', [(0, 1), (1, 0)])  6.89 us
    pallas_call x1, Pallas kernels, prepare(): pl.pallas_call(prepare_kernel, out_shape=[jax.ShapeDtypeStruct(x.shape, x...  6.41 us
    ppermute x2, starting transfers between devices, lines(): lax.ppermute(array, 'dp', [(a * 4 + rest, b * 4 + rest) for a, b in pairs...  5.91 us
  transfers between devices with their start and end apart: 28, of which 11 were waited for; matrix products, arithmetic and copies ran while one was open for 5% of the time, Pallas kernels for 42%

profile of v19, /device:TPU:9, one launch (start us, length us, event | category | flops | bytes accessed | tf_op | source)
XLA Modules:
  0.0 203.4 jit_solution(10993355828612344325)
XLA Ops:
  0.7 2.2 %constant_dynamic-slice_fusion.refs_4_ = bf16[64,7168]{1,0:T(8,128)(2,1)} fusion(bf16[64,14336]{1,0:T(8,128)(2,1)} %bitcast.19, s32[]{:T(128)S(6)} %select_n.20), kind=kLoop, calls=%fused_computation.22 | loop fusion | bytes 1835012 | tf_op jit(solution)/shard_map/dynamic_slice | solution.py:266
  2.9 1.2 collective-permute-start.1
  4.3 4.3 %collective-permute-start.3 = (bf16[64,7168]{1,0:T(8,128)(2,1)}, bf16[64,7168]{1,0:T(8,128)(2,1)}, u32[]{:S(2)}, u32[]{:S(2)}) collective-permute-start(bf16[64,7168]{1,0:T(8,128)(2,1)} %constant_dynamic-slice_fusion.refs_4_), channel_id=1, source_target_pairs={{4,8},{5,9},{6,10},{7,11},{8,4},{9,5},{10,6},{11,7},{20,24},{21,25... | collective-permute-start | bytes 2752520 | tf_op jit(solution)/shard_map/ppermute | solution.py:158
  8.6 6.4 %shard_map.73 = (bf16[64,7168]{1,0:T(8,128)(2,1)}, bf16[64,8192]{1,0:T(8,128)(2,1)}, bf16[64,8192]{1,0:T(8,128)(2,1)}, s32[1]{0:T(128)}) custom-call(s32[1]{0:T(128)} %constant.21.clone.1.works_ref, s32[1]{0:T(128)} %constant.14.clone.1.turn_ref, s32[1]{0:T(128)S(6)} %sub.13.first_ref, bf16[64,14336]{1,0:T(8,128)(2,1)} %bitcast.20, bf16[64,8192]{1,0:T(8,128)(2,1)} %bitcast.17), custom_call_target="tpu_custom_call" | custom-call | flops 1 | bytes 1 | tf_op jit(solution)/shard_map/pallas_call | solution.py:141
  15.0 9.6 %collective-permute-done.1.refs_1_ = bf16[64,7168]{1,0:T(8,128)(2,1)} collective-permute-done((bf16[64,7168]{1,0:T(8,128)(2,1)}, bf16[64,7168]{1,0:T(8,128)(2,1)}, u32[]{:S(2)}, u32[]{:S(2)}) %collective-permute-start.1) | collective-permute-done | bytes 917536 | tf_op jit(solution)/shard_map/ppermute | solution.py:62
  24.6 1.2 collective-permute-start.6
  25.8 2.7 %collective-permute-done.3.refs_3_ = bf16[64,7168]{1,0:T(8,128)(2,1)} collective-permute-done((bf16[64,7168]{1,0:T(8,128)(2,1)}, bf16[64,7168]{1,0:T(8,128)(2,1)}, u32[]{:S(2)}, u32[]{:S(2)}) %collective-permute-start.3) | collective-permute-done | bytes 917536 | tf_op jit(solution)/shard_map/ppermute | solution.py:158
  29.7 1.6 collective-permute-start.5
  31.3 1.2 collective-permute-start.7
  34.0 14.2 %collective-permute-done.6.refs_3_ = bf16[64,8192]{1,0:T(8,128)(2,1)} collective-permute-done((bf16[64,8192]{1,0:T(8,128)(2,1)}, bf16[64,8192]{1,0:T(8,128)(2,1)}, u32[]{:S(2)}, u32[]{:S(2)}) %collective-permute-start.6) | collective-permute-done | bytes 1048608 | tf_op jit(solution)/shard_map/ppermute | solution.py:62
  49.4 2.3 %collective-permute-done.7.refs_4_ = bf16[64,7168]{1,0:T(8,128)(2,1)} collective-permute-done((bf16[64,7168]{1,0:T(8,128)(2,1)}, bf16[64,7168]{1,0:T(8,128)(2,1)}, u32[]{:S(2)}, u32[]{:S(2)}) %collective-permute-start.7) | collective-permute-done | bytes 917536 | tf_op jit(solution)/shard_map/ppermute | solution.py:66
  51.7 3.2 %shard_map.76 = (bf16[64,7168]{1,0:T(8,128)(2,1)}, bf16[64,8192]{1,0:T(8,128)(2,1)}, bf16[64,7168]{1,0:T(8,128)(2,1)}, s32[1]{0:T(128)}) custom-call(s32[1]{0:T(128)} %bitcast.inside_ref, s32[1]{0:T(128)} %shard_map.75.turn_ref, bf16[64,7168]{1,0:T(8,128)(2,1)} %get-tuple-element.59.refs_0_, ...), custom_call_target="tpu_custom_call", output_to_operand_aliasing={{0}: (4, {}), {1}: (5, {}), {2}: (6, {})} | custom-call | flops 1 | bytes 1 | tf_op jit(solution)/shard_map/pallas_call | solution.py:106
  56.2 15.2 %collective-permute-done.10.refs_2_ = bf16[64,7168]{1,0:T(8,128)(2,1)} collective-permute-done((bf16[64,7168]{1,0:T(8,128)(2,1)}, bf16[64,7168]{1,0:T(8,128)(2,1)}, u32[]{:S(2)}, u32[]{:S(2)}) %collective-permute-start.10) | collective-permute-done | bytes 917536 | tf_op jit(solution)/shard_map/ppermute | solution.py:66
  74.1 1.2 collective-permute-start.13
  76.1 10.9 %shard_map.79 = (f32[1024,256]{1,0:T(8,128)}, s32[1]{0:T(128)}) custom-call(s32[1]{0:T(128)} %get-tuple-element.67.turn_ref, s32[3]{0:T(128)} %concatenate.21.at_ref, bf16[512,14336]{1,0:T(8,128)(2,1)} %own_ref.11, bf16[512,14336]{1,0:T(8,128)(2,1)} %collective-permute-done.refs_0_.other_ref, bf16[64,7168]{1,0:T(8,128)(2,1)} %get-tuple-element.60.refs_0_, ...), custom_call_target="tpu_custom_call" | custom-call | flops 1 | bytes 1 | tf_op jit(solution)/shard_map/pallas_call | solution.py:222
  87.1 2.4 %collective-permute-done.12.refs_1_ = bf16[64,7168]{1,0:T(8,128)(2,1)} collective-permute-done((bf16[64,7168]{1,0:T(8,128)(2,1)}, bf16[64,7168]{1,0:T(8,128)(2,1)}, u32[]{:S(2)}, u32[]{:S(2)}) %collective-permute-start.12) | collective-permute-done | bytes 917536 | tf_op jit(solution)/shard_map/ppermute | solution.py:62
  89.5 4.5 %collective-permute-done.11.refs_0_ = bf16[64,8192]{1,0:T(8,128)(2,1)} collective-permute-done((bf16[64,8192]{1,0:T(8,128)(2,1)}, bf16[64,8192]{1,0:T(8,128)(2,1)}, u32[]{:S(2)}, u32[]{:S(2)}) %collective-permute-start.11) | collective-permute-done | bytes 1048608 | tf_op jit(solution)/shard_map/ppermute | solution.py:62
  95.5 1.2 collective-permute-start.16
  97.4 10.8 %shard_map.81 = (f32[1024,256]{1,0:T(8,128)}, s32[1]{0:T(128)}) custom-call(s32[1]{0:T(128)} %get-tuple-element.72.turn_ref, s32[3]{0:T(128)} %concatenate.22.at_ref, bf16[512,14336]{1,0:T(8,128)(2,1)} %own_ref.11, bf16[512,14336]{1,0:T(8,128)(2,1)} %collective-permute-done.refs_0_.other_ref, bf16[64,7168]{1,0:T(8,128)(2,1)} %get-tuple-element.73.refs_0_, ...), custom_call_target="tpu_custom_call" | custom-call | flops 1 | bytes 1 | tf_op jit(solution)/shard_map/pallas_call | solution.py:222
  109.5 9.3 %collective-permute-start.18 = (bf16[64,8192]{1,0:T(8,128)(2,1)}, bf16[64,8192]{1,0:T(8,128)(2,1)}, u32[]{:S(2)}, u32[]{:S(2)}) collective-permute-start(bf16[64,8192]{1,0:T(8,128)(2,1)} %get-tuple-element.83.refs_3_), channel_id=1, source_target_pairs={{0,4},{1,5},{2,6},{3,7},{4,0},{5,1},{6,2},{7,3},{8,12},{9,13},{10,... | collective-permute-start | bytes 3145736 | tf_op jit(solution)/shard_map/ppermute | solution.py:62
  119.1 1.3 collective-permute-start.20
  120.4 9.8 %collective-permute-start.17 = (s32[2,4]{1,0:T(2,128)S(1)}, s32[2,4]{1,0:T(2,128)S(1)}, u32[]{:S(2)}, u32[]{:S(2)}) collective-permute-start(s32[2,4]{1,0:T(2,128)S(1)} %pad_add_fusion), channel_id=1, source_target_pairs={{0,1},{1,0},{2,3},{3,2},{4,5},{5,4},{6,7},{7,6},{8,9},{9,8},{10,11... | collective-permute-start | bytes 104 | tf_op jit(solution)/shard_map/ppermute | solution.py:62
  132.6 13.8 %shard_map.83 = (f32[8,256]{1,0:T(8,128)}, s32[1]{0:T(128)}) custom-call(s32[1]{0:T(128)} %get-tuple-element.80.turn_ref, s32[3]{0:T(128)} %broadcast_7_at_ref.2.at_ref, bf16[512,8192]{1,0:T(8,128)(2,1)} %own_ref.10, bf16[512,8192]{1,0:T(8,128)(2,1)} %collective-permute-done.4.refs_1_.other_ref, bf16[64,8192]{1,0:T(8,128)(2,1)} %bitcast.18, ...), custom_call_target="tpu_custom_call" | custom-call | flops 1 | bytes 1 | tf_op jit(solution)/shard_map/pallas_call | solution.py:222
  149.2 1.8 slice.19
  151.2 1.8 slice.20
  153.0 1.3 collective-permute-start.25
  154.3 10.9 %shard_map.85 = (f32[1024,256]{1,0:T(8,128)}, s32[1]{0:T(128)}) custom-call(s32[1]{0:T(128)} %get-tuple-element.92.turn_ref, s32[3]{0:T(128)} %concatenate.21.at_ref, bf16[512,14336]{1,0:T(8,128)(2,1)} %own_ref.11, bf16[512,14336]{1,0:T(8,128)(2,1)} %collective-permute-done.refs_0_.other_ref, bf16[64,7168]{1,0:T(8,128)(2,1)} %get-tuple-element.87.refs_0_, ...), custom_call_target="tpu_custom_call" | custom-call | flops 1 | bytes 1 | tf_op jit(solution)/shard_map/pallas_call | solution.py:222
  165.2 5.4 %collective-permute-done.22.refs_1_ = bf16[64,7168]{1,0:T(8,128)(2,1)} collective-permute-done((bf16[64,7168]{1,0:T(8,128)(2,1)}, bf16[64,7168]{1,0:T(8,128)(2,1)}, u32[]{:S(2)}, u32[]{:S(2)}) %collective-permute-start.22) | collective-permute-done | bytes 917536 | tf_op jit(solution)/shard_map/ppermute | solution.py:66
  170.6 2.3 %collective-permute-start.26 = (f32[8,256]{1,0:T(8,128)S(1)}, f32[8,256]{1,0:T(8,128)S(1)}, u32[]{:S(2)}, u32[]{:S(2)}) collective-permute-start(f32[8,256]{1,0:T(8,128)S(1)} %copy-done), channel_id=1, source_target_pairs={{0,1},{1,0},{2,3},{3,2},{4,5},{5,4},{6,7},{7,6},{8,9},{9,8},{10,11... | collective-permute-start | bytes 24584 | tf_op jit(solution)/shard_map/ppermute | solution.py:62
  174.7 11.7 %shard_map.87 = (f32[1024,256]{1,0:T(8,128)}, s32[1]{0:T(128)}) custom-call(s32[1]{0:T(128)} %get-tuple-element.98.turn_ref, s32[3]{0:T(128)} %broadcast_7_at_ref.2.at_ref, bf16[512,8192]{1,0:T(8,128)(2,1)} %own_ref.10, bf16[512,8192]{1,0:T(8,128)(2,1)} %collective-permute-done.4.refs_1_.other_ref, bf16[64,8192]{1,0:T(8,128)(2,1)} %get-tuple-element.99.refs_0_, ...), custom_call_target="tpu_custom_call" | custom-call | flops 1 | bytes 1 | tf_op jit(solution)/shard_map/pallas_call | solution.py:222
  186.5 12.9 %shard_map.88 = (f32[8,256]{1,0:T(8,128)}, s32[1]{0:T(128)}) custom-call(s32[1]{0:T(128)} %get-tuple-element.102.turn_ref, s32[3]{0:T(128)} %concatenate.22.at_ref, bf16[512,14336]{1,0:T(8,128)(2,1)} %own_ref.11, bf16[512,14336]{1,0:T(8,128)(2,1)} %collective-permute-done.refs_0_.other_ref, bf16[64,7168]{1,0:T(8,128)(2,1)} %get-tuple-element.103.refs_0_, ...), custom_call_target="tpu_custom_call" | custom-call | flops 1 | bytes 1 | tf_op jit(solution)/shard_map/pallas_call | solution.py:222
  201.6 1.9 fusion.1
  (71 shorter events, 22.4 us)
Async XLA Ops:
  0.0 28.5 %collective-permute-start = (bf16[512,14336]{1,0:T(8,128)(2,1)}, bf16[512,14336]{1,0:T(8,128)(2,1)}, u32[]{:S(2)}, u32[]{:S(2)}) collective-permute-start(bf16[512,14336]{1,0:T(8,128)(2,1)} %own_ref.11), channel_id=1, source_target_pairs={{0,1},{1,0},{2,3},{3,2},{4,5},{5,4},{6,7},{7,6},{8,9},{9,8},{10,11... | collective-permute-start | bytes 44040200 | tf_op jit(solution)/shard_map/ppermute | solution.py:62
  0.7 48.7 %collective-permute-start.4 = (bf16[512,8192]{1,0:T(8,128)(2,1)}, bf16[512,8192]{1,0:T(8,128)(2,1)}, u32[]{:S(2)}, u32[]{:S(2)}) collective-permute-start(bf16[512,8192]{1,0:T(8,128)(2,1)} %own_ref.10), channel_id=1, source_target_pairs={{0,1},{1,0},{2,3},{3,2},{4,5},{5,4},{6,7},{7,6},{8,9},{9,8},{10,11... | collective-permute-start | bytes 25165832 | tf_op jit(solution)/shard_map/ppermute | solution.py:62
  2.9 21.7 %collective-permute-start.1 = (bf16[64,7168]{1,0:T(8,128)(2,1)}, bf16[64,7168]{1,0:T(8,128)(2,1)}, u32[]{:S(2)}, u32[]{:S(2)}) collective-permute-start(bf16[64,7168]{1,0:T(8,128)(2,1)} %constant_dynamic-slice_fusion.refs_4_), channel_id=1, source_target_pairs={{0,2},{1,3},{2,0},{3,1},{4,6},{5,7},{6,4},{7,5},{8,10},{9,11},{10,... | collective-permute-start | bytes 2752520 | tf_op jit(solution)/shard_map/ppermute | solution.py:62
  4.1 21.7 %collective-permute-start.2 = (bf16[64,7168]{1,0:T(8,128)(2,1)}, bf16[64,7168]{1,0:T(8,128)(2,1)}, u32[]{:S(2)}, u32[]{:S(2)}) collective-permute-start(bf16[64,7168]{1,0:T(8,128)(2,1)} %constant_dynamic-slice_fusion.refs_4_), channel_id=1, source_target_pairs={{0,4},{1,5},{2,6},{3,7},{4,0},{5,1},{6,2},{7,3},{8,12},{9,13},{10,... | collective-permute-start | bytes 2752520 | tf_op jit(solution)/shard_map/ppermute | solution.py:62
  4.3 24.3 %collective-permute-start.3 = (bf16[64,7168]{1,0:T(8,128)(2,1)}, bf16[64,7168]{1,0:T(8,128)(2,1)}, u32[]{:S(2)}, u32[]{:S(2)}) collective-permute-start(bf16[64,7168]{1,0:T(8,128)(2,1)} %constant_dynamic-slice_fusion.refs_4_), channel_id=1, source_target_pairs={{4,8},{5,9},{6,10},{7,11},{8,4},{9,5},{10,6},{11,7},{20,24},{21,25... | collective-permute-start | bytes 2752520 | tf_op jit(solution)/shard_map/ppermute | solution.py:158
  24.6 23.6 %collective-permute-start.6 = (bf16[64,8192]{1,0:T(8,128)(2,1)}, bf16[64,8192]{1,0:T(8,128)(2,1)}, u32[]{:S(2)}, u32[]{:S(2)}) collective-permute-start(bf16[64,8192]{1,0:T(8,128)(2,1)} %get-tuple-element.61), channel_id=1, source_target_pairs={{0,2},{1,3},{2,0},{3,1},{4,6},{5,7},{6,4},{7,5},{8,10},{9,11},{10,... | collective-permute-start | bytes 3145736 | tf_op jit(solution)/shard_map/ppermute | solution.py:62
  29.7 19.8 %collective-permute-start.5 = (bf16[64,7168]{1,0:T(8,128)(2,1)}, bf16[64,7168]{1,0:T(8,128)(2,1)}, u32[]{:S(2)}, u32[]{:S(2)}) collective-permute-start(bf16[64,7168]{1,0:T(8,128)(2,1)} %get-tuple-element.60.refs_0_), channel_id=1, source_target_pairs={{0,12},{1,13},{2,14},{3,15},{12,0},{13,1},{14,2},{15,3},{16,28},{1... | collective-permute-start | bytes 2752520 | tf_op jit(solution)/shard_map/ppermute | solution.py:158
  31.3 20.5 %collective-permute-start.7 = (bf16[64,7168]{1,0:T(8,128)(2,1)}, bf16[64,7168]{1,0:T(8,128)(2,1)}, u32[]{:S(2)}, u32[]{:S(2)}) collective-permute-start(bf16[64,7168]{1,0:T(8,128)(2,1)} %get-tuple-element.62.refs_1_), channel_id=1, source_target_pairs={{0,16},{16,0},{1,17},{17,1},{2,18},{18,2},{3,19},{19,3},{4,20},{20... | collective-permute-start | bytes 2752520 | tf_op jit(solution)/shard_map/ppermute | solution.py:66
  33.7 37.7 %collective-permute-start.10 = (bf16[64,7168]{1,0:T(8,128)(2,1)}, bf16[64,7168]{1,0:T(8,128)(2,1)}, u32[]{:S(2)}, u32[]{:S(2)}) collective-permute-start(bf16[64,7168]{1,0:T(8,128)(2,1)} %get-tuple-element.65.refs_2_), channel_id=1, source_target_pairs={{0,16},{16,0},{1,17},{17,1},{2,18},{18,2},{3,19},{19,3},{4,20},{20... | collective-permute-start | bytes 2752520 | tf_op jit(solution)/shard_map/ppermute | solution.py:66
  48.2 23.2 %collective-permute-start.9 = (bf16[64,7168]{1,0:T(8,128)(2,1)}, bf16[64,7168]{1,0:T(8,128)(2,1)}, u32[]{:S(2)}, u32[]{:S(2)}) collective-permute-start(bf16[64,7168]{1,0:T(8,128)(2,1)} %get-tuple-element.65.refs_2_), channel_id=1, source_target_pairs={{0,2},{1,3},{2,0},{3,1},{4,6},{5,7},{6,4},{7,5},{8,10},{9,11},{10,... | collective-permute-start | bytes 2752520 | tf_op jit(solution)/shard_map/ppermute | solution.py:62
  54.9 17.4 %collective-permute-start.8 = (bf16[64,7168]{1,0:T(8,128)(2,1)}, bf16[64,7168]{1,0:T(8,128)(2,1)}, u32[]{:S(2)}, u32[]{:S(2)}) collective-permute-start(bf16[64,7168]{1,0:T(8,128)(2,1)} %get-tuple-element.64.refs_3_), channel_id=1, source_target_pairs={{0,4},{1,5},{2,6},{3,7},{4,0},{5,1},{6,2},{7,3},{8,12},{9,13},{10,... | collective-permute-start | bytes 2752520 | tf_op jit(solution)/shard_map/ppermute | solution.py:62
  73.5 20.5 %collective-permute-start.11 = (bf16[64,8192]{1,0:T(8,128)(2,1)}, bf16[64,8192]{1,0:T(8,128)(2,1)}, u32[]{:S(2)}, u32[]{:S(2)}) collective-permute-start(bf16[64,8192]{1,0:T(8,128)(2,1)} %get-tuple-element.69), channel_id=1, source_target_pairs={{0,4},{1,5},{2,6},{3,7},{4,0},{5,1},{6,2},{7,3},{8,12},{9,13},{10,... | collective-permute-start | bytes 3145736 | tf_op jit(solution)/shard_map/ppermute | solution.py:62
  73.9 15.6 %collective-permute-start.12 = (bf16[64,7168]{1,0:T(8,128)(2,1)}, bf16[64,7168]{1,0:T(8,128)(2,1)}, u32[]{:S(2)}, u32[]{:S(2)}) collective-permute-start(bf16[64,7168]{1,0:T(8,128)(2,1)} %get-tuple-element.64.refs_3_), channel_id=1, source_target_pairs={{0,2},{1,3},{2,0},{3,1},{4,6},{5,7},{6,4},{7,5},{8,10},{9,11},{10,... | collective-permute-start | bytes 2752520 | tf_op jit(solution)/shard_map/ppermute | solution.py:62
  74.1 15.4 %collective-permute-start.13 = (bf16[64,7168]{1,0:T(8,128)(2,1)}, bf16[64,7168]{1,0:T(8,128)(2,1)}, u32[]{:S(2)}, u32[]{:S(2)}) collective-permute-start(bf16[64,7168]{1,0:T(8,128)(2,1)} %get-tuple-element.64.refs_3_), channel_id=1, source_target_pairs={{0,16},{16,0},{1,17},{17,1},{2,18},{18,2},{3,19},{19,3},{4,20},{20... | collective-permute-start | bytes 2752520 | tf_op jit(solution)/shard_map/ppermute | solution.py:66
  75.3 32.9 %collective-permute-start.14 = (bf16[64,8192]{1,0:T(8,128)(2,1)}, bf16[64,8192]{1,0:T(8,128)(2,1)}, u32[]{:S(2)}, u32[]{:S(2)}) collective-permute-start(bf16[64,8192]{1,0:T(8,128)(2,1)} %get-tuple-element.61), channel_id=1, source_target_pairs={{0,12},{1,13},{2,14},{3,15},{4,8},{5,9},{6,10},{7,11},{8,4},{9,5},... | collective-permute-start | bytes 3145736 | tf_op jit(solution)/shard_map/ppermute | solution.py:62
  76.1 21.1 %copy-start.1 = (s32[4]{0:T(128)S(1)}, s32[4]{0:T(128)}, u32[]{:S(2)}) copy-start(s32[4]{0:T(128)} %param.11) | copy-start | bytes 52
  95.1 13.2 %collective-permute-start.15 = (bf16[64,7168]{1,0:T(8,128)(2,1)}, bf16[64,7168]{1,0:T(8,128)(2,1)}, u32[]{:S(2)}, u32[]{:S(2)}) collective-permute-start(bf16[64,7168]{1,0:T(8,128)(2,1)} %get-tuple-element.78.refs_2_), channel_id=1, source_target_pairs={{0,2},{1,3},{2,0},{3,1},{4,6},{5,7},{6,4},{7,5},{8,10},{9,11},{10,... | collective-permute-start | bytes 2752520 | tf_op jit(solution)/shard_map/ppermute | solution.py:62
  95.5 12.9 %collective-permute-start.16 = (bf16[64,7168]{1,0:T(8,128)(2,1)}, bf16[64,7168]{1,0:T(8,128)(2,1)}, u32[]{:S(2)}, u32[]{:S(2)}) collective-permute-start(bf16[64,7168]{1,0:T(8,128)(2,1)} %get-tuple-element.78.refs_2_), channel_id=1, source_target_pairs={{0,16},{16,0},{1,17},{17,1},{2,18},{18,2},{3,19},{19,3},{4,20},{20... | collective-permute-start | bytes 2752520 | tf_op jit(solution)/shard_map/ppermute | solution.py:66
  97.4 21.7 %copy-start.2 = (s32[4]{0:T(128)S(1)}, s32[4]{0:T(128)}, u32[]{:S(2)}) copy-start(s32[4]{0:T(128)} %param.12) | copy-start | bytes 52
  97.4 32.8 %copy-start.3 = (s32[8]{0:T(128)S(1)}, s32[8]{0:T(128)}, u32[]{:S(2)}) copy-start(s32[8]{0:T(128)} %constant.51.clone) | copy-start | bytes 100
  109.5 37.0 %collective-permute-start.18 = (bf16[64,8192]{1,0:T(8,128)(2,1)}, bf16[64,8192]{1,0:T(8,128)(2,1)}, u32[]{:S(2)}, u32[]{:S(2)}) collective-permute-start(bf16[64,8192]{1,0:T(8,128)(2,1)} %get-tuple-element.83.refs_3_), channel_id=1, source_target_pairs={{0,4},{1,5},{2,6},{3,7},{4,0},{5,1},{6,2},{7,3},{8,12},{9,13},{10,... | collective-permute-start | bytes 3145736 | tf_op jit(solution)/shard_map/ppermute | solution.py:62
  118.8 27.7 %collective-permute-start.19 = (bf16[64,8192]{1,0:T(8,128)(2,1)}, bf16[64,8192]{1,0:T(8,128)(2,1)}, u32[]{:S(2)}, u32[]{:S(2)}) collective-permute-start(bf16[64,8192]{1,0:T(8,128)(2,1)} %get-tuple-element.83.refs_3_), channel_id=1, source_target_pairs={{0,2},{1,3},{2,0},{3,1},{4,6},{5,7},{6,4},{7,5},{8,10},{9,11},{10,... | collective-permute-start | bytes 3145736 | tf_op jit(solution)/shard_map/ppermute | solution.py:62
  119.1 27.4 %collective-permute-start.20 = (bf16[64,7168]{1,0:T(8,128)(2,1)}, bf16[64,7168]{1,0:T(8,128)(2,1)}, u32[]{:S(2)}, u32[]{:S(2)}) collective-permute-start(bf16[64,7168]{1,0:T(8,128)(2,1)} %get-tuple-element.87.refs_0_), channel_id=1, source_target_pairs={{0,16},{16,0},{1,17},{17,1},{2,18},{18,2},{3,19},{19,3},{4,20},{20... | collective-permute-start | bytes 2752520 | tf_op jit(solution)/shard_map/ppermute | solution.py:66
  120.4 11.0 %collective-permute-start.17 = (s32[2,4]{1,0:T(2,128)S(1)}, s32[2,4]{1,0:T(2,128)S(1)}, u32[]{:S(2)}, u32[]{:S(2)}) collective-permute-start(s32[2,4]{1,0:T(2,128)S(1)} %pad_add_fusion), channel_id=1, source_target_pairs={{0,1},{1,0},{2,3},{3,2},{4,5},{5,4},{6,7},{7,6},{8,9},{9,8},{10,11... | collective-permute-start | bytes 104 | tf_op jit(solution)/shard_map/ppermute | solution.py:62
  147.6 25.3 %collective-permute-start.21 = (bf16[64,8192]{1,0:T(8,128)(2,1)}, bf16[64,8192]{1,0:T(8,128)(2,1)}, u32[]{:S(2)}, u32[]{:S(2)}) collective-permute-start(bf16[64,8192]{1,0:T(8,128)(2,1)} %get-tuple-element.96.refs_2_), channel_id=1, source_target_pairs={{0,2},{1,3},{2,0},{3,1},{4,6},{5,7},{6,4},{7,5},{8,10},{9,11},{10,... | collective-permute-start | bytes 3145736 | tf_op jit(solution)/shard_map/ppermute | solution.py:62
  148.8 24.8 %collective-permute-start.23 = (bf16[64,8192]{1,0:T(8,128)(2,1)}, bf16[64,8192]{1,0:T(8,128)(2,1)}, u32[]{:S(2)}, u32[]{:S(2)}) collective-permute-start(bf16[64,8192]{1,0:T(8,128)(2,1)} %get-tuple-element.97), channel_id=1, source_target_pairs={{0,4},{1,5},{2,6},{3,7},{4,0},{5,1},{6,2},{7,3},{8,12},{9,13},{10,... | collective-permute-start | bytes 3145736 | tf_op jit(solution)/shard_map/ppermute | solution.py:62
  148.8 21.7 %collective-permute-start.22 = (bf16[64,7168]{1,0:T(8,128)(2,1)}, bf16[64,7168]{1,0:T(8,128)(2,1)}, u32[]{:S(2)}, u32[]{:S(2)}) collective-permute-start(bf16[64,7168]{1,0:T(8,128)(2,1)} %get-tuple-element.93.refs_1_), channel_id=1, source_target_pairs={{0,16},{16,0},{1,17},{17,1},{2,18},{18,2},{3,19},{19,3},{4,20},{20... | collective-permute-start | bytes 2752520 | tf_op jit(solution)/shard_map/ppermute | solution.py:66
  151.0 35.4 %collective-permute-start.24 = (bf16[32,7168]{1,0:T(8,128)(2,1)}, bf16[32,7168]{1,0:T(8,128)(2,1)}, u32[]{:S(2)}, u32[]{:S(2)}) collective-permute-start(bf16[32,7168]{1,0:T(8,128)(2,1)} %slice.19), channel_id=1, source_target_pairs={{0,2},{1,3},{2,0},{3,1},{4,6},{5,7},{6,4},{7,5},{8,10},{9,11},{10,... | collective-permute-start | bytes 1376264 | tf_op jit(solution)/shard_map/ppermute | solution.py:62
  153.0 33.4 %collective-permute-start.25 = (bf16[32,7168]{1,0:T(8,128)(2,1)}, bf16[32,7168]{1,0:T(8,128)(2,1)}, u32[]{:S(2)}, u32[]{:S(2)}) collective-permute-start(bf16[32,7168]{1,0:T(8,128)(2,1)} %slice.20), channel_id=1, source_target_pairs={{0,16},{16,0},{1,17},{17,1},{2,18},{18,2},{3,19},{19,3},{4,20},{20... | collective-permute-start | bytes 1376264 | tf_op jit(solution)/shard_map/ppermute | solution.py:66
  154.3 16.3 %copy-start = (f32[8,256]{1,0:T(8,128)S(1)}, f32[8,256]{1,0:T(8,128)}, u32[]{:S(2)}) copy-start(f32[8,256]{1,0:T(8,128)} %get-tuple-element.91) | copy-start | bytes 24580
  170.6 30.0 %collective-permute-start.26 = (f32[8,256]{1,0:T(8,128)S(1)}, f32[8,256]{1,0:T(8,128)S(1)}, u32[]{:S(2)}, u32[]{:S(2)}) collective-permute-start(f32[8,256]{1,0:T(8,128)S(1)} %copy-done), channel_id=1, source_target_pairs={{0,1},{1,0},{2,3},{3,2},{4,5},{5,4},{6,7},{7,6},{8,9},{9,8},{10,11... | collective-permute-start | bytes 24584 | tf_op jit(solution)/shard_map/ppermute | solution.py:62
  199.3 2.2 %collective-permute-start.27 = (f32[8,256]{1,0:T(8,128)}, f32[8,256]{1,0:T(8,128)S(1)}, u32[]{:S(2)}, u32[]{:S(2)}) collective-permute-start(f32[8,256]{1,0:T(8,128)} %get-tuple-element.108), channel_id=1, source_target_pairs={{0,1},{1,0},{2,3},{3,2},{4,5},{5,4},{6,7},{7,6},{8,9},{9,8},{10,11... | collective-permute-start | bytes 24584 | tf_op jit(solution)/shard_map/ppermute | solution.py:62

commit v20 on v19

--- a/solution.py
+++ b/solution.py
@@ -86,7 +86,7 @@
 def after_kernel(count, merges, inside_ref, turn_ref, *refs):
     if merges:
         refs, staging = refs[:-3], refs[-3:]
-        source, target = refs[0], refs[-1 - count]
+        source, target = refs[0], refs[-2]
 
         @pl.when(inside_ref[0] == 1)
         def _():
@@ -327,7 +327,7 @@
     c["x"] = swap_groups(a["x"])
     turn = pause(turn)
 
-    turn, (a["f"], b["x"], c["x"]) = after(turn, [a_end, b["x"], c["x"]], inside, a_mid, [grads_there])
+    turn, (c["x"], b["x"], a["f"]) = after(turn, [c["x"], b["x"], a_end], inside, a_mid, [grads_there])
     a["o"] = near(a["f"])
     a["xn"] = over_x(a["n"])
     c["n"] = swap_groups(a["n"])

time: 205 us -> 218 us (1.063)
  the two profiles are of different devices: /device:TPU:9 before, /device:TPU:25 now
where the time goes in v20:
time: 218 us
  Pallas kernels  87.7 us (40%)
  waiting for transfers between devices  70.1 us (32%)
  starting transfers between devices  47.7 us (22%)
  local copies, waits for them, and re-layouts  8.5 us (4%)
    pallas_call x6, Pallas kernels, proj(): pl.pallas_call(functools.partial(proj_kernel, len(pieces), last), out_sha...  70.8 us
    ppermute x19, waiting for transfers between devices, flip(): return lax.ppermute(array, 'dp', [(i, i ^ code) for i in range(count)])  50.3 us
    ppermute x19, starting transfers between devices, flip(): return lax.ppermute(array, 'dp', [(i, i ^ code) for i in range(count)])  38.8 us
    ppermute x7, waiting for transfers between devices, swap_groups(): return lax.ppermute(array, 'groups', [(0, 1), (1, 0)])  17 us
    pallas_call x9, Pallas kernels, after(): pl.pallas_call(functools.partial(after_kernel, count, merge is not None),...  10.5 us
    pallas_call x1, Pallas kernels, prepare(): pl.pallas_call(prepare_kernel, out_shape=[jax.ShapeDtypeStruct(x.shape, x...  6.4 us
    ppermute x7, starting transfers between devices, swap_groups(): return lax.ppermute(array, 'groups', [(0, 1), (1, 0)])  5.33 us
  transfers between devices with their start and end apart: 28, of which 12 were waited for; matrix products, arithmetic and copies ran while one was open for 5% of the time, Pallas kernels for 39%

profile of v20, /device:TPU:25, one launch (start us, length us, event | category | flops | bytes accessed | tf_op | source)
XLA Modules:
  0.0 217.8 jit_solution(17386964510183792916)
XLA Ops:
  0.7 2.2 %constant_dynamic-slice_fusion.refs_4_ = bf16[64,7168]{1,0:T(8,128)(2,1)} fusion(bf16[64,14336]{1,0:T(8,128)(2,1)} %bitcast.19, s32[]{:T(128)S(6)} %select_n.20), kind=kLoop, calls=%fused_computation.22 | loop fusion | bytes 1835012 | tf_op jit(solution)/shard_map/dynamic_slice | solution.py:266
  2.9 1.2 collective-permute-start.1
  4.3 1.6 collective-permute-start.3
  5.9 6.4 %shard_map.73 = (bf16[64,7168]{1,0:T(8,128)(2,1)}, bf16[64,8192]{1,0:T(8,128)(2,1)}, bf16[64,8192]{1,0:T(8,128)(2,1)}, s32[1]{0:T(128)}) custom-call(s32[1]{0:T(128)} %constant.21.clone.1.works_ref, s32[1]{0:T(128)} %constant.14.clone.1.turn_ref, s32[1]{0:T(128)S(6)} %sub.13.first_ref, bf16[64,14336]{1,0:T(8,128)(2,1)} %bitcast.20, bf16[64,8192]{1,0:T(8,128)(2,1)} %bitcast.17), custom_call_target="tpu_custom_call" | custom-call | flops 1 | bytes 1 | tf_op jit(solution)/shard_map/pallas_call | solution.py:141
  12.3 12.3 %collective-permute-done.1.refs_1_ = bf16[64,7168]{1,0:T(8,128)(2,1)} collective-permute-done((bf16[64,7168]{1,0:T(8,128)(2,1)}, bf16[64,7168]{1,0:T(8,128)(2,1)}, u32[]{:S(2)}, u32[]{:S(2)}) %collective-permute-start.1) | collective-permute-done | bytes 917536 | tf_op jit(solution)/shard_map/ppermute | solution.py:62
  24.6 1.2 collective-permute-start.6
  27.0 1.3 collective-permute-start.5
  28.3 1.9 collective-permute-start.7
  31.7 16.5 %collective-permute-done.6.refs_3_ = bf16[64,8192]{1,0:T(8,128)(2,1)} collective-permute-done((bf16[64,8192]{1,0:T(8,128)(2,1)}, bf16[64,8192]{1,0:T(8,128)(2,1)}, u32[]{:S(2)}, u32[]{:S(2)}) %collective-permute-start.6) | collective-permute-done | bytes 1048608 | tf_op jit(solution)/shard_map/ppermute | solution.py:62
  48.2 1.2 collective-permute-start.9
  49.4 2.8 %collective-permute-done.7.refs_4_ = bf16[64,7168]{1,0:T(8,128)(2,1)} collective-permute-done((bf16[64,7168]{1,0:T(8,128)(2,1)}, bf16[64,7168]{1,0:T(8,128)(2,1)}, u32[]{:S(2)}, u32[]{:S(2)}) %collective-permute-start.7) | collective-permute-done | bytes 917536 | tf_op jit(solution)/shard_map/ppermute | solution.py:158
  52.2 1.2 shard_map.76
  54.7 12.5 %collective-permute-done.10.refs_2_ = bf16[64,7168]{1,0:T(8,128)(2,1)} collective-permute-done((bf16[64,7168]{1,0:T(8,128)(2,1)}, bf16[64,7168]{1,0:T(8,128)(2,1)}, u32[]{:S(2)}, u32[]{:S(2)}) %collective-permute-start.10) | collective-permute-done | bytes 917536 | tf_op jit(solution)/shard_map/ppermute | solution.py:66
  68.1 4.2 %collective-permute-done.8.refs_0_ = bf16[64,7168]{1,0:T(8,128)(2,1)} collective-permute-done((bf16[64,7168]{1,0:T(8,128)(2,1)}, bf16[64,7168]{1,0:T(8,128)(2,1)}, u32[]{:S(2)}, u32[]{:S(2)}) %collective-permute-start.8) | collective-permute-done | bytes 917536 | tf_op jit(solution)/shard_map/ppermute | solution.py:62
  75.3 10.9 %shard_map.79 = (f32[1024,256]{1,0:T(8,128)}, s32[1]{0:T(128)}) custom-call(s32[1]{0:T(128)} %get-tuple-element.67.turn_ref, s32[3]{0:T(128)} %concatenate.21.at_ref, bf16[512,14336]{1,0:T(8,128)(2,1)} %own_ref.11, bf16[512,14336]{1,0:T(8,128)(2,1)} %collective-permute-done.refs_0_.other_ref, bf16[64,7168]{1,0:T(8,128)(2,1)} %get-tuple-element.62.refs_0_, ...), custom_call_target="tpu_custom_call" | custom-call | flops 1 | bytes 1 | tf_op jit(solution)/shard_map/pallas_call | solution.py:222
  86.2 5.1 %collective-permute-done.12.refs_1_ = bf16[64,7168]{1,0:T(8,128)(2,1)} collective-permute-done((bf16[64,7168]{1,0:T(8,128)(2,1)}, bf16[64,7168]{1,0:T(8,128)(2,1)}, u32[]{:S(2)}, u32[]{:S(2)}) %collective-permute-start.12) | collective-permute-done | bytes 917536 | tf_op jit(solution)/shard_map/ppermute | solution.py:62
  91.3 4.9 %collective-permute-done.11.refs_0_ = bf16[64,8192]{1,0:T(8,128)(2,1)} collective-permute-done((bf16[64,8192]{1,0:T(8,128)(2,1)}, bf16[64,8192]{1,0:T(8,128)(2,1)}, u32[]{:S(2)}, u32[]{:S(2)}) %collective-permute-start.11) | collective-permute-done | bytes 1048608 | tf_op jit(solution)/shard_map/ppermute | solution.py:62
  98.5 10.8 %shard_map.81 = (f32[1024,256]{1,0:T(8,128)}, s32[1]{0:T(128)}) custom-call(s32[1]{0:T(128)} %get-tuple-element.72.turn_ref, s32[3]{0:T(128)} %concatenate.22.at_ref, bf16[512,14336]{1,0:T(8,128)(2,1)} %own_ref.11, bf16[512,14336]{1,0:T(8,128)(2,1)} %collective-permute-done.refs_0_.other_ref, bf16[64,7168]{1,0:T(8,128)(2,1)} %get-tuple-element.73.refs_0_, ...), custom_call_target="tpu_custom_call" | custom-call | flops 1 | bytes 1 | tf_op jit(solution)/shard_map/pallas_call | solution.py:222
  109.3 5.4 %collective-permute-done.14.refs_0_ = bf16[64,8192]{1,0:T(8,128)(2,1)} collective-permute-done((bf16[64,8192]{1,0:T(8,128)(2,1)}, bf16[64,8192]{1,0:T(8,128)(2,1)}, u32[]{:S(2)}, u32[]{:S(2)}) %collective-permute-start.14) | collective-permute-done | bytes 1048608 | tf_op jit(solution)/shard_map/ppermute | solution.py:62
  116.3 1.3 collective-permute-start.20
  117.6 27.8 %collective-permute-start.17 = (s32[2,4]{1,0:T(2,128)S(1)}, s32[2,4]{1,0:T(2,128)S(1)}, u32[]{:S(2)}, u32[]{:S(2)}) collective-permute-start(s32[2,4]{1,0:T(2,128)S(1)} %pad_add_fusion), channel_id=1, source_target_pairs={{0,1},{1,0},{2,3},{3,2},{4,5},{5,4},{6,7},{7,6},{8,9},{9,8},{10,11... | collective-permute-start | bytes 104 | tf_op jit(solution)/shard_map/ppermute | solution.py:62
  147.8 13.7 %shard_map.83 = (f32[8,256]{1,0:T(8,128)}, s32[1]{0:T(128)}) custom-call(s32[1]{0:T(128)} %get-tuple-element.80.turn_ref, s32[3]{0:T(128)} %broadcast_7_at_ref.2.at_ref, bf16[512,8192]{1,0:T(8,128)(2,1)} %own_ref.10, bf16[512,8192]{1,0:T(8,128)(2,1)} %collective-permute-done.4.refs_1_.other_ref, bf16[64,8192]{1,0:T(8,128)(2,1)} %bitcast.18, ...), custom_call_target="tpu_custom_call" | custom-call | flops 1 | bytes 1 | tf_op jit(solution)/shard_map/pallas_call | solution.py:222
  163.2 1.3 collective-permute-start.22
  164.5 1.8 slice.19
  166.6 1.8 slice.20
  169.5 10.9 %shard_map.85 = (f32[1024,256]{1,0:T(8,128)}, s32[1]{0:T(128)}) custom-call(s32[1]{0:T(128)} %get-tuple-element.92.turn_ref, s32[3]{0:T(128)} %concatenate.21.at_ref, bf16[512,14336]{1,0:T(8,128)(2,1)} %own_ref.11, bf16[512,14336]{1,0:T(8,128)(2,1)} %collective-permute-done.refs_0_.other_ref, bf16[64,7168]{1,0:T(8,128)(2,1)} %get-tuple-element.87.refs_0_, ...), custom_call_target="tpu_custom_call" | custom-call | flops 1 | bytes 1 | tf_op jit(solution)/shard_map/pallas_call | solution.py:222
  180.4 4.4 %collective-permute-done.22.refs_1_ = bf16[64,7168]{1,0:T(8,128)(2,1)} collective-permute-done((bf16[64,7168]{1,0:T(8,128)(2,1)}, bf16[64,7168]{1,0:T(8,128)(2,1)}, u32[]{:S(2)}, u32[]{:S(2)}) %collective-permute-start.22) | collective-permute-done | bytes 917536 | tf_op jit(solution)/shard_map/ppermute | solution.py:66
  184.8 2.5 %collective-permute-start.26 = (f32[8,256]{1,0:T(8,128)S(1)}, f32[8,256]{1,0:T(8,128)S(1)}, u32[]{:S(2)}, u32[]{:S(2)}) collective-permute-start(f32[8,256]{1,0:T(8,128)S(1)} %copy-done), channel_id=1, source_target_pairs={{0,1},{1,0},{2,3},{3,2},{4,5},{5,4},{6,7},{7,6},{8,9},{9,8},{10,11... | collective-permute-start | bytes 24584 | tf_op jit(solution)/shard_map/ppermute | solution.py:62
  189.1 11.7 %shard_map.87 = (f32[1024,256]{1,0:T(8,128)}, s32[1]{0:T(128)}) custom-call(s32[1]{0:T(128)} %get-tuple-element.98.turn_ref, s32[3]{0:T(128)} %broadcast_7_at_ref.2.at_ref, bf16[512,8192]{1,0:T(8,128)(2,1)} %own_ref.10, bf16[512,8192]{1,0:T(8,128)(2,1)} %collective-permute-done.4.refs_1_.other_ref, bf16[64,8192]{1,0:T(8,128)(2,1)} %get-tuple-element.99.refs_0_, ...), custom_call_target="tpu_custom_call" | custom-call | flops 1 | bytes 1 | tf_op jit(solution)/shard_map/pallas_call | solution.py:222
  200.8 12.9 %shard_map.88 = (f32[8,256]{1,0:T(8,128)}, s32[1]{0:T(128)}) custom-call(s32[1]{0:T(128)} %get-tuple-element.102.turn_ref, s32[3]{0:T(128)} %concatenate.22.at_ref, bf16[512,14336]{1,0:T(8,128)(2,1)} %own_ref.11, bf16[512,14336]{1,0:T(8,128)(2,1)} %collective-permute-done.refs_0_.other_ref, bf16[64,7168]{1,0:T(8,128)(2,1)} %get-tuple-element.103.refs_0_, ...), custom_call_target="tpu_custom_call" | custom-call | flops 1 | bytes 1 | tf_op jit(solution)/shard_map/pallas_call | solution.py:222
  213.7 1.3 collective-permute-start.27
  216.0 1.9 fusion.1
  (71 shorter events, 20.6 us)
Async XLA Ops:
  0.0 25.8 %collective-permute-start = (bf16[512,14336]{1,0:T(8,128)(2,1)}, bf16[512,14336]{1,0:T(8,128)(2,1)}, u32[]{:S(2)}, u32[]{:S(2)}) collective-permute-start(bf16[512,14336]{1,0:T(8,128)(2,1)} %own_ref.11), channel_id=1, source_target_pairs={{0,1},{1,0},{2,3},{3,2},{4,5},{5,4},{6,7},{7,6},{8,9},{9,8},{10,11... | collective-permute-start | bytes 44040200 | tf_op jit(solution)/shard_map/ppermute | solution.py:62
  0.7 48.7 %collective-permute-start.4 = (bf16[512,8192]{1,0:T(8,128)(2,1)}, bf16[512,8192]{1,0:T(8,128)(2,1)}, u32[]{:S(2)}, u32[]{:S(2)}) collective-permute-start(bf16[512,8192]{1,0:T(8,128)(2,1)} %own_ref.10), channel_id=1, source_target_pairs={{0,1},{1,0},{2,3},{3,2},{4,5},{5,4},{6,7},{7,6},{8,9},{9,8},{10,11... | collective-permute-start | bytes 25165832 | tf_op jit(solution)/shard_map/ppermute | solution.py:62
  2.9 21.7 %collective-permute-start.1 = (bf16[64,7168]{1,0:T(8,128)(2,1)}, bf16[64,7168]{1,0:T(8,128)(2,1)}, u32[]{:S(2)}, u32[]{:S(2)}) collective-permute-start(bf16[64,7168]{1,0:T(8,128)(2,1)} %constant_dynamic-slice_fusion.refs_4_), channel_id=1, source_target_pairs={{0,2},{1,3},{2,0},{3,1},{4,6},{5,7},{6,4},{7,5},{8,10},{9,11},{10,... | collective-permute-start | bytes 2752520 | tf_op jit(solution)/shard_map/ppermute | solution.py:62
  4.1 21.7 %collective-permute-start.2 = (bf16[64,7168]{1,0:T(8,128)(2,1)}, bf16[64,7168]{1,0:T(8,128)(2,1)}, u32[]{:S(2)}, u32[]{:S(2)}) collective-permute-start(bf16[64,7168]{1,0:T(8,128)(2,1)} %constant_dynamic-slice_fusion.refs_4_), channel_id=1, source_target_pairs={{0,4},{1,5},{2,6},{3,7},{4,0},{5,1},{6,2},{7,3},{8,12},{9,13},{10,... | collective-permute-start | bytes 2752520 | tf_op jit(solution)/shard_map/ppermute | solution.py:62
  4.3 21.6 %collective-permute-start.3 = (bf16[64,7168]{1,0:T(8,128)(2,1)}, bf16[64,7168]{1,0:T(8,128)(2,1)}, u32[]{:S(2)}, u32[]{:S(2)}) collective-permute-start(bf16[64,7168]{1,0:T(8,128)(2,1)} %constant_dynamic-slice_fusion.refs_4_), channel_id=1, source_target_pairs={{4,8},{5,9},{6,10},{7,11},{8,4},{9,5},{10,6},{11,7},{20,24},{21,25... | collective-permute-start | bytes 2752520 | tf_op jit(solution)/shard_map/ppermute | solution.py:158
  24.6 23.6 %collective-permute-start.6 = (bf16[64,8192]{1,0:T(8,128)(2,1)}, bf16[64,8192]{1,0:T(8,128)(2,1)}, u32[]{:S(2)}, u32[]{:S(2)}) collective-permute-start(bf16[64,8192]{1,0:T(8,128)(2,1)} %get-tuple-element.61), channel_id=1, source_target_pairs={{0,2},{1,3},{2,0},{3,1},{4,6},{5,7},{6,4},{7,5},{8,10},{9,11},{10,... | collective-permute-start | bytes 3145736 | tf_op jit(solution)/shard_map/ppermute | solution.py:62
  27.0 22.5 %collective-permute-start.5 = (bf16[64,7168]{1,0:T(8,128)(2,1)}, bf16[64,7168]{1,0:T(8,128)(2,1)}, u32[]{:S(2)}, u32[]{:S(2)}) collective-permute-start(bf16[64,7168]{1,0:T(8,128)(2,1)} %get-tuple-element.60.refs_1_), channel_id=1, source_target_pairs={{0,16},{16,0},{1,17},{17,1},{2,18},{18,2},{3,19},{19,3},{4,20},{20... | collective-permute-start | bytes 2752520 | tf_op jit(solution)/shard_map/ppermute | solution.py:66
  28.3 23.9 %collective-permute-start.7 = (bf16[64,7168]{1,0:T(8,128)(2,1)}, bf16[64,7168]{1,0:T(8,128)(2,1)}, u32[]{:S(2)}, u32[]{:S(2)}) collective-permute-start(bf16[64,7168]{1,0:T(8,128)(2,1)} %get-tuple-element.62.refs_0_), channel_id=1, source_target_pairs={{0,12},{1,13},{2,14},{3,15},{12,0},{13,1},{14,2},{15,3},{16,28},{1... | collective-permute-start | bytes 2752520 | tf_op jit(solution)/shard_map/ppermute | solution.py:158
  31.4 35.8 %collective-permute-start.10 = (bf16[64,7168]{1,0:T(8,128)(2,1)}, bf16[64,7168]{1,0:T(8,128)(2,1)}, u32[]{:S(2)}, u32[]{:S(2)}) collective-permute-start(bf16[64,7168]{1,0:T(8,128)(2,1)} %get-tuple-element.65.refs_2_), channel_id=1, source_target_pairs={{0,16},{16,0},{1,17},{17,1},{2,18},{18,2},{3,19},{19,3},{4,20},{20... | collective-permute-start | bytes 2752520 | tf_op jit(solution)/shard_map/ppermute | solution.py:66
  48.2 19.9 %collective-permute-start.9 = (bf16[64,7168]{1,0:T(8,128)(2,1)}, bf16[64,7168]{1,0:T(8,128)(2,1)}, u32[]{:S(2)}, u32[]{:S(2)}) collective-permute-start(bf16[64,7168]{1,0:T(8,128)(2,1)} %get-tuple-element.65.refs_2_), channel_id=1, source_target_pairs={{0,2},{1,3},{2,0},{3,1},{4,6},{5,7},{6,4},{7,5},{8,10},{9,11},{10,... | collective-permute-start | bytes 2752520 | tf_op jit(solution)/shard_map/ppermute | solution.py:62
  53.4 18.9 %collective-permute-start.8 = (bf16[64,7168]{1,0:T(8,128)(2,1)}, bf16[64,7168]{1,0:T(8,128)(2,1)}, u32[]{:S(2)}, u32[]{:S(2)}) collective-permute-start(bf16[64,7168]{1,0:T(8,128)(2,1)} %get-tuple-element.64.refs_3_), channel_id=1, source_target_pairs={{0,4},{1,5},{2,6},{3,7},{4,0},{5,1},{6,2},{7,3},{8,12},{9,13},{10,... | collective-permute-start | bytes 2752520 | tf_op jit(solution)/shard_map/ppermute | solution.py:62
  73.5 22.7 %collective-permute-start.11 = (bf16[64,8192]{1,0:T(8,128)(2,1)}, bf16[64,8192]{1,0:T(8,128)(2,1)}, u32[]{:S(2)}, u32[]{:S(2)}) collective-permute-start(bf16[64,8192]{1,0:T(8,128)(2,1)} %get-tuple-element.69), channel_id=1, source_target_pairs={{0,4},{1,5},{2,6},{3,7},{4,0},{5,1},{6,2},{7,3},{8,12},{9,13},{10,... | collective-permute-start | bytes 3145736 | tf_op jit(solution)/shard_map/ppermute | solution.py:62
  73.5 17.7 %collective-permute-start.12 = (bf16[64,7168]{1,0:T(8,128)(2,1)}, bf16[64,7168]{1,0:T(8,128)(2,1)}, u32[]{:S(2)}, u32[]{:S(2)}) collective-permute-start(bf16[64,7168]{1,0:T(8,128)(2,1)} %get-tuple-element.64.refs_3_), channel_id=1, source_target_pairs={{0,2},{1,3},{2,0},{3,1},{4,6},{5,7},{6,4},{7,5},{8,10},{9,11},{10,... | collective-permute-start | bytes 2752520 | tf_op jit(solution)/shard_map/ppermute | solution.py:62
  73.9 17.4 %collective-permute-start.13 = (bf16[64,7168]{1,0:T(8,128)(2,1)}, bf16[64,7168]{1,0:T(8,128)(2,1)}, u32[]{:S(2)}, u32[]{:S(2)}) collective-permute-start(bf16[64,7168]{1,0:T(8,128)(2,1)} %get-tuple-element.64.refs_3_), channel_id=1, source_target_pairs={{0,16},{16,0},{1,17},{17,1},{2,18},{18,2},{3,19},{19,3},{4,20},{20... | collective-permute-start | bytes 2752520 | tf_op jit(solution)/shard_map/ppermute | solution.py:66
  73.9 40.9 %collective-permute-start.14 = (bf16[64,8192]{1,0:T(8,128)(2,1)}, bf16[64,8192]{1,0:T(8,128)(2,1)}, u32[]{:S(2)}, u32[]{:S(2)}) collective-permute-start(bf16[64,8192]{1,0:T(8,128)(2,1)} %get-tuple-element.61), channel_id=1, source_target_pairs={{0,12},{1,13},{2,14},{3,15},{4,8},{5,9},{6,10},{7,11},{8,4},{9,5},... | collective-permute-start | bytes 3145736 | tf_op jit(solution)/shard_map/ppermute | solution.py:62
  75.3 23.0 %copy-start.1 = (s32[4]{0:T(128)S(1)}, s32[4]{0:T(128)}, u32[]{:S(2)}) copy-start(s32[4]{0:T(128)} %param.11) | copy-start | bytes 52
  97.4 17.4 %collective-permute-start.15 = (bf16[64,7168]{1,0:T(8,128)(2,1)}, bf16[64,7168]{1,0:T(8,128)(2,1)}, u32[]{:S(2)}, u32[]{:S(2)}) collective-permute-start(bf16[64,7168]{1,0:T(8,128)(2,1)} %get-tuple-element.78.refs_2_), channel_id=1, source_target_pairs={{0,2},{1,3},{2,0},{3,1},{4,6},{5,7},{6,4},{7,5},{8,10},{9,11},{10,... | collective-permute-start | bytes 2752520 | tf_op jit(solution)/shard_map/ppermute | solution.py:62
  97.7 17.1 %collective-permute-start.16 = (bf16[64,7168]{1,0:T(8,128)(2,1)}, bf16[64,7168]{1,0:T(8,128)(2,1)}, u32[]{:S(2)}, u32[]{:S(2)}) collective-permute-start(bf16[64,7168]{1,0:T(8,128)(2,1)} %get-tuple-element.78.refs_2_), channel_id=1, source_target_pairs={{0,16},{16,0},{1,17},{17,1},{2,18},{18,2},{3,19},{19,3},{4,20},{20... | collective-permute-start | bytes 2752520 | tf_op jit(solution)/shard_map/ppermute | solution.py:66
  98.5 17.8 %copy-start.2 = (s32[4]{0:T(128)S(1)}, s32[4]{0:T(128)}, u32[]{:S(2)}) copy-start(s32[4]{0:T(128)} %param.12) | copy-start | bytes 52
  98.5 47.0 %copy-start.3 = (s32[8]{0:T(128)S(1)}, s32[8]{0:T(128)}, u32[]{:S(2)}) copy-start(s32[8]{0:T(128)} %constant.51.clone) | copy-start | bytes 100
  115.9 45.6 %collective-permute-start.18 = (bf16[64,8192]{1,0:T(8,128)(2,1)}, bf16[64,8192]{1,0:T(8,128)(2,1)}, u32[]{:S(2)}, u32[]{:S(2)}) collective-permute-start(bf16[64,8192]{1,0:T(8,128)(2,1)} %get-tuple-element.83.refs_3_), channel_id=1, source_target_pairs={{0,4},{1,5},{2,6},{3,7},{4,0},{5,1},{6,2},{7,3},{8,12},{9,13},{10,... | collective-permute-start | bytes 3145736 | tf_op jit(solution)/shard_map/ppermute | solution.py:62
  116.0 45.6 %collective-permute-start.19 = (bf16[64,8192]{1,0:T(8,128)(2,1)}, bf16[64,8192]{1,0:T(8,128)(2,1)}, u32[]{:S(2)}, u32[]{:S(2)}) collective-permute-start(bf16[64,8192]{1,0:T(8,128)(2,1)} %get-tuple-element.83.refs_3_), channel_id=1, source_target_pairs={{0,2},{1,3},{2,0},{3,1},{4,6},{5,7},{6,4},{7,5},{8,10},{9,11},{10,... | collective-permute-start | bytes 3145736 | tf_op jit(solution)/shard_map/ppermute | solution.py:62
  116.3 45.2 %collective-permute-start.20 = (bf16[64,7168]{1,0:T(8,128)(2,1)}, bf16[64,7168]{1,0:T(8,128)(2,1)}, u32[]{:S(2)}, u32[]{:S(2)}) collective-permute-start(bf16[64,7168]{1,0:T(8,128)(2,1)} %get-tuple-element.87.refs_0_), channel_id=1, source_target_pairs={{0,16},{16,0},{1,17},{17,1},{2,18},{18,2},{3,19},{19,3},{4,20},{20... | collective-permute-start | bytes 2752520 | tf_op jit(solution)/shard_map/ppermute | solution.py:66
  117.6 29.0 %collective-permute-start.17 = (s32[2,4]{1,0:T(2,128)S(1)}, s32[2,4]{1,0:T(2,128)S(1)}, u32[]{:S(2)}, u32[]{:S(2)}) collective-permute-start(s32[2,4]{1,0:T(2,128)S(1)} %pad_add_fusion), channel_id=1, source_target_pairs={{0,1},{1,0},{2,3},{3,2},{4,5},{5,4},{6,7},{7,6},{8,9},{9,8},{10,11... | collective-permute-start | bytes 104 | tf_op jit(solution)/shard_map/ppermute | solution.py:62
  162.8 25.1 %collective-permute-start.21 = (bf16[64,8192]{1,0:T(8,128)(2,1)}, bf16[64,8192]{1,0:T(8,128)(2,1)}, u32[]{:S(2)}, u32[]{:S(2)}) collective-permute-start(bf16[64,8192]{1,0:T(8,128)(2,1)} %get-tuple-element.96.refs_2_), channel_id=1, source_target_pairs={{0,2},{1,3},{2,0},{3,1},{4,6},{5,7},{6,4},{7,5},{8,10},{9,11},{10,... | collective-permute-start | bytes 3145736 | tf_op jit(solution)/shard_map/ppermute | solution.py:62
  163.1 24.8 %collective-permute-start.23 = (bf16[64,8192]{1,0:T(8,128)(2,1)}, bf16[64,8192]{1,0:T(8,128)(2,1)}, u32[]{:S(2)}, u32[]{:S(2)}) collective-permute-start(bf16[64,8192]{1,0:T(8,128)(2,1)} %get-tuple-element.97), channel_id=1, source_target_pairs={{0,4},{1,5},{2,6},{3,7},{4,0},{5,1},{6,2},{7,3},{8,12},{9,13},{10,... | collective-permute-start | bytes 3145736 | tf_op jit(solution)/shard_map/ppermute | solution.py:62
  163.2 21.6 %collective-permute-start.22 = (bf16[64,7168]{1,0:T(8,128)(2,1)}, bf16[64,7168]{1,0:T(8,128)(2,1)}, u32[]{:S(2)}, u32[]{:S(2)}) collective-permute-start(bf16[64,7168]{1,0:T(8,128)(2,1)} %get-tuple-element.93.refs_1_), channel_id=1, source_target_pairs={{0,16},{16,0},{1,17},{17,1},{2,18},{18,2},{3,19},{19,3},{4,20},{20... | collective-permute-start | bytes 2752520 | tf_op jit(solution)/shard_map/ppermute | solution.py:66
  166.3 34.5 %collective-permute-start.24 = (bf16[32,7168]{1,0:T(8,128)(2,1)}, bf16[32,7168]{1,0:T(8,128)(2,1)}, u32[]{:S(2)}, u32[]{:S(2)}) collective-permute-start(bf16[32,7168]{1,0:T(8,128)(2,1)} %slice.19), channel_id=1, source_target_pairs={{0,2},{1,3},{2,0},{3,1},{4,6},{5,7},{6,4},{7,5},{8,10},{9,11},{10,... | collective-permute-start | bytes 1376264 | tf_op jit(solution)/shard_map/ppermute | solution.py:62
  168.4 32.4 %collective-permute-start.25 = (bf16[32,7168]{1,0:T(8,128)(2,1)}, bf16[32,7168]{1,0:T(8,128)(2,1)}, u32[]{:S(2)}, u32[]{:S(2)}) collective-permute-start(bf16[32,7168]{1,0:T(8,128)(2,1)} %slice.20), channel_id=1, source_target_pairs={{0,16},{16,0},{1,17},{17,1},{2,18},{18,2},{3,19},{19,3},{4,20},{20... | collective-permute-start | bytes 1376264 | tf_op jit(solution)/shard_map/ppermute | solution.py:66
  169.5 15.3 %copy-start = (f32[8,256]{1,0:T(8,128)S(1)}, f32[8,256]{1,0:T(8,128)}, u32[]{:S(2)}) copy-start(f32[8,256]{1,0:T(8,128)} %get-tuple-element.91) | copy-start | bytes 24580
  184.8 30.1 %collective-permute-start.26 = (f32[8,256]{1,0:T(8,128)S(1)}, f32[8,256]{1,0:T(8,128)S(1)}, u32[]{:S(2)}, u32[]{:S(2)}) collective-permute-start(f32[8,256]{1,0:T(8,128)S(1)} %copy-done), channel_id=1, source_target_pairs={{0,1},{1,0},{2,3},{3,2},{4,5},{5,4},{6,7},{7,6},{8,9},{9,8},{10,11... | collective-permute-start | bytes 24584 | tf_op jit(solution)/shard_map/ppermute | solution.py:62
  213.7 2.3 %collective-permute-start.27 = (f32[8,256]{1,0:T(8,128)}, f32[8,256]{1,0:T(8,128)S(1)}, u32[]{:S(2)}, u32[]{:S(2)}) collective-permute-start(f32[8,256]{1,0:T(8,128)} %get-tuple-element.108), channel_id=1, source_target_pairs={{0,1},{1,0},{2,3},{3,2},{4,5},{5,4},{6,7},{7,6},{8,9},{9,8},{10,11... | collective-permute-start | bytes 24584 | tf_op jit(solution)/shard_map/ppermute | solution.py:62

commit v21 on v19

--- a/solution.py
+++ b/solution.py
@@ -364,7 +364,7 @@
     c["low"] = swap_groups(a["xo"][split:])
     turn, a_second = times_a(turn, 1)
 
-    turn, (b["xo"], c["xf"], b["xn"]) = after(turn, [b["xo"], c["xf"], b["xn"]], inside)
+    turn, (b["xo"], b["xn"]) = after(turn, [b["xo"], b["xn"]], inside)
     turn, b_second = times_b(turn, 1)
     groups = (groups[0], ("xn", "xf", "o", "top", "low"))
     turn, score_second = times_c(turn, 1, False, spans, (a_second, b_second))

time: 205 us -> 206 us (level)
    ppermute x19, waiting for transfers between devices: 32.7 us -> 39.7 us  [flip(): return lax.ppermute(array, 'dp', [(i, i ^ code) for i in range(count)])]
    ppermute x7, waiting for transfers between devices: 23 us -> 17.6 us  [swap_groups(): return lax.ppermute(array, 'groups', [(0, 1), (1, 0)])]
  transfers between devices with their start and end apart: 28 -> 28, of which waited for: 11 -> 10; matrix products, arithmetic and copies ran while one was open for 5% -> 5% of each run, Pallas kernels for 42% -> 42%
where the time goes in v21:
time: 206 us; the launch traced here: 204 us
  Pallas kernels  89.9 us (44%)
  waiting for transfers between devices  59.9 us (29%)
  starting transfers between devices  41.3 us (20%)
  local copies, waits for them, and re-layouts  8.51 us (4%)
    pallas_call x6, Pallas kernels, proj(): pl.pallas_call(functools.partial(proj_kernel, len(pieces), last), out_sha...  71.1 us
    ppermute x19, waiting for transfers between devices, flip(): return lax.ppermute(array, 'dp', [(i, i ^ code) for i in range(count)])  39.7 us
    ppermute x19, starting transfers between devices, flip(): return lax.ppermute(array, 'dp', [(i, i ^ code) for i in range(count)])  28.5 us
    ppermute x7, waiting for transfers between devices, swap_groups(): return lax.ppermute(array, 'groups', [(0, 1), (1, 0)])  17.6 us
    pallas_call x9, Pallas kernels, after(): pl.pallas_call(functools.partial(after_kernel, count, merge is not None),...  12.4 us
    ppermute x7, starting transfers between devices, swap_groups(): return lax.ppermute(array, 'groups', [(0, 1), (1, 0)])  6.89 us
    pallas_call x1, Pallas kernels, prepare(): pl.pallas_call(prepare_kernel, out_shape=[jax.ShapeDtypeStruct(x.shape, x...  6.41 us
    ppermute x2, starting transfers between devices, lines(): lax.ppermute(array, 'dp', [(a * 4 + rest, b * 4 + rest) for a, b in pairs...  5.91 us
  transfers between devices with their start and end apart: 28, of which 10 were waited for; matrix products, arithmetic and copies ran while one was open for 5% of the time, Pallas kernels for 42%

profile of v21, /device:TPU:9, one launch (start us, length us, event | category | flops | bytes accessed | tf_op | source)
XLA Modules:
  0.0 203.5 jit_solution(13067013219064118831)
XLA Ops:
  0.7 2.2 %constant_dynamic-slice_fusion.refs_4_ = bf16[64,7168]{1,0:T(8,128)(2,1)} fusion(bf16[64,14336]{1,0:T(8,128)(2,1)} %bitcast.19, s32[]{:T(128)S(6)} %select_n.20), kind=kLoop, calls=%fused_computation.22 | loop fusion | bytes 1835012 | tf_op jit(solution)/shard_map/dynamic_slice | solution.py:266
  2.9 1.2 collective-permute-start.1
  4.3 4.3 %collective-permute-start.3 = (bf16[64,7168]{1,0:T(8,128)(2,1)}, bf16[64,7168]{1,0:T(8,128)(2,1)}, u32[]{:S(2)}, u32[]{:S(2)}) collective-permute-start(bf16[64,7168]{1,0:T(8,128)(2,1)} %constant_dynamic-slice_fusion.refs_4_), channel_id=1, source_target_pairs={{4,8},{5,9},{6,10},{7,11},{8,4},{9,5},{10,6},{11,7},{20,24},{21,25... | collective-permute-start | bytes 2752520 | tf_op jit(solution)/shard_map/ppermute | solution.py:158
  8.6 6.4 %shard_map.73 = (bf16[64,7168]{1,0:T(8,128)(2,1)}, bf16[64,8192]{1,0:T(8,128)(2,1)}, bf16[64,8192]{1,0:T(8,128)(2,1)}, s32[1]{0:T(128)}) custom-call(s32[1]{0:T(128)} %constant.21.clone.1.works_ref, s32[1]{0:T(128)} %constant.14.clone.1.turn_ref, s32[1]{0:T(128)S(6)} %sub.13.first_ref, bf16[64,14336]{1,0:T(8,128)(2,1)} %bitcast.20, bf16[64,8192]{1,0:T(8,128)(2,1)} %bitcast.17), custom_call_target="tpu_custom_call" | custom-call | flops 1 | bytes 1 | tf_op jit(solution)/shard_map/pallas_call | solution.py:141
  15.0 9.6 %collective-permute-done.1.refs_1_ = bf16[64,7168]{1,0:T(8,128)(2,1)} collective-permute-done((bf16[64,7168]{1,0:T(8,128)(2,1)}, bf16[64,7168]{1,0:T(8,128)(2,1)}, u32[]{:S(2)}, u32[]{:S(2)}) %collective-permute-start.1) | collective-permute-done | bytes 917536 | tf_op jit(solution)/shard_map/ppermute | solution.py:62
  24.6 1.2 collective-permute-start.6
  25.8 2.7 %collective-permute-done.3.refs_3_ = bf16[64,7168]{1,0:T(8,128)(2,1)} collective-permute-done((bf16[64,7168]{1,0:T(8,128)(2,1)}, bf16[64,7168]{1,0:T(8,128)(2,1)}, u32[]{:S(2)}, u32[]{:S(2)}) %collective-permute-start.3) | collective-permute-done | bytes 917536 | tf_op jit(solution)/shard_map/ppermute | solution.py:158
  29.7 1.6 collective-permute-start.5
  31.3 1.2 collective-permute-start.7
  34.0 14.2 %collective-permute-done.6.refs_3_ = bf16[64,8192]{1,0:T(8,128)(2,1)} collective-permute-done((bf16[64,8192]{1,0:T(8,128)(2,1)}, bf16[64,8192]{1,0:T(8,128)(2,1)}, u32[]{:S(2)}, u32[]{:S(2)}) %collective-permute-start.6) | collective-permute-done | bytes 1048608 | tf_op jit(solution)/shard_map/ppermute | solution.py:62
  49.4 2.3 %collective-permute-done.7.refs_4_ = bf16[64,7168]{1,0:T(8,128)(2,1)} collective-permute-done((bf16[64,7168]{1,0:T(8,128)(2,1)}, bf16[64,7168]{1,0:T(8,128)(2,1)}, u32[]{:S(2)}, u32[]{:S(2)}) %collective-permute-start.7) | collective-permute-done | bytes 917536 | tf_op jit(solution)/shard_map/ppermute | solution.py:66
  51.7 3.2 %shard_map.76 = (bf16[64,7168]{1,0:T(8,128)(2,1)}, bf16[64,8192]{1,0:T(8,128)(2,1)}, bf16[64,7168]{1,0:T(8,128)(2,1)}, s32[1]{0:T(128)}) custom-call(s32[1]{0:T(128)} %bitcast.inside_ref, s32[1]{0:T(128)} %shard_map.75.turn_ref, bf16[64,7168]{1,0:T(8,128)(2,1)} %get-tuple-element.58.refs_0_, ...), custom_call_target="tpu_custom_call", output_to_operand_aliasing={{0}: (4, {}), {1}: (5, {}), {2}: (6, {})} | custom-call | flops 1 | bytes 1 | tf_op jit(solution)/shard_map/pallas_call | solution.py:106
  56.2 15.2 %collective-permute-done.10.refs_2_ = bf16[64,7168]{1,0:T(8,128)(2,1)} collective-permute-done((bf16[64,7168]{1,0:T(8,128)(2,1)}, bf16[64,7168]{1,0:T(8,128)(2,1)}, u32[]{:S(2)}, u32[]{:S(2)}) %collective-permute-start.10) | collective-permute-done | bytes 917536 | tf_op jit(solution)/shard_map/ppermute | solution.py:66
  74.1 1.2 collective-permute-start.13
  76.1 10.9 %shard_map.79 = (f32[1024,256]{1,0:T(8,128)}, s32[1]{0:T(128)}) custom-call(s32[1]{0:T(128)} %get-tuple-element.66.turn_ref, s32[3]{0:T(128)} %concatenate.21.at_ref, bf16[512,14336]{1,0:T(8,128)(2,1)} %own_ref.11, bf16[512,14336]{1,0:T(8,128)(2,1)} %collective-permute-done.refs_0_.other_ref, bf16[64,7168]{1,0:T(8,128)(2,1)} %get-tuple-element.59.refs_0_, ...), custom_call_target="tpu_custom_call" | custom-call | flops 1 | bytes 1 | tf_op jit(solution)/shard_map/pallas_call | solution.py:222
  87.1 2.4 %collective-permute-done.12.refs_1_ = bf16[64,7168]{1,0:T(8,128)(2,1)} collective-permute-done((bf16[64,7168]{1,0:T(8,128)(2,1)}, bf16[64,7168]{1,0:T(8,128)(2,1)}, u32[]{:S(2)}, u32[]{:S(2)}) %collective-permute-start.12) | collective-permute-done | bytes 917536 | tf_op jit(solution)/shard_map/ppermute | solution.py:62
  89.5 4.5 %collective-permute-done.11.refs_0_ = bf16[64,8192]{1,0:T(8,128)(2,1)} collective-permute-done((bf16[64,8192]{1,0:T(8,128)(2,1)}, bf16[64,8192]{1,0:T(8,128)(2,1)}, u32[]{:S(2)}, u32[]{:S(2)}) %collective-permute-start.11) | collective-permute-done | bytes 1048608 | tf_op jit(solution)/shard_map/ppermute | solution.py:62
  95.5 1.2 collective-permute-start.16
  97.4 10.8 %shard_map.81 = (f32[1024,256]{1,0:T(8,128)}, s32[1]{0:T(128)}) custom-call(s32[1]{0:T(128)} %get-tuple-element.71.turn_ref, s32[3]{0:T(128)} %concatenate.22.at_ref, bf16[512,14336]{1,0:T(8,128)(2,1)} %own_ref.11, bf16[512,14336]{1,0:T(8,128)(2,1)} %collective-permute-done.refs_0_.other_ref, bf16[64,7168]{1,0:T(8,128)(2,1)} %get-tuple-element.72.refs_0_, ...), custom_call_target="tpu_custom_call" | custom-call | flops 1 | bytes 1 | tf_op jit(solution)/shard_map/pallas_call | solution.py:222
  109.5 9.3 %collective-permute-start.18 = (bf16[64,8192]{1,0:T(8,128)(2,1)}, bf16[64,8192]{1,0:T(8,128)(2,1)}, u32[]{:S(2)}, u32[]{:S(2)}) collective-permute-start(bf16[64,8192]{1,0:T(8,128)(2,1)} %get-tuple-element.82.refs_3_), channel_id=1, source_target_pairs={{0,4},{1,5},{2,6},{3,7},{4,0},{5,1},{6,2},{7,3},{8,12},{9,13},{10,... | collective-permute-start | bytes 3145736 | tf_op jit(solution)/shard_map/ppermute | solution.py:62
  119.1 1.3 collective-permute-start.20
  120.4 9.8 %collective-permute-start.17 = (s32[2,4]{1,0:T(2,128)S(1)}, s32[2,4]{1,0:T(2,128)S(1)}, u32[]{:S(2)}, u32[]{:S(2)}) collective-permute-start(s32[2,4]{1,0:T(2,128)S(1)} %pad_add_fusion), channel_id=1, source_target_pairs={{0,1},{1,0},{2,3},{3,2},{4,5},{5,4},{6,7},{7,6},{8,9},{9,8},{10,11... | collective-permute-start | bytes 104 | tf_op jit(solution)/shard_map/ppermute | solution.py:62
  132.6 13.8 %shard_map.83 = (f32[8,256]{1,0:T(8,128)}, s32[1]{0:T(128)}) custom-call(s32[1]{0:T(128)} %get-tuple-element.79.turn_ref, s32[3]{0:T(128)} %broadcast_7_at_ref.2.at_ref, bf16[512,8192]{1,0:T(8,128)(2,1)} %own_ref.10, bf16[512,8192]{1,0:T(8,128)(2,1)} %collective-permute-done.4.refs_1_.other_ref, bf16[64,8192]{1,0:T(8,128)(2,1)} %bitcast.18, ...), custom_call_target="tpu_custom_call" | custom-call | flops 1 | bytes 1 | tf_op jit(solution)/shard_map/pallas_call | solution.py:222
  149.2 1.8 slice.19
  151.2 1.8 slice.20
  153.0 1.3 collective-permute-start.25
  154.3 10.9 %shard_map.85 = (f32[1024,256]{1,0:T(8,128)}, s32[1]{0:T(128)}) custom-call(s32[1]{0:T(128)} %get-tuple-element.91.turn_ref, s32[3]{0:T(128)} %concatenate.21.at_ref, bf16[512,14336]{1,0:T(8,128)(2,1)} %own_ref.11, bf16[512,14336]{1,0:T(8,128)(2,1)} %collective-permute-done.refs_0_.other_ref, bf16[64,7168]{1,0:T(8,128)(2,1)} %get-tuple-element.86.refs_0_, ...), custom_call_target="tpu_custom_call" | custom-call | flops 1 | bytes 1 | tf_op jit(solution)/shard_map/pallas_call | solution.py:222
  165.2 7.6 %collective-permute-done.21.refs_0_ = bf16[64,8192]{1,0:T(8,128)(2,1)} collective-permute-done((bf16[64,8192]{1,0:T(8,128)(2,1)}, bf16[64,8192]{1,0:T(8,128)(2,1)}, u32[]{:S(2)}, u32[]{:S(2)}) %collective-permute-start.21) | collective-permute-done | bytes 1048608 | tf_op jit(solution)/shard_map/ppermute | solution.py:62
  172.8 1.2 collective-permute-start.26
  175.2 11.7 %shard_map.87 = (f32[1024,256]{1,0:T(8,128)}, s32[1]{0:T(128)}) custom-call(s32[1]{0:T(128)} %get-tuple-element.97.turn_ref, s32[3]{0:T(128)} %broadcast_7_at_ref.2.at_ref, bf16[512,8192]{1,0:T(8,128)(2,1)} %own_ref.10, bf16[512,8192]{1,0:T(8,128)(2,1)} %collective-permute-done.4.refs_1_.other_ref, bf16[64,8192]{1,0:T(8,128)(2,1)} %get-tuple-element.98.refs_0_, ...), custom_call_target="tpu_custom_call" | custom-call | flops 1 | bytes 1 | tf_op jit(solution)/shard_map/pallas_call | solution.py:222
  186.9 12.9 %shard_map.88 = (f32[8,256]{1,0:T(8,128)}, s32[1]{0:T(128)}) custom-call(s32[1]{0:T(128)} %get-tuple-element.101.turn_ref, s32[3]{0:T(128)} %concatenate.22.at_ref, bf16[512,14336]{1,0:T(8,128)(2,1)} %own_ref.11, bf16[512,14336]{1,0:T(8,128)(2,1)} %collective-permute-done.refs_0_.other_ref, bf16[64,7168]{1,0:T(8,128)(2,1)} %get-tuple-element.102.refs_0_, ...), custom_call_target="tpu_custom_call" | custom-call | flops 1 | bytes 1 | tf_op jit(solution)/shard_map/pallas_call | solution.py:222
  201.7 1.9 fusion.1
  (71 shorter events, 21.3 us)
Async XLA Ops:
  0.0 28.5 %collective-permute-start = (bf16[512,14336]{1,0:T(8,128)(2,1)}, bf16[512,14336]{1,0:T(8,128)(2,1)}, u32[]{:S(2)}, u32[]{:S(2)}) collective-permute-start(bf16[512,14336]{1,0:T(8,128)(2,1)} %own_ref.11), channel_id=1, source_target_pairs={{0,1},{1,0},{2,3},{3,2},{4,5},{5,4},{6,7},{7,6},{8,9},{9,8},{10,11... | collective-permute-start | bytes 44040200 | tf_op jit(solution)/shard_map/ppermute | solution.py:62
  0.7 48.7 %collective-permute-start.4 = (bf16[512,8192]{1,0:T(8,128)(2,1)}, bf16[512,8192]{1,0:T(8,128)(2,1)}, u32[]{:S(2)}, u32[]{:S(2)}) collective-permute-start(bf16[512,8192]{1,0:T(8,128)(2,1)} %own_ref.10), channel_id=1, source_target_pairs={{0,1},{1,0},{2,3},{3,2},{4,5},{5,4},{6,7},{7,6},{8,9},{9,8},{10,11... | collective-permute-start | bytes 25165832 | tf_op jit(solution)/shard_map/ppermute | solution.py:62
  2.9 21.7 %collective-permute-start.1 = (bf16[64,7168]{1,0:T(8,128)(2,1)}, bf16[64,7168]{1,0:T(8,128)(2,1)}, u32[]{:S(2)}, u32[]{:S(2)}) collective-permute-start(bf16[64,7168]{1,0:T(8,128)(2,1)} %constant_dynamic-slice_fusion.refs_4_), channel_id=1, source_target_pairs={{0,2},{1,3},{2,0},{3,1},{4,6},{5,7},{6,4},{7,5},{8,10},{9,11},{10,... | collective-permute-start | bytes 2752520 | tf_op jit(solution)/shard_map/ppermute | solution.py:62
  4.1 21.7 %collective-permute-start.2 = (bf16[64,7168]{1,0:T(8,128)(2,1)}, bf16[64,7168]{1,0:T(8,128)(2,1)}, u32[]{:S(2)}, u32[]{:S(2)}) collective-permute-start(bf16[64,7168]{1,0:T(8,128)(2,1)} %constant_dynamic-slice_fusion.refs_4_), channel_id=1, source_target_pairs={{0,4},{1,5},{2,6},{3,7},{4,0},{5,1},{6,2},{7,3},{8,12},{9,13},{10,... | collective-permute-start | bytes 2752520 | tf_op jit(solution)/shard_map/ppermute | solution.py:62
  4.3 24.3 %collective-permute-start.3 = (bf16[64,7168]{1,0:T(8,128)(2,1)}, bf16[64,7168]{1,0:T(8,128)(2,1)}, u32[]{:S(2)}, u32[]{:S(2)}) collective-permute-start(bf16[64,7168]{1,0:T(8,128)(2,1)} %constant_dynamic-slice_fusion.refs_4_), channel_id=1, source_target_pairs={{4,8},{5,9},{6,10},{7,11},{8,4},{9,5},{10,6},{11,7},{20,24},{21,25... | collective-permute-start | bytes 2752520 | tf_op jit(solution)/shard_map/ppermute | solution.py:158
  24.6 23.6 %collective-permute-start.6 = (bf16[64,8192]{1,0:T(8,128)(2,1)}, bf16[64,8192]{1,0:T(8,128)(2,1)}, u32[]{:S(2)}, u32[]{:S(2)}) collective-permute-start(bf16[64,8192]{1,0:T(8,128)(2,1)} %get-tuple-element.60), channel_id=1, source_target_pairs={{0,2},{1,3},{2,0},{3,1},{4,6},{5,7},{6,4},{7,5},{8,10},{9,11},{10,... | collective-permute-start | bytes 3145736 | tf_op jit(solution)/shard_map/ppermute | solution.py:62
  29.7 19.8 %collective-permute-start.5 = (bf16[64,7168]{1,0:T(8,128)(2,1)}, bf16[64,7168]{1,0:T(8,128)(2,1)}, u32[]{:S(2)}, u32[]{:S(2)}) collective-permute-start(bf16[64,7168]{1,0:T(8,128)(2,1)} %get-tuple-element.59.refs_0_), channel_id=1, source_target_pairs={{0,12},{1,13},{2,14},{3,15},{12,0},{13,1},{14,2},{15,3},{16,28},{1... | collective-permute-start | bytes 2752520 | tf_op jit(solution)/shard_map/ppermute | solution.py:158
  31.3 20.5 %collective-permute-start.7 = (bf16[64,7168]{1,0:T(8,128)(2,1)}, bf16[64,7168]{1,0:T(8,128)(2,1)}, u32[]{:S(2)}, u32[]{:S(2)}) collective-permute-start(bf16[64,7168]{1,0:T(8,128)(2,1)} %get-tuple-element.61.refs_1_), channel_id=1, source_target_pairs={{0,16},{16,0},{1,17},{17,1},{2,18},{18,2},{3,19},{19,3},{4,20},{20... | collective-permute-start | bytes 2752520 | tf_op jit(solution)/shard_map/ppermute | solution.py:66
  33.7 37.7 %collective-permute-start.10 = (bf16[64,7168]{1,0:T(8,128)(2,1)}, bf16[64,7168]{1,0:T(8,128)(2,1)}, u32[]{:S(2)}, u32[]{:S(2)}) collective-permute-start(bf16[64,7168]{1,0:T(8,128)(2,1)} %get-tuple-element.64.refs_2_), channel_id=1, source_target_pairs={{0,16},{16,0},{1,17},{17,1},{2,18},{18,2},{3,19},{19,3},{4,20},{20... | collective-permute-start | bytes 2752520 | tf_op jit(solution)/shard_map/ppermute | solution.py:66
  48.2 23.2 %collective-permute-start.9 = (bf16[64,7168]{1,0:T(8,128)(2,1)}, bf16[64,7168]{1,0:T(8,128)(2,1)}, u32[]{:S(2)}, u32[]{:S(2)}) collective-permute-start(bf16[64,7168]{1,0:T(8,128)(2,1)} %get-tuple-element.64.refs_2_), channel_id=1, source_target_pairs={{0,2},{1,3},{2,0},{3,1},{4,6},{5,7},{6,4},{7,5},{8,10},{9,11},{10,... | collective-permute-start | bytes 2752520 | tf_op jit(solution)/shard_map/ppermute | solution.py:62
  54.9 17.4 %collective-permute-start.8 = (bf16[64,7168]{1,0:T(8,128)(2,1)}, bf16[64,7168]{1,0:T(8,128)(2,1)}, u32[]{:S(2)}, u32[]{:S(2)}) collective-permute-start(bf16[64,7168]{1,0:T(8,128)(2,1)} %get-tuple-element.63.refs_3_), channel_id=1, source_target_pairs={{0,4},{1,5},{2,6},{3,7},{4,0},{5,1},{6,2},{7,3},{8,12},{9,13},{10,... | collective-permute-start | bytes 2752520 | tf_op jit(solution)/shard_map/ppermute | solution.py:62
  73.5 20.5 %collective-permute-start.11 = (bf16[64,8192]{1,0:T(8,128)(2,1)}, bf16[64,8192]{1,0:T(8,128)(2,1)}, u32[]{:S(2)}, u32[]{:S(2)}) collective-permute-start(bf16[64,8192]{1,0:T(8,128)(2,1)} %get-tuple-element.68), channel_id=1, source_target_pairs={{0,4},{1,5},{2,6},{3,7},{4,0},{5,1},{6,2},{7,3},{8,12},{9,13},{10,... | collective-permute-start | bytes 3145736 | tf_op jit(solution)/shard_map/ppermute | solution.py:62
  73.9 15.6 %collective-permute-start.12 = (bf16[64,7168]{1,0:T(8,128)(2,1)}, bf16[64,7168]{1,0:T(8,128)(2,1)}, u32[]{:S(2)}, u32[]{:S(2)}) collective-permute-start(bf16[64,7168]{1,0:T(8,128)(2,1)} %get-tuple-element.63.refs_3_), channel_id=1, source_target_pairs={{0,2},{1,3},{2,0},{3,1},{4,6},{5,7},{6,4},{7,5},{8,10},{9,11},{10,... | collective-permute-start | bytes 2752520 | tf_op jit(solution)/shard_map/ppermute | solution.py:62
  74.1 15.4 %collective-permute-start.13 = (bf16[64,7168]{1,0:T(8,128)(2,1)}, bf16[64,7168]{1,0:T(8,128)(2,1)}, u32[]{:S(2)}, u32[]{:S(2)}) collective-permute-start(bf16[64,7168]{1,0:T(8,128)(2,1)} %get-tuple-element.63.refs_3_), channel_id=1, source_target_pairs={{0,16},{16,0},{1,17},{17,1},{2,18},{18,2},{3,19},{19,3},{4,20},{20... | collective-permute-start | bytes 2752520 | tf_op jit(solution)/shard_map/ppermute | solution.py:66
  75.3 32.9 %collective-permute-start.14 = (bf16[64,8192]{1,0:T(8,128)(2,1)}, bf16[64,8192]{1,0:T(8,128)(2,1)}, u32[]{:S(2)}, u32[]{:S(2)}) collective-permute-start(bf16[64,8192]{1,0:T(8,128)(2,1)} %get-tuple-element.60), channel_id=1, source_target_pairs={{0,12},{1,13},{2,14},{3,15},{4,8},{5,9},{6,10},{7,11},{8,4},{9,5},... | collective-permute-start | bytes 3145736 | tf_op jit(solution)/shard_map/ppermute | solution.py:62
  76.1 21.1 %copy-start.1 = (s32[4]{0:T(128)S(1)}, s32[4]{0:T(128)}, u32[]{:S(2)}) copy-start(s32[4]{0:T(128)} %param.11) | copy-start | bytes 52
  95.1 13.2 %collective-permute-start.15 = (bf16[64,7168]{1,0:T(8,128)(2,1)}, bf16[64,7168]{1,0:T(8,128)(2,1)}, u32[]{:S(2)}, u32[]{:S(2)}) collective-permute-start(bf16[64,7168]{1,0:T(8,128)(2,1)} %get-tuple-element.77.refs_2_), channel_id=1, source_target_pairs={{0,2},{1,3},{2,0},{3,1},{4,6},{5,7},{6,4},{7,5},{8,10},{9,11},{10,... | collective-permute-start | bytes 2752520 | tf_op jit(solution)/shard_map/ppermute | solution.py:62
  95.5 12.9 %collective-permute-start.16 = (bf16[64,7168]{1,0:T(8,128)(2,1)}, bf16[64,7168]{1,0:T(8,128)(2,1)}, u32[]{:S(2)}, u32[]{:S(2)}) collective-permute-start(bf16[64,7168]{1,0:T(8,128)(2,1)} %get-tuple-element.77.refs_2_), channel_id=1, source_target_pairs={{0,16},{16,0},{1,17},{17,1},{2,18},{18,2},{3,19},{19,3},{4,20},{20... | collective-permute-start | bytes 2752520 | tf_op jit(solution)/shard_map/ppermute | solution.py:66
  97.4 21.7 %copy-start.2 = (s32[4]{0:T(128)S(1)}, s32[4]{0:T(128)}, u32[]{:S(2)}) copy-start(s32[4]{0:T(128)} %param.12) | copy-start | bytes 52
  97.4 32.8 %copy-start.3 = (s32[8]{0:T(128)S(1)}, s32[8]{0:T(128)}, u32[]{:S(2)}) copy-start(s32[8]{0:T(128)} %constant.51.clone) | copy-start | bytes 100
  109.5 37.0 %collective-permute-start.18 = (bf16[64,8192]{1,0:T(8,128)(2,1)}, bf16[64,8192]{1,0:T(8,128)(2,1)}, u32[]{:S(2)}, u32[]{:S(2)}) collective-permute-start(bf16[64,8192]{1,0:T(8,128)(2,1)} %get-tuple-element.82.refs_3_), channel_id=1, source_target_pairs={{0,4},{1,5},{2,6},{3,7},{4,0},{5,1},{6,2},{7,3},{8,12},{9,13},{10,... | collective-permute-start | bytes 3145736 | tf_op jit(solution)/shard_map/ppermute | solution.py:62
  118.8 27.7 %collective-permute-start.19 = (bf16[64,8192]{1,0:T(8,128)(2,1)}, bf16[64,8192]{1,0:T(8,128)(2,1)}, u32[]{:S(2)}, u32[]{:S(2)}) collective-permute-start(bf16[64,8192]{1,0:T(8,128)(2,1)} %get-tuple-element.82.refs_3_), channel_id=1, source_target_pairs={{0,2},{1,3},{2,0},{3,1},{4,6},{5,7},{6,4},{7,5},{8,10},{9,11},{10,... | collective-permute-start | bytes 3145736 | tf_op jit(solution)/shard_map/ppermute | solution.py:62
  119.1 27.4 %collective-permute-start.20 = (bf16[64,7168]{1,0:T(8,128)(2,1)}, bf16[64,7168]{1,0:T(8,128)(2,1)}, u32[]{:S(2)}, u32[]{:S(2)}) collective-permute-start(bf16[64,7168]{1,0:T(8,128)(2,1)} %get-tuple-element.86.refs_0_), channel_id=1, source_target_pairs={{0,16},{16,0},{1,17},{17,1},{2,18},{18,2},{3,19},{19,3},{4,20},{20... | collective-permute-start | bytes 2752520 | tf_op jit(solution)/shard_map/ppermute | solution.py:66
  120.4 11.0 %collective-permute-start.17 = (s32[2,4]{1,0:T(2,128)S(1)}, s32[2,4]{1,0:T(2,128)S(1)}, u32[]{:S(2)}, u32[]{:S(2)}) collective-permute-start(s32[2,4]{1,0:T(2,128)S(1)} %pad_add_fusion), channel_id=1, source_target_pairs={{0,1},{1,0},{2,3},{3,2},{4,5},{5,4},{6,7},{7,6},{8,9},{9,8},{10,11... | collective-permute-start | bytes 104 | tf_op jit(solution)/shard_map/ppermute | solution.py:62
  147.6 25.1 %collective-permute-start.21 = (bf16[64,8192]{1,0:T(8,128)(2,1)}, bf16[64,8192]{1,0:T(8,128)(2,1)}, u32[]{:S(2)}, u32[]{:S(2)}) collective-permute-start(bf16[64,8192]{1,0:T(8,128)(2,1)} %get-tuple-element.95.refs_2_), channel_id=1, source_target_pairs={{0,2},{1,3},{2,0},{3,1},{4,6},{5,7},{6,4},{7,5},{8,10},{9,11},{10,... | collective-permute-start | bytes 3145736 | tf_op jit(solution)/shard_map/ppermute | solution.py:62
  148.8 25.2 %collective-permute-start.22 = (bf16[64,8192]{1,0:T(8,128)(2,1)}, bf16[64,8192]{1,0:T(8,128)(2,1)}, u32[]{:S(2)}, u32[]{:S(2)}) collective-permute-start(bf16[64,8192]{1,0:T(8,128)(2,1)} %get-tuple-element.96), channel_id=1, source_target_pairs={{0,4},{1,5},{2,6},{3,7},{4,0},{5,1},{6,2},{7,3},{8,12},{9,13},{10,... | collective-permute-start | bytes 3145736 | tf_op jit(solution)/shard_map/ppermute | solution.py:62
  148.8 38.1 %collective-permute-start.23 = (bf16[64,7168]{1,0:T(8,128)(2,1)}, bf16[64,7168]{1,0:T(8,128)(2,1)}, u32[]{:S(2)}, u32[]{:S(2)}) collective-permute-start(bf16[64,7168]{1,0:T(8,128)(2,1)} %get-tuple-element.92.refs_1_), channel_id=1, source_target_pairs={{0,16},{16,0},{1,17},{17,1},{2,18},{18,2},{3,19},{19,3},{4,20},{20... | collective-permute-start | bytes 2752520 | tf_op jit(solution)/shard_map/ppermute | solution.py:66
  151.0 35.9 %collective-permute-start.24 = (bf16[32,7168]{1,0:T(8,128)(2,1)}, bf16[32,7168]{1,0:T(8,128)(2,1)}, u32[]{:S(2)}, u32[]{:S(2)}) collective-permute-start(bf16[32,7168]{1,0:T(8,128)(2,1)} %slice.19), channel_id=1, source_target_pairs={{0,2},{1,3},{2,0},{3,1},{4,6},{5,7},{6,4},{7,5},{8,10},{9,11},{10,... | collective-permute-start | bytes 1376264 | tf_op jit(solution)/shard_map/ppermute | solution.py:62
  153.0 33.9 %collective-permute-start.25 = (bf16[32,7168]{1,0:T(8,128)(2,1)}, bf16[32,7168]{1,0:T(8,128)(2,1)}, u32[]{:S(2)}, u32[]{:S(2)}) collective-permute-start(bf16[32,7168]{1,0:T(8,128)(2,1)} %slice.20), channel_id=1, source_target_pairs={{0,16},{16,0},{1,17},{17,1},{2,18},{18,2},{3,19},{19,3},{4,20},{20... | collective-permute-start | bytes 1376264 | tf_op jit(solution)/shard_map/ppermute | solution.py:66
  154.3 18.5 %copy-start = (f32[8,256]{1,0:T(8,128)S(1)}, f32[8,256]{1,0:T(8,128)}, u32[]{:S(2)}) copy-start(f32[8,256]{1,0:T(8,128)} %get-tuple-element.90) | copy-start | bytes 24580
  172.8 27.9 %collective-permute-start.26 = (f32[8,256]{1,0:T(8,128)S(1)}, f32[8,256]{1,0:T(8,128)S(1)}, u32[]{:S(2)}, u32[]{:S(2)}) collective-permute-start(f32[8,256]{1,0:T(8,128)S(1)} %copy-done), channel_id=1, source_target_pairs={{0,1},{1,0},{2,3},{3,2},{4,5},{5,4},{6,7},{7,6},{8,9},{9,8},{10,11... | collective-permute-start | bytes 24584 | tf_op jit(solution)/shard_map/ppermute | solution.py:62
  199.9 1.8 collective-permute-start.27
